TPU v7x, 32 devices: a whole 2x2x4 slice. The times are simulated.
32 devices in a mesh: ctx: 16 (over z, x, core), tp: 2 (over y).
Axes of the slice: x: 2, y: 2, z: 4, core: 2. Of those that a mesh axis runs over, the one named last changes fastest.
Arguments:
- features: bfloat16 [32, 196, 1152], P('ctx', None, 'tp'), may hold values from -6 to 6
- group_kernel: bfloat16 [9, 1152, 48], P(None, 'tp'), may hold values from -0.3125 to 0.3125
- squeeze_in: bfloat16 [1152, 288], P('tp'), may hold values from -0.75 to 0.75
- squeeze_out: bfloat16 [288, 1152], P(None, 'tp'), may hold values from -0.75 to 0.75
- sampler_kernel: bfloat16 [1152, 8, 1152], P('ctx', None, 'tp'), may hold values from -0.0625 to 0.0625
- readout_kernel: bfloat16 [1152, 8192], P('ctx', 'tp'), may hold values from -0.1875 to 0.1875
- frame_clip: int32 [32], replicated, may hold values from 0 to 3, as said below
- clip_keep: int32 [4], replicated, may hold values from 1 to 512, as said below
- token_cotangent: bfloat16 [1024, 8192], P('ctx', 'tp'), may hold values from -6 to 6
Outputs:
- llm_tokens: bfloat16 [1024, 8192], P('ctx', 'tp')
- grad_features: bfloat16 [32, 196, 1152], P('ctx', None, 'tp')
Inputs may be any that keep to these rules, and one draw needn't show every extreme that they name: `frame_clip`: clip ids start at 0 and never fall along the frames; every clip covers an even number of frames from 2 to 16 and starts at an even frame; some clip covers 16. `clip_keep`: each clip keeps at least one and at most 8 * 8 times half its frames of its tokens; the clip of 16 frames keeps all of its tokens, and some clip keeps a single token.
All inputs are finite; a program needn't handle non-finite values.
Results may differ from a plain program's by a relative error of at most 0.009.
Values may be sent and summed in bfloat16 or wider, within the bound.
No kernel may reach another device: no remote copies, remote signals or barrier semaphores. Data moves between devices by JAX's collectives and lax.ppermute only.
A program may use at most 128 MiB of HBM per device.

v0:
```python
import jax
import jax.numpy as jnp
from jax import lax
from jax.experimental import pallas as pl
from jax.experimental.pallas import tpu as pltpu
from jax.sharding import PartitionSpec as P

SIDE = 14
OUT_SIDE = 8
WIDE = 16
FRAME_ROWS = WIDE * WIDE
EDGE = 8
LANES = 128
VMEM_BYTES = 40 * 2**20


def whole_call(kernel, outs, scratch, flops, moved):
    return pl.pallas_call(
        kernel,
        out_shape=outs,
        scratch_shapes=scratch,
        compiler_params=pltpu.CompilerParams(vmem_limit_bytes=VMEM_BYTES),
        cost_estimate=pl.CostEstimate(flops=flops, bytes_accessed=moved, transcendentals=0),
    )


def silu_slope(values):
    sigma = jax.nn.sigmoid(values)
    return sigma * (1.0 + values * (1.0 - sigma))


def inside(rows):
    row = lax.broadcasted_iota(jnp.int32, (rows, 1), 0)
    across, down = row & (WIDE - 1), (row // WIDE) & (WIDE - 1)
    good = (across >= 1) & (across <= SIDE) & (down >= 1) & (down <= SIDE)
    return good.astype(jnp.float32)


def channel_blocks(chans, width):
    span = 4 * width
    blocks = []
    for low in range(0, chans, span):
        high = min(chans, low + span)
        blocks.append((low, high, low // LANES * LANES, min(chans, -(-high // LANES) * LANES)))
    return blocks


def block_tools(block, width):
    low, high, start, end = block
    size = end - start
    out_lane = lax.broadcasted_iota(jnp.int32, (width, size), 1) + start
    within = lax.broadcasted_iota(jnp.int32, (width, size), 0)
    lane = lax.broadcasted_iota(jnp.int32, (size, size), 1) + start
    row = lax.broadcasted_iota(jnp.int32, (size, size), 0) + start
    spread = jnp.zeros((width, size), jnp.float32)
    same = jnp.zeros((size, size), jnp.float32)
    for first in range(low, high, width):
        spread += (out_lane == within + first).astype(jnp.float32)
        in_lane = (lane >= first) & (lane < first + width)
        in_row = (row >= first) & (row < first + width)
        same += (in_lane & in_row).astype(jnp.float32)
    return spread.astype(jnp.bfloat16), same


def dense_tap(group_ref, tap, block, spread, same):
    _, _, start, end = block
    full = jnp.dot(group_ref[tap, start:end, :], spread, preferred_element_type=jnp.float32)
    return (full * same).astype(jnp.bfloat16)


def store_shifts(wide_ref, shift_ref, sign):
    rows = shift_ref.shape[1]
    for col in range(3):
        at = EDGE + sign * (col - 1)
        shift_ref[col] = wide_ref[at : at + rows, :].astype(jnp.bfloat16)


def conv_kernel(feat_ref, group_ref, squeeze_ref, conv_ref, pad_ref, sq_ref, flat_ref, wide_ref, shift_ref):
    frames, _, chans = feat_ref.shape
    width = group_ref.shape[2]
    rows = frames * FRAME_ROWS
    wide_ref[...] = jnp.zeros_like(wide_ref)
    for frame in range(frames):
        flat_ref[...] = feat_ref[frame].astype(jnp.float32)
        for y in range(SIDE):
            at = EDGE + frame * FRAME_ROWS + (y + 1) * WIDE + 1
            wide_ref[at : at + SIDE, :] = flat_ref[y * SIDE : (y + 1) * SIDE, :]
    store_shifts(wide_ref, shift_ref, 1)
    pad_ref[...] = shift_ref[1]
    conv_ref[...] = jnp.zeros_like(conv_ref)
    body = rows - 2 * WIDE
    for block in channel_blocks(chans, width):
        _, _, start, end = block
        spread, same = block_tools(block, width)
        total = jnp.zeros((body, end - start), jnp.float32)
        for tap in range(9):
            down, across = divmod(tap, 3)
            weights = dense_tap(group_ref, tap, block, spread, same)
            source = shift_ref[across, down * WIDE : down * WIDE + body, start:end]
            total += jnp.dot(source, weights, preferred_element_type=jnp.float32)
        conv_ref[WIDE : WIDE + body, start:end] += total
    conv = conv_ref[...] * inside(rows)
    conv_ref[...] = conv
    active = conv * jax.nn.sigmoid(conv)
    pooled = jnp.concatenate(
        [
            jnp.sum(active[f * FRAME_ROWS : (f + 1) * FRAME_ROWS], axis=0, keepdims=True)
            for f in range(frames)
        ],
        axis=0,
    ) * (1.0 / (SIDE * SIDE))
    sq_ref[...] = jnp.dot(
        pooled, squeeze_ref[...].astype(jnp.float32), precision=lax.Precision.HIGHEST
    )


def hidden_kernel(conv_ref, pad_ref, sq_ref, expand_ref, even_ref, odd_ref, excite_ref):
    squeezed = sq_ref[...]
    relaxed = squeezed * jax.nn.sigmoid(squeezed)
    excite = jax.nn.sigmoid(
        jnp.dot(relaxed, expand_ref[...].astype(jnp.float32), precision=lax.Precision.HIGHEST)
    )
    excite_ref[...] = excite
    for frame, out_ref in enumerate((even_ref, odd_ref)):
        rows = slice(frame * FRAME_ROWS, (frame + 1) * FRAME_ROWS)
        conv = conv_ref[rows, :]
        active = conv * jax.nn.sigmoid(conv)
        hidden = pad_ref[rows, :].astype(jnp.float32) + active * excite[frame : frame + 1]
        out_ref[...] = hidden.astype(jnp.bfloat16)


def select_rows(to_patches):
    shape = (FRAME_ROWS, FRAME_ROWS)
    out_row = lax.broadcasted_iota(jnp.int32, shape, 0)
    in_row = lax.broadcasted_iota(jnp.int32, shape, 1)
    patch_row, frame_row = (out_row, in_row) if to_patches else (in_row, out_row)
    down, across = patch_row >> 7, (patch_row >> 6) & 1
    a, b = (patch_row >> 3) & 7, patch_row & 7
    return ((2 * a + down) * WIDE + 2 * b + across == frame_row).astype(jnp.float32)


def patch_kernel(mask_ref, halo_ref, even_ref, out_ref):
    chans = halo_ref.shape[1]
    per_frame = OUT_SIDE * OUT_SIDE
    select = select_rows(True).astype(jnp.bfloat16)
    for frame, source in enumerate((halo_ref, even_ref)):
        rows = jnp.dot(select, source[...], preferred_element_type=jnp.float32)
        if frame == 0:
            rows = rows * mask_ref[0, 0]
        rows = rows.astype(jnp.bfloat16)
        for tap in range(4):
            at = (frame * 4 + tap) * chans
            out_ref[:, at : at + chans] = rows[tap * per_frame : (tap + 1) * per_frame]


def unpatch_kernel(mask_ref, own_ref, mate_ref, lead_ref, even_ref):
    chans = lead_ref.shape[1]
    select = select_rows(False)
    frames = []
    for frame in range(2):
        pieces = []
        for tap in range(frame * 4, frame * 4 + 4):
            lanes = slice(tap * chans, (tap + 1) * chans)
            pieces.append(own_ref[:, lanes] + mate_ref[:, lanes])
        frames.append(
            jnp.dot(select, jnp.concatenate(pieces, axis=0), precision=lax.Precision.HIGHEST)
        )
    good = inside(FRAME_ROWS)
    lead_ref[...] = (frames[0] * (good * mask_ref[0, 0])).astype(jnp.bfloat16)
    even_ref[...] = frames[1] * good


def excite_grad_kernel(even_ref, odd_ref, conv_ref, excite_ref, expand_ref, out_ref):
    sums = []
    for frame, grad_ref in enumerate((even_ref, odd_ref)):
        conv = conv_ref[frame * FRAME_ROWS : (frame + 1) * FRAME_ROWS, :]
        active = conv * jax.nn.sigmoid(conv)
        sums.append(jnp.sum(grad_ref[...].astype(jnp.float32) * active, axis=0, keepdims=True))
    excite = excite_ref[...]
    inner = jnp.concatenate(sums, axis=0) * excite * (1.0 - excite)
    out_ref[...] = lax.dot_general(
        inner,
        expand_ref[...].astype(jnp.float32),
        (((1,), (1,)), ((), ())),
        precision=lax.Precision.HIGHEST,
        preferred_element_type=jnp.float32,
    )


def conv_grad_kernel(
    even_ref, odd_ref, conv_ref, excite_ref, sq_ref, relaxed_ref, squeeze_ref, group_ref,
    out_ref, flat_ref, wide_ref, shift_ref, grad_ref,
):
    frames, _, chans = out_ref.shape
    width = group_ref.shape[2]
    rows = frames * FRAME_ROWS
    grad_squeezed = relaxed_ref[...] * silu_slope(sq_ref[...])
    pooled = lax.dot_general(
        grad_squeezed,
        squeeze_ref[...].astype(jnp.float32),
        (((1,), (1,)), ((), ())),
        precision=lax.Precision.HIGHEST,
        preferred_element_type=jnp.float32,
    ) * (1.0 / (SIDE * SIDE))
    wide_ref[0:EDGE, :] = jnp.zeros((EDGE, chans), jnp.float32)
    wide_ref[EDGE + rows :, :] = jnp.zeros((EDGE, chans), jnp.float32)
    good = inside(FRAME_ROWS)
    for frame, source in enumerate((even_ref, odd_ref)):
        at = frame * FRAME_ROWS
        grad = source[...].astype(jnp.float32)
        grad_ref[at : at + FRAME_ROWS, :] = grad
        active = grad * excite_ref[frame : frame + 1, :] + pooled[frame : frame + 1]
        slope = silu_slope(conv_ref[at : at + FRAME_ROWS, :])
        wide_ref[EDGE + at : EDGE + at + FRAME_ROWS, :] = active * slope * good
    store_shifts(wide_ref, shift_ref, -1)
    body = rows - 2 * WIDE
    for block in channel_blocks(chans, width):
        _, _, start, end = block
        spread, same = block_tools(block, width)
        total = jnp.zeros((body, end - start), jnp.float32)
        for tap in range(9):
            down, across = divmod(tap, 3)
            weights = dense_tap(group_ref, tap, block, spread, same)
            at = (2 - down) * WIDE
            source = shift_ref[across, at : at + body, start:end]
            total += lax.dot_general(
                source, weights, (((1,), (1,)), ((), ())), preferred_element_type=jnp.float32
            )
        grad_ref[WIDE : WIDE + body, start:end] += total
    for frame in range(frames):
        for y in range(SIDE):
            at = frame * FRAME_ROWS + (y + 1) * WIDE + 1
            flat_ref[y * SIDE : (y + 1) * SIDE, :] = grad_ref[at : at + SIDE, :]
        out_ref[frame] = flat_ref[...].astype(jnp.bfloat16)


def f32(*shape):
    return jax.ShapeDtypeStruct(shape, jnp.float32)


def bf16(*shape):
    return jax.ShapeDtypeStruct(shape, jnp.bfloat16)


def conv_forward(features, group_kernel, squeeze_in):
    frames, cells, chans = features.shape
    rows = frames * FRAME_ROWS
    return whole_call(
        conv_kernel,
        (f32(rows, chans), bf16(rows, chans), f32(frames, squeeze_in.shape[1])),
        [
            pltpu.VMEM((cells, chans), jnp.float32),
            pltpu.VMEM((rows + 2 * EDGE, chans), jnp.float32),
            pltpu.VMEM((3, rows, chans), jnp.bfloat16),
        ],
        rows * chans * 256 * 18 * 2,
        rows * chans * 8 + 9 * chans * 256,
    )(features, group_kernel, squeeze_in)


def hidden_frames(conv, padded, squeezed, squeeze_out):
    rows, chans = conv.shape
    return whole_call(
        hidden_kernel,
        (bf16(FRAME_ROWS, chans), bf16(FRAME_ROWS, chans), f32(rows // FRAME_ROWS, chans)),
        [],
        rows * chans * 10,
        rows * chans * 8,
    )(conv, padded, squeezed, squeeze_out)


def vmem_specs(count):
    return [pl.BlockSpec(memory_space=pltpu.SMEM)] + [pl.BlockSpec(memory_space=pltpu.VMEM)] * count


def take_patches(mask, halo, even):
    chans = even.shape[1]
    return pl.pallas_call(
        patch_kernel,
        out_shape=bf16(OUT_SIDE * OUT_SIDE, 8 * chans),
        in_specs=vmem_specs(2),
        compiler_params=pltpu.CompilerParams(vmem_limit_bytes=VMEM_BYTES),
        cost_estimate=pl.CostEstimate(
            flops=8 * FRAME_ROWS * chans, bytes_accessed=8 * FRAME_ROWS * chans, transcendentals=0
        ),
    )(mask, halo, even)


def return_patches(mask, own, mate, chans):
    return pl.pallas_call(
        unpatch_kernel,
        out_shape=(bf16(FRAME_ROWS, chans), f32(FRAME_ROWS, chans)),
        in_specs=vmem_specs(2),
        compiler_params=pltpu.CompilerParams(vmem_limit_bytes=VMEM_BYTES),
        cost_estimate=pl.CostEstimate(
            flops=8 * FRAME_ROWS * chans, bytes_accessed=24 * FRAME_ROWS * chans, transcendentals=0
        ),
    )(mask, own, mate)


def excite_grad(even, odd, conv, excite, squeeze_out):
    rows, chans = conv.shape
    return whole_call(
        excite_grad_kernel,
        f32(rows // FRAME_ROWS, squeeze_out.shape[0]),
        [],
        rows * chans * 10,
        rows * chans * 7,
    )(even, odd, conv, excite, squeeze_out)


def conv_backward(even, odd, conv, excite, squeezed, grad_relaxed, squeeze_in, group_kernel):
    rows, chans = conv.shape
    frames = rows // FRAME_ROWS
    return whole_call(
        conv_grad_kernel,
        bf16(frames, SIDE * SIDE, chans),
        [
            pltpu.VMEM((SIDE * SIDE, chans), jnp.float32),
            pltpu.VMEM((rows + 2 * EDGE, chans), jnp.float32),
            pltpu.VMEM((3, rows, chans), jnp.bfloat16),
            pltpu.VMEM((rows, chans), jnp.float32),
        ],
        rows * chans * 256 * 18 * 2,
        rows * chans * 10 + 9 * chans * 256,
    )(even, odd, conv, excite, squeezed, grad_relaxed, squeeze_in, group_kernel)


def shifted(value, axis, by):
    count = lax.axis_size(axis)
    pairs = [(i, i + by) for i in range(count) if 0 <= i + by < count]
    return lax.ppermute(value, axis, pairs)


def ring_order(chips):
    return list(range(0, chips, 2)) + list(range(1, chips, 2))[::-1]


def ring_pairs(count, by):
    order = ring_order(count // 2)
    pairs = []
    for place, chip in enumerate(order):
        target = order[(place + by) % len(order)]
        pairs += [(2 * chip, 2 * target), (2 * chip + 1, 2 * target + 1)]
    return pairs


def swap_cores(value):
    return lax.ppermute(value, "ctx", [(i, i ^ 1) for i in range(lax.axis_size("ctx"))])


def sum_tp(value):
    size = lax.axis_size("tp")
    reach = 1
    while reach < size:
        value = value + lax.ppermute(value, "tp", [(i, i ^ reach) for i in range(size)])
        reach *= 2
    return value


def ring_gather(samplers, readouts):
    count = lax.axis_size("ctx")
    chips = count // 2
    onward, backward = ring_pairs(count, 1), ring_pairs(count, -1)
    groups = [([samplers], [readouts])]
    up_s = down_s = samplers
    up_r = down_r = readouts
    for step in range(1, chips // 2):
        up_r, down_r = lax.ppermute(up_r, "ctx", onward), lax.ppermute(down_r, "ctx", backward)
        up_s, down_s = lax.ppermute(up_s, "ctx", onward), lax.ppermute(down_s, "ctx", backward)
        groups.append(([up_s, down_s], [up_r, down_r]))
    up_s = lax.ppermute(up_s, "ctx", onward)
    down_r = lax.ppermute(down_r, "ctx", backward)
    groups.append(([up_s], [down_r]))
    return groups


def contract_last(left, right):
    return lax.dot_general(
        left, right, (((1,), (1,)), ((), ())), preferred_element_type=jnp.float32
    )


def per_device(
    features,
    group_kernel,
    squeeze_in,
    squeeze_out,
    sampler_kernel,
    readout_kernel,
    frame_clip,
    clip_keep,
    token_cotangent,
):
    shard_index = lax.axis_index("ctx")
    frames_dev, cells, chans = features.shape
    pairs_dev = frames_dev // 2
    flat_sampler = sampler_kernel.reshape(sampler_kernel.shape[0], 8 * chans)
    groups = ring_gather(flat_sampler, readout_kernel)

    local_clip = lax.dynamic_slice_in_dim(frame_clip, shard_index * frames_dev, frames_dev)
    edge_clip = lax.dynamic_slice_in_dim(
        frame_clip, jnp.maximum(shard_index * frames_dev - 1, 0), 1
    )
    first_keep = jnp.logical_and(shard_index > 0, edge_clip[0] == local_clip[0])
    mask = first_keep.astype(jnp.float32).reshape(1, 1)
    per_frame = OUT_SIDE * OUT_SIDE
    pair_clip = frame_clip[0::2]
    clip_ids = jnp.arange(clip_keep.shape[0], dtype=jnp.int32)
    start_pair = jnp.sum((pair_clip[None, :] < clip_ids[:, None]).astype(jnp.int32), axis=1)
    own_clip = local_clip[0::2]
    one_hot = (own_clip[:, None] == clip_ids[None, :]).astype(jnp.int32)
    own_start = jnp.sum(one_hot * start_pair[None, :], axis=1)
    own_keep = jnp.sum(one_hot * clip_keep[None, :], axis=1)
    pair_index = shard_index * pairs_dev + jnp.arange(pairs_dev, dtype=jnp.int32)
    position = (pair_index - own_start)[:, None] * per_frame + jnp.arange(
        per_frame, dtype=jnp.int32
    )[None, :]
    live = (position < own_keep[:, None]).reshape(-1).astype(jnp.bfloat16)

    back = (
        lax.all_to_all(token_cotangent, "ctx", split_axis=0, concat_axis=0, tiled=True)
        * live[:, None]
    )
    rows = back.shape[0]
    both_back = jnp.concatenate([back, swap_cores(back)], axis=0)

    conv, padded, squeezed = conv_forward(features, group_kernel, squeeze_in)
    squeezed = sum_tp(squeezed)
    even, odd, excite = hidden_frames(conv, padded, squeezed, squeeze_out)
    patches = take_patches(mask, shifted(odd, "ctx", 1), even)
    both_patches = jnp.concatenate([patches, swap_cores(patches)], axis=0)

    both_tokens = both_grads = 0.0
    for group_s, group_r in groups:
        partial = jnp.concatenate(
            [contract_last(both_patches, part) for part in group_s]
            + [contract_last(both_back, part) for part in group_r],
            axis=1,
        )
        pre, grad_act = jnp.split(sum_tp(partial), 2, axis=1)
        act = jax.nn.silu(pre).astype(jnp.bfloat16)
        grad_pre = (grad_act * silu_slope(pre)).astype(jnp.bfloat16)
        for piece, part in zip(jnp.split(act, len(group_r), axis=1), group_r):
            both_tokens += jnp.dot(piece, part, preferred_element_type=jnp.float32)
        for piece, part in zip(jnp.split(grad_pre, len(group_s), axis=1), group_s):
            both_grads += jnp.dot(piece, part, preferred_element_type=jnp.float32)
    lead, grad_even = return_patches(mask, both_grads[:rows], swap_cores(both_grads[rows:]), chans)
    grad_odd = shifted(lead, "ctx", -1)
    grad_relaxed = sum_tp(excite_grad(grad_even, grad_odd, conv, excite, squeeze_out))
    grad_features = conv_backward(
        grad_even, grad_odd, conv, excite, squeezed, grad_relaxed, squeeze_in, group_kernel
    )
    tokens = (both_tokens[:rows] + swap_cores(both_tokens[rows:])).astype(jnp.bfloat16) * live[:, None]
    llm_tokens = lax.all_to_all(tokens, "ctx", split_axis=0, concat_axis=0, tiled=True)
    return (llm_tokens, grad_features)


def solution(mesh):
    placed = (
        P("ctx", None, "tp"),
        P(None, "tp", None),
        P("tp", None),
        P(None, "tp"),
        P("ctx", None, "tp"),
        P("ctx", "tp"),
        P(),
        P(),
        P("ctx", "tp"),
    )
    return jax.shard_map(
        per_device,
        mesh=mesh,
        in_specs=placed,
        out_specs=(P("ctx", "tp"), P("ctx", None, "tp")),
        check_vma=False,
    )
```

profile of v0, /device:TPU:3, one launch (start us, length us, event | category | flops | bytes accessed | tf_op | source)
XLA Modules:
  0.0 190.9 jit_solution(2050140156293675317)
XLA Ops:
  0.6 2.5 %copy.18.group_ref = bf16[9,576,48]{2,1,0:T(8,128)(2,1)} copy(bf16[9,576,48]{1,2,0:T(8,128)(2,1)} %param.10) | data formatting | bytes 995328 | tf_op args[1]
  3.4 1.3 copy-done.1
  4.8 4.3 %shard_map.104 = (f32[512,576]{1,0:T(8,128)S(1)}, bf16[512,576]{1,0:T(8,128)(2,1)S(1)}, f32[2,288]{1,0:T(2,128)S(1)}) custom-call(bf16[2,196,576]{2,1,0:T(8,128)(2,1)S(1)} %copy.17.feat_ref, bf16[9,576,48]{2,1,0:T(8,128)(2,1)S(1)} %copy-done.1, bf16[576,288]{1,0:T(8,128)(2,1)S(1)} %copy.19.squeeze_ref), custom_call_target="tpu_custom_call" | custom-call | flops 2717908992 | bytes 3686400 | tf_op jit(solution)/shard_map/pallas_call | solution.py:248
  9.1 1.3 collective-permute-start
  10.3 1.2 collective-permute-done
  11.6 1.5 shard_map.105
  13.0 5.0 %collective-permute-start.1 = (bf16[256,576]{1,0:T(8,128)(2,1)}, bf16[256,576]{1,0:T(8,128)(2,1)S(1)}, u32[]{:S(2)}, u32[]{:S(2)}) collective-permute-start(bf16[256,576]{1,0:T(8,128)(2,1)} %get-tuple-element.13), channel_id=1, source_target_pairs={{0,2},{2,4},{4,6},{6,8},{8,10},{10,12},{12,14},{14,16},{16,18},{18... | collective-permute-start | bytes 884744 | tf_op jit(solution)/shard_map/ppermute | solution.py:332
  18.0 2.3 %reshape.54 = bf16[72,4608]{1,0:T(8,128)(2,1)} reshape(bf16[72,8,576]{2,1,0:T(8,128)(2,1)} %param.13) | data formatting | bytes 1327104 | tf_op jit(solution)/shard_map/reshape | solution.py:398
  20.6 1.3 collective-permute-start.6
  21.8 1.3 collective-permute-start.8
  25.3 1.0 copy-done.4
  26.8 2.0 %all_to_all.16 = bf16[16,4,4096]{2,1,0:T(4,128)(2,1)} reshape(bf16[64,4096]{1,0:T(8,128)(2,1)} %param.17) | data formatting | bytes 1048576 | tf_op jit(solution)/shard_map/all_to_all | solution.py:422
  28.9 6.1 %all-to-all-start = ((bf16[16,4,4096]{2,1,0:T(4,128)(2,1)}), bf16[16,4,4096]{2,1,0:T(4,128)(2,1)S(1)}, u32[]{:S(2)}, u32[]{:S(2)}) async-start(bf16[16,4,4096]{2,1,0:T(4,128)(2,1)} %all_to_all.16), calls=%async_computation | async-start | bytes 1048576 | tf_op jit(solution)/shard_map/all_to_all | solution.py:422
  37.8 12.6 %collective-permute-done.8 = bf16[72,4096]{1,0:T(8,128)(2,1)} collective-permute-done((bf16[72,4096]{1,0:T(8,128)(2,1)}, bf16[72,4096]{1,0:T(8,128)(2,1)}, u32[]{:S(2)}, u32[]{:S(2)}) %collective-permute-start.8) | collective-permute-done | bytes 589856 | tf_op jit(solution)/shard_map/ppermute | solution.py:369
  50.5 1.1 collective-permute-start.13
  51.9 1.1 collective-permute-start.10
  53.4 1.8 fusion.60
  55.2 1.8 fusion.59
  57.0 4.6 %all-to-all-done = bf16[16,4,4096]{2,1,0:T(4,128)(2,1)S(1)} async-done(((bf16[16,4,4096]{2,1,0:T(4,128)(2,1)}), bf16[16,4,4096]{2,1,0:T(4,128)(2,1)S(1)}, u32[]{:S(2)}, u32[]{:S(2)}) %all-to-all-start) | async-done | bytes 524320 | tf_op jit(solution)/shard_map/all_to_all | solution.py:422
  62.5 1.1 broadcast_multiply_fusion
  63.7 1.0 collective-permute-start.3
  64.7 1.8 fusion.61
  66.5 4.2 %collective-permute-done.13 = bf16[72,4096]{1,0:T(8,128)(2,1)} collective-permute-done((bf16[72,4096]{1,0:T(8,128)(2,1)}, bf16[72,4096]{1,0:T(8,128)(2,1)}, u32[]{:S(2)}, u32[]{:S(2)}) %collective-permute-start.13) | collective-permute-done | bytes 589856 | tf_op jit(solution)/shard_map/ppermute | solution.py:369
  70.7 4.0 %collective-permute-start.18 = (bf16[72,4096]{1,0:T(8,128)(2,1)}, bf16[72,4096]{1,0:T(8,128)(2,1)S(1)}, u32[]{:S(2)}, u32[]{:S(2)}) collective-permute-start(bf16[72,4096]{1,0:T(8,128)(2,1)} %collective-permute-done.13), channel_id=1, source_target_pairs={{0,4},{2,6},{8,0},{10,2},{16,8},{18,10},{24,16},{26,18},{28,24},{3... | collective-permute-start | bytes 1769480 | tf_op jit(solution)/shard_map/ppermute | solution.py:369
  74.7 10.0 %collective-permute-done.10 = bf16[72,4608]{1,0:T(8,128)(2,1)} collective-permute-done((bf16[72,4608]{1,0:T(8,128)(2,1)}, bf16[72,4608]{1,0:T(8,128)(2,1)}, u32[]{:S(2)}, u32[]{:S(2)}) %collective-permute-start.10) | collective-permute-done | bytes 663584 | tf_op jit(solution)/shard_map/ppermute | solution.py:370
  84.9 4.6 %collective-permute-start.16 = (bf16[72,4608]{1,0:T(8,128)(2,1)}, bf16[72,4608]{1,0:T(8,128)(2,1)S(1)}, u32[]{:S(2)}, u32[]{:S(2)}) collective-permute-start(bf16[72,4608]{1,0:T(8,128)(2,1)} %collective-permute-done.11), channel_id=1, source_target_pairs={{0,4},{2,6},{8,0},{10,2},{16,8},{18,10},{24,16},{26,18},{28,24},{3... | collective-permute-start | bytes 1990664 | tf_op jit(solution)/shard_map/ppermute | solution.py:370
  89.5 1.8 fusion.58
  91.3 1.8 fusion.57
  93.6 1.3 collective-permute-start.4
  94.9 1.6 fusion.51
  96.5 1.6 fusion.52
  98.1 1.6 fusion.49
  99.6 1.6 fusion.50
  101.6 5.3 %collective-permute-done.9 = f32[128,288]{0,1:T(8,128)S(1)} collective-permute-done((f32[128,288]{0,1:T(8,128)S(1)}, f32[128,288]{0,1:T(8,128)S(1)}, u32[]{:S(2)}, u32[]{:S(2)}) %collective-permute-start.9) | collective-permute-done | bytes 147488 | tf_op jit(solution)/shard_map/ppermute | solution.py:356
  107.2 4.4 %collective-permute-done.14 = f32[128,288]{0,1:T(8,128)S(1)} collective-permute-done((f32[128,288]{0,1:T(8,128)S(1)}, f32[128,288]{0,1:T(8,128)S(1)}, u32[]{:S(2)}, u32[]{:S(2)}) %collective-permute-start.14) | collective-permute-done | bytes 147488 | tf_op jit(solution)/shard_map/ppermute | solution.py:356
  111.7 1.6 fusion.20
  113.8 1.5 fusion.29
  115.8 1.6 convolution_add_fusion.3
  117.4 1.6 fusion.16
  119.0 1.6 fusion.1
  120.6 1.5 convolution_add_fusion.8
  122.2 1.5 fusion.25
  124.7 1.6 fusion.56
  126.3 1.6 fusion.55
  128.2 1.5 fusion.3
  130.3 1.0 collective-permute-start.20
  133.6 9.2 %collective-permute-done.21 = bf16[72,4096]{1,0:T(8,128)(2,1)S(1)} collective-permute-done((bf16[72,4096]{1,0:T(8,128)(2,1)S(1)}, bf16[72,4096]{1,0:T(8,128)(2,1)S(1)}, u32[]{:S(2)}, u32[]{:S(2)}) %collective-permute-start.21) | collective-permute-done | bytes 589856 | tf_op jit(solution)/shard_map/ppermute | solution.py:373
  143.9 1.6 fusion.54
  145.6 1.3 collective-permute-start.22
  147.3 1.5 collective-permute-done.22
  149.4 4.9 %collective-permute-start.23 = (f32[64,4096]{1,0:T(8,128)S(1)}, f32[64,4096]{1,0:T(8,128)S(1)}, u32[]{:S(2)}, u32[]{:S(2)}) collective-permute-start(f32[64,4096]{1,0:T(8,128)S(1)} %slice.27), channel_id=1, source_target_pairs={{0,2},{2,0},{4,6},{6,4},{8,10},{10,8},{12,14},{14,12},{16,18},{18,... | collective-permute-start | bytes 3145736 | tf_op jit(solution)/shard_map/ppermute | solution.py:349
  154.8 1.2 fusion.62
  156.6 0.9 fusion.5
  157.5 2.0 %all_to_all.19 = bf16[16,4,4096]{2,1,0:T(4,128)(2,1)} reshape(bf16[64,4096]{1,0:T(8,128)(2,1)} %fusion.5) | data formatting | bytes 1048576 | tf_op jit(solution)/shard_map/all_to_all | solution.py:455
  159.5 5.2 %all-to-all-start.1 = ((bf16[16,4,4096]{2,1,0:T(4,128)(2,1)}), bf16[16,4,4096]{2,1,0:T(4,128)(2,1)}, u32[]{:S(2)}, u32[]{:S(2)}) async-start(bf16[16,4,4096]{2,1,0:T(4,128)(2,1)} %all_to_all.19), calls=%async_computation.1 | async-start | bytes 1048576 | tf_op jit(solution)/shard_map/all_to_all | solution.py:455
  164.8 2.9 %shard_map.107 = (bf16[256,576]{1,0:T(8,128)(2,1)S(1)}, f32[256,576]{1,0:T(8,128)S(1)}) custom-call(f32[1,1]{1,0:T(1,128)} %bitcast.2.mask_ref, f32[64,4608]{1,0:T(8,128)S(1)} %get-tuple-element.23.own_ref, f32[64,4608]{1,0:T(8,128)} %collective-permute-done.24.mate_ref), custom_call_target="tpu_custom_call" | custom-call | flops 1179648 | bytes 3538944 | tf_op jit(solution)/shard_map/pallas_call | solution.py:290
  167.7 2.3 %collective-permute-start.25 = (bf16[256,576]{1,0:T(8,128)(2,1)S(1)}, bf16[256,576]{1,0:T(8,128)(2,1)S(1)}, u32[]{:S(2)}, u32[]{:S(2)}) collective-permute-start(bf16[256,576]{1,0:T(8,128)(2,1)S(1)} %get-tuple-element.16), channel_id=1, source_target_pairs={{2,0},{4,2},{6,4},{8,6},{10,8},{12,10},{14,12},{16,14},{18,16},{20... | collective-permute-start | bytes 884744 | tf_op jit(solution)/shard_map/ppermute | solution.py:332
  170.0 9.5 %collective-permute-done.25.odd_ref = bf16[256,576]{1,0:T(8,128)(2,1)S(1)} collective-permute-done((bf16[256,576]{1,0:T(8,128)(2,1)S(1)}, bf16[256,576]{1,0:T(8,128)(2,1)S(1)}, u32[]{:S(2)}, u32[]{:S(2)}) %collective-permute-start.25) | collective-permute-done | bytes 294944 | tf_op jit(solution)/shard_map/ppermute | solution.py:332
  179.5 0.9 shard_map.108
  180.4 1.3 collective-permute-start.26
  181.7 1.2 collective-permute-done.26
  182.9 4.9 %shard_map.109 = bf16[2,196,576]{2,1,0:T(8,128)(2,1)S(1)} custom-call(f32[256,576]{1,0:T(8,128)S(1)} %get-tuple-element.15.even_ref, bf16[256,576]{1,0:T(8,128)(2,1)S(1)} %collective-permute-done.25.odd_ref, f32[512,576]{1,0:T(8,128)S(1)} %get-tuple-element.10.conv_ref, f32[2,576]{1,0:T(2,128)S(1)} %get-tuple-element.17.excite_ref, ...), custom_call_target="tpu_custom_call" | custom-call | flops 2717908992 | bytes 4276224 | tf_op jit(solution)/shard_map/pallas_call | solution.py:315
  187.8 1.2 copy.22
  189.0 2.0 %all_to_all.21 = bf16[64,4096]{1,0:T(8,128)(2,1)} reshape(bf16[16,4,4096]{2,1,0:T(4,128)(2,1)} %all-to-all-done.1) | data formatting | bytes 1048576 | tf_op jit(solution)/shard_map/all_to_all | solution.py:455
  (89 shorter events, 16.2 us)
Async XLA Ops:
  0.6 2.5 %copy-start.8 = (bf16[576,288]{0,1:T(8,128)(2,1)S(1)}, bf16[576,288]{0,1:T(8,128)(2,1)}, u32[]{:S(2)}) copy-start(bf16[576,288]{0,1:T(8,128)(2,1)} %param.11) | copy-start | bytes 995332
  0.6 2.7 %copy-start.7 = (bf16[2,196,576]{2,0,1:T(2,128)(2,1)S(1)}, bf16[2,196,576]{2,0,1:T(2,128)(2,1)}, u32[]{:S(2)}) copy-start(bf16[2,196,576]{2,0,1:T(2,128)(2,1)} %param.9) | copy-start | bytes 1354756
  3.4 1.3 copy-start.1
  4.8 6.8 %copy-start = (bf16[288,576]{1,0:T(8,128)(2,1)S(1)}, bf16[288,576]{1,0:T(8,128)(2,1)}, u32[]{:S(2)}) copy-start(bf16[288,576]{1,0:T(8,128)(2,1)} %expand_ref.3) | copy-start | bytes 995332
  9.1 14.2 %copy-start.9 = (s32[32]{0:T(128)S(1)}, s32[32]{0:T(128)}, u32[]{:S(2)}) copy-start(s32[32]{0:T(128)} %param.15) | copy-start | bytes 388
  9.1 2.5 %collective-permute-start = (f32[2,288]{1,0:T(2,128)S(1)}, f32[2,288]{1,0:T(2,128)S(1)}, u32[]{:S(2)}, u32[]{:S(2)}) collective-permute-start(f32[2,288]{1,0:T(2,128)S(1)} %get-tuple-element.12), channel_id=1, source_target_pairs={{0,1},{1,0},{2,3},{3,2},{4,5},{5,4},{6,7},{7,6},{8,9},{9,8},{10,11... | collective-permute-start | bytes 6920 | tf_op jit(solution)/shard_map/ppermute | solution.py:356
  13.0 23.5 %copy-start.10 = (s32[4]{0:T(128)S(1)}, s32[4]{0:T(128)}, u32[]{:S(2)}) copy-start(s32[4]{0:T(128)} %param.16) | copy-start | bytes 52
  13.0 11.6 %collective-permute-start.1 = (bf16[256,576]{1,0:T(8,128)(2,1)}, bf16[256,576]{1,0:T(8,128)(2,1)S(1)}, u32[]{:S(2)}, u32[]{:S(2)}) collective-permute-start(bf16[256,576]{1,0:T(8,128)(2,1)} %get-tuple-element.13), channel_id=1, source_target_pairs={{0,2},{2,4},{4,6},{6,8},{8,10},{10,12},{12,14},{14,16},{16,18},{18... | collective-permute-start | bytes 884744 | tf_op jit(solution)/shard_map/ppermute | solution.py:332
  20.4 31.6 %collective-permute-start.5 = (bf16[72,4608]{1,0:T(8,128)(2,1)}, bf16[72,4608]{1,0:T(8,128)(2,1)}, u32[]{:S(2)}, u32[]{:S(2)}) collective-permute-start(bf16[72,4608]{1,0:T(8,128)(2,1)} %reshape.54), channel_id=1, source_target_pairs={{0,8},{2,10},{8,16},{10,18},{16,24},{18,26},{24,28},{26,30},{28,20... | collective-permute-start | bytes 1990664 | tf_op jit(solution)/shard_map/ppermute | solution.py:370
  20.6 32.5 %collective-permute-start.6 = (bf16[72,4608]{1,0:T(8,128)(2,1)}, bf16[72,4608]{1,0:T(8,128)(2,1)}, u32[]{:S(2)}, u32[]{:S(2)}) collective-permute-start(bf16[72,4608]{1,0:T(8,128)(2,1)} %reshape.54), channel_id=1, source_target_pairs={{0,4},{2,6},{8,0},{10,2},{16,8},{18,10},{24,16},{26,18},{28,24},{3... | collective-permute-start | bytes 1990664 | tf_op jit(solution)/shard_map/ppermute | solution.py:370
  21.8 28.6 %collective-permute-start.8 = (bf16[72,4096]{1,0:T(8,128)(2,1)}, bf16[72,4096]{1,0:T(8,128)(2,1)}, u32[]{:S(2)}, u32[]{:S(2)}) collective-permute-start(bf16[72,4096]{1,0:T(8,128)(2,1)} %param.14), channel_id=1, source_target_pairs={{0,4},{2,6},{8,0},{10,2},{16,8},{18,10},{24,16},{26,18},{28,24},{3... | collective-permute-start | bytes 1769480 | tf_op jit(solution)/shard_map/ppermute | solution.py:369
  23.1 28.5 %collective-permute-start.7 = (bf16[72,4096]{1,0:T(8,128)(2,1)}, bf16[72,4096]{1,0:T(8,128)(2,1)}, u32[]{:S(2)}, u32[]{:S(2)}) collective-permute-start(bf16[72,4096]{1,0:T(8,128)(2,1)} %param.14), channel_id=1, source_target_pairs={{0,8},{2,10},{8,16},{10,18},{16,24},{18,26},{24,28},{26,30},{28,20... | collective-permute-start | bytes 1769480 | tf_op jit(solution)/shard_map/ppermute | solution.py:369
  24.6 0.7 copy-start.3
  25.3 1.0 copy-start.4
  26.8 26.6 %collective-permute-start.2 = (bf16[64,4608]{1,0:T(8,128)(2,1)S(1)}, bf16[64,4608]{1,0:T(8,128)(2,1)}, u32[]{:S(2)}, u32[]{:S(2)}) collective-permute-start(bf16[64,4608]{1,0:T(8,128)(2,1)S(1)} %shard_map.106), channel_id=1, source_target_pairs={{0,2},{2,0},{4,6},{6,4},{8,10},{10,8},{12,14},{14,12},{16,18},{18,... | collective-permute-start | bytes 1769480 | tf_op jit(solution)/shard_map/ppermute | solution.py:349
  28.9 32.7 %all-to-all-start = ((bf16[16,4,4096]{2,1,0:T(4,128)(2,1)}), bf16[16,4,4096]{2,1,0:T(4,128)(2,1)S(1)}, u32[]{:S(2)}, u32[]{:S(2)}) async-start(bf16[16,4,4096]{2,1,0:T(4,128)(2,1)} %all_to_all.16), calls=%async_computation | async-start | bytes 1048576 | tf_op jit(solution)/shard_map/all_to_all | solution.py:422
  50.5 20.2 %collective-permute-start.13 = (bf16[72,4096]{1,0:T(8,128)(2,1)}, bf16[72,4096]{1,0:T(8,128)(2,1)}, u32[]{:S(2)}, u32[]{:S(2)}) collective-permute-start(bf16[72,4096]{1,0:T(8,128)(2,1)} %collective-permute-done.8), channel_id=1, source_target_pairs={{0,4},{2,6},{8,0},{10,2},{16,8},{18,10},{24,16},{26,18},{28,24},{3... | collective-permute-start | bytes 1769480 | tf_op jit(solution)/shard_map/ppermute | solution.py:369
  51.6 23.1 %collective-permute-start.12 = (bf16[72,4096]{1,0:T(8,128)(2,1)}, bf16[72,4096]{1,0:T(8,128)(2,1)}, u32[]{:S(2)}, u32[]{:S(2)}) collective-permute-start(bf16[72,4096]{1,0:T(8,128)(2,1)} %collective-permute-done.7), channel_id=1, source_target_pairs={{0,8},{2,10},{8,16},{10,18},{16,24},{18,26},{24,28},{26,30},{28,20... | collective-permute-start | bytes 1769480 | tf_op jit(solution)/shard_map/ppermute | solution.py:369
  51.9 32.8 %collective-permute-start.10 = (bf16[72,4608]{1,0:T(8,128)(2,1)}, bf16[72,4608]{1,0:T(8,128)(2,1)}, u32[]{:S(2)}, u32[]{:S(2)}) collective-permute-start(bf16[72,4608]{1,0:T(8,128)(2,1)} %collective-permute-done.5), channel_id=1, source_target_pairs={{0,8},{2,10},{8,16},{10,18},{16,24},{18,26},{24,28},{26,30},{28,20... | collective-permute-start | bytes 1990664 | tf_op jit(solution)/shard_map/ppermute | solution.py:370
  53.0 31.9 %collective-permute-start.11 = (bf16[72,4608]{1,0:T(8,128)(2,1)}, bf16[72,4608]{1,0:T(8,128)(2,1)}, u32[]{:S(2)}, u32[]{:S(2)}) collective-permute-start(bf16[72,4608]{1,0:T(8,128)(2,1)} %collective-permute-done.6), channel_id=1, source_target_pairs={{0,4},{2,6},{8,0},{10,2},{16,8},{18,10},{24,16},{26,18},{28,24},{3... | collective-permute-start | bytes 1990664 | tf_op jit(solution)/shard_map/ppermute | solution.py:370
  63.7 29.4 %collective-permute-start.3 = (bf16[64,4096]{1,0:T(8,128)(2,1)S(1)}, bf16[64,4096]{1,0:T(8,128)(2,1)S(1)}, u32[]{:S(2)}, u32[]{:S(2)}) collective-permute-start(bf16[64,4096]{1,0:T(8,128)(2,1)S(1)} %broadcast_multiply_fusion), channel_id=1, source_target_pairs={{0,2},{2,0},{4,6},{6,4},{8,10},{10,8},{12,14},{14,12},{16,18},{18,... | collective-permute-start | bytes 1572872 | tf_op jit(solution)/shard_map/ppermute | solution.py:349
  66.5 26.6 %copy-start.6 = (bf16[72,4096]{1,0:T(8,128)(2,1)S(1)}, bf16[72,4096]{1,0:T(8,128)(2,1)}, u32[]{:S(2)}) copy-start(bf16[72,4096]{1,0:T(8,128)(2,1)} %param.14) | copy-start | bytes 1769476
  70.7 53.0 %collective-permute-start.18 = (bf16[72,4096]{1,0:T(8,128)(2,1)}, bf16[72,4096]{1,0:T(8,128)(2,1)S(1)}, u32[]{:S(2)}, u32[]{:S(2)}) collective-permute-start(bf16[72,4096]{1,0:T(8,128)(2,1)} %collective-permute-done.13), channel_id=1, source_target_pairs={{0,4},{2,6},{8,0},{10,2},{16,8},{18,10},{24,16},{26,18},{28,24},{3... | collective-permute-start | bytes 1769480 | tf_op jit(solution)/shard_map/ppermute | solution.py:369
  74.7 49.5 %collective-permute-start.17 = (bf16[72,4096]{1,0:T(8,128)(2,1)}, bf16[72,4096]{1,0:T(8,128)(2,1)S(1)}, u32[]{:S(2)}, u32[]{:S(2)}) collective-permute-start(bf16[72,4096]{1,0:T(8,128)(2,1)} %collective-permute-done.12), channel_id=1, source_target_pairs={{0,8},{2,10},{8,16},{10,18},{16,24},{18,26},{24,28},{26,30},{28,20... | collective-permute-start | bytes 1769480 | tf_op jit(solution)/shard_map/ppermute | solution.py:369
  84.8 40.0 %collective-permute-start.15 = (bf16[72,4608]{1,0:T(8,128)(2,1)}, bf16[72,4608]{1,0:T(8,128)(2,1)S(1)}, u32[]{:S(2)}, u32[]{:S(2)}) collective-permute-start(bf16[72,4608]{1,0:T(8,128)(2,1)} %collective-permute-done.10), channel_id=1, source_target_pairs={{0,8},{2,10},{8,16},{10,18},{16,24},{18,26},{24,28},{26,30},{28,20... | collective-permute-start | bytes 1990664 | tf_op jit(solution)/shard_map/ppermute | solution.py:370
  84.9 41.4 %collective-permute-start.16 = (bf16[72,4608]{1,0:T(8,128)(2,1)}, bf16[72,4608]{1,0:T(8,128)(2,1)S(1)}, u32[]{:S(2)}, u32[]{:S(2)}) collective-permute-start(bf16[72,4608]{1,0:T(8,128)(2,1)} %collective-permute-done.11), channel_id=1, source_target_pairs={{0,4},{2,6},{8,0},{10,2},{16,8},{18,10},{24,16},{26,18},{28,24},{3... | collective-permute-start | bytes 1990664 | tf_op jit(solution)/shard_map/ppermute | solution.py:370
  93.6 7.7 %collective-permute-start.4 = (f32[128,144]{0,1:T(8,128)S(1)}, f32[128,144]{0,1:T(8,128)S(1)}, u32[]{:S(2)}, u32[]{:S(2)}) collective-permute-start(f32[128,144]{0,1:T(8,128)S(1)} %pad_maximum_fusion.5), channel_id=1, source_target_pairs={{0,1},{1,0},{2,3},{3,2},{4,5},{5,4},{6,7},{7,6},{8,9},{9,8},{10,11... | collective-permute-start | bytes 221192 | tf_op jit(solution)/shard_map/ppermute | solution.py:356
  101.3 5.7 %collective-permute-start.9 = (f32[128,288]{0,1:T(8,128)S(1)}, f32[128,288]{0,1:T(8,128)S(1)}, u32[]{:S(2)}, u32[]{:S(2)}) collective-permute-start(f32[128,288]{0,1:T(8,128)S(1)} %pad_maximum_fusion.2), channel_id=1, source_target_pairs={{0,1},{1,0},{2,3},{3,2},{4,5},{5,4},{6,7},{7,6},{8,9},{9,8},{10,11... | collective-permute-start | bytes 442376 | tf_op jit(solution)/shard_map/ppermute | solution.py:356
  101.6 11.7 %copy-start.5 = (bf16[72,4608]{1,0:T(8,128)(2,1)S(1)}, bf16[72,4608]{1,0:T(8,128)(2,1)}, u32[]{:S(2)}) copy-start(bf16[72,4608]{1,0:T(8,128)(2,1)} %reshape.54) | copy-start | bytes 1990660
  106.9 4.7 %collective-permute-start.14 = (f32[128,288]{0,1:T(8,128)S(1)}, f32[128,288]{0,1:T(8,128)S(1)}, u32[]{:S(2)}, u32[]{:S(2)}) collective-permute-start(f32[128,288]{0,1:T(8,128)S(1)} %pad_maximum_fusion.3), channel_id=1, source_target_pairs={{0,1},{1,0},{2,3},{3,2},{4,5},{5,4},{6,7},{7,6},{8,9},{9,8},{10,11... | collective-permute-start | bytes 442376 | tf_op jit(solution)/shard_map/ppermute | solution.py:356
  127.9 4.1 %collective-permute-start.19 = (f32[128,288]{0,1:T(8,128)S(1)}, f32[128,288]{0,1:T(8,128)S(1)}, u32[]{:S(2)}, u32[]{:S(2)}) collective-permute-start(f32[128,288]{0,1:T(8,128)S(1)} %pad_maximum_fusion.4), channel_id=1, source_target_pairs={{0,1},{1,0},{2,3},{3,2},{4,5},{5,4},{6,7},{7,6},{8,9},{9,8},{10,11... | collective-permute-start | bytes 442376 | tf_op jit(solution)/shard_map/ppermute | solution.py:356
  129.8 13.0 %collective-permute-start.21 = (bf16[72,4096]{1,0:T(8,128)(2,1)S(1)}, bf16[72,4096]{1,0:T(8,128)(2,1)S(1)}, u32[]{:S(2)}, u32[]{:S(2)}) collective-permute-start(bf16[72,4096]{1,0:T(8,128)(2,1)S(1)} %collective-permute-done.18), channel_id=1, source_target_pairs={{0,4},{2,6},{8,0},{10,2},{16,8},{18,10},{24,16},{26,18},{28,24},{3... | collective-permute-start | bytes 1769480 | tf_op jit(solution)/shard_map/ppermute | solution.py:373
  130.3 13.7 %collective-permute-start.20 = (bf16[72,4608]{1,0:T(8,128)(2,1)S(1)}, bf16[72,4608]{1,0:T(8,128)(2,1)S(1)}, u32[]{:S(2)}, u32[]{:S(2)}) collective-permute-start(bf16[72,4608]{1,0:T(8,128)(2,1)S(1)} %collective-permute-done.15), channel_id=1, source_target_pairs={{0,8},{2,10},{8,16},{10,18},{16,24},{18,26},{24,28},{26,30},{28,20... | collective-permute-start | bytes 1990664 | tf_op jit(solution)/shard_map/ppermute | solution.py:372
  145.6 3.3 %collective-permute-start.22 = (f32[128,144]{0,1:T(8,128)S(1)}, f32[128,144]{0,1:T(8,128)S(1)}, u32[]{:S(2)}, u32[]{:S(2)}) collective-permute-start(f32[128,144]{0,1:T(8,128)S(1)} %pad_maximum_fusion.6), channel_id=1, source_target_pairs={{0,1},{1,0},{2,3},{3,2},{4,5},{5,4},{6,7},{7,6},{8,9},{9,8},{10,11... | collective-permute-start | bytes 221192 | tf_op jit(solution)/shard_map/ppermute | solution.py:356
  149.4 7.2 %collective-permute-start.23 = (f32[64,4096]{1,0:T(8,128)S(1)}, f32[64,4096]{1,0:T(8,128)S(1)}, u32[]{:S(2)}, u32[]{:S(2)}) collective-permute-start(f32[64,4096]{1,0:T(8,128)S(1)} %slice.27), channel_id=1, source_target_pairs={{0,2},{2,0},{4,6},{6,4},{8,10},{10,8},{12,14},{14,12},{16,18},{18,... | collective-permute-start | bytes 3145736 | tf_op jit(solution)/shard_map/ppermute | solution.py:349
  156.0 8.8 %collective-permute-start.24 = (f32[64,4608]{1,0:T(8,128)}, f32[64,4608]{1,0:T(8,128)}, u32[]{:S(2)}, u32[]{:S(2)}) collective-permute-start(f32[64,4608]{1,0:T(8,128)} %get-tuple-element.22), channel_id=1, source_target_pairs={{0,2},{2,0},{4,6},{6,4},{8,10},{10,8},{12,14},{14,12},{16,18},{18,... | collective-permute-start | bytes 3538952 | tf_op jit(solution)/shard_map/ppermute | solution.py:349
  159.5 29.4 %all-to-all-start.1 = ((bf16[16,4,4096]{2,1,0:T(4,128)(2,1)}), bf16[16,4,4096]{2,1,0:T(4,128)(2,1)}, u32[]{:S(2)}, u32[]{:S(2)}) async-start(bf16[16,4,4096]{2,1,0:T(4,128)(2,1)} %all_to_all.19), calls=%async_computation.1 | async-start | bytes 1048576 | tf_op jit(solution)/shard_map/all_to_all | solution.py:455
  164.8 18.1 %copy-start.2 = (bf16[9,576,48]{2,1,0:T(8,128)(2,1)S(1)}, bf16[9,576,48]{2,1,0:T(8,128)(2,1)}, u32[]{:S(2)}) copy-start(bf16[9,576,48]{2,1,0:T(8,128)(2,1)} %copy.18.group_ref) | copy-start | bytes 1492996
  167.7 11.7 %collective-permute-start.25 = (bf16[256,576]{1,0:T(8,128)(2,1)S(1)}, bf16[256,576]{1,0:T(8,128)(2,1)S(1)}, u32[]{:S(2)}, u32[]{:S(2)}) collective-permute-start(bf16[256,576]{1,0:T(8,128)(2,1)S(1)} %get-tuple-element.16), channel_id=1, source_target_pairs={{2,0},{4,2},{6,4},{8,6},{10,8},{12,10},{14,12},{16,14},{18,16},{20... | collective-permute-start | bytes 884744 | tf_op jit(solution)/shard_map/ppermute | solution.py:332
  180.4 2.5 %collective-permute-start.26 = (f32[2,288]{1,0:T(2,128)S(1)}, f32[2,288]{1,0:T(2,128)S(1)}, u32[]{:S(2)}, u32[]{:S(2)}) collective-permute-start(f32[2,288]{1,0:T(2,128)S(1)} %shard_map.108), channel_id=1, source_target_pairs={{0,1},{1,0},{2,3},{3,2},{4,5},{5,4},{6,7},{7,6},{8,9},{9,8},{10,11... | collective-permute-start | bytes 6920 | tf_op jit(solution)/shard_map/ppermute | solution.py:356
where the time goes:
time: 195 us; the launch traced here: 191 us
  waiting for transfers between devices  65.9 us (34%)
  starting transfers between devices  46.5 us (24%)
  matrix products  38.4 us (20%)
  local copies, waits for them, and re-layouts  18.2 us (9%)
  Pallas kernels  15 us (8%)
  other arithmetic  4.48 us (2%)
  between operations  2.43 us (1%)
    dot_general x16, matrix products, contract_last(): lax.dot_general(left, right, (((1,), (1,)), ((), ())), preferred_element_...  21.9 us
    ppermute x3, waiting for transfers between devices, ring_gather(): lax.ppermute(down_r, 'ctx', backward)  16.8 us
    ppermute x7, waiting for transfers between devices, sum_tp(): lax.ppermute(value, 'tp', [(i, i ^ reach) for i in range(size)])  14.3 us
    ppermute x3, waiting for transfers between devices, ring_gather(): lax.ppermute(up_s, 'ctx', onward)  10 us
    ppermute x2, waiting for transfers between devices, shifted(): return lax.ppermute(value, axis, pairs)  9.46 us
    ppermute x1, waiting for transfers between devices, ring_gather(): down_r = lax.ppermute(down_r, 'ctx', backward)  9.22 us
    dot_general x8, matrix products, per_device(): both_grads += jnp.dot(piece, part, preferred_element_type=jnp.float32)  8.42 us
    dot_general x8, matrix products, per_device(): both_tokens += jnp.dot(piece, part, preferred_element_type=jnp.float32)  8.04 us
  transfers between devices with their start and end apart: 29, of which 15 were waited for; matrix products, arithmetic and copies ran while one was open for 23% of the time, Pallas kernels for 5%

commit v1 on v0

--- a/solution.py
+++ b/solution.py
@@ -1,3 +1,5 @@
+import functools
+
 import jax
 import jax.numpy as jnp
 from jax import lax
@@ -12,15 +14,32 @@
 EDGE = 8
 LANES = 128
 VMEM_BYTES = 40 * 2**20
-
-
-def whole_call(kernel, outs, scratch, flops, moved):
+FREE = pl.CostEstimate(flops=0, bytes_accessed=0, transcendentals=0)
+
+
+def whole_call(kernel, outs, scratch, cost=FREE):
     return pl.pallas_call(
         kernel,
         out_shape=outs,
         scratch_shapes=scratch,
         compiler_params=pltpu.CompilerParams(vmem_limit_bytes=VMEM_BYTES),
-        cost_estimate=pl.CostEstimate(flops=flops, bytes_accessed=moved, transcendentals=0),
+        cost_estimate=cost,
+    )
+
+
+def contract_last(left, right):
+    return lax.dot_general(
+        left, right, (((1,), (1,)), ((), ())), preferred_element_type=jnp.float32
+    )
+
+
+def contract_exact(left, right):
+    return lax.dot_general(
+        left,
+        right,
+        (((1,), (1,)), ((), ())),
+        precision=lax.Precision.HIGHEST,
+        preferred_element_type=jnp.float32,
     )
 
 
@@ -48,14 +67,14 @@
 def block_tools(block, width):
     low, high, start, end = block
     size = end - start
-    out_lane = lax.broadcasted_iota(jnp.int32, (width, size), 1) + start
-    within = lax.broadcasted_iota(jnp.int32, (width, size), 0)
+    out_row = lax.broadcasted_iota(jnp.int32, (size, width), 0) + start
+    within = lax.broadcasted_iota(jnp.int32, (size, width), 1)
     lane = lax.broadcasted_iota(jnp.int32, (size, size), 1) + start
     row = lax.broadcasted_iota(jnp.int32, (size, size), 0) + start
-    spread = jnp.zeros((width, size), jnp.float32)
+    spread = jnp.zeros((size, width), jnp.float32)
     same = jnp.zeros((size, size), jnp.float32)
     for first in range(low, high, width):
-        spread += (out_lane == within + first).astype(jnp.float32)
+        spread += (out_row == within + first).astype(jnp.float32)
         in_lane = (lane >= first) & (lane < first + width)
         in_row = (row >= first) & (row < first + width)
         same += (in_lane & in_row).astype(jnp.float32)
@@ -64,7 +83,7 @@
 
 def dense_tap(group_ref, tap, block, spread, same):
     _, _, start, end = block
-    full = jnp.dot(group_ref[tap, start:end, :], spread, preferred_element_type=jnp.float32)
+    full = jnp.dot(spread, group_ref[tap, :, start:end], preferred_element_type=jnp.float32)
     return (full * same).astype(jnp.bfloat16)
 
 
@@ -77,7 +96,7 @@
 
 def conv_kernel(feat_ref, group_ref, squeeze_ref, conv_ref, pad_ref, sq_ref, flat_ref, wide_ref, shift_ref):
     frames, _, chans = feat_ref.shape
-    width = group_ref.shape[2]
+    width = group_ref.shape[1]
     rows = frames * FRAME_ROWS
     wide_ref[...] = jnp.zeros_like(wide_ref)
     for frame in range(frames):
@@ -97,7 +116,7 @@
             down, across = divmod(tap, 3)
             weights = dense_tap(group_ref, tap, block, spread, same)
             source = shift_ref[across, down * WIDE : down * WIDE + body, start:end]
-            total += jnp.dot(source, weights, preferred_element_type=jnp.float32)
+            total += contract_last(source, weights)
         conv_ref[WIDE : WIDE + body, start:end] += total
     conv = conv_ref[...] * inside(rows)
     conv_ref[...] = conv
@@ -109,9 +128,7 @@
         ],
         axis=0,
     ) * (1.0 / (SIDE * SIDE))
-    sq_ref[...] = jnp.dot(
-        pooled, squeeze_ref[...].astype(jnp.float32), precision=lax.Precision.HIGHEST
-    )
+    sq_ref[...] = contract_exact(pooled, squeeze_ref[...].astype(jnp.float32))
 
 
 def hidden_kernel(conv_ref, pad_ref, sq_ref, expand_ref, even_ref, odd_ref, excite_ref):
@@ -178,13 +195,7 @@
         sums.append(jnp.sum(grad_ref[...].astype(jnp.float32) * active, axis=0, keepdims=True))
     excite = excite_ref[...]
     inner = jnp.concatenate(sums, axis=0) * excite * (1.0 - excite)
-    out_ref[...] = lax.dot_general(
-        inner,
-        expand_ref[...].astype(jnp.float32),
-        (((1,), (1,)), ((), ())),
-        precision=lax.Precision.HIGHEST,
-        preferred_element_type=jnp.float32,
-    )
+    out_ref[...] = contract_exact(inner, expand_ref[...].astype(jnp.float32))
 
 
 def conv_grad_kernel(
@@ -192,15 +203,11 @@
     out_ref, flat_ref, wide_ref, shift_ref, grad_ref,
 ):
     frames, _, chans = out_ref.shape
-    width = group_ref.shape[2]
+    width = group_ref.shape[1]
     rows = frames * FRAME_ROWS
     grad_squeezed = relaxed_ref[...] * silu_slope(sq_ref[...])
-    pooled = lax.dot_general(
-        grad_squeezed,
-        squeeze_ref[...].astype(jnp.float32),
-        (((1,), (1,)), ((), ())),
-        precision=lax.Precision.HIGHEST,
-        preferred_element_type=jnp.float32,
+    pooled = jnp.dot(
+        grad_squeezed, squeeze_ref[...].astype(jnp.float32), precision=lax.Precision.HIGHEST
     ) * (1.0 / (SIDE * SIDE))
     wide_ref[0:EDGE, :] = jnp.zeros((EDGE, chans), jnp.float32)
     wide_ref[EDGE + rows :, :] = jnp.zeros((EDGE, chans), jnp.float32)
@@ -223,9 +230,7 @@
             weights = dense_tap(group_ref, tap, block, spread, same)
             at = (2 - down) * WIDE
             source = shift_ref[across, at : at + body, start:end]
-            total += lax.dot_general(
-                source, weights, (((1,), (1,)), ((), ())), preferred_element_type=jnp.float32
-            )
+            total += jnp.dot(source, weights, preferred_element_type=jnp.float32)
         grad_ref[WIDE : WIDE + body, start:end] += total
     for frame in range(frames):
         for y in range(SIDE):
@@ -247,14 +252,12 @@
     rows = frames * FRAME_ROWS
     return whole_call(
         conv_kernel,
-        (f32(rows, chans), bf16(rows, chans), f32(frames, squeeze_in.shape[1])),
+        (f32(rows, chans), bf16(rows, chans), f32(frames, squeeze_in.shape[0])),
         [
             pltpu.VMEM((cells, chans), jnp.float32),
             pltpu.VMEM((rows + 2 * EDGE, chans), jnp.float32),
             pltpu.VMEM((3, rows, chans), jnp.bfloat16),
         ],
-        rows * chans * 256 * 18 * 2,
-        rows * chans * 8 + 9 * chans * 256,
     )(features, group_kernel, squeeze_in)
 
 
@@ -264,8 +267,6 @@
         hidden_kernel,
         (bf16(FRAME_ROWS, chans), bf16(FRAME_ROWS, chans), f32(rows // FRAME_ROWS, chans)),
         [],
-        rows * chans * 10,
-        rows * chans * 8,
     )(conv, padded, squeezed, squeeze_out)
 
 
@@ -280,9 +281,7 @@
         out_shape=bf16(OUT_SIDE * OUT_SIDE, 8 * chans),
         in_specs=vmem_specs(2),
         compiler_params=pltpu.CompilerParams(vmem_limit_bytes=VMEM_BYTES),
-        cost_estimate=pl.CostEstimate(
-            flops=8 * FRAME_ROWS * chans, bytes_accessed=8 * FRAME_ROWS * chans, transcendentals=0
-        ),
+        cost_estimate=FREE,
     )(mask, halo, even)
 
 
@@ -292,9 +291,7 @@
         out_shape=(bf16(FRAME_ROWS, chans), f32(FRAME_ROWS, chans)),
         in_specs=vmem_specs(2),
         compiler_params=pltpu.CompilerParams(vmem_limit_bytes=VMEM_BYTES),
-        cost_estimate=pl.CostEstimate(
-            flops=8 * FRAME_ROWS * chans, bytes_accessed=24 * FRAME_ROWS * chans, transcendentals=0
-        ),
+        cost_estimate=FREE,
     )(mask, own, mate)
 
 
@@ -304,8 +301,6 @@
         excite_grad_kernel,
         f32(rows // FRAME_ROWS, squeeze_out.shape[0]),
         [],
-        rows * chans * 10,
-        rows * chans * 7,
     )(even, odd, conv, excite, squeeze_out)
 
 
@@ -321,8 +316,7 @@
             pltpu.VMEM((3, rows, chans), jnp.bfloat16),
             pltpu.VMEM((rows, chans), jnp.float32),
         ],
-        rows * chans * 256 * 18 * 2,
-        rows * chans * 10 + 9 * chans * 256,
+        pl.CostEstimate(flops=rows * chans * 9216, bytes_accessed=16 * rows * chans, transcendentals=0),
     )(even, odd, conv, excite, squeezed, grad_relaxed, squeeze_in, group_kernel)
 
 
@@ -349,36 +343,72 @@
     return lax.ppermute(value, "ctx", [(i, i ^ 1) for i in range(lax.axis_size("ctx"))])
 
 
+def tp_terms(value):
+    size = lax.axis_size("tp")
+    reach, other = 1, None
+    while reach < size:
+        value = value if other is None else value + other
+        other = lax.ppermute(value, "tp", [(i, i ^ reach) for i in range(size)])
+        reach *= 2
+    return value, jnp.zeros_like(value) if other is None else other
+
+
 def sum_tp(value):
-    size = lax.axis_size("tp")
-    reach = 1
-    while reach < size:
-        value = value + lax.ppermute(value, "tp", [(i, i ^ reach) for i in range(size)])
-        reach *= 2
-    return value
-
-
-def ring_gather(samplers, readouts):
+    value, other = tp_terms(value)
+    return value + other
+
+
+def ring_step(blocks):
     count = lax.axis_size("ctx")
-    chips = count // 2
     onward, backward = ring_pairs(count, 1), ring_pairs(count, -1)
-    groups = [([samplers], [readouts])]
-    up_s = down_s = samplers
-    up_r = down_r = readouts
-    for step in range(1, chips // 2):
-        up_r, down_r = lax.ppermute(up_r, "ctx", onward), lax.ppermute(down_r, "ctx", backward)
-        up_s, down_s = lax.ppermute(up_s, "ctx", onward), lax.ppermute(down_s, "ctx", backward)
-        groups.append(([up_s, down_s], [up_r, down_r]))
-    up_s = lax.ppermute(up_s, "ctx", onward)
-    down_r = lax.ppermute(down_r, "ctx", backward)
-    groups.append(([up_s], [down_r]))
-    return groups
-
-
-def contract_last(left, right):
-    return lax.dot_general(
-        left, right, (((1,), (1,)), ((), ())), preferred_element_type=jnp.float32
-    )
+    up_s, up_r, down_s, down_r = blocks
+    send = lambda value, pairs: None if value is None else lax.ppermute(value, "ctx", pairs)
+    up_r, down_r = send(up_r, onward), send(down_r, backward)
+    up_s, down_s = send(up_s, onward), send(down_s, backward)
+    return up_s, up_r, down_s, down_r
+
+
+def tie(*values):
+    return lax.optimization_barrier(values)
+
+
+def sums_kernel(count, *refs):
+    patch_ref, back_ref, *blocks, out_ref = refs
+    products = [contract_last(patch_ref[...], ref[...]) for ref in blocks[:count]]
+    products += [contract_last(back_ref[...], ref[...]) for ref in blocks[count:]]
+    out_ref[...] = jnp.concatenate(products, axis=1)
+
+
+def totals_kernel(count, backward, first, *refs):
+    sums = refs[0][...] + refs[1][...]
+    blocks, refs = refs[2 : 2 + count], refs[2 + count :]
+    before, after = refs[:-2], refs[-2:]
+    depth = sums.shape[1] // 2
+    pre, grad_act = sums[:, :depth], sums[:, depth:]
+    factor = grad_act * silu_slope(pre) if backward else pre * jax.nn.sigmoid(pre)
+    factor = factor.astype(jnp.bfloat16)
+    width = depth // count
+    total = 0.0
+    for place, ref in enumerate(blocks):
+        piece = factor[:, place * width : (place + 1) * width]
+        total += jnp.dot(piece, ref[...], preferred_element_type=jnp.float32)
+    rows = after[0].shape[0]
+    for half, ref in enumerate(after):
+        value = total[half * rows : (half + 1) * rows]
+        ref[...] = value if first else before[half][...] + value
+
+
+def partial_sums(patches, back, samplers, readouts):
+    count, width = len(samplers), samplers[0].shape[0]
+    return whole_call(
+        functools.partial(sums_kernel, count), f32(patches.shape[0], 2 * count * width), []
+    )(patches, back, *samplers, *readouts)
+
+
+def add_products(sums, blocks, before, backward):
+    rows, columns = sums[0].shape[0] // 2, blocks[0].shape[1]
+    kernel = functools.partial(totals_kernel, len(blocks), backward, not before)
+    return whole_call(kernel, (f32(rows, columns),) * 2, [])(*sums, *blocks, *before)
 
 
 def per_device(
@@ -396,7 +426,9 @@
     frames_dev, cells, chans = features.shape
     pairs_dev = frames_dev // 2
     flat_sampler = sampler_kernel.reshape(sampler_kernel.shape[0], 8 * chans)
-    groups = ring_gather(flat_sampler, readout_kernel)
+    blocks = ring_step((flat_sampler, readout_kernel) * 2)
+    group_kernel = jnp.swapaxes(group_kernel, 1, 2)
+    squeeze_in = squeeze_in.T
 
     local_clip = lax.dynamic_slice_in_dim(frame_clip, shard_index * frames_dev, frames_dev)
     edge_clip = lax.dynamic_slice_in_dim(
@@ -422,7 +454,6 @@
         lax.all_to_all(token_cotangent, "ctx", split_axis=0, concat_axis=0, tiled=True)
         * live[:, None]
     )
-    rows = back.shape[0]
     both_back = jnp.concatenate([back, swap_cores(back)], axis=0)
 
     conv, padded, squeezed = conv_forward(features, group_kernel, squeeze_in)
@@ -431,28 +462,37 @@
     patches = take_patches(mask, shifted(odd, "ctx", 1), even)
     both_patches = jnp.concatenate([patches, swap_cores(patches)], axis=0)
 
-    both_tokens = both_grads = 0.0
-    for group_s, group_r in groups:
-        partial = jnp.concatenate(
-            [contract_last(both_patches, part) for part in group_s]
-            + [contract_last(both_back, part) for part in group_r],
-            axis=1,
-        )
-        pre, grad_act = jnp.split(sum_tp(partial), 2, axis=1)
-        act = jax.nn.silu(pre).astype(jnp.bfloat16)
-        grad_pre = (grad_act * silu_slope(pre)).astype(jnp.bfloat16)
-        for piece, part in zip(jnp.split(act, len(group_r), axis=1), group_r):
-            both_tokens += jnp.dot(piece, part, preferred_element_type=jnp.float32)
-        for piece, part in zip(jnp.split(grad_pre, len(group_s), axis=1), group_s):
-            both_grads += jnp.dot(piece, part, preferred_element_type=jnp.float32)
-    lead, grad_even = return_patches(mask, both_grads[:rows], swap_cores(both_grads[rows:]), chans)
+    steps = lax.axis_size("ctx") // 4
+    samplers, readouts = [flat_sampler], [readout_kernel]
+    tokens = grads = ()
+    for step in range(1, steps + 1):
+        here = blocks
+        if step < steps:
+            samplers, readouts = samplers + [here[0], here[2]], readouts + [here[1], here[3]]
+            if step == 1:
+                *here, even = tie(*here, even)
+            elif step > 2:
+                *here, token_own, token_mate, grad_own, grad_mate = tie(*here, *tokens, *grads)
+                tokens, grads = (token_own, token_mate), (grad_own, grad_mate)
+            if step == steps - 1:
+                here = here[0], None, None, here[3]
+            blocks = ring_step(here)
+        else:
+            samplers, readouts = samplers + [here[0]], readouts + [here[3]]
+        sums = tp_terms(partial_sums(both_patches, both_back, samplers, readouts))
+        tokens = add_products(sums, readouts, tokens, False)
+        grads = add_products(sums, samplers, grads, True)
+        samplers, readouts = [], []
+    lead, grad_even = return_patches(mask, grads[0], swap_cores(grads[1]), chans)
+    token_own, token_mate, lead = tie(*tokens, lead)
     grad_odd = shifted(lead, "ctx", -1)
     grad_relaxed = sum_tp(excite_grad(grad_even, grad_odd, conv, excite, squeeze_out))
+    tokens = (token_own + swap_cores(token_mate)).astype(jnp.bfloat16) * live[:, None]
+    tokens, grad_relaxed = tie(tokens, grad_relaxed)
+    llm_tokens = lax.all_to_all(tokens, "ctx", split_axis=0, concat_axis=0, tiled=True)
     grad_features = conv_backward(
         grad_even, grad_odd, conv, excite, squeezed, grad_relaxed, squeeze_in, group_kernel
     )
-    tokens = (both_tokens[:rows] + swap_cores(both_tokens[rows:])).astype(jnp.bfloat16) * live[:, None]
-    llm_tokens = lax.all_to_all(tokens, "ctx", split_axis=0, concat_axis=0, tiled=True)
     return (llm_tokens, grad_features)
 
 

time: 195 us -> 181 us (0.928); the launches traced: 191 us -> 179 us
  matrix products: 38.4 us -> 0 us
  Pallas kernels: 15 us -> 32.5 us
  waiting for transfers between devices: 65.9 us -> 79.1 us
  starting transfers between devices: 46.5 us -> 43.5 us
  local copies, waits for them, and re-layouts: 18.2 us -> 16.1 us
    dot_general x32 -> x0, matrix products: 38.4 us -> none  [the longest x16 21.9 us: contract_last(): lax.dot_general(left, right, (((1,), (1,)), ((), ())), preferred_element_...]
    pallas_call x0 -> x12, Pallas kernels: none -> 18.3 us  [the longest x8 10.2 us: add_products(): whole_call(kernel, (f32(rows, columns),) * 2, [])(*sums, *blocks, *before)]
    ppermute x2, waiting for transfers between devices: 9.46 us -> 23.1 us  [shifted(): return lax.ppermute(value, axis, pairs)]
    all_to_all x1, waiting for transfers between devices: 0.01 us -> 7.07 us  [per_device(): lax.all_to_all(tokens, 'ctx', split_axis=0, concat_axis=0, tiled=True)]
    all_to_all x1, waiting for transfers between devices: 4.64 us -> 0.01 us  [per_device(): lax.all_to_all(token_cotangent, 'ctx', split_axis=0, concat_axis=0, tiled...]
    ppermute x21 -> x20, waiting for transfers between devices: 51.2 us -> 47.6 us  [the longest x14 42.4 us: ring_step(): lax.ppermute(value, 'ctx', pairs)]
    ppermute x21 -> x20, starting transfers between devices: 22 us -> 19.1 us  [the longest x14 11.4 us: ring_step(): lax.ppermute(value, 'ctx', pairs)]
    unnamed x26 -> x38, local copies, waits for them, and re-layouts: 6.96 us -> 6.72 us
  transfers between devices with their start and end apart: 29 -> 28, of which waited for: 15 -> 13; matrix products, arithmetic and copies ran while one was open for 23% -> 4% of each run, Pallas kernels for 5% -> 17%
where the time goes in v1:
time: 181 us; the launch traced here: 179 us
  waiting for transfers between devices  79.1 us (44%)
  starting transfers between devices  43.5 us (24%)
  Pallas kernels  32.5 us (18%)
  local copies, waits for them, and re-layouts  16.1 us (9%)
  other arithmetic  5.57 us (3%)
  between operations  2.24 us (1%)
    ppermute x14, waiting for transfers between devices, ring_step(): lax.ppermute(value, 'ctx', pairs)  42.4 us
    ppermute x2, waiting for transfers between devices, shifted(): return lax.ppermute(value, axis, pairs)  23.1 us
    ppermute x14, starting transfers between devices, ring_step(): lax.ppermute(value, 'ctx', pairs)  11.4 us
    pallas_call x8, Pallas kernels, add_products(): whole_call(kernel, (f32(rows, columns),) * 2, [])(*sums, *blocks, *before)  10.2 us
    pallas_call x4, Pallas kernels, partial_sums(): whole_call(functools.partial(sums_kernel, count), f32(patches.shape[0], 2...  8.16 us
    ppermute x6, starting transfers between devices, tp_terms(): other = lax.ppermute(value, 'tp', [(i, i ^ reach) for i in range(size)])  7.68 us
    ppermute x2, starting transfers between devices, shifted(): return lax.ppermute(value, axis, pairs)  7.23 us
    all_to_all x1, waiting for transfers between devices, per_device(): lax.all_to_all(tokens, 'ctx', split_axis=0, concat_axis=0, tiled=True)  7.07 us
  transfers between devices with their start and end apart: 28, of which 13 were waited for; matrix products, arithmetic and copies ran while one was open for 4% of the time, Pallas kernels for 17%

profile of v1, /device:TPU:3, one launch (start us, length us, event | category | flops | bytes accessed | tf_op | source)
XLA Modules:
  0.0 178.9 jit_solution(15000341390973622314)
XLA Ops:
  0.6 2.1 %all_to_all.16 = bf16[16,4,4096]{2,1,0:T(4,128)(2,1)} reshape(bf16[64,4096]{1,0:T(8,128)(2,1)} %param.17) | data formatting | bytes 1048576 | tf_op jit(solution)/shard_map/all_to_all | solution.py:454
  2.7 6.8 %all-to-all-start = ((bf16[16,4,4096]{2,1,0:T(4,128)(2,1)}), bf16[16,4,4096]{2,1,0:T(4,128)(2,1)}, u32[]{:S(2)}, u32[]{:S(2)}) async-start(bf16[16,4,4096]{2,1,0:T(4,128)(2,1)} %all_to_all.16), calls=%async_computation | async-start | bytes 1048576 | tf_op jit(solution)/shard_map/all_to_all | solution.py:454
  10.2 1.4 collective-permute-start.6
  11.7 1.4 collective-permute-start.7
  13.1 1.0 copy-done.10
  14.1 4.5 %shard_map.104 = (f32[512,576]{1,0:T(8,128)S(1)}, bf16[512,576]{1,0:T(8,128)(2,1)S(1)}, f32[2,288]{1,0:T(2,128)S(1)}) custom-call(bf16[2,196,576]{2,1,0:T(8,128)(2,1)S(1)} %copy.13.feat_ref, bf16[9,48,576]{2,1,0:T(8,128)(2,1)S(1)} %bitcast.6, bf16[288,576]{1,0:T(8,128)(2,1)S(1)} %bitcast.8), custom_call_target="tpu_custom_call" | custom-call | tf_op jit(solution)/shard_map/pallas_call | solution.py:253
  18.6 0.9 copy-done.6
  19.5 1.2 collective-permute-start
  22.3 1.1 copy-done.7
  23.4 1.5 shard_map.105
  24.9 0.7 copy-done.12
  25.6 5.2 %collective-permute-start.1 = (bf16[256,576]{1,0:T(8,128)(2,1)}, bf16[256,576]{1,0:T(8,128)(2,1)S(1)}, u32[]{:S(2)}, u32[]{:S(2)}) collective-permute-start(bf16[256,576]{1,0:T(8,128)(2,1)} %get-tuple-element.44), channel_id=1, source_target_pairs={{0,2},{2,4},{4,6},{6,8},{8,10},{10,12},{12,14},{14,16},{16,18},{18... | collective-permute-start | bytes 884744 | tf_op jit(solution)/shard_map/ppermute | solution.py:326
  30.8 0.7 fusion.1
  32.1 0.7 fusion.2
  33.3 15.9 %collective-permute-done.1.halo_ref = bf16[256,576]{1,0:T(8,128)(2,1)S(1)} collective-permute-done((bf16[256,576]{1,0:T(8,128)(2,1)}, bf16[256,576]{1,0:T(8,128)(2,1)S(1)}, u32[]{:S(2)}, u32[]{:S(2)}) %collective-permute-start.1) | collective-permute-done | bytes 294944 | tf_op jit(solution)/shard_map/ppermute | solution.py:326
  49.2 1.0 copy-done.13
  50.2 1.3 shard_map.106
  51.5 0.8 copy-done.2
  52.3 3.7 %collective-permute-start.10 = (bf16[72,4096]{1,0:T(8,128)(2,1)}, bf16[72,4096]{1,0:T(8,128)(2,1)}, u32[]{:S(2)}, u32[]{:S(2)}) collective-permute-start(bf16[72,4096]{1,0:T(8,128)(2,1)} %collective-permute-done.5.refs_6_.refs_3_), channel_id=1, source_target_pairs={{0,8},{2,10},{8,16},{10,18},{16,24},{18,26},{24,28},{26,30},{28,20... | collective-permute-start | bytes 1769480 | tf_op jit(solution)/shard_map/ppermute | solution.py:365
  56.3 1.4 collective-permute-start.14
  57.8 2.0 %all_to_all.18 = bf16[64,4096]{1,0:T(8,128)(2,1)} reshape(bf16[16,4,4096]{2,1,0:T(4,128)(2,1)} %all-to-all-done) | data formatting | bytes 1048576 | tf_op jit(solution)/shard_map/all_to_all | solution.py:454
  59.7 1.1 broadcast_multiply_fusion
  60.9 1.4 collective-permute-start.3
  62.3 1.3 pad_maximum_fusion.refs_0_
  63.6 20.4 %collective-permute-done.10.refs_4_.refs_2_ = bf16[72,4096]{1,0:T(8,128)(2,1)} collective-permute-done((bf16[72,4096]{1,0:T(8,128)(2,1)}, bf16[72,4096]{1,0:T(8,128)(2,1)}, u32[]{:S(2)}, u32[]{:S(2)}) %collective-permute-start.10) | collective-permute-done | bytes 589856 | tf_op jit(solution)/shard_map/ppermute | solution.py:365
  84.0 3.6 %collective-permute-done.14.refs_5_.refs_3_ = bf16[72,4096]{1,0:T(8,128)(2,1)} collective-permute-done((bf16[72,4096]{1,0:T(8,128)(2,1)}, bf16[72,4096]{1,0:T(8,128)(2,1)}, u32[]{:S(2)}, u32[]{:S(2)}) %collective-permute-start.14) | collective-permute-done | bytes 589856 | tf_op jit(solution)/shard_map/ppermute | solution.py:365
  87.6 1.5 collective-permute-start.9
  89.2 3.4 %shard_map.108.refs_0_ = f32[128,432]{1,0:T(8,128)S(1)} custom-call(bf16[128,4608]{1,0:T(8,128)(2,1)S(1)} %pad_maximum_fusion.refs_0_, bf16[128,4096]{1,0:T(8,128)(2,1)S(1)} %pad_maximum_fusion.1.refs_1_, bf16[72,4608]{1,0:T(8,128)(2,1)S(1)} %reshape.54.refs_2_, bf16[72,4608]{1,0:T(8,128)(2,1)} %collective-permute-done.4.refs_3_, ...), custom_call_target="tpu_custom_call" | custom-call | tf_op jit(solution)/shard_map/pallas_call | solution.py:403
  92.7 1.3 collective-permute-start.17
  94.0 2.6 %shard_map.107.refs_0_ = f32[128,288]{1,0:T(8,128)S(1)} custom-call(bf16[128,4608]{1,0:T(8,128)(2,1)S(1)} %pad_maximum_fusion.refs_0_, bf16[128,4096]{1,0:T(8,128)(2,1)S(1)} %pad_maximum_fusion.1.refs_1_, bf16[72,4608]{1,0:T(8,128)(2,1)S(1)} %collective-permute-done.8.refs_2_, bf16[72,4608]{1,0:T(8,128)(2,1)S(1)} %collective-permute-done.12.refs_3_, ...), custom_call_target="tpu_custom_call" | custom-call | tf_op jit(solution)/shard_map/pallas_call | solution.py:403
  96.6 2.3 %collective-permute-done.17.refs_1_ = f32[128,432]{1,0:T(8,128)S(1)} collective-permute-done((f32[128,432]{1,0:T(8,128)S(1)}, f32[128,432]{1,0:T(8,128)S(1)}, u32[]{:S(2)}, u32[]{:S(2)}) %collective-permute-start.17) | collective-permute-done | bytes 221216 | tf_op jit(solution)/shard_map/ppermute | solution.py:351
  98.8 1.3 collective-permute-start.16
  100.1 2.1 %shard_map.109 = (f32[64,4096]{1,0:T(8,128)S(1)}, f32[64,4096]{1,0:T(8,128)S(1)}) custom-call(f32[128,432]{1,0:T(8,128)S(1)} %shard_map.108.refs_0_, f32[128,432]{1,0:T(8,128)S(1)} %collective-permute-done.17.refs_1_, bf16[72,4096]{1,0:T(8,128)(2,1)S(1)} %copy-done.1, bf16[72,4096]{1,0:T(8,128)(2,1)} %collective-permute-done.5.refs_6_.refs_3_, ...), custom_call_target="tpu_custom_call" | custom-call | tf_op jit(solution)/shard_map/pallas_call | solution.py:411
  102.2 2.5 %shard_map.111 = (f32[64,4608]{1,0:T(8,128)S(1)}, f32[64,4608]{1,0:T(8,128)S(1)}) custom-call(f32[128,432]{1,0:T(8,128)S(1)} %shard_map.108.refs_0_, f32[128,432]{1,0:T(8,128)S(1)} %collective-permute-done.17.refs_1_, bf16[72,4608]{1,0:T(8,128)(2,1)S(1)} %reshape.54.refs_2_, bf16[72,4608]{1,0:T(8,128)(2,1)} %collective-permute-done.4.refs_3_, ...), custom_call_target="tpu_custom_call" | custom-call | tf_op jit(solution)/shard_map/pallas_call | solution.py:411
  104.7 2.0 %shard_map.110 = (f32[64,4096]{1,0:T(8,128)S(1)}, f32[64,4096]{1,0:T(8,128)S(1)}) custom-call(f32[128,288]{1,0:T(8,128)S(1)} %shard_map.107.refs_0_, f32[128,288]{1,0:T(8,128)S(1)} %collective-permute-done.16.refs_1_, bf16[72,4096]{1,0:T(8,128)(2,1)} %collective-permute-done.10.refs_4_.refs_2_, bf16[72,4096]{1,0:T(8,128)(2,1)} %collective-permute-done.14.refs_5_.refs_3_, ...), custom_call_target="tpu_custom_call" | custom-call | tf_op jit(solution)/shard_map/pallas_call | solution.py:411
  106.7 0.9 shard_map.112
  107.6 4.6 %collective-permute-done.9.refs_2_ = bf16[72,4608]{1,0:T(8,128)(2,1)S(1)} collective-permute-done((bf16[72,4608]{1,0:T(8,128)(2,1)S(1)}, bf16[72,4608]{1,0:T(8,128)(2,1)S(1)}, u32[]{:S(2)}, u32[]{:S(2)}) %collective-permute-start.9) | collective-permute-done | bytes 663584 | tf_op jit(solution)/shard_map/ppermute | solution.py:365
  112.2 3.5 %collective-permute-done.13.refs_3_ = bf16[72,4608]{1,0:T(8,128)(2,1)S(1)} collective-permute-done((bf16[72,4608]{1,0:T(8,128)(2,1)S(1)}, bf16[72,4608]{1,0:T(8,128)(2,1)S(1)}, u32[]{:S(2)}, u32[]{:S(2)}) %collective-permute-start.13) | collective-permute-done | bytes 663584 | tf_op jit(solution)/shard_map/ppermute | solution.py:365
  115.8 0.8 collective-permute-start.18
  116.6 0.6 collective-permute-start.19
  117.2 1.4 shard_map.114.refs_0_
  118.6 1.3 collective-permute-start.21
  119.9 8.9 %collective-permute-done.19.refs_3_.refs_2_ = bf16[72,4096]{1,0:T(8,128)(2,1)S(1)} collective-permute-done((bf16[72,4096]{1,0:T(8,128)(2,1)S(1)}, bf16[72,4096]{1,0:T(8,128)(2,1)S(1)}, u32[]{:S(2)}, u32[]{:S(2)}) %collective-permute-start.19) | collective-permute-done | bytes 589856 | tf_op jit(solution)/shard_map/ppermute | solution.py:365
  128.8 1.4 collective-permute-done.18.refs_2_
  130.2 0.8 shard_map.113.refs_0_
  131.0 1.3 collective-permute-start.20
  132.3 0.9 shard_map.117
  133.2 1.7 collective-permute-done.20.refs_1_
  135.4 4.2 %collective-permute-start.22 = (f32[64,4608]{1,0:T(8,128)S(1)}, f32[64,4608]{1,0:T(8,128)S(1)}, u32[]{:S(2)}, u32[]{:S(2)}) collective-permute-start(f32[64,4608]{1,0:T(8,128)S(1)} %get-tuple-element.71), channel_id=1, source_target_pairs={{0,2},{2,0},{4,6},{6,4},{8,10},{10,8},{12,14},{14,12},{16,18},{18,... | collective-permute-start | bytes 3538952 | tf_op jit(solution)/shard_map/ppermute | solution.py:343
  139.6 0.8 shard_map.115
  140.8 1.3 collective-permute-done.22.mate_ref
  142.1 1.6 shard_map.119
  144.1 2.0 %collective-permute-start.24 = (bf16[256,576]{1,0:T(8,128)(2,1)S(1)}, bf16[256,576]{1,0:T(8,128)(2,1)S(1)}, u32[]{:S(2)}, u32[]{:S(2)}) collective-permute-start(bf16[256,576]{1,0:T(8,128)(2,1)S(1)} %get-tuple-element.76), channel_id=1, source_target_pairs={{2,0},{4,2},{6,4},{8,6},{10,8},{12,10},{14,12},{16,14},{18,16},{20... | collective-permute-start | bytes 884744 | tf_op jit(solution)/shard_map/ppermute | solution.py:326
  146.1 7.2 %collective-permute-done.24.odd_ref = bf16[256,576]{1,0:T(8,128)(2,1)S(1)} collective-permute-done((bf16[256,576]{1,0:T(8,128)(2,1)S(1)}, bf16[256,576]{1,0:T(8,128)(2,1)S(1)}, u32[]{:S(2)}, u32[]{:S(2)}) %collective-permute-start.24) | collective-permute-done | bytes 294944 | tf_op jit(solution)/shard_map/ppermute | solution.py:326
  153.4 0.9 shard_map.120
  154.3 1.3 collective-permute-start.25
  155.6 1.2 collective-permute-done.25
  156.8 1.0 fusion
  157.8 2.1 %all_to_all.19 = bf16[16,4,4096]{2,1,0:T(4,128)(2,1)} reshape(bf16[64,4096]{1,0:T(8,128)(2,1)} %fusion) | data formatting | bytes 1048576 | tf_op jit(solution)/shard_map/all_to_all | solution.py:492
  159.9 4.4 %all-to-all-start.1 = ((bf16[16,4,4096]{2,1,0:T(4,128)(2,1)}), bf16[16,4,4096]{2,1,0:T(4,128)(2,1)}, u32[]{:S(2)}, u32[]{:S(2)}) async-start(bf16[16,4,4096]{2,1,0:T(4,128)(2,1)} %all_to_all.19), calls=%async_computation.1 | async-start | bytes 1048576 | tf_op jit(solution)/shard_map/all_to_all | solution.py:492
  164.3 4.4 %shard_map.121 = bf16[2,196,576]{2,1,0:T(8,128)(2,1)S(1)} custom-call(f32[256,576]{1,0:T(8,128)S(1)} %get-tuple-element.75.even_ref, bf16[256,576]{1,0:T(8,128)(2,1)S(1)} %collective-permute-done.24.odd_ref, f32[512,576]{1,0:T(8,128)S(1)} %get-tuple-element.41.conv_ref, f32[2,576]{1,0:T(2,128)S(1)} %get-tuple-element.77.excite_ref, ...), custom_call_target="tpu_custom_call" | custom-call | flops 2717908992 | bytes 4718592 | tf_op jit(solution)/shard_map/pallas_call | solution.py:310
  168.8 1.2 copy.14
  169.9 7.1 %all-to-all-done.1 = bf16[16,4,4096]{2,1,0:T(4,128)(2,1)} async-done(((bf16[16,4,4096]{2,1,0:T(4,128)(2,1)}), bf16[16,4,4096]{2,1,0:T(4,128)(2,1)}, u32[]{:S(2)}, u32[]{:S(2)}) %all-to-all-start.1) | async-done | bytes 524320 | tf_op jit(solution)/shard_map/all_to_all | solution.py:492
  177.0 2.0 %all_to_all.21 = bf16[64,4096]{1,0:T(8,128)(2,1)} reshape(bf16[16,4,4096]{2,1,0:T(4,128)(2,1)} %all-to-all-done.1) | data formatting | bytes 1048576 | tf_op jit(solution)/shard_map/all_to_all | solution.py:492
  (66 shorter events, 4.3 us)
Async XLA Ops:
  0.6 8.9 %copy-start.14 = (bf16[72,8,576]{2,1,0:T(8,128)(2,1)S(1)}, bf16[72,8,576]{2,1,0:T(8,128)(2,1)}, u32[]{:S(2)}) copy-start(bf16[72,8,576]{2,1,0:T(8,128)(2,1)} %param.13) | copy-start | bytes 1990660
  2.7 8.9 %copy-start = (bf16[72,4096]{1,0:T(8,128)(2,1)S(1)}, bf16[72,4096]{1,0:T(8,128)(2,1)}, u32[]{:S(2)}) copy-start(bf16[72,4096]{1,0:T(8,128)(2,1)} %refs_2_.1) | copy-start | bytes 1769476
  2.7 10.3 %copy-start.15 = (bf16[2,196,576]{2,0,1:T(2,128)(2,1)S(1)}, bf16[2,196,576]{2,0,1:T(2,128)(2,1)}, u32[]{:S(2)}) copy-start(bf16[2,196,576]{2,0,1:T(2,128)(2,1)} %param.9) | copy-start | bytes 1354756
  2.7 55.0 %all-to-all-start = ((bf16[16,4,4096]{2,1,0:T(4,128)(2,1)}), bf16[16,4,4096]{2,1,0:T(4,128)(2,1)}, u32[]{:S(2)}, u32[]{:S(2)}) async-start(bf16[16,4,4096]{2,1,0:T(4,128)(2,1)} %all_to_all.16), calls=%async_computation | async-start | bytes 1048576 | tf_op jit(solution)/shard_map/all_to_all | solution.py:454
  10.0 3.1 %copy-start.8 = (bf16[9,576,48]{1,2,0:T(8,128)(2,1)S(1)}, bf16[9,576,48]{1,2,0:T(8,128)(2,1)}, u32[]{:S(2)}) copy-start(bf16[9,576,48]{1,2,0:T(8,128)(2,1)} %param.10) | copy-start | bytes 1492996
  10.0 10.7 %copy-start.16 = (s32[32]{0:T(128)S(1)}, s32[32]{0:T(128)}, u32[]{:S(2)}) copy-start(s32[32]{0:T(128)} %param.15) | copy-start | bytes 388
  10.1 12.2 %copy-start.4 = (bf16[288,576]{1,0:T(8,128)(2,1)S(1)}, bf16[288,576]{1,0:T(8,128)(2,1)}, u32[]{:S(2)}) copy-start(bf16[288,576]{1,0:T(8,128)(2,1)} %expand_ref.3) | copy-start | bytes 995332
  10.1 41.4 %collective-permute-start.4 = (bf16[72,4608]{1,0:T(8,128)(2,1)S(1)}, bf16[72,4608]{1,0:T(8,128)(2,1)}, u32[]{:S(2)}, u32[]{:S(2)}) collective-permute-start(bf16[72,4608]{1,0:T(8,128)(2,1)S(1)} %reshape.54.refs_2_), channel_id=1, source_target_pairs={{0,8},{2,10},{8,16},{10,18},{16,24},{18,26},{24,28},{26,30},{28,20... | collective-permute-start | bytes 1990664 | tf_op jit(solution)/shard_map/ppermute | solution.py:365
  10.2 42.1 %collective-permute-start.6 = (bf16[72,4608]{1,0:T(8,128)(2,1)S(1)}, bf16[72,4608]{1,0:T(8,128)(2,1)}, u32[]{:S(2)}, u32[]{:S(2)}) collective-permute-start(bf16[72,4608]{1,0:T(8,128)(2,1)S(1)} %reshape.54.refs_2_), channel_id=1, source_target_pairs={{0,4},{2,6},{8,0},{10,2},{16,8},{18,10},{24,16},{26,18},{28,24},{3... | collective-permute-start | bytes 1990664 | tf_op jit(solution)/shard_map/ppermute | solution.py:365
  11.6 39.9 %collective-permute-start.5 = (bf16[72,4096]{1,0:T(8,128)(2,1)S(1)}, bf16[72,4096]{1,0:T(8,128)(2,1)}, u32[]{:S(2)}, u32[]{:S(2)}) collective-permute-start(bf16[72,4096]{1,0:T(8,128)(2,1)S(1)} %copy-done), channel_id=1, source_target_pairs={{0,8},{2,10},{8,16},{10,18},{16,24},{18,26},{24,28},{26,30},{28,20... | collective-permute-start | bytes 1769480 | tf_op jit(solution)/shard_map/ppermute | solution.py:365
  11.7 39.8 %collective-permute-start.7 = (bf16[72,4096]{1,0:T(8,128)(2,1)S(1)}, bf16[72,4096]{1,0:T(8,128)(2,1)S(1)}, u32[]{:S(2)}, u32[]{:S(2)}) collective-permute-start(bf16[72,4096]{1,0:T(8,128)(2,1)S(1)} %copy-done), channel_id=1, source_target_pairs={{0,4},{2,6},{8,0},{10,2},{16,8},{18,10},{24,16},{26,18},{28,24},{3... | collective-permute-start | bytes 1769480 | tf_op jit(solution)/shard_map/ppermute | solution.py:365
  13.1 1.0 copy-start.10
  18.6 0.9 copy-start.6
  19.5 2.8 %collective-permute-start = (f32[2,288]{1,0:T(2,128)S(1)}, f32[2,288]{1,0:T(2,128)S(1)}, u32[]{:S(2)}, u32[]{:S(2)}) collective-permute-start(f32[2,288]{1,0:T(2,128)S(1)} %get-tuple-element.43), channel_id=1, source_target_pairs={{0,1},{1,0},{2,3},{3,2},{4,5},{5,4},{6,7},{7,6},{8,9},{9,8},{10,11... | collective-permute-start | bytes 6920 | tf_op jit(solution)/shard_map/ppermute | solution.py:351
  22.2 9.8 %copy-start.17 = (s32[4]{0:T(128)S(1)}, s32[4]{0:T(128)}, u32[]{:S(2)}) copy-start(s32[4]{0:T(128)} %param.16) | copy-start | bytes 52
  22.3 1.1 copy-start.7
  24.9 0.7 copy-start.12
  25.6 23.6 %collective-permute-start.1 = (bf16[256,576]{1,0:T(8,128)(2,1)}, bf16[256,576]{1,0:T(8,128)(2,1)S(1)}, u32[]{:S(2)}, u32[]{:S(2)}) collective-permute-start(bf16[256,576]{1,0:T(8,128)(2,1)} %get-tuple-element.44), channel_id=1, source_target_pairs={{0,2},{2,4},{4,6},{6,8},{8,10},{10,12},{12,14},{14,16},{16,18},{18... | collective-permute-start | bytes 884744 | tf_op jit(solution)/shard_map/ppermute | solution.py:326
  49.2 1.0 copy-start.13
  51.5 9.4 %collective-permute-start.2 = (bf16[64,4608]{1,0:T(8,128)(2,1)}, bf16[64,4608]{1,0:T(8,128)(2,1)}, u32[]{:S(2)}, u32[]{:S(2)}) collective-permute-start(bf16[64,4608]{1,0:T(8,128)(2,1)} %shard_map.106), channel_id=1, source_target_pairs={{0,2},{2,0},{4,6},{6,4},{8,10},{10,8},{12,14},{14,12},{16,18},{18,... | collective-permute-start | bytes 1769480 | tf_op jit(solution)/shard_map/ppermute | solution.py:343
  51.5 0.8 copy-start.2
  52.3 35.3 %collective-permute-start.8 = (bf16[72,4608]{1,0:T(8,128)(2,1)}, bf16[72,4608]{1,0:T(8,128)(2,1)S(1)}, u32[]{:S(2)}, u32[]{:S(2)}) collective-permute-start(bf16[72,4608]{1,0:T(8,128)(2,1)} %collective-permute-done.4.refs_3_), channel_id=1, source_target_pairs={{0,8},{2,10},{8,16},{10,18},{16,24},{18,26},{24,28},{26,30},{28,20... | collective-permute-start | bytes 1990664 | tf_op jit(solution)/shard_map/ppermute | solution.py:365
  52.3 31.7 %collective-permute-start.10 = (bf16[72,4096]{1,0:T(8,128)(2,1)}, bf16[72,4096]{1,0:T(8,128)(2,1)}, u32[]{:S(2)}, u32[]{:S(2)}) collective-permute-start(bf16[72,4096]{1,0:T(8,128)(2,1)} %collective-permute-done.5.refs_6_.refs_3_), channel_id=1, source_target_pairs={{0,8},{2,10},{8,16},{10,18},{16,24},{18,26},{24,28},{26,30},{28,20... | collective-permute-start | bytes 1769480 | tf_op jit(solution)/shard_map/ppermute | solution.py:365
  56.0 33.1 %collective-permute-start.12 = (bf16[72,4608]{1,0:T(8,128)(2,1)}, bf16[72,4608]{1,0:T(8,128)(2,1)S(1)}, u32[]{:S(2)}, u32[]{:S(2)}) collective-permute-start(bf16[72,4608]{1,0:T(8,128)(2,1)} %collective-permute-done.6.refs_4_), channel_id=1, source_target_pairs={{0,4},{2,6},{8,0},{10,2},{16,8},{18,10},{24,16},{26,18},{28,24},{3... | collective-permute-start | bytes 1990664 | tf_op jit(solution)/shard_map/ppermute | solution.py:365
  56.3 31.3 %collective-permute-start.14 = (bf16[72,4096]{1,0:T(8,128)(2,1)}, bf16[72,4096]{1,0:T(8,128)(2,1)}, u32[]{:S(2)}, u32[]{:S(2)}) collective-permute-start(bf16[72,4096]{1,0:T(8,128)(2,1)} %copy-done.2), channel_id=1, source_target_pairs={{0,4},{2,6},{8,0},{10,2},{16,8},{18,10},{24,16},{26,18},{28,24},{3... | collective-permute-start | bytes 1769480 | tf_op jit(solution)/shard_map/ppermute | solution.py:365
  60.9 28.2 %collective-permute-start.3 = (bf16[64,4096]{1,0:T(8,128)(2,1)S(1)}, bf16[64,4096]{1,0:T(8,128)(2,1)S(1)}, u32[]{:S(2)}, u32[]{:S(2)}) collective-permute-start(bf16[64,4096]{1,0:T(8,128)(2,1)S(1)} %broadcast_multiply_fusion), channel_id=1, source_target_pairs={{0,2},{2,0},{4,6},{6,4},{8,10},{10,8},{12,14},{14,12},{16,18},{18,... | collective-permute-start | bytes 1572872 | tf_op jit(solution)/shard_map/ppermute | solution.py:343
  63.6 25.6 %copy-start.1 = (bf16[72,4096]{1,0:T(8,128)(2,1)S(1)}, bf16[72,4096]{1,0:T(8,128)(2,1)}, u32[]{:S(2)}) copy-start(bf16[72,4096]{1,0:T(8,128)(2,1)} %refs_2_.1) | copy-start | bytes 1769476
  63.6 25.6 %copy-start.3 = (bf16[72,4096]{1,0:T(8,128)(2,1)S(1)}, bf16[72,4096]{1,0:T(8,128)(2,1)}, u32[]{:S(2)}) copy-start(bf16[72,4096]{1,0:T(8,128)(2,1)} %copy-done.2) | copy-start | bytes 1769476
  84.0 23.6 %collective-permute-start.11 = (bf16[72,4096]{1,0:T(8,128)(2,1)}, bf16[72,4096]{1,0:T(8,128)(2,1)S(1)}, u32[]{:S(2)}, u32[]{:S(2)}) collective-permute-start(bf16[72,4096]{1,0:T(8,128)(2,1)} %collective-permute-done.10.refs_4_.refs_2_), channel_id=1, source_target_pairs={{0,8},{2,10},{8,16},{10,18},{16,24},{18,26},{24,28},{26,30},{28,20... | collective-permute-start | bytes 1769480 | tf_op jit(solution)/shard_map/ppermute | solution.py:365
  87.6 20.0 %collective-permute-start.15 = (bf16[72,4096]{1,0:T(8,128)(2,1)}, bf16[72,4096]{1,0:T(8,128)(2,1)S(1)}, u32[]{:S(2)}, u32[]{:S(2)}) collective-permute-start(bf16[72,4096]{1,0:T(8,128)(2,1)} %collective-permute-done.14.refs_5_.refs_3_), channel_id=1, source_target_pairs={{0,4},{2,6},{8,0},{10,2},{16,8},{18,10},{24,16},{26,18},{28,24},{3... | collective-permute-start | bytes 1769480 | tf_op jit(solution)/shard_map/ppermute | solution.py:365
  87.6 24.6 %collective-permute-start.9 = (bf16[72,4608]{1,0:T(8,128)(2,1)S(1)}, bf16[72,4608]{1,0:T(8,128)(2,1)S(1)}, u32[]{:S(2)}, u32[]{:S(2)}) collective-permute-start(bf16[72,4608]{1,0:T(8,128)(2,1)S(1)} %collective-permute-done.8.refs_2_), channel_id=1, source_target_pairs={{0,8},{2,10},{8,16},{10,18},{16,24},{18,26},{24,28},{26,30},{28,20... | collective-permute-start | bytes 1990664 | tf_op jit(solution)/shard_map/ppermute | solution.py:365
  89.1 26.7 %collective-permute-start.13 = (bf16[72,4608]{1,0:T(8,128)(2,1)S(1)}, bf16[72,4608]{1,0:T(8,128)(2,1)S(1)}, u32[]{:S(2)}, u32[]{:S(2)}) collective-permute-start(bf16[72,4608]{1,0:T(8,128)(2,1)S(1)} %collective-permute-done.12.refs_3_), channel_id=1, source_target_pairs={{0,4},{2,6},{8,0},{10,2},{16,8},{18,10},{24,16},{26,18},{28,24},{3... | collective-permute-start | bytes 1990664 | tf_op jit(solution)/shard_map/ppermute | solution.py:365
  92.7 6.2 %collective-permute-start.17 = (f32[128,432]{1,0:T(8,128)S(1)}, f32[128,432]{1,0:T(8,128)S(1)}, u32[]{:S(2)}, u32[]{:S(2)}) collective-permute-start(f32[128,432]{1,0:T(8,128)S(1)} %shard_map.108.refs_0_), channel_id=1, source_target_pairs={{0,1},{1,0},{2,3},{3,2},{4,5},{5,4},{6,7},{7,6},{8,9},{9,8},{10,11... | collective-permute-start | bytes 663560 | tf_op jit(solution)/shard_map/ppermute | solution.py:351
  98.8 5.8 %collective-permute-start.16 = (f32[128,288]{1,0:T(8,128)S(1)}, f32[128,288]{1,0:T(8,128)S(1)}, u32[]{:S(2)}, u32[]{:S(2)}) collective-permute-start(f32[128,288]{1,0:T(8,128)S(1)} %shard_map.107.refs_0_), channel_id=1, source_target_pairs={{0,1},{1,0},{2,3},{3,2},{4,5},{5,4},{6,7},{7,6},{8,9},{9,8},{10,11... | collective-permute-start | bytes 442376 | tf_op jit(solution)/shard_map/ppermute | solution.py:351
  115.8 14.4 %collective-permute-start.18 = (bf16[72,4608]{1,0:T(8,128)(2,1)S(1)}, bf16[72,4608]{1,0:T(8,128)(2,1)S(1)}, u32[]{:S(2)}, u32[]{:S(2)}) collective-permute-start(bf16[72,4608]{1,0:T(8,128)(2,1)S(1)} %collective-permute-done.9.refs_2_), channel_id=1, source_target_pairs={{0,8},{2,10},{8,16},{10,18},{16,24},{18,26},{24,28},{26,30},{28,20... | collective-permute-start | bytes 1990664 | tf_op jit(solution)/shard_map/ppermute | solution.py:365
  116.6 12.2 %collective-permute-start.19 = (bf16[72,4096]{1,0:T(8,128)(2,1)S(1)}, bf16[72,4096]{1,0:T(8,128)(2,1)S(1)}, u32[]{:S(2)}, u32[]{:S(2)}) collective-permute-start(bf16[72,4096]{1,0:T(8,128)(2,1)S(1)} %collective-permute-done.15.refs_5_.refs_3_), channel_id=1, source_target_pairs={{0,4},{2,6},{8,0},{10,2},{16,8},{18,10},{24,16},{26,18},{28,24},{3... | collective-permute-start | bytes 1769480 | tf_op jit(solution)/shard_map/ppermute | solution.py:365
  118.6 13.6 %collective-permute-start.21 = (f32[128,288]{1,0:T(8,128)S(1)}, f32[128,288]{1,0:T(8,128)S(1)}, u32[]{:S(2)}, u32[]{:S(2)}) collective-permute-start(f32[128,288]{1,0:T(8,128)S(1)} %shard_map.114.refs_0_), channel_id=1, source_target_pairs={{0,1},{1,0},{2,3},{3,2},{4,5},{5,4},{6,7},{7,6},{8,9},{9,8},{10,11... | collective-permute-start | bytes 442376 | tf_op jit(solution)/shard_map/ppermute | solution.py:351
  131.0 3.9 %collective-permute-start.20 = (f32[128,144]{1,0:T(8,128)S(1)}, f32[128,144]{1,0:T(8,128)S(1)}, u32[]{:S(2)}, u32[]{:S(2)}) collective-permute-start(f32[128,144]{1,0:T(8,128)S(1)} %shard_map.113.refs_0_), channel_id=1, source_target_pairs={{0,1},{1,0},{2,3},{3,2},{4,5},{5,4},{6,7},{7,6},{8,9},{9,8},{10,11... | collective-permute-start | bytes 221192 | tf_op jit(solution)/shard_map/ppermute | solution.py:351
  135.4 6.6 %collective-permute-start.22 = (f32[64,4608]{1,0:T(8,128)S(1)}, f32[64,4608]{1,0:T(8,128)S(1)}, u32[]{:S(2)}, u32[]{:S(2)}) collective-permute-start(f32[64,4608]{1,0:T(8,128)S(1)} %get-tuple-element.71), channel_id=1, source_target_pairs={{0,2},{2,0},{4,6},{6,4},{8,10},{10,8},{12,14},{14,12},{16,18},{18,... | collective-permute-start | bytes 3538952 | tf_op jit(solution)/shard_map/ppermute | solution.py:343
  142.1 11.3 %copy-start.5 = (bf16[288,576]{1,0:T(8,128)(2,1)S(1)}, bf16[288,576]{1,0:T(8,128)(2,1)}, u32[]{:S(2)}) copy-start(bf16[288,576]{1,0:T(8,128)(2,1)} %expand_ref.3) | copy-start | bytes 995332
  143.7 13.1 %collective-permute-start.23 = (f32[64,4096]{1,0:T(8,128)S(1)}, f32[64,4096]{1,0:T(8,128)S(1)}, u32[]{:S(2)}, u32[]{:S(2)}) collective-permute-start(f32[64,4096]{1,0:T(8,128)S(1)} %get-tuple-element.74), channel_id=1, source_target_pairs={{0,2},{2,0},{4,6},{6,4},{8,10},{10,8},{12,14},{14,12},{16,18},{18,... | collective-permute-start | bytes 3145736 | tf_op jit(solution)/shard_map/ppermute | solution.py:343
  144.1 9.3 %collective-permute-start.24 = (bf16[256,576]{1,0:T(8,128)(2,1)S(1)}, bf16[256,576]{1,0:T(8,128)(2,1)S(1)}, u32[]{:S(2)}, u32[]{:S(2)}) collective-permute-start(bf16[256,576]{1,0:T(8,128)(2,1)S(1)} %get-tuple-element.76), channel_id=1, source_target_pairs={{2,0},{4,2},{6,4},{8,6},{10,8},{12,10},{14,12},{16,14},{18,16},{20... | collective-permute-start | bytes 884744 | tf_op jit(solution)/shard_map/ppermute | solution.py:326
  154.3 2.5 %collective-permute-start.25 = (f32[2,288]{1,0:T(2,128)S(1)}, f32[2,288]{1,0:T(2,128)S(1)}, u32[]{:S(2)}, u32[]{:S(2)}) collective-permute-start(f32[2,288]{1,0:T(2,128)S(1)} %shard_map.120), channel_id=1, source_target_pairs={{0,1},{1,0},{2,3},{3,2},{4,5},{5,4},{6,7},{7,6},{8,9},{9,8},{10,11... | collective-permute-start | bytes 6920 | tf_op jit(solution)/shard_map/ppermute | solution.py:351
  157.8 6.5 %copy-start.9 = (bf16[9,576,48]{1,2,0:T(8,128)(2,1)S(1)}, bf16[9,576,48]{1,2,0:T(8,128)(2,1)}, u32[]{:S(2)}) copy-start(bf16[9,576,48]{1,2,0:T(8,128)(2,1)} %param.10) | copy-start | bytes 1492996
  157.8 6.5 %copy-start.11 = (bf16[576,288]{0,1:T(8,128)(2,1)S(1)}, bf16[576,288]{0,1:T(8,128)(2,1)}, u32[]{:S(2)}) copy-start(bf16[576,288]{0,1:T(8,128)(2,1)} %param.11) | copy-start | bytes 995332
  159.9 17.1 %all-to-all-start.1 = ((bf16[16,4,4096]{2,1,0:T(4,128)(2,1)}), bf16[16,4,4096]{2,1,0:T(4,128)(2,1)}, u32[]{:S(2)}, u32[]{:S(2)}) async-start(bf16[16,4,4096]{2,1,0:T(4,128)(2,1)} %all_to_all.19), calls=%async_computation.1 | async-start | bytes 1048576 | tf_op jit(solution)/shard_map/all_to_all | solution.py:492

commit v2 on v1

--- a/solution.py
+++ b/solution.py
@@ -13,7 +13,7 @@
 FRAME_ROWS = WIDE * WIDE
 EDGE = 8
 LANES = 128
-VMEM_BYTES = 40 * 2**20
+VMEM_BYTES = 20 * 2**20
 FREE = pl.CostEstimate(flops=0, bytes_accessed=0, transcendentals=0)
 
 
@@ -156,21 +156,60 @@
     return ((2 * a + down) * WIDE + 2 * b + across == frame_row).astype(jnp.float32)
 
 
-def patch_kernel(mask_ref, halo_ref, even_ref, out_ref):
+def facts_kernel(clip_ref, keep_ref, out_ref):
+    shard = lax.axis_index("ctx")
+    frames = clip_ref.shape[0]
+    out_ref[0] = shard % 2
+    for block in range(2):
+        pair = shard // 2 * 2 + block
+        clip = clip_ref[2 * pair]
+        start = jnp.int32(0)
+        for other in range(0, frames, 2):
+            start += jnp.where(clip_ref[other] < clip, 1, 0)
+        out_ref[1 + block] = keep_ref[clip] - (pair - start) * (OUT_SIDE * OUT_SIDE)
+    before = clip_ref[jnp.maximum(2 * shard - 1, 0)]
+    out_ref[3] = jnp.where((shard > 0) & (before == clip_ref[2 * shard]), 1, 0)
+
+
+def token_place(row, core, unit):
+    per_block = OUT_SIDE * OUT_SIDE
+    within = row % per_block
+    block = (within // unit) % 2
+    target_core = jnp.where(row < per_block, core, 1 - core)
+    return block, unit * (2 * (within // (2 * unit)) + target_core) + within % unit
+
+
+def reorder_matrix(core, unit, to_sent):
+    shape = (2 * OUT_SIDE * OUT_SIDE,) * 2
+    out_row = lax.broadcasted_iota(jnp.int32, shape, 0)
+    in_row = lax.broadcasted_iota(jnp.int32, shape, 1)
+    sent, natural = (out_row, in_row) if to_sent else (in_row, out_row)
+    block, token = token_place(sent, core, unit)
+    source = jnp.where(block == core, 0, OUT_SIDE * OUT_SIDE) + token
+    return (source == natural).astype(jnp.bfloat16)
+
+
+def order_kernel(unit, facts_ref, own_ref, mate_ref, out_ref):
+    rows = jnp.concatenate([own_ref[...], mate_ref[...]], axis=0)
+    matrix = reorder_matrix(facts_ref[0], unit, True)
+    out_ref[...] = jnp.dot(matrix, rows, preferred_element_type=jnp.float32).astype(jnp.bfloat16)
+
+
+def patch_kernel(facts_ref, halo_ref, even_ref, out_ref):
     chans = halo_ref.shape[1]
     per_frame = OUT_SIDE * OUT_SIDE
     select = select_rows(True).astype(jnp.bfloat16)
     for frame, source in enumerate((halo_ref, even_ref)):
         rows = jnp.dot(select, source[...], preferred_element_type=jnp.float32)
         if frame == 0:
-            rows = rows * mask_ref[0, 0]
+            rows = rows * facts_ref[3].astype(jnp.float32)
         rows = rows.astype(jnp.bfloat16)
         for tap in range(4):
             at = (frame * 4 + tap) * chans
             out_ref[:, at : at + chans] = rows[tap * per_frame : (tap + 1) * per_frame]
 
 
-def unpatch_kernel(mask_ref, own_ref, mate_ref, lead_ref, even_ref):
+def unpatch_kernel(facts_ref, own_ref, mate_ref, lead_ref, even_ref):
     chans = lead_ref.shape[1]
     select = select_rows(False)
     frames = []
@@ -183,7 +222,7 @@
             jnp.dot(select, jnp.concatenate(pieces, axis=0), precision=lax.Precision.HIGHEST)
         )
     good = inside(FRAME_ROWS)
-    lead_ref[...] = (frames[0] * (good * mask_ref[0, 0])).astype(jnp.bfloat16)
+    lead_ref[...] = (frames[0] * (good * facts_ref[3].astype(jnp.float32))).astype(jnp.bfloat16)
     even_ref[...] = frames[1] * good
 
 
@@ -274,7 +313,29 @@
     return [pl.BlockSpec(memory_space=pltpu.SMEM)] + [pl.BlockSpec(memory_space=pltpu.VMEM)] * count
 
 
-def take_patches(mask, halo, even):
+def facts_of(frame_clip, clip_keep):
+    smem = pl.BlockSpec(memory_space=pltpu.SMEM)
+    return pl.pallas_call(
+        facts_kernel,
+        out_shape=jax.ShapeDtypeStruct((4,), jnp.int32),
+        in_specs=[smem, smem],
+        out_specs=smem,
+        cost_estimate=FREE,
+    )(frame_clip, clip_keep)
+
+
+def order_rows(facts, own, mate, unit):
+    rows, columns = own.shape
+    return pl.pallas_call(
+        functools.partial(order_kernel, unit),
+        out_shape=bf16(2 * rows, columns),
+        in_specs=vmem_specs(2),
+        compiler_params=pltpu.CompilerParams(vmem_limit_bytes=VMEM_BYTES),
+        cost_estimate=FREE,
+    )(facts, own, mate)
+
+
+def take_patches(facts, halo, even):
     chans = even.shape[1]
     return pl.pallas_call(
         patch_kernel,
@@ -282,17 +343,17 @@
         in_specs=vmem_specs(2),
         compiler_params=pltpu.CompilerParams(vmem_limit_bytes=VMEM_BYTES),
         cost_estimate=FREE,
-    )(mask, halo, even)
-
-
-def return_patches(mask, own, mate, chans):
+    )(facts, halo, even)
+
+
+def return_patches(facts, own, mate, chans):
     return pl.pallas_call(
         unpatch_kernel,
         out_shape=(bf16(FRAME_ROWS, chans), f32(FRAME_ROWS, chans)),
         in_specs=vmem_specs(2),
         compiler_params=pltpu.CompilerParams(vmem_limit_bytes=VMEM_BYTES),
         cost_estimate=FREE,
-    )(mask, own, mate)
+    )(facts, own, mate)
 
 
 def excite_grad(even, odd, conv, excite, squeeze_out):
@@ -372,29 +433,35 @@
     return lax.optimization_barrier(values)
 
 
-def sums_kernel(count, *refs):
-    patch_ref, back_ref, *blocks, out_ref = refs
+def sums_kernel(count, patch_ref, keep_ref, send_ref, *refs):
+    *blocks, out_ref = refs
     products = [contract_last(patch_ref[...], ref[...]) for ref in blocks[:count]]
-    products += [contract_last(back_ref[...], ref[...]) for ref in blocks[count:]]
+    back = jnp.concatenate([keep_ref[...], send_ref[...]], axis=0)
+    products += [contract_last(back, ref[...]) for ref in blocks[count:]]
     out_ref[...] = jnp.concatenate(products, axis=1)
 
 
-def totals_kernel(count, backward, first, *refs):
+def totals_kernel(count, unit, backward, first, facts_ref, *refs):
     sums = refs[0][...] + refs[1][...]
     blocks, refs = refs[2 : 2 + count], refs[2 + count :]
     before, after = refs[:-2], refs[-2:]
-    depth = sums.shape[1] // 2
+    rows, depth = sums.shape[0], sums.shape[1] // 2
     pre, grad_act = sums[:, :depth], sums[:, depth:]
+    core = facts_ref[0]
+    block, token = token_place(lax.broadcasted_iota(jnp.int32, (rows, 1), 0), core, unit)
+    live = (token < jnp.where(block == 0, facts_ref[1], facts_ref[2])).astype(jnp.float32)
     factor = grad_act * silu_slope(pre) if backward else pre * jax.nn.sigmoid(pre)
-    factor = factor.astype(jnp.bfloat16)
+    factor = (factor * live).astype(jnp.bfloat16)
+    if backward:
+        matrix = reorder_matrix(core, unit, False)
+        factor = jnp.dot(matrix, factor, preferred_element_type=jnp.float32).astype(jnp.bfloat16)
     width = depth // count
     total = 0.0
     for place, ref in enumerate(blocks):
         piece = factor[:, place * width : (place + 1) * width]
         total += jnp.dot(piece, ref[...], preferred_element_type=jnp.float32)
-    rows = after[0].shape[0]
     for half, ref in enumerate(after):
-        value = total[half * rows : (half + 1) * rows]
+        value = total[half * rows // 2 : (half + 1) * rows // 2]
         ref[...] = value if first else before[half][...] + value
 
 
@@ -402,13 +469,28 @@
     count, width = len(samplers), samplers[0].shape[0]
     return whole_call(
         functools.partial(sums_kernel, count), f32(patches.shape[0], 2 * count * width), []
-    )(patches, back, *samplers, *readouts)
-
-
-def add_products(sums, blocks, before, backward):
+    )(patches, *back, *samplers, *readouts)
+
+
+def add_products(facts, sums, blocks, before, unit, backward):
     rows, columns = sums[0].shape[0] // 2, blocks[0].shape[1]
-    kernel = functools.partial(totals_kernel, len(blocks), backward, not before)
-    return whole_call(kernel, (f32(rows, columns),) * 2, [])(*sums, *blocks, *before)
+    kernel = functools.partial(totals_kernel, len(blocks), unit, backward, not before)
+    operands = (*sums, *blocks, *before)
+    return pl.pallas_call(
+        kernel,
+        out_shape=(f32(rows, columns),) * 2,
+        in_specs=vmem_specs(len(operands)),
+        compiler_params=pltpu.CompilerParams(vmem_limit_bytes=VMEM_BYTES),
+        cost_estimate=FREE,
+    )(facts, *operands)
+
+
+def chips_exchange(value):
+    count = lax.axis_size("ctx")
+    groups = [list(range(core, count, 2)) for core in range(2)]
+    return lax.all_to_all(
+        value, "ctx", split_axis=0, concat_axis=0, tiled=True, axis_index_groups=groups
+    )
 
 
 def per_device(
@@ -422,74 +504,51 @@
     clip_keep,
     token_cotangent,
 ):
-    shard_index = lax.axis_index("ctx")
-    frames_dev, cells, chans = features.shape
-    pairs_dev = frames_dev // 2
+    chans = features.shape[2]
+    count = lax.axis_size("ctx")
+    steps, unit = count // 4, OUT_SIDE * OUT_SIDE // count
     flat_sampler = sampler_kernel.reshape(sampler_kernel.shape[0], 8 * chans)
     blocks = ring_step((flat_sampler, readout_kernel) * 2)
     group_kernel = jnp.swapaxes(group_kernel, 1, 2)
     squeeze_in = squeeze_in.T
-
-    local_clip = lax.dynamic_slice_in_dim(frame_clip, shard_index * frames_dev, frames_dev)
-    edge_clip = lax.dynamic_slice_in_dim(
-        frame_clip, jnp.maximum(shard_index * frames_dev - 1, 0), 1
-    )
-    first_keep = jnp.logical_and(shard_index > 0, edge_clip[0] == local_clip[0])
-    mask = first_keep.astype(jnp.float32).reshape(1, 1)
-    per_frame = OUT_SIDE * OUT_SIDE
-    pair_clip = frame_clip[0::2]
-    clip_ids = jnp.arange(clip_keep.shape[0], dtype=jnp.int32)
-    start_pair = jnp.sum((pair_clip[None, :] < clip_ids[:, None]).astype(jnp.int32), axis=1)
-    own_clip = local_clip[0::2]
-    one_hot = (own_clip[:, None] == clip_ids[None, :]).astype(jnp.int32)
-    own_start = jnp.sum(one_hot * start_pair[None, :], axis=1)
-    own_keep = jnp.sum(one_hot * clip_keep[None, :], axis=1)
-    pair_index = shard_index * pairs_dev + jnp.arange(pairs_dev, dtype=jnp.int32)
-    position = (pair_index - own_start)[:, None] * per_frame + jnp.arange(
-        per_frame, dtype=jnp.int32
-    )[None, :]
-    live = (position < own_keep[:, None]).reshape(-1).astype(jnp.bfloat16)
-
-    back = (
-        lax.all_to_all(token_cotangent, "ctx", split_axis=0, concat_axis=0, tiled=True)
-        * live[:, None]
-    )
-    both_back = jnp.concatenate([back, swap_cores(back)], axis=0)
+    facts = facts_of(frame_clip, clip_keep)
 
     conv, padded, squeezed = conv_forward(features, group_kernel, squeeze_in)
+    token_cotangent, squeezed = tie(token_cotangent, squeezed)
+    back = chips_exchange(token_cotangent)
     squeezed = sum_tp(squeezed)
     even, odd, excite = hidden_frames(conv, padded, squeezed, squeeze_out)
-    patches = take_patches(mask, shifted(odd, "ctx", 1), even)
-    both_patches = jnp.concatenate([patches, swap_cores(patches)], axis=0)
-
-    steps = lax.axis_size("ctx") // 4
+    halo = shifted(odd, "ctx", 1)
+    halo, *blocks = tie(halo, *blocks)
+    patches = take_patches(facts, halo, even)
+    patches = order_rows(facts, patches, swap_cores(patches), unit)
+    back = (back, swap_cores(back))
+
     samplers, readouts = [flat_sampler], [readout_kernel]
     tokens = grads = ()
     for step in range(1, steps + 1):
         here = blocks
         if step < steps:
             samplers, readouts = samplers + [here[0], here[2]], readouts + [here[1], here[3]]
-            if step == 1:
-                *here, even = tie(*here, even)
-            elif step > 2:
-                *here, token_own, token_mate, grad_own, grad_mate = tie(*here, *tokens, *grads)
-                tokens, grads = (token_own, token_mate), (grad_own, grad_mate)
             if step == steps - 1:
+                *here, token_keep, token_send, grad_own, grad_mate = tie(*here, *tokens, *grads)
+                tokens, grads = (token_keep, token_send), (grad_own, grad_mate)
                 here = here[0], None, None, here[3]
             blocks = ring_step(here)
         else:
             samplers, readouts = samplers + [here[0]], readouts + [here[3]]
-        sums = tp_terms(partial_sums(both_patches, both_back, samplers, readouts))
-        tokens = add_products(sums, readouts, tokens, False)
-        grads = add_products(sums, samplers, grads, True)
-        samplers, readouts = [], []
-    lead, grad_even = return_patches(mask, grads[0], swap_cores(grads[1]), chans)
-    token_own, token_mate, lead = tie(*tokens, lead)
+        if step >= steps - 2:
+            sums = tp_terms(partial_sums(patches, back, samplers, readouts))
+            tokens = add_products(facts, sums, readouts, tokens, unit, False)
+            grads = add_products(facts, sums, samplers, grads, unit, True)
+            samplers, readouts = [], []
+    lead, grad_even = return_patches(facts, grads[0], swap_cores(grads[1]), chans)
+    token_keep, token_send, lead = tie(*tokens, lead)
     grad_odd = shifted(lead, "ctx", -1)
+    tokens = (token_keep + swap_cores(token_send)).astype(jnp.bfloat16)
+    tokens, grad_odd = tie(tokens, grad_odd)
+    llm_tokens = chips_exchange(tokens)
     grad_relaxed = sum_tp(excite_grad(grad_even, grad_odd, conv, excite, squeeze_out))
-    tokens = (token_own + swap_cores(token_mate)).astype(jnp.bfloat16) * live[:, None]
-    tokens, grad_relaxed = tie(tokens, grad_relaxed)
-    llm_tokens = lax.all_to_all(tokens, "ctx", split_axis=0, concat_axis=0, tiled=True)
     grad_features = conv_backward(
         grad_even, grad_odd, conv, excite, squeezed, grad_relaxed, squeeze_in, group_kernel
     )

time: 181 us -> 168 us (0.928)
  local copies, waits for them, and re-layouts: 16.1 us -> 8.12 us
  Pallas kernels: 32.5 us -> 38.5 us
  waiting for transfers between devices: 79.1 us -> 74.1 us
  other arithmetic: 5.57 us -> 0.9 us
    all_to_all x4 -> x0, local copies, waits for them, and re-layouts: 8.15 us -> none  [the longest x2 4.09 us: per_device(): lax.all_to_all(tokens, 'ctx', split_axis=0, concat_axis=0, tiled=True)]
    ppermute x6 -> x5, waiting for transfers between devices: 5.2 us -> 11.1 us  [tp_terms(): other = lax.ppermute(value, 'tp', [(i, i ^ reach) for i in range(size)])]
    pallas_call x8, Pallas kernels: 10.2 us -> 15.2 us  [the longest x6 12.2 us: add_products(): pl.pallas_call(kernel, out_shape=(f32(rows, columns),) * 2, in_specs=vmem...]
    ppermute x2, waiting for transfers between devices: 23.1 us -> 19.1 us  [shifted(): return lax.ppermute(value, axis, pairs)]
    ppermute x14, waiting for transfers between devices: 42.4 us -> 38.5 us  [ring_step(): lax.ppermute(value, 'ctx', pairs)]
    ppermute x14, starting transfers between devices: 11.4 us -> 14.1 us  [ring_step(): lax.ppermute(value, 'ctx', pairs)]
    all_to_all x2, waiting for transfers between devices: 7.07 us -> 4.85 us  [chips_exchange(): lax.all_to_all(value, 'ctx', split_axis=0, concat_axis=0, tiled=True, axi...]
    mul x2 -> x0, other arithmetic: 2.12 us -> none  [the longest x1 1.14 us: per_device(): lax.all_to_all(token_cotangent, 'ctx', split_axis=0, concat_axis=0, tiled...]
  transfers between devices with their start and end apart: 28 -> 27, of which waited for: 13 -> 16; matrix products, arithmetic and copies ran while one was open for 4% -> 1% of each run, Pallas kernels for 17% -> 21%
where the time goes in v2:
time: 168 us; the launch traced here: 166 us
  waiting for transfers between devices  74.1 us (44%)
  starting transfers between devices  43.4 us (26%)
  Pallas kernels  38.5 us (23%)
  local copies, waits for them, and re-layouts  8.12 us (5%)
    ppermute x14, waiting for transfers between devices, ring_step(): lax.ppermute(value, 'ctx', pairs)  38.5 us
    ppermute x2, waiting for transfers between devices, shifted(): return lax.ppermute(value, axis, pairs)  19.1 us
    ppermute x14, starting transfers between devices, ring_step(): lax.ppermute(value, 'ctx', pairs)  14.1 us
    pallas_call x6, Pallas kernels, add_products(): pl.pallas_call(kernel, out_shape=(f32(rows, columns),) * 2, in_specs=vmem...  12.2 us
    ppermute x5, waiting for transfers between devices, tp_terms(): other = lax.ppermute(value, 'tp', [(i, i ^ reach) for i in range(size)])  11.1 us
    all_to_all x2, starting transfers between devices, chips_exchange(): lax.all_to_all(value, 'ctx', split_axis=0, concat_axis=0, tiled=True, axi...  9.84 us
    ppermute x2, starting transfers between devices, shifted(): return lax.ppermute(value, axis, pairs)  8.11 us
    pallas_call x3, Pallas kernels, partial_sums(): whole_call(functools.partial(sums_kernel, count), f32(patches.shape[0], 2...  7.62 us
  transfers between devices with their start and end apart: 27, of which 16 were waited for; matrix products, arithmetic and copies ran while one was open for 1% of the time, Pallas kernels for 21%

profile of v2, /device:TPU:3, one launch (start us, length us, event | category | flops | bytes accessed | tf_op | source)
XLA Modules:
  0.0 165.9 jit_solution(2236125448275397404)
XLA Ops:
  0.7 1.7 %reshape.11.refs_0_.refs_2_ = bf16[72,4608]{1,0:T(8,128)(2,1)S(1)} reshape(bf16[72,8,576]{2,1,0:T(8,128)(2,1)} %param.13) | data formatting | bytes 1327104 | tf_op jit(solution)/shard_map/reshape | solution.py:510
  2.4 1.3 collective-permute-start.4
  3.7 0.2 collective-permute-start.2
  3.9 1.3 collective-permute-start.5
  5.2 0.2 collective-permute-start.3
  5.5 4.5 %shard_map.105 = (f32[512,576]{1,0:T(8,128)S(1)}, bf16[512,576]{1,0:T(8,128)(2,1)S(1)}, f32[2,288]{1,0:T(2,128)S(1)}) custom-call(bf16[2,196,576]{2,1,0:T(8,128)(2,1)S(1)} %copy.11.feat_ref, bf16[9,48,576]{2,1,0:T(8,128)(2,1)S(1)} %bitcast.10, bf16[288,576]{1,0:T(8,128)(2,1)S(1)} %bitcast.12), custom_call_target="tpu_custom_call" | custom-call | tf_op jit(solution)/shard_map/pallas_call | solution.py:292
  9.9 0.9 copy-done.1
  10.8 5.8 %all-to-all-start = ((bf16[8,8,4096]{2,1,0:T(8,128)(2,1)}), bf16[8,8,4096]{2,1,0:T(8,128)(2,1)S(1)}, u32[]{:S(2)}, u32[]{:S(2)}) async-start(bf16[8,8,4096]{2,1,0:T(8,128)(2,1)} %bitcast.15), calls=%async_computation | async-start | bytes 1048576 | tf_op jit(solution)/shard_map/all_to_all | solution.py:491
  16.6 1.2 collective-permute-start
  17.9 1.6 collective-permute-done
  19.5 1.1 copy-done.2
  20.5 1.5 shard_map.106
  22.0 0.7 copy-done.7
  22.8 6.1 %collective-permute-start.1 = (bf16[256,576]{1,0:T(8,128)(2,1)}, bf16[256,576]{1,0:T(8,128)(2,1)}, u32[]{:S(2)}, u32[]{:S(2)}) collective-permute-start(bf16[256,576]{1,0:T(8,128)(2,1)} %get-tuple-element.44), channel_id=1, source_target_pairs={{0,2},{2,4},{4,6},{6,8},{8,10},{10,12},{12,14},{14,16},{16,18},{18... | collective-permute-start | bytes 884744 | tf_op jit(solution)/shard_map/ppermute | solution.py:387
  28.8 1.3 shard_map.104.facts_ref
  30.1 13.0 %collective-permute-done.1.halo_ref = bf16[256,576]{1,0:T(8,128)(2,1)} collective-permute-done((bf16[256,576]{1,0:T(8,128)(2,1)}, bf16[256,576]{1,0:T(8,128)(2,1)}, u32[]{:S(2)}, u32[]{:S(2)}) %collective-permute-start.1) | collective-permute-done | bytes 294944 | tf_op jit(solution)/shard_map/ppermute | solution.py:387
  43.2 1.0 copy-done.8
  44.2 0.7 copy-done.9
  44.8 2.2 %shard_map.107.own_ref = bf16[64,4608]{1,0:T(8,128)(2,1)} custom-call(s32[4]{0:T(128)S(1)} %copy-done.9, bf16[256,576]{1,0:T(8,128)(2,1)} %collective-permute-done.1.halo_ref, bf16[256,576]{1,0:T(8,128)(2,1)S(1)} %copy-done.8), custom_call_target="tpu_custom_call" | custom-call | tf_op jit(solution)/shard_map/pallas_call | solution.py:340
  47.1 4.1 %collective-permute-start.12 = (bf16[72,4608]{1,0:T(8,128)(2,1)S(1)}, bf16[72,4608]{1,0:T(8,128)(2,1)}, u32[]{:S(2)}, u32[]{:S(2)}) collective-permute-start(bf16[72,4608]{1,0:T(8,128)(2,1)S(1)} %collective-permute-done.4.refs_2_.refs_4_), channel_id=1, source_target_pairs={{0,4},{2,6},{8,0},{10,2},{16,8},{18,10},{24,16},{26,18},{28,24},{3... | collective-permute-start | bytes 1990664 | tf_op jit(solution)/shard_map/ppermute | solution.py:426
  51.2 0.4 collective-permute-start.10
  51.6 1.1 collective-permute-start.14
  52.7 1.3 collective-permute-start.7
  54.0 12.3 %collective-permute-done.8.refs_3_.refs_5_ = bf16[72,4608]{1,0:T(8,128)(2,1)} collective-permute-done((bf16[72,4608]{1,0:T(8,128)(2,1)}, bf16[72,4608]{1,0:T(8,128)(2,1)}, u32[]{:S(2)}, u32[]{:S(2)}) %collective-permute-start.8) | collective-permute-done | bytes 663584 | tf_op jit(solution)/shard_map/ppermute | solution.py:426
  66.3 0.4 collective-permute-done.12.refs_4_.refs_6_
  66.7 1.1 collective-permute-start.13
  67.8 11.2 %collective-permute-done.10.refs_8_.refs_5_ = bf16[72,4096]{1,0:T(8,128)(2,1)} collective-permute-done((bf16[72,4096]{1,0:T(8,128)(2,1)}, bf16[72,4096]{1,0:T(8,128)(2,1)}, u32[]{:S(2)}, u32[]{:S(2)}) %collective-permute-start.10) | collective-permute-done | bytes 589856 | tf_op jit(solution)/shard_map/ppermute | solution.py:426
  79.0 0.4 collective-permute-done.14.refs_9_.refs_6_
  79.4 1.1 collective-permute-start.15
  80.4 1.7 %shard_map.108.patch_ref = bf16[128,4608]{1,0:T(8,128)(2,1)S(1)} custom-call(s32[4]{0:T(128)S(1)} %copy-done.10, bf16[64,4608]{1,0:T(8,128)(2,1)} %shard_map.107.own_ref, bf16[64,4608]{1,0:T(8,128)(2,1)} %collective-permute-done.6.mate_ref), custom_call_target="tpu_custom_call" | custom-call | tf_op jit(solution)/shard_map/pallas_call | solution.py:329
  82.2 5.5 %shard_map.109.refs_0_ = f32[128,720]{1,0:T(8,128)S(1)} custom-call(bf16[128,4608]{1,0:T(8,128)(2,1)S(1)} %shard_map.108.patch_ref, bf16[64,4096]{1,0:T(8,128)(2,1)S(1)} %bitcast.7, bf16[64,4096]{1,0:T(8,128)(2,1)S(1)} %collective-permute-done.7.send_ref, bf16[72,4608]{1,0:T(8,128)(2,1)S(1)} %reshape.11.refs_0_.refs_2_, ...), custom_call_target="tpu_custom_call" | custom-call | tf_op jit(solution)/shard_map/pallas_call | solution.py:470
  87.6 1.3 collective-permute-start.16
  89.0 7.1 %collective-permute-done.16.refs_1_ = f32[128,720]{1,0:T(8,128)S(1)} collective-permute-done((f32[128,720]{1,0:T(8,128)S(1)}, f32[128,720]{1,0:T(8,128)S(1)}, u32[]{:S(2)}, u32[]{:S(2)}) %collective-permute-start.16) | collective-permute-done | bytes 368672 | tf_op jit(solution)/shard_map/ppermute | solution.py:412
  96.0 3.6 %shard_map.111 = (f32[64,4608]{1,0:T(8,128)S(1)}, f32[64,4608]{1,0:T(8,128)S(1)}) custom-call(s32[4]{0:T(128)S(1)} %copy-done.10, f32[128,720]{1,0:T(8,128)S(1)} %shard_map.109.refs_0_, f32[128,720]{1,0:T(8,128)S(1)} %collective-permute-done.16.refs_1_, bf16[72,4608]{1,0:T(8,128)(2,1)S(1)} %reshape.11.refs_0_.refs_2_, ...), custom_call_target="tpu_custom_call" | custom-call | tf_op jit(solution)/shard_map/pallas_call | solution.py:479
  99.6 3.4 %shard_map.110 = (f32[64,4096]{1,0:T(8,128)S(1)}, f32[64,4096]{1,0:T(8,128)S(1)}) custom-call(s32[4]{0:T(128)S(1)} %copy-done.10, f32[128,720]{1,0:T(8,128)S(1)} %shard_map.109.refs_0_, f32[128,720]{1,0:T(8,128)S(1)} %collective-permute-done.16.refs_1_, bf16[72,4096]{1,0:T(8,128)(2,1)} %refs_2_.1, bf16[72,4096]{1,0:T(8,128)(2,1)} %collective-permute-done.3.refs_6_.refs_3_, ...), custom_call_target="tpu_custom_call" | custom-call | tf_op jit(solution)/shard_map/pallas_call | solution.py:479
  103.0 2.7 %collective-permute-done.11.refs_2_ = bf16[72,4096]{1,0:T(8,128)(2,1)S(1)} collective-permute-done((bf16[72,4096]{1,0:T(8,128)(2,1)}, bf16[72,4096]{1,0:T(8,128)(2,1)S(1)}, u32[]{:S(2)}, u32[]{:S(2)}) %collective-permute-start.11) | collective-permute-done | bytes 589856 | tf_op jit(solution)/shard_map/ppermute | solution.py:426
  105.7 0.4 collective-permute-done.15.refs_3_
  106.1 3.4 %collective-permute-start.17 = (bf16[72,4608]{1,0:T(8,128)(2,1)S(1)}, bf16[72,4608]{1,0:T(8,128)(2,1)S(1)}, u32[]{:S(2)}, u32[]{:S(2)}) collective-permute-start(bf16[72,4608]{1,0:T(8,128)(2,1)S(1)} %collective-permute-done.9.refs_0_.refs_2_), channel_id=1, source_target_pairs={{0,8},{2,10},{8,16},{10,18},{16,24},{18,26},{24,28},{26,30},{28,20... | collective-permute-start | bytes 1990664 | tf_op jit(solution)/shard_map/ppermute | solution.py:426
  109.5 1.4 shard_map.113.refs_0_
  110.9 1.3 collective-permute-start.20
  112.2 11.1 %collective-permute-done.18.refs_1_.refs_2_ = bf16[72,4096]{1,0:T(8,128)(2,1)S(1)} collective-permute-done((bf16[72,4096]{1,0:T(8,128)(2,1)S(1)}, bf16[72,4096]{1,0:T(8,128)(2,1)S(1)}, u32[]{:S(2)}, u32[]{:S(2)}) %collective-permute-start.18) | collective-permute-done | bytes 589856 | tf_op jit(solution)/shard_map/ppermute | solution.py:426
  123.3 0.8 shard_map.112.refs_0_
  124.1 1.3 collective-permute-start.19
  125.4 1.7 %shard_map.116 = (f32[64,4608]{1,0:T(8,128)S(1)}, f32[64,4608]{1,0:T(8,128)S(1)}) custom-call(s32[4]{0:T(128)S(1)} %copy-done.10, f32[128,288]{1,0:T(8,128)S(1)} %shard_map.113.refs_0_, f32[128,288]{1,0:T(8,128)S(1)} %collective-permute-done.20.refs_1_, bf16[72,4608]{1,0:T(8,128)(2,1)S(1)} %collective-permute-done.9.refs_0_.refs_2_, ...), custom_call_target="tpu_custom_call" | custom-call | tf_op jit(solution)/shard_map/pallas_call | solution.py:479
  127.1 0.9 collective-permute-done.19.refs_1_
  128.0 1.3 shard_map.117
  129.3 3.2 %collective-permute-start.21 = (f32[64,4608]{1,0:T(8,128)S(1)}, f32[64,4608]{1,0:T(8,128)S(1)}, u32[]{:S(2)}, u32[]{:S(2)}) collective-permute-start(f32[64,4608]{1,0:T(8,128)S(1)} %get-tuple-element.69), channel_id=1, source_target_pairs={{0,2},{2,0},{4,6},{6,4},{8,10},{10,8},{12,14},{14,12},{16,18},{18,... | collective-permute-start | bytes 3538952 | tf_op jit(solution)/shard_map/ppermute | solution.py:404
  132.5 1.3 shard_map.114
  133.8 1.0 shard_map.115
  134.8 0.2 collective-permute-done.21.mate_ref
  134.9 2.1 %shard_map.118 = (bf16[256,576]{1,0:T(8,128)(2,1)S(1)}, f32[256,576]{1,0:T(8,128)S(1)}) custom-call(s32[4]{0:T(128)S(1)} %copy-done.10, f32[64,4608]{1,0:T(8,128)S(1)} %get-tuple-element.68.own_ref, f32[64,4608]{1,0:T(8,128)S(1)} %collective-permute-done.21.mate_ref), custom_call_target="tpu_custom_call" | custom-call | tf_op jit(solution)/shard_map/pallas_call | solution.py:350
  137.1 0.4 collective-permute-start.22
  137.5 2.0 %collective-permute-start.23 = (bf16[256,576]{1,0:T(8,128)(2,1)S(1)}, bf16[256,576]{1,0:T(8,128)(2,1)S(1)}, u32[]{:S(2)}, u32[]{:S(2)}) collective-permute-start(bf16[256,576]{1,0:T(8,128)(2,1)S(1)} %get-tuple-element.73), channel_id=1, source_target_pairs={{2,0},{4,2},{6,4},{8,6},{10,8},{12,10},{14,12},{16,14},{18,16},{20... | collective-permute-start | bytes 884744 | tf_op jit(solution)/shard_map/ppermute | solution.py:387
  139.5 0.2 collective-permute-done.22
  139.8 0.9 add_convert_fusion
  140.7 6.1 %collective-permute-done.23.odd_ref = bf16[256,576]{1,0:T(8,128)(2,1)S(1)} collective-permute-done((bf16[256,576]{1,0:T(8,128)(2,1)S(1)}, bf16[256,576]{1,0:T(8,128)(2,1)S(1)}, u32[]{:S(2)}, u32[]{:S(2)}) %collective-permute-start.23) | collective-permute-done | bytes 294944 | tf_op jit(solution)/shard_map/ppermute | solution.py:387
  146.8 4.1 %all-to-all-start.1 = ((bf16[8,8,4096]{2,1,0:T(8,128)(2,1)}), bf16[8,8,4096]{2,1,0:T(8,128)(2,1)S(1)}, u32[]{:S(2)}, u32[]{:S(2)}) async-start(bf16[8,8,4096]{2,1,0:T(8,128)(2,1)} %bitcast.4), calls=%async_computation.1 | async-start | bytes 1048576 | tf_op jit(solution)/shard_map/all_to_all | solution.py:491
  150.9 0.9 shard_map.119
  151.8 1.3 collective-permute-start.24
  153.0 1.5 collective-permute-done.24
  154.6 4.5 %shard_map.120 = bf16[2,196,576]{2,1,0:T(8,128)(2,1)S(1)} custom-call(f32[256,576]{1,0:T(8,128)S(1)} %get-tuple-element.75.even_ref, bf16[256,576]{1,0:T(8,128)(2,1)S(1)} %collective-permute-done.23.odd_ref, f32[512,576]{1,0:T(8,128)S(1)} %get-tuple-element.40.conv_ref, f32[2,576]{1,0:T(2,128)S(1)} %get-tuple-element.77.excite_ref, f32[2,288]{1,0:T(2,128)S(1)} %add.9.sq_ref, ...), custom_call_target="tpu_custom_call" | custom-call | flops 2717908992 | bytes 4718592 | tf_op jit(solution)/shard_map/pallas_call | solution.py:371
  159.0 1.2 copy.12
  160.2 4.9 %all-to-all-done.1 = bf16[8,8,4096]{2,1,0:T(8,128)(2,1)S(1)} async-done(((bf16[8,8,4096]{2,1,0:T(8,128)(2,1)}), bf16[8,8,4096]{2,1,0:T(8,128)(2,1)S(1)}, u32[]{:S(2)}, u32[]{:S(2)}) %all-to-all-start.1) | async-done | bytes 524320 | tf_op jit(solution)/shard_map/all_to_all | solution.py:491
  165.1 0.8 copy.14
  (38 shorter events, 0.2 us)
Async XLA Ops:
  0.6 4.8 %copy-start.11 = (bf16[2,196,576]{2,0,1:T(2,128)(2,1)S(1)}, bf16[2,196,576]{2,0,1:T(2,128)(2,1)}, u32[]{:S(2)}) copy-start(bf16[2,196,576]{2,0,1:T(2,128)(2,1)} %param.9) | copy-start | bytes 1354756
  0.6 4.8 %copy-start.5 = (bf16[576,288]{0,1:T(8,128)(2,1)S(1)}, bf16[576,288]{0,1:T(8,128)(2,1)}, u32[]{:S(2)}) copy-start(bf16[576,288]{0,1:T(8,128)(2,1)} %param.11) | copy-start | bytes 995332
  2.4 3.1 %copy-start.3 = (bf16[9,576,48]{1,2,0:T(8,128)(2,1)S(1)}, bf16[9,576,48]{1,2,0:T(8,128)(2,1)}, u32[]{:S(2)}) copy-start(bf16[9,576,48]{1,2,0:T(8,128)(2,1)} %param.10) | copy-start | bytes 1492996
  2.4 40.8 %collective-permute-start.4 = (bf16[72,4608]{1,0:T(8,128)(2,1)S(1)}, bf16[72,4608]{1,0:T(8,128)(2,1)S(1)}, u32[]{:S(2)}, u32[]{:S(2)}) collective-permute-start(bf16[72,4608]{1,0:T(8,128)(2,1)S(1)} %reshape.11.refs_0_.refs_2_), channel_id=1, source_target_pairs={{0,4},{2,6},{8,0},{10,2},{16,8},{18,10},{24,16},{26,18},{28,24},{3... | collective-permute-start | bytes 1990664 | tf_op jit(solution)/shard_map/ppermute | solution.py:426
  3.7 39.4 %collective-permute-start.2 = (bf16[72,4608]{1,0:T(8,128)(2,1)S(1)}, bf16[72,4608]{1,0:T(8,128)(2,1)}, u32[]{:S(2)}, u32[]{:S(2)}) collective-permute-start(bf16[72,4608]{1,0:T(8,128)(2,1)S(1)} %reshape.11.refs_0_.refs_2_), channel_id=1, source_target_pairs={{0,8},{2,10},{8,16},{10,18},{16,24},{18,26},{24,28},{26,30},{28,20... | collective-permute-start | bytes 1990664 | tf_op jit(solution)/shard_map/ppermute | solution.py:426
  3.9 39.2 %collective-permute-start.5 = (bf16[72,4096]{1,0:T(8,128)(2,1)}, bf16[72,4096]{1,0:T(8,128)(2,1)}, u32[]{:S(2)}, u32[]{:S(2)}) collective-permute-start(bf16[72,4096]{1,0:T(8,128)(2,1)} %refs_2_.1), channel_id=1, source_target_pairs={{0,4},{2,6},{8,0},{10,2},{16,8},{18,10},{24,16},{26,18},{28,24},{3... | collective-permute-start | bytes 1769480 | tf_op jit(solution)/shard_map/ppermute | solution.py:426
  5.2 38.0 %collective-permute-start.3 = (bf16[72,4096]{1,0:T(8,128)(2,1)}, bf16[72,4096]{1,0:T(8,128)(2,1)}, u32[]{:S(2)}, u32[]{:S(2)}) collective-permute-start(bf16[72,4096]{1,0:T(8,128)(2,1)} %refs_2_.1), channel_id=1, source_target_pairs={{0,8},{2,10},{8,16},{10,18},{16,24},{18,26},{24,28},{26,30},{28,20... | collective-permute-start | bytes 1769480 | tf_op jit(solution)/shard_map/ppermute | solution.py:426
  5.5 14.0 %copy-start = (bf16[288,576]{1,0:T(8,128)(2,1)S(1)}, bf16[288,576]{1,0:T(8,128)(2,1)}, u32[]{:S(2)}) copy-start(bf16[288,576]{1,0:T(8,128)(2,1)} %expand_ref.3) | copy-start | bytes 995332
  9.9 0.9 copy-start.1
  10.8 41.8 %all-to-all-start = ((bf16[8,8,4096]{2,1,0:T(8,128)(2,1)}), bf16[8,8,4096]{2,1,0:T(8,128)(2,1)S(1)}, u32[]{:S(2)}, u32[]{:S(2)}) async-start(bf16[8,8,4096]{2,1,0:T(8,128)(2,1)} %bitcast.15), calls=%async_computation | async-start | bytes 1048576 | tf_op jit(solution)/shard_map/all_to_all | solution.py:491
  16.6 2.8 %collective-permute-start = (f32[2,288]{1,0:T(2,128)S(1)}, f32[2,288]{1,0:T(2,128)S(1)}, u32[]{:S(2)}, u32[]{:S(2)}) collective-permute-start(f32[2,288]{1,0:T(2,128)S(1)} %get-tuple-element.43), channel_id=1, source_target_pairs={{0,1},{1,0},{2,3},{3,2},{4,5},{5,4},{6,7},{7,6},{8,9},{9,8},{10,11... | collective-permute-start | bytes 6920 | tf_op jit(solution)/shard_map/ppermute | solution.py:412
  19.5 1.1 copy-start.2
  22.0 0.7 copy-start.7
  22.8 20.4 %collective-permute-start.1 = (bf16[256,576]{1,0:T(8,128)(2,1)}, bf16[256,576]{1,0:T(8,128)(2,1)}, u32[]{:S(2)}, u32[]{:S(2)}) collective-permute-start(bf16[256,576]{1,0:T(8,128)(2,1)} %get-tuple-element.44), channel_id=1, source_target_pairs={{0,2},{2,4},{4,6},{6,8},{8,10},{10,12},{12,14},{14,16},{16,18},{18... | collective-permute-start | bytes 884744 | tf_op jit(solution)/shard_map/ppermute | solution.py:387
  30.1 50.3 %copy-start.10 = (s32[4]{0:T(128)S(1)}, s32[4]{0:T(128)}, u32[]{:S(2)}) copy-start(s32[4]{0:T(128)} %shard_map.104.facts_ref) | copy-start | bytes 52
  43.2 1.0 copy-start.8
  44.2 0.7 copy-start.9
  47.1 5.6 %collective-permute-start.6 = (bf16[64,4608]{1,0:T(8,128)(2,1)}, bf16[64,4608]{1,0:T(8,128)(2,1)}, u32[]{:S(2)}, u32[]{:S(2)}) collective-permute-start(bf16[64,4608]{1,0:T(8,128)(2,1)} %shard_map.107.own_ref), channel_id=1, source_target_pairs={{0,2},{2,0},{4,6},{6,4},{8,10},{10,8},{12,14},{14,12},{16,18},{18,... | collective-permute-start | bytes 1769480 | tf_op jit(solution)/shard_map/ppermute | solution.py:404
  47.1 19.2 %collective-permute-start.8 = (bf16[72,4608]{1,0:T(8,128)(2,1)}, bf16[72,4608]{1,0:T(8,128)(2,1)}, u32[]{:S(2)}, u32[]{:S(2)}) collective-permute-start(bf16[72,4608]{1,0:T(8,128)(2,1)} %collective-permute-done.2.refs_1_.refs_3_), channel_id=1, source_target_pairs={{0,8},{2,10},{8,16},{10,18},{16,24},{18,26},{24,28},{26,30},{28,20... | collective-permute-start | bytes 1990664 | tf_op jit(solution)/shard_map/ppermute | solution.py:426
  47.1 19.7 %collective-permute-start.12 = (bf16[72,4608]{1,0:T(8,128)(2,1)S(1)}, bf16[72,4608]{1,0:T(8,128)(2,1)}, u32[]{:S(2)}, u32[]{:S(2)}) collective-permute-start(bf16[72,4608]{1,0:T(8,128)(2,1)S(1)} %collective-permute-done.4.refs_2_.refs_4_), channel_id=1, source_target_pairs={{0,4},{2,6},{8,0},{10,2},{16,8},{18,10},{24,16},{26,18},{28,24},{3... | collective-permute-start | bytes 1990664 | tf_op jit(solution)/shard_map/ppermute | solution.py:426
  51.2 27.8 %collective-permute-start.10 = (bf16[72,4096]{1,0:T(8,128)(2,1)}, bf16[72,4096]{1,0:T(8,128)(2,1)}, u32[]{:S(2)}, u32[]{:S(2)}) collective-permute-start(bf16[72,4096]{1,0:T(8,128)(2,1)} %collective-permute-done.3.refs_6_.refs_3_), channel_id=1, source_target_pairs={{0,8},{2,10},{8,16},{10,18},{16,24},{18,26},{24,28},{26,30},{28,20... | collective-permute-start | bytes 1769480 | tf_op jit(solution)/shard_map/ppermute | solution.py:426
  51.6 27.8 %collective-permute-start.14 = (bf16[72,4096]{1,0:T(8,128)(2,1)}, bf16[72,4096]{1,0:T(8,128)(2,1)}, u32[]{:S(2)}, u32[]{:S(2)}) collective-permute-start(bf16[72,4096]{1,0:T(8,128)(2,1)} %collective-permute-done.5.refs_7_.refs_4_), channel_id=1, source_target_pairs={{0,4},{2,6},{8,0},{10,2},{16,8},{18,10},{24,16},{26,18},{28,24},{3... | collective-permute-start | bytes 1769480 | tf_op jit(solution)/shard_map/ppermute | solution.py:426
  52.7 29.5 %collective-permute-start.7 = (bf16[64,4096]{1,0:T(8,128)(2,1)S(1)}, bf16[64,4096]{1,0:T(8,128)(2,1)S(1)}, u32[]{:S(2)}, u32[]{:S(2)}) collective-permute-start(bf16[64,4096]{1,0:T(8,128)(2,1)S(1)} %bitcast.6), channel_id=1, source_target_pairs={{0,2},{2,0},{4,6},{6,4},{8,10},{10,8},{12,14},{14,12},{16,18},{18,... | collective-permute-start | bytes 1572872 | tf_op jit(solution)/shard_map/ppermute | solution.py:404
  66.3 39.8 %collective-permute-start.9 = (bf16[72,4608]{1,0:T(8,128)(2,1)}, bf16[72,4608]{1,0:T(8,128)(2,1)S(1)}, u32[]{:S(2)}, u32[]{:S(2)}) collective-permute-start(bf16[72,4608]{1,0:T(8,128)(2,1)} %collective-permute-done.8.refs_3_.refs_5_), channel_id=1, source_target_pairs={{0,8},{2,10},{8,16},{10,18},{16,24},{18,26},{24,28},{26,30},{28,20... | collective-permute-start | bytes 1990664 | tf_op jit(solution)/shard_map/ppermute | solution.py:426
  66.7 39.4 %collective-permute-start.13 = (bf16[72,4608]{1,0:T(8,128)(2,1)}, bf16[72,4608]{1,0:T(8,128)(2,1)S(1)}, u32[]{:S(2)}, u32[]{:S(2)}) collective-permute-start(bf16[72,4608]{1,0:T(8,128)(2,1)} %collective-permute-done.12.refs_4_.refs_6_), channel_id=1, source_target_pairs={{0,4},{2,6},{8,0},{10,2},{16,8},{18,10},{24,16},{26,18},{28,24},{3... | collective-permute-start | bytes 1990664 | tf_op jit(solution)/shard_map/ppermute | solution.py:426
  79.0 26.8 %collective-permute-start.11 = (bf16[72,4096]{1,0:T(8,128)(2,1)}, bf16[72,4096]{1,0:T(8,128)(2,1)S(1)}, u32[]{:S(2)}, u32[]{:S(2)}) collective-permute-start(bf16[72,4096]{1,0:T(8,128)(2,1)} %collective-permute-done.10.refs_8_.refs_5_), channel_id=1, source_target_pairs={{0,8},{2,10},{8,16},{10,18},{16,24},{18,26},{24,28},{26,30},{28,20... | collective-permute-start | bytes 1769480 | tf_op jit(solution)/shard_map/ppermute | solution.py:426
  79.4 26.8 %collective-permute-start.15 = (bf16[72,4096]{1,0:T(8,128)(2,1)}, bf16[72,4096]{1,0:T(8,128)(2,1)S(1)}, u32[]{:S(2)}, u32[]{:S(2)}) collective-permute-start(bf16[72,4096]{1,0:T(8,128)(2,1)} %collective-permute-done.14.refs_9_.refs_6_), channel_id=1, source_target_pairs={{0,4},{2,6},{8,0},{10,2},{16,8},{18,10},{24,16},{26,18},{28,24},{3... | collective-permute-start | bytes 1769480 | tf_op jit(solution)/shard_map/ppermute | solution.py:426
  87.6 8.4 %collective-permute-start.16 = (f32[128,720]{1,0:T(8,128)S(1)}, f32[128,720]{1,0:T(8,128)S(1)}, u32[]{:S(2)}, u32[]{:S(2)}) collective-permute-start(f32[128,720]{1,0:T(8,128)S(1)} %shard_map.109.refs_0_), channel_id=1, source_target_pairs={{0,1},{1,0},{2,3},{3,2},{4,5},{5,4},{6,7},{7,6},{8,9},{9,8},{10,11... | collective-permute-start | bytes 1105928 | tf_op jit(solution)/shard_map/ppermute | solution.py:412
  106.1 17.2 %collective-permute-start.17 = (bf16[72,4608]{1,0:T(8,128)(2,1)S(1)}, bf16[72,4608]{1,0:T(8,128)(2,1)S(1)}, u32[]{:S(2)}, u32[]{:S(2)}) collective-permute-start(bf16[72,4608]{1,0:T(8,128)(2,1)S(1)} %collective-permute-done.9.refs_0_.refs_2_), channel_id=1, source_target_pairs={{0,8},{2,10},{8,16},{10,18},{16,24},{18,26},{24,28},{26,30},{28,20... | collective-permute-start | bytes 1990664 | tf_op jit(solution)/shard_map/ppermute | solution.py:426
  109.5 13.8 %collective-permute-start.18 = (bf16[72,4096]{1,0:T(8,128)(2,1)S(1)}, bf16[72,4096]{1,0:T(8,128)(2,1)S(1)}, u32[]{:S(2)}, u32[]{:S(2)}) collective-permute-start(bf16[72,4096]{1,0:T(8,128)(2,1)S(1)} %collective-permute-done.15.refs_3_), channel_id=1, source_target_pairs={{0,4},{2,6},{8,0},{10,2},{16,8},{18,10},{24,16},{26,18},{28,24},{3... | collective-permute-start | bytes 1769480 | tf_op jit(solution)/shard_map/ppermute | solution.py:426
  110.9 14.5 %collective-permute-start.20 = (f32[128,288]{1,0:T(8,128)S(1)}, f32[128,288]{1,0:T(8,128)S(1)}, u32[]{:S(2)}, u32[]{:S(2)}) collective-permute-start(f32[128,288]{1,0:T(8,128)S(1)} %shard_map.113.refs_0_), channel_id=1, source_target_pairs={{0,1},{1,0},{2,3},{3,2},{4,5},{5,4},{6,7},{7,6},{8,9},{9,8},{10,11... | collective-permute-start | bytes 442376 | tf_op jit(solution)/shard_map/ppermute | solution.py:412
  124.1 3.9 %collective-permute-start.19 = (f32[128,144]{1,0:T(8,128)S(1)}, f32[128,144]{1,0:T(8,128)S(1)}, u32[]{:S(2)}, u32[]{:S(2)}) collective-permute-start(f32[128,144]{1,0:T(8,128)S(1)} %shard_map.112.refs_0_), channel_id=1, source_target_pairs={{0,1},{1,0},{2,3},{3,2},{4,5},{5,4},{6,7},{7,6},{8,9},{9,8},{10,11... | collective-permute-start | bytes 221192 | tf_op jit(solution)/shard_map/ppermute | solution.py:412
  129.3 5.7 %collective-permute-start.21 = (f32[64,4608]{1,0:T(8,128)S(1)}, f32[64,4608]{1,0:T(8,128)S(1)}, u32[]{:S(2)}, u32[]{:S(2)}) collective-permute-start(f32[64,4608]{1,0:T(8,128)S(1)} %get-tuple-element.69), channel_id=1, source_target_pairs={{0,2},{2,0},{4,6},{6,4},{8,10},{10,8},{12,14},{14,12},{16,18},{18,... | collective-permute-start | bytes 3538952 | tf_op jit(solution)/shard_map/ppermute | solution.py:404
  137.1 2.7 %collective-permute-start.22 = (f32[64,4096]{1,0:T(8,128)S(1)}, f32[64,4096]{1,0:T(8,128)S(1)}, u32[]{:S(2)}, u32[]{:S(2)}) collective-permute-start(f32[64,4096]{1,0:T(8,128)S(1)} %get-tuple-element.72), channel_id=1, source_target_pairs={{0,2},{2,0},{4,6},{6,4},{8,10},{10,8},{12,14},{14,12},{16,18},{18,... | collective-permute-start | bytes 3145736 | tf_op jit(solution)/shard_map/ppermute | solution.py:404
  137.5 9.3 %collective-permute-start.23 = (bf16[256,576]{1,0:T(8,128)(2,1)S(1)}, bf16[256,576]{1,0:T(8,128)(2,1)S(1)}, u32[]{:S(2)}, u32[]{:S(2)}) collective-permute-start(bf16[256,576]{1,0:T(8,128)(2,1)S(1)} %get-tuple-element.73), channel_id=1, source_target_pairs={{2,0},{4,2},{6,4},{8,6},{10,8},{12,10},{14,12},{16,14},{18,16},{20... | collective-permute-start | bytes 884744 | tf_op jit(solution)/shard_map/ppermute | solution.py:387
  146.8 18.3 %all-to-all-start.1 = ((bf16[8,8,4096]{2,1,0:T(8,128)(2,1)}), bf16[8,8,4096]{2,1,0:T(8,128)(2,1)S(1)}, u32[]{:S(2)}, u32[]{:S(2)}) async-start(bf16[8,8,4096]{2,1,0:T(8,128)(2,1)} %bitcast.4), calls=%async_computation.1 | async-start | bytes 1048576 | tf_op jit(solution)/shard_map/all_to_all | solution.py:491
  150.9 3.7 %copy-start.4 = (bf16[9,576,48]{1,2,0:T(8,128)(2,1)S(1)}, bf16[9,576,48]{1,2,0:T(8,128)(2,1)}, u32[]{:S(2)}) copy-start(bf16[9,576,48]{1,2,0:T(8,128)(2,1)} %param.10) | copy-start | bytes 1492996
  150.9 3.7 %copy-start.6 = (bf16[576,288]{0,1:T(8,128)(2,1)S(1)}, bf16[576,288]{0,1:T(8,128)(2,1)}, u32[]{:S(2)}) copy-start(bf16[576,288]{0,1:T(8,128)(2,1)} %param.11) | copy-start | bytes 995332
  151.8 2.8 %collective-permute-start.24 = (f32[2,288]{1,0:T(2,128)S(1)}, f32[2,288]{1,0:T(2,128)S(1)}, u32[]{:S(2)}, u32[]{:S(2)}) collective-permute-start(f32[2,288]{1,0:T(2,128)S(1)} %shard_map.119), channel_id=1, source_target_pairs={{0,1},{1,0},{2,3},{3,2},{4,5},{5,4},{6,7},{7,6},{8,9},{9,8},{10,11... | collective-permute-start | bytes 6920 | tf_op jit(solution)/shard_map/ppermute | solution.py:412

commit v3 on v2

--- a/solution.py
+++ b/solution.py
@@ -94,7 +94,8 @@
         shift_ref[col] = wide_ref[at : at + rows, :].astype(jnp.bfloat16)
 
 
-def conv_kernel(feat_ref, group_ref, squeeze_ref, conv_ref, pad_ref, sq_ref, flat_ref, wide_ref, shift_ref):
+def conv_kernel(feat_ref, group_ref, squeeze_ref, *refs):
+    conv_ref, pad_ref, sq_ref, *dense_refs, flat_ref, wide_ref, shift_ref = refs
     frames, _, chans = feat_ref.shape
     width = group_ref.shape[1]
     rows = frames * FRAME_ROWS
@@ -108,13 +109,14 @@
     pad_ref[...] = shift_ref[1]
     conv_ref[...] = jnp.zeros_like(conv_ref)
     body = rows - 2 * WIDE
-    for block in channel_blocks(chans, width):
+    for block, dense_ref in zip(channel_blocks(chans, width), dense_refs):
         _, _, start, end = block
         spread, same = block_tools(block, width)
         total = jnp.zeros((body, end - start), jnp.float32)
         for tap in range(9):
             down, across = divmod(tap, 3)
             weights = dense_tap(group_ref, tap, block, spread, same)
+            dense_ref[tap] = weights
             source = shift_ref[across, down * WIDE : down * WIDE + body, start:end]
             total += contract_last(source, weights)
         conv_ref[WIDE : WIDE + body, start:end] += total
@@ -131,17 +133,23 @@
     sq_ref[...] = contract_exact(pooled, squeeze_ref[...].astype(jnp.float32))
 
 
-def hidden_kernel(conv_ref, pad_ref, sq_ref, expand_ref, even_ref, odd_ref, excite_ref):
+def hidden_kernel(
+    conv_ref, pad_ref, sq_ref, expand_ref, even_ref, odd_ref, excite_ref, active_ref, slope_ref
+):
     squeezed = sq_ref[...]
     relaxed = squeezed * jax.nn.sigmoid(squeezed)
     excite = jax.nn.sigmoid(
         jnp.dot(relaxed, expand_ref[...].astype(jnp.float32), precision=lax.Precision.HIGHEST)
     )
     excite_ref[...] = excite
+    good = inside(FRAME_ROWS)
     for frame, out_ref in enumerate((even_ref, odd_ref)):
         rows = slice(frame * FRAME_ROWS, (frame + 1) * FRAME_ROWS)
         conv = conv_ref[rows, :]
-        active = conv * jax.nn.sigmoid(conv)
+        sigma = jax.nn.sigmoid(conv)
+        active = conv * sigma
+        active_ref[rows, :] = active
+        slope_ref[rows, :] = sigma * (1.0 + conv * (1.0 - sigma)) * good
         hidden = pad_ref[rows, :].astype(jnp.float32) + active * excite[frame : frame + 1]
         out_ref[...] = hidden.astype(jnp.bfloat16)
 
@@ -226,11 +234,10 @@
     even_ref[...] = frames[1] * good
 
 
-def excite_grad_kernel(even_ref, odd_ref, conv_ref, excite_ref, expand_ref, out_ref):
+def excite_grad_kernel(even_ref, odd_ref, active_ref, excite_ref, expand_ref, out_ref):
     sums = []
     for frame, grad_ref in enumerate((even_ref, odd_ref)):
-        conv = conv_ref[frame * FRAME_ROWS : (frame + 1) * FRAME_ROWS, :]
-        active = conv * jax.nn.sigmoid(conv)
+        active = active_ref[frame * FRAME_ROWS : (frame + 1) * FRAME_ROWS, :]
         sums.append(jnp.sum(grad_ref[...].astype(jnp.float32) * active, axis=0, keepdims=True))
     excite = excite_ref[...]
     inner = jnp.concatenate(sums, axis=0) * excite * (1.0 - excite)
@@ -238,11 +245,10 @@
 
 
 def conv_grad_kernel(
-    even_ref, odd_ref, conv_ref, excite_ref, sq_ref, relaxed_ref, squeeze_ref, group_ref,
-    out_ref, flat_ref, wide_ref, shift_ref, grad_ref,
+    width, even_ref, odd_ref, slope_ref, excite_ref, sq_ref, relaxed_ref, squeeze_ref, *refs
 ):
+    *dense_refs, out_ref, flat_ref, wide_ref, shift_ref, grad_ref = refs
     frames, _, chans = out_ref.shape
-    width = group_ref.shape[1]
     rows = frames * FRAME_ROWS
     grad_squeezed = relaxed_ref[...] * silu_slope(sq_ref[...])
     pooled = jnp.dot(
@@ -250,26 +256,23 @@
     ) * (1.0 / (SIDE * SIDE))
     wide_ref[0:EDGE, :] = jnp.zeros((EDGE, chans), jnp.float32)
     wide_ref[EDGE + rows :, :] = jnp.zeros((EDGE, chans), jnp.float32)
-    good = inside(FRAME_ROWS)
     for frame, source in enumerate((even_ref, odd_ref)):
         at = frame * FRAME_ROWS
         grad = source[...].astype(jnp.float32)
         grad_ref[at : at + FRAME_ROWS, :] = grad
         active = grad * excite_ref[frame : frame + 1, :] + pooled[frame : frame + 1]
-        slope = silu_slope(conv_ref[at : at + FRAME_ROWS, :])
-        wide_ref[EDGE + at : EDGE + at + FRAME_ROWS, :] = active * slope * good
+        slope = slope_ref[at : at + FRAME_ROWS, :]
+        wide_ref[EDGE + at : EDGE + at + FRAME_ROWS, :] = active * slope
     store_shifts(wide_ref, shift_ref, -1)
     body = rows - 2 * WIDE
-    for block in channel_blocks(chans, width):
+    for block, dense_ref in zip(channel_blocks(chans, width), dense_refs):
         _, _, start, end = block
-        spread, same = block_tools(block, width)
         total = jnp.zeros((body, end - start), jnp.float32)
         for tap in range(9):
             down, across = divmod(tap, 3)
-            weights = dense_tap(group_ref, tap, block, spread, same)
             at = (2 - down) * WIDE
             source = shift_ref[across, at : at + body, start:end]
-            total += jnp.dot(source, weights, preferred_element_type=jnp.float32)
+            total += jnp.dot(source, dense_ref[tap], preferred_element_type=jnp.float32)
         grad_ref[WIDE : WIDE + body, start:end] += total
     for frame in range(frames):
         for y in range(SIDE):
@@ -291,7 +294,11 @@
     rows = frames * FRAME_ROWS
     return whole_call(
         conv_kernel,
-        (f32(rows, chans), bf16(rows, chans), f32(frames, squeeze_in.shape[0])),
+        (f32(rows, chans), bf16(rows, chans), f32(frames, squeeze_in.shape[0]))
+        + tuple(
+            bf16(9, end - start, end - start)
+            for _, _, start, end in channel_blocks(chans, group_kernel.shape[1])
+        ),
         [
             pltpu.VMEM((cells, chans), jnp.float32),
             pltpu.VMEM((rows + 2 * EDGE, chans), jnp.float32),
@@ -304,7 +311,8 @@
     rows, chans = conv.shape
     return whole_call(
         hidden_kernel,
-        (bf16(FRAME_ROWS, chans), bf16(FRAME_ROWS, chans), f32(rows // FRAME_ROWS, chans)),
+        (bf16(FRAME_ROWS, chans),) * 2
+        + (f32(rows // FRAME_ROWS, chans), f32(rows, chans), f32(rows, chans)),
         [],
     )(conv, padded, squeezed, squeeze_out)
 
@@ -356,20 +364,20 @@
     )(facts, own, mate)
 
 
-def excite_grad(even, odd, conv, excite, squeeze_out):
-    rows, chans = conv.shape
+def excite_grad(even, odd, active, excite, squeeze_out):
+    rows, chans = active.shape
     return whole_call(
         excite_grad_kernel,
         f32(rows // FRAME_ROWS, squeeze_out.shape[0]),
         [],
-    )(even, odd, conv, excite, squeeze_out)
-
-
-def conv_backward(even, odd, conv, excite, squeezed, grad_relaxed, squeeze_in, group_kernel):
-    rows, chans = conv.shape
+    )(even, odd, active, excite, squeeze_out)
+
+
+def conv_backward(even, odd, slope, excite, squeezed, grad_relaxed, squeeze_in, dense, width):
+    rows, chans = slope.shape
     frames = rows // FRAME_ROWS
     return whole_call(
-        conv_grad_kernel,
+        functools.partial(conv_grad_kernel, width),
         bf16(frames, SIDE * SIDE, chans),
         [
             pltpu.VMEM((SIDE * SIDE, chans), jnp.float32),
@@ -378,7 +386,7 @@
             pltpu.VMEM((rows, chans), jnp.float32),
         ],
         pl.CostEstimate(flops=rows * chans * 9216, bytes_accessed=16 * rows * chans, transcendentals=0),
-    )(even, odd, conv, excite, squeezed, grad_relaxed, squeeze_in, group_kernel)
+    )(even, odd, slope, excite, squeezed, grad_relaxed, squeeze_in, *dense)
 
 
 def shifted(value, axis, by):
@@ -504,7 +512,7 @@
     clip_keep,
     token_cotangent,
 ):
-    chans = features.shape[2]
+    chans, width = features.shape[2], group_kernel.shape[2]
     count = lax.axis_size("ctx")
     steps, unit = count // 4, OUT_SIDE * OUT_SIDE // count
     flat_sampler = sampler_kernel.reshape(sampler_kernel.shape[0], 8 * chans)
@@ -513,20 +521,25 @@
     squeeze_in = squeeze_in.T
     facts = facts_of(frame_clip, clip_keep)
 
-    conv, padded, squeezed = conv_forward(features, group_kernel, squeeze_in)
+    conv, padded, squeezed, *dense = conv_forward(features, group_kernel, squeeze_in)
     token_cotangent, squeezed = tie(token_cotangent, squeezed)
     back = chips_exchange(token_cotangent)
     squeezed = sum_tp(squeezed)
-    even, odd, excite = hidden_frames(conv, padded, squeezed, squeeze_out)
+    even, odd, excite, active, slope = hidden_frames(conv, padded, squeezed, squeeze_out)
     halo = shifted(odd, "ctx", 1)
-    halo, *blocks = tie(halo, *blocks)
-    patches = take_patches(facts, halo, even)
-    patches = order_rows(facts, patches, swap_cores(patches), unit)
-    back = (back, swap_cores(back))
 
     samplers, readouts = [flat_sampler], [readout_kernel]
     tokens = grads = ()
     for step in range(1, steps + 1):
+        if step == 1:
+            *blocks, even = tie(*blocks, even)
+        if step == 2:
+            up_s, up_r, down_s, down_r = blocks
+            halo, up_s, down_s = tie(halo, up_s, down_s)
+            blocks = up_s, up_r, down_s, down_r
+            patches = take_patches(facts, halo, even)
+            patches = order_rows(facts, patches, swap_cores(patches), unit)
+            back = (back, swap_cores(back))
         here = blocks
         if step < steps:
             samplers, readouts = samplers + [here[0], here[2]], readouts + [here[1], here[3]]
@@ -536,7 +549,9 @@
                 here = here[0], None, None, here[3]
             blocks = ring_step(here)
         else:
-            samplers, readouts = samplers + [here[0]], readouts + [here[3]]
+            last_s, last_r, *held = tie(here[0], here[3], *tokens, *grads)
+            tokens, grads = held[:2], held[2:]
+            samplers, readouts = samplers + [last_s], readouts + [last_r]
         if step >= steps - 2:
             sums = tp_terms(partial_sums(patches, back, samplers, readouts))
             tokens = add_products(facts, sums, readouts, tokens, unit, False)
@@ -546,11 +561,11 @@
     token_keep, token_send, lead = tie(*tokens, lead)
     grad_odd = shifted(lead, "ctx", -1)
     tokens = (token_keep + swap_cores(token_send)).astype(jnp.bfloat16)
-    tokens, grad_odd = tie(tokens, grad_odd)
+    tokens, grad_even = tie(tokens, grad_even)
     llm_tokens = chips_exchange(tokens)
-    grad_relaxed = sum_tp(excite_grad(grad_even, grad_odd, conv, excite, squeeze_out))
+    grad_relaxed = sum_tp(excite_grad(grad_even, grad_odd, active, excite, squeeze_out))
     grad_features = conv_backward(
-        grad_even, grad_odd, conv, excite, squeezed, grad_relaxed, squeeze_in, group_kernel
+        grad_even, grad_odd, slope, excite, squeezed, grad_relaxed, squeeze_in, dense, width
     )
     return (llm_tokens, grad_features)
 

time: 168 us -> 170 us (1.012)
  the two profiles are of different devices: /device:TPU:3 before, /device:TPU:15 now
where the time goes in v3:
time: 170 us; the launch traced here: 169 us
  waiting for transfers between devices  83.6 us (49%)
  Pallas kernels  34.4 us (20%)
  starting transfers between devices  32.1 us (19%)
  local copies, waits for them, and re-layouts  16.9 us (10%)
    ppermute x2, waiting for transfers between devices, shifted(): return lax.ppermute(value, axis, pairs)  31.4 us
    ppermute x5, waiting for transfers between devices, tp_terms(): other = lax.ppermute(value, 'tp', [(i, i ^ reach) for i in range(size)])  25.4 us
    ppermute x14, waiting for transfers between devices, ring_step(): lax.ppermute(value, 'ctx', pairs)  22.9 us
    unnamed x57, local copies, waits for them, and re-layouts  15.2 us
    pallas_call x6, Pallas kernels, add_products(): pl.pallas_call(kernel, out_shape=(f32(rows, columns),) * 2, in_specs=vmem...  11.3 us
    ppermute x14, starting transfers between devices, ring_step(): lax.ppermute(value, 'ctx', pairs)  10.2 us
    all_to_all x2, starting transfers between devices, chips_exchange(): lax.all_to_all(value, 'ctx', split_axis=0, concat_axis=0, tiled=True, axi...  9.44 us
    ppermute x2, starting transfers between devices, shifted(): return lax.ppermute(value, axis, pairs)  8.68 us
  transfers between devices with their start and end apart: 27, of which 16 were waited for; matrix products, arithmetic and copies ran while one was open for 1% of the time, Pallas kernels for 18%

profile of v3, /device:TPU:15, one launch (start us, length us, event | category | flops | bytes accessed | tf_op | source)
XLA Modules:
  0.0 168.9 jit_solution(8177311645755046319)
XLA Ops:
  0.7 1.7 %reshape.11.refs_0_.refs_2_ = bf16[72,4608]{1,0:T(8,128)(2,1)S(1)} reshape(bf16[72,8,576]{2,1,0:T(8,128)(2,1)} %param.13) | data formatting | bytes 1327104 | tf_op jit(solution)/shard_map/reshape | solution.py:518
  2.4 1.3 collective-permute-start.4
  3.9 1.3 collective-permute-start.5
  5.4 1.1 copy.11.feat_ref
  6.5 4.5 %shard_map.105 = (f32[512,576]{1,0:T(8,128)S(1)}, bf16[512,576]{1,0:T(8,128)(2,1)S(1)}, f32[2,288]{1,0:T(2,128)S(1)}, bf16[9,256,256]{2,1,0:T(8,128)(2,1)S(1)}, ...) custom-call(bf16[2,196,576]{2,1,0:T(8,128)(2,1)S(1)} %copy.11.feat_ref, ...), custom_call_target="tpu_custom_call" | custom-call | tf_op jit(solution)/shard_map/pallas_call | solution.py:295
  11.0 1.1 copy-done.20
  12.1 1.1 copy-done.22
  13.2 0.9 copy-done.24
  14.3 2.5 %collective-permute-done = f32[2,288]{1,0:T(2,128)S(1)} collective-permute-done((f32[2,288]{1,0:T(2,128)S(1)}, f32[2,288]{1,0:T(2,128)S(1)}, u32[]{:S(2)}, u32[]{:S(2)}) %collective-permute-start) | collective-permute-done | bytes 2336 | tf_op jit(solution)/shard_map/ppermute | solution.py:420
  16.9 1.1 shard_map.106
  18.0 1.1 copy-done.7
  19.1 0.7 copy-done.12
  19.8 0.6 copy-done.16
  20.4 1.1 copy-done.18
  21.5 0.7 copy-done.26
  22.2 8.7 %collective-permute-done.5.refs_7_.refs_4_ = bf16[72,4096]{1,0:T(8,128)(2,1)S(1)} collective-permute-done((bf16[72,4096]{1,0:T(8,128)(2,1)S(1)}, bf16[72,4096]{1,0:T(8,128)(2,1)S(1)}, u32[]{:S(2)}, u32[]{:S(2)}) %collective-permute-start.5) | collective-permute-done | bytes 589856 | tf_op jit(solution)/shard_map/ppermute | solution.py:434
  30.9 1.0 collective-permute-done.3.refs_6_.refs_3_
  32.1 0.6 copy-done.4
  32.7 1.3 collective-permute-start.7
  34.0 4.8 %all-to-all-start = ((bf16[8,8,4096]{2,1,0:T(8,128)(2,1)}), bf16[8,8,4096]{2,1,0:T(8,128)(2,1)S(1)}, u32[]{:S(2)}, u32[]{:S(2)}) async-start(bf16[8,8,4096]{2,1,0:T(8,128)(2,1)} %bitcast.14), calls=%async_computation | async-start | bytes 1048576 | tf_op jit(solution)/shard_map/all_to_all | solution.py:499
  38.9 5.6 %collective-permute-start.1 = (bf16[256,576]{1,0:T(8,128)(2,1)}, bf16[256,576]{1,0:T(8,128)(2,1)}, u32[]{:S(2)}, u32[]{:S(2)}) collective-permute-start(bf16[256,576]{1,0:T(8,128)(2,1)} %copy-done.26), channel_id=1, source_target_pairs={{0,2},{2,4},{4,6},{6,8},{8,10},{10,12},{12,14},{14,16},{16,18},{18... | collective-permute-start | bytes 884744 | tf_op jit(solution)/shard_map/ppermute | solution.py:395
  44.8 1.2 shard_map.104.facts_ref
  46.1 1.2 collective-permute-start.14
  47.3 17.4 %collective-permute-done.1.halo_ref = bf16[256,576]{1,0:T(8,128)(2,1)} collective-permute-done((bf16[256,576]{1,0:T(8,128)(2,1)}, bf16[256,576]{1,0:T(8,128)(2,1)}, u32[]{:S(2)}, u32[]{:S(2)}) %collective-permute-start.1) | collective-permute-done | bytes 294944 | tf_op jit(solution)/shard_map/ppermute | solution.py:395
  64.8 1.0 copy-done.13
  65.7 0.7 copy-done.14
  66.4 2.2 %shard_map.107.own_ref = bf16[64,4608]{1,0:T(8,128)(2,1)} custom-call(s32[4]{0:T(128)S(1)} %copy-done.14, bf16[256,576]{1,0:T(8,128)(2,1)} %collective-permute-done.1.halo_ref, bf16[256,576]{1,0:T(8,128)(2,1)S(1)} %copy-done.13), custom_call_target="tpu_custom_call" | custom-call | tf_op jit(solution)/shard_map/pallas_call | solution.py:348
  68.7 0.6 collective-permute-start.9
  69.2 1.3 collective-permute-done.11.refs_8_.refs_5_
  70.7 6.4 %collective-permute-done.14.refs_9_.refs_6_ = bf16[72,4096]{1,0:T(8,128)(2,1)} collective-permute-done((bf16[72,4096]{1,0:T(8,128)(2,1)}, bf16[72,4096]{1,0:T(8,128)(2,1)}, u32[]{:S(2)}, u32[]{:S(2)}) %collective-permute-start.14) | collective-permute-done | bytes 589856 | tf_op jit(solution)/shard_map/ppermute | solution.py:434
  77.1 2.1 %collective-permute-start.15 = (bf16[72,4096]{1,0:T(8,128)(2,1)}, bf16[72,4096]{1,0:T(8,128)(2,1)S(1)}, u32[]{:S(2)}, u32[]{:S(2)}) collective-permute-start(bf16[72,4096]{1,0:T(8,128)(2,1)} %collective-permute-done.14.refs_9_.refs_6_), channel_id=1, source_target_pairs={{0,4},{2,6},{8,0},{10,2},{16,8},{18,10},{24,16},{26,18},{28,24},{3... | collective-permute-start | bytes 1769480 | tf_op jit(solution)/shard_map/ppermute | solution.py:434
  79.2 1.7 %shard_map.108.patch_ref = bf16[128,4608]{1,0:T(8,128)(2,1)S(1)} custom-call(s32[4]{0:T(128)S(1)} %copy-done.15, bf16[64,4608]{1,0:T(8,128)(2,1)} %shard_map.107.own_ref, bf16[64,4608]{1,0:T(8,128)(2,1)} %collective-permute-done.8.mate_ref), custom_call_target="tpu_custom_call" | custom-call | tf_op jit(solution)/shard_map/pallas_call | solution.py:337
  80.9 4.5 %shard_map.109.refs_0_ = f32[128,720]{1,0:T(8,128)S(1)} custom-call(bf16[128,4608]{1,0:T(8,128)(2,1)S(1)} %shard_map.108.patch_ref, bf16[64,4096]{1,0:T(8,128)(2,1)S(1)} %bitcast.7, bf16[64,4096]{1,0:T(8,128)(2,1)S(1)} %collective-permute-done.9.send_ref, bf16[72,4608]{1,0:T(8,128)(2,1)S(1)} %reshape.11.refs_0_.refs_2_, ...), custom_call_target="tpu_custom_call" | custom-call | tf_op jit(solution)/shard_map/pallas_call | solution.py:478
  85.8 10.2 %collective-permute-done.16.refs_1_ = f32[128,720]{1,0:T(8,128)S(1)} collective-permute-done((f32[128,720]{1,0:T(8,128)S(1)}, f32[128,720]{1,0:T(8,128)S(1)}, u32[]{:S(2)}, u32[]{:S(2)}) %collective-permute-start.16) | collective-permute-done | bytes 368672 | tf_op jit(solution)/shard_map/ppermute | solution.py:420
  96.0 2.8 %shard_map.110 = (f32[64,4096]{1,0:T(8,128)S(1)}, f32[64,4096]{1,0:T(8,128)S(1)}) custom-call(s32[4]{0:T(128)S(1)} %copy-done.15, f32[128,720]{1,0:T(8,128)S(1)} %shard_map.109.refs_0_, f32[128,720]{1,0:T(8,128)S(1)} %collective-permute-done.16.refs_1_, bf16[72,4096]{1,0:T(8,128)(2,1)S(1)} %copy-done.1, bf16[72,4096]{1,0:T(8,128)(2,1)S(1)} %copy-done.5, ...), custom_call_target="tpu_custom_call" | custom-call | tf_op jit(solution)/shard_map/pallas_call | solution.py:487
  98.8 3.2 %shard_map.111 = (f32[64,4608]{1,0:T(8,128)S(1)}, f32[64,4608]{1,0:T(8,128)S(1)}) custom-call(s32[4]{0:T(128)S(1)} %copy-done.15, f32[128,720]{1,0:T(8,128)S(1)} %shard_map.109.refs_0_, f32[128,720]{1,0:T(8,128)S(1)} %collective-permute-done.16.refs_1_, bf16[72,4608]{1,0:T(8,128)(2,1)S(1)} %reshape.11.refs_0_.refs_2_, ...), custom_call_target="tpu_custom_call" | custom-call | tf_op jit(solution)/shard_map/pallas_call | solution.py:487
  102.0 1.1 collective-permute-done.15.refs_3_
  103.1 1.9 %collective-permute-start.18 = (bf16[72,4096]{1,0:T(8,128)(2,1)S(1)}, bf16[72,4096]{1,0:T(8,128)(2,1)S(1)}, u32[]{:S(2)}, u32[]{:S(2)}) collective-permute-start(bf16[72,4096]{1,0:T(8,128)(2,1)S(1)} %collective-permute-done.15.refs_3_), channel_id=1, source_target_pairs={{0,4},{2,6},{8,0},{10,2},{16,8},{18,10},{24,16},{26,18},{28,24},{3... | collective-permute-start | bytes 1769480 | tf_op jit(solution)/shard_map/ppermute | solution.py:434
  105.0 1.4 shard_map.112.refs_0_
  106.7 6.1 %collective-permute-done.19.refs_1_ = f32[128,288]{1,0:T(8,128)S(1)} collective-permute-done((f32[128,288]{1,0:T(8,128)S(1)}, f32[128,288]{1,0:T(8,128)S(1)}, u32[]{:S(2)}, u32[]{:S(2)}) %collective-permute-start.19) | collective-permute-done | bytes 147488 | tf_op jit(solution)/shard_map/ppermute | solution.py:420
  112.8 1.7 %shard_map.114 = (f32[64,4608]{1,0:T(8,128)S(1)}, f32[64,4608]{1,0:T(8,128)S(1)}) custom-call(s32[4]{0:T(128)S(1)} %copy-done.15, f32[128,288]{1,0:T(8,128)S(1)} %shard_map.112.refs_0_, f32[128,288]{1,0:T(8,128)S(1)} %collective-permute-done.19.refs_1_, bf16[72,4608]{1,0:T(8,128)(2,1)S(1)} %collective-permute-done.10.refs_0_.refs_2_, ...), custom_call_target="tpu_custom_call" | custom-call | tf_op jit(solution)/shard_map/pallas_call | solution.py:487
  114.5 1.3 shard_map.113
  115.8 2.7 %collective-permute-done.18.refs_1_.refs_2_ = bf16[72,4096]{1,0:T(8,128)(2,1)S(1)} collective-permute-done((bf16[72,4096]{1,0:T(8,128)(2,1)S(1)}, bf16[72,4096]{1,0:T(8,128)(2,1)S(1)}, u32[]{:S(2)}, u32[]{:S(2)}) %collective-permute-start.18) | collective-permute-done | bytes 589856 | tf_op jit(solution)/shard_map/ppermute | solution.py:434
  118.5 1.8 %collective-permute-done.17.refs_0_.refs_2_ = bf16[72,4608]{1,0:T(8,128)(2,1)S(1)} collective-permute-done((bf16[72,4608]{1,0:T(8,128)(2,1)S(1)}, bf16[72,4608]{1,0:T(8,128)(2,1)S(1)}, u32[]{:S(2)}, u32[]{:S(2)}) %collective-permute-start.17) | collective-permute-done | bytes 663584 | tf_op jit(solution)/shard_map/ppermute | solution.py:434
  120.3 0.8 shard_map.115.refs_0_
  121.4 4.4 %collective-permute-done.20.refs_1_ = f32[128,144]{1,0:T(8,128)S(1)} collective-permute-done((f32[128,144]{1,0:T(8,128)S(1)}, f32[128,144]{1,0:T(8,128)S(1)}, u32[]{:S(2)}, u32[]{:S(2)}) %collective-permute-start.20) | collective-permute-done | bytes 73760 | tf_op jit(solution)/shard_map/ppermute | solution.py:420
  125.8 1.3 shard_map.117
  127.0 1.4 collective-permute-start.21
  128.4 1.0 shard_map.116
  129.4 1.5 collective-permute-done.21.mate_ref
  130.9 2.1 %shard_map.118 = (bf16[256,576]{1,0:T(8,128)(2,1)S(1)}, f32[256,576]{1,0:T(8,128)S(1)}) custom-call(s32[4]{0:T(128)S(1)} %copy-done.15, f32[64,4608]{1,0:T(8,128)S(1)} %get-tuple-element.91.own_ref, f32[64,4608]{1,0:T(8,128)S(1)} %collective-permute-done.21.mate_ref), custom_call_target="tpu_custom_call" | custom-call | tf_op jit(solution)/shard_map/pallas_call | solution.py:358
  133.0 0.4 collective-permute-start.22
  133.5 2.3 %collective-permute-done.22 = f32[64,4096]{1,0:T(8,128)S(1)} collective-permute-done((f32[64,4096]{1,0:T(8,128)S(1)}, f32[64,4096]{1,0:T(8,128)S(1)}, u32[]{:S(2)}, u32[]{:S(2)}) %collective-permute-start.22) | collective-permute-done | bytes 1048608 | tf_op jit(solution)/shard_map/ppermute | solution.py:412
  135.8 0.9 add_convert_fusion
  136.7 4.6 %all-to-all-start.1 = ((bf16[8,8,4096]{2,1,0:T(8,128)(2,1)}), bf16[8,8,4096]{2,1,0:T(8,128)(2,1)S(1)}, u32[]{:S(2)}, u32[]{:S(2)}) async-start(bf16[8,8,4096]{2,1,0:T(8,128)(2,1)} %bitcast.4), calls=%async_computation.1 | async-start | bytes 1048576 | tf_op jit(solution)/shard_map/all_to_all | solution.py:499
  141.3 3.1 %collective-permute-start.23 = (bf16[256,576]{1,0:T(8,128)(2,1)S(1)}, bf16[256,576]{1,0:T(8,128)(2,1)S(1)}, u32[]{:S(2)}, u32[]{:S(2)}) collective-permute-start(bf16[256,576]{1,0:T(8,128)(2,1)S(1)} %get-tuple-element.99), channel_id=1, source_target_pairs={{2,0},{4,2},{6,4},{8,6},{10,8},{12,10},{14,12},{16,14},{18,16},{20... | collective-permute-start | bytes 884744 | tf_op jit(solution)/shard_map/ppermute | solution.py:395
  144.4 14.0 %collective-permute-done.23.odd_ref = bf16[256,576]{1,0:T(8,128)(2,1)S(1)} collective-permute-done((bf16[256,576]{1,0:T(8,128)(2,1)S(1)}, bf16[256,576]{1,0:T(8,128)(2,1)S(1)}, u32[]{:S(2)}, u32[]{:S(2)}) %collective-permute-start.23) | collective-permute-done | bytes 294944 | tf_op jit(solution)/shard_map/ppermute | solution.py:395
  158.4 0.8 shard_map.119
  159.5 2.2 %collective-permute-done.24 = f32[2,288]{1,0:T(2,128)S(1)} collective-permute-done((f32[2,288]{1,0:T(2,128)S(1)}, f32[2,288]{1,0:T(2,128)S(1)}, u32[]{:S(2)}, u32[]{:S(2)}) %collective-permute-start.24) | collective-permute-done | bytes 2336 | tf_op jit(solution)/shard_map/ppermute | solution.py:420
  161.7 1.3 copy-done.21
  163.0 1.3 copy-done.23
  164.3 2.6 %shard_map.120 = bf16[2,196,576]{2,1,0:T(8,128)(2,1)S(1)} custom-call(f32[256,576]{1,0:T(8,128)S(1)} %get-tuple-element.98.even_ref, bf16[256,576]{1,0:T(8,128)(2,1)S(1)} %collective-permute-done.23.odd_ref, f32[512,576]{1,0:T(8,128)S(1)} %copy-done.19, f32[2,576]{1,0:T(2,128)S(1)} %copy-done.17, f32[2,288]{1,0:T(2,128)S(1)} %add.9.sq_ref, ...), custom_call_target="tpu_custom_call" | custom-call | flops 2717908992 | bytes 4718592 | tf_op jit(solution)/shard_map/pallas_call | solution.py:379
  166.9 1.2 copy.12
  168.1 0.8 copy.14
  (68 shorter events, 2.6 us)
Async XLA Ops:
  0.6 3.3 %copy-start = (bf16[72,4096]{1,0:T(8,128)(2,1)S(1)}, bf16[72,4096]{1,0:T(8,128)(2,1)}, u32[]{:S(2)}) copy-start(bf16[72,4096]{1,0:T(8,128)(2,1)} %refs_2_.1) | copy-start | bytes 1769476
  0.6 5.9 %copy-start.9 = (bf16[9,576,48]{1,2,0:T(8,128)(2,1)S(1)}, bf16[9,576,48]{1,2,0:T(8,128)(2,1)}, u32[]{:S(2)}) copy-start(bf16[9,576,48]{1,2,0:T(8,128)(2,1)} %param.10) | copy-start | bytes 1492996
  2.4 4.1 %copy-start.10 = (bf16[576,288]{0,1:T(8,128)(2,1)S(1)}, bf16[576,288]{0,1:T(8,128)(2,1)}, u32[]{:S(2)}) copy-start(bf16[576,288]{0,1:T(8,128)(2,1)} %param.11) | copy-start | bytes 995332
  2.4 14.4 %copy-start.6 = (bf16[288,576]{1,0:T(8,128)(2,1)S(1)}, bf16[288,576]{1,0:T(8,128)(2,1)}, u32[]{:S(2)}) copy-start(bf16[288,576]{1,0:T(8,128)(2,1)} %expand_ref.3) | copy-start | bytes 995332
  2.4 29.5 %collective-permute-start.4 = (bf16[72,4608]{1,0:T(8,128)(2,1)S(1)}, bf16[72,4608]{1,0:T(8,128)(2,1)S(1)}, u32[]{:S(2)}, u32[]{:S(2)}) collective-permute-start(bf16[72,4608]{1,0:T(8,128)(2,1)S(1)} %reshape.11.refs_0_.refs_2_), channel_id=1, source_target_pairs={{0,4},{2,6},{8,0},{10,2},{16,8},{18,10},{24,16},{26,18},{28,24},{3... | collective-permute-start | bytes 1990664 | tf_op jit(solution)/shard_map/ppermute | solution.py:434
  3.8 28.1 %collective-permute-start.2 = (bf16[72,4608]{1,0:T(8,128)(2,1)S(1)}, bf16[72,4608]{1,0:T(8,128)(2,1)S(1)}, u32[]{:S(2)}, u32[]{:S(2)}) collective-permute-start(bf16[72,4608]{1,0:T(8,128)(2,1)S(1)} %reshape.11.refs_0_.refs_2_), channel_id=1, source_target_pairs={{0,8},{2,10},{8,16},{10,18},{16,24},{18,26},{24,28},{26,30},{28,20... | collective-permute-start | bytes 1990664 | tf_op jit(solution)/shard_map/ppermute | solution.py:434
  3.9 26.9 %collective-permute-start.5 = (bf16[72,4096]{1,0:T(8,128)(2,1)S(1)}, bf16[72,4096]{1,0:T(8,128)(2,1)S(1)}, u32[]{:S(2)}, u32[]{:S(2)}) collective-permute-start(bf16[72,4096]{1,0:T(8,128)(2,1)S(1)} %copy-done), channel_id=1, source_target_pairs={{0,4},{2,6},{8,0},{10,2},{16,8},{18,10},{24,16},{26,18},{28,24},{3... | collective-permute-start | bytes 1769480 | tf_op jit(solution)/shard_map/ppermute | solution.py:434
  5.2 26.6 %collective-permute-start.3 = (bf16[72,4096]{1,0:T(8,128)(2,1)S(1)}, bf16[72,4096]{1,0:T(8,128)(2,1)S(1)}, u32[]{:S(2)}, u32[]{:S(2)}) collective-permute-start(bf16[72,4096]{1,0:T(8,128)(2,1)S(1)} %copy-done), channel_id=1, source_target_pairs={{0,8},{2,10},{8,16},{10,18},{16,24},{18,26},{24,28},{26,30},{28,20... | collective-permute-start | bytes 1769480 | tf_op jit(solution)/shard_map/ppermute | solution.py:434
  11.0 1.1 copy-start.20
  12.1 1.1 copy-start.22
  13.2 0.9 copy-start.24
  14.1 2.7 %collective-permute-start = (f32[2,288]{1,0:T(2,128)S(1)}, f32[2,288]{1,0:T(2,128)S(1)}, u32[]{:S(2)}, u32[]{:S(2)}) collective-permute-start(f32[2,288]{1,0:T(2,128)S(1)} %get-tuple-element.57), channel_id=1, source_target_pairs={{0,1},{1,0},{2,3},{3,2},{4,5},{5,4},{6,7},{7,6},{8,9},{9,8},{10,11... | collective-permute-start | bytes 6920 | tf_op jit(solution)/shard_map/ppermute | solution.py:420
  18.0 1.1 copy-start.7
  19.1 0.7 copy-start.12
  19.8 0.6 copy-start.16
  20.4 1.1 copy-start.18
  21.5 0.7 copy-start.26
  30.9 1.0 copy-start.2
  31.9 0.9 copy-start.4
  31.9 32.8 %collective-permute-start.6 = (bf16[72,4608]{1,0:T(8,128)(2,1)S(1)}, bf16[72,4608]{1,0:T(8,128)(2,1)S(1)}, u32[]{:S(2)}, u32[]{:S(2)}) collective-permute-start(bf16[72,4608]{1,0:T(8,128)(2,1)S(1)} %collective-permute-done.2.refs_1_.refs_3_), channel_id=1, source_target_pairs={{0,8},{2,10},{8,16},{10,18},{16,24},{18,26},{24,28},{26,30},{28,20... | collective-permute-start | bytes 1990664 | tf_op jit(solution)/shard_map/ppermute | solution.py:434
  32.7 32.0 %collective-permute-start.7 = (bf16[72,4608]{1,0:T(8,128)(2,1)S(1)}, bf16[72,4608]{1,0:T(8,128)(2,1)}, u32[]{:S(2)}, u32[]{:S(2)}) collective-permute-start(bf16[72,4608]{1,0:T(8,128)(2,1)S(1)} %collective-permute-done.4.refs_2_.refs_4_), channel_id=1, source_target_pairs={{0,4},{2,6},{8,0},{10,2},{16,8},{18,10},{24,16},{26,18},{28,24},{3... | collective-permute-start | bytes 1990664 | tf_op jit(solution)/shard_map/ppermute | solution.py:434
  34.0 34.6 %all-to-all-start = ((bf16[8,8,4096]{2,1,0:T(8,128)(2,1)}), bf16[8,8,4096]{2,1,0:T(8,128)(2,1)S(1)}, u32[]{:S(2)}, u32[]{:S(2)}) async-start(bf16[8,8,4096]{2,1,0:T(8,128)(2,1)} %bitcast.14), calls=%async_computation | async-start | bytes 1048576 | tf_op jit(solution)/shard_map/all_to_all | solution.py:499
  38.9 25.9 %collective-permute-start.1 = (bf16[256,576]{1,0:T(8,128)(2,1)}, bf16[256,576]{1,0:T(8,128)(2,1)}, u32[]{:S(2)}, u32[]{:S(2)}) collective-permute-start(bf16[256,576]{1,0:T(8,128)(2,1)} %copy-done.26), channel_id=1, source_target_pairs={{0,2},{2,4},{4,6},{6,8},{8,10},{10,12},{12,14},{14,16},{16,18},{18... | collective-permute-start | bytes 884744 | tf_op jit(solution)/shard_map/ppermute | solution.py:395
  44.5 26.0 %collective-permute-start.11 = (bf16[72,4096]{1,0:T(8,128)(2,1)}, bf16[72,4096]{1,0:T(8,128)(2,1)}, u32[]{:S(2)}, u32[]{:S(2)}) collective-permute-start(bf16[72,4096]{1,0:T(8,128)(2,1)} %copy-done.4), channel_id=1, source_target_pairs={{0,8},{2,10},{8,16},{10,18},{16,24},{18,26},{24,28},{26,30},{28,20... | collective-permute-start | bytes 1769480 | tf_op jit(solution)/shard_map/ppermute | solution.py:434
  46.1 31.0 %collective-permute-start.14 = (bf16[72,4096]{1,0:T(8,128)(2,1)}, bf16[72,4096]{1,0:T(8,128)(2,1)}, u32[]{:S(2)}, u32[]{:S(2)}) collective-permute-start(bf16[72,4096]{1,0:T(8,128)(2,1)} %copy-done.2), channel_id=1, source_target_pairs={{0,4},{2,6},{8,0},{10,2},{16,8},{18,10},{24,16},{26,18},{28,24},{3... | collective-permute-start | bytes 1769480 | tf_op jit(solution)/shard_map/ppermute | solution.py:434
  64.7 1.0 copy-start.13
  65.7 0.7 copy-start.14
  66.4 12.8 %copy-start.15 = (s32[4]{0:T(128)S(1)}, s32[4]{0:T(128)}, u32[]{:S(2)}) copy-start(s32[4]{0:T(128)} %shard_map.104.facts_ref) | copy-start | bytes 52
  68.6 8.4 %collective-permute-start.8 = (bf16[64,4608]{1,0:T(8,128)(2,1)}, bf16[64,4608]{1,0:T(8,128)(2,1)}, u32[]{:S(2)}, u32[]{:S(2)}) collective-permute-start(bf16[64,4608]{1,0:T(8,128)(2,1)} %shard_map.107.own_ref), channel_id=1, source_target_pairs={{0,2},{2,0},{4,6},{6,4},{8,10},{10,8},{12,14},{14,12},{16,18},{18,... | collective-permute-start | bytes 1769480 | tf_op jit(solution)/shard_map/ppermute | solution.py:412
  68.6 12.3 %copy-start.1 = (bf16[72,4096]{1,0:T(8,128)(2,1)S(1)}, bf16[72,4096]{1,0:T(8,128)(2,1)}, u32[]{:S(2)}) copy-start(bf16[72,4096]{1,0:T(8,128)(2,1)} %refs_2_.1) | copy-start | bytes 1769476
  68.6 12.3 %copy-start.3 = (bf16[72,4096]{1,0:T(8,128)(2,1)S(1)}, bf16[72,4096]{1,0:T(8,128)(2,1)}, u32[]{:S(2)}) copy-start(bf16[72,4096]{1,0:T(8,128)(2,1)} %copy-done.2) | copy-start | bytes 1769476
  68.6 12.3 %copy-start.5 = (bf16[72,4096]{1,0:T(8,128)(2,1)S(1)}, bf16[72,4096]{1,0:T(8,128)(2,1)}, u32[]{:S(2)}) copy-start(bf16[72,4096]{1,0:T(8,128)(2,1)} %copy-done.4) | copy-start | bytes 1769476
  68.7 12.2 %collective-permute-start.9 = (bf16[64,4096]{1,0:T(8,128)(2,1)S(1)}, bf16[64,4096]{1,0:T(8,128)(2,1)S(1)}, u32[]{:S(2)}, u32[]{:S(2)}) collective-permute-start(bf16[64,4096]{1,0:T(8,128)(2,1)S(1)} %bitcast.6), channel_id=1, source_target_pairs={{0,2},{2,0},{4,6},{6,4},{8,10},{10,8},{12,14},{14,12},{16,18},{18,... | collective-permute-start | bytes 1572872 | tf_op jit(solution)/shard_map/ppermute | solution.py:412
  69.2 33.9 %collective-permute-start.10 = (bf16[72,4608]{1,0:T(8,128)(2,1)S(1)}, bf16[72,4608]{1,0:T(8,128)(2,1)S(1)}, u32[]{:S(2)}, u32[]{:S(2)}) collective-permute-start(bf16[72,4608]{1,0:T(8,128)(2,1)S(1)} %collective-permute-done.6.refs_3_.refs_5_), channel_id=1, source_target_pairs={{0,8},{2,10},{8,16},{10,18},{16,24},{18,26},{24,28},{26,30},{28,20... | collective-permute-start | bytes 1990664 | tf_op jit(solution)/shard_map/ppermute | solution.py:434
  70.5 32.7 %collective-permute-start.13 = (bf16[72,4608]{1,0:T(8,128)(2,1)}, bf16[72,4608]{1,0:T(8,128)(2,1)S(1)}, u32[]{:S(2)}, u32[]{:S(2)}) collective-permute-start(bf16[72,4608]{1,0:T(8,128)(2,1)} %collective-permute-done.7.refs_4_.refs_6_), channel_id=1, source_target_pairs={{0,4},{2,6},{8,0},{10,2},{16,8},{18,10},{24,16},{26,18},{28,24},{3... | collective-permute-start | bytes 1990664 | tf_op jit(solution)/shard_map/ppermute | solution.py:434
  77.0 25.0 %collective-permute-start.12 = (bf16[72,4096]{1,0:T(8,128)(2,1)}, bf16[72,4096]{1,0:T(8,128)(2,1)S(1)}, u32[]{:S(2)}, u32[]{:S(2)}) collective-permute-start(bf16[72,4096]{1,0:T(8,128)(2,1)} %collective-permute-done.11.refs_8_.refs_5_), channel_id=1, source_target_pairs={{0,8},{2,10},{8,16},{10,18},{16,24},{18,26},{24,28},{26,30},{28,20... | collective-permute-start | bytes 1769480 | tf_op jit(solution)/shard_map/ppermute | solution.py:434
  77.1 26.1 %collective-permute-start.15 = (bf16[72,4096]{1,0:T(8,128)(2,1)}, bf16[72,4096]{1,0:T(8,128)(2,1)S(1)}, u32[]{:S(2)}, u32[]{:S(2)}) collective-permute-start(bf16[72,4096]{1,0:T(8,128)(2,1)} %collective-permute-done.14.refs_9_.refs_6_), channel_id=1, source_target_pairs={{0,4},{2,6},{8,0},{10,2},{16,8},{18,10},{24,16},{26,18},{28,24},{3... | collective-permute-start | bytes 1769480 | tf_op jit(solution)/shard_map/ppermute | solution.py:434
  85.5 10.5 %collective-permute-start.16 = (f32[128,720]{1,0:T(8,128)S(1)}, f32[128,720]{1,0:T(8,128)S(1)}, u32[]{:S(2)}, u32[]{:S(2)}) collective-permute-start(f32[128,720]{1,0:T(8,128)S(1)} %shard_map.109.refs_0_), channel_id=1, source_target_pairs={{0,1},{1,0},{2,3},{3,2},{4,5},{5,4},{6,7},{7,6},{8,9},{9,8},{10,11... | collective-permute-start | bytes 1105928 | tf_op jit(solution)/shard_map/ppermute | solution.py:420
  103.1 17.2 %collective-permute-start.17 = (bf16[72,4608]{1,0:T(8,128)(2,1)S(1)}, bf16[72,4608]{1,0:T(8,128)(2,1)S(1)}, u32[]{:S(2)}, u32[]{:S(2)}) collective-permute-start(bf16[72,4608]{1,0:T(8,128)(2,1)S(1)} %collective-permute-done.10.refs_0_.refs_2_), channel_id=1, source_target_pairs={{0,8},{2,10},{8,16},{10,18},{16,24},{18,26},{24,28},{26,30},{28,20... | collective-permute-start | bytes 1990664 | tf_op jit(solution)/shard_map/ppermute | solution.py:434
  103.1 15.3 %collective-permute-start.18 = (bf16[72,4096]{1,0:T(8,128)(2,1)S(1)}, bf16[72,4096]{1,0:T(8,128)(2,1)S(1)}, u32[]{:S(2)}, u32[]{:S(2)}) collective-permute-start(bf16[72,4096]{1,0:T(8,128)(2,1)S(1)} %collective-permute-done.15.refs_3_), channel_id=1, source_target_pairs={{0,4},{2,6},{8,0},{10,2},{16,8},{18,10},{24,16},{26,18},{28,24},{3... | collective-permute-start | bytes 1769480 | tf_op jit(solution)/shard_map/ppermute | solution.py:434
  106.4 6.4 %collective-permute-start.19 = (f32[128,288]{1,0:T(8,128)S(1)}, f32[128,288]{1,0:T(8,128)S(1)}, u32[]{:S(2)}, u32[]{:S(2)}) collective-permute-start(f32[128,288]{1,0:T(8,128)S(1)} %shard_map.112.refs_0_), channel_id=1, source_target_pairs={{0,1},{1,0},{2,3},{3,2},{4,5},{5,4},{6,7},{7,6},{8,9},{9,8},{10,11... | collective-permute-start | bytes 442376 | tf_op jit(solution)/shard_map/ppermute | solution.py:420
  121.1 4.7 %collective-permute-start.20 = (f32[128,144]{1,0:T(8,128)S(1)}, f32[128,144]{1,0:T(8,128)S(1)}, u32[]{:S(2)}, u32[]{:S(2)}) collective-permute-start(f32[128,144]{1,0:T(8,128)S(1)} %shard_map.115.refs_0_), channel_id=1, source_target_pairs={{0,1},{1,0},{2,3},{3,2},{4,5},{5,4},{6,7},{7,6},{8,9},{9,8},{10,11... | collective-permute-start | bytes 221192 | tf_op jit(solution)/shard_map/ppermute | solution.py:420
  127.0 3.9 %collective-permute-start.21 = (f32[64,4608]{1,0:T(8,128)S(1)}, f32[64,4608]{1,0:T(8,128)S(1)}, u32[]{:S(2)}, u32[]{:S(2)}) collective-permute-start(f32[64,4608]{1,0:T(8,128)S(1)} %get-tuple-element.92), channel_id=1, source_target_pairs={{0,2},{2,0},{4,6},{6,4},{8,10},{10,8},{12,14},{14,12},{16,18},{18,... | collective-permute-start | bytes 3538952 | tf_op jit(solution)/shard_map/ppermute | solution.py:412
  133.0 25.3 %copy-start.17 = (f32[2,576]{1,0:T(2,128)S(1)}, f32[2,576]{1,0:T(2,128)}, u32[]{:S(2)}) copy-start(f32[2,576]{1,0:T(2,128)} %copy-done.16) | copy-start | bytes 13828
  133.0 2.7 %collective-permute-start.22 = (f32[64,4096]{1,0:T(8,128)S(1)}, f32[64,4096]{1,0:T(8,128)S(1)}, u32[]{:S(2)}, u32[]{:S(2)}) collective-permute-start(f32[64,4096]{1,0:T(8,128)S(1)} %get-tuple-element.95), channel_id=1, source_target_pairs={{0,2},{2,0},{4,6},{6,4},{8,10},{10,8},{12,14},{14,12},{16,18},{18,... | collective-permute-start | bytes 3145736 | tf_op jit(solution)/shard_map/ppermute | solution.py:412
  135.8 22.6 %copy-start.8 = (f32[512,576]{1,0:T(8,128)S(1)}, f32[512,576]{1,0:T(8,128)}, u32[]{:S(2)}) copy-start(f32[512,576]{1,0:T(8,128)} %copy-done.7) | copy-start | bytes 3538948
  136.7 31.4 %all-to-all-start.1 = ((bf16[8,8,4096]{2,1,0:T(8,128)(2,1)}), bf16[8,8,4096]{2,1,0:T(8,128)(2,1)S(1)}, u32[]{:S(2)}, u32[]{:S(2)}) async-start(bf16[8,8,4096]{2,1,0:T(8,128)(2,1)} %bitcast.4), calls=%async_computation.1 | async-start | bytes 1048576 | tf_op jit(solution)/shard_map/all_to_all | solution.py:499
  141.3 17.1 %collective-permute-start.23 = (bf16[256,576]{1,0:T(8,128)(2,1)S(1)}, bf16[256,576]{1,0:T(8,128)(2,1)S(1)}, u32[]{:S(2)}, u32[]{:S(2)}) collective-permute-start(bf16[256,576]{1,0:T(8,128)(2,1)S(1)} %get-tuple-element.99), channel_id=1, source_target_pairs={{2,0},{4,2},{6,4},{8,6},{10,8},{12,10},{14,12},{16,14},{18,16},{20... | collective-permute-start | bytes 884744 | tf_op jit(solution)/shard_map/ppermute | solution.py:395
  158.4 3.3 %copy-start.11 = (bf16[576,288]{0,1:T(8,128)(2,1)S(1)}, bf16[576,288]{0,1:T(8,128)(2,1)}, u32[]{:S(2)}) copy-start(bf16[576,288]{0,1:T(8,128)(2,1)} %param.11) | copy-start | bytes 995332
  158.4 3.3 %copy-start.19 = (f32[512,576]{1,0:T(8,128)S(1)}, f32[512,576]{1,0:T(8,128)}, u32[]{:S(2)}) copy-start(f32[512,576]{1,0:T(8,128)} %copy-done.18) | copy-start | bytes 3538948
  158.4 3.3 %copy-start.25 = (bf16[9,192,192]{2,1,0:T(8,128)(2,1)S(1)}, bf16[9,192,192]{2,1,0:T(8,128)(2,1)}, u32[]{:S(2)}) copy-start(bf16[9,192,192]{2,1,0:T(8,128)(2,1)} %copy-done.24) | copy-start | bytes 1990660
  159.2 2.5 %collective-permute-start.24 = (f32[2,288]{1,0:T(2,128)S(1)}, f32[2,288]{1,0:T(2,128)S(1)}, u32[]{:S(2)}, u32[]{:S(2)}) collective-permute-start(f32[2,288]{1,0:T(2,128)S(1)} %shard_map.119), channel_id=1, source_target_pairs={{0,1},{1,0},{2,3},{3,2},{4,5},{5,4},{6,7},{7,6},{8,9},{9,8},{10,11... | collective-permute-start | bytes 6920 | tf_op jit(solution)/shard_map/ppermute | solution.py:420
  161.7 1.3 copy-start.21
  163.0 1.3 copy-start.23

commit v4 on v3

--- a/solution.py
+++ b/solution.py
@@ -95,7 +95,7 @@
 
 
 def conv_kernel(feat_ref, group_ref, squeeze_ref, *refs):
-    conv_ref, pad_ref, sq_ref, *dense_refs, flat_ref, wide_ref, shift_ref = refs
+    conv_ref, pad_ref, sq_ref, flat_ref, wide_ref, shift_ref = refs
     frames, _, chans = feat_ref.shape
     width = group_ref.shape[1]
     rows = frames * FRAME_ROWS
@@ -109,14 +109,13 @@
     pad_ref[...] = shift_ref[1]
     conv_ref[...] = jnp.zeros_like(conv_ref)
     body = rows - 2 * WIDE
-    for block, dense_ref in zip(channel_blocks(chans, width), dense_refs):
+    for block in channel_blocks(chans, width):
         _, _, start, end = block
         spread, same = block_tools(block, width)
         total = jnp.zeros((body, end - start), jnp.float32)
         for tap in range(9):
             down, across = divmod(tap, 3)
             weights = dense_tap(group_ref, tap, block, spread, same)
-            dense_ref[tap] = weights
             source = shift_ref[across, down * WIDE : down * WIDE + body, start:end]
             total += contract_last(source, weights)
         conv_ref[WIDE : WIDE + body, start:end] += total
@@ -217,21 +216,16 @@
             out_ref[:, at : at + chans] = rows[tap * per_frame : (tap + 1) * per_frame]
 
 
-def unpatch_kernel(facts_ref, own_ref, mate_ref, lead_ref, even_ref):
-    chans = lead_ref.shape[1]
-    select = select_rows(False)
-    frames = []
-    for frame in range(2):
-        pieces = []
-        for tap in range(frame * 4, frame * 4 + 4):
-            lanes = slice(tap * chans, (tap + 1) * chans)
-            pieces.append(own_ref[:, lanes] + mate_ref[:, lanes])
-        frames.append(
-            jnp.dot(select, jnp.concatenate(pieces, axis=0), precision=lax.Precision.HIGHEST)
-        )
-    good = inside(FRAME_ROWS)
-    lead_ref[...] = (frames[0] * (good * facts_ref[3].astype(jnp.float32))).astype(jnp.bfloat16)
-    even_ref[...] = frames[1] * good
+def unpatch_kernel(facts_ref, own_ref, mate_ref, out_ref):
+    chans = out_ref.shape[1]
+    rows = own_ref[...] + mate_ref[...].astype(jnp.float32)
+    pieces = [rows[:, tap * chans : (tap + 1) * chans] for tap in range(4)]
+    frame = jnp.dot(
+        select_rows(False), jnp.concatenate(pieces, axis=0), precision=lax.Precision.HIGHEST
+    ) * inside(FRAME_ROWS)
+    if out_ref.dtype == jnp.bfloat16:
+        frame = frame * facts_ref[3].astype(jnp.float32)
+    out_ref[...] = frame.astype(out_ref.dtype)
 
 
 def excite_grad_kernel(even_ref, odd_ref, active_ref, excite_ref, expand_ref, out_ref):
@@ -281,6 +275,20 @@
         out_ref[frame] = flat_ref[...].astype(jnp.bfloat16)
 
 
+def dense_kernel(group_ref, *dense_refs):
+    width, chans = group_ref.shape[1:]
+    for block, dense_ref in zip(channel_blocks(chans, width), dense_refs):
+        spread, same = block_tools(block, width)
+        for tap in range(9):
+            dense_ref[tap] = dense_tap(group_ref, tap, block, spread, same)
+
+
+def dense_weights(group_kernel):
+    _, width, chans = group_kernel.shape
+    sizes = [end - start for _, _, start, end in channel_blocks(chans, width)]
+    return whole_call(dense_kernel, tuple(bf16(9, size, size) for size in sizes), [])(group_kernel)
+
+
 def f32(*shape):
     return jax.ShapeDtypeStruct(shape, jnp.float32)
 
@@ -294,11 +302,7 @@
     rows = frames * FRAME_ROWS
     return whole_call(
         conv_kernel,
-        (f32(rows, chans), bf16(rows, chans), f32(frames, squeeze_in.shape[0]))
-        + tuple(
-            bf16(9, end - start, end - start)
-            for _, _, start, end in channel_blocks(chans, group_kernel.shape[1])
-        ),
+        (f32(rows, chans), bf16(rows, chans), f32(frames, squeeze_in.shape[0])),
         [
             pltpu.VMEM((cells, chans), jnp.float32),
             pltpu.VMEM((rows + 2 * EDGE, chans), jnp.float32),
@@ -354,10 +358,10 @@
     )(facts, halo, even)
 
 
-def return_patches(facts, own, mate, chans):
+def return_patches(facts, own, mate, chans, dtype):
     return pl.pallas_call(
         unpatch_kernel,
-        out_shape=(bf16(FRAME_ROWS, chans), f32(FRAME_ROWS, chans)),
+        out_shape=jax.ShapeDtypeStruct((FRAME_ROWS, chans), dtype),
         in_specs=vmem_specs(2),
         compiler_params=pltpu.CompilerParams(vmem_limit_bytes=VMEM_BYTES),
         cost_estimate=FREE,
@@ -449,7 +453,7 @@
     out_ref[...] = jnp.concatenate(products, axis=1)
 
 
-def totals_kernel(count, unit, backward, first, facts_ref, *refs):
+def totals_kernel(count, unit, lanes, backward, first, facts_ref, *refs):
     sums = refs[0][...] + refs[1][...]
     blocks, refs = refs[2 : 2 + count], refs[2 + count :]
     before, after = refs[:-2], refs[-2:]
@@ -467,10 +471,11 @@
     total = 0.0
     for place, ref in enumerate(blocks):
         piece = factor[:, place * width : (place + 1) * width]
-        total += jnp.dot(piece, ref[...], preferred_element_type=jnp.float32)
+        total += jnp.dot(piece, ref[:, lanes], preferred_element_type=jnp.float32)
     for half, ref in enumerate(after):
         value = total[half * rows // 2 : (half + 1) * rows // 2]
-        ref[...] = value if first else before[half][...] + value
+        value = value if first else before[half][...] + value
+        ref[...] = value.astype(ref.dtype)
 
 
 def partial_sums(patches, back, samplers, readouts):
@@ -480,13 +485,13 @@
     )(patches, *back, *samplers, *readouts)
 
 
-def add_products(facts, sums, blocks, before, unit, backward):
-    rows, columns = sums[0].shape[0] // 2, blocks[0].shape[1]
-    kernel = functools.partial(totals_kernel, len(blocks), unit, backward, not before)
+def add_products(facts, sums, blocks, before, unit, lanes, backward, last):
+    rows, columns = sums[0].shape[0] // 2, lanes.stop - lanes.start
+    kernel = functools.partial(totals_kernel, len(blocks), unit, lanes, backward, not before)
     operands = (*sums, *blocks, *before)
     return pl.pallas_call(
         kernel,
-        out_shape=(f32(rows, columns),) * 2,
+        out_shape=(f32(rows, columns), (bf16 if last else f32)(rows, columns)),
         in_specs=vmem_specs(len(operands)),
         compiler_params=pltpu.CompilerParams(vmem_limit_bytes=VMEM_BYTES),
         cost_estimate=FREE,
@@ -521,18 +526,20 @@
     squeeze_in = squeeze_in.T
     facts = facts_of(frame_clip, clip_keep)
 
-    conv, padded, squeezed, *dense = conv_forward(features, group_kernel, squeeze_in)
+    conv, padded, squeezed = conv_forward(features, group_kernel, squeeze_in)
     token_cotangent, squeezed = tie(token_cotangent, squeezed)
     back = chips_exchange(token_cotangent)
     squeezed = sum_tp(squeezed)
     even, odd, excite, active, slope = hidden_frames(conv, padded, squeezed, squeeze_out)
     halo = shifted(odd, "ctx", 1)
 
+    every = slice(0, readout_kernel.shape[1])
+    halo_lanes, even_lanes = slice(0, 4 * chans), slice(4 * chans, 8 * chans)
     samplers, readouts = [flat_sampler], [readout_kernel]
-    tokens = grads = ()
+    tokens = halo_grads = even_grads = ()
     for step in range(1, steps + 1):
         if step == 1:
-            *blocks, even = tie(*blocks, even)
+            *blocks, halo, even = tie(*blocks, halo, even)
         if step == 2:
             up_s, up_r, down_s, down_r = blocks
             halo, up_s, down_s = tie(halo, up_s, down_s)
@@ -542,26 +549,44 @@
             back = (back, swap_cores(back))
         here = blocks
         if step < steps:
+            if step == steps - 1:
+                held = *tokens, *halo_grads, *even_grads
+                *held, up_s, up_r, down_s, down_r, group_kernel = tie(*held, *here, group_kernel)
+                tokens, halo_grads, even_grads = held[:2], held[2:4], held[4:]
+                dense = dense_weights(group_kernel)
+                here = up_s, up_r, down_s, down_r
             samplers, readouts = samplers + [here[0], here[2]], readouts + [here[1], here[3]]
             if step == steps - 1:
-                *here, token_keep, token_send, grad_own, grad_mate = tie(*here, *tokens, *grads)
-                tokens, grads = (token_keep, token_send), (grad_own, grad_mate)
-                here = here[0], None, None, here[3]
+                here = up_s, None, None, down_r
             blocks = ring_step(here)
         else:
-            last_s, last_r, *held = tie(here[0], here[3], *tokens, *grads)
-            tokens, grads = held[:2], held[2:]
+            held = *tokens, *halo_grads, *even_grads, *dense
+            last_s, last_r, *held = tie(here[0], here[3], *held)
+            tokens, halo_grads, even_grads, dense = held[:2], held[2:4], held[4:6], held[6:]
             samplers, readouts = samplers + [last_s], readouts + [last_r]
         if step >= steps - 2:
+            last = step == steps
             sums = tp_terms(partial_sums(patches, back, samplers, readouts))
-            tokens = add_products(facts, sums, readouts, tokens, unit, False)
-            grads = add_products(facts, sums, samplers, grads, unit, True)
+            halo_grads = add_products(
+                facts, sums, samplers, halo_grads, unit, halo_lanes, True, last
+            )
+            if last:
+                sums, halo_grads = list(sums), list(halo_grads)
+                sums[0], halo_grads[1] = tie(sums[0], halo_grads[1])
+            even_grads = add_products(
+                facts, sums, samplers, even_grads, unit, even_lanes, True, last
+            )
+            tokens = add_products(facts, sums, readouts, tokens, unit, every, False, last)
             samplers, readouts = [], []
-    lead, grad_even = return_patches(facts, grads[0], swap_cores(grads[1]), chans)
-    token_keep, token_send, lead = tie(*tokens, lead)
+    halo_mate = swap_cores(halo_grads[1])
+    halo_own, even_own, token_keep = tie(halo_grads[0], even_grads[0], tokens[0])
+    lead = return_patches(facts, halo_own, halo_mate, chans, jnp.bfloat16)
     grad_odd = shifted(lead, "ctx", -1)
-    tokens = (token_keep + swap_cores(token_send)).astype(jnp.bfloat16)
-    tokens, grad_even = tie(tokens, grad_even)
+    grad_even = return_patches(
+        facts, even_own, swap_cores(even_grads[1]), chans, jnp.float32
+    )
+    tokens = (token_keep + swap_cores(tokens[1]).astype(jnp.float32)).astype(jnp.bfloat16)
+    tokens, grad_odd = tie(tokens, grad_odd)
     llm_tokens = chips_exchange(tokens)
     grad_relaxed = sum_tp(excite_grad(grad_even, grad_odd, active, excite, squeeze_out))
     grad_features = conv_backward(

time: 170 us -> 166 us (0.976)
  the two profiles are of different devices: /device:TPU:15 before, /device:TPU:3 now
where the time goes in v4:
time: 166 us; the launch traced here: 164 us
  waiting for transfers between devices  53.2 us (32%)
  starting transfers between devices  52.4 us (32%)
  Pallas kernels  39.3 us (24%)
  local copies, waits for them, and re-layouts  17.4 us (10%)
    ppermute x5, waiting for transfers between devices, tp_terms(): other = lax.ppermute(value, 'tp', [(i, i ^ reach) for i in range(size)])  17.8 us
    ppermute x2, waiting for transfers between devices, shifted(): return lax.ppermute(value, axis, pairs)  16.7 us
    ppermute x14, starting transfers between devices, ring_step(): lax.ppermute(value, 'ctx', pairs)  16.3 us
    unnamed x67, local copies, waits for them, and re-layouts  15.7 us
    pallas_call x9, Pallas kernels, add_products(): pl.pallas_call(kernel, out_shape=(f32(rows, columns), (bf16 if last else...  14.9 us
    ppermute x14, waiting for transfers between devices, ring_step(): lax.ppermute(value, 'ctx', pairs)  12.8 us
    ppermute x5, starting transfers between devices, swap_cores(): lax.ppermute(value, 'ctx', [(i, i ^ 1) for i in range(lax.axis_size('ctx'...  12.3 us
    all_to_all x2, starting transfers between devices, chips_exchange(): lax.all_to_all(value, 'ctx', split_axis=0, concat_axis=0, tiled=True, axi...  9.09 us
  transfers between devices with their start and end apart: 28, of which 14 were waited for; matrix products, arithmetic and copies ran while one was open for 2% of the time, Pallas kernels for 22%

profile of v4, /device:TPU:3, one launch (start us, length us, event | category | flops | bytes accessed | tf_op | source)
XLA Modules:
  0.0 164.3 jit_solution(5455575547661604890)
XLA Ops:
  0.7 1.7 %reshape.11.refs_0_.refs_2_ = bf16[72,4608]{1,0:T(8,128)(2,1)S(1)} reshape(bf16[72,8,576]{2,1,0:T(8,128)(2,1)} %param.13) | data formatting | bytes 1327104 | tf_op jit(solution)/shard_map/reshape | solution.py:523
  2.5 1.5 collective-permute-start.2
  4.0 1.4 collective-permute-start.3
  5.4 1.1 copy.11.feat_ref
  6.5 4.5 %shard_map.105 = (f32[512,576]{1,0:T(8,128)S(1)}, bf16[512,576]{1,0:T(8,128)(2,1)S(1)}, f32[2,288]{1,0:T(2,128)S(1)}) custom-call(bf16[2,196,576]{2,1,0:T(8,128)(2,1)S(1)} %copy.11.feat_ref, bf16[9,48,576]{2,1,0:T(8,128)(2,1)S(1)} %bitcast.10, bf16[288,576]{1,0:T(8,128)(2,1)S(1)} %bitcast.12), custom_call_target="tpu_custom_call" | custom-call | tf_op jit(solution)/shard_map/pallas_call | solution.py:303
  11.0 1.3 collective-permute-start.4
  12.3 1.5 collective-permute-done.4
  13.8 1.1 shard_map.106
  14.9 1.1 copy-done.9
  17.3 1.1 copy-done.24
  18.4 5.7 %collective-permute-start.5 = (bf16[256,576]{1,0:T(8,128)(2,1)S(1)}, bf16[256,576]{1,0:T(8,128)(2,1)S(1)}, u32[]{:S(2)}, u32[]{:S(2)}) collective-permute-start(bf16[256,576]{1,0:T(8,128)(2,1)S(1)} %get-tuple-element.75), channel_id=1, source_target_pairs={{0,2},{2,4},{4,6},{6,8},{8,10},{10,12},{12,14},{14,16},{16,18},{18... | collective-permute-start | bytes 884744 | tf_op jit(solution)/shard_map/ppermute | solution.py:399
  24.1 10.7 %collective-permute-done.5.halo_ref = bf16[256,576]{1,0:T(8,128)(2,1)S(1)} collective-permute-done((bf16[256,576]{1,0:T(8,128)(2,1)S(1)}, bf16[256,576]{1,0:T(8,128)(2,1)S(1)}, u32[]{:S(2)}, u32[]{:S(2)}) %collective-permute-start.5) | collective-permute-done | bytes 294944 | tf_op jit(solution)/shard_map/ppermute | solution.py:399
  36.6 1.3 collective-permute-start.7
  37.9 4.8 %all-to-all-start = ((bf16[8,8,4096]{2,1,0:T(8,128)(2,1)}), bf16[8,8,4096]{2,1,0:T(8,128)(2,1)S(1)}, u32[]{:S(2)}, u32[]{:S(2)}) async-start(bf16[8,8,4096]{2,1,0:T(8,128)(2,1)} %bitcast.14), calls=%async_computation | async-start | bytes 1048576 | tf_op jit(solution)/shard_map/all_to_all | solution.py:504
  42.7 1.2 shard_map.104.facts_ref
  43.9 1.5 collective-permute-start.11
  45.4 6.9 %collective-permute-done.6.refs_3_.refs_5_ = bf16[72,4608]{1,0:T(8,128)(2,1)S(1)} collective-permute-done((bf16[72,4608]{1,0:T(8,128)(2,1)S(1)}, bf16[72,4608]{1,0:T(8,128)(2,1)S(1)}, u32[]{:S(2)}, u32[]{:S(2)}) %collective-permute-start.6) | collective-permute-done | bytes 663584 | tf_op jit(solution)/shard_map/ppermute | solution.py:438
  52.4 1.0 copy-done.16
  53.3 1.0 copy-done.18
  55.0 1.8 %shard_map.107.own_ref = bf16[64,4608]{1,0:T(8,128)(2,1)} custom-call(s32[4]{0:T(128)S(1)} %copy-done.19, bf16[256,576]{1,0:T(8,128)(2,1)S(1)} %copy-done.18, bf16[256,576]{1,0:T(8,128)(2,1)S(1)} %copy-done.16), custom_call_target="tpu_custom_call" | custom-call | tf_op jit(solution)/shard_map/pallas_call | solution.py:352
  56.8 6.4 %collective-permute-start.8 = (bf16[64,4608]{1,0:T(8,128)(2,1)}, bf16[64,4608]{1,0:T(8,128)(2,1)}, u32[]{:S(2)}, u32[]{:S(2)}) collective-permute-start(bf16[64,4608]{1,0:T(8,128)(2,1)} %shard_map.107.own_ref), channel_id=1, source_target_pairs={{0,2},{2,0},{4,6},{6,4},{8,10},{10,8},{12,14},{14,12},{16,18},{18,... | collective-permute-start | bytes 1769480 | tf_op jit(solution)/shard_map/ppermute | solution.py:416
  63.2 2.1 %all-to-all-done = bf16[8,8,4096]{2,1,0:T(8,128)(2,1)S(1)} async-done(((bf16[8,8,4096]{2,1,0:T(8,128)(2,1)}), bf16[8,8,4096]{2,1,0:T(8,128)(2,1)S(1)}, u32[]{:S(2)}, u32[]{:S(2)}) %all-to-all-start) | async-done | bytes 524320 | tf_op jit(solution)/shard_map/all_to_all | solution.py:504
  65.3 3.5 %collective-permute-start.9 = (bf16[64,4096]{1,0:T(8,128)(2,1)S(1)}, bf16[64,4096]{1,0:T(8,128)(2,1)S(1)}, u32[]{:S(2)}, u32[]{:S(2)}) collective-permute-start(bf16[64,4096]{1,0:T(8,128)(2,1)S(1)} %bitcast.6), channel_id=1, source_target_pairs={{0,2},{2,0},{4,6},{6,4},{8,10},{10,8},{12,14},{14,12},{16,18},{18,... | collective-permute-start | bytes 1572872 | tf_op jit(solution)/shard_map/ppermute | solution.py:416
  68.9 1.7 %collective-permute-start.13 = (bf16[72,4608]{1,0:T(8,128)(2,1)S(1)}, bf16[72,4608]{1,0:T(8,128)(2,1)S(1)}, u32[]{:S(2)}, u32[]{:S(2)}) collective-permute-start(bf16[72,4608]{1,0:T(8,128)(2,1)S(1)} %collective-permute-done.6.refs_3_.refs_5_), channel_id=1, source_target_pairs={{0,8},{2,10},{8,16},{10,18},{16,24},{18,26},{24,28},{26,30},{28,20... | collective-permute-start | bytes 1990664 | tf_op jit(solution)/shard_map/ppermute | solution.py:438
  70.5 2.2 %collective-permute-done.10.refs_8_.refs_5_ = bf16[72,4096]{1,0:T(8,128)(2,1)} collective-permute-done((bf16[72,4096]{1,0:T(8,128)(2,1)}, bf16[72,4096]{1,0:T(8,128)(2,1)}, u32[]{:S(2)}, u32[]{:S(2)}) %collective-permute-start.10) | collective-permute-done | bytes 589856 | tf_op jit(solution)/shard_map/ppermute | solution.py:438
  72.7 5.8 %collective-permute-start.15 = (bf16[72,4608]{1,0:T(8,128)(2,1)}, bf16[72,4608]{1,0:T(8,128)(2,1)S(1)}, u32[]{:S(2)}, u32[]{:S(2)}) collective-permute-start(bf16[72,4608]{1,0:T(8,128)(2,1)} %collective-permute-done.7.refs_4_.refs_6_), channel_id=1, source_target_pairs={{0,4},{2,6},{8,0},{10,2},{16,8},{18,10},{24,16},{26,18},{28,24},{3... | collective-permute-start | bytes 1990664 | tf_op jit(solution)/shard_map/ppermute | solution.py:438
  78.5 1.5 collective-permute-start.16
  80.7 1.7 %shard_map.108.patch_ref = bf16[128,4608]{1,0:T(8,128)(2,1)S(1)} custom-call(s32[4]{0:T(128)S(1)} %copy-done.20, bf16[64,4608]{1,0:T(8,128)(2,1)} %shard_map.107.own_ref, bf16[64,4608]{1,0:T(8,128)(2,1)} %collective-permute-done.8.mate_ref), custom_call_target="tpu_custom_call" | custom-call | tf_op jit(solution)/shard_map/pallas_call | solution.py:341
  82.4 4.5 %shard_map.109.refs_0_ = f32[128,720]{1,0:T(8,128)S(1)} custom-call(bf16[128,4608]{1,0:T(8,128)(2,1)S(1)} %shard_map.108.patch_ref, bf16[64,4096]{1,0:T(8,128)(2,1)S(1)} %bitcast.7, bf16[64,4096]{1,0:T(8,128)(2,1)S(1)} %collective-permute-done.9.send_ref, bf16[72,4608]{1,0:T(8,128)(2,1)S(1)} %reshape.11.refs_0_.refs_2_, ...), custom_call_target="tpu_custom_call" | custom-call | tf_op jit(solution)/shard_map/pallas_call | solution.py:483
  87.0 1.3 collective-permute-start.12
  88.3 9.8 %collective-permute-done.12.refs_1_ = f32[128,720]{1,0:T(8,128)S(1)} collective-permute-done((f32[128,720]{1,0:T(8,128)S(1)}, f32[128,720]{1,0:T(8,128)S(1)}, u32[]{:S(2)}, u32[]{:S(2)}) %collective-permute-start.12) | collective-permute-done | bytes 368672 | tf_op jit(solution)/shard_map/ppermute | solution.py:424
  98.0 2.4 %shard_map.112 = (f32[64,2304]{1,0:T(8,128)S(1)}, f32[64,2304]{1,0:T(8,128)S(1)}) custom-call(s32[4]{0:T(128)S(1)} %copy-done.20, f32[128,720]{1,0:T(8,128)S(1)} %shard_map.109.refs_0_, f32[128,720]{1,0:T(8,128)S(1)} %collective-permute-done.12.refs_1_, bf16[72,4608]{1,0:T(8,128)(2,1)S(1)} %reshape.11.refs_0_.refs_2_, ...), custom_call_target="tpu_custom_call" | custom-call | tf_op jit(solution)/shard_map/pallas_call | solution.py:492
  100.4 2.4 %shard_map.111 = (f32[64,2304]{1,0:T(8,128)S(1)}, f32[64,2304]{1,0:T(8,128)S(1)}) custom-call(s32[4]{0:T(128)S(1)} %copy-done.20, f32[128,720]{1,0:T(8,128)S(1)} %shard_map.109.refs_0_, f32[128,720]{1,0:T(8,128)S(1)} %collective-permute-done.12.refs_1_, bf16[72,4608]{1,0:T(8,128)(2,1)S(1)} %reshape.11.refs_0_.refs_2_, ...), custom_call_target="tpu_custom_call" | custom-call | tf_op jit(solution)/shard_map/pallas_call | solution.py:492
  102.8 2.8 %shard_map.110 = (f32[64,4096]{1,0:T(8,128)S(1)}, f32[64,4096]{1,0:T(8,128)S(1)}) custom-call(s32[4]{0:T(128)S(1)} %copy-done.20, f32[128,720]{1,0:T(8,128)S(1)} %shard_map.109.refs_0_, f32[128,720]{1,0:T(8,128)S(1)} %collective-permute-done.12.refs_1_, bf16[72,4096]{1,0:T(8,128)(2,1)S(1)} %copy-done.1, bf16[72,4096]{1,0:T(8,128)(2,1)S(1)} %copy-done.3, ...), custom_call_target="tpu_custom_call" | custom-call | tf_op jit(solution)/shard_map/pallas_call | solution.py:492
  105.8 1.5 collective-permute-start.18
  107.2 1.4 shard_map.113.refs_0_
  108.6 1.3 collective-permute-start.19
  109.9 1.0 shard_map.117
  110.9 1.0 copy-done.28
  111.9 2.4 %collective-permute-done.19.refs_1_ = f32[128,288]{1,0:T(8,128)S(1)} collective-permute-done((f32[128,288]{1,0:T(8,128)S(1)}, f32[128,288]{1,0:T(8,128)S(1)}, u32[]{:S(2)}, u32[]{:S(2)}) %collective-permute-start.19) | collective-permute-done | bytes 147488 | tf_op jit(solution)/shard_map/ppermute | solution.py:424
  114.3 1.4 shard_map.116
  115.7 1.4 shard_map.115
  117.1 1.3 shard_map.114
  118.4 1.3 collective-permute-done.18.refs_1_.refs_2_
  119.7 2.3 %collective-permute-done.17.refs_0_.refs_2_ = bf16[72,4608]{1,0:T(8,128)(2,1)S(1)} collective-permute-done((bf16[72,4608]{1,0:T(8,128)(2,1)S(1)}, bf16[72,4608]{1,0:T(8,128)(2,1)S(1)}, u32[]{:S(2)}, u32[]{:S(2)}) %collective-permute-start.17) | collective-permute-done | bytes 663584 | tf_op jit(solution)/shard_map/ppermute | solution.py:438
  122.8 1.3 collective-permute-start.20
  124.2 2.6 %collective-permute-done.20.refs_1_ = f32[128,144]{1,0:T(8,128)S(1)} collective-permute-done((f32[128,144]{1,0:T(8,128)S(1)}, f32[128,144]{1,0:T(8,128)S(1)}, u32[]{:S(2)}, u32[]{:S(2)}) %collective-permute-start.20) | collective-permute-done | bytes 73760 | tf_op jit(solution)/shard_map/ppermute | solution.py:424
  126.7 1.1 shard_map.119
  127.9 1.0 shard_map.121
  128.9 2.3 %collective-permute-start.21 = (bf16[64,4096]{1,0:T(8,128)(2,1)S(1)}, bf16[64,4096]{1,0:T(8,128)(2,1)S(1)}, u32[]{:S(2)}, u32[]{:S(2)}) collective-permute-start(bf16[64,4096]{1,0:T(8,128)(2,1)S(1)} %get-tuple-element.127), channel_id=1, source_target_pairs={{0,2},{2,0},{4,6},{6,4},{8,10},{10,8},{12,14},{14,12},{16,18},{18,... | collective-permute-start | bytes 1572872 | tf_op jit(solution)/shard_map/ppermute | solution.py:416
  131.2 1.1 shard_map.120
  133.1 1.4 shard_map.122
  134.6 2.5 %collective-permute-start.23 = (bf16[256,576]{1,0:T(8,128)(2,1)S(1)}, bf16[256,576]{1,0:T(8,128)(2,1)S(1)}, u32[]{:S(2)}, u32[]{:S(2)}) collective-permute-start(bf16[256,576]{1,0:T(8,128)(2,1)S(1)} %shard_map.122), channel_id=1, source_target_pairs={{2,0},{4,2},{6,4},{8,6},{10,8},{12,10},{14,12},{16,14},{18,16},{20... | collective-permute-start | bytes 884744 | tf_op jit(solution)/shard_map/ppermute | solution.py:399
  138.0 6.0 %collective-permute-done.23.odd_ref = bf16[256,576]{1,0:T(8,128)(2,1)S(1)} collective-permute-done((bf16[256,576]{1,0:T(8,128)(2,1)S(1)}, bf16[256,576]{1,0:T(8,128)(2,1)S(1)}, u32[]{:S(2)}, u32[]{:S(2)}) %collective-permute-start.23) | collective-permute-done | bytes 294944 | tf_op jit(solution)/shard_map/ppermute | solution.py:399
  144.0 4.3 %all-to-all-start.1 = ((bf16[8,8,4096]{2,1,0:T(8,128)(2,1)}), bf16[8,8,4096]{2,1,0:T(8,128)(2,1)}, u32[]{:S(2)}, u32[]{:S(2)}) async-start(bf16[8,8,4096]{2,1,0:T(8,128)(2,1)} %bitcast.4), calls=%async_computation.1 | async-start | bytes 1048576 | tf_op jit(solution)/shard_map/all_to_all | solution.py:504
  148.4 1.6 collective-permute-done.24.mate_ref
  150.0 1.4 shard_map.123.even_ref
  152.3 1.3 collective-permute-start.25
  153.6 1.6 collective-permute-done.25
  155.2 1.3 copy-done.29
  156.5 2.6 %shard_map.125 = bf16[2,196,576]{2,1,0:T(8,128)(2,1)S(1)} custom-call(f32[256,576]{1,0:T(8,128)S(1)} %shard_map.123.even_ref, bf16[256,576]{1,0:T(8,128)(2,1)S(1)} %collective-permute-done.23.odd_ref, f32[512,576]{1,0:T(8,128)S(1)} %copy-done.25, f32[2,576]{1,0:T(2,128)S(1)} %copy-done.23, f32[2,288]{1,0:T(2,128)S(1)} %add.9.sq_ref, ...), custom_call_target="tpu_custom_call" | custom-call | flops 2717908992 | bytes 4718592 | tf_op jit(solution)/shard_map/pallas_call | solution.py:383
  159.1 1.2 copy.12
  160.3 2.2 %all-to-all-done.1 = bf16[8,8,4096]{2,1,0:T(8,128)(2,1)} async-done(((bf16[8,8,4096]{2,1,0:T(8,128)(2,1)}), bf16[8,8,4096]{2,1,0:T(8,128)(2,1)}, u32[]{:S(2)}, u32[]{:S(2)}) %all-to-all-start.1) | async-done | bytes 524320 | tf_op jit(solution)/shard_map/all_to_all | solution.py:504
  162.4 1.9 %copy.14 = bf16[64,4096]{1,0:T(8,128)(2,1)} copy(bf16[64,4096]{1,0:T(8,128)(2,1)} %bitcast.5) | data formatting | bytes 1048576
  (85 shorter events, 8.2 us)
Async XLA Ops:
  0.6 3.3 %copy-start = (bf16[72,4096]{1,0:T(8,128)(2,1)S(1)}, bf16[72,4096]{1,0:T(8,128)(2,1)}, u32[]{:S(2)}) copy-start(bf16[72,4096]{1,0:T(8,128)(2,1)} %refs_2_.1) | copy-start | bytes 1769476
  0.6 5.9 %copy-start.13 = (bf16[576,288]{0,1:T(8,128)(2,1)S(1)}, bf16[576,288]{0,1:T(8,128)(2,1)}, u32[]{:S(2)}) copy-start(bf16[576,288]{0,1:T(8,128)(2,1)} %param.11) | copy-start | bytes 995332
  2.4 4.1 %copy-start.6 = (bf16[9,576,48]{1,2,0:T(8,128)(2,1)S(1)}, bf16[9,576,48]{1,2,0:T(8,128)(2,1)}, u32[]{:S(2)}) copy-start(bf16[9,576,48]{1,2,0:T(8,128)(2,1)} %param.10) | copy-start | bytes 1492996
  2.4 11.4 %copy-start.8 = (bf16[288,576]{1,0:T(8,128)(2,1)S(1)}, bf16[288,576]{1,0:T(8,128)(2,1)}, u32[]{:S(2)}) copy-start(bf16[288,576]{1,0:T(8,128)(2,1)} %expand_ref.3) | copy-start | bytes 995332
  2.4 33.1 %collective-permute-start = (bf16[72,4608]{1,0:T(8,128)(2,1)S(1)}, bf16[72,4608]{1,0:T(8,128)(2,1)S(1)}, u32[]{:S(2)}, u32[]{:S(2)}) collective-permute-start(bf16[72,4608]{1,0:T(8,128)(2,1)S(1)} %reshape.11.refs_0_.refs_2_), channel_id=1, source_target_pairs={{0,8},{2,10},{8,16},{10,18},{16,24},{18,26},{24,28},{26,30},{28,20... | collective-permute-start | bytes 1990664 | tf_op jit(solution)/shard_map/ppermute | solution.py:438
  2.5 33.1 %collective-permute-start.2 = (bf16[72,4608]{1,0:T(8,128)(2,1)S(1)}, bf16[72,4608]{1,0:T(8,128)(2,1)S(1)}, u32[]{:S(2)}, u32[]{:S(2)}) collective-permute-start(bf16[72,4608]{1,0:T(8,128)(2,1)S(1)} %reshape.11.refs_0_.refs_2_), channel_id=1, source_target_pairs={{0,4},{2,6},{8,0},{10,2},{16,8},{18,10},{24,16},{26,18},{28,24},{3... | collective-permute-start | bytes 1990664 | tf_op jit(solution)/shard_map/ppermute | solution.py:438
  3.9 31.6 %collective-permute-start.1 = (bf16[72,4096]{1,0:T(8,128)(2,1)S(1)}, bf16[72,4096]{1,0:T(8,128)(2,1)S(1)}, u32[]{:S(2)}, u32[]{:S(2)}) collective-permute-start(bf16[72,4096]{1,0:T(8,128)(2,1)S(1)} %copy-done), channel_id=1, source_target_pairs={{0,8},{2,10},{8,16},{10,18},{16,24},{18,26},{24,28},{26,30},{28,20... | collective-permute-start | bytes 1769480 | tf_op jit(solution)/shard_map/ppermute | solution.py:438
  4.0 31.5 %collective-permute-start.3 = (bf16[72,4096]{1,0:T(8,128)(2,1)S(1)}, bf16[72,4096]{1,0:T(8,128)(2,1)S(1)}, u32[]{:S(2)}, u32[]{:S(2)}) collective-permute-start(bf16[72,4096]{1,0:T(8,128)(2,1)S(1)} %copy-done), channel_id=1, source_target_pairs={{0,4},{2,6},{8,0},{10,2},{16,8},{18,10},{24,16},{26,18},{28,24},{3... | collective-permute-start | bytes 1769480 | tf_op jit(solution)/shard_map/ppermute | solution.py:438
  11.0 2.8 %collective-permute-start.4 = (f32[2,288]{1,0:T(2,128)S(1)}, f32[2,288]{1,0:T(2,128)S(1)}, u32[]{:S(2)}, u32[]{:S(2)}) collective-permute-start(f32[2,288]{1,0:T(2,128)S(1)} %get-tuple-element.74), channel_id=1, source_target_pairs={{0,1},{1,0},{2,3},{3,2},{4,5},{5,4},{6,7},{7,6},{8,9},{9,8},{10,11... | collective-permute-start | bytes 6920 | tf_op jit(solution)/shard_map/ppermute | solution.py:424
  14.9 1.1 copy-start.9
  16.0 0.7 copy-start.15
  16.7 0.6 copy-start.22
  17.3 1.1 copy-start.24
  18.4 16.4 %collective-permute-start.5 = (bf16[256,576]{1,0:T(8,128)(2,1)S(1)}, bf16[256,576]{1,0:T(8,128)(2,1)S(1)}, u32[]{:S(2)}, u32[]{:S(2)}) collective-permute-start(bf16[256,576]{1,0:T(8,128)(2,1)S(1)} %get-tuple-element.75), channel_id=1, source_target_pairs={{0,2},{2,4},{4,6},{6,8},{8,10},{10,12},{12,14},{14,16},{16,18},{18... | collective-permute-start | bytes 884744 | tf_op jit(solution)/shard_map/ppermute | solution.py:399
  34.8 0.7 copy-start.17
  35.5 0.8 copy-start.2
  35.6 1.0 copy-start.4
  36.4 16.0 %collective-permute-start.6 = (bf16[72,4608]{1,0:T(8,128)(2,1)S(1)}, bf16[72,4608]{1,0:T(8,128)(2,1)S(1)}, u32[]{:S(2)}, u32[]{:S(2)}) collective-permute-start(bf16[72,4608]{1,0:T(8,128)(2,1)S(1)} %collective-permute-done.refs_1_.refs_3_), channel_id=1, source_target_pairs={{0,8},{2,10},{8,16},{10,18},{16,24},{18,26},{24,28},{26,30},{28,20... | collective-permute-start | bytes 1990664 | tf_op jit(solution)/shard_map/ppermute | solution.py:438
  36.6 15.8 %collective-permute-start.7 = (bf16[72,4608]{1,0:T(8,128)(2,1)S(1)}, bf16[72,4608]{1,0:T(8,128)(2,1)}, u32[]{:S(2)}, u32[]{:S(2)}) collective-permute-start(bf16[72,4608]{1,0:T(8,128)(2,1)S(1)} %collective-permute-done.2.refs_2_.refs_4_), channel_id=1, source_target_pairs={{0,4},{2,6},{8,0},{10,2},{16,8},{18,10},{24,16},{26,18},{28,24},{3... | collective-permute-start | bytes 1990664 | tf_op jit(solution)/shard_map/ppermute | solution.py:438
  37.9 27.4 %all-to-all-start = ((bf16[8,8,4096]{2,1,0:T(8,128)(2,1)}), bf16[8,8,4096]{2,1,0:T(8,128)(2,1)S(1)}, u32[]{:S(2)}, u32[]{:S(2)}) async-start(bf16[8,8,4096]{2,1,0:T(8,128)(2,1)} %bitcast.14), calls=%async_computation | async-start | bytes 1048576 | tf_op jit(solution)/shard_map/all_to_all | solution.py:504
  42.7 30.1 %collective-permute-start.10 = (bf16[72,4096]{1,0:T(8,128)(2,1)}, bf16[72,4096]{1,0:T(8,128)(2,1)}, u32[]{:S(2)}, u32[]{:S(2)}) collective-permute-start(bf16[72,4096]{1,0:T(8,128)(2,1)} %copy-done.2), channel_id=1, source_target_pairs={{0,8},{2,10},{8,16},{10,18},{16,24},{18,26},{24,28},{26,30},{28,20... | collective-permute-start | bytes 1769480 | tf_op jit(solution)/shard_map/ppermute | solution.py:438
  43.9 34.6 %collective-permute-start.11 = (bf16[72,4096]{1,0:T(8,128)(2,1)}, bf16[72,4096]{1,0:T(8,128)(2,1)}, u32[]{:S(2)}, u32[]{:S(2)}) collective-permute-start(bf16[72,4096]{1,0:T(8,128)(2,1)} %copy-done.4), channel_id=1, source_target_pairs={{0,4},{2,6},{8,0},{10,2},{16,8},{18,10},{24,16},{26,18},{28,24},{3... | collective-permute-start | bytes 1769480 | tf_op jit(solution)/shard_map/ppermute | solution.py:438
  52.4 1.0 copy-start.16
  53.3 1.0 copy-start.18
  54.3 0.7 copy-start.19
  56.8 21.7 %collective-permute-start.8 = (bf16[64,4608]{1,0:T(8,128)(2,1)}, bf16[64,4608]{1,0:T(8,128)(2,1)}, u32[]{:S(2)}, u32[]{:S(2)}) collective-permute-start(bf16[64,4608]{1,0:T(8,128)(2,1)} %shard_map.107.own_ref), channel_id=1, source_target_pairs={{0,2},{2,0},{4,6},{6,4},{8,10},{10,8},{12,14},{14,12},{16,18},{18,... | collective-permute-start | bytes 1769480 | tf_op jit(solution)/shard_map/ppermute | solution.py:416
  65.3 17.1 %copy-start.1 = (bf16[72,4096]{1,0:T(8,128)(2,1)S(1)}, bf16[72,4096]{1,0:T(8,128)(2,1)}, u32[]{:S(2)}) copy-start(bf16[72,4096]{1,0:T(8,128)(2,1)} %refs_2_.1) | copy-start | bytes 1769476
  65.3 17.1 %copy-start.3 = (bf16[72,4096]{1,0:T(8,128)(2,1)S(1)}, bf16[72,4096]{1,0:T(8,128)(2,1)}, u32[]{:S(2)}) copy-start(bf16[72,4096]{1,0:T(8,128)(2,1)} %copy-done.2) | copy-start | bytes 1769476
  65.3 17.1 %copy-start.5 = (bf16[72,4096]{1,0:T(8,128)(2,1)S(1)}, bf16[72,4096]{1,0:T(8,128)(2,1)}, u32[]{:S(2)}) copy-start(bf16[72,4096]{1,0:T(8,128)(2,1)} %copy-done.4) | copy-start | bytes 1769476
  65.3 17.1 %collective-permute-start.9 = (bf16[64,4096]{1,0:T(8,128)(2,1)S(1)}, bf16[64,4096]{1,0:T(8,128)(2,1)S(1)}, u32[]{:S(2)}, u32[]{:S(2)}) collective-permute-start(bf16[64,4096]{1,0:T(8,128)(2,1)S(1)} %bitcast.6), channel_id=1, source_target_pairs={{0,2},{2,0},{4,6},{6,4},{8,10},{10,8},{12,14},{14,12},{16,18},{18,... | collective-permute-start | bytes 1572872 | tf_op jit(solution)/shard_map/ppermute | solution.py:416
  68.9 36.8 %collective-permute-start.13 = (bf16[72,4608]{1,0:T(8,128)(2,1)S(1)}, bf16[72,4608]{1,0:T(8,128)(2,1)S(1)}, u32[]{:S(2)}, u32[]{:S(2)}) collective-permute-start(bf16[72,4608]{1,0:T(8,128)(2,1)S(1)} %collective-permute-done.6.refs_3_.refs_5_), channel_id=1, source_target_pairs={{0,8},{2,10},{8,16},{10,18},{16,24},{18,26},{24,28},{26,30},{28,20... | collective-permute-start | bytes 1990664 | tf_op jit(solution)/shard_map/ppermute | solution.py:438
  72.7 33.0 %collective-permute-start.15 = (bf16[72,4608]{1,0:T(8,128)(2,1)}, bf16[72,4608]{1,0:T(8,128)(2,1)S(1)}, u32[]{:S(2)}, u32[]{:S(2)}) collective-permute-start(bf16[72,4608]{1,0:T(8,128)(2,1)} %collective-permute-done.7.refs_4_.refs_6_), channel_id=1, source_target_pairs={{0,4},{2,6},{8,0},{10,2},{16,8},{18,10},{24,16},{26,18},{28,24},{3... | collective-permute-start | bytes 1990664 | tf_op jit(solution)/shard_map/ppermute | solution.py:438
  78.5 27.1 %collective-permute-start.14 = (bf16[72,4096]{1,0:T(8,128)(2,1)}, bf16[72,4096]{1,0:T(8,128)(2,1)S(1)}, u32[]{:S(2)}, u32[]{:S(2)}) collective-permute-start(bf16[72,4096]{1,0:T(8,128)(2,1)} %collective-permute-done.10.refs_8_.refs_5_), channel_id=1, source_target_pairs={{0,8},{2,10},{8,16},{10,18},{16,24},{18,26},{24,28},{26,30},{28,20... | collective-permute-start | bytes 1769480 | tf_op jit(solution)/shard_map/ppermute | solution.py:438
  78.5 27.1 %collective-permute-start.16 = (bf16[72,4096]{1,0:T(8,128)(2,1)}, bf16[72,4096]{1,0:T(8,128)(2,1)S(1)}, u32[]{:S(2)}, u32[]{:S(2)}) collective-permute-start(bf16[72,4096]{1,0:T(8,128)(2,1)} %collective-permute-done.11.refs_9_.refs_6_), channel_id=1, source_target_pairs={{0,4},{2,6},{8,0},{10,2},{16,8},{18,10},{24,16},{26,18},{28,24},{3... | collective-permute-start | bytes 1769480 | tf_op jit(solution)/shard_map/ppermute | solution.py:438
  80.0 0.7 copy-start.20
  87.0 11.1 %collective-permute-start.12 = (f32[128,720]{1,0:T(8,128)S(1)}, f32[128,720]{1,0:T(8,128)S(1)}, u32[]{:S(2)}, u32[]{:S(2)}) collective-permute-start(f32[128,720]{1,0:T(8,128)S(1)} %shard_map.109.refs_0_), channel_id=1, source_target_pairs={{0,1},{1,0},{2,3},{3,2},{4,5},{5,4},{6,7},{7,6},{8,9},{9,8},{10,11... | collective-permute-start | bytes 1105928 | tf_op jit(solution)/shard_map/ppermute | solution.py:424
  105.7 4.2 %copy-start.7 = (bf16[9,576,48]{1,2,0:T(8,128)(2,1)S(1)}, bf16[9,576,48]{1,2,0:T(8,128)(2,1)}, u32[]{:S(2)}) copy-start(bf16[9,576,48]{1,2,0:T(8,128)(2,1)} %param.10) | copy-start | bytes 1492996
  105.7 16.3 %collective-permute-start.17 = (bf16[72,4608]{1,0:T(8,128)(2,1)S(1)}, bf16[72,4608]{1,0:T(8,128)(2,1)S(1)}, u32[]{:S(2)}, u32[]{:S(2)}) collective-permute-start(bf16[72,4608]{1,0:T(8,128)(2,1)S(1)} %collective-permute-done.13.refs_0_.refs_2_), channel_id=1, source_target_pairs={{0,8},{2,10},{8,16},{10,18},{16,24},{18,26},{24,28},{26,30},{28,20... | collective-permute-start | bytes 1990664 | tf_op jit(solution)/shard_map/ppermute | solution.py:438
  105.8 13.9 %collective-permute-start.18 = (bf16[72,4096]{1,0:T(8,128)(2,1)S(1)}, bf16[72,4096]{1,0:T(8,128)(2,1)S(1)}, u32[]{:S(2)}, u32[]{:S(2)}) collective-permute-start(bf16[72,4096]{1,0:T(8,128)(2,1)S(1)} %collective-permute-done.16.refs_3_), channel_id=1, source_target_pairs={{0,4},{2,6},{8,0},{10,2},{16,8},{18,10},{24,16},{26,18},{28,24},{3... | collective-permute-start | bytes 1769480 | tf_op jit(solution)/shard_map/ppermute | solution.py:438
  108.6 5.7 %collective-permute-start.19 = (f32[128,288]{1,0:T(8,128)S(1)}, f32[128,288]{1,0:T(8,128)S(1)}, u32[]{:S(2)}, u32[]{:S(2)}) collective-permute-start(f32[128,288]{1,0:T(8,128)S(1)} %shard_map.113.refs_0_), channel_id=1, source_target_pairs={{0,1},{1,0},{2,3},{3,2},{4,5},{5,4},{6,7},{7,6},{8,9},{9,8},{10,11... | collective-permute-start | bytes 442376 | tf_op jit(solution)/shard_map/ppermute | solution.py:424
  110.9 1.0 copy-start.28
  111.9 3.7 %copy-start.26 = (bf16[9,256,256]{2,1,0:T(8,128)(2,1)}, bf16[9,256,256]{2,1,0:T(8,128)(2,1)S(1)}, u32[]{:S(2)}) copy-start(bf16[9,256,256]{2,1,0:T(8,128)(2,1)S(1)} %get-tuple-element.137.refs_0_) | copy-start | bytes 3538948
  111.9 3.8 %copy-start.30 = (bf16[9,192,192]{2,1,0:T(8,128)(2,1)}, bf16[9,192,192]{2,1,0:T(8,128)(2,1)S(1)}, u32[]{:S(2)}) copy-start(bf16[9,192,192]{2,1,0:T(8,128)(2,1)S(1)} %get-tuple-element.139.refs_2_) | copy-start | bytes 1990660
  115.7 1.4 copy-start.21
  122.8 3.9 %collective-permute-start.20 = (f32[128,144]{1,0:T(8,128)S(1)}, f32[128,144]{1,0:T(8,128)S(1)}, u32[]{:S(2)}, u32[]{:S(2)}) collective-permute-start(f32[128,144]{1,0:T(8,128)S(1)} %shard_map.118.refs_0_), channel_id=1, source_target_pairs={{0,1},{1,0},{2,3},{3,2},{4,5},{5,4},{6,7},{7,6},{8,9},{9,8},{10,11... | collective-permute-start | bytes 221192 | tf_op jit(solution)/shard_map/ppermute | solution.py:424
  128.9 8.2 %collective-permute-start.21 = (bf16[64,4096]{1,0:T(8,128)(2,1)S(1)}, bf16[64,4096]{1,0:T(8,128)(2,1)S(1)}, u32[]{:S(2)}, u32[]{:S(2)}) collective-permute-start(bf16[64,4096]{1,0:T(8,128)(2,1)S(1)} %get-tuple-element.127), channel_id=1, source_target_pairs={{0,2},{2,0},{4,6},{6,4},{8,10},{10,8},{12,14},{14,12},{16,18},{18,... | collective-permute-start | bytes 1572872 | tf_op jit(solution)/shard_map/ppermute | solution.py:416
  131.1 2.0 %collective-permute-start.22 = (bf16[64,2304]{1,0:T(8,128)(2,1)S(1)}, bf16[64,2304]{1,0:T(8,128)(2,1)S(1)}, u32[]{:S(2)}, u32[]{:S(2)}) collective-permute-start(bf16[64,2304]{1,0:T(8,128)(2,1)S(1)} %get-tuple-element.129), channel_id=1, source_target_pairs={{0,2},{2,0},{4,6},{6,4},{8,10},{10,8},{12,14},{14,12},{16,18},{18,... | collective-permute-start | bytes 884744 | tf_op jit(solution)/shard_map/ppermute | solution.py:416
  132.3 0.8 copy-start.11
  134.6 15.4 %copy-start.12 = (f32[64,2304]{1,0:T(8,128)S(1)}, f32[64,2304]{1,0:T(8,128)}, u32[]{:S(2)}) copy-start(f32[64,2304]{1,0:T(8,128)} %copy-done.11) | copy-start | bytes 1769476
  134.6 9.4 %collective-permute-start.23 = (bf16[256,576]{1,0:T(8,128)(2,1)S(1)}, bf16[256,576]{1,0:T(8,128)(2,1)S(1)}, u32[]{:S(2)}, u32[]{:S(2)}) collective-permute-start(bf16[256,576]{1,0:T(8,128)(2,1)S(1)} %shard_map.122), channel_id=1, source_target_pairs={{2,0},{4,2},{6,4},{8,6},{10,8},{12,10},{14,12},{16,14},{18,16},{20... | collective-permute-start | bytes 884744 | tf_op jit(solution)/shard_map/ppermute | solution.py:399
  138.0 13.4 %copy-start.10 = (f32[512,576]{1,0:T(8,128)S(1)}, f32[512,576]{1,0:T(8,128)}, u32[]{:S(2)}) copy-start(f32[512,576]{1,0:T(8,128)} %copy-done.9) | copy-start | bytes 3538948
  138.0 13.4 %copy-start.23 = (f32[2,576]{1,0:T(2,128)S(1)}, f32[2,576]{1,0:T(2,128)}, u32[]{:S(2)}) copy-start(f32[2,576]{1,0:T(2,128)} %copy-done.22) | copy-start | bytes 13828
  144.0 18.4 %all-to-all-start.1 = ((bf16[8,8,4096]{2,1,0:T(8,128)(2,1)}), bf16[8,8,4096]{2,1,0:T(8,128)(2,1)}, u32[]{:S(2)}, u32[]{:S(2)}) async-start(bf16[8,8,4096]{2,1,0:T(8,128)(2,1)} %bitcast.4), calls=%async_computation.1 | async-start | bytes 1048576 | tf_op jit(solution)/shard_map/all_to_all | solution.py:504
  148.3 1.6 %collective-permute-start.24 = (bf16[64,2304]{1,0:T(8,128)(2,1)S(1)}, bf16[64,2304]{1,0:T(8,128)(2,1)S(1)}, u32[]{:S(2)}, u32[]{:S(2)}) collective-permute-start(bf16[64,2304]{1,0:T(8,128)(2,1)S(1)} %get-tuple-element.132), channel_id=1, source_target_pairs={{0,2},{2,0},{4,6},{6,4},{8,10},{10,8},{12,14},{14,12},{16,18},{18,... | collective-permute-start | bytes 884744 | tf_op jit(solution)/shard_map/ppermute | solution.py:416
  150.0 5.2 %copy-start.27 = (bf16[9,256,256]{2,1,0:T(8,128)(2,1)S(1)}, bf16[9,256,256]{2,1,0:T(8,128)(2,1)}, u32[]{:S(2)}) copy-start(bf16[9,256,256]{2,1,0:T(8,128)(2,1)} %copy-done.26) | copy-start | bytes 3538948
  151.5 3.7 %copy-start.14 = (bf16[576,288]{0,1:T(8,128)(2,1)S(1)}, bf16[576,288]{0,1:T(8,128)(2,1)}, u32[]{:S(2)}) copy-start(bf16[576,288]{0,1:T(8,128)(2,1)} %param.11) | copy-start | bytes 995332
  151.5 3.7 %copy-start.25 = (f32[512,576]{1,0:T(8,128)S(1)}, f32[512,576]{1,0:T(8,128)}, u32[]{:S(2)}) copy-start(f32[512,576]{1,0:T(8,128)} %copy-done.24) | copy-start | bytes 3538948
  151.5 3.7 %copy-start.31 = (bf16[9,192,192]{2,1,0:T(8,128)(2,1)S(1)}, bf16[9,192,192]{2,1,0:T(8,128)(2,1)}, u32[]{:S(2)}) copy-start(bf16[9,192,192]{2,1,0:T(8,128)(2,1)} %copy-done.30) | copy-start | bytes 1990660
  152.3 2.9 %collective-permute-start.25 = (f32[2,288]{1,0:T(2,128)S(1)}, f32[2,288]{1,0:T(2,128)S(1)}, u32[]{:S(2)}, u32[]{:S(2)}) collective-permute-start(f32[2,288]{1,0:T(2,128)S(1)} %shard_map.124), channel_id=1, source_target_pairs={{0,1},{1,0},{2,3},{3,2},{4,5},{5,4},{6,7},{7,6},{8,9},{9,8},{10,11... | collective-permute-start | bytes 6920 | tf_op jit(solution)/shard_map/ppermute | solution.py:424
  155.2 1.3 copy-start.29

commit v5 on v4

--- a/solution.py
+++ b/solution.py
@@ -13,7 +13,7 @@
 FRAME_ROWS = WIDE * WIDE
 EDGE = 8
 LANES = 128
-VMEM_BYTES = 20 * 2**20
+VMEM_BYTES = 16 * 2**20
 FREE = pl.CostEstimate(flops=0, bytes_accessed=0, transcendentals=0)
 
 
@@ -175,6 +175,8 @@
             start += jnp.where(clip_ref[other] < clip, 1, 0)
         out_ref[1 + block] = keep_ref[clip] - (pair - start) * (OUT_SIDE * OUT_SIDE)
     before = clip_ref[jnp.maximum(2 * shard - 1, 0)]
+    chip, chips = shard // 2, lax.axis_size("ctx") // 2
+    out_ref[4] = jnp.where(chip % 2 == 0, chip // 2, chips - 1 - chip // 2)
     out_ref[3] = jnp.where((shard > 0) & (before == clip_ref[2 * shard]), 1, 0)
 
 
@@ -216,7 +218,9 @@
             out_ref[:, at : at + chans] = rows[tap * per_frame : (tap + 1) * per_frame]
 
 
-def unpatch_kernel(facts_ref, own_ref, mate_ref, out_ref):
+def unpatch_kernel(facts_ref, own_ref, mate_ref, out_ref, facts_out_ref):
+    for place in range(facts_ref.shape[0]):
+        facts_out_ref[place] = facts_ref[place]
     chans = out_ref.shape[1]
     rows = own_ref[...] + mate_ref[...].astype(jnp.float32)
     pieces = [rows[:, tap * chans : (tap + 1) * chans] for tap in range(4)]
@@ -329,7 +333,7 @@
     smem = pl.BlockSpec(memory_space=pltpu.SMEM)
     return pl.pallas_call(
         facts_kernel,
-        out_shape=jax.ShapeDtypeStruct((4,), jnp.int32),
+        out_shape=jax.ShapeDtypeStruct((5,), jnp.int32),
         in_specs=[smem, smem],
         out_specs=smem,
         cost_estimate=FREE,
@@ -361,8 +365,12 @@
 def return_patches(facts, own, mate, chans, dtype):
     return pl.pallas_call(
         unpatch_kernel,
-        out_shape=jax.ShapeDtypeStruct((FRAME_ROWS, chans), dtype),
+        out_shape=(
+            jax.ShapeDtypeStruct((FRAME_ROWS, chans), dtype),
+            jax.ShapeDtypeStruct(facts.shape, jnp.int32),
+        ),
         in_specs=vmem_specs(2),
+        out_specs=vmem_specs(1)[::-1],
         compiler_params=pltpu.CompilerParams(vmem_limit_bytes=VMEM_BYTES),
         cost_estimate=FREE,
     )(facts, own, mate)
@@ -453,20 +461,23 @@
     out_ref[...] = jnp.concatenate(products, axis=1)
 
 
-def totals_kernel(count, unit, lanes, backward, first, facts_ref, *refs):
+def live_rows(facts_ref, rows, unit):
+    block, token = token_place(
+        lax.broadcasted_iota(jnp.int32, (rows, 1), 0), facts_ref[0], unit
+    )
+    return (token < jnp.where(block == 0, facts_ref[1], facts_ref[2])).astype(jnp.float32)
+
+
+def totals_kernel(count, unit, lanes, first, facts_ref, *refs):
     sums = refs[0][...] + refs[1][...]
     blocks, refs = refs[2 : 2 + count], refs[2 + count :]
     before, after = refs[:-2], refs[-2:]
     rows, depth = sums.shape[0], sums.shape[1] // 2
-    pre, grad_act = sums[:, :depth], sums[:, depth:]
-    core = facts_ref[0]
-    block, token = token_place(lax.broadcasted_iota(jnp.int32, (rows, 1), 0), core, unit)
-    live = (token < jnp.where(block == 0, facts_ref[1], facts_ref[2])).astype(jnp.float32)
-    factor = grad_act * silu_slope(pre) if backward else pre * jax.nn.sigmoid(pre)
-    factor = (factor * live).astype(jnp.bfloat16)
-    if backward:
-        matrix = reorder_matrix(core, unit, False)
-        factor = jnp.dot(matrix, factor, preferred_element_type=jnp.float32).astype(jnp.bfloat16)
+    factor = sums[:, depth:] * silu_slope(sums[:, :depth]) * live_rows(facts_ref, rows, unit)
+    matrix = reorder_matrix(facts_ref[0], unit, False)
+    factor = jnp.dot(
+        matrix, factor.astype(jnp.bfloat16), preferred_element_type=jnp.float32
+    ).astype(jnp.bfloat16)
     width = depth // count
     total = 0.0
     for place, ref in enumerate(blocks):
@@ -478,6 +489,68 @@
         ref[...] = value.astype(ref.dtype)
 
 
+def ring_offsets(chips):
+    offsets = [0]
+    for step in range(1, chips // 2):
+        offsets += [-step, step]
+    return offsets + [chips // 2]
+
+
+def block_columns(facts_ref, offset, chips, width):
+    shape = (width, chips * width)
+    place = (facts_ref[4] + offset + chips) % chips
+    column = lax.broadcasted_iota(jnp.int32, shape, 1)
+    return (column == lax.broadcasted_iota(jnp.int32, shape, 0) + place * width).astype(jnp.bfloat16)
+
+
+def exchange_matrix(core, unit, to_sent):
+    per_block = OUT_SIDE * OUT_SIDE
+    shape = (2 * per_block,) * 2
+    out_row = lax.broadcasted_iota(jnp.int32, shape, 0)
+    in_row = lax.broadcasted_iota(jnp.int32, shape, 1)
+    sent, kept = (out_row, in_row) if to_sent else (in_row, out_row)
+    target_core = (sent // (2 * unit)) % 2
+    within = sent // (4 * unit) * (2 * unit) + sent % (2 * unit)
+    return (within + jnp.where(target_core == core, 0, per_block) == kept).astype(jnp.bfloat16)
+
+
+def act_kernel(counts, unit, facts_ref, *refs):
+    *terms, out_ref = refs
+    rows = terms[0].shape[0]
+    live = live_rows(facts_ref, rows, unit)
+    chips = sum(counts)
+    offsets = iter(ring_offsets(chips))
+    total = 0.0
+    for group, count in enumerate(counts):
+        depth = terms[2 * group].shape[1] // 2
+        pre = terms[2 * group][:, :depth] + terms[2 * group + 1][:, :depth]
+        act = (pre * jax.nn.sigmoid(pre) * live).astype(jnp.bfloat16)
+        width = depth // count
+        for place in range(count):
+            columns = block_columns(facts_ref, next(offsets), chips, width)
+            piece = act[:, place * width : (place + 1) * width]
+            total += jnp.dot(piece, columns, preferred_element_type=jnp.float32)
+    matrix = exchange_matrix(facts_ref[0], unit, True)
+    out_ref[...] = jnp.dot(
+        matrix, total.astype(jnp.bfloat16), preferred_element_type=jnp.float32
+    ).astype(jnp.bfloat16)
+
+
+def token_kernel(unit, facts_ref, act_ref, *refs):
+    *blocks, keep_ref, send_ref = refs
+    chips, width = len(blocks), blocks[0].shape[0]
+    matrix = exchange_matrix(facts_ref[0], unit, False)
+    act = jnp.dot(matrix, act_ref[...], preferred_element_type=jnp.float32).astype(jnp.bfloat16)
+    total = 0.0
+    for offset, ref in zip(ring_offsets(chips), blocks):
+        columns = block_columns(facts_ref, offset, chips, width)
+        piece = contract_last(act, columns).astype(jnp.bfloat16)
+        total += jnp.dot(piece, ref[...], preferred_element_type=jnp.float32)
+    rows = keep_ref.shape[0]
+    keep_ref[...] = total[:rows]
+    send_ref[...] = total[rows:].astype(jnp.bfloat16)
+
+
 def partial_sums(patches, back, samplers, readouts):
     count, width = len(samplers), samplers[0].shape[0]
     return whole_call(
@@ -485,17 +558,38 @@
     )(patches, *back, *samplers, *readouts)
 
 
-def add_products(facts, sums, blocks, before, unit, lanes, backward, last):
-    rows, columns = sums[0].shape[0] // 2, lanes.stop - lanes.start
-    kernel = functools.partial(totals_kernel, len(blocks), unit, lanes, backward, not before)
-    operands = (*sums, *blocks, *before)
+def facts_call(kernel, outs, facts, operands, cost=FREE):
     return pl.pallas_call(
         kernel,
-        out_shape=(f32(rows, columns), (bf16 if last else f32)(rows, columns)),
+        out_shape=outs,
         in_specs=vmem_specs(len(operands)),
         compiler_params=pltpu.CompilerParams(vmem_limit_bytes=VMEM_BYTES),
-        cost_estimate=FREE,
+        cost_estimate=cost,
     )(facts, *operands)
+
+
+def add_products(facts, sums, blocks, before, unit, lanes, last):
+    rows, columns = sums[0].shape[0] // 2, lanes.stop - lanes.start
+    kernel = functools.partial(totals_kernel, len(blocks), unit, lanes, not before)
+    outs = f32(rows, columns), (bf16 if last else f32)(rows, columns)
+    return facts_call(kernel, outs, facts, (*sums, *blocks, *before))
+
+
+def act_to_send(facts, groups, counts, unit):
+    rows, columns = groups[0][0].shape[0], sum(terms[0].shape[1] // 2 for terms in groups)
+    kernel = functools.partial(act_kernel, counts, unit)
+    operands = [term for terms in groups for term in terms]
+    return facts_call(kernel, bf16(rows, columns), facts, operands)
+
+
+def token_products(facts, act, readouts, unit):
+    rows, columns = act.shape[0] // 2, readouts[0].shape[1]
+    kernel = functools.partial(token_kernel, unit)
+    outs = f32(rows, columns), bf16(rows, columns)
+    cost = pl.CostEstimate(
+        flops=40 * act.size * columns, bytes_accessed=2 * act.shape[1] * columns, transcendentals=0
+    )
+    return facts_call(kernel, outs, facts, (act, *readouts), cost)
 
 
 def chips_exchange(value):
@@ -533,10 +627,10 @@
     even, odd, excite, active, slope = hidden_frames(conv, padded, squeezed, squeeze_out)
     halo = shifted(odd, "ctx", 1)
 
-    every = slice(0, readout_kernel.shape[1])
     halo_lanes, even_lanes = slice(0, 4 * chans), slice(4 * chans, 8 * chans)
     samplers, readouts = [flat_sampler], [readout_kernel]
-    tokens = halo_grads = even_grads = ()
+    halo_grads = even_grads = ()
+    all_readouts, groups, counts = [], [], []
     for step in range(1, steps + 1):
         if step == 1:
             *blocks, halo, even = tie(*blocks, halo, even)
@@ -547,12 +641,12 @@
             patches = take_patches(facts, halo, even)
             patches = order_rows(facts, patches, swap_cores(patches), unit)
             back = (back, swap_cores(back))
-        here = blocks
-        if step < steps:
+        here, last = blocks, step == steps
+        if not last:
             if step == steps - 1:
-                held = *tokens, *halo_grads, *even_grads
+                held = *halo_grads, *even_grads
                 *held, up_s, up_r, down_s, down_r, group_kernel = tie(*held, *here, group_kernel)
-                tokens, halo_grads, even_grads = held[:2], held[2:4], held[4:]
+                halo_grads, even_grads = held[:2], held[2:]
                 dense = dense_weights(group_kernel)
                 here = up_s, up_r, down_s, down_r
             samplers, readouts = samplers + [here[0], here[2]], readouts + [here[1], here[3]]
@@ -560,35 +654,31 @@
                 here = up_s, None, None, down_r
             blocks = ring_step(here)
         else:
-            held = *tokens, *halo_grads, *even_grads, *dense
+            held = *halo_grads, *even_grads, *dense
             last_s, last_r, *held = tie(here[0], here[3], *held)
-            tokens, halo_grads, even_grads, dense = held[:2], held[2:4], held[4:6], held[6:]
+            halo_grads, even_grads, dense = held[:2], held[2:4], held[4:]
             samplers, readouts = samplers + [last_s], readouts + [last_r]
         if step >= steps - 2:
-            last = step == steps
             sums = tp_terms(partial_sums(patches, back, samplers, readouts))
-            halo_grads = add_products(
-                facts, sums, samplers, halo_grads, unit, halo_lanes, True, last
-            )
+            halo_grads = add_products(facts, sums, samplers, halo_grads, unit, halo_lanes, last)
             if last:
-                sums, halo_grads = list(sums), list(halo_grads)
-                sums[0], halo_grads[1] = tie(sums[0], halo_grads[1])
-            even_grads = add_products(
-                facts, sums, samplers, even_grads, unit, even_lanes, True, last
-            )
-            tokens = add_products(facts, sums, readouts, tokens, unit, every, False, last)
+                halo_own, halo_mate = halo_grads
+                halo_mate, first_sums = tie(halo_mate, sums[0])
+                sums = first_sums, sums[1]
+                halo_mate = swap_cores(halo_mate)
+                lead, facts_late = return_patches(facts, halo_own, halo_mate, chans, jnp.bfloat16)
+                grad_odd = shifted(lead, "ctx", -1)
+            even_grads = add_products(facts, sums, samplers, even_grads, unit, even_lanes, last)
+            groups, counts = groups + [sums], counts + [len(samplers)]
+            all_readouts += readouts
             samplers, readouts = [], []
-    halo_mate = swap_cores(halo_grads[1])
-    halo_own, even_own, token_keep = tie(halo_grads[0], even_grads[0], tokens[0])
-    lead = return_patches(facts, halo_own, halo_mate, chans, jnp.bfloat16)
-    grad_odd = shifted(lead, "ctx", -1)
-    grad_even = return_patches(
-        facts, even_own, swap_cores(even_grads[1]), chans, jnp.float32
-    )
-    tokens = (token_keep + swap_cores(tokens[1]).astype(jnp.float32)).astype(jnp.bfloat16)
-    tokens, grad_odd = tie(tokens, grad_odd)
-    llm_tokens = chips_exchange(tokens)
+    act = chips_exchange(act_to_send(facts, groups, counts, unit))
+    grad_even, facts_late = return_patches(
+        facts_late, even_grads[0], swap_cores(even_grads[1]), chans, jnp.float32
+    )
     grad_relaxed = sum_tp(excite_grad(grad_even, grad_odd, active, excite, squeeze_out))
+    tokens, send = token_products(facts_late, act, all_readouts, unit)
+    llm_tokens = (tokens + swap_cores(send).astype(jnp.float32)).astype(jnp.bfloat16)
     grad_features = conv_backward(
         grad_even, grad_odd, slope, excite, squeezed, grad_relaxed, squeeze_in, dense, width
     )

time: 166 us -> 168 us (1.012)
  waiting for transfers between devices: 53.2 us -> 42.5 us
  Pallas kernels: 39.3 us -> 46.4 us
  local copies, waits for them, and re-layouts: 17.4 us -> 19.6 us
  starting transfers between devices: 52.4 us -> 54.2 us
    ppermute x2, waiting for transfers between devices: 16.7 us -> 9.57 us  [shifted(): return lax.ppermute(value, axis, pairs)]
    pallas_call x12 -> x11, Pallas kernels: 19 us -> 24.1 us  [the longest x8 18.3 us: facts_call(): pl.pallas_call(kernel, out_shape=outs, in_specs=vmem_specs(len(operands))...]
    all_to_all x2, waiting for transfers between devices: 4.31 us -> 2.11 us  [chips_exchange(): lax.all_to_all(value, 'ctx', split_axis=0, concat_axis=0, tiled=True, axi...]
    unnamed x67 -> x84, local copies, waits for them, and re-layouts: 15.7 us -> 17.8 us
    ppermute x14, waiting for transfers between devices: 12.8 us -> 14.7 us  [ring_step(): lax.ppermute(value, 'ctx', pairs)]
    ppermute x5, waiting for transfers between devices: 17.8 us -> 16.1 us  [tp_terms(): other = lax.ppermute(value, 'tp', [(i, i ^ reach) for i in range(size)])]
  transfers between devices with their start and end apart: 28 -> 28, of which waited for: 14 -> 13; matrix products, arithmetic and copies ran while one was open for 2% -> 1% of each run, Pallas kernels for 22% -> 27%
where the time goes in v5:
time: 168 us; the launch traced here: 165 us
  starting transfers between devices  54.2 us (32%)
  Pallas kernels  46.4 us (28%)
  waiting for transfers between devices  42.5 us (25%)
  local copies, waits for them, and re-layouts  19.6 us (12%)
    pallas_call x8, Pallas kernels, facts_call(): pl.pallas_call(kernel, out_shape=outs, in_specs=vmem_specs(len(operands))...  18.3 us
    unnamed x84, local copies, waits for them, and re-layouts  17.8 us
    ppermute x14, starting transfers between devices, ring_step(): lax.ppermute(value, 'ctx', pairs)  17.1 us
    ppermute x5, waiting for transfers between devices, tp_terms(): other = lax.ppermute(value, 'tp', [(i, i ^ reach) for i in range(size)])  16.1 us
    ppermute x14, waiting for transfers between devices, ring_step(): lax.ppermute(value, 'ctx', pairs)  14.7 us
    ppermute x5, starting transfers between devices, swap_cores(): lax.ppermute(value, 'ctx', [(i, i ^ 1) for i in range(lax.axis_size('ctx'...  12.3 us
    ppermute x2, waiting for transfers between devices, shifted(): return lax.ppermute(value, axis, pairs)  9.57 us
    all_to_all x2, starting transfers between devices, chips_exchange(): lax.all_to_all(value, 'ctx', split_axis=0, concat_axis=0, tiled=True, axi...  9.37 us
  transfers between devices with their start and end apart: 28, of which 13 were waited for; matrix products, arithmetic and copies ran while one was open for 1% of the time, Pallas kernels for 27%

profile of v5, /device:TPU:3, one launch (start us, length us, event | category | flops | bytes accessed | tf_op | source)
XLA Modules:
  0.0 164.7 jit_solution(18229980202053805606)
XLA Ops:
  0.7 1.7 %reshape.11.refs_0_.refs_2_ = bf16[72,4608]{1,0:T(8,128)(2,1)S(1)} reshape(bf16[72,8,576]{2,1,0:T(8,128)(2,1)} %param.13) | data formatting | bytes 1327104 | tf_op jit(solution)/shard_map/reshape | solution.py:617
  2.4 1.3 collective-permute-start.2
  3.9 1.3 collective-permute-start.3
  5.4 1.1 copy.11.feat_ref
  6.5 1.0 copy-done.22
  7.5 4.5 %shard_map.105 = (f32[512,576]{1,0:T(8,128)S(1)}, bf16[512,576]{1,0:T(8,128)(2,1)S(1)}, f32[2,288]{1,0:T(2,128)S(1)}) custom-call(bf16[2,196,576]{2,1,0:T(8,128)(2,1)S(1)} %copy.11.feat_ref, bf16[9,48,576]{2,1,0:T(8,128)(2,1)S(1)} %bitcast.10, bf16[288,576]{1,0:T(8,128)(2,1)S(1)} %bitcast.12), custom_call_target="tpu_custom_call" | custom-call | tf_op jit(solution)/shard_map/pallas_call | solution.py:307
  12.0 1.3 collective-permute-start.4
  13.2 1.5 collective-permute-done.4
  14.7 1.2 shard_map.106
  15.9 1.1 copy-done.3
  18.3 1.1 copy-done.33
  19.4 5.7 %collective-permute-start.5 = (bf16[256,576]{1,0:T(8,128)(2,1)S(1)}, bf16[256,576]{1,0:T(8,128)(2,1)S(1)}, u32[]{:S(2)}, u32[]{:S(2)}) collective-permute-start(bf16[256,576]{1,0:T(8,128)(2,1)S(1)} %get-tuple-element.66), channel_id=1, source_target_pairs={{0,2},{2,4},{4,6},{6,8},{8,10},{10,12},{12,14},{14,16},{16,18},{18... | collective-permute-start | bytes 884744 | tf_op jit(solution)/shard_map/ppermute | solution.py:407
  25.1 9.6 %collective-permute-done.5.halo_ref = bf16[256,576]{1,0:T(8,128)(2,1)S(1)} collective-permute-done((bf16[256,576]{1,0:T(8,128)(2,1)S(1)}, bf16[256,576]{1,0:T(8,128)(2,1)S(1)}, u32[]{:S(2)}, u32[]{:S(2)}) %collective-permute-start.5) | collective-permute-done | bytes 294944 | tf_op jit(solution)/shard_map/ppermute | solution.py:407
  36.4 1.3 collective-permute-start.7
  37.7 5.0 %all-to-all-start = ((bf16[8,8,4096]{2,1,0:T(8,128)(2,1)}), bf16[8,8,4096]{2,1,0:T(8,128)(2,1)S(1)}, u32[]{:S(2)}, u32[]{:S(2)}) async-start(bf16[8,8,4096]{2,1,0:T(8,128)(2,1)} %bitcast.15), calls=%async_computation | async-start | bytes 1048576 | tf_op jit(solution)/shard_map/all_to_all | solution.py:598
  42.7 1.3 shard_map.104.facts_ref
  44.0 1.5 collective-permute-start.11
  45.5 5.9 %collective-permute-done.6.refs_3_.refs_5_ = bf16[72,4608]{1,0:T(8,128)(2,1)S(1)} collective-permute-done((bf16[72,4608]{1,0:T(8,128)(2,1)S(1)}, bf16[72,4608]{1,0:T(8,128)(2,1)S(1)}, u32[]{:S(2)}, u32[]{:S(2)}) %collective-permute-start.6) | collective-permute-done | bytes 663584 | tf_op jit(solution)/shard_map/ppermute | solution.py:446
  51.5 1.0 copy-done.25
  52.5 1.0 copy-done.27
  54.1 1.8 %shard_map.107.own_ref = bf16[64,4608]{1,0:T(8,128)(2,1)} custom-call(s32[5]{0:T(128)S(1)} %copy-done.28, bf16[256,576]{1,0:T(8,128)(2,1)S(1)} %copy-done.27, bf16[256,576]{1,0:T(8,128)(2,1)S(1)} %copy-done.25), custom_call_target="tpu_custom_call" | custom-call | tf_op jit(solution)/shard_map/pallas_call | solution.py:356
  56.0 7.1 %collective-permute-start.8 = (bf16[64,4608]{1,0:T(8,128)(2,1)}, bf16[64,4608]{1,0:T(8,128)(2,1)}, u32[]{:S(2)}, u32[]{:S(2)}) collective-permute-start(bf16[64,4608]{1,0:T(8,128)(2,1)} %shard_map.107.own_ref), channel_id=1, source_target_pairs={{0,2},{2,0},{4,6},{6,4},{8,10},{10,8},{12,14},{14,12},{16,18},{18,... | collective-permute-start | bytes 1769480 | tf_op jit(solution)/shard_map/ppermute | solution.py:424
  63.0 2.1 %all-to-all-done = bf16[8,8,4096]{2,1,0:T(8,128)(2,1)S(1)} async-done(((bf16[8,8,4096]{2,1,0:T(8,128)(2,1)}), bf16[8,8,4096]{2,1,0:T(8,128)(2,1)S(1)}, u32[]{:S(2)}, u32[]{:S(2)}) %all-to-all-start) | async-done | bytes 524320 | tf_op jit(solution)/shard_map/all_to_all | solution.py:598
  65.2 3.6 %collective-permute-start.9 = (bf16[64,4096]{1,0:T(8,128)(2,1)S(1)}, bf16[64,4096]{1,0:T(8,128)(2,1)S(1)}, u32[]{:S(2)}, u32[]{:S(2)}) collective-permute-start(bf16[64,4096]{1,0:T(8,128)(2,1)S(1)} %bitcast.6), channel_id=1, source_target_pairs={{0,2},{2,0},{4,6},{6,4},{8,10},{10,8},{12,14},{14,12},{16,18},{18,... | collective-permute-start | bytes 1572872 | tf_op jit(solution)/shard_map/ppermute | solution.py:424
  68.7 1.7 %collective-permute-start.13 = (bf16[72,4608]{1,0:T(8,128)(2,1)S(1)}, bf16[72,4608]{1,0:T(8,128)(2,1)S(1)}, u32[]{:S(2)}, u32[]{:S(2)}) collective-permute-start(bf16[72,4608]{1,0:T(8,128)(2,1)S(1)} %collective-permute-done.6.refs_3_.refs_5_), channel_id=1, source_target_pairs={{0,8},{2,10},{8,16},{10,18},{16,24},{18,26},{24,28},{26,30},{28,20... | collective-permute-start | bytes 1990664 | tf_op jit(solution)/shard_map/ppermute | solution.py:446
  70.4 2.1 %collective-permute-done.10.refs_8_.refs_3_ = bf16[72,4096]{1,0:T(8,128)(2,1)} collective-permute-done((bf16[72,4096]{1,0:T(8,128)(2,1)}, bf16[72,4096]{1,0:T(8,128)(2,1)}, u32[]{:S(2)}, u32[]{:S(2)}) %collective-permute-start.10) | collective-permute-done | bytes 589856 | tf_op jit(solution)/shard_map/ppermute | solution.py:446
  72.5 5.9 %collective-permute-start.15 = (bf16[72,4608]{1,0:T(8,128)(2,1)}, bf16[72,4608]{1,0:T(8,128)(2,1)S(1)}, u32[]{:S(2)}, u32[]{:S(2)}) collective-permute-start(bf16[72,4608]{1,0:T(8,128)(2,1)} %collective-permute-done.7.refs_4_.refs_6_), channel_id=1, source_target_pairs={{0,4},{2,6},{8,0},{10,2},{16,8},{18,10},{24,16},{26,18},{28,24},{3... | collective-permute-start | bytes 1990664 | tf_op jit(solution)/shard_map/ppermute | solution.py:446
  78.4 1.5 collective-permute-start.16
  80.5 1.7 %shard_map.108.patch_ref = bf16[128,4608]{1,0:T(8,128)(2,1)S(1)} custom-call(s32[5]{0:T(128)S(1)} %copy-done.29, bf16[64,4608]{1,0:T(8,128)(2,1)} %shard_map.107.own_ref, bf16[64,4608]{1,0:T(8,128)(2,1)} %collective-permute-done.8.mate_ref), custom_call_target="tpu_custom_call" | custom-call | tf_op jit(solution)/shard_map/pallas_call | solution.py:345
  82.3 4.5 %shard_map.109.refs_0_ = f32[128,720]{1,0:T(8,128)S(1)} custom-call(bf16[128,4608]{1,0:T(8,128)(2,1)S(1)} %shard_map.108.patch_ref, bf16[64,4096]{1,0:T(8,128)(2,1)S(1)} %bitcast.7, bf16[64,4096]{1,0:T(8,128)(2,1)S(1)} %collective-permute-done.9.send_ref, bf16[72,4608]{1,0:T(8,128)(2,1)S(1)} %reshape.11.refs_0_.refs_2_, ...), custom_call_target="tpu_custom_call" | custom-call | tf_op jit(solution)/shard_map/pallas_call | solution.py:556
  86.8 1.3 collective-permute-start.12
  88.1 9.6 %collective-permute-done.12.refs_1_ = f32[128,720]{1,0:T(8,128)S(1)} collective-permute-done((f32[128,720]{1,0:T(8,128)S(1)}, f32[128,720]{1,0:T(8,128)S(1)}, u32[]{:S(2)}, u32[]{:S(2)}) %collective-permute-start.12) | collective-permute-done | bytes 368672 | tf_op jit(solution)/shard_map/ppermute | solution.py:432
  97.7 2.4 %shard_map.111 = (f32[64,2304]{1,0:T(8,128)S(1)}, f32[64,2304]{1,0:T(8,128)S(1)}) custom-call(s32[5]{0:T(128)S(1)} %copy-done.30, f32[128,720]{1,0:T(8,128)S(1)} %shard_map.109.refs_0_, f32[128,720]{1,0:T(8,128)S(1)} %collective-permute-done.12.refs_1_, bf16[72,4608]{1,0:T(8,128)(2,1)S(1)} %reshape.11.refs_0_.refs_2_, ...), custom_call_target="tpu_custom_call" | custom-call | tf_op jit(solution)/shard_map/pallas_call | solution.py:562
  100.1 2.4 %shard_map.110 = (f32[64,2304]{1,0:T(8,128)S(1)}, f32[64,2304]{1,0:T(8,128)S(1)}) custom-call(s32[5]{0:T(128)S(1)} %copy-done.30, f32[128,720]{1,0:T(8,128)S(1)} %shard_map.109.refs_0_, f32[128,720]{1,0:T(8,128)S(1)} %collective-permute-done.12.refs_1_, bf16[72,4608]{1,0:T(8,128)(2,1)S(1)} %reshape.11.refs_0_.refs_2_, ...), custom_call_target="tpu_custom_call" | custom-call | tf_op jit(solution)/shard_map/pallas_call | solution.py:562
  102.6 1.8 %collective-permute-done.16.refs_3_.refs_6_ = bf16[72,4096]{1,0:T(8,128)(2,1)S(1)} collective-permute-done((bf16[72,4096]{1,0:T(8,128)(2,1)}, bf16[72,4096]{1,0:T(8,128)(2,1)S(1)}, u32[]{:S(2)}, u32[]{:S(2)}) %collective-permute-start.16) | collective-permute-done | bytes 589856 | tf_op jit(solution)/shard_map/ppermute | solution.py:446
  104.5 2.0 %collective-permute-start.18 = (bf16[72,4096]{1,0:T(8,128)(2,1)S(1)}, bf16[72,4096]{1,0:T(8,128)(2,1)S(1)}, u32[]{:S(2)}, u32[]{:S(2)}) collective-permute-start(bf16[72,4096]{1,0:T(8,128)(2,1)S(1)} %collective-permute-done.16.refs_3_.refs_6_), channel_id=1, source_target_pairs={{0,4},{2,6},{8,0},{10,2},{16,8},{18,10},{24,16},{26,18},{28,24},{3... | collective-permute-start | bytes 1769480 | tf_op jit(solution)/shard_map/ppermute | solution.py:446
  106.5 1.4 shard_map.112.refs_0_.refs_2_
  107.9 1.3 collective-permute-start.19
  109.2 1.0 shard_map.115
  110.2 1.0 copy-done.35
  111.3 1.0 copy-done.37
  113.9 1.4 shard_map.114
  115.3 1.4 shard_map.113
  116.7 2.3 %collective-permute-done.18.refs_1_.refs_7_ = bf16[72,4096]{1,0:T(8,128)(2,1)S(1)} collective-permute-done((bf16[72,4096]{1,0:T(8,128)(2,1)S(1)}, bf16[72,4096]{1,0:T(8,128)(2,1)S(1)}, u32[]{:S(2)}, u32[]{:S(2)}) %collective-permute-start.18) | collective-permute-done | bytes 589856 | tf_op jit(solution)/shard_map/ppermute | solution.py:446
  119.0 2.4 %collective-permute-done.17.refs_0_.refs_2_ = bf16[72,4608]{1,0:T(8,128)(2,1)S(1)} collective-permute-done((bf16[72,4608]{1,0:T(8,128)(2,1)S(1)}, bf16[72,4608]{1,0:T(8,128)(2,1)S(1)}, u32[]{:S(2)}, u32[]{:S(2)}) %collective-permute-start.17) | collective-permute-done | bytes 663584 | tf_op jit(solution)/shard_map/ppermute | solution.py:446
  122.2 1.3 collective-permute-start.20
  123.5 3.1 %collective-permute-done.20.refs_1_.refs_5_ = f32[128,144]{1,0:T(8,128)S(1)} collective-permute-done((f32[128,144]{1,0:T(8,128)S(1)}, f32[128,144]{1,0:T(8,128)S(1)}, u32[]{:S(2)}, u32[]{:S(2)}) %collective-permute-start.20) | collective-permute-done | bytes 73760 | tf_op jit(solution)/shard_map/ppermute | solution.py:432
  126.6 1.8 %shard_map.117 = (f32[64,2304]{1,0:T(8,128)S(1)}, bf16[64,2304]{1,0:T(8,128)(2,1)}) custom-call(s32[5]{0:T(128)S(1)} %copy-done.30, f32[128,144]{1,0:T(8,128)S(1)} %shard_map.116.refs_0_.refs_4_, f32[128,144]{1,0:T(8,128)S(1)} %collective-permute-done.20.refs_1_.refs_5_, bf16[72,4608]{1,0:T(8,128)(2,1)S(1)} %collective-permute-done.17.refs_0_.refs_2_, ...), custom_call_target="tpu_custom_call" | custom-call | tf_op jit(solution)/shard_map/pallas_call | solution.py:562
  128.4 1.6 collective-permute-start.21
  130.0 1.8 %shard_map.119 = (f32[64,2304]{1,0:T(8,128)S(1)}, bf16[64,2304]{1,0:T(8,128)(2,1)}) custom-call(s32[5]{0:T(128)S(1)} %copy-done.30, f32[128,144]{1,0:T(8,128)S(1)} %shard_map.116.refs_0_.refs_4_, f32[128,144]{1,0:T(8,128)S(1)} %collective-permute-done.20.refs_1_.refs_5_, bf16[72,4608]{1,0:T(8,128)(2,1)S(1)} %collective-permute-done.17.refs_0_.refs_2_, ...), custom_call_target="tpu_custom_call" | custom-call | tf_op jit(solution)/shard_map/pallas_call | solution.py:562
  131.9 2.0 %shard_map.121 = bf16[128,576]{1,0:T(8,128)(2,1)} custom-call(s32[5]{0:T(128)S(1)} %copy-done.30, f32[128,720]{1,0:T(8,128)S(1)} %shard_map.109.refs_0_, f32[128,720]{1,0:T(8,128)S(1)} %collective-permute-done.12.refs_1_, f32[128,288]{1,0:T(8,128)S(1)} %shard_map.112.refs_0_.refs_2_, f32[128,288]{1,0:T(8,128)S(1)} %collective-permute-done.19.refs_1_.refs_3_, ...), custom_call_target="tpu_custom_call" | custom-call | tf_op jit(solution)/shard_map/pallas_call | solution.py:562
  133.9 4.4 %all-to-all-start.1 = ((bf16[8,16,576]{2,1,0:T(8,128)(2,1)}), bf16[8,16,576]{2,1,0:T(8,128)(2,1)S(1)}, u32[]{:S(2)}, u32[]{:S(2)}) async-start(bf16[8,16,576]{2,1,0:T(8,128)(2,1)} %bitcast.4), calls=%async_computation.1 | async-start | bytes 327680 | tf_op jit(solution)/shard_map/all_to_all | solution.py:598
  138.3 2.6 %shard_map.118 = (bf16[256,576]{1,0:T(8,128)(2,1)}, s32[5]{0:T(128)S(1)}) custom-call(s32[5]{0:T(128)S(1)} %copy-done.30, f32[64,2304]{1,0:T(8,128)S(1)} %get-tuple-element.102.own_ref, bf16[64,2304]{1,0:T(8,128)(2,1)} %collective-permute-done.21.mate_ref), custom_call_target="tpu_custom_call" | custom-call | tf_op jit(solution)/shard_map/pallas_call | solution.py:366
  140.9 3.2 %collective-permute-start.24 = (bf16[256,576]{1,0:T(8,128)(2,1)}, bf16[256,576]{1,0:T(8,128)(2,1)}, u32[]{:S(2)}, u32[]{:S(2)}) collective-permute-start(bf16[256,576]{1,0:T(8,128)(2,1)} %get-tuple-element.115), channel_id=1, source_target_pairs={{2,0},{4,2},{6,4},{8,6},{10,8},{12,10},{14,12},{16,14},{18,16},{20... | collective-permute-start | bytes 884744 | tf_op jit(solution)/shard_map/ppermute | solution.py:407
  144.2 1.1 copy-done.21
  145.2 1.9 %shard_map.120 = (f32[256,576]{1,0:T(8,128)S(1)}, s32[5]{0:T(128)S(1)}) custom-call(s32[5]{0:T(128)S(1)} %get-tuple-element.105.facts_ref, f32[64,2304]{1,0:T(8,128)S(1)} %copy-done.21, bf16[64,2304]{1,0:T(8,128)(2,1)} %collective-permute-done.22.mate_ref), custom_call_target="tpu_custom_call" | custom-call | tf_op jit(solution)/shard_map/pallas_call | solution.py:366
  147.2 1.1 copy-done.17
  148.2 1.1 copy-done.19
  149.3 5.1 %shard_map.122 = (f32[64,4096]{1,0:T(8,128)S(1)}, bf16[64,4096]{1,0:T(8,128)(2,1)S(1)}) custom-call(s32[5]{0:T(128)S(1)} %get-tuple-element.111.facts_ref, bf16[128,576]{1,0:T(8,128)(2,1)S(1)} %bitcast.14, bf16[72,4096]{1,0:T(8,128)(2,1)S(1)} %copy-done.7, bf16[72,4096]{1,0:T(8,128)(2,1)S(1)} %copy-done.13, bf16[72,4096]{1,0:T(8,128)(2,1)S(1)} %copy-done.10, ...), custom_call_target="tpu_custom_call" | custom-call | flops 12079595520 | bytes 4718592 | tf_op jit(solution)/shard_map/pallas_call | solution.py:562
  154.6 1.9 %shard_map.123 = f32[2,288]{1,0:T(2,128)S(1)} custom-call(f32[256,576]{1,0:T(8,128)S(1)} %get-tuple-element.114.even_ref, bf16[256,576]{1,0:T(8,128)(2,1)} %collective-permute-done.24.odd_ref, f32[512,576]{1,0:T(8,128)S(1)} %copy-done.4, f32[2,576]{1,0:T(2,128)S(1)} %copy-done.32, bf16[288,576]{1,0:T(8,128)(2,1)S(1)} %copy-done.2), custom_call_target="tpu_custom_call" | custom-call | tf_op jit(solution)/shard_map/pallas_call | solution.py:381
  156.5 1.3 collective-permute-start.25
  157.8 1.2 collective-permute-done.25
  159.0 3.6 %shard_map.124 = bf16[2,196,576]{2,1,0:T(8,128)(2,1)S(1)} custom-call(f32[256,576]{1,0:T(8,128)S(1)} %get-tuple-element.114.even_ref, bf16[256,576]{1,0:T(8,128)(2,1)} %collective-permute-done.24.odd_ref, f32[512,576]{1,0:T(8,128)S(1)} %copy-done.34, f32[2,576]{1,0:T(2,128)S(1)} %copy-done.32, f32[2,288]{1,0:T(2,128)S(1)} %add.9.sq_ref, ...), custom_call_target="tpu_custom_call" | custom-call | flops 2717908992 | bytes 4718592 | tf_op jit(solution)/shard_map/pallas_call | solution.py:391
  162.6 1.2 copy.12
  (101 shorter events, 8.5 us)
Async XLA Ops:
  0.6 3.3 %copy-start.5 = (bf16[72,4096]{1,0:T(8,128)(2,1)S(1)}, bf16[72,4096]{1,0:T(8,128)(2,1)}, u32[]{:S(2)}) copy-start(bf16[72,4096]{1,0:T(8,128)(2,1)} %refs_0_.1) | copy-start | bytes 1769476
  0.6 5.9 %copy-start = (bf16[9,576,48]{1,2,0:T(8,128)(2,1)S(1)}, bf16[9,576,48]{1,2,0:T(8,128)(2,1)}, u32[]{:S(2)}) copy-start(bf16[9,576,48]{1,2,0:T(8,128)(2,1)} %param.10) | copy-start | bytes 1492996
  2.4 12.3 %copy-start.2 = (bf16[288,576]{1,0:T(8,128)(2,1)S(1)}, bf16[288,576]{1,0:T(8,128)(2,1)}, u32[]{:S(2)}) copy-start(bf16[288,576]{1,0:T(8,128)(2,1)} %expand_ref.3) | copy-start | bytes 995332
  2.4 33.0 %collective-permute-start.2 = (bf16[72,4608]{1,0:T(8,128)(2,1)S(1)}, bf16[72,4608]{1,0:T(8,128)(2,1)S(1)}, u32[]{:S(2)}, u32[]{:S(2)}) collective-permute-start(bf16[72,4608]{1,0:T(8,128)(2,1)S(1)} %reshape.11.refs_0_.refs_2_), channel_id=1, source_target_pairs={{0,4},{2,6},{8,0},{10,2},{16,8},{18,10},{24,16},{26,18},{28,24},{3... | collective-permute-start | bytes 1990664 | tf_op jit(solution)/shard_map/ppermute | solution.py:446
  3.8 31.6 %collective-permute-start = (bf16[72,4608]{1,0:T(8,128)(2,1)S(1)}, bf16[72,4608]{1,0:T(8,128)(2,1)S(1)}, u32[]{:S(2)}, u32[]{:S(2)}) collective-permute-start(bf16[72,4608]{1,0:T(8,128)(2,1)S(1)} %reshape.11.refs_0_.refs_2_), channel_id=1, source_target_pairs={{0,8},{2,10},{8,16},{10,18},{16,24},{18,26},{24,28},{26,30},{28,20... | collective-permute-start | bytes 1990664 | tf_op jit(solution)/shard_map/ppermute | solution.py:446
  3.9 31.4 %collective-permute-start.3 = (bf16[72,4096]{1,0:T(8,128)(2,1)S(1)}, bf16[72,4096]{1,0:T(8,128)(2,1)S(1)}, u32[]{:S(2)}, u32[]{:S(2)}) collective-permute-start(bf16[72,4096]{1,0:T(8,128)(2,1)S(1)} %copy-done.5), channel_id=1, source_target_pairs={{0,4},{2,6},{8,0},{10,2},{16,8},{18,10},{24,16},{26,18},{28,24},{3... | collective-permute-start | bytes 1769480 | tf_op jit(solution)/shard_map/ppermute | solution.py:446
  5.2 30.1 %collective-permute-start.1 = (bf16[72,4096]{1,0:T(8,128)(2,1)S(1)}, bf16[72,4096]{1,0:T(8,128)(2,1)S(1)}, u32[]{:S(2)}, u32[]{:S(2)}) collective-permute-start(bf16[72,4096]{1,0:T(8,128)(2,1)S(1)} %copy-done.5), channel_id=1, source_target_pairs={{0,8},{2,10},{8,16},{10,18},{16,24},{18,26},{24,28},{26,30},{28,20... | collective-permute-start | bytes 1769480 | tf_op jit(solution)/shard_map/ppermute | solution.py:446
  6.5 1.0 copy-start.22
  12.0 2.8 %collective-permute-start.4 = (f32[2,288]{1,0:T(2,128)S(1)}, f32[2,288]{1,0:T(2,128)S(1)}, u32[]{:S(2)}, u32[]{:S(2)}) collective-permute-start(f32[2,288]{1,0:T(2,128)S(1)} %get-tuple-element.65), channel_id=1, source_target_pairs={{0,1},{1,0},{2,3},{3,2},{4,5},{5,4},{6,7},{7,6},{8,9},{9,8},{10,11... | collective-permute-start | bytes 6920 | tf_op jit(solution)/shard_map/ppermute | solution.py:432
  15.9 1.1 copy-start.3
  18.3 1.1 copy-start.33
  19.4 15.3 %collective-permute-start.5 = (bf16[256,576]{1,0:T(8,128)(2,1)S(1)}, bf16[256,576]{1,0:T(8,128)(2,1)S(1)}, u32[]{:S(2)}, u32[]{:S(2)}) collective-permute-start(bf16[256,576]{1,0:T(8,128)(2,1)S(1)} %get-tuple-element.66), channel_id=1, source_target_pairs={{0,2},{2,4},{4,6},{6,8},{8,10},{10,12},{12,14},{14,16},{16,18},{18... | collective-permute-start | bytes 884744 | tf_op jit(solution)/shard_map/ppermute | solution.py:407
  35.4 0.8 copy-start.8
  35.4 1.0 copy-start.11
  36.2 15.2 %collective-permute-start.6 = (bf16[72,4608]{1,0:T(8,128)(2,1)S(1)}, bf16[72,4608]{1,0:T(8,128)(2,1)S(1)}, u32[]{:S(2)}, u32[]{:S(2)}) collective-permute-start(bf16[72,4608]{1,0:T(8,128)(2,1)S(1)} %collective-permute-done.refs_1_.refs_3_), channel_id=1, source_target_pairs={{0,8},{2,10},{8,16},{10,18},{16,24},{18,26},{24,28},{26,30},{28,20... | collective-permute-start | bytes 1990664 | tf_op jit(solution)/shard_map/ppermute | solution.py:446
  36.4 15.1 %collective-permute-start.7 = (bf16[72,4608]{1,0:T(8,128)(2,1)S(1)}, bf16[72,4608]{1,0:T(8,128)(2,1)}, u32[]{:S(2)}, u32[]{:S(2)}) collective-permute-start(bf16[72,4608]{1,0:T(8,128)(2,1)S(1)} %collective-permute-done.2.refs_2_.refs_4_), channel_id=1, source_target_pairs={{0,4},{2,6},{8,0},{10,2},{16,8},{18,10},{24,16},{26,18},{28,24},{3... | collective-permute-start | bytes 1990664 | tf_op jit(solution)/shard_map/ppermute | solution.py:446
  37.7 27.4 %all-to-all-start = ((bf16[8,8,4096]{2,1,0:T(8,128)(2,1)}), bf16[8,8,4096]{2,1,0:T(8,128)(2,1)S(1)}, u32[]{:S(2)}, u32[]{:S(2)}) async-start(bf16[8,8,4096]{2,1,0:T(8,128)(2,1)} %bitcast.15), calls=%async_computation | async-start | bytes 1048576 | tf_op jit(solution)/shard_map/all_to_all | solution.py:598
  42.7 29.8 %collective-permute-start.10 = (bf16[72,4096]{1,0:T(8,128)(2,1)}, bf16[72,4096]{1,0:T(8,128)(2,1)}, u32[]{:S(2)}, u32[]{:S(2)}) collective-permute-start(bf16[72,4096]{1,0:T(8,128)(2,1)} %copy-done.11), channel_id=1, source_target_pairs={{0,8},{2,10},{8,16},{10,18},{16,24},{18,26},{24,28},{26,30},{28,20... | collective-permute-start | bytes 1769480 | tf_op jit(solution)/shard_map/ppermute | solution.py:446
  44.0 34.4 %collective-permute-start.11 = (bf16[72,4096]{1,0:T(8,128)(2,1)}, bf16[72,4096]{1,0:T(8,128)(2,1)}, u32[]{:S(2)}, u32[]{:S(2)}) collective-permute-start(bf16[72,4096]{1,0:T(8,128)(2,1)} %copy-done.8), channel_id=1, source_target_pairs={{0,4},{2,6},{8,0},{10,2},{16,8},{18,10},{24,16},{26,18},{28,24},{3... | collective-permute-start | bytes 1769480 | tf_op jit(solution)/shard_map/ppermute | solution.py:446
  51.5 1.0 copy-start.25
  52.5 1.0 copy-start.27
  56.0 22.4 %collective-permute-start.8 = (bf16[64,4608]{1,0:T(8,128)(2,1)}, bf16[64,4608]{1,0:T(8,128)(2,1)}, u32[]{:S(2)}, u32[]{:S(2)}) collective-permute-start(bf16[64,4608]{1,0:T(8,128)(2,1)} %shard_map.107.own_ref), channel_id=1, source_target_pairs={{0,2},{2,0},{4,6},{6,4},{8,10},{10,8},{12,14},{14,12},{16,18},{18,... | collective-permute-start | bytes 1769480 | tf_op jit(solution)/shard_map/ppermute | solution.py:424
  65.1 17.1 %copy-start.6 = (bf16[72,4096]{1,0:T(8,128)(2,1)S(1)}, bf16[72,4096]{1,0:T(8,128)(2,1)}, u32[]{:S(2)}) copy-start(bf16[72,4096]{1,0:T(8,128)(2,1)} %refs_0_.1) | copy-start | bytes 1769476
  65.1 17.1 %copy-start.9 = (bf16[72,4096]{1,0:T(8,128)(2,1)S(1)}, bf16[72,4096]{1,0:T(8,128)(2,1)}, u32[]{:S(2)}) copy-start(bf16[72,4096]{1,0:T(8,128)(2,1)} %copy-done.8) | copy-start | bytes 1769476
  65.1 17.1 %copy-start.12 = (bf16[72,4096]{1,0:T(8,128)(2,1)S(1)}, bf16[72,4096]{1,0:T(8,128)(2,1)}, u32[]{:S(2)}) copy-start(bf16[72,4096]{1,0:T(8,128)(2,1)} %copy-done.11) | copy-start | bytes 1769476
  65.2 17.1 %collective-permute-start.9 = (bf16[64,4096]{1,0:T(8,128)(2,1)S(1)}, bf16[64,4096]{1,0:T(8,128)(2,1)S(1)}, u32[]{:S(2)}, u32[]{:S(2)}) collective-permute-start(bf16[64,4096]{1,0:T(8,128)(2,1)S(1)} %bitcast.6), channel_id=1, source_target_pairs={{0,2},{2,0},{4,6},{6,4},{8,10},{10,8},{12,14},{14,12},{16,18},{18,... | collective-permute-start | bytes 1572872 | tf_op jit(solution)/shard_map/ppermute | solution.py:424
  68.7 35.7 %collective-permute-start.13 = (bf16[72,4608]{1,0:T(8,128)(2,1)S(1)}, bf16[72,4608]{1,0:T(8,128)(2,1)S(1)}, u32[]{:S(2)}, u32[]{:S(2)}) collective-permute-start(bf16[72,4608]{1,0:T(8,128)(2,1)S(1)} %collective-permute-done.6.refs_3_.refs_5_), channel_id=1, source_target_pairs={{0,8},{2,10},{8,16},{10,18},{16,24},{18,26},{24,28},{26,30},{28,20... | collective-permute-start | bytes 1990664 | tf_op jit(solution)/shard_map/ppermute | solution.py:446
  72.5 31.9 %collective-permute-start.15 = (bf16[72,4608]{1,0:T(8,128)(2,1)}, bf16[72,4608]{1,0:T(8,128)(2,1)S(1)}, u32[]{:S(2)}, u32[]{:S(2)}) collective-permute-start(bf16[72,4608]{1,0:T(8,128)(2,1)} %collective-permute-done.7.refs_4_.refs_6_), channel_id=1, source_target_pairs={{0,4},{2,6},{8,0},{10,2},{16,8},{18,10},{24,16},{26,18},{28,24},{3... | collective-permute-start | bytes 1990664 | tf_op jit(solution)/shard_map/ppermute | solution.py:446
  78.4 24.2 %collective-permute-start.14 = (bf16[72,4096]{1,0:T(8,128)(2,1)}, bf16[72,4096]{1,0:T(8,128)(2,1)S(1)}, u32[]{:S(2)}, u32[]{:S(2)}) collective-permute-start(bf16[72,4096]{1,0:T(8,128)(2,1)} %collective-permute-done.10.refs_8_.refs_3_), channel_id=1, source_target_pairs={{0,8},{2,10},{8,16},{10,18},{16,24},{18,26},{24,28},{26,30},{28,20... | collective-permute-start | bytes 1769480 | tf_op jit(solution)/shard_map/ppermute | solution.py:446
  78.4 26.0 %collective-permute-start.16 = (bf16[72,4096]{1,0:T(8,128)(2,1)}, bf16[72,4096]{1,0:T(8,128)(2,1)S(1)}, u32[]{:S(2)}, u32[]{:S(2)}) collective-permute-start(bf16[72,4096]{1,0:T(8,128)(2,1)} %collective-permute-done.11.refs_9_.refs_4_), channel_id=1, source_target_pairs={{0,4},{2,6},{8,0},{10,2},{16,8},{18,10},{24,16},{26,18},{28,24},{3... | collective-permute-start | bytes 1769480 | tf_op jit(solution)/shard_map/ppermute | solution.py:446
  82.2 15.5 %copy-start.30 = (s32[5]{0:T(128)S(1)}, s32[5]{0:T(128)}, u32[]{:S(2)}) copy-start(s32[5]{0:T(128)} %shard_map.104.facts_ref) | copy-start | bytes 64
  86.8 10.9 %collective-permute-start.12 = (f32[128,720]{1,0:T(8,128)S(1)}, f32[128,720]{1,0:T(8,128)S(1)}, u32[]{:S(2)}, u32[]{:S(2)}) collective-permute-start(f32[128,720]{1,0:T(8,128)S(1)} %shard_map.109.refs_0_), channel_id=1, source_target_pairs={{0,1},{1,0},{2,3},{3,2},{4,5},{5,4},{6,7},{7,6},{8,9},{9,8},{10,11... | collective-permute-start | bytes 1105928 | tf_op jit(solution)/shard_map/ppermute | solution.py:432
  102.5 5.4 %copy-start.14 = (bf16[72,4096]{1,0:T(8,128)(2,1)}, bf16[72,4096]{1,0:T(8,128)(2,1)S(1)}, u32[]{:S(2)}) copy-start(bf16[72,4096]{1,0:T(8,128)(2,1)S(1)} %collective-permute-done.14.refs_2_.refs_5_) | copy-start | bytes 1769476
  104.4 3.5 %copy-start.16 = (bf16[72,4096]{1,0:T(8,128)(2,1)}, bf16[72,4096]{1,0:T(8,128)(2,1)S(1)}, u32[]{:S(2)}) copy-start(bf16[72,4096]{1,0:T(8,128)(2,1)S(1)} %collective-permute-done.16.refs_3_.refs_6_) | copy-start | bytes 1769476
  104.4 4.8 %copy-start.1 = (bf16[9,576,48]{1,2,0:T(8,128)(2,1)S(1)}, bf16[9,576,48]{1,2,0:T(8,128)(2,1)}, u32[]{:S(2)}) copy-start(bf16[9,576,48]{1,2,0:T(8,128)(2,1)} %param.10) | copy-start | bytes 1492996
  104.4 17.0 %collective-permute-start.17 = (bf16[72,4608]{1,0:T(8,128)(2,1)S(1)}, bf16[72,4608]{1,0:T(8,128)(2,1)S(1)}, u32[]{:S(2)}, u32[]{:S(2)}) collective-permute-start(bf16[72,4608]{1,0:T(8,128)(2,1)S(1)} %collective-permute-done.13.refs_0_.refs_2_), channel_id=1, source_target_pairs={{0,8},{2,10},{8,16},{10,18},{16,24},{18,26},{24,28},{26,30},{28,20... | collective-permute-start | bytes 1990664 | tf_op jit(solution)/shard_map/ppermute | solution.py:446
  104.5 14.5 %collective-permute-start.18 = (bf16[72,4096]{1,0:T(8,128)(2,1)S(1)}, bf16[72,4096]{1,0:T(8,128)(2,1)S(1)}, u32[]{:S(2)}, u32[]{:S(2)}) collective-permute-start(bf16[72,4096]{1,0:T(8,128)(2,1)S(1)} %collective-permute-done.16.refs_3_.refs_6_), channel_id=1, source_target_pairs={{0,4},{2,6},{8,0},{10,2},{16,8},{18,10},{24,16},{26,18},{28,24},{3... | collective-permute-start | bytes 1769480 | tf_op jit(solution)/shard_map/ppermute | solution.py:446
  107.9 6.0 %collective-permute-start.19 = (f32[128,288]{1,0:T(8,128)S(1)}, f32[128,288]{1,0:T(8,128)S(1)}, u32[]{:S(2)}, u32[]{:S(2)}) collective-permute-start(f32[128,288]{1,0:T(8,128)S(1)} %shard_map.112.refs_0_.refs_2_), channel_id=1, source_target_pairs={{0,1},{1,0},{2,3},{3,2},{4,5},{5,4},{6,7},{7,6},{8,9},{9,8},{10,11... | collective-permute-start | bytes 442376 | tf_op jit(solution)/shard_map/ppermute | solution.py:432
  110.2 1.0 copy-start.35
  111.3 1.0 copy-start.37
  112.3 0.9 copy-start.39
  119.0 3.2 %copy-start.18 = (bf16[72,4096]{1,0:T(8,128)(2,1)}, bf16[72,4096]{1,0:T(8,128)(2,1)S(1)}, u32[]{:S(2)}) copy-start(bf16[72,4096]{1,0:T(8,128)(2,1)S(1)} %collective-permute-done.18.refs_1_.refs_7_) | copy-start | bytes 1769476
  122.2 4.4 %collective-permute-start.20 = (f32[128,144]{1,0:T(8,128)S(1)}, f32[128,144]{1,0:T(8,128)S(1)}, u32[]{:S(2)}, u32[]{:S(2)}) collective-permute-start(f32[128,144]{1,0:T(8,128)S(1)} %shard_map.116.refs_0_.refs_4_), channel_id=1, source_target_pairs={{0,1},{1,0},{2,3},{3,2},{4,5},{5,4},{6,7},{7,6},{8,9},{9,8},{10,11... | collective-permute-start | bytes 221192 | tf_op jit(solution)/shard_map/ppermute | solution.py:432
  128.4 9.9 %collective-permute-start.21 = (bf16[64,2304]{1,0:T(8,128)(2,1)}, bf16[64,2304]{1,0:T(8,128)(2,1)}, u32[]{:S(2)}, u32[]{:S(2)}) collective-permute-start(bf16[64,2304]{1,0:T(8,128)(2,1)} %get-tuple-element.104), channel_id=1, source_target_pairs={{0,2},{2,0},{4,6},{6,4},{8,10},{10,8},{12,14},{14,12},{16,18},{18,... | collective-permute-start | bytes 884744 | tf_op jit(solution)/shard_map/ppermute | solution.py:424
  131.9 2.1 %copy-start.20 = (f32[64,2304]{1,0:T(8,128)}, f32[64,2304]{1,0:T(8,128)S(1)}, u32[]{:S(2)}) copy-start(f32[64,2304]{1,0:T(8,128)S(1)} %get-tuple-element.109.own_ref) | copy-start | bytes 1769476
  131.9 12.3 %collective-permute-start.22 = (bf16[64,2304]{1,0:T(8,128)(2,1)}, bf16[64,2304]{1,0:T(8,128)(2,1)}, u32[]{:S(2)}, u32[]{:S(2)}) collective-permute-start(bf16[64,2304]{1,0:T(8,128)(2,1)} %get-tuple-element.110), channel_id=1, source_target_pairs={{0,2},{2,0},{4,6},{6,4},{8,10},{10,8},{12,14},{14,12},{16,18},{18,... | collective-permute-start | bytes 884744 | tf_op jit(solution)/shard_map/ppermute | solution.py:424
  131.9 15.2 %copy-start.15 = (bf16[72,4096]{1,0:T(8,128)(2,1)S(1)}, bf16[72,4096]{1,0:T(8,128)(2,1)}, u32[]{:S(2)}) copy-start(bf16[72,4096]{1,0:T(8,128)(2,1)} %copy-done.14) | copy-start | bytes 1769476
  133.9 13.2 %copy-start.7 = (bf16[72,4096]{1,0:T(8,128)(2,1)S(1)}, bf16[72,4096]{1,0:T(8,128)(2,1)}, u32[]{:S(2)}) copy-start(bf16[72,4096]{1,0:T(8,128)(2,1)} %refs_0_.1) | copy-start | bytes 1769476
  133.9 13.2 %copy-start.10 = (bf16[72,4096]{1,0:T(8,128)(2,1)S(1)}, bf16[72,4096]{1,0:T(8,128)(2,1)}, u32[]{:S(2)}) copy-start(bf16[72,4096]{1,0:T(8,128)(2,1)} %copy-done.8) | copy-start | bytes 1769476
  133.9 13.2 %copy-start.13 = (bf16[72,4096]{1,0:T(8,128)(2,1)S(1)}, bf16[72,4096]{1,0:T(8,128)(2,1)}, u32[]{:S(2)}) copy-start(bf16[72,4096]{1,0:T(8,128)(2,1)} %copy-done.11) | copy-start | bytes 1769476
  133.9 13.2 %all-to-all-start.1 = ((bf16[8,16,576]{2,1,0:T(8,128)(2,1)}), bf16[8,16,576]{2,1,0:T(8,128)(2,1)S(1)}, u32[]{:S(2)}, u32[]{:S(2)}) async-start(bf16[8,16,576]{2,1,0:T(8,128)(2,1)} %bitcast.4), calls=%async_computation.1 | async-start | bytes 327680 | tf_op jit(solution)/shard_map/all_to_all | solution.py:598
  140.9 13.6 %collective-permute-start.24 = (bf16[256,576]{1,0:T(8,128)(2,1)}, bf16[256,576]{1,0:T(8,128)(2,1)}, u32[]{:S(2)}, u32[]{:S(2)}) collective-permute-start(bf16[256,576]{1,0:T(8,128)(2,1)} %get-tuple-element.115), channel_id=1, source_target_pairs={{2,0},{4,2},{6,4},{8,6},{10,8},{12,10},{14,12},{16,14},{18,16},{20... | collective-permute-start | bytes 884744 | tf_op jit(solution)/shard_map/ppermute | solution.py:407
  144.2 1.1 copy-start.21
  147.2 1.1 copy-start.17
  148.2 1.1 copy-start.19
  149.3 5.2 %copy-start.4 = (f32[512,576]{1,0:T(8,128)S(1)}, f32[512,576]{1,0:T(8,128)}, u32[]{:S(2)}) copy-start(f32[512,576]{1,0:T(8,128)} %copy-done.3) | copy-start | bytes 3538948
  149.3 5.2 %copy-start.32 = (f32[2,576]{1,0:T(2,128)S(1)}, f32[2,576]{1,0:T(2,128)}, u32[]{:S(2)}) copy-start(f32[2,576]{1,0:T(2,128)} %copy-done.31) | copy-start | bytes 13828
  149.3 9.7 %copy-start.36 = (bf16[9,256,256]{2,1,0:T(8,128)(2,1)S(1)}, bf16[9,256,256]{2,1,0:T(8,128)(2,1)}, u32[]{:S(2)}) copy-start(bf16[9,256,256]{2,1,0:T(8,128)(2,1)} %copy-done.35) | copy-start | bytes 3538948
  149.3 9.7 %copy-start.38 = (bf16[9,256,256]{2,1,0:T(8,128)(2,1)S(1)}, bf16[9,256,256]{2,1,0:T(8,128)(2,1)}, u32[]{:S(2)}) copy-start(bf16[9,256,256]{2,1,0:T(8,128)(2,1)} %copy-done.37) | copy-start | bytes 3538948
  154.4 9.4 %collective-permute-start.23 = (bf16[64,4096]{1,0:T(8,128)(2,1)S(1)}, bf16[64,4096]{1,0:T(8,128)(2,1)S(1)}, u32[]{:S(2)}, u32[]{:S(2)}) collective-permute-start(bf16[64,4096]{1,0:T(8,128)(2,1)S(1)} %get-tuple-element.113), channel_id=1, source_target_pairs={{0,2},{2,0},{4,6},{6,4},{8,10},{10,8},{12,14},{14,12},{16,18},{18,... | collective-permute-start | bytes 1572872 | tf_op jit(solution)/shard_map/ppermute | solution.py:424
  154.5 4.4 %copy-start.23 = (bf16[576,288]{0,1:T(8,128)(2,1)S(1)}, bf16[576,288]{0,1:T(8,128)(2,1)}, u32[]{:S(2)}) copy-start(bf16[576,288]{0,1:T(8,128)(2,1)} %param.11) | copy-start | bytes 995332
  154.5 4.4 %copy-start.34 = (f32[512,576]{1,0:T(8,128)S(1)}, f32[512,576]{1,0:T(8,128)}, u32[]{:S(2)}) copy-start(f32[512,576]{1,0:T(8,128)} %copy-done.33) | copy-start | bytes 3538948
  154.5 4.4 %copy-start.40 = (bf16[9,192,192]{2,1,0:T(8,128)(2,1)S(1)}, bf16[9,192,192]{2,1,0:T(8,128)(2,1)}, u32[]{:S(2)}) copy-start(bf16[9,192,192]{2,1,0:T(8,128)(2,1)} %copy-done.39) | copy-start | bytes 1990660
  156.5 2.5 %collective-permute-start.25 = (f32[2,288]{1,0:T(2,128)S(1)}, f32[2,288]{1,0:T(2,128)S(1)}, u32[]{:S(2)}, u32[]{:S(2)}) collective-permute-start(f32[2,288]{1,0:T(2,128)S(1)} %shard_map.123), channel_id=1, source_target_pairs={{0,1},{1,0},{2,3},{3,2},{4,5},{5,4},{6,7},{7,6},{8,9},{9,8},{10,11... | collective-permute-start | bytes 6920 | tf_op jit(solution)/shard_map/ppermute | solution.py:432
  (5 other events, 3.4 us)

commit v6 on v5

--- a/solution.py
+++ b/solution.py
@@ -439,26 +439,24 @@
     return value + other
 
 
-def ring_step(blocks):
-    count = lax.axis_size("ctx")
-    onward, backward = ring_pairs(count, 1), ring_pairs(count, -1)
-    up_s, up_r, down_s, down_r = blocks
-    send = lambda value, pairs: None if value is None else lax.ppermute(value, "ctx", pairs)
-    up_r, down_r = send(up_r, onward), send(down_r, backward)
-    up_s, down_s = send(up_s, onward), send(down_s, backward)
-    return up_s, up_r, down_s, down_r
+def ring_send(value, by):
+    return lax.ppermute(value, "ctx", ring_pairs(lax.axis_size("ctx"), by))
 
 
 def tie(*values):
     return lax.optimization_barrier(values)
 
 
-def sums_kernel(count, patch_ref, keep_ref, send_ref, *refs):
+def pre_kernel(patch_ref, *refs):
     *blocks, out_ref = refs
-    products = [contract_last(patch_ref[...], ref[...]) for ref in blocks[:count]]
+    products = [contract_last(patch_ref[...], ref[...]) for ref in blocks]
+    out_ref[...] = jnp.concatenate(products, axis=1)
+
+
+def back_kernel(keep_ref, send_ref, *refs):
+    *blocks, out_ref = refs
     back = jnp.concatenate([keep_ref[...], send_ref[...]], axis=0)
-    products += [contract_last(back, ref[...]) for ref in blocks[count:]]
-    out_ref[...] = jnp.concatenate(products, axis=1)
+    out_ref[...] = jnp.concatenate([contract_last(back, ref[...]) for ref in blocks], axis=1)
 
 
 def live_rows(facts_ref, rows, unit):
@@ -468,20 +466,20 @@
     return (token < jnp.where(block == 0, facts_ref[1], facts_ref[2])).astype(jnp.float32)
 
 
-def totals_kernel(count, unit, lanes, first, facts_ref, *refs):
-    sums = refs[0][...] + refs[1][...]
-    blocks, refs = refs[2 : 2 + count], refs[2 + count :]
-    before, after = refs[:-2], refs[-2:]
-    rows, depth = sums.shape[0], sums.shape[1] // 2
-    factor = sums[:, depth:] * silu_slope(sums[:, :depth]) * live_rows(facts_ref, rows, unit)
+def totals_kernel(pieces, unit, lanes, first, facts_ref, *refs):
+    grad_act = refs[0][...] + refs[1][...]
+    count = len(pieces)
+    slopes, blocks = refs[2:4], refs[4 : 4 + count]
+    before, after = refs[4 + count : -2], refs[-2:]
+    rows, width = grad_act.shape[0], blocks[0].shape[0]
     matrix = reorder_matrix(facts_ref[0], unit, False)
-    factor = jnp.dot(
-        matrix, factor.astype(jnp.bfloat16), preferred_element_type=jnp.float32
-    ).astype(jnp.bfloat16)
-    width = depth // count
     total = 0.0
-    for place, ref in enumerate(blocks):
-        piece = factor[:, place * width : (place + 1) * width]
+    for place, ((source, index), ref) in enumerate(zip(pieces, blocks)):
+        piece = grad_act[:, place * width : (place + 1) * width]
+        piece = piece * slopes[source][:, index * width : (index + 1) * width]
+        piece = jnp.dot(
+            matrix, piece.astype(jnp.bfloat16), preferred_element_type=jnp.float32
+        ).astype(jnp.bfloat16)
         total += jnp.dot(piece, ref[:, lanes], preferred_element_type=jnp.float32)
     for half, ref in enumerate(after):
         value = total[half * rows // 2 : (half + 1) * rows // 2]
@@ -514,48 +512,47 @@
     return (within + jnp.where(target_core == core, 0, per_block) == kept).astype(jnp.bfloat16)
 
 
-def act_kernel(counts, unit, facts_ref, *refs):
-    *terms, out_ref = refs
-    rows = terms[0].shape[0]
-    live = live_rows(facts_ref, rows, unit)
-    chips = sum(counts)
-    offsets = iter(ring_offsets(chips))
-    total = 0.0
-    for group, count in enumerate(counts):
-        depth = terms[2 * group].shape[1] // 2
-        pre = terms[2 * group][:, :depth] + terms[2 * group + 1][:, :depth]
-        act = (pre * jax.nn.sigmoid(pre) * live).astype(jnp.bfloat16)
-        width = depth // count
-        for place in range(count):
-            columns = block_columns(facts_ref, next(offsets), chips, width)
-            piece = act[:, place * width : (place + 1) * width]
-            total += jnp.dot(piece, columns, preferred_element_type=jnp.float32)
-    matrix = exchange_matrix(facts_ref[0], unit, True)
-    out_ref[...] = jnp.dot(
-        matrix, total.astype(jnp.bfloat16), preferred_element_type=jnp.float32
-    ).astype(jnp.bfloat16)
-
-
-def token_kernel(unit, facts_ref, act_ref, *refs):
-    *blocks, keep_ref, send_ref = refs
-    chips, width = len(blocks), blocks[0].shape[0]
+def act_kernel(offsets, chips, unit, last, facts_ref, own_ref, other_ref, *refs):
+    *before, slope_ref, out_ref = refs
+    pre = own_ref[...] + other_ref[...]
+    width = pre.shape[1] // len(offsets)
+    live = live_rows(facts_ref, pre.shape[0], unit)
+    sigma = jax.nn.sigmoid(pre)
+    slope_ref[...] = sigma * (1.0 + pre * (1.0 - sigma)) * live
+    act = (pre * sigma * live).astype(jnp.bfloat16)
+    total = before[0][...].astype(jnp.float32) if last else 0.0
+    for place, offset in enumerate(offsets):
+        columns = block_columns(facts_ref, offset, chips, width)
+        piece = act[:, place * width : (place + 1) * width]
+        total += jnp.dot(piece, columns, preferred_element_type=jnp.float32)
+    total = total.astype(jnp.bfloat16)
+    if last:
+        matrix = exchange_matrix(facts_ref[0], unit, True)
+        total = jnp.dot(matrix, total, preferred_element_type=jnp.float32).astype(jnp.bfloat16)
+    out_ref[...] = total
+
+
+def token_kernel(offsets, chips, unit, first, facts_ref, act_ref, *refs):
+    count = len(offsets)
+    blocks, before, after = refs[:count], refs[count:-2], refs[-2:]
+    width = blocks[0].shape[0]
     matrix = exchange_matrix(facts_ref[0], unit, False)
     act = jnp.dot(matrix, act_ref[...], preferred_element_type=jnp.float32).astype(jnp.bfloat16)
     total = 0.0
-    for offset, ref in zip(ring_offsets(chips), blocks):
+    for offset, ref in zip(offsets, blocks):
         columns = block_columns(facts_ref, offset, chips, width)
         piece = contract_last(act, columns).astype(jnp.bfloat16)
         total += jnp.dot(piece, ref[...], preferred_element_type=jnp.float32)
-    rows = keep_ref.shape[0]
-    keep_ref[...] = total[:rows]
-    send_ref[...] = total[rows:].astype(jnp.bfloat16)
-
-
-def partial_sums(patches, back, samplers, readouts):
-    count, width = len(samplers), samplers[0].shape[0]
-    return whole_call(
-        functools.partial(sums_kernel, count), f32(patches.shape[0], 2 * count * width), []
-    )(patches, *back, *samplers, *readouts)
+    rows = after[0].shape[0]
+    for half, ref in enumerate(after):
+        value = total[half * rows : (half + 1) * rows]
+        value = value if first else before[half][...] + value
+        ref[...] = value.astype(ref.dtype)
+
+
+def block_products(kernel, left, blocks):
+    rows = 2 * OUT_SIDE * OUT_SIDE
+    return whole_call(kernel, f32(rows, len(blocks) * blocks[0].shape[0]), [])(*left, *blocks)
 
 
 def facts_call(kernel, outs, facts, operands, cost=FREE):
@@ -568,28 +565,30 @@
     )(facts, *operands)
 
 
-def add_products(facts, sums, blocks, before, unit, lanes, last):
-    rows, columns = sums[0].shape[0] // 2, lanes.stop - lanes.start
-    kernel = functools.partial(totals_kernel, len(blocks), unit, lanes, not before)
+def add_gradients(facts, terms, slopes, pieces, blocks, before, unit, lanes, last):
+    rows, columns = terms[0].shape[0] // 2, lanes.stop - lanes.start
+    kernel = functools.partial(totals_kernel, pieces, unit, lanes, not before)
     outs = f32(rows, columns), (bf16 if last else f32)(rows, columns)
-    return facts_call(kernel, outs, facts, (*sums, *blocks, *before))
-
-
-def act_to_send(facts, groups, counts, unit):
-    rows, columns = groups[0][0].shape[0], sum(terms[0].shape[1] // 2 for terms in groups)
-    kernel = functools.partial(act_kernel, counts, unit)
-    operands = [term for terms in groups for term in terms]
-    return facts_call(kernel, bf16(rows, columns), facts, operands)
-
-
-def token_products(facts, act, readouts, unit):
-    rows, columns = act.shape[0] // 2, readouts[0].shape[1]
-    kernel = functools.partial(token_kernel, unit)
-    outs = f32(rows, columns), bf16(rows, columns)
+    return facts_call(kernel, outs, facts, (*terms, *slopes, *blocks, *before))
+
+
+def act_and_slope(facts, terms, offsets, chips, before, unit):
+    rows, columns = terms[0].shape
+    kernel = functools.partial(act_kernel, offsets, chips, unit, bool(before))
+    outs = f32(rows, columns), bf16(rows, columns // len(offsets) * chips)
+    return facts_call(kernel, outs, facts, (*terms, *before))
+
+
+def add_tokens(facts, act, offsets, chips, blocks, before, unit):
+    rows, columns = act.shape[0] // 2, blocks[0].shape[1]
+    kernel = functools.partial(token_kernel, offsets, chips, unit, not before)
+    outs = f32(rows, columns), (bf16 if before else f32)(rows, columns)
     cost = pl.CostEstimate(
-        flops=40 * act.size * columns, bytes_accessed=2 * act.shape[1] * columns, transcendentals=0
-    )
-    return facts_call(kernel, outs, facts, (act, *readouts), cost)
+        flops=5 * len(blocks) * act.shape[1] * act.shape[0] * columns // chips * 8,
+        bytes_accessed=0,
+        transcendentals=0,
+    )
+    return facts_call(kernel, outs, facts, (act, *blocks, *before), cost if before else FREE)
 
 
 def chips_exchange(value):
@@ -615,7 +614,8 @@
     count = lax.axis_size("ctx")
     steps, unit = count // 4, OUT_SIDE * OUT_SIDE // count
     flat_sampler = sampler_kernel.reshape(sampler_kernel.shape[0], 8 * chans)
-    blocks = ring_step((flat_sampler, readout_kernel) * 2)
+    chips = count // 2
+    s_up, s_down = [ring_send(flat_sampler, 1)], [ring_send(flat_sampler, -1)]
     group_kernel = jnp.swapaxes(group_kernel, 1, 2)
     squeeze_in = squeeze_in.T
     facts = facts_of(frame_clip, clip_keep)
@@ -627,57 +627,87 @@
     even, odd, excite, active, slope = hidden_frames(conv, padded, squeezed, squeeze_out)
     halo = shifted(odd, "ctx", 1)
 
-    halo_lanes, even_lanes = slice(0, 4 * chans), slice(4 * chans, 8 * chans)
-    samplers, readouts = [flat_sampler], [readout_kernel]
-    halo_grads = even_grads = ()
-    all_readouts, groups, counts = [], [], []
-    for step in range(1, steps + 1):
+    s_up[0], s_down[0], even = tie(s_up[0], s_down[0], even)
+    for step in range(1, steps - 1):
+        s_up.append(ring_send(s_up[-1], 1))
+        s_down.append(ring_send(s_down[-1], -1))
         if step == 1:
-            *blocks, halo, even = tie(*blocks, halo, even)
-        if step == 2:
-            up_s, up_r, down_s, down_r = blocks
-            halo, up_s, down_s = tie(halo, up_s, down_s)
-            blocks = up_s, up_r, down_s, down_r
+            halo, s_up[1], s_down[1] = tie(halo, s_up[1], s_down[1])
             patches = take_patches(facts, halo, even)
             patches = order_rows(facts, patches, swap_cores(patches), unit)
             back = (back, swap_cores(back))
-        here, last = blocks, step == steps
-        if not last:
-            if step == steps - 1:
-                held = *halo_grads, *even_grads
-                *held, up_s, up_r, down_s, down_r, group_kernel = tie(*held, *here, group_kernel)
-                halo_grads, even_grads = held[:2], held[2:]
-                dense = dense_weights(group_kernel)
-                here = up_s, up_r, down_s, down_r
-            samplers, readouts = samplers + [here[0], here[2]], readouts + [here[1], here[3]]
-            if step == steps - 1:
-                here = up_s, None, None, down_r
-            blocks = ring_step(here)
-        else:
-            held = *halo_grads, *even_grads, *dense
-            last_s, last_r, *held = tie(here[0], here[3], *held)
-            halo_grads, even_grads, dense = held[:2], held[2:4], held[4:]
-            samplers, readouts = samplers + [last_s], readouts + [last_r]
-        if step >= steps - 2:
-            sums = tp_terms(partial_sums(patches, back, samplers, readouts))
-            halo_grads = add_products(facts, sums, samplers, halo_grads, unit, halo_lanes, last)
-            if last:
-                halo_own, halo_mate = halo_grads
-                halo_mate, first_sums = tie(halo_mate, sums[0])
-                sums = first_sums, sums[1]
-                halo_mate = swap_cores(halo_mate)
-                lead, facts_late = return_patches(facts, halo_own, halo_mate, chans, jnp.bfloat16)
-                grad_odd = shifted(lead, "ctx", -1)
-            even_grads = add_products(facts, sums, samplers, even_grads, unit, even_lanes, last)
-            groups, counts = groups + [sums], counts + [len(samplers)]
-            all_readouts += readouts
-            samplers, readouts = [], []
-    act = chips_exchange(act_to_send(facts, groups, counts, unit))
+    s_up[-1], s_down[-1], readout_kernel = tie(s_up[-1], s_down[-1], readout_kernel)
+    s_last = ring_send(s_up[-1], 1)
+    r_up, r_down = [ring_send(readout_kernel, 1)], [ring_send(readout_kernel, -1)]
+    samplers = [flat_sampler] + [block for pair in zip(s_up, s_down) for block in pair]
+    offsets = ring_offsets(chips)
+    first_pre = block_products(pre_kernel, (patches,), samplers)
+    r_up[0], r_down[0], first_pre = tie(r_up[0], r_down[0], first_pre)
+    for step in range(1, steps - 2):
+        r_up.append(ring_send(r_up[-1], 1))
+        r_down.append(ring_send(r_down[-1], -1))
+    first_slope, first_act = act_and_slope(
+        facts, tp_terms(first_pre), offsets[:-1], chips, (), unit
+    )
+    last_pre = tp_terms(block_products(pre_kernel, (patches,), [s_last]))
+    last_slope, act = act_and_slope(facts, last_pre, offsets[-1:], chips, (first_act,), unit)
+    slopes = first_slope, last_slope
+
+    early = [readout_kernel]
+    for step in range(steps - 3):
+        early += [r_up[step], r_down[step]]
+    early_sums = block_products(back_kernel, back, early)
+    r_up[-1], early_sums = tie(r_up[-1], early_sums)
+    r_up.append(ring_send(r_up[-1], 1))
+    r_down.append(ring_send(r_down[-1], -1))
+    halo_lanes, even_lanes = slice(0, 4 * chans), slice(4 * chans, 8 * chans)
+    index = len(early)
+    *middle, act = tie(r_up[steps - 3], r_down[steps - 3], r_down[steps - 2], act)
+    act = chips_exchange(act)
+    pieces = [(0, place) for place in range(index)]
+    terms = tp_terms(early_sums)
+    halo_grads = add_gradients(
+        facts, terms, slopes, pieces, samplers[:index], (), unit, halo_lanes, False
+    )
+    even_grads = add_gradients(
+        facts, terms, slopes, pieces, samplers[:index], (), unit, even_lanes, False
+    )
+    r_last = ring_send(r_down[-1], -1)
+    held = tie(group_kernel, *middle, *halo_grads, *even_grads)
+    group_kernel, middle, halo_grads, even_grads = held[0], held[1:4], held[4:6], held[6:]
+    dense = dense_weights(group_kernel)
+    pieces = [(0, index), (0, index + 1), (0, index + 3)]
+    blocks = [samplers[index], samplers[index + 1], samplers[index + 3]]
+    terms = tp_terms(block_products(back_kernel, back, middle))
+    halo_grads = add_gradients(
+        facts, terms, slopes, pieces, blocks, halo_grads, unit, halo_lanes, False
+    )
+    even_grads = add_gradients(
+        facts, terms, slopes, pieces, blocks, even_grads, unit, even_lanes, False
+    )
+    places = offsets[: index + 2] + [offsets[index + 3]]
+    tokens = add_tokens(facts, act, places, chips, early + list(middle), (), unit)
+
+    held = tie(r_up[-1], r_last, *halo_grads, *even_grads, *dense, *tokens)
+    late, halo_grads, even_grads = held[:2], held[2:4], held[4:6]
+    dense, tokens = held[6:-2], held[-2:]
+    pieces, blocks = [(0, index + 2), (1, 0)], [samplers[index + 2], s_last]
+    terms = tp_terms(block_products(back_kernel, back, late))
+    halo_own, halo_mate = add_gradients(
+        facts, terms, slopes, pieces, blocks, halo_grads, unit, halo_lanes, True
+    )
+    halo_mate, first_term = tie(halo_mate, terms[0])
+    even_own, even_mate = add_gradients(
+        facts, (first_term, terms[1]), slopes, pieces, blocks, even_grads, unit, even_lanes, True
+    )
+    lead, facts_late = return_patches(facts, halo_own, swap_cores(halo_mate), chans, jnp.bfloat16)
+    grad_odd = shifted(lead, "ctx", -1)
     grad_even, facts_late = return_patches(
-        facts_late, even_grads[0], swap_cores(even_grads[1]), chans, jnp.float32
+        facts_late, even_own, swap_cores(even_mate), chans, jnp.float32
     )
     grad_relaxed = sum_tp(excite_grad(grad_even, grad_odd, active, excite, squeeze_out))
-    tokens, send = token_products(facts_late, act, all_readouts, unit)
+    places = [offsets[index + 2], offsets[-1]]
+    tokens, send = add_tokens(facts_late, act, places, chips, late, tokens, unit)
     llm_tokens = (tokens + swap_cores(send).astype(jnp.float32)).astype(jnp.bfloat16)
     grad_features = conv_backward(
         grad_even, grad_odd, slope, excite, squeezed, grad_relaxed, squeeze_in, dense, width

time: 168 us -> 187 us (1.11); the launches traced: 165 us -> 187 us
  waiting for transfers between devices: 42.5 us -> 66.7 us
  starting transfers between devices: 54.2 us -> 48.6 us
  Pallas kernels: 46.4 us -> 48.6 us
    ppermute x14, waiting for transfers between devices: 14.7 us -> 38.6 us  [ring_send(): return lax.ppermute(value, 'ctx', ring_pairs(lax.axis_size('ctx'), by))]
    ppermute x2, waiting for transfers between devices: 9.57 us -> 15.7 us  [shifted(): return lax.ppermute(value, axis, pairs)]
    ppermute x5 -> x7, waiting for transfers between devices: 16.1 us -> 10.8 us  [tp_terms(): other = lax.ppermute(value, 'tp', [(i, i ^ reach) for i in range(size)])]
    pallas_call x3 -> x5, Pallas kernels: 6.69 us -> 11.2 us  [block_products(): whole_call(kernel, f32(rows, len(blocks) * blocks[0].shape[0]), [])]
    ppermute x14, starting transfers between devices: 17.1 us -> 14.6 us  [ring_send(): return lax.ppermute(value, 'ctx', ring_pairs(lax.axis_size('ctx'), by))]
    ppermute x5, starting transfers between devices: 12.3 us -> 9.98 us  [swap_cores(): lax.ppermute(value, 'ctx', [(i, i ^ 1) for i in range(lax.axis_size('ctx'...]
    all_to_all x2, waiting for transfers between devices: 2.11 us -> 0.01 us  [chips_exchange(): lax.all_to_all(value, 'ctx', split_axis=0, concat_axis=0, tiled=True, axi...]
    ppermute x2, starting transfers between devices: 8.89 us -> 6.86 us  [shifted(): return lax.ppermute(value, axis, pairs)]
  transfers between devices with their start and end apart: 28 -> 30, of which waited for: 13 -> 14; matrix products, arithmetic and copies ran while one was open for 1% -> 1% of each run, Pallas kernels for 27% -> 24%
where the time goes in v6:
time: 187 us
  waiting for transfers between devices  66.7 us (36%)
  starting transfers between devices  48.6 us (26%)
  Pallas kernels  48.6 us (26%)
  local copies, waits for them, and re-layouts  20.6 us (11%)
    ppermute x14, waiting for transfers between devices, ring_send(): return lax.ppermute(value, 'ctx', ring_pairs(lax.axis_size('ctx'), by))  38.6 us
    pallas_call x10, Pallas kernels, facts_call(): pl.pallas_call(kernel, out_shape=outs, in_specs=vmem_specs(len(operands))...  20 us
    unnamed x100, local copies, waits for them, and re-layouts  18.8 us
    ppermute x2, waiting for transfers between devices, shifted(): return lax.ppermute(value, axis, pairs)  15.7 us
    ppermute x14, starting transfers between devices, ring_send(): return lax.ppermute(value, 'ctx', ring_pairs(lax.axis_size('ctx'), by))  14.6 us
    pallas_call x5, Pallas kernels, block_products(): whole_call(kernel, f32(rows, len(blocks) * blocks[0].shape[0]), [])  11.2 us
    ppermute x7, waiting for transfers between devices, tp_terms(): other = lax.ppermute(value, 'tp', [(i, i ^ reach) for i in range(size)])  10.8 us
    ppermute x5, starting transfers between devices, swap_cores(): lax.ppermute(value, 'ctx', [(i, i ^ 1) for i in range(lax.axis_size('ctx'...  9.98 us
  transfers between devices with their start and end apart: 30, of which 14 were waited for; matrix products, arithmetic and copies ran while one was open for 1% of the time, Pallas kernels for 24%

profile of v6, /device:TPU:3, one launch (start us, length us, event | category | flops | bytes accessed | tf_op | source)
XLA Modules:
  0.0 186.6 jit_solution(8892641318963912089)
XLA Ops:
  0.7 1.8 reshape.11.refs_0_.refs_4_
  2.4 1.3 collective-permute-start.4
  4.0 4.4 %shard_map.105 = (f32[512,576]{1,0:T(8,128)S(1)}, bf16[512,576]{1,0:T(8,128)(2,1)S(1)}, f32[2,288]{1,0:T(2,128)S(1)}) custom-call(bf16[2,196,576]{2,1,0:T(8,128)(2,1)S(1)} %copy.11.feat_ref, bf16[9,48,576]{2,1,0:T(8,128)(2,1)S(1)} %bitcast.10, bf16[288,576]{1,0:T(8,128)(2,1)S(1)} %bitcast.14), custom_call_target="tpu_custom_call" | custom-call | tf_op jit(solution)/shard_map/pallas_call | solution.py:307
  8.5 1.3 collective-permute-start.1
  9.8 1.5 collective-permute-done.1
  11.3 1.1 shard_map.106
  12.4 1.1 copy-done.15
  14.1 1.1 copy-done.40
  15.1 3.1 %collective-permute-done.4.refs_2_.refs_6_ = bf16[72,4608]{1,0:T(8,128)(2,1)S(1)} collective-permute-done((bf16[72,4608]{1,0:T(8,128)(2,1)S(1)}, bf16[72,4608]{1,0:T(8,128)(2,1)S(1)}, u32[]{:S(2)}, u32[]{:S(2)}) %collective-permute-start.4) | collective-permute-done | bytes 663584 | tf_op jit(solution)/shard_map/ppermute | solution.py:443
  20.3 1.3 collective-permute-start.6
  22.4 4.2 %collective-permute-start.2 = (bf16[256,576]{1,0:T(8,128)(2,1)S(1)}, bf16[256,576]{1,0:T(8,128)(2,1)S(1)}, u32[]{:S(2)}, u32[]{:S(2)}) collective-permute-start(bf16[256,576]{1,0:T(8,128)(2,1)S(1)} %get-tuple-element.83), channel_id=1, source_target_pairs={{0,2},{2,4},{4,6},{6,8},{8,10},{10,12},{12,14},{14,16},{16,18},{18... | collective-permute-start | bytes 884744 | tf_op jit(solution)/shard_map/ppermute | solution.py:407
  26.7 13.1 %collective-permute-done.2.halo_ref = bf16[256,576]{1,0:T(8,128)(2,1)S(1)} collective-permute-done((bf16[256,576]{1,0:T(8,128)(2,1)S(1)}, bf16[256,576]{1,0:T(8,128)(2,1)S(1)}, u32[]{:S(2)}, u32[]{:S(2)}) %collective-permute-start.2) | collective-permute-done | bytes 294944 | tf_op jit(solution)/shard_map/ppermute | solution.py:407
  40.0 1.3 collective-permute-start.8
  41.3 1.3 shard_map.104.facts_ref
  43.2 1.8 shard_map.107.own_ref
  45.0 1.9 collective-permute-start.11
  46.9 8.2 %collective-permute-done.7.refs_5_.refs_4_ = bf16[72,4608]{1,0:T(8,128)(2,1)S(1)} collective-permute-done((bf16[72,4608]{1,0:T(8,128)(2,1)S(1)}, bf16[72,4608]{1,0:T(8,128)(2,1)S(1)}, u32[]{:S(2)}, u32[]{:S(2)}) %collective-permute-start.7) | collective-permute-done | bytes 663584 | tf_op jit(solution)/shard_map/ppermute | solution.py:443
  55.1 2.2 %collective-permute-start.10 = (bf16[72,4096]{1,0:T(8,128)(2,1)}, bf16[72,4096]{1,0:T(8,128)(2,1)}, u32[]{:S(2)}, u32[]{:S(2)}) collective-permute-start(bf16[72,4096]{1,0:T(8,128)(2,1)} %refs_0_.1), channel_id=1, source_target_pairs={{0,4},{2,6},{8,0},{10,2},{16,8},{18,10},{24,16},{26,18},{28,24},{3... | collective-permute-start | bytes 1769480 | tf_op jit(solution)/shard_map/ppermute | solution.py:443
  57.3 6.0 %all-to-all-start = ((bf16[8,8,4096]{2,1,0:T(8,128)(2,1)}), bf16[8,8,4096]{2,1,0:T(8,128)(2,1)S(1)}, u32[]{:S(2)}, u32[]{:S(2)}) async-start(bf16[8,8,4096]{2,1,0:T(8,128)(2,1)} %bitcast.16), calls=%async_computation | async-start | bytes 1048576 | tf_op jit(solution)/shard_map/all_to_all | solution.py:597
  64.1 1.1 copy-done.28
  65.8 1.6 shard_map.108.patch_ref
  67.4 3.6 %shard_map.109.own_ref = f32[128,504]{1,0:T(8,128)S(1)} custom-call(bf16[128,4608]{1,0:T(8,128)(2,1)S(1)} %shard_map.108.patch_ref, bf16[72,4608]{1,0:T(8,128)(2,1)S(1)} %reshape.11.refs_0_.refs_4_, bf16[72,4608]{1,0:T(8,128)(2,1)S(1)} %copy-done.6, bf16[72,4608]{1,0:T(8,128)(2,1)S(1)} %copy-done.3, bf16[72,4608]{1,0:T(8,128)(2,1)S(1)} %copy-done.9, ...), custom_call_target="tpu_custom_call" | custom-call | tf_op jit(solution)/shard_map/pallas_call | solution.py:555
  71.8 1.2 collective-permute-start.14
  73.2 16.3 %collective-permute-done.14.refs_1_.refs_4_ = bf16[72,4096]{1,0:T(8,128)(2,1)} collective-permute-done((bf16[72,4096]{1,0:T(8,128)(2,1)}, bf16[72,4096]{1,0:T(8,128)(2,1)}, u32[]{:S(2)}, u32[]{:S(2)}) %collective-permute-start.14) | collective-permute-done | bytes 589856 | tf_op jit(solution)/shard_map/ppermute | solution.py:443
  89.6 4.2 %collective-permute-start.15 = (bf16[72,4096]{1,0:T(8,128)(2,1)}, bf16[72,4096]{1,0:T(8,128)(2,1)}, u32[]{:S(2)}, u32[]{:S(2)}) collective-permute-start(bf16[72,4096]{1,0:T(8,128)(2,1)} %collective-permute-done.14.refs_1_.refs_4_), channel_id=1, source_target_pairs={{0,4},{2,6},{8,0},{10,2},{16,8},{18,10},{24,16},{26,18},{28,24},{3... | collective-permute-start | bytes 1769480 | tf_op jit(solution)/shard_map/ppermute | solution.py:443
  93.8 2.9 %collective-permute-start = (bf16[64,4096]{1,0:T(8,128)(2,1)S(1)}, bf16[64,4096]{1,0:T(8,128)(2,1)S(1)}, u32[]{:S(2)}, u32[]{:S(2)}) collective-permute-start(bf16[64,4096]{1,0:T(8,128)(2,1)S(1)} %bitcast.6), channel_id=1, source_target_pairs={{0,2},{2,0},{4,6},{6,4},{8,10},{10,8},{12,14},{14,12},{16,18},{18,... | collective-permute-start | bytes 1572872 | tf_op jit(solution)/shard_map/ppermute | solution.py:424
  96.7 1.5 collective-permute-done.send_ref
  98.2 2.4 %shard_map.110.refs_0_ = f32[128,216]{1,0:T(8,128)S(1)} custom-call(bf16[64,4096]{1,0:T(8,128)(2,1)S(1)} %bitcast.7, bf16[64,4096]{1,0:T(8,128)(2,1)S(1)} %collective-permute-done.send_ref, bf16[72,4096]{1,0:T(8,128)(2,1)} %refs_0_.1, bf16[72,4096]{1,0:T(8,128)(2,1)} %collective-permute-done.9.refs_1_, bf16[72,4096]{1,0:T(8,128)(2,1)} %collective-permute-done.10.refs_2_), custom_call_target="tpu_custom_call" | custom-call | tf_op jit(solution)/shard_map/pallas_call | solution.py:555
  100.7 3.4 %collective-permute-done.15.refs_2_.refs_5_ = bf16[72,4096]{1,0:T(8,128)(2,1)} collective-permute-done((bf16[72,4096]{1,0:T(8,128)(2,1)}, bf16[72,4096]{1,0:T(8,128)(2,1)}, u32[]{:S(2)}, u32[]{:S(2)}) %collective-permute-start.15) | collective-permute-done | bytes 589856 | tf_op jit(solution)/shard_map/ppermute | solution.py:443
  104.1 2.2 %collective-permute-start.16 = (bf16[72,4096]{1,0:T(8,128)(2,1)}, bf16[72,4096]{1,0:T(8,128)(2,1)}, u32[]{:S(2)}, u32[]{:S(2)}) collective-permute-start(bf16[72,4096]{1,0:T(8,128)(2,1)} %collective-permute-done.15.refs_2_.refs_5_), channel_id=1, source_target_pairs={{0,4},{2,6},{8,0},{10,2},{16,8},{18,10},{24,16},{26,18},{28,24},{3... | collective-permute-start | bytes 1769480 | tf_op jit(solution)/shard_map/ppermute | solution.py:443
  106.3 1.2 collective-permute-start.19
  107.6 6.6 %collective-permute-done.17.refs_0_.refs_5_ = bf16[72,4608]{1,0:T(8,128)(2,1)S(1)} collective-permute-done((bf16[72,4608]{1,0:T(8,128)(2,1)S(1)}, bf16[72,4608]{1,0:T(8,128)(2,1)S(1)}, u32[]{:S(2)}, u32[]{:S(2)}) %collective-permute-start.17) | collective-permute-done | bytes 663584 | tf_op jit(solution)/shard_map/ppermute | solution.py:443
  114.6 1.3 collective-permute-start.18
  115.9 1.1 shard_map.112
  117.1 1.1 collective-permute-done.18.other_ref
  118.2 1.6 shard_map.113
  119.8 3.7 %all-to-all-start.1 = ((bf16[8,16,576]{2,1,0:T(8,128)(2,1)}), bf16[8,16,576]{2,1,0:T(8,128)(2,1)S(1)}, u32[]{:S(2)}, u32[]{:S(2)}) async-start(bf16[8,16,576]{2,1,0:T(8,128)(2,1)} %bitcast.4), calls=%async_computation.1 | async-start | bytes 327680 | tf_op jit(solution)/shard_map/all_to_all | solution.py:597
  123.5 1.2 collective-permute-start.20
  124.8 3.0 %collective-permute-done.20.refs_1_ = f32[128,216]{1,0:T(8,128)S(1)} collective-permute-done((f32[128,216]{1,0:T(8,128)}, f32[128,216]{1,0:T(8,128)S(1)}, u32[]{:S(2)}, u32[]{:S(2)}) %collective-permute-start.20) | collective-permute-done | bytes 110624 | tf_op jit(solution)/shard_map/ppermute | solution.py:432
  127.8 1.1 copy-done.4
  128.9 1.1 copy-done.7
  131.5 1.5 shard_map.115
  133.0 1.5 shard_map.114
  134.5 2.5 %shard_map.116.refs_0_ = f32[128,216]{1,0:T(8,128)S(1)} custom-call(bf16[64,4096]{1,0:T(8,128)(2,1)S(1)} %bitcast.8, bf16[64,4096]{1,0:T(8,128)(2,1)S(1)} %collective-permute-done.send_ref, bf16[72,4096]{1,0:T(8,128)(2,1)} %collective-permute-done.12.refs_0_.refs_3_, bf16[72,4096]{1,0:T(8,128)(2,1)} %collective-permute-done.14.refs_1_.refs_4_, ...), custom_call_target="tpu_custom_call" | custom-call | tf_op jit(solution)/shard_map/pallas_call | solution.py:555
  137.1 1.1 collective-permute-start.21
  138.2 1.0 shard_map.119
  139.2 1.0 copy-done.42
  140.2 1.1 copy-done.44
  142.2 2.3 %shard_map.118 = (f32[64,2304]{1,0:T(8,128)S(1)}, f32[64,2304]{1,0:T(8,128)S(1)}) custom-call(s32[5]{0:T(128)S(1)} %copy-done.35, f32[128,216]{1,0:T(8,128)S(1)} %shard_map.116.refs_0_, f32[128,216]{1,0:T(8,128)S(1)} %collective-permute-done.21.refs_1_, f32[128,504]{1,0:T(8,128)S(1)} %get-tuple-element.104.refs_2_, ...), custom_call_target="tpu_custom_call" | custom-call | tf_op jit(solution)/shard_map/pallas_call | solution.py:559
  145.4 2.3 %shard_map.117 = (f32[64,2304]{1,0:T(8,128)S(1)}, f32[64,2304]{1,0:T(8,128)S(1)}) custom-call(s32[5]{0:T(128)S(1)} %copy-done.35, f32[128,216]{1,0:T(8,128)S(1)} %shard_map.116.refs_0_, f32[128,216]{1,0:T(8,128)S(1)} %collective-permute-done.21.refs_1_, f32[128,504]{1,0:T(8,128)S(1)} %get-tuple-element.104.refs_2_, ...), custom_call_target="tpu_custom_call" | custom-call | tf_op jit(solution)/shard_map/pallas_call | solution.py:559
  149.4 4.8 %shard_map.120 = (f32[64,4096]{1,0:T(8,128)S(1)}, f32[64,4096]{1,0:T(8,128)S(1)}) custom-call(s32[5]{0:T(128)S(1)} %copy-done.35, bf16[128,576]{1,0:T(8,128)(2,1)S(1)} %bitcast.12, bf16[72,4096]{1,0:T(8,128)(2,1)} %refs_0_.1, bf16[72,4096]{1,0:T(8,128)(2,1)} %collective-permute-done.9.refs_1_, bf16[72,4096]{1,0:T(8,128)(2,1)} %collective-permute-done.10.refs_2_, ...), custom_call_target="tpu_custom_call" | custom-call | tf_op jit(solution)/shard_map/pallas_call | solution.py:559
  154.2 2.1 %shard_map.121.refs_0_ = f32[128,144]{1,0:T(8,128)S(1)} custom-call(bf16[64,4096]{1,0:T(8,128)(2,1)S(1)} %bitcast.9, bf16[64,4096]{1,0:T(8,128)(2,1)S(1)} %collective-permute-done.send_ref, bf16[72,4096]{1,0:T(8,128)(2,1)} %collective-permute-done.13.refs_0_, bf16[72,4096]{1,0:T(8,128)(2,1)} %collective-permute-done.16.refs_1_), custom_call_target="tpu_custom_call" | custom-call | tf_op jit(solution)/shard_map/pallas_call | solution.py:555
  156.8 3.4 %collective-permute-done.22.refs_1_ = f32[128,144]{1,0:T(8,128)S(1)} collective-permute-done((f32[128,144]{1,0:T(8,128)S(1)}, f32[128,144]{1,0:T(8,128)S(1)}, u32[]{:S(2)}, u32[]{:S(2)}) %collective-permute-start.22) | collective-permute-done | bytes 73760 | tf_op jit(solution)/shard_map/ppermute | solution.py:432
  160.2 1.2 shard_map.122
  161.5 5.1 %collective-permute-start.23 = (bf16[64,2304]{1,0:T(8,128)(2,1)S(1)}, bf16[64,2304]{1,0:T(8,128)(2,1)S(1)}, u32[]{:S(2)}, u32[]{:S(2)}) collective-permute-start(bf16[64,2304]{1,0:T(8,128)(2,1)S(1)} %get-tuple-element.134), channel_id=1, source_target_pairs={{0,2},{2,0},{4,6},{6,4},{8,10},{10,8},{12,14},{14,12},{16,18},{18,... | collective-permute-start | bytes 884744 | tf_op jit(solution)/shard_map/ppermute | solution.py:424
  166.6 1.2 shard_map.124
  167.9 1.5 shard_map.123
  169.4 2.6 %collective-permute-start.26 = (bf16[256,576]{1,0:T(8,128)(2,1)S(1)}, bf16[256,576]{1,0:T(8,128)(2,1)S(1)}, u32[]{:S(2)}, u32[]{:S(2)}) collective-permute-start(bf16[256,576]{1,0:T(8,128)(2,1)S(1)} %get-tuple-element.147), channel_id=1, source_target_pairs={{2,0},{4,2},{6,4},{8,6},{10,8},{12,10},{14,12},{16,14},{18,16},{20... | collective-permute-start | bytes 884744 | tf_op jit(solution)/shard_map/ppermute | solution.py:407
  172.0 1.5 shard_map.125
  173.5 2.4 %shard_map.126 = (f32[64,4096]{1,0:T(8,128)S(1)}, bf16[64,4096]{1,0:T(8,128)(2,1)S(1)}) custom-call(s32[5]{0:T(128)S(1)} %get-tuple-element.141.facts_ref, bf16[128,576]{1,0:T(8,128)(2,1)S(1)} %bitcast.13, bf16[72,4096]{1,0:T(8,128)(2,1)} %collective-permute-done.13.refs_0_, bf16[72,4096]{1,0:T(8,128)(2,1)} %collective-permute-done.16.refs_1_, ...), custom_call_target="tpu_custom_call" | custom-call | flops 3019898880 | tf_op jit(solution)/shard_map/pallas_call | solution.py:559
  176.1 2.6 %collective-permute-done.26.odd_ref = bf16[256,576]{1,0:T(8,128)(2,1)S(1)} collective-permute-done((bf16[256,576]{1,0:T(8,128)(2,1)S(1)}, bf16[256,576]{1,0:T(8,128)(2,1)S(1)}, u32[]{:S(2)}, u32[]{:S(2)}) %collective-permute-start.26) | collective-permute-done | bytes 294944 | tf_op jit(solution)/shard_map/ppermute | solution.py:407
  180.2 1.7 collective-permute-done.27
  182.0 2.5 %shard_map.128 = bf16[2,196,576]{2,1,0:T(8,128)(2,1)S(1)} custom-call(f32[256,576]{1,0:T(8,128)S(1)} %get-tuple-element.146.even_ref, bf16[256,576]{1,0:T(8,128)(2,1)S(1)} %collective-permute-done.26.odd_ref, f32[512,576]{1,0:T(8,128)S(1)} %copy-done.41, f32[2,576]{1,0:T(2,128)S(1)} %copy-done.39, f32[2,288]{1,0:T(2,128)S(1)} %copy-done.37, ...), custom_call_target="tpu_custom_call" | custom-call | flops 2717908992 | bytes 4718592 | tf_op jit(solution)/shard_map/pallas_call | solution.py:391
  184.6 1.2 copy.12
  (125 shorter events, 15.7 us)
Async XLA Ops:
  0.6 3.3 %copy-start.48 = (bf16[2,196,576]{2,0,1:T(2,128)(2,1)S(1)}, bf16[2,196,576]{2,0,1:T(2,128)(2,1)}, u32[]{:S(2)}) copy-start(bf16[2,196,576]{2,0,1:T(2,128)(2,1)} %param.9) | copy-start | bytes 1354756
  0.6 3.4 %copy-start.29 = (bf16[576,288]{0,1:T(8,128)(2,1)S(1)}, bf16[576,288]{0,1:T(8,128)(2,1)}, u32[]{:S(2)}) copy-start(bf16[576,288]{0,1:T(8,128)(2,1)} %param.11) | copy-start | bytes 995332
  0.7 3.4 %copy-start.11 = (bf16[9,576,48]{1,2,0:T(8,128)(2,1)S(1)}, bf16[9,576,48]{1,2,0:T(8,128)(2,1)}, u32[]{:S(2)}) copy-start(bf16[9,576,48]{1,2,0:T(8,128)(2,1)} %param.10) | copy-start | bytes 1492996
  2.4 8.8 %copy-start.13 = (bf16[288,576]{1,0:T(8,128)(2,1)S(1)}, bf16[288,576]{1,0:T(8,128)(2,1)}, u32[]{:S(2)}) copy-start(bf16[288,576]{1,0:T(8,128)(2,1)} %expand_ref.3) | copy-start | bytes 995332
  2.4 15.8 %collective-permute-start.4 = (bf16[72,4608]{1,0:T(8,128)(2,1)S(1)}, bf16[72,4608]{1,0:T(8,128)(2,1)S(1)}, u32[]{:S(2)}, u32[]{:S(2)}) collective-permute-start(bf16[72,4608]{1,0:T(8,128)(2,1)S(1)} %reshape.11.refs_0_.refs_4_), channel_id=1, source_target_pairs={{0,4},{2,6},{8,0},{10,2},{16,8},{18,10},{24,16},{26,18},{28,24},{3... | collective-permute-start | bytes 1990664 | tf_op jit(solution)/shard_map/ppermute | solution.py:443
  3.8 15.5 %collective-permute-start.3 = (bf16[72,4608]{1,0:T(8,128)(2,1)S(1)}, bf16[72,4608]{1,0:T(8,128)(2,1)S(1)}, u32[]{:S(2)}, u32[]{:S(2)}) collective-permute-start(bf16[72,4608]{1,0:T(8,128)(2,1)S(1)} %reshape.11.refs_0_.refs_4_), channel_id=1, source_target_pairs={{0,8},{2,10},{8,16},{10,18},{16,24},{18,26},{24,28},{26,30},{28,20... | collective-permute-start | bytes 1990664 | tf_op jit(solution)/shard_map/ppermute | solution.py:443
  8.5 2.8 %collective-permute-start.1 = (f32[2,288]{1,0:T(2,128)S(1)}, f32[2,288]{1,0:T(2,128)S(1)}, u32[]{:S(2)}, u32[]{:S(2)}) collective-permute-start(f32[2,288]{1,0:T(2,128)S(1)} %get-tuple-element.82), channel_id=1, source_target_pairs={{0,1},{1,0},{2,3},{3,2},{4,5},{5,4},{6,7},{7,6},{8,9},{9,8},{10,11... | collective-permute-start | bytes 6920 | tf_op jit(solution)/shard_map/ppermute | solution.py:432
  11.3 28.6 %copy-start.36 = (f32[2,288]{1,0:T(2,128)}, f32[2,288]{1,0:T(2,128)S(1)}, u32[]{:S(2)}) copy-start(f32[2,288]{1,0:T(2,128)S(1)} %add.9.sq_ref) | copy-start | bytes 6916
  12.4 1.1 copy-start.15
  14.1 1.1 copy-start.40
  19.2 20.6 %collective-permute-start.5 = (bf16[72,4608]{1,0:T(8,128)(2,1)S(1)}, bf16[72,4608]{1,0:T(8,128)(2,1)S(1)}, u32[]{:S(2)}, u32[]{:S(2)}) collective-permute-start(bf16[72,4608]{1,0:T(8,128)(2,1)S(1)} %collective-permute-done.3.refs_1_.refs_5_), channel_id=1, source_target_pairs={{0,8},{2,10},{8,16},{10,18},{16,24},{18,26},{24,28},{26,30},{28,20... | collective-permute-start | bytes 1990664 | tf_op jit(solution)/shard_map/ppermute | solution.py:443
  20.3 19.5 %collective-permute-start.6 = (bf16[72,4608]{1,0:T(8,128)(2,1)S(1)}, bf16[72,4608]{1,0:T(8,128)(2,1)}, u32[]{:S(2)}, u32[]{:S(2)}) collective-permute-start(bf16[72,4608]{1,0:T(8,128)(2,1)S(1)} %collective-permute-done.4.refs_2_.refs_6_), channel_id=1, source_target_pairs={{0,4},{2,6},{8,0},{10,2},{16,8},{18,10},{24,16},{26,18},{28,24},{3... | collective-permute-start | bytes 1990664 | tf_op jit(solution)/shard_map/ppermute | solution.py:443
  22.4 17.4 %collective-permute-start.2 = (bf16[256,576]{1,0:T(8,128)(2,1)S(1)}, bf16[256,576]{1,0:T(8,128)(2,1)S(1)}, u32[]{:S(2)}, u32[]{:S(2)}) collective-permute-start(bf16[256,576]{1,0:T(8,128)(2,1)S(1)} %get-tuple-element.83), channel_id=1, source_target_pairs={{0,2},{2,4},{4,6},{6,8},{8,10},{10,12},{12,14},{14,16},{16,18},{18... | collective-permute-start | bytes 884744 | tf_op jit(solution)/shard_map/ppermute | solution.py:407
  39.8 23.5 %copy-start.8 = (bf16[72,4608]{1,0:T(8,128)(2,1)}, bf16[72,4608]{1,0:T(8,128)(2,1)S(1)}, u32[]{:S(2)}) copy-start(bf16[72,4608]{1,0:T(8,128)(2,1)S(1)} %collective-permute-done.5.refs_3_.refs_4_) | copy-start | bytes 1990660
  39.8 15.3 %collective-permute-start.7 = (bf16[72,4608]{1,0:T(8,128)(2,1)S(1)}, bf16[72,4608]{1,0:T(8,128)(2,1)S(1)}, u32[]{:S(2)}, u32[]{:S(2)}) collective-permute-start(bf16[72,4608]{1,0:T(8,128)(2,1)S(1)} %collective-permute-done.5.refs_3_.refs_4_), channel_id=1, source_target_pairs={{0,8},{2,10},{8,16},{10,18},{16,24},{18,26},{24,28},{26,30},{28,20... | collective-permute-start | bytes 1990664 | tf_op jit(solution)/shard_map/ppermute | solution.py:443
  40.0 15.0 %collective-permute-start.8 = (bf16[72,4608]{1,0:T(8,128)(2,1)}, bf16[72,4608]{1,0:T(8,128)(2,1)}, u32[]{:S(2)}, u32[]{:S(2)}) collective-permute-start(bf16[72,4608]{1,0:T(8,128)(2,1)} %collective-permute-done.6.refs_4_.refs_5_), channel_id=1, source_target_pairs={{0,4},{2,6},{8,0},{10,2},{16,8},{18,10},{24,16},{26,18},{28,24},{3... | collective-permute-start | bytes 1990664 | tf_op jit(solution)/shard_map/ppermute | solution.py:443
  45.0 18.2 %collective-permute-start.11 = (bf16[64,4608]{1,0:T(8,128)(2,1)}, bf16[64,4608]{1,0:T(8,128)(2,1)S(1)}, u32[]{:S(2)}, u32[]{:S(2)}) collective-permute-start(bf16[64,4608]{1,0:T(8,128)(2,1)} %shard_map.107.own_ref), channel_id=1, source_target_pairs={{0,2},{2,0},{4,6},{6,4},{8,10},{10,8},{12,14},{14,12},{16,18},{18,... | collective-permute-start | bytes 1769480 | tf_op jit(solution)/shard_map/ppermute | solution.py:424
  55.1 16.7 %collective-permute-start.10 = (bf16[72,4096]{1,0:T(8,128)(2,1)}, bf16[72,4096]{1,0:T(8,128)(2,1)}, u32[]{:S(2)}, u32[]{:S(2)}) collective-permute-start(bf16[72,4096]{1,0:T(8,128)(2,1)} %refs_0_.1), channel_id=1, source_target_pairs={{0,4},{2,6},{8,0},{10,2},{16,8},{18,10},{24,16},{26,18},{28,24},{3... | collective-permute-start | bytes 1769480 | tf_op jit(solution)/shard_map/ppermute | solution.py:443
  57.3 14.5 %collective-permute-start.9 = (bf16[72,4096]{1,0:T(8,128)(2,1)}, bf16[72,4096]{1,0:T(8,128)(2,1)}, u32[]{:S(2)}, u32[]{:S(2)}) collective-permute-start(bf16[72,4096]{1,0:T(8,128)(2,1)} %refs_0_.1), channel_id=1, source_target_pairs={{0,8},{2,10},{8,16},{10,18},{16,24},{18,26},{24,28},{26,30},{28,20... | collective-permute-start | bytes 1769480 | tf_op jit(solution)/shard_map/ppermute | solution.py:443
  57.3 36.5 %all-to-all-start = ((bf16[8,8,4096]{2,1,0:T(8,128)(2,1)}), bf16[8,8,4096]{2,1,0:T(8,128)(2,1)S(1)}, u32[]{:S(2)}, u32[]{:S(2)}) async-start(bf16[8,8,4096]{2,1,0:T(8,128)(2,1)} %bitcast.16), calls=%async_computation | async-start | bytes 1048576 | tf_op jit(solution)/shard_map/all_to_all | solution.py:597
  63.3 4.1 %copy-start.3 = (bf16[72,4608]{1,0:T(8,128)(2,1)S(1)}, bf16[72,4608]{1,0:T(8,128)(2,1)}, u32[]{:S(2)}) copy-start(bf16[72,4608]{1,0:T(8,128)(2,1)} %copy-done.2) | copy-start | bytes 1990660
  63.3 4.1 %copy-start.6 = (bf16[72,4608]{1,0:T(8,128)(2,1)S(1)}, bf16[72,4608]{1,0:T(8,128)(2,1)}, u32[]{:S(2)}) copy-start(bf16[72,4608]{1,0:T(8,128)(2,1)} %copy-done.5) | copy-start | bytes 1990660
  64.1 1.1 copy-start.28
  65.8 1.6 copy-start.9
  71.8 17.8 %collective-permute-start.14 = (bf16[72,4096]{1,0:T(8,128)(2,1)}, bf16[72,4096]{1,0:T(8,128)(2,1)}, u32[]{:S(2)}, u32[]{:S(2)}) collective-permute-start(bf16[72,4096]{1,0:T(8,128)(2,1)} %collective-permute-done.10.refs_2_), channel_id=1, source_target_pairs={{0,4},{2,6},{8,0},{10,2},{16,8},{18,10},{24,16},{26,18},{28,24},{3... | collective-permute-start | bytes 1769480 | tf_op jit(solution)/shard_map/ppermute | solution.py:443
  73.0 27.7 %collective-permute-start.12 = (bf16[72,4096]{1,0:T(8,128)(2,1)}, bf16[72,4096]{1,0:T(8,128)(2,1)}, u32[]{:S(2)}, u32[]{:S(2)}) collective-permute-start(bf16[72,4096]{1,0:T(8,128)(2,1)} %collective-permute-done.9.refs_1_), channel_id=1, source_target_pairs={{0,8},{2,10},{8,16},{10,18},{16,24},{18,26},{24,28},{26,30},{28,20... | collective-permute-start | bytes 1769480 | tf_op jit(solution)/shard_map/ppermute | solution.py:443
  89.6 14.5 %collective-permute-start.15 = (bf16[72,4096]{1,0:T(8,128)(2,1)}, bf16[72,4096]{1,0:T(8,128)(2,1)}, u32[]{:S(2)}, u32[]{:S(2)}) collective-permute-start(bf16[72,4096]{1,0:T(8,128)(2,1)} %collective-permute-done.14.refs_1_.refs_4_), channel_id=1, source_target_pairs={{0,4},{2,6},{8,0},{10,2},{16,8},{18,10},{24,16},{26,18},{28,24},{3... | collective-permute-start | bytes 1769480 | tf_op jit(solution)/shard_map/ppermute | solution.py:443
  93.8 12.5 %copy-start.20 = (f32[128,504]{1,0:T(8,128)S(1)}, f32[128,504]{1,0:T(8,128)}, u32[]{:S(2)}) copy-start(f32[128,504]{1,0:T(8,128)} %copy-done.19) | copy-start | bytes 774148
  93.8 4.4 %collective-permute-start = (bf16[64,4096]{1,0:T(8,128)(2,1)S(1)}, bf16[64,4096]{1,0:T(8,128)(2,1)S(1)}, u32[]{:S(2)}, u32[]{:S(2)}) collective-permute-start(bf16[64,4096]{1,0:T(8,128)(2,1)S(1)} %bitcast.6), channel_id=1, source_target_pairs={{0,2},{2,0},{4,6},{6,4},{8,10},{10,8},{12,14},{14,12},{16,18},{18,... | collective-permute-start | bytes 1572872 | tf_op jit(solution)/shard_map/ppermute | solution.py:424
  96.6 17.5 %collective-permute-start.17 = (bf16[72,4608]{1,0:T(8,128)(2,1)S(1)}, bf16[72,4608]{1,0:T(8,128)(2,1)S(1)}, u32[]{:S(2)}, u32[]{:S(2)}) collective-permute-start(bf16[72,4608]{1,0:T(8,128)(2,1)S(1)} %collective-permute-done.7.refs_5_.refs_4_), channel_id=1, source_target_pairs={{0,8},{2,10},{8,16},{10,18},{16,24},{18,26},{24,28},{26,30},{28,20... | collective-permute-start | bytes 1990664 | tf_op jit(solution)/shard_map/ppermute | solution.py:443
  100.6 19.2 %copy-start.17 = (f32[128,216]{1,0:T(8,128)}, f32[128,216]{1,0:T(8,128)S(1)}, u32[]{:S(2)}) copy-start(f32[128,216]{1,0:T(8,128)S(1)} %shard_map.110.refs_0_) | copy-start | bytes 331780
  100.7 15.3 %copy-start.33 = (s32[5]{0:T(128)S(1)}, s32[5]{0:T(128)}, u32[]{:S(2)}) copy-start(s32[5]{0:T(128)} %shard_map.104.facts_ref) | copy-start | bytes 64
  100.7 53.5 %collective-permute-start.13 = (bf16[72,4096]{1,0:T(8,128)(2,1)}, bf16[72,4096]{1,0:T(8,128)(2,1)}, u32[]{:S(2)}, u32[]{:S(2)}) collective-permute-start(bf16[72,4096]{1,0:T(8,128)(2,1)} %collective-permute-done.12.refs_0_.refs_3_), channel_id=1, source_target_pairs={{0,8},{2,10},{8,16},{10,18},{16,24},{18,26},{24,28},{26,30},{28,20... | collective-permute-start | bytes 1769480 | tf_op jit(solution)/shard_map/ppermute | solution.py:443
  104.1 50.1 %collective-permute-start.16 = (bf16[72,4096]{1,0:T(8,128)(2,1)}, bf16[72,4096]{1,0:T(8,128)(2,1)}, u32[]{:S(2)}, u32[]{:S(2)}) collective-permute-start(bf16[72,4096]{1,0:T(8,128)(2,1)} %collective-permute-done.15.refs_2_.refs_5_), channel_id=1, source_target_pairs={{0,4},{2,6},{8,0},{10,2},{16,8},{18,10},{24,16},{26,18},{28,24},{3... | collective-permute-start | bytes 1769480 | tf_op jit(solution)/shard_map/ppermute | solution.py:443
  106.3 9.6 %collective-permute-start.19 = (f32[128,504]{1,0:T(8,128)S(1)}, f32[128,504]{1,0:T(8,128)S(1)}, u32[]{:S(2)}, u32[]{:S(2)}) collective-permute-start(f32[128,504]{1,0:T(8,128)S(1)} %copy-done.20), channel_id=1, source_target_pairs={{0,1},{1,0},{2,3},{3,2},{4,5},{5,4},{6,7},{7,6},{8,9},{9,8},{10,11... | collective-permute-start | bytes 774152 | tf_op jit(solution)/shard_map/ppermute | solution.py:432
  114.2 5.6 %copy-start = (bf16[72,4608]{1,0:T(8,128)(2,1)}, bf16[72,4608]{1,0:T(8,128)(2,1)S(1)}, u32[]{:S(2)}) copy-start(bf16[72,4608]{1,0:T(8,128)(2,1)S(1)} %collective-permute-done.17.refs_0_.refs_5_) | copy-start | bytes 1990660
  114.6 3.6 %collective-permute-start.18 = (f32[128,72]{1,0:T(8,128)S(1)}, f32[128,72]{1,0:T(8,128)S(1)}, u32[]{:S(2)}, u32[]{:S(2)}) collective-permute-start(f32[128,72]{1,0:T(8,128)S(1)} %shard_map.111.own_ref), channel_id=1, source_target_pairs={{0,1},{1,0},{2,3},{3,2},{4,5},{5,4},{6,7},{7,6},{8,9},{9,8},{10,11... | collective-permute-start | bytes 110600 | tf_op jit(solution)/shard_map/ppermute | solution.py:432
  119.8 29.6 %all-to-all-start.1 = ((bf16[8,16,576]{2,1,0:T(8,128)(2,1)}), bf16[8,16,576]{2,1,0:T(8,128)(2,1)S(1)}, u32[]{:S(2)}, u32[]{:S(2)}) async-start(bf16[8,16,576]{2,1,0:T(8,128)(2,1)} %bitcast.4), calls=%async_computation.1 | async-start | bytes 327680 | tf_op jit(solution)/shard_map/all_to_all | solution.py:597
  123.5 4.3 %collective-permute-start.20 = (f32[128,216]{1,0:T(8,128)}, f32[128,216]{1,0:T(8,128)S(1)}, u32[]{:S(2)}, u32[]{:S(2)}) collective-permute-start(f32[128,216]{1,0:T(8,128)} %copy-done.17), channel_id=1, source_target_pairs={{0,1},{1,0},{2,3},{3,2},{4,5},{5,4},{6,7},{7,6},{8,9},{9,8},{10,11... | collective-permute-start | bytes 331784 | tf_op jit(solution)/shard_map/ppermute | solution.py:432
  127.8 1.1 copy-start.4
  128.9 1.1 copy-start.7
  134.5 3.7 %copy-start.12 = (bf16[9,576,48]{1,2,0:T(8,128)(2,1)S(1)}, bf16[9,576,48]{1,2,0:T(8,128)(2,1)}, u32[]{:S(2)}) copy-start(bf16[9,576,48]{1,2,0:T(8,128)(2,1)} %param.10) | copy-start | bytes 1492996
  134.5 7.7 %copy-start.10 = (bf16[72,4608]{1,0:T(8,128)(2,1)S(1)}, bf16[72,4608]{1,0:T(8,128)(2,1)}, u32[]{:S(2)}) copy-start(bf16[72,4608]{1,0:T(8,128)(2,1)} %copy-done.8) | copy-start | bytes 1990660
  134.5 7.7 %copy-start.35 = (s32[5]{0:T(128)S(1)}, s32[5]{0:T(128)}, u32[]{:S(2)}) copy-start(s32[5]{0:T(128)} %shard_map.104.facts_ref) | copy-start | bytes 64
  137.1 5.1 %collective-permute-start.21 = (f32[128,216]{1,0:T(8,128)S(1)}, f32[128,216]{1,0:T(8,128)S(1)}, u32[]{:S(2)}, u32[]{:S(2)}) collective-permute-start(f32[128,216]{1,0:T(8,128)S(1)} %shard_map.116.refs_0_), channel_id=1, source_target_pairs={{0,1},{1,0},{2,3},{3,2},{4,5},{5,4},{6,7},{7,6},{8,9},{9,8},{10,11... | collective-permute-start | bytes 331784 | tf_op jit(solution)/shard_map/ppermute | solution.py:432
  154.1 6.1 %copy-start.1 = (bf16[72,4608]{1,0:T(8,128)(2,1)S(1)}, bf16[72,4608]{1,0:T(8,128)(2,1)}, u32[]{:S(2)}) copy-start(bf16[72,4608]{1,0:T(8,128)(2,1)} %copy-done) | copy-start | bytes 1990660
  154.2 6.1 %copy-start.24 = (f32[64,2304]{1,0:T(8,128)S(1)}, f32[64,2304]{1,0:T(8,128)}, u32[]{:S(2)}) copy-start(f32[64,2304]{1,0:T(8,128)} %copy-done.23) | copy-start | bytes 1769476
  154.2 6.1 %copy-start.26 = (f32[64,2304]{1,0:T(8,128)S(1)}, f32[64,2304]{1,0:T(8,128)}, u32[]{:S(2)}) copy-start(f32[64,2304]{1,0:T(8,128)} %copy-done.25) | copy-start | bytes 1769476
  156.3 10.2 %copy-start.22 = (f32[64,2304]{1,0:T(8,128)S(1)}, f32[64,2304]{1,0:T(8,128)}, u32[]{:S(2)}) copy-start(f32[64,2304]{1,0:T(8,128)} %copy-done.21) | copy-start | bytes 1769476
  156.3 3.9 %collective-permute-start.22 = (f32[128,144]{1,0:T(8,128)S(1)}, f32[128,144]{1,0:T(8,128)S(1)}, u32[]{:S(2)}, u32[]{:S(2)}) collective-permute-start(f32[128,144]{1,0:T(8,128)S(1)} %shard_map.121.refs_0_), channel_id=1, source_target_pairs={{0,1},{1,0},{2,3},{3,2},{4,5},{5,4},{6,7},{7,6},{8,9},{9,8},{10,11... | collective-permute-start | bytes 221192 | tf_op jit(solution)/shard_map/ppermute | solution.py:432
  161.5 6.4 %collective-permute-start.23 = (bf16[64,2304]{1,0:T(8,128)(2,1)S(1)}, bf16[64,2304]{1,0:T(8,128)(2,1)S(1)}, u32[]{:S(2)}, u32[]{:S(2)}) collective-permute-start(bf16[64,2304]{1,0:T(8,128)(2,1)S(1)} %get-tuple-element.134), channel_id=1, source_target_pairs={{0,2},{2,0},{4,6},{6,4},{8,10},{10,8},{12,14},{14,12},{16,18},{18,... | collective-permute-start | bytes 884744 | tf_op jit(solution)/shard_map/ppermute | solution.py:424
  167.8 4.2 %collective-permute-start.24 = (bf16[64,2304]{1,0:T(8,128)(2,1)S(1)}, bf16[64,2304]{1,0:T(8,128)(2,1)S(1)}, u32[]{:S(2)}, u32[]{:S(2)}) collective-permute-start(bf16[64,2304]{1,0:T(8,128)(2,1)S(1)} %get-tuple-element.140), channel_id=1, source_target_pairs={{0,2},{2,0},{4,6},{6,4},{8,10},{10,8},{12,14},{14,12},{16,18},{18,... | collective-permute-start | bytes 884744 | tf_op jit(solution)/shard_map/ppermute | solution.py:424
  169.4 9.3 %collective-permute-start.26 = (bf16[256,576]{1,0:T(8,128)(2,1)S(1)}, bf16[256,576]{1,0:T(8,128)(2,1)S(1)}, u32[]{:S(2)}, u32[]{:S(2)}) collective-permute-start(bf16[256,576]{1,0:T(8,128)(2,1)S(1)} %get-tuple-element.147), channel_id=1, source_target_pairs={{2,0},{4,2},{6,4},{8,6},{10,8},{12,10},{14,12},{16,14},{18,16},{20... | collective-permute-start | bytes 884744 | tf_op jit(solution)/shard_map/ppermute | solution.py:407
  173.5 5.2 %copy-start.14 = (bf16[288,576]{1,0:T(8,128)(2,1)S(1)}, bf16[288,576]{1,0:T(8,128)(2,1)}, u32[]{:S(2)}) copy-start(bf16[288,576]{1,0:T(8,128)(2,1)} %expand_ref.3) | copy-start | bytes 995332
  173.5 5.2 %copy-start.16 = (f32[512,576]{1,0:T(8,128)S(1)}, f32[512,576]{1,0:T(8,128)}, u32[]{:S(2)}) copy-start(f32[512,576]{1,0:T(8,128)} %copy-done.15) | copy-start | bytes 3538948
  173.5 5.2 %copy-start.39 = (f32[2,576]{1,0:T(2,128)S(1)}, f32[2,576]{1,0:T(2,128)}, u32[]{:S(2)}) copy-start(f32[2,576]{1,0:T(2,128)} %copy-done.38) | copy-start | bytes 13828
  173.5 8.5 %copy-start.43 = (bf16[9,256,256]{2,1,0:T(8,128)(2,1)S(1)}, bf16[9,256,256]{2,1,0:T(8,128)(2,1)}, u32[]{:S(2)}) copy-start(bf16[9,256,256]{2,1,0:T(8,128)(2,1)} %copy-done.42) | copy-start | bytes 3538948
  173.5 8.5 %copy-start.45 = (bf16[9,256,256]{2,1,0:T(8,128)(2,1)S(1)}, bf16[9,256,256]{2,1,0:T(8,128)(2,1)}, u32[]{:S(2)}) copy-start(bf16[9,256,256]{2,1,0:T(8,128)(2,1)} %copy-done.44) | copy-start | bytes 3538948
  176.0 9.8 %collective-permute-start.25 = (bf16[64,4096]{1,0:T(8,128)(2,1)S(1)}, bf16[64,4096]{1,0:T(8,128)(2,1)S(1)}, u32[]{:S(2)}, u32[]{:S(2)}) collective-permute-start(bf16[64,4096]{1,0:T(8,128)(2,1)S(1)} %get-tuple-element.145), channel_id=1, source_target_pairs={{0,2},{2,0},{4,6},{6,4},{8,10},{10,8},{12,14},{14,12},{16,18},{18,... | collective-permute-start | bytes 1572872 | tf_op jit(solution)/shard_map/ppermute | solution.py:424
  178.7 3.3 %copy-start.30 = (bf16[576,288]{0,1:T(8,128)(2,1)S(1)}, bf16[576,288]{0,1:T(8,128)(2,1)}, u32[]{:S(2)}) copy-start(bf16[576,288]{0,1:T(8,128)(2,1)} %param.11) | copy-start | bytes 995332
  178.7 3.3 %copy-start.37 = (f32[2,288]{1,0:T(2,128)S(1)}, f32[2,288]{1,0:T(2,128)}, u32[]{:S(2)}) copy-start(f32[2,288]{1,0:T(2,128)} %copy-done.36) | copy-start | bytes 6916
  178.7 3.3 %copy-start.41 = (f32[512,576]{1,0:T(8,128)S(1)}, f32[512,576]{1,0:T(8,128)}, u32[]{:S(2)}) copy-start(f32[512,576]{1,0:T(8,128)} %copy-done.40) | copy-start | bytes 3538948
  178.7 3.3 %copy-start.47 = (bf16[9,192,192]{2,1,0:T(8,128)(2,1)S(1)}, bf16[9,192,192]{2,1,0:T(8,128)(2,1)}, u32[]{:S(2)}) copy-start(bf16[9,192,192]{2,1,0:T(8,128)(2,1)} %copy-done.46) | copy-start | bytes 1990660
  179.5 2.5 %collective-permute-start.27 = (f32[2,288]{1,0:T(2,128)S(1)}, f32[2,288]{1,0:T(2,128)S(1)}, u32[]{:S(2)}, u32[]{:S(2)}) collective-permute-start(f32[2,288]{1,0:T(2,128)S(1)} %shard_map.127), channel_id=1, source_target_pairs={{0,1},{1,0},{2,3},{3,2},{4,5},{5,4},{6,7},{7,6},{8,9},{9,8},{10,11... | collective-permute-start | bytes 6920 | tf_op jit(solution)/shard_map/ppermute | solution.py:432
  (15 other events, 12.2 us)

commit v7 on v6

--- a/solution.py
+++ b/solution.py
@@ -132,23 +132,17 @@
     sq_ref[...] = contract_exact(pooled, squeeze_ref[...].astype(jnp.float32))
 
 
-def hidden_kernel(
-    conv_ref, pad_ref, sq_ref, expand_ref, even_ref, odd_ref, excite_ref, active_ref, slope_ref
-):
+def hidden_kernel(conv_ref, pad_ref, sq_ref, expand_ref, even_ref, odd_ref, excite_ref):
     squeezed = sq_ref[...]
     relaxed = squeezed * jax.nn.sigmoid(squeezed)
     excite = jax.nn.sigmoid(
         jnp.dot(relaxed, expand_ref[...].astype(jnp.float32), precision=lax.Precision.HIGHEST)
     )
     excite_ref[...] = excite
-    good = inside(FRAME_ROWS)
     for frame, out_ref in enumerate((even_ref, odd_ref)):
         rows = slice(frame * FRAME_ROWS, (frame + 1) * FRAME_ROWS)
         conv = conv_ref[rows, :]
-        sigma = jax.nn.sigmoid(conv)
-        active = conv * sigma
-        active_ref[rows, :] = active
-        slope_ref[rows, :] = sigma * (1.0 + conv * (1.0 - sigma)) * good
+        active = conv * jax.nn.sigmoid(conv)
         hidden = pad_ref[rows, :].astype(jnp.float32) + active * excite[frame : frame + 1]
         out_ref[...] = hidden.astype(jnp.bfloat16)
 
@@ -232,10 +226,11 @@
     out_ref[...] = frame.astype(out_ref.dtype)
 
 
-def excite_grad_kernel(even_ref, odd_ref, active_ref, excite_ref, expand_ref, out_ref):
+def excite_grad_kernel(even_ref, odd_ref, conv_ref, excite_ref, expand_ref, out_ref):
     sums = []
     for frame, grad_ref in enumerate((even_ref, odd_ref)):
-        active = active_ref[frame * FRAME_ROWS : (frame + 1) * FRAME_ROWS, :]
+        conv = conv_ref[frame * FRAME_ROWS : (frame + 1) * FRAME_ROWS, :]
+        active = conv * jax.nn.sigmoid(conv)
         sums.append(jnp.sum(grad_ref[...].astype(jnp.float32) * active, axis=0, keepdims=True))
     excite = excite_ref[...]
     inner = jnp.concatenate(sums, axis=0) * excite * (1.0 - excite)
@@ -243,10 +238,11 @@
 
 
 def conv_grad_kernel(
-    width, even_ref, odd_ref, slope_ref, excite_ref, sq_ref, relaxed_ref, squeeze_ref, *refs
+    even_ref, odd_ref, conv_ref, excite_ref, sq_ref, relaxed_ref, squeeze_ref, group_ref,
+    out_ref, flat_ref, wide_ref, shift_ref, grad_ref,
 ):
-    *dense_refs, out_ref, flat_ref, wide_ref, shift_ref, grad_ref = refs
     frames, _, chans = out_ref.shape
+    width = group_ref.shape[1]
     rows = frames * FRAME_ROWS
     grad_squeezed = relaxed_ref[...] * silu_slope(sq_ref[...])
     pooled = jnp.dot(
@@ -254,43 +250,32 @@
     ) * (1.0 / (SIDE * SIDE))
     wide_ref[0:EDGE, :] = jnp.zeros((EDGE, chans), jnp.float32)
     wide_ref[EDGE + rows :, :] = jnp.zeros((EDGE, chans), jnp.float32)
+    good = inside(FRAME_ROWS)
     for frame, source in enumerate((even_ref, odd_ref)):
         at = frame * FRAME_ROWS
         grad = source[...].astype(jnp.float32)
         grad_ref[at : at + FRAME_ROWS, :] = grad
         active = grad * excite_ref[frame : frame + 1, :] + pooled[frame : frame + 1]
-        slope = slope_ref[at : at + FRAME_ROWS, :]
-        wide_ref[EDGE + at : EDGE + at + FRAME_ROWS, :] = active * slope
+        slope = silu_slope(conv_ref[at : at + FRAME_ROWS, :])
+        wide_ref[EDGE + at : EDGE + at + FRAME_ROWS, :] = active * slope * good
     store_shifts(wide_ref, shift_ref, -1)
     body = rows - 2 * WIDE
-    for block, dense_ref in zip(channel_blocks(chans, width), dense_refs):
+    for block in channel_blocks(chans, width):
         _, _, start, end = block
+        spread, same = block_tools(block, width)
         total = jnp.zeros((body, end - start), jnp.float32)
         for tap in range(9):
             down, across = divmod(tap, 3)
+            weights = dense_tap(group_ref, tap, block, spread, same)
             at = (2 - down) * WIDE
             source = shift_ref[across, at : at + body, start:end]
-            total += jnp.dot(source, dense_ref[tap], preferred_element_type=jnp.float32)
+            total += jnp.dot(source, weights, preferred_element_type=jnp.float32)
         grad_ref[WIDE : WIDE + body, start:end] += total
     for frame in range(frames):
         for y in range(SIDE):
             at = frame * FRAME_ROWS + (y + 1) * WIDE + 1
             flat_ref[y * SIDE : (y + 1) * SIDE, :] = grad_ref[at : at + SIDE, :]
         out_ref[frame] = flat_ref[...].astype(jnp.bfloat16)
-
-
-def dense_kernel(group_ref, *dense_refs):
-    width, chans = group_ref.shape[1:]
-    for block, dense_ref in zip(channel_blocks(chans, width), dense_refs):
-        spread, same = block_tools(block, width)
-        for tap in range(9):
-            dense_ref[tap] = dense_tap(group_ref, tap, block, spread, same)
-
-
-def dense_weights(group_kernel):
-    _, width, chans = group_kernel.shape
-    sizes = [end - start for _, _, start, end in channel_blocks(chans, width)]
-    return whole_call(dense_kernel, tuple(bf16(9, size, size) for size in sizes), [])(group_kernel)
 
 
 def f32(*shape):
@@ -319,8 +304,7 @@
     rows, chans = conv.shape
     return whole_call(
         hidden_kernel,
-        (bf16(FRAME_ROWS, chans),) * 2
-        + (f32(rows // FRAME_ROWS, chans), f32(rows, chans), f32(rows, chans)),
+        (bf16(FRAME_ROWS, chans), bf16(FRAME_ROWS, chans), f32(rows // FRAME_ROWS, chans)),
         [],
     )(conv, padded, squeezed, squeeze_out)
 
@@ -376,20 +360,20 @@
     )(facts, own, mate)
 
 
-def excite_grad(even, odd, active, excite, squeeze_out):
-    rows, chans = active.shape
+def excite_grad(even, odd, conv, excite, squeeze_out):
+    rows, chans = conv.shape
     return whole_call(
         excite_grad_kernel,
         f32(rows // FRAME_ROWS, squeeze_out.shape[0]),
         [],
-    )(even, odd, active, excite, squeeze_out)
-
-
-def conv_backward(even, odd, slope, excite, squeezed, grad_relaxed, squeeze_in, dense, width):
-    rows, chans = slope.shape
+    )(even, odd, conv, excite, squeeze_out)
+
+
+def conv_backward(even, odd, conv, excite, squeezed, grad_relaxed, squeeze_in, group_kernel):
+    rows, chans = conv.shape
     frames = rows // FRAME_ROWS
     return whole_call(
-        functools.partial(conv_grad_kernel, width),
+        conv_grad_kernel,
         bf16(frames, SIDE * SIDE, chans),
         [
             pltpu.VMEM((SIDE * SIDE, chans), jnp.float32),
@@ -398,7 +382,7 @@
             pltpu.VMEM((rows, chans), jnp.float32),
         ],
         pl.CostEstimate(flops=rows * chans * 9216, bytes_accessed=16 * rows * chans, transcendentals=0),
-    )(even, odd, slope, excite, squeezed, grad_relaxed, squeeze_in, *dense)
+    )(even, odd, conv, excite, squeezed, grad_relaxed, squeeze_in, group_kernel)
 
 
 def shifted(value, axis, by):
@@ -466,25 +450,28 @@
     return (token < jnp.where(block == 0, facts_ref[1], facts_ref[2])).astype(jnp.float32)
 
 
-def totals_kernel(pieces, unit, lanes, first, facts_ref, *refs):
+def totals_kernel(pieces, unit, parts, first, facts_ref, *refs):
     grad_act = refs[0][...] + refs[1][...]
     count = len(pieces)
     slopes, blocks = refs[2:4], refs[4 : 4 + count]
-    before, after = refs[4 + count : -2], refs[-2:]
+    before, after = refs[4 + count : -2 * len(parts)], refs[-2 * len(parts) :]
     rows, width = grad_act.shape[0], blocks[0].shape[0]
     matrix = reorder_matrix(facts_ref[0], unit, False)
-    total = 0.0
-    for place, ((source, index), ref) in enumerate(zip(pieces, blocks)):
+    factors = []
+    for place, (source, index) in enumerate(pieces):
         piece = grad_act[:, place * width : (place + 1) * width]
         piece = piece * slopes[source][:, index * width : (index + 1) * width]
-        piece = jnp.dot(
-            matrix, piece.astype(jnp.bfloat16), preferred_element_type=jnp.float32
-        ).astype(jnp.bfloat16)
-        total += jnp.dot(piece, ref[:, lanes], preferred_element_type=jnp.float32)
-    for half, ref in enumerate(after):
-        value = total[half * rows // 2 : (half + 1) * rows // 2]
-        value = value if first else before[half][...] + value
-        ref[...] = value.astype(ref.dtype)
+        piece = jnp.dot(matrix, piece.astype(jnp.bfloat16), preferred_element_type=jnp.float32)
+        factors.append(piece.astype(jnp.bfloat16))
+    for part, lanes in enumerate(parts):
+        total = 0.0
+        for factor, ref in zip(factors, blocks):
+            total += jnp.dot(factor, ref[:, lanes], preferred_element_type=jnp.float32)
+        for half in range(2):
+            value = total[half * rows // 2 : (half + 1) * rows // 2]
+            value = value if first else before[2 * part + half][...] + value
+            ref = after[2 * part + half]
+            ref[...] = value.astype(ref.dtype)
 
 
 def ring_offsets(chips):
@@ -565,11 +552,14 @@
     )(facts, *operands)
 
 
-def add_gradients(facts, terms, slopes, pieces, blocks, before, unit, lanes, last):
-    rows, columns = terms[0].shape[0] // 2, lanes.stop - lanes.start
-    kernel = functools.partial(totals_kernel, pieces, unit, lanes, not before)
-    outs = f32(rows, columns), (bf16 if last else f32)(rows, columns)
-    return facts_call(kernel, outs, facts, (*terms, *slopes, *blocks, *before))
+def add_gradients(facts, terms, slopes, pieces, blocks, before, unit, parts, last):
+    rows = terms[0].shape[0] // 2
+    kernel = functools.partial(totals_kernel, pieces, unit, parts, not before)
+    outs = ()
+    for lanes in parts:
+        shape = rows, lanes.stop - lanes.start
+        outs += f32(*shape), (bf16 if last else f32)(*shape)
+    return tuple(facts_call(kernel, outs, facts, (*terms, *slopes, *blocks, *before)))
 
 
 def act_and_slope(facts, terms, offsets, chips, before, unit):
@@ -610,12 +600,12 @@
     clip_keep,
     token_cotangent,
 ):
-    chans, width = features.shape[2], group_kernel.shape[2]
+    chans = features.shape[2]
     count = lax.axis_size("ctx")
     steps, unit = count // 4, OUT_SIDE * OUT_SIDE // count
     flat_sampler = sampler_kernel.reshape(sampler_kernel.shape[0], 8 * chans)
     chips = count // 2
-    s_up, s_down = [ring_send(flat_sampler, 1)], [ring_send(flat_sampler, -1)]
+    s_up, s_down = ring_send(flat_sampler, 1), ring_send(flat_sampler, -1)
     group_kernel = jnp.swapaxes(group_kernel, 1, 2)
     squeeze_in = squeeze_in.T
     facts = facts_of(frame_clip, clip_keep)
@@ -624,93 +614,88 @@
     token_cotangent, squeezed = tie(token_cotangent, squeezed)
     back = chips_exchange(token_cotangent)
     squeezed = sum_tp(squeezed)
-    even, odd, excite, active, slope = hidden_frames(conv, padded, squeezed, squeeze_out)
+    even, odd, excite = hidden_frames(conv, padded, squeezed, squeeze_out)
     halo = shifted(odd, "ctx", 1)
 
-    s_up[0], s_down[0], even = tie(s_up[0], s_down[0], even)
-    for step in range(1, steps - 1):
+    s_up, s_down = [flat_sampler, s_up], [flat_sampler, s_down]
+    s_up[1], s_down[1], even = tie(s_up[1], s_down[1], even)
+    for step in range(2, steps):
         s_up.append(ring_send(s_up[-1], 1))
         s_down.append(ring_send(s_down[-1], -1))
-        if step == 1:
-            halo, s_up[1], s_down[1] = tie(halo, s_up[1], s_down[1])
+        if step == 2:
+            halo, s_up[2], s_down[2] = tie(halo, s_up[2], s_down[2])
             patches = take_patches(facts, halo, even)
             patches = order_rows(facts, patches, swap_cores(patches), unit)
-            back = (back, swap_cores(back))
-    s_up[-1], s_down[-1], readout_kernel = tie(s_up[-1], s_down[-1], readout_kernel)
+    s_up[-1], s_down[-1], readout_kernel, back = tie(s_up[-1], s_down[-1], readout_kernel, back)
+    back = (back, swap_cores(back))
     s_last = ring_send(s_up[-1], 1)
-    r_up, r_down = [ring_send(readout_kernel, 1)], [ring_send(readout_kernel, -1)]
-    samplers = [flat_sampler] + [block for pair in zip(s_up, s_down) for block in pair]
+    samplers = [flat_sampler] + [block for pair in zip(s_up[1:], s_down[1:]) for block in pair]
     offsets = ring_offsets(chips)
     first_pre = block_products(pre_kernel, (patches,), samplers)
-    r_up[0], r_down[0], first_pre = tie(r_up[0], r_down[0], first_pre)
-    for step in range(1, steps - 2):
-        r_up.append(ring_send(r_up[-1], 1))
-        r_down.append(ring_send(r_down[-1], -1))
-    first_slope, first_act = act_and_slope(
-        facts, tp_terms(first_pre), offsets[:-1], chips, (), unit
-    )
+    r_down = [readout_kernel, ring_send(readout_kernel, -1)]
+    readout_kernel, first_pre = tie(readout_kernel, first_pre)
+    r_up = [readout_kernel, ring_send(readout_kernel, 1)]
+    first_pre = tp_terms(first_pre)
+    r_down[1], s_last, *first_pre = tie(r_down[1], s_last, *first_pre)
+    r_down.append(ring_send(r_down[1], -1))
+    sums = block_products(back_kernel, back, [r_up[0], r_down[1]])
+    first_slope, first_act = act_and_slope(facts, first_pre, offsets[:-1], chips, (), unit)
     last_pre = tp_terms(block_products(pre_kernel, (patches,), [s_last]))
     last_slope, act = act_and_slope(facts, last_pre, offsets[-1:], chips, (first_act,), unit)
     slopes = first_slope, last_slope
-
-    early = [readout_kernel]
-    for step in range(steps - 3):
-        early += [r_up[step], r_down[step]]
-    early_sums = block_products(back_kernel, back, early)
-    r_up[-1], early_sums = tie(r_up[-1], early_sums)
-    r_up.append(ring_send(r_up[-1], 1))
-    r_down.append(ring_send(r_down[-1], -1))
+    r_up[1], sums, act = tie(r_up[1], sums, act)
+    r_up.append(ring_send(r_up[1], 1))
+    act = chips_exchange(act)
     halo_lanes, even_lanes = slice(0, 4 * chans), slice(4 * chans, 8 * chans)
-    index = len(early)
-    *middle, act = tie(r_up[steps - 3], r_down[steps - 3], r_down[steps - 2], act)
-    act = chips_exchange(act)
-    pieces = [(0, place) for place in range(index)]
-    terms = tp_terms(early_sums)
-    halo_grads = add_gradients(
-        facts, terms, slopes, pieces, samplers[:index], (), unit, halo_lanes, False
-    )
-    even_grads = add_gradients(
-        facts, terms, slopes, pieces, samplers[:index], (), unit, even_lanes, False
-    )
-    r_last = ring_send(r_down[-1], -1)
-    held = tie(group_kernel, *middle, *halo_grads, *even_grads)
-    group_kernel, middle, halo_grads, even_grads = held[0], held[1:4], held[4:6], held[6:]
-    dense = dense_weights(group_kernel)
-    pieces = [(0, index), (0, index + 1), (0, index + 3)]
-    blocks = [samplers[index], samplers[index + 1], samplers[index + 3]]
-    terms = tp_terms(block_products(back_kernel, back, middle))
-    halo_grads = add_gradients(
-        facts, terms, slopes, pieces, blocks, halo_grads, unit, halo_lanes, False
-    )
-    even_grads = add_gradients(
-        facts, terms, slopes, pieces, blocks, even_grads, unit, even_lanes, False
-    )
-    places = offsets[: index + 2] + [offsets[index + 3]]
-    tokens = add_tokens(facts, act, places, chips, early + list(middle), (), unit)
-
-    held = tie(r_up[-1], r_last, *halo_grads, *even_grads, *dense, *tokens)
-    late, halo_grads, even_grads = held[:2], held[2:4], held[4:6]
-    dense, tokens = held[6:-2], held[-2:]
-    pieces, blocks = [(0, index + 2), (1, 0)], [samplers[index + 2], s_last]
+    grads = ()
+    terms = tp_terms(sums)
+    pieces, blocks = [(0, 0), (0, 2)], [samplers[0], samplers[2]]
+    for step in range(2, steps):
+        r_down[step], *terms = tie(r_down[step], *terms)
+        r_down.append(ring_send(r_down[step], -1))
+        sums = block_products(back_kernel, back, [r_up[step - 1], r_down[step]])
+        grads = add_gradients(
+            facts, terms, slopes, pieces, blocks, grads, unit, (halo_lanes, even_lanes), False
+        )
+        if step < steps - 1:
+            r_up[step], sums, *grads = tie(r_up[step], sums, *grads)
+            r_up.append(ring_send(r_up[step], 1))
+        terms = tp_terms(sums)
+        pieces = [(0, 2 * step - 3), (0, 2 * step)]
+        blocks = [samplers[2 * step - 3], samplers[2 * step]]
+    grads = add_gradients(
+        facts, terms, slopes, pieces, blocks, grads, unit, (halo_lanes, even_lanes), False
+    )
+    places, blocks = [0], [r_up[0]]
+    for step in range(1, steps):
+        places, blocks = places + [step], blocks + [r_down[step]]
+        if step < steps - 1:
+            places, blocks = places + [-step], blocks + [r_up[step]]
+    tokens = add_tokens(facts, act, places, chips, blocks, (), unit)
+
+    held = tie(r_up[-1], r_down[-1], *grads, *tokens)
+    late, grads, tokens = held[:2], held[2:6], held[6:]
     terms = tp_terms(block_products(back_kernel, back, late))
+    pieces, blocks = [(0, 2 * steps - 3), (1, 0)], [samplers[2 * steps - 3], s_last]
     halo_own, halo_mate = add_gradients(
-        facts, terms, slopes, pieces, blocks, halo_grads, unit, halo_lanes, True
+        facts, terms, slopes, pieces, blocks, grads[:2], unit, (halo_lanes,), True
     )
     halo_mate, first_term = tie(halo_mate, terms[0])
     even_own, even_mate = add_gradients(
-        facts, (first_term, terms[1]), slopes, pieces, blocks, even_grads, unit, even_lanes, True
+        facts, (first_term, terms[1]), slopes, pieces, blocks, grads[2:], unit, (even_lanes,), True
     )
     lead, facts_late = return_patches(facts, halo_own, swap_cores(halo_mate), chans, jnp.bfloat16)
     grad_odd = shifted(lead, "ctx", -1)
     grad_even, facts_late = return_patches(
         facts_late, even_own, swap_cores(even_mate), chans, jnp.float32
     )
-    grad_relaxed = sum_tp(excite_grad(grad_even, grad_odd, active, excite, squeeze_out))
-    places = [offsets[index + 2], offsets[-1]]
-    tokens, send = add_tokens(facts_late, act, places, chips, late, tokens, unit)
+    grad_relaxed = sum_tp(excite_grad(grad_even, grad_odd, conv, excite, squeeze_out))
+    tokens, send = add_tokens(
+        facts_late, act, [1 - steps, steps], chips, late, tokens, unit
+    )
     llm_tokens = (tokens + swap_cores(send).astype(jnp.float32)).astype(jnp.bfloat16)
     grad_features = conv_backward(
-        grad_even, grad_odd, slope, excite, squeezed, grad_relaxed, squeeze_in, dense, width
+        grad_even, grad_odd, conv, excite, squeezed, grad_relaxed, squeeze_in, group_kernel
     )
     return (llm_tokens, grad_features)
 

time: 187 us -> 177 us (0.947)
  local copies, waits for them, and re-layouts: 20.6 us -> 11.8 us
  waiting for transfers between devices: 66.7 us -> 64.5 us
    ppermute x14, waiting for transfers between devices: 38.6 us -> 27.7 us  [ring_send(): return lax.ppermute(value, 'ctx', ring_pairs(lax.axis_size('ctx'), by))]
    unnamed x100 -> x78, local copies, waits for them, and re-layouts: 18.8 us -> 10.1 us
    ppermute x7 -> x8, waiting for transfers between devices: 10.8 us -> 18.4 us  [tp_terms(): other = lax.ppermute(value, 'tp', [(i, i ^ reach) for i in range(size)])]
    all_to_all x2, waiting for transfers between devices: 0.01 us -> 5.75 us  [chips_exchange(): lax.all_to_all(value, 'ctx', split_axis=0, concat_axis=0, tiled=True, axi...]
    ppermute x2, waiting for transfers between devices: 15.7 us -> 12.6 us  [shifted(): return lax.ppermute(value, axis, pairs)]
    ppermute x7 -> x8, starting transfers between devices: 7.41 us -> 10.2 us  [tp_terms(): other = lax.ppermute(value, 'tp', [(i, i ^ reach) for i in range(size)])]
    pallas_call x10 -> x9, Pallas kernels: 20 us -> 17.9 us  [facts_call(): pl.pallas_call(kernel, out_shape=outs, in_specs=vmem_specs(len(operands))...]
    ppermute x5, starting transfers between devices: 9.98 us -> 8 us  [swap_cores(): lax.ppermute(value, 'ctx', [(i, i ^ 1) for i in range(lax.axis_size('ctx'...]
  transfers between devices with their start and end apart: 30 -> 31, of which waited for: 14 -> 17; matrix products, arithmetic and copies ran while one was open for 1% -> 1% of each run, Pallas kernels for 24% -> 25%
where the time goes in v7:
time: 177 us; the launch traced here: 176 us
  waiting for transfers between devices  64.5 us (36%)
  starting transfers between devices  49.8 us (28%)
  Pallas kernels  47.7 us (27%)
  local copies, waits for them, and re-layouts  11.8 us (7%)
    ppermute x14, waiting for transfers between devices, ring_send(): return lax.ppermute(value, 'ctx', ring_pairs(lax.axis_size('ctx'), by))  27.7 us
    ppermute x8, waiting for transfers between devices, tp_terms(): other = lax.ppermute(value, 'tp', [(i, i ^ reach) for i in range(size)])  18.4 us
    pallas_call x9, Pallas kernels, facts_call(): pl.pallas_call(kernel, out_shape=outs, in_specs=vmem_specs(len(operands))...  17.9 us
    ppermute x14, starting transfers between devices, ring_send(): return lax.ppermute(value, 'ctx', ring_pairs(lax.axis_size('ctx'), by))  15.9 us
    ppermute x2, waiting for transfers between devices, shifted(): return lax.ppermute(value, axis, pairs)  12.6 us
    pallas_call x6, Pallas kernels, block_products(): whole_call(kernel, f32(rows, len(blocks) * blocks[0].shape[0]), [])  10.3 us
    ppermute x8, starting transfers between devices, tp_terms(): other = lax.ppermute(value, 'tp', [(i, i ^ reach) for i in range(size)])  10.2 us
    unnamed x78, local copies, waits for them, and re-layouts  10.1 us
  transfers between devices with their start and end apart: 31, of which 17 were waited for; matrix products, arithmetic and copies ran while one was open for 1% of the time, Pallas kernels for 25%

profile of v7, /device:TPU:3, one launch (start us, length us, event | category | flops | bytes accessed | tf_op | source)
XLA Modules:
  0.0 175.8 jit_solution(5333736269899269107)
XLA Ops:
  0.6 1.7 reshape.11.refs_0_.refs_4_
  2.4 1.3 collective-permute-start.3
  3.9 1.1 copy.11.feat_ref
  5.0 4.5 %shard_map.105 = (f32[512,576]{1,0:T(8,128)S(1)}, bf16[512,576]{1,0:T(8,128)(2,1)S(1)}, f32[2,288]{1,0:T(2,128)S(1)}) custom-call(bf16[2,196,576]{2,1,0:T(8,128)(2,1)S(1)} %copy.11.feat_ref, bf16[9,48,576]{2,1,0:T(8,128)(2,1)S(1)} %bitcast.13, bf16[288,576]{1,0:T(8,128)(2,1)S(1)} %bitcast.15), custom_call_target="tpu_custom_call" | custom-call | tf_op jit(solution)/shard_map/pallas_call | solution.py:292
  9.5 1.3 collective-permute-start
  10.8 1.5 collective-permute-done
  12.3 1.5 shard_map.106
  13.8 4.4 %collective-permute-done.3.refs_2_.refs_5_ = bf16[72,4608]{1,0:T(8,128)(2,1)S(1)} collective-permute-done((bf16[72,4608]{1,0:T(8,128)(2,1)S(1)}, bf16[72,4608]{1,0:T(8,128)(2,1)S(1)}, u32[]{:S(2)}, u32[]{:S(2)}) %collective-permute-start.3) | collective-permute-done | bytes 663584 | tf_op jit(solution)/shard_map/ppermute | solution.py:427
  18.2 1.0 collective-permute-done.2.refs_1_.refs_4_
  19.4 1.3 collective-permute-start.5
  20.7 4.2 %collective-permute-start.1 = (bf16[256,576]{1,0:T(8,128)(2,1)}, bf16[256,576]{1,0:T(8,128)(2,1)}, u32[]{:S(2)}, u32[]{:S(2)}) collective-permute-start(bf16[256,576]{1,0:T(8,128)(2,1)} %get-tuple-element.83), channel_id=1, source_target_pairs={{0,2},{2,4},{4,6},{6,8},{8,10},{10,12},{12,14},{14,16},{16,18},{18... | collective-permute-start | bytes 884744 | tf_op jit(solution)/shard_map/ppermute | solution.py:391
  24.9 5.0 %all-to-all-start = ((bf16[8,8,4096]{2,1,0:T(8,128)(2,1)}), bf16[8,8,4096]{2,1,0:T(8,128)(2,1)S(1)}, u32[]{:S(2)}, u32[]{:S(2)}) async-start(bf16[8,8,4096]{2,1,0:T(8,128)(2,1)} %bitcast.17), calls=%async_computation | async-start | bytes 1048576 | tf_op jit(solution)/shard_map/all_to_all | solution.py:587
  29.9 9.9 %collective-permute-done.1.halo_ref = bf16[256,576]{1,0:T(8,128)(2,1)} collective-permute-done((bf16[256,576]{1,0:T(8,128)(2,1)}, bf16[256,576]{1,0:T(8,128)(2,1)}, u32[]{:S(2)}, u32[]{:S(2)}) %collective-permute-start.1) | collective-permute-done | bytes 294944 | tf_op jit(solution)/shard_map/ppermute | solution.py:391
  39.9 3.5 %collective-permute-start.6 = (bf16[72,4608]{1,0:T(8,128)(2,1)S(1)}, bf16[72,4608]{1,0:T(8,128)(2,1)S(1)}, u32[]{:S(2)}, u32[]{:S(2)}) collective-permute-start(bf16[72,4608]{1,0:T(8,128)(2,1)S(1)} %collective-permute-done.4.refs_3_.refs_4_), channel_id=1, source_target_pairs={{0,8},{2,10},{8,16},{10,18},{16,24},{18,26},{24,28},{26,30},{28,20... | collective-permute-start | bytes 1990664 | tf_op jit(solution)/shard_map/ppermute | solution.py:427
  43.6 1.3 shard_map.104.facts_ref
  45.6 2.2 %shard_map.107.own_ref = bf16[64,4608]{1,0:T(8,128)(2,1)} custom-call(s32[5]{0:T(128)S(1)} %copy-done.35, bf16[256,576]{1,0:T(8,128)(2,1)} %collective-permute-done.1.halo_ref, bf16[256,576]{1,0:T(8,128)(2,1)S(1)} %get-tuple-element.93.even_ref), custom_call_target="tpu_custom_call" | custom-call | tf_op jit(solution)/shard_map/pallas_call | solution.py:340
  47.8 3.0 %collective-permute-start.9 = (bf16[64,4608]{1,0:T(8,128)(2,1)}, bf16[64,4608]{1,0:T(8,128)(2,1)}, u32[]{:S(2)}, u32[]{:S(2)}) collective-permute-start(bf16[64,4608]{1,0:T(8,128)(2,1)} %shard_map.107.own_ref), channel_id=1, source_target_pairs={{0,2},{2,0},{4,6},{6,4},{8,10},{10,8},{12,14},{14,12},{16,18},{18,... | collective-permute-start | bytes 1769480 | tf_op jit(solution)/shard_map/ppermute | solution.py:408
  50.8 7.5 %collective-permute-done.6.refs_5_.refs_4_ = bf16[72,4608]{1,0:T(8,128)(2,1)S(1)} collective-permute-done((bf16[72,4608]{1,0:T(8,128)(2,1)S(1)}, bf16[72,4608]{1,0:T(8,128)(2,1)S(1)}, u32[]{:S(2)}, u32[]{:S(2)}) %collective-permute-start.6) | collective-permute-done | bytes 663584 | tf_op jit(solution)/shard_map/ppermute | solution.py:427
  58.3 3.2 %collective-permute-done.7.refs_6_.refs_5_ = bf16[72,4608]{1,0:T(8,128)(2,1)} collective-permute-done((bf16[72,4608]{1,0:T(8,128)(2,1)}, bf16[72,4608]{1,0:T(8,128)(2,1)}, u32[]{:S(2)}, u32[]{:S(2)}) %collective-permute-start.7) | collective-permute-done | bytes 663584 | tf_op jit(solution)/shard_map/ppermute | solution.py:427
  61.5 4.3 %collective-permute-start.11 = (bf16[72,4096]{1,0:T(8,128)(2,1)}, bf16[72,4096]{1,0:T(8,128)(2,1)S(1)}, u32[]{:S(2)}, u32[]{:S(2)}) collective-permute-start(bf16[72,4096]{1,0:T(8,128)(2,1)} %refs_0_.1), channel_id=1, source_target_pairs={{0,4},{2,6},{8,0},{10,2},{16,8},{18,10},{24,16},{26,18},{28,24},{3... | collective-permute-start | bytes 1769480 | tf_op jit(solution)/shard_map/ppermute | solution.py:427
  66.4 1.7 shard_map.108.patch_ref
  68.2 3.7 %shard_map.109.own_ref = f32[128,504]{1,0:T(8,128)S(1)} custom-call(bf16[128,4608]{1,0:T(8,128)(2,1)S(1)} %shard_map.108.patch_ref, bf16[72,4608]{1,0:T(8,128)(2,1)S(1)} %reshape.11.refs_0_.refs_4_, bf16[72,4608]{1,0:T(8,128)(2,1)S(1)} %collective-permute-done.2.refs_1_.refs_4_, bf16[72,4608]{1,0:T(8,128)(2,1)S(1)} %copy-done.8, ...), custom_call_target="tpu_custom_call" | custom-call | tf_op jit(solution)/shard_map/pallas_call | solution.py:542
  71.9 1.3 collective-permute-start.13
  73.3 6.7 %collective-permute-done.13.other_ref = f32[128,504]{1,0:T(8,128)S(1)} collective-permute-done((f32[128,504]{1,0:T(8,128)S(1)}, f32[128,504]{1,0:T(8,128)S(1)}, u32[]{:S(2)}, u32[]{:S(2)}) %collective-permute-start.13) | collective-permute-done | bytes 258080 | tf_op jit(solution)/shard_map/ppermute | solution.py:416
  80.0 1.2 collective-permute-done.12.refs_0_.refs_5_
  81.2 1.9 %collective-permute-start.16 = (bf16[72,4096]{1,0:T(8,128)(2,1)S(1)}, bf16[72,4096]{1,0:T(8,128)(2,1)S(1)}, u32[]{:S(2)}, u32[]{:S(2)}) collective-permute-start(bf16[72,4096]{1,0:T(8,128)(2,1)S(1)} %collective-permute-done.11.refs_1_), channel_id=1, source_target_pairs={{0,4},{2,6},{8,0},{10,2},{16,8},{18,10},{24,16},{26,18},{28,24},{3... | collective-permute-start | bytes 1769480 | tf_op jit(solution)/shard_map/ppermute | solution.py:427
  83.5 1.3 collective-permute-start.14
  84.9 1.1 shard_map.112
  87.0 1.6 shard_map.113
  88.6 5.0 %collective-permute-done.10.refs_0_.refs_2_ = bf16[72,4096]{1,0:T(8,128)(2,1)S(1)} collective-permute-done((bf16[72,4096]{1,0:T(8,128)(2,1)S(1)}, bf16[72,4096]{1,0:T(8,128)(2,1)S(1)}, u32[]{:S(2)}, u32[]{:S(2)}) %collective-permute-start.10) | collective-permute-done | bytes 589856 | tf_op jit(solution)/shard_map/ppermute | solution.py:427
  93.6 1.2 collective-permute-start.17
  94.8 3.8 %collective-permute-done.17.refs_1_ = f32[128,144]{1,0:T(8,128)S(1)} collective-permute-done((f32[128,144]{1,0:T(8,128)S(1)}, f32[128,144]{1,0:T(8,128)S(1)}, u32[]{:S(2)}, u32[]{:S(2)}) %collective-permute-start.17) | collective-permute-done | bytes 73760 | tf_op jit(solution)/shard_map/ppermute | solution.py:416
  98.7 1.8 %collective-permute-start.19 = (bf16[72,4096]{1,0:T(8,128)(2,1)S(1)}, bf16[72,4096]{1,0:T(8,128)(2,1)}, u32[]{:S(2)}, u32[]{:S(2)}) collective-permute-start(bf16[72,4096]{1,0:T(8,128)(2,1)S(1)} %collective-permute-done.16.refs_1_.refs_3_), channel_id=1, source_target_pairs={{0,4},{2,6},{8,0},{10,2},{16,8},{18,10},{24,16},{26,18},{28,24},{3... | collective-permute-start | bytes 1769480 | tf_op jit(solution)/shard_map/ppermute | solution.py:427
  100.5 1.6 shard_map.115
  103.8 5.4 %collective-permute-done.15.refs_0_.refs_4_ = bf16[72,4096]{1,0:T(8,128)(2,1)} collective-permute-done((bf16[72,4096]{1,0:T(8,128)(2,1)S(1)}, bf16[72,4096]{1,0:T(8,128)(2,1)}, u32[]{:S(2)}, u32[]{:S(2)}) %collective-permute-start.15) | collective-permute-done | bytes 589856 | tf_op jit(solution)/shard_map/ppermute | solution.py:427
  109.2 1.2 collective-permute-start.20
  111.1 2.3 %collective-permute-done.20.refs_1_ = f32[128,144]{1,0:T(8,128)S(1)} collective-permute-done((f32[128,144]{1,0:T(8,128)S(1)}, f32[128,144]{1,0:T(8,128)S(1)}, u32[]{:S(2)}, u32[]{:S(2)}) %collective-permute-start.20) | collective-permute-done | bytes 73760 | tf_op jit(solution)/shard_map/ppermute | solution.py:416
  114.1 1.1 collective-permute-start.21
  115.2 3.8 %all-to-all-start.1 = ((bf16[8,16,576]{2,1,0:T(8,128)(2,1)}), bf16[8,16,576]{2,1,0:T(8,128)(2,1)S(1)}, u32[]{:S(2)}, u32[]{:S(2)}) async-start(bf16[8,16,576]{2,1,0:T(8,128)(2,1)} %bitcast.4), calls=%async_computation.1 | async-start | bytes 327680 | tf_op jit(solution)/shard_map/all_to_all | solution.py:587
  119.0 2.7 %shard_map.116.refs_0_ = f32[128,144]{1,0:T(8,128)} custom-call(bf16[64,4096]{1,0:T(8,128)(2,1)S(1)} %bitcast.9, bf16[64,4096]{1,0:T(8,128)(2,1)S(1)} %collective-permute-done.8.send_ref, bf16[72,4096]{1,0:T(8,128)(2,1)} %collective-permute-done.15.refs_0_.refs_4_, bf16[72,4096]{1,0:T(8,128)(2,1)} %collective-permute-done.19.refs_1_.refs_5_), custom_call_target="tpu_custom_call" | custom-call | tf_op jit(solution)/shard_map/pallas_call | solution.py:542
  121.7 1.2 collective-permute-start.22
  122.9 5.7 %all-to-all-done.1 = bf16[8,16,576]{2,1,0:T(8,128)(2,1)S(1)} async-done(((bf16[8,16,576]{2,1,0:T(8,128)(2,1)}), bf16[8,16,576]{2,1,0:T(8,128)(2,1)S(1)}, u32[]{:S(2)}, u32[]{:S(2)}) %all-to-all-start.1) | async-done | bytes 147488 | tf_op jit(solution)/shard_map/all_to_all | solution.py:587
  128.7 1.1 copy-done.10
  129.7 1.1 copy-done.12
  130.8 1.1 copy-done.14
  131.9 1.1 copy-done.16
  133.0 4.2 %shard_map.119 = (f32[64,4096]{1,0:T(8,128)S(1)}, f32[64,4096]{1,0:T(8,128)S(1)}) custom-call(s32[5]{0:T(128)S(1)} %copy-done.37, bf16[128,576]{1,0:T(8,128)(2,1)S(1)} %bitcast.11, bf16[72,4096]{1,0:T(8,128)(2,1)S(1)} %copy-done.10, bf16[72,4096]{1,0:T(8,128)(2,1)S(1)} %copy-done.12, bf16[72,4096]{1,0:T(8,128)(2,1)S(1)} %copy-done.14, ...), custom_call_target="tpu_custom_call" | custom-call | tf_op jit(solution)/shard_map/pallas_call | solution.py:546
  137.3 2.2 %shard_map.117 = (f32[64,2304]{1,0:T(8,128)S(1)}, f32[64,2304]{1,0:T(8,128)S(1)}, f32[64,2304]{1,0:T(8,128)S(1)}, f32[64,2304]{1,0:T(8,128)S(1)}) custom-call(s32[5]{0:T(128)S(1)} %copy-done.37, f32[128,144]{1,0:T(8,128)S(1)} %copy-done.30, f32[128,144]{1,0:T(8,128)S(1)} %copy-done.34, f32[128,504]{1,0:T(8,128)S(1)} %get-tuple-element.109.refs_2_, ...), custom_call_target="tpu_custom_call" | custom-call | tf_op jit(solution)/shard_map/pallas_call | solution.py:546
  139.5 2.3 %shard_map.118 = (f32[64,2304]{1,0:T(8,128)S(1)}, f32[64,2304]{1,0:T(8,128)S(1)}, f32[64,2304]{1,0:T(8,128)S(1)}, f32[64,2304]{1,0:T(8,128)S(1)}) custom-call(s32[5]{0:T(128)S(1)} %copy-done.37, f32[128,144]{1,0:T(8,128)} %shard_map.116.refs_0_, f32[128,144]{1,0:T(8,128)} %collective-permute-done.22.refs_1_, f32[128,504]{1,0:T(8,128)S(1)} %get-tuple-element.109.refs_2_, ...), custom_call_target="tpu_custom_call" | custom-call | tf_op jit(solution)/shard_map/pallas_call | solution.py:546
  141.8 2.0 %shard_map.120.refs_0_ = f32[128,144]{1,0:T(8,128)S(1)} custom-call(bf16[64,4096]{1,0:T(8,128)(2,1)S(1)} %bitcast.10, bf16[64,4096]{1,0:T(8,128)(2,1)S(1)} %collective-permute-done.8.send_ref, bf16[72,4096]{1,0:T(8,128)(2,1)} %collective-permute-done.18.refs_0_, bf16[72,4096]{1,0:T(8,128)(2,1)} %collective-permute-done.21.refs_1_), custom_call_target="tpu_custom_call" | custom-call | tf_op jit(solution)/shard_map/pallas_call | solution.py:542
  143.8 1.3 collective-permute-start.23
  145.1 2.6 %collective-permute-done.23.refs_1_ = f32[128,144]{1,0:T(8,128)S(1)} collective-permute-done((f32[128,144]{1,0:T(8,128)S(1)}, f32[128,144]{1,0:T(8,128)S(1)}, u32[]{:S(2)}, u32[]{:S(2)}) %collective-permute-start.23) | collective-permute-done | bytes 73760 | tf_op jit(solution)/shard_map/ppermute | solution.py:416
  147.7 1.2 shard_map.121
  148.9 4.3 %collective-permute-start.24 = (bf16[64,2304]{1,0:T(8,128)(2,1)S(1)}, bf16[64,2304]{1,0:T(8,128)(2,1)S(1)}, u32[]{:S(2)}, u32[]{:S(2)}) collective-permute-start(bf16[64,2304]{1,0:T(8,128)(2,1)S(1)} %get-tuple-element.141), channel_id=1, source_target_pairs={{0,2},{2,0},{4,6},{6,4},{8,10},{10,8},{12,14},{14,12},{16,18},{18,... | collective-permute-start | bytes 884744 | tf_op jit(solution)/shard_map/ppermute | solution.py:408
  153.3 1.3 shard_map.123
  154.6 1.5 shard_map.122
  156.1 2.6 %collective-permute-start.27 = (bf16[256,576]{1,0:T(8,128)(2,1)S(1)}, bf16[256,576]{1,0:T(8,128)(2,1)S(1)}, u32[]{:S(2)}, u32[]{:S(2)}) collective-permute-start(bf16[256,576]{1,0:T(8,128)(2,1)S(1)} %get-tuple-element.154), channel_id=1, source_target_pairs={{2,0},{4,2},{6,4},{8,6},{10,8},{12,10},{14,12},{16,14},{18,16},{20... | collective-permute-start | bytes 884744 | tf_op jit(solution)/shard_map/ppermute | solution.py:391
  158.7 1.5 shard_map.124
  160.2 2.4 %shard_map.125 = (f32[64,4096]{1,0:T(8,128)S(1)}, bf16[64,4096]{1,0:T(8,128)(2,1)S(1)}) custom-call(s32[5]{0:T(128)S(1)} %get-tuple-element.148.facts_ref, bf16[128,576]{1,0:T(8,128)(2,1)S(1)} %bitcast.12, bf16[72,4096]{1,0:T(8,128)(2,1)} %collective-permute-done.18.refs_0_, bf16[72,4096]{1,0:T(8,128)(2,1)} %collective-permute-done.21.refs_1_, ...), custom_call_target="tpu_custom_call" | custom-call | flops 3019898880 | tf_op jit(solution)/shard_map/pallas_call | solution.py:546
  163.2 2.7 %collective-permute-done.27.odd_ref = bf16[256,576]{1,0:T(8,128)(2,1)S(1)} collective-permute-done((bf16[256,576]{1,0:T(8,128)(2,1)S(1)}, bf16[256,576]{1,0:T(8,128)(2,1)S(1)}, u32[]{:S(2)}, u32[]{:S(2)}) %collective-permute-start.27) | collective-permute-done | bytes 294944 | tf_op jit(solution)/shard_map/ppermute | solution.py:391
  166.7 1.3 collective-permute-start.28
  168.0 1.2 collective-permute-done.28
  169.2 4.5 %shard_map.127 = bf16[2,196,576]{2,1,0:T(8,128)(2,1)S(1)} custom-call(f32[256,576]{1,0:T(8,128)S(1)} %get-tuple-element.153.even_ref, bf16[256,576]{1,0:T(8,128)(2,1)S(1)} %collective-permute-done.27.odd_ref, f32[512,576]{1,0:T(8,128)S(1)} %copy-done.1, f32[2,576]{1,0:T(2,128)S(1)} %get-tuple-element.155.excite_ref, f32[2,288]{1,0:T(2,128)S(1)} %add.9.sq_ref, ...), custom_call_target="tpu_custom_call" | custom-call | flops 2717908992 | bytes 4718592 | tf_op jit(solution)/shard_map/pallas_call | solution.py:375
  173.7 1.2 copy.12
  (104 shorter events, 9.0 us)
Async XLA Ops:
  0.6 4.4 %copy-start.31 = (bf16[576,288]{0,1:T(8,128)(2,1)S(1)}, bf16[576,288]{0,1:T(8,128)(2,1)}, u32[]{:S(2)}) copy-start(bf16[576,288]{0,1:T(8,128)(2,1)} %param.11) | copy-start | bytes 995332
  2.3 2.6 %copy-start.27 = (bf16[9,576,48]{1,2,0:T(8,128)(2,1)S(1)}, bf16[9,576,48]{1,2,0:T(8,128)(2,1)}, u32[]{:S(2)}) copy-start(bf16[9,576,48]{1,2,0:T(8,128)(2,1)} %param.10) | copy-start | bytes 1492996
  2.4 9.9 %copy-start.17 = (bf16[288,576]{1,0:T(8,128)(2,1)S(1)}, bf16[288,576]{1,0:T(8,128)(2,1)}, u32[]{:S(2)}) copy-start(bf16[288,576]{1,0:T(8,128)(2,1)} %expand_ref.3) | copy-start | bytes 995332
  2.4 15.8 %collective-permute-start.3 = (bf16[72,4608]{1,0:T(8,128)(2,1)S(1)}, bf16[72,4608]{1,0:T(8,128)(2,1)S(1)}, u32[]{:S(2)}, u32[]{:S(2)}) collective-permute-start(bf16[72,4608]{1,0:T(8,128)(2,1)S(1)} %reshape.11.refs_0_.refs_4_), channel_id=1, source_target_pairs={{0,4},{2,6},{8,0},{10,2},{16,8},{18,10},{24,16},{26,18},{28,24},{3... | collective-permute-start | bytes 1990664 | tf_op jit(solution)/shard_map/ppermute | solution.py:427
  3.7 15.5 %collective-permute-start.2 = (bf16[72,4608]{1,0:T(8,128)(2,1)S(1)}, bf16[72,4608]{1,0:T(8,128)(2,1)S(1)}, u32[]{:S(2)}, u32[]{:S(2)}) collective-permute-start(bf16[72,4608]{1,0:T(8,128)(2,1)S(1)} %reshape.11.refs_0_.refs_4_), channel_id=1, source_target_pairs={{0,8},{2,10},{8,16},{10,18},{16,24},{18,26},{24,28},{26,30},{28,20... | collective-permute-start | bytes 1990664 | tf_op jit(solution)/shard_map/ppermute | solution.py:427
  9.5 9.7 %copy-start = (f32[512,576]{1,0:T(8,128)}, f32[512,576]{1,0:T(8,128)S(1)}, u32[]{:S(2)}) copy-start(f32[512,576]{1,0:T(8,128)S(1)} %get-tuple-element.79.conv_ref) | copy-start | bytes 3538948
  9.5 2.8 %collective-permute-start = (f32[2,288]{1,0:T(2,128)S(1)}, f32[2,288]{1,0:T(2,128)S(1)}, u32[]{:S(2)}, u32[]{:S(2)}) collective-permute-start(f32[2,288]{1,0:T(2,128)S(1)} %get-tuple-element.82), channel_id=1, source_target_pairs={{0,1},{1,0},{2,3},{3,2},{4,5},{5,4},{6,7},{7,6},{8,9},{9,8},{10,11... | collective-permute-start | bytes 6920 | tf_op jit(solution)/shard_map/ppermute | solution.py:416
  18.2 21.6 %copy-start.7 = (bf16[72,4608]{1,0:T(8,128)(2,1)}, bf16[72,4608]{1,0:T(8,128)(2,1)S(1)}, u32[]{:S(2)}) copy-start(bf16[72,4608]{1,0:T(8,128)(2,1)S(1)} %collective-permute-done.3.refs_2_.refs_5_) | copy-start | bytes 1990660
  19.2 49.0 %copy-start.2 = (bf16[72,4608]{1,0:T(8,128)(2,1)}, bf16[72,4608]{1,0:T(8,128)(2,1)S(1)}, u32[]{:S(2)}) copy-start(bf16[72,4608]{1,0:T(8,128)(2,1)S(1)} %collective-permute-done.2.refs_1_.refs_4_) | copy-start | bytes 1990660
  19.2 20.7 %collective-permute-start.4 = (bf16[72,4608]{1,0:T(8,128)(2,1)S(1)}, bf16[72,4608]{1,0:T(8,128)(2,1)S(1)}, u32[]{:S(2)}, u32[]{:S(2)}) collective-permute-start(bf16[72,4608]{1,0:T(8,128)(2,1)S(1)} %collective-permute-done.2.refs_1_.refs_4_), channel_id=1, source_target_pairs={{0,8},{2,10},{8,16},{10,18},{16,24},{18,26},{24,28},{26,30},{28,20... | collective-permute-start | bytes 1990664 | tf_op jit(solution)/shard_map/ppermute | solution.py:427
  19.4 20.5 %collective-permute-start.5 = (bf16[72,4608]{1,0:T(8,128)(2,1)S(1)}, bf16[72,4608]{1,0:T(8,128)(2,1)}, u32[]{:S(2)}, u32[]{:S(2)}) collective-permute-start(bf16[72,4608]{1,0:T(8,128)(2,1)S(1)} %collective-permute-done.3.refs_2_.refs_5_), channel_id=1, source_target_pairs={{0,4},{2,6},{8,0},{10,2},{16,8},{18,10},{24,16},{26,18},{28,24},{3... | collective-permute-start | bytes 1990664 | tf_op jit(solution)/shard_map/ppermute | solution.py:427
  20.7 19.2 %collective-permute-start.1 = (bf16[256,576]{1,0:T(8,128)(2,1)}, bf16[256,576]{1,0:T(8,128)(2,1)}, u32[]{:S(2)}, u32[]{:S(2)}) collective-permute-start(bf16[256,576]{1,0:T(8,128)(2,1)} %get-tuple-element.83), channel_id=1, source_target_pairs={{0,2},{2,4},{4,6},{6,8},{8,10},{10,12},{12,14},{14,16},{16,18},{18... | collective-permute-start | bytes 884744 | tf_op jit(solution)/shard_map/ppermute | solution.py:391
  24.9 25.9 %all-to-all-start = ((bf16[8,8,4096]{2,1,0:T(8,128)(2,1)}), bf16[8,8,4096]{2,1,0:T(8,128)(2,1)S(1)}, u32[]{:S(2)}, u32[]{:S(2)}) async-start(bf16[8,8,4096]{2,1,0:T(8,128)(2,1)} %bitcast.17), calls=%async_computation | async-start | bytes 1048576 | tf_op jit(solution)/shard_map/all_to_all | solution.py:587
  39.8 21.6 %copy-start.4 = (bf16[72,4608]{1,0:T(8,128)(2,1)}, bf16[72,4608]{1,0:T(8,128)(2,1)S(1)}, u32[]{:S(2)}) copy-start(bf16[72,4608]{1,0:T(8,128)(2,1)S(1)} %collective-permute-done.4.refs_3_.refs_4_) | copy-start | bytes 1990660
  39.9 18.5 %collective-permute-start.6 = (bf16[72,4608]{1,0:T(8,128)(2,1)S(1)}, bf16[72,4608]{1,0:T(8,128)(2,1)S(1)}, u32[]{:S(2)}, u32[]{:S(2)}) collective-permute-start(bf16[72,4608]{1,0:T(8,128)(2,1)S(1)} %collective-permute-done.4.refs_3_.refs_4_), channel_id=1, source_target_pairs={{0,8},{2,10},{8,16},{10,18},{16,24},{18,26},{24,28},{26,30},{28,20... | collective-permute-start | bytes 1990664 | tf_op jit(solution)/shard_map/ppermute | solution.py:427
  43.4 18.1 %collective-permute-start.7 = (bf16[72,4608]{1,0:T(8,128)(2,1)}, bf16[72,4608]{1,0:T(8,128)(2,1)}, u32[]{:S(2)}, u32[]{:S(2)}) collective-permute-start(bf16[72,4608]{1,0:T(8,128)(2,1)} %collective-permute-done.5.refs_4_.refs_5_), channel_id=1, source_target_pairs={{0,4},{2,6},{8,0},{10,2},{16,8},{18,10},{24,16},{26,18},{28,24},{3... | collective-permute-start | bytes 1990664 | tf_op jit(solution)/shard_map/ppermute | solution.py:427
  47.8 17.9 %collective-permute-start.9 = (bf16[64,4608]{1,0:T(8,128)(2,1)}, bf16[64,4608]{1,0:T(8,128)(2,1)}, u32[]{:S(2)}, u32[]{:S(2)}) collective-permute-start(bf16[64,4608]{1,0:T(8,128)(2,1)} %shard_map.107.own_ref), channel_id=1, source_target_pairs={{0,2},{2,0},{4,6},{6,4},{8,10},{10,8},{12,14},{14,12},{16,18},{18,... | collective-permute-start | bytes 1769480 | tf_op jit(solution)/shard_map/ppermute | solution.py:408
  50.8 17.4 %copy-start.8 = (bf16[72,4608]{1,0:T(8,128)(2,1)S(1)}, bf16[72,4608]{1,0:T(8,128)(2,1)}, u32[]{:S(2)}) copy-start(bf16[72,4608]{1,0:T(8,128)(2,1)} %copy-done.7) | copy-start | bytes 1990660
  61.5 6.7 %copy-start.5 = (bf16[72,4608]{1,0:T(8,128)(2,1)S(1)}, bf16[72,4608]{1,0:T(8,128)(2,1)}, u32[]{:S(2)}) copy-start(bf16[72,4608]{1,0:T(8,128)(2,1)} %copy-done.4) | copy-start | bytes 1990660
  61.5 19.7 %collective-permute-start.12 = (bf16[72,4608]{1,0:T(8,128)(2,1)S(1)}, bf16[72,4608]{1,0:T(8,128)(2,1)S(1)}, u32[]{:S(2)}, u32[]{:S(2)}) collective-permute-start(bf16[72,4608]{1,0:T(8,128)(2,1)S(1)} %collective-permute-done.6.refs_5_.refs_4_), channel_id=1, source_target_pairs={{0,8},{2,10},{8,16},{10,18},{16,24},{18,26},{24,28},{26,30},{28,20... | collective-permute-start | bytes 1990664 | tf_op jit(solution)/shard_map/ppermute | solution.py:427
  61.5 18.5 %collective-permute-start.11 = (bf16[72,4096]{1,0:T(8,128)(2,1)}, bf16[72,4096]{1,0:T(8,128)(2,1)S(1)}, u32[]{:S(2)}, u32[]{:S(2)}) collective-permute-start(bf16[72,4096]{1,0:T(8,128)(2,1)} %refs_0_.1), channel_id=1, source_target_pairs={{0,4},{2,6},{8,0},{10,2},{16,8},{18,10},{24,16},{26,18},{28,24},{3... | collective-permute-start | bytes 1769480 | tf_op jit(solution)/shard_map/ppermute | solution.py:427
  68.2 5.1 %copy-start.9 = (bf16[72,4096]{1,0:T(8,128)(2,1)S(1)}, bf16[72,4096]{1,0:T(8,128)(2,1)}, u32[]{:S(2)}) copy-start(bf16[72,4096]{1,0:T(8,128)(2,1)} %refs_0_.1) | copy-start | bytes 1769476
  71.9 13.0 %copy-start.37 = (s32[5]{0:T(128)S(1)}, s32[5]{0:T(128)}, u32[]{:S(2)}) copy-start(s32[5]{0:T(128)} %shard_map.104.facts_ref) | copy-start | bytes 64
  71.9 8.1 %collective-permute-start.13 = (f32[128,504]{1,0:T(8,128)S(1)}, f32[128,504]{1,0:T(8,128)S(1)}, u32[]{:S(2)}, u32[]{:S(2)}) collective-permute-start(f32[128,504]{1,0:T(8,128)S(1)} %shard_map.109.own_ref), channel_id=1, source_target_pairs={{0,1},{1,0},{2,3},{3,2},{4,5},{5,4},{6,7},{7,6},{8,9},{9,8},{10,11... | collective-permute-start | bytes 774152 | tf_op jit(solution)/shard_map/ppermute | solution.py:416
  73.2 20.4 %collective-permute-start.10 = (bf16[72,4096]{1,0:T(8,128)(2,1)S(1)}, bf16[72,4096]{1,0:T(8,128)(2,1)S(1)}, u32[]{:S(2)}, u32[]{:S(2)}) collective-permute-start(bf16[72,4096]{1,0:T(8,128)(2,1)S(1)} %copy-done.9), channel_id=1, source_target_pairs={{0,8},{2,10},{8,16},{10,18},{16,24},{18,26},{24,28},{26,30},{28,20... | collective-permute-start | bytes 1769480 | tf_op jit(solution)/shard_map/ppermute | solution.py:427
  73.2 12.8 %collective-permute-start.8 = (bf16[64,4096]{1,0:T(8,128)(2,1)S(1)}, bf16[64,4096]{1,0:T(8,128)(2,1)S(1)}, u32[]{:S(2)}, u32[]{:S(2)}) collective-permute-start(bf16[64,4096]{1,0:T(8,128)(2,1)S(1)} %bitcast.6), channel_id=1, source_target_pairs={{0,2},{2,0},{4,6},{6,4},{8,10},{10,8},{12,14},{14,12},{16,18},{18,... | collective-permute-start | bytes 1572872 | tf_op jit(solution)/shard_map/ppermute | solution.py:408
  80.0 6.7 %copy-start.11 = (bf16[72,4096]{1,0:T(8,128)(2,1)}, bf16[72,4096]{1,0:T(8,128)(2,1)S(1)}, u32[]{:S(2)}) copy-start(bf16[72,4096]{1,0:T(8,128)(2,1)S(1)} %collective-permute-done.11.refs_1_) | copy-start | bytes 1769476
  81.2 17.4 %collective-permute-start.16 = (bf16[72,4096]{1,0:T(8,128)(2,1)S(1)}, bf16[72,4096]{1,0:T(8,128)(2,1)S(1)}, u32[]{:S(2)}, u32[]{:S(2)}) collective-permute-start(bf16[72,4096]{1,0:T(8,128)(2,1)S(1)} %collective-permute-done.11.refs_1_), channel_id=1, source_target_pairs={{0,4},{2,6},{8,0},{10,2},{16,8},{18,10},{24,16},{26,18},{28,24},{3... | collective-permute-start | bytes 1769480 | tf_op jit(solution)/shard_map/ppermute | solution.py:427
  83.5 3.5 %collective-permute-start.14 = (f32[128,72]{1,0:T(8,128)S(1)}, f32[128,72]{1,0:T(8,128)S(1)}, u32[]{:S(2)}, u32[]{:S(2)}) collective-permute-start(f32[128,72]{1,0:T(8,128)S(1)} %shard_map.111.own_ref), channel_id=1, source_target_pairs={{0,1},{1,0},{2,3},{3,2},{4,5},{5,4},{6,7},{7,6},{8,9},{9,8},{10,11... | collective-permute-start | bytes 110600 | tf_op jit(solution)/shard_map/ppermute | solution.py:416
  93.6 10.1 %copy-start.13 = (bf16[72,4096]{1,0:T(8,128)(2,1)}, bf16[72,4096]{1,0:T(8,128)(2,1)S(1)}, u32[]{:S(2)}) copy-start(bf16[72,4096]{1,0:T(8,128)(2,1)S(1)} %collective-permute-done.10.refs_0_.refs_2_) | copy-start | bytes 1769476
  93.6 15.6 %collective-permute-start.15 = (bf16[72,4096]{1,0:T(8,128)(2,1)S(1)}, bf16[72,4096]{1,0:T(8,128)(2,1)}, u32[]{:S(2)}, u32[]{:S(2)}) collective-permute-start(bf16[72,4096]{1,0:T(8,128)(2,1)S(1)} %collective-permute-done.10.refs_0_.refs_2_), channel_id=1, source_target_pairs={{0,8},{2,10},{8,16},{10,18},{16,24},{18,26},{24,28},{26,30},{28,20... | collective-permute-start | bytes 1769480 | tf_op jit(solution)/shard_map/ppermute | solution.py:427
  93.6 5.1 %collective-permute-start.17 = (f32[128,144]{1,0:T(8,128)S(1)}, f32[128,144]{1,0:T(8,128)S(1)}, u32[]{:S(2)}, u32[]{:S(2)}) collective-permute-start(f32[128,144]{1,0:T(8,128)S(1)} %shard_map.110.refs_0_), channel_id=1, source_target_pairs={{0,1},{1,0},{2,3},{3,2},{4,5},{5,4},{6,7},{7,6},{8,9},{9,8},{10,11... | collective-permute-start | bytes 221192 | tf_op jit(solution)/shard_map/ppermute | solution.py:416
  98.7 5.1 %copy-start.15 = (bf16[72,4096]{1,0:T(8,128)(2,1)}, bf16[72,4096]{1,0:T(8,128)(2,1)S(1)}, u32[]{:S(2)}) copy-start(bf16[72,4096]{1,0:T(8,128)(2,1)S(1)} %collective-permute-done.16.refs_1_.refs_3_) | copy-start | bytes 1769476
  98.7 15.4 %collective-permute-start.19 = (bf16[72,4096]{1,0:T(8,128)(2,1)S(1)}, bf16[72,4096]{1,0:T(8,128)(2,1)}, u32[]{:S(2)}, u32[]{:S(2)}) collective-permute-start(bf16[72,4096]{1,0:T(8,128)(2,1)S(1)} %collective-permute-done.16.refs_1_.refs_3_), channel_id=1, source_target_pairs={{0,4},{2,6},{8,0},{10,2},{16,8},{18,10},{24,16},{26,18},{28,24},{3... | collective-permute-start | bytes 1769480 | tf_op jit(solution)/shard_map/ppermute | solution.py:427
  103.0 11.1 %copy-start.21 = (f32[64,2304]{1,0:T(8,128)}, f32[64,2304]{1,0:T(8,128)S(1)}, u32[]{:S(2)}) copy-start(f32[64,2304]{1,0:T(8,128)S(1)} %get-tuple-element.121.refs_7_) | copy-start | bytes 1769476
  103.0 12.2 %copy-start.23 = (f32[64,2304]{1,0:T(8,128)}, f32[64,2304]{1,0:T(8,128)S(1)}, u32[]{:S(2)}) copy-start(f32[64,2304]{1,0:T(8,128)S(1)} %get-tuple-element.122.refs_8_) | copy-start | bytes 1769476
  103.0 12.2 %copy-start.25 = (f32[64,2304]{1,0:T(8,128)}, f32[64,2304]{1,0:T(8,128)S(1)}, u32[]{:S(2)}) copy-start(f32[64,2304]{1,0:T(8,128)S(1)} %get-tuple-element.123.refs_9_) | copy-start | bytes 1769476
  109.2 4.2 %collective-permute-start.20 = (f32[128,144]{1,0:T(8,128)S(1)}, f32[128,144]{1,0:T(8,128)S(1)}, u32[]{:S(2)}, u32[]{:S(2)}) collective-permute-start(f32[128,144]{1,0:T(8,128)S(1)} %shard_map.114.refs_0_), channel_id=1, source_target_pairs={{0,1},{1,0},{2,3},{3,2},{4,5},{5,4},{6,7},{7,6},{8,9},{9,8},{10,11... | collective-permute-start | bytes 221192 | tf_op jit(solution)/shard_map/ppermute | solution.py:416
  111.1 30.7 %collective-permute-start.18 = (bf16[72,4096]{1,0:T(8,128)(2,1)}, bf16[72,4096]{1,0:T(8,128)(2,1)}, u32[]{:S(2)}, u32[]{:S(2)}) collective-permute-start(bf16[72,4096]{1,0:T(8,128)(2,1)} %collective-permute-done.15.refs_0_.refs_4_), channel_id=1, source_target_pairs={{0,8},{2,10},{8,16},{10,18},{16,24},{18,26},{24,28},{26,30},{28,20... | collective-permute-start | bytes 1769480 | tf_op jit(solution)/shard_map/ppermute | solution.py:427
  114.1 27.7 %collective-permute-start.21 = (bf16[72,4096]{1,0:T(8,128)(2,1)}, bf16[72,4096]{1,0:T(8,128)(2,1)}, u32[]{:S(2)}, u32[]{:S(2)}) collective-permute-start(bf16[72,4096]{1,0:T(8,128)(2,1)} %collective-permute-done.19.refs_1_.refs_5_), channel_id=1, source_target_pairs={{0,4},{2,6},{8,0},{10,2},{16,8},{18,10},{24,16},{26,18},{28,24},{3... | collective-permute-start | bytes 1769480 | tf_op jit(solution)/shard_map/ppermute | solution.py:427
  115.2 13.4 %all-to-all-start.1 = ((bf16[8,16,576]{2,1,0:T(8,128)(2,1)}), bf16[8,16,576]{2,1,0:T(8,128)(2,1)S(1)}, u32[]{:S(2)}, u32[]{:S(2)}) async-start(bf16[8,16,576]{2,1,0:T(8,128)(2,1)} %bitcast.4), calls=%async_computation.1 | async-start | bytes 327680 | tf_op jit(solution)/shard_map/all_to_all | solution.py:587
  121.7 17.8 %collective-permute-start.22 = (f32[128,144]{1,0:T(8,128)}, f32[128,144]{1,0:T(8,128)}, u32[]{:S(2)}, u32[]{:S(2)}) collective-permute-start(f32[128,144]{1,0:T(8,128)} %shard_map.116.refs_0_), channel_id=1, source_target_pairs={{0,1},{1,0},{2,3},{3,2},{4,5},{5,4},{6,7},{7,6},{8,9},{9,8},{10,11... | collective-permute-start | bytes 221192 | tf_op jit(solution)/shard_map/ppermute | solution.py:416
  128.7 1.1 copy-start.10
  129.7 1.1 copy-start.12
  130.8 1.1 copy-start.14
  131.9 1.1 copy-start.16
  132.9 4.3 %copy-start.3 = (bf16[72,4608]{1,0:T(8,128)(2,1)S(1)}, bf16[72,4608]{1,0:T(8,128)(2,1)}, u32[]{:S(2)}) copy-start(bf16[72,4608]{1,0:T(8,128)(2,1)} %copy-done.2) | copy-start | bytes 1990660
  132.9 4.3 %copy-start.20 = (f32[64,2304]{1,0:T(8,128)S(1)}, f32[64,2304]{1,0:T(8,128)}, u32[]{:S(2)}) copy-start(f32[64,2304]{1,0:T(8,128)} %copy-done.19) | copy-start | bytes 1769476
  132.9 4.3 %copy-start.22 = (f32[64,2304]{1,0:T(8,128)S(1)}, f32[64,2304]{1,0:T(8,128)}, u32[]{:S(2)}) copy-start(f32[64,2304]{1,0:T(8,128)} %copy-done.21) | copy-start | bytes 1769476
  132.9 4.3 %copy-start.24 = (f32[64,2304]{1,0:T(8,128)S(1)}, f32[64,2304]{1,0:T(8,128)}, u32[]{:S(2)}) copy-start(f32[64,2304]{1,0:T(8,128)} %copy-done.23) | copy-start | bytes 1769476
  132.9 4.3 %copy-start.26 = (f32[64,2304]{1,0:T(8,128)S(1)}, f32[64,2304]{1,0:T(8,128)}, u32[]{:S(2)}) copy-start(f32[64,2304]{1,0:T(8,128)} %copy-done.25) | copy-start | bytes 1769476
  132.9 4.3 %copy-start.30 = (f32[128,144]{1,0:T(8,128)S(1)}, f32[128,144]{1,0:T(8,128)}, u32[]{:S(2)}) copy-start(f32[128,144]{1,0:T(8,128)} %copy-done.29) | copy-start | bytes 221188
  133.0 4.3 %copy-start.34 = (f32[128,144]{1,0:T(8,128)S(1)}, f32[128,144]{1,0:T(8,128)}, u32[]{:S(2)}) copy-start(f32[128,144]{1,0:T(8,128)} %copy-done.33) | copy-start | bytes 221188
  137.3 2.2 %copy-start.6 = (bf16[72,4608]{1,0:T(8,128)(2,1)S(1)}, bf16[72,4608]{1,0:T(8,128)(2,1)}, u32[]{:S(2)}) copy-start(bf16[72,4608]{1,0:T(8,128)(2,1)} %copy-done.4) | copy-start | bytes 1990660
  143.8 3.9 %collective-permute-start.23 = (f32[128,144]{1,0:T(8,128)S(1)}, f32[128,144]{1,0:T(8,128)S(1)}, u32[]{:S(2)}, u32[]{:S(2)}) collective-permute-start(f32[128,144]{1,0:T(8,128)S(1)} %shard_map.120.refs_0_), channel_id=1, source_target_pairs={{0,1},{1,0},{2,3},{3,2},{4,5},{5,4},{6,7},{7,6},{8,9},{9,8},{10,11... | collective-permute-start | bytes 221192 | tf_op jit(solution)/shard_map/ppermute | solution.py:416
  148.9 5.7 %collective-permute-start.24 = (bf16[64,2304]{1,0:T(8,128)(2,1)S(1)}, bf16[64,2304]{1,0:T(8,128)(2,1)S(1)}, u32[]{:S(2)}, u32[]{:S(2)}) collective-permute-start(bf16[64,2304]{1,0:T(8,128)(2,1)S(1)} %get-tuple-element.141), channel_id=1, source_target_pairs={{0,2},{2,0},{4,6},{6,4},{8,10},{10,8},{12,14},{14,12},{16,18},{18,... | collective-permute-start | bytes 884744 | tf_op jit(solution)/shard_map/ppermute | solution.py:408
  154.5 4.2 %collective-permute-start.25 = (bf16[64,2304]{1,0:T(8,128)(2,1)S(1)}, bf16[64,2304]{1,0:T(8,128)(2,1)S(1)}, u32[]{:S(2)}, u32[]{:S(2)}) collective-permute-start(bf16[64,2304]{1,0:T(8,128)(2,1)S(1)} %get-tuple-element.147), channel_id=1, source_target_pairs={{0,2},{2,0},{4,6},{6,4},{8,10},{10,8},{12,14},{14,12},{16,18},{18,... | collective-permute-start | bytes 884744 | tf_op jit(solution)/shard_map/ppermute | solution.py:408
  156.1 9.7 %collective-permute-start.27 = (bf16[256,576]{1,0:T(8,128)(2,1)S(1)}, bf16[256,576]{1,0:T(8,128)(2,1)S(1)}, u32[]{:S(2)}, u32[]{:S(2)}) collective-permute-start(bf16[256,576]{1,0:T(8,128)(2,1)S(1)} %get-tuple-element.154), channel_id=1, source_target_pairs={{2,0},{4,2},{6,4},{8,6},{10,8},{12,10},{14,12},{16,14},{18,16},{20... | collective-permute-start | bytes 884744 | tf_op jit(solution)/shard_map/ppermute | solution.py:391
  160.2 5.6 %copy-start.1 = (f32[512,576]{1,0:T(8,128)S(1)}, f32[512,576]{1,0:T(8,128)}, u32[]{:S(2)}) copy-start(f32[512,576]{1,0:T(8,128)} %copy-done) | copy-start | bytes 3538948
  160.2 5.6 %copy-start.18 = (bf16[288,576]{1,0:T(8,128)(2,1)S(1)}, bf16[288,576]{1,0:T(8,128)(2,1)}, u32[]{:S(2)}) copy-start(bf16[288,576]{1,0:T(8,128)(2,1)} %expand_ref.3) | copy-start | bytes 995332
  162.6 12.3 %collective-permute-start.26 = (bf16[64,4096]{1,0:T(8,128)(2,1)S(1)}, bf16[64,4096]{1,0:T(8,128)(2,1)S(1)}, u32[]{:S(2)}, u32[]{:S(2)}) collective-permute-start(bf16[64,4096]{1,0:T(8,128)(2,1)S(1)} %get-tuple-element.152), channel_id=1, source_target_pairs={{0,2},{2,0},{4,6},{6,4},{8,10},{10,8},{12,14},{14,12},{16,18},{18,... | collective-permute-start | bytes 1572872 | tf_op jit(solution)/shard_map/ppermute | solution.py:408
  165.8 3.4 %copy-start.28 = (bf16[9,576,48]{1,2,0:T(8,128)(2,1)S(1)}, bf16[9,576,48]{1,2,0:T(8,128)(2,1)}, u32[]{:S(2)}) copy-start(bf16[9,576,48]{1,2,0:T(8,128)(2,1)} %param.10) | copy-start | bytes 1492996
  165.8 3.4 %copy-start.32 = (bf16[576,288]{0,1:T(8,128)(2,1)S(1)}, bf16[576,288]{0,1:T(8,128)(2,1)}, u32[]{:S(2)}) copy-start(bf16[576,288]{0,1:T(8,128)(2,1)} %param.11) | copy-start | bytes 995332
  166.7 2.5 %collective-permute-start.28 = (f32[2,288]{1,0:T(2,128)S(1)}, f32[2,288]{1,0:T(2,128)S(1)}, u32[]{:S(2)}, u32[]{:S(2)}) collective-permute-start(f32[2,288]{1,0:T(2,128)S(1)} %shard_map.126), channel_id=1, source_target_pairs={{0,1},{1,0},{2,3},{3,2},{4,5},{5,4},{6,7},{7,6},{8,9},{9,8},{10,11... | collective-permute-start | bytes 6920 | tf_op jit(solution)/shard_map/ppermute | solution.py:416
  (5 other events, 3.5 us)

commit v8 on v7

--- a/solution.py
+++ b/solution.py
@@ -520,16 +520,25 @@
 
 
 def token_kernel(offsets, chips, unit, first, facts_ref, act_ref, *refs):
-    count = len(offsets)
-    blocks, before, after = refs[:count], refs[count:-2], refs[-2:]
-    width = blocks[0].shape[0]
+    count, held = len(offsets), 2 if first else 4
+    blocks, refs = refs[:count], refs[count:]
+    before, after = refs[: held - 2], refs[held - 2 : held]
+    buffers, sems = refs[held:-1], refs[-1]
+    copies = [
+        pltpu.make_async_copy(ref, buffer, sems.at[place])
+        for place, (ref, buffer) in enumerate(zip(blocks, buffers))
+    ]
+    for copy in copies:
+        copy.start()
+    width = buffers[0].shape[0]
     matrix = exchange_matrix(facts_ref[0], unit, False)
     act = jnp.dot(matrix, act_ref[...], preferred_element_type=jnp.float32).astype(jnp.bfloat16)
     total = 0.0
-    for offset, ref in zip(offsets, blocks):
+    for offset, copy, buffer in zip(offsets, copies, buffers):
         columns = block_columns(facts_ref, offset, chips, width)
         piece = contract_last(act, columns).astype(jnp.bfloat16)
-        total += jnp.dot(piece, ref[...], preferred_element_type=jnp.float32)
+        copy.wait()
+        total += jnp.dot(piece, buffer[...], preferred_element_type=jnp.float32)
     rows = after[0].shape[0]
     for half, ref in enumerate(after):
         value = total[half * rows : (half + 1) * rows]
@@ -572,13 +581,22 @@
 def add_tokens(facts, act, offsets, chips, blocks, before, unit):
     rows, columns = act.shape[0] // 2, blocks[0].shape[1]
     kernel = functools.partial(token_kernel, offsets, chips, unit, not before)
-    outs = f32(rows, columns), (bf16 if before else f32)(rows, columns)
     cost = pl.CostEstimate(
-        flops=5 * len(blocks) * act.shape[1] * act.shape[0] * columns // chips * 8,
+        flops=40 * len(blocks) * act.shape[1] * act.shape[0] * columns // chips,
         bytes_accessed=0,
         transcendentals=0,
     )
-    return facts_call(kernel, outs, facts, (act, *blocks, *before), cost if before else FREE)
+    vmem = pl.BlockSpec(memory_space=pltpu.VMEM)
+    anywhere = pl.BlockSpec(memory_space=pl.ANY)
+    return pl.pallas_call(
+        kernel,
+        out_shape=(f32(rows, columns), (bf16 if before else f32)(rows, columns)),
+        in_specs=vmem_specs(1) + [anywhere] * len(blocks) + [vmem] * len(before),
+        scratch_shapes=[pltpu.VMEM(block.shape, block.dtype) for block in blocks]
+        + [pltpu.SemaphoreType.DMA((len(blocks),))],
+        compiler_params=pltpu.CompilerParams(vmem_limit_bytes=VMEM_BYTES),
+        cost_estimate=cost if before else FREE,
+    )(facts, act, *blocks, *before)
 
 
 def chips_exchange(value):
@@ -618,47 +636,50 @@
     halo = shifted(odd, "ctx", 1)
 
     s_up, s_down = [flat_sampler, s_up], [flat_sampler, s_down]
-    s_up[1], s_down[1], even = tie(s_up[1], s_down[1], even)
+    s_up[1], s_down[1], even, readout_kernel = tie(s_up[1], s_down[1], even, readout_kernel)
     for step in range(2, steps):
         s_up.append(ring_send(s_up[-1], 1))
         s_down.append(ring_send(s_down[-1], -1))
         if step == 2:
             halo, s_up[2], s_down[2] = tie(halo, s_up[2], s_down[2])
+            r_up = [readout_kernel, ring_send(readout_kernel, 1)]
+            r_down = [readout_kernel, ring_send(readout_kernel, -1)]
             patches = take_patches(facts, halo, even)
-            patches = order_rows(facts, patches, swap_cores(patches), unit)
-    s_up[-1], s_down[-1], readout_kernel, back = tie(s_up[-1], s_down[-1], readout_kernel, back)
+            mate_patches, r_up[1], r_down[1] = tie(swap_cores(patches), r_up[1], r_down[1])
+            patches = order_rows(facts, patches, mate_patches, unit)
+            r_down.append(ring_send(r_down[1], -1))
+    held = tie(s_up[-1], s_down[-1], r_up[1], back, patches)
+    s_up[-1], s_down[-1], r_up[1], back, patches = held
     back = (back, swap_cores(back))
     s_last = ring_send(s_up[-1], 1)
     samplers = [flat_sampler] + [block for pair in zip(s_up[1:], s_down[1:]) for block in pair]
     offsets = ring_offsets(chips)
     first_pre = block_products(pre_kernel, (patches,), samplers)
-    r_down = [readout_kernel, ring_send(readout_kernel, -1)]
-    readout_kernel, first_pre = tie(readout_kernel, first_pre)
-    r_up = [readout_kernel, ring_send(readout_kernel, 1)]
-    first_pre = tp_terms(first_pre)
-    r_down[1], s_last, *first_pre = tie(r_down[1], s_last, *first_pre)
-    r_down.append(ring_send(r_down[1], -1))
+    r_up.append(ring_send(r_up[1], 1))
     sums = block_products(back_kernel, back, [r_up[0], r_down[1]])
+    held = tie(*tp_terms(first_pre), sums, s_last, r_down[2])
+    first_pre, sums, s_last, r_down[2] = held[:2], *held[2:]
     first_slope, first_act = act_and_slope(facts, first_pre, offsets[:-1], chips, (), unit)
     last_pre = tp_terms(block_products(pre_kernel, (patches,), [s_last]))
     last_slope, act = act_and_slope(facts, last_pre, offsets[-1:], chips, (first_act,), unit)
     slopes = first_slope, last_slope
-    r_up[1], sums, act = tie(r_up[1], sums, act)
-    r_up.append(ring_send(r_up[1], 1))
+    r_up[2], act, *terms = tie(r_up[2], act, *tp_terms(sums))
     act = chips_exchange(act)
     halo_lanes, even_lanes = slice(0, 4 * chans), slice(4 * chans, 8 * chans)
     grads = ()
-    terms = tp_terms(sums)
     pieces, blocks = [(0, 0), (0, 2)], [samplers[0], samplers[2]]
     for step in range(2, steps):
-        r_down[step], *terms = tie(r_down[step], *terms)
         r_down.append(ring_send(r_down[step], -1))
-        sums = block_products(back_kernel, back, [r_up[step - 1], r_down[step]])
+        group = r_up[step - 1], r_down[step]
+        if step == steps - 1:
+            *group, act = tie(*group, act)
+        sums = block_products(back_kernel, back, group)
         grads = add_gradients(
             facts, terms, slopes, pieces, blocks, grads, unit, (halo_lanes, even_lanes), False
         )
         if step < steps - 1:
-            r_up[step], sums, *grads = tie(r_up[step], sums, *grads)
+            if step > 2:
+                r_up[step], sums, *grads = tie(r_up[step], sums, *grads)
             r_up.append(ring_send(r_up[step], 1))
         terms = tp_terms(sums)
         pieces = [(0, 2 * step - 3), (0, 2 * step)]

time: 177 us -> 177 us (level)
  waiting for transfers between devices: 64.5 us -> 58.9 us
  local copies, waits for them, and re-layouts: 11.8 us -> 15.7 us
  starting transfers between devices: 49.8 us -> 52.5 us
    pallas_call x0 -> x2, Pallas kernels: none -> 6.97 us  [add_tokens(): pl.pallas_call(kernel, out_shape=(f32(rows, columns), (bf16 if before els...]
    pallas_call x9 -> x7, Pallas kernels: 17.9 us -> 11.3 us  [facts_call(): pl.pallas_call(kernel, out_shape=outs, in_specs=vmem_specs(len(operands))...]
    ppermute x8, waiting for transfers between devices: 18.4 us -> 14.2 us  [tp_terms(): other = lax.ppermute(value, 'tp', [(i, i ^ reach) for i in range(size)])]
    unnamed x78 -> x98, local copies, waits for them, and re-layouts: 10.1 us -> 13.9 us
    ppermute x8, starting transfers between devices: 10.2 us -> 7.18 us  [tp_terms(): other = lax.ppermute(value, 'tp', [(i, i ^ reach) for i in range(size)])]
    ppermute x14, starting transfers between devices: 15.9 us -> 18.3 us  [ring_send(): return lax.ppermute(value, 'ctx', ring_pairs(lax.axis_size('ctx'), by))]
    ppermute x2, waiting for transfers between devices: 12.6 us -> 10.4 us  [shifted(): return lax.ppermute(value, axis, pairs)]
    ppermute x2, starting transfers between devices: 6.86 us -> 8.98 us  [shifted(): return lax.ppermute(value, axis, pairs)]
  transfers between devices with their start and end apart: 31 -> 31, of which waited for: 17 -> 13; matrix products, arithmetic and copies ran while one was open for 1% -> 1% of each run, Pallas kernels for 25% -> 25%
where the time goes in v8:
time: 177 us; the launch traced here: 176 us
  waiting for transfers between devices  58.9 us (33%)
  starting transfers between devices  52.5 us (30%)
  Pallas kernels  46.5 us (26%)
  local copies, waits for them, and re-layouts  15.7 us (9%)
    ppermute x14, waiting for transfers between devices, ring_send(): return lax.ppermute(value, 'ctx', ring_pairs(lax.axis_size('ctx'), by))  27.5 us
    ppermute x14, starting transfers between devices, ring_send(): return lax.ppermute(value, 'ctx', ring_pairs(lax.axis_size('ctx'), by))  18.3 us
    ppermute x8, waiting for transfers between devices, tp_terms(): other = lax.ppermute(value, 'tp', [(i, i ^ reach) for i in range(size)])  14.2 us
    unnamed x98, local copies, waits for them, and re-layouts  13.9 us
    pallas_call x6, Pallas kernels, block_products(): whole_call(kernel, f32(rows, len(blocks) * blocks[0].shape[0]), [])  11.5 us
    pallas_call x7, Pallas kernels, facts_call(): pl.pallas_call(kernel, out_shape=outs, in_specs=vmem_specs(len(operands))...  11.3 us
    ppermute x2, waiting for transfers between devices, shifted(): return lax.ppermute(value, axis, pairs)  10.4 us
    all_to_all x2, starting transfers between devices, chips_exchange(): lax.all_to_all(value, 'ctx', split_axis=0, concat_axis=0, tiled=True, axi...  9.2 us
  transfers between devices with their start and end apart: 31, of which 13 were waited for; matrix products, arithmetic and copies ran while one was open for 1% of the time, Pallas kernels for 25%

profile of v8, /device:TPU:3, one launch (start us, length us, event | category | flops | bytes accessed | tf_op | source)
XLA Modules:
  0.0 175.7 jit_solution(17617984325679604996)
XLA Ops:
  0.7 1.8 reshape.11.refs_0_.refs_4_
  2.5 1.5 collective-permute-start.3
  4.1 4.5 %shard_map.105 = (f32[512,576]{1,0:T(8,128)S(1)}, bf16[512,576]{1,0:T(8,128)(2,1)S(1)}, f32[2,288]{1,0:T(2,128)S(1)}) custom-call(bf16[2,196,576]{2,1,0:T(8,128)(2,1)S(1)} %copy.11.feat_ref, bf16[9,48,576]{2,1,0:T(8,128)(2,1)S(1)} %bitcast.13, bf16[288,576]{1,0:T(8,128)(2,1)S(1)} %bitcast.15), custom_call_target="tpu_custom_call" | custom-call | tf_op jit(solution)/shard_map/pallas_call | solution.py:292
  8.5 1.3 collective-permute-start
  9.8 1.5 collective-permute-done
  13.4 4.9 %collective-permute-done.2.refs_1_.refs_4_ = bf16[72,4608]{1,0:T(8,128)(2,1)S(1)} collective-permute-done((bf16[72,4608]{1,0:T(8,128)(2,1)S(1)}, bf16[72,4608]{1,0:T(8,128)(2,1)S(1)}, u32[]{:S(2)}, u32[]{:S(2)}) %collective-permute-start.2) | collective-permute-done | bytes 663584 | tf_op jit(solution)/shard_map/ppermute | solution.py:427
  18.4 1.1 collective-permute-start.4
  19.8 6.4 %collective-permute-start.1 = (bf16[256,576]{1,0:T(8,128)(2,1)S(1)}, bf16[256,576]{1,0:T(8,128)(2,1)S(1)}, u32[]{:S(2)}, u32[]{:S(2)}) collective-permute-start(bf16[256,576]{1,0:T(8,128)(2,1)S(1)} %get-tuple-element.79), channel_id=1, source_target_pairs={{0,2},{2,4},{4,6},{6,8},{8,10},{10,12},{12,14},{14,16},{16,18},{18... | collective-permute-start | bytes 884744 | tf_op jit(solution)/shard_map/ppermute | solution.py:391
  26.2 4.7 %all-to-all-start = ((bf16[8,8,4096]{2,1,0:T(8,128)(2,1)}), bf16[8,8,4096]{2,1,0:T(8,128)(2,1)S(1)}, u32[]{:S(2)}, u32[]{:S(2)}) async-start(bf16[8,8,4096]{2,1,0:T(8,128)(2,1)} %bitcast.17), calls=%async_computation | async-start | bytes 1048576 | tf_op jit(solution)/shard_map/all_to_all | solution.py:605
  30.9 8.3 %collective-permute-done.1.halo_ref = bf16[256,576]{1,0:T(8,128)(2,1)S(1)} collective-permute-done((bf16[256,576]{1,0:T(8,128)(2,1)S(1)}, bf16[256,576]{1,0:T(8,128)(2,1)S(1)}, u32[]{:S(2)}, u32[]{:S(2)}) %collective-permute-start.1) | collective-permute-done | bytes 294944 | tf_op jit(solution)/shard_map/ppermute | solution.py:391
  40.0 3.6 %collective-permute-start.6 = (bf16[72,4608]{1,0:T(8,128)(2,1)S(1)}, bf16[72,4608]{1,0:T(8,128)(2,1)S(1)}, u32[]{:S(2)}, u32[]{:S(2)}) collective-permute-start(bf16[72,4608]{1,0:T(8,128)(2,1)S(1)} %collective-permute-done.4.refs_3_.refs_4_), channel_id=1, source_target_pairs={{0,8},{2,10},{8,16},{10,18},{16,24},{18,26},{24,28},{26,30},{28,20... | collective-permute-start | bytes 1990664 | tf_op jit(solution)/shard_map/ppermute | solution.py:427
  43.6 0.9 collective-permute-start.7
  44.5 1.3 shard_map.104.facts_ref
  45.7 1.5 collective-permute-start.10
  47.3 1.0 copy-done.34
  48.2 1.0 copy-done.36
  49.9 1.0 shard_map.107.own_ref
  50.9 2.8 %collective-permute-start.8 = (bf16[64,4608]{1,0:T(8,128)(2,1)S(1)}, bf16[64,4608]{1,0:T(8,128)(2,1)S(1)}, u32[]{:S(2)}, u32[]{:S(2)}) collective-permute-start(bf16[64,4608]{1,0:T(8,128)(2,1)S(1)} %shard_map.107.own_ref), channel_id=1, source_target_pairs={{0,2},{2,0},{4,6},{6,4},{8,10},{10,8},{12,14},{14,12},{16,18},{18,... | collective-permute-start | bytes 1769480 | tf_op jit(solution)/shard_map/ppermute | solution.py:408
  53.7 18.8 %collective-permute-done.10.refs_1_ = bf16[72,4096]{1,0:T(8,128)(2,1)} collective-permute-done((bf16[72,4096]{1,0:T(8,128)(2,1)}, bf16[72,4096]{1,0:T(8,128)(2,1)}, u32[]{:S(2)}, u32[]{:S(2)}) %collective-permute-start.10) | collective-permute-done | bytes 589856 | tf_op jit(solution)/shard_map/ppermute | solution.py:427
  73.3 1.0 shard_map.108.patch_ref
  74.4 5.1 %collective-permute-start.15 = (bf16[72,4096]{1,0:T(8,128)(2,1)}, bf16[72,4096]{1,0:T(8,128)(2,1)S(1)}, u32[]{:S(2)}, u32[]{:S(2)}) collective-permute-start(bf16[72,4096]{1,0:T(8,128)(2,1)} %collective-permute-done.10.refs_1_), channel_id=1, source_target_pairs={{0,4},{2,6},{8,0},{10,2},{16,8},{18,10},{24,16},{26,18},{28,24},{3... | collective-permute-start | bytes 1769480 | tf_op jit(solution)/shard_map/ppermute | solution.py:427
  79.6 1.1 copy-done.1
  80.6 1.1 copy-done.6
  81.7 1.1 copy-done.9
  82.8 1.1 copy-done.12
  83.9 3.7 %shard_map.109.own_ref = f32[128,504]{1,0:T(8,128)S(1)} custom-call(bf16[128,4608]{1,0:T(8,128)(2,1)S(1)} %shard_map.108.patch_ref, bf16[72,4608]{1,0:T(8,128)(2,1)S(1)} %copy-done.1, bf16[72,4608]{1,0:T(8,128)(2,1)S(1)} %copy-done.6, bf16[72,4608]{1,0:T(8,128)(2,1)S(1)} %copy-done.12, bf16[72,4608]{1,0:T(8,128)(2,1)S(1)} %copy-done.9, ...), custom_call_target="tpu_custom_call" | custom-call | tf_op jit(solution)/shard_map/pallas_call | solution.py:551
  87.7 1.3 collective-permute-start.13
  89.3 1.8 %shard_map.110.refs_0_ = f32[128,144]{1,0:T(8,128)S(1)} custom-call(bf16[64,4096]{1,0:T(8,128)(2,1)S(1)} %bitcast.7, bf16[64,4096]{1,0:T(8,128)(2,1)S(1)} %collective-permute-done.11.send_ref, bf16[72,4096]{1,0:T(8,128)(2,1)S(1)} %copy-done.14, bf16[72,4096]{1,0:T(8,128)(2,1)} %collective-permute-done.10.refs_1_), custom_call_target="tpu_custom_call" | custom-call | tf_op jit(solution)/shard_map/pallas_call | solution.py:551
  91.1 4.1 %collective-permute-done.13.other_ref = f32[128,504]{1,0:T(8,128)S(1)} collective-permute-done((f32[128,504]{1,0:T(8,128)S(1)}, f32[128,504]{1,0:T(8,128)S(1)}, u32[]{:S(2)}, u32[]{:S(2)}) %collective-permute-start.13) | collective-permute-done | bytes 258080 | tf_op jit(solution)/shard_map/ppermute | solution.py:416
  95.2 1.9 %collective-permute-start.19 = (bf16[72,4096]{1,0:T(8,128)(2,1)S(1)}, bf16[72,4096]{1,0:T(8,128)(2,1)}, u32[]{:S(2)}, u32[]{:S(2)}) collective-permute-start(bf16[72,4096]{1,0:T(8,128)(2,1)S(1)} %collective-permute-done.15.refs_1_.refs_3_), channel_id=1, source_target_pairs={{0,4},{2,6},{8,0},{10,2},{16,8},{18,10},{24,16},{26,18},{28,24},{3... | collective-permute-start | bytes 1769480 | tf_op jit(solution)/shard_map/ppermute | solution.py:427
  97.2 1.3 collective-permute-start.17
  99.1 1.1 shard_map.112
  100.3 2.7 %collective-permute-done.16.other_ref = f32[128,72]{1,0:T(8,128)S(1)} collective-permute-done((f32[128,72]{1,0:T(8,128)S(1)}, f32[128,72]{1,0:T(8,128)S(1)}, u32[]{:S(2)}, u32[]{:S(2)}) %collective-permute-start.16) | collective-permute-done | bytes 36896 | tf_op jit(solution)/shard_map/ppermute | solution.py:416
  102.9 1.6 shard_map.113
  104.5 2.7 %collective-permute-done.12.refs_0_.refs_4_ = bf16[72,4096]{1,0:T(8,128)(2,1)} collective-permute-done((bf16[72,4096]{1,0:T(8,128)(2,1)S(1)}, bf16[72,4096]{1,0:T(8,128)(2,1)}, u32[]{:S(2)}, u32[]{:S(2)}) %collective-permute-start.12) | collective-permute-done | bytes 589856 | tf_op jit(solution)/shard_map/ppermute | solution.py:427
  107.9 1.1 collective-permute-done.19.refs_1_.refs_5_
  108.9 1.9 %collective-permute-start.20 = (bf16[72,4096]{1,0:T(8,128)(2,1)}, bf16[72,4096]{1,0:T(8,128)(2,1)}, u32[]{:S(2)}, u32[]{:S(2)}) collective-permute-start(bf16[72,4096]{1,0:T(8,128)(2,1)} %collective-permute-done.19.refs_1_.refs_5_), channel_id=1, source_target_pairs={{0,4},{2,6},{8,0},{10,2},{16,8},{18,10},{24,16},{26,18},{28,24},{3... | collective-permute-start | bytes 1769480 | tf_op jit(solution)/shard_map/ppermute | solution.py:427
  110.8 4.5 %all-to-all-start.1 = ((bf16[8,16,576]{2,1,0:T(8,128)(2,1)}), bf16[8,16,576]{2,1,0:T(8,128)(2,1)S(1)}, u32[]{:S(2)}, u32[]{:S(2)}) async-start(bf16[8,16,576]{2,1,0:T(8,128)(2,1)} %bitcast.4), calls=%async_computation.1 | async-start | bytes 327680 | tf_op jit(solution)/shard_map/all_to_all | solution.py:605
  115.3 1.1 copy-done.18
  116.4 1.1 copy-done.21
  117.5 1.4 shard_map.115.refs_0_
  118.9 1.2 collective-permute-start.22
  120.1 6.7 %all-to-all-done.1 = bf16[8,16,576]{2,1,0:T(8,128)(2,1)S(1)} async-done(((bf16[8,16,576]{2,1,0:T(8,128)(2,1)}), bf16[8,16,576]{2,1,0:T(8,128)(2,1)S(1)}, u32[]{:S(2)}, u32[]{:S(2)}) %all-to-all-start.1) | async-done | bytes 147488 | tf_op jit(solution)/shard_map/all_to_all | solution.py:605
  126.9 2.1 %shard_map.114.refs_0_ = f32[128,144]{1,0:T(8,128)S(1)} custom-call(bf16[64,4096]{1,0:T(8,128)(2,1)S(1)} %bitcast.9, bf16[64,4096]{1,0:T(8,128)(2,1)S(1)} %collective-permute-done.11.send_ref, bf16[72,4096]{1,0:T(8,128)(2,1)} %collective-permute-done.12.refs_0_.refs_4_, bf16[72,4096]{1,0:T(8,128)(2,1)} %collective-permute-done.19.refs_1_.refs_5_), custom_call_target="tpu_custom_call" | custom-call | tf_op jit(solution)/shard_map/pallas_call | solution.py:551
  129.0 1.4 collective-permute-start.21
  130.4 1.6 shard_map.116
  132.0 2.4 %shard_map.117 = (f32[64,2304]{1,0:T(8,128)S(1)}, f32[64,2304]{1,0:T(8,128)S(1)}, f32[64,2304]{1,0:T(8,128)S(1)}, f32[64,2304]{1,0:T(8,128)S(1)}) custom-call(s32[5]{0:T(128)S(1)} %copy-done.41, f32[128,144]{1,0:T(8,128)} %shard_map.115.refs_0_, f32[128,144]{1,0:T(8,128)} %collective-permute-done.22.refs_1_, f32[128,504]{1,0:T(8,128)S(1)} %get-tuple-element.108.refs_2_, ...), custom_call_target="tpu_custom_call" | custom-call | tf_op jit(solution)/shard_map/pallas_call | solution.py:555
  134.4 4.4 %shard_map.119 = (f32[64,4096]{1,0:T(8,128)S(1)}, f32[64,4096]{1,0:T(8,128)S(1)}) custom-call(s32[5]{0:T(128)S(1)} %copy-done.41, bf16[128,576]{1,0:T(8,128)(2,1)S(1)} %bitcast.11, bf16[72,4096]{1,0:T(8,128)(2,1)S(1)} %copy-done.15, bf16[72,4096]{1,0:T(8,128)(2,1)} %collective-permute-done.10.refs_1_, bf16[72,4096]{1,0:T(8,128)(2,1)S(1)} %copy-done.19, ...), custom_call_target="tpu_custom_call" | custom-call | tf_op jit(solution)/shard_map/pallas_call | solution.py:591
  138.9 2.1 %shard_map.118 = (f32[64,2304]{1,0:T(8,128)S(1)}, f32[64,2304]{1,0:T(8,128)S(1)}, f32[64,2304]{1,0:T(8,128)S(1)}, f32[64,2304]{1,0:T(8,128)S(1)}) custom-call(s32[5]{0:T(128)S(1)} %copy-done.41, f32[128,144]{1,0:T(8,128)S(1)} %shard_map.114.refs_0_, f32[128,144]{1,0:T(8,128)S(1)} %collective-permute-done.21.refs_1_, ...), custom_call_target="tpu_custom_call" | custom-call | tf_op jit(solution)/shard_map/pallas_call | solution.py:555
  141.0 2.0 %shard_map.120.refs_0_ = f32[128,144]{1,0:T(8,128)S(1)} custom-call(bf16[64,4096]{1,0:T(8,128)(2,1)S(1)} %bitcast.10, bf16[64,4096]{1,0:T(8,128)(2,1)S(1)} %collective-permute-done.11.send_ref, bf16[72,4096]{1,0:T(8,128)(2,1)} %collective-permute-done.18.refs_0_, bf16[72,4096]{1,0:T(8,128)(2,1)} %collective-permute-done.20.refs_1_), custom_call_target="tpu_custom_call" | custom-call | tf_op jit(solution)/shard_map/pallas_call | solution.py:551
  143.3 3.7 %collective-permute-done.23.refs_1_ = f32[128,144]{1,0:T(8,128)S(1)} collective-permute-done((f32[128,144]{1,0:T(8,128)S(1)}, f32[128,144]{1,0:T(8,128)S(1)}, u32[]{:S(2)}, u32[]{:S(2)}) %collective-permute-start.23) | collective-permute-done | bytes 73760 | tf_op jit(solution)/shard_map/ppermute | solution.py:416
  146.9 1.3 shard_map.121
  148.2 5.4 %collective-permute-start.24 = (bf16[64,2304]{1,0:T(8,128)(2,1)S(1)}, bf16[64,2304]{1,0:T(8,128)(2,1)S(1)}, u32[]{:S(2)}, u32[]{:S(2)}) collective-permute-start(bf16[64,2304]{1,0:T(8,128)(2,1)S(1)} %get-tuple-element.133), channel_id=1, source_target_pairs={{0,2},{2,0},{4,6},{6,4},{8,10},{10,8},{12,14},{14,12},{16,18},{18,... | collective-permute-start | bytes 884744 | tf_op jit(solution)/shard_map/ppermute | solution.py:408
  153.6 1.3 shard_map.123
  154.9 1.5 shard_map.122
  156.4 2.6 %collective-permute-start.27 = (bf16[256,576]{1,0:T(8,128)(2,1)S(1)}, bf16[256,576]{1,0:T(8,128)(2,1)S(1)}, u32[]{:S(2)}, u32[]{:S(2)}) collective-permute-start(bf16[256,576]{1,0:T(8,128)(2,1)S(1)} %get-tuple-element.146), channel_id=1, source_target_pairs={{2,0},{4,2},{6,4},{8,6},{10,8},{12,10},{14,12},{16,14},{18,16},{20... | collective-permute-start | bytes 884744 | tf_op jit(solution)/shard_map/ppermute | solution.py:391
  159.0 1.5 shard_map.124
  160.5 2.6 %shard_map.125 = (f32[64,4096]{1,0:T(8,128)S(1)}, bf16[64,4096]{1,0:T(8,128)(2,1)S(1)}) custom-call(s32[5]{0:T(128)S(1)} %get-tuple-element.140.facts_ref, bf16[128,576]{1,0:T(8,128)(2,1)S(1)} %bitcast.12, bf16[72,4096]{1,0:T(8,128)(2,1)} %collective-permute-done.18.refs_0_, bf16[72,4096]{1,0:T(8,128)(2,1)} %collective-permute-done.20.refs_1_, ...), custom_call_target="tpu_custom_call" | custom-call | flops 3019898880 | tf_op jit(solution)/shard_map/pallas_call | solution.py:591
  163.6 2.1 %collective-permute-done.27.odd_ref = bf16[256,576]{1,0:T(8,128)(2,1)S(1)} collective-permute-done((bf16[256,576]{1,0:T(8,128)(2,1)S(1)}, bf16[256,576]{1,0:T(8,128)(2,1)S(1)}, u32[]{:S(2)}, u32[]{:S(2)}) %collective-permute-start.27) | collective-permute-done | bytes 294944 | tf_op jit(solution)/shard_map/ppermute | solution.py:391
  165.7 0.9 shard_map.126
  166.9 2.3 %collective-permute-done.28 = f32[2,288]{1,0:T(2,128)S(1)} collective-permute-done((f32[2,288]{1,0:T(2,128)S(1)}, f32[2,288]{1,0:T(2,128)S(1)}, u32[]{:S(2)}, u32[]{:S(2)}) %collective-permute-start.28) | collective-permute-done | bytes 2336 | tf_op jit(solution)/shard_map/ppermute | solution.py:416
  169.2 4.5 %shard_map.127 = bf16[2,196,576]{2,1,0:T(8,128)(2,1)S(1)} custom-call(f32[256,576]{1,0:T(8,128)S(1)} %get-tuple-element.145.even_ref, bf16[256,576]{1,0:T(8,128)(2,1)S(1)} %collective-permute-done.27.odd_ref, f32[512,576]{1,0:T(8,128)S(1)} %copy-done.4, f32[2,576]{1,0:T(2,128)S(1)} %copy-done.46, f32[2,288]{1,0:T(2,128)S(1)} %copy-done.44, ...), custom_call_target="tpu_custom_call" | custom-call | flops 2717908992 | bytes 4718592 | tf_op jit(solution)/shard_map/pallas_call | solution.py:375
  173.6 1.2 copy.12
  174.8 0.9 add_convert_fusion
  (124 shorter events, 7.7 us)
Async XLA Ops:
  0.6 3.3 %copy-start.47 = (bf16[2,196,576]{2,0,1:T(2,128)(2,1)S(1)}, bf16[2,196,576]{2,0,1:T(2,128)(2,1)}, u32[]{:S(2)}) copy-start(bf16[2,196,576]{2,0,1:T(2,128)(2,1)} %param.9) | copy-start | bytes 1354756
  0.6 3.4 %copy-start.27 = (bf16[9,576,48]{1,2,0:T(8,128)(2,1)S(1)}, bf16[9,576,48]{1,2,0:T(8,128)(2,1)}, u32[]{:S(2)}) copy-start(bf16[9,576,48]{1,2,0:T(8,128)(2,1)} %param.10) | copy-start | bytes 1492996
  0.7 3.4 %copy-start.31 = (bf16[576,288]{0,1:T(8,128)(2,1)S(1)}, bf16[576,288]{0,1:T(8,128)(2,1)}, u32[]{:S(2)}) copy-start(bf16[576,288]{0,1:T(8,128)(2,1)} %param.11) | copy-start | bytes 995332
  2.4 9.6 %copy-start = (bf16[72,4608]{1,0:T(8,128)(2,1)}, bf16[72,4608]{1,0:T(8,128)(2,1)S(1)}, u32[]{:S(2)}) copy-start(bf16[72,4608]{1,0:T(8,128)(2,1)S(1)} %reshape.11.refs_0_.refs_4_) | copy-start | bytes 1990660
  2.4 8.9 %copy-start.23 = (bf16[288,576]{1,0:T(8,128)(2,1)S(1)}, bf16[288,576]{1,0:T(8,128)(2,1)}, u32[]{:S(2)}) copy-start(bf16[288,576]{1,0:T(8,128)(2,1)} %expand_ref.3) | copy-start | bytes 995332
  2.5 15.8 %collective-permute-start.2 = (bf16[72,4608]{1,0:T(8,128)(2,1)S(1)}, bf16[72,4608]{1,0:T(8,128)(2,1)S(1)}, u32[]{:S(2)}, u32[]{:S(2)}) collective-permute-start(bf16[72,4608]{1,0:T(8,128)(2,1)S(1)} %reshape.11.refs_0_.refs_4_), channel_id=1, source_target_pairs={{0,8},{2,10},{8,16},{10,18},{16,24},{18,26},{24,28},{26,30},{28,20... | collective-permute-start | bytes 1990664 | tf_op jit(solution)/shard_map/ppermute | solution.py:427
  2.5 15.9 %collective-permute-start.3 = (bf16[72,4608]{1,0:T(8,128)(2,1)S(1)}, bf16[72,4608]{1,0:T(8,128)(2,1)S(1)}, u32[]{:S(2)}, u32[]{:S(2)}) collective-permute-start(bf16[72,4608]{1,0:T(8,128)(2,1)S(1)} %reshape.11.refs_0_.refs_4_), channel_id=1, source_target_pairs={{0,4},{2,6},{8,0},{10,2},{16,8},{18,10},{24,16},{26,18},{28,24},{3... | collective-permute-start | bytes 1990664 | tf_op jit(solution)/shard_map/ppermute | solution.py:427
  8.5 9.9 %copy-start.3 = (f32[512,576]{1,0:T(8,128)}, f32[512,576]{1,0:T(8,128)S(1)}, u32[]{:S(2)}) copy-start(f32[512,576]{1,0:T(8,128)S(1)} %get-tuple-element.75.conv_ref) | copy-start | bytes 3538948
  8.5 2.8 %collective-permute-start = (f32[2,288]{1,0:T(2,128)S(1)}, f32[2,288]{1,0:T(2,128)S(1)}, u32[]{:S(2)}, u32[]{:S(2)}) collective-permute-start(f32[2,288]{1,0:T(2,128)S(1)} %get-tuple-element.78), channel_id=1, source_target_pairs={{0,1},{1,0},{2,3},{3,2},{4,5},{5,4},{6,7},{7,6},{8,9},{9,8},{10,11... | collective-permute-start | bytes 6920 | tf_op jit(solution)/shard_map/ppermute | solution.py:416
  11.3 8.6 %copy-start.43 = (f32[2,288]{1,0:T(2,128)}, f32[2,288]{1,0:T(2,128)S(1)}, u32[]{:S(2)}) copy-start(f32[2,288]{1,0:T(2,128)S(1)} %add.9.sq_ref) | copy-start | bytes 6916
  18.3 54.2 %copy-start.5 = (bf16[72,4608]{1,0:T(8,128)(2,1)}, bf16[72,4608]{1,0:T(8,128)(2,1)S(1)}, u32[]{:S(2)}) copy-start(bf16[72,4608]{1,0:T(8,128)(2,1)S(1)} %collective-permute-done.2.refs_1_.refs_4_) | copy-start | bytes 1990660
  18.4 54.1 %copy-start.11 = (bf16[72,4608]{1,0:T(8,128)(2,1)}, bf16[72,4608]{1,0:T(8,128)(2,1)S(1)}, u32[]{:S(2)}) copy-start(bf16[72,4608]{1,0:T(8,128)(2,1)S(1)} %collective-permute-done.3.refs_2_.refs_5_) | copy-start | bytes 1990660
  18.4 21.6 %collective-permute-start.4 = (bf16[72,4608]{1,0:T(8,128)(2,1)S(1)}, bf16[72,4608]{1,0:T(8,128)(2,1)S(1)}, u32[]{:S(2)}, u32[]{:S(2)}) collective-permute-start(bf16[72,4608]{1,0:T(8,128)(2,1)S(1)} %collective-permute-done.2.refs_1_.refs_4_), channel_id=1, source_target_pairs={{0,8},{2,10},{8,16},{10,18},{16,24},{18,26},{24,28},{26,30},{28,20... | collective-permute-start | bytes 1990664 | tf_op jit(solution)/shard_map/ppermute | solution.py:427
  19.5 20.4 %collective-permute-start.5 = (bf16[72,4608]{1,0:T(8,128)(2,1)S(1)}, bf16[72,4608]{1,0:T(8,128)(2,1)}, u32[]{:S(2)}, u32[]{:S(2)}) collective-permute-start(bf16[72,4608]{1,0:T(8,128)(2,1)S(1)} %collective-permute-done.3.refs_2_.refs_5_), channel_id=1, source_target_pairs={{0,4},{2,6},{8,0},{10,2},{16,8},{18,10},{24,16},{26,18},{28,24},{3... | collective-permute-start | bytes 1990664 | tf_op jit(solution)/shard_map/ppermute | solution.py:427
  19.8 19.4 %collective-permute-start.1 = (bf16[256,576]{1,0:T(8,128)(2,1)S(1)}, bf16[256,576]{1,0:T(8,128)(2,1)S(1)}, u32[]{:S(2)}, u32[]{:S(2)}) collective-permute-start(bf16[256,576]{1,0:T(8,128)(2,1)S(1)} %get-tuple-element.79), channel_id=1, source_target_pairs={{0,2},{2,4},{4,6},{6,8},{8,10},{10,12},{12,14},{14,16},{16,18},{18... | collective-permute-start | bytes 884744 | tf_op jit(solution)/shard_map/ppermute | solution.py:391
  26.2 48.1 %all-to-all-start = ((bf16[8,8,4096]{2,1,0:T(8,128)(2,1)}), bf16[8,8,4096]{2,1,0:T(8,128)(2,1)S(1)}, u32[]{:S(2)}, u32[]{:S(2)}) async-start(bf16[8,8,4096]{2,1,0:T(8,128)(2,1)} %bitcast.17), calls=%async_computation | async-start | bytes 1048576 | tf_op jit(solution)/shard_map/all_to_all | solution.py:605
  40.0 34.3 %copy-start.8 = (bf16[72,4608]{1,0:T(8,128)(2,1)}, bf16[72,4608]{1,0:T(8,128)(2,1)S(1)}, u32[]{:S(2)}) copy-start(bf16[72,4608]{1,0:T(8,128)(2,1)S(1)} %collective-permute-done.4.refs_3_.refs_4_) | copy-start | bytes 1990660
  40.0 34.3 %collective-permute-start.6 = (bf16[72,4608]{1,0:T(8,128)(2,1)S(1)}, bf16[72,4608]{1,0:T(8,128)(2,1)S(1)}, u32[]{:S(2)}, u32[]{:S(2)}) collective-permute-start(bf16[72,4608]{1,0:T(8,128)(2,1)S(1)} %collective-permute-done.4.refs_3_.refs_4_), channel_id=1, source_target_pairs={{0,8},{2,10},{8,16},{10,18},{16,24},{18,26},{24,28},{26,30},{28,20... | collective-permute-start | bytes 1990664 | tf_op jit(solution)/shard_map/ppermute | solution.py:427
  43.6 30.8 %collective-permute-start.7 = (bf16[72,4608]{1,0:T(8,128)(2,1)}, bf16[72,4608]{1,0:T(8,128)(2,1)}, u32[]{:S(2)}, u32[]{:S(2)}) collective-permute-start(bf16[72,4608]{1,0:T(8,128)(2,1)} %collective-permute-done.5.refs_4_.refs_5_), channel_id=1, source_target_pairs={{0,4},{2,6},{8,0},{10,2},{16,8},{18,10},{24,16},{26,18},{28,24},{3... | collective-permute-start | bytes 1990664 | tf_op jit(solution)/shard_map/ppermute | solution.py:427
  45.7 26.7 %collective-permute-start.10 = (bf16[72,4096]{1,0:T(8,128)(2,1)}, bf16[72,4096]{1,0:T(8,128)(2,1)}, u32[]{:S(2)}, u32[]{:S(2)}) collective-permute-start(bf16[72,4096]{1,0:T(8,128)(2,1)} %refs_0_.1), channel_id=1, source_target_pairs={{0,4},{2,6},{8,0},{10,2},{16,8},{18,10},{24,16},{26,18},{28,24},{3... | collective-permute-start | bytes 1769480 | tf_op jit(solution)/shard_map/ppermute | solution.py:427
  47.2 25.3 %collective-permute-start.9 = (bf16[72,4096]{1,0:T(8,128)(2,1)}, bf16[72,4096]{1,0:T(8,128)(2,1)S(1)}, u32[]{:S(2)}, u32[]{:S(2)}) collective-permute-start(bf16[72,4096]{1,0:T(8,128)(2,1)} %refs_0_.1), channel_id=1, source_target_pairs={{0,8},{2,10},{8,16},{10,18},{16,24},{18,26},{24,28},{26,30},{28,20... | collective-permute-start | bytes 1769480 | tf_op jit(solution)/shard_map/ppermute | solution.py:427
  50.9 21.6 %collective-permute-start.8 = (bf16[64,4608]{1,0:T(8,128)(2,1)S(1)}, bf16[64,4608]{1,0:T(8,128)(2,1)S(1)}, u32[]{:S(2)}, u32[]{:S(2)}) collective-permute-start(bf16[64,4608]{1,0:T(8,128)(2,1)S(1)} %shard_map.107.own_ref), channel_id=1, source_target_pairs={{0,2},{2,0},{4,6},{6,4},{8,10},{10,8},{12,14},{14,12},{16,18},{18,... | collective-permute-start | bytes 1769480 | tf_op jit(solution)/shard_map/ppermute | solution.py:408
  74.3 20.9 %collective-permute-start.14 = (bf16[72,4608]{1,0:T(8,128)(2,1)S(1)}, bf16[72,4608]{1,0:T(8,128)(2,1)S(1)}, u32[]{:S(2)}, u32[]{:S(2)}) collective-permute-start(bf16[72,4608]{1,0:T(8,128)(2,1)S(1)} %collective-permute-done.6.refs_5_.refs_4_), channel_id=1, source_target_pairs={{0,8},{2,10},{8,16},{10,18},{16,24},{18,26},{24,28},{26,30},{28,20... | collective-permute-start | bytes 1990664 | tf_op jit(solution)/shard_map/ppermute | solution.py:427
  74.4 20.8 %collective-permute-start.15 = (bf16[72,4096]{1,0:T(8,128)(2,1)}, bf16[72,4096]{1,0:T(8,128)(2,1)S(1)}, u32[]{:S(2)}, u32[]{:S(2)}) collective-permute-start(bf16[72,4096]{1,0:T(8,128)(2,1)} %collective-permute-done.10.refs_1_), channel_id=1, source_target_pairs={{0,4},{2,6},{8,0},{10,2},{16,8},{18,10},{24,16},{26,18},{28,24},{3... | collective-permute-start | bytes 1769480 | tf_op jit(solution)/shard_map/ppermute | solution.py:427
  79.5 9.7 %collective-permute-start.11 = (bf16[64,4096]{1,0:T(8,128)(2,1)S(1)}, bf16[64,4096]{1,0:T(8,128)(2,1)S(1)}, u32[]{:S(2)}, u32[]{:S(2)}) collective-permute-start(bf16[64,4096]{1,0:T(8,128)(2,1)S(1)} %bitcast.6), channel_id=1, source_target_pairs={{0,2},{2,0},{4,6},{6,4},{8,10},{10,8},{12,14},{14,12},{16,18},{18,... | collective-permute-start | bytes 1572872 | tf_op jit(solution)/shard_map/ppermute | solution.py:408
  83.9 5.0 %copy-start.17 = (bf16[72,4096]{1,0:T(8,128)(2,1)S(1)}, bf16[72,4096]{1,0:T(8,128)(2,1)}, u32[]{:S(2)}) copy-start(bf16[72,4096]{1,0:T(8,128)(2,1)} %copy-done.16) | copy-start | bytes 1769476
  83.9 5.4 %copy-start.14 = (bf16[72,4096]{1,0:T(8,128)(2,1)S(1)}, bf16[72,4096]{1,0:T(8,128)(2,1)}, u32[]{:S(2)}) copy-start(bf16[72,4096]{1,0:T(8,128)(2,1)} %refs_0_.1) | copy-start | bytes 1769476
  87.7 7.5 %collective-permute-start.13 = (f32[128,504]{1,0:T(8,128)S(1)}, f32[128,504]{1,0:T(8,128)S(1)}, u32[]{:S(2)}, u32[]{:S(2)}) collective-permute-start(f32[128,504]{1,0:T(8,128)S(1)} %shard_map.109.own_ref), channel_id=1, source_target_pairs={{0,1},{1,0},{2,3},{3,2},{4,5},{5,4},{6,7},{7,6},{8,9},{9,8},{10,11... | collective-permute-start | bytes 774152 | tf_op jit(solution)/shard_map/ppermute | solution.py:416
  89.0 18.2 %collective-permute-start.12 = (bf16[72,4096]{1,0:T(8,128)(2,1)S(1)}, bf16[72,4096]{1,0:T(8,128)(2,1)}, u32[]{:S(2)}, u32[]{:S(2)}) collective-permute-start(bf16[72,4096]{1,0:T(8,128)(2,1)S(1)} %copy-done.17), channel_id=1, source_target_pairs={{0,8},{2,10},{8,16},{10,18},{16,24},{18,26},{24,28},{26,30},{28,20... | collective-permute-start | bytes 1769480 | tf_op jit(solution)/shard_map/ppermute | solution.py:427
  91.1 13.4 %copy-start.29 = (f32[128,144]{1,0:T(8,128)}, f32[128,144]{1,0:T(8,128)S(1)}, u32[]{:S(2)}) copy-start(f32[128,144]{1,0:T(8,128)S(1)} %shard_map.110.refs_0_) | copy-start | bytes 221188
  91.1 8.0 %copy-start.40 = (s32[5]{0:T(128)S(1)}, s32[5]{0:T(128)}, u32[]{:S(2)}) copy-start(s32[5]{0:T(128)} %shard_map.104.facts_ref) | copy-start | bytes 64
  95.2 9.3 %copy-start.20 = (bf16[72,4096]{1,0:T(8,128)(2,1)}, bf16[72,4096]{1,0:T(8,128)(2,1)S(1)}, u32[]{:S(2)}) copy-start(bf16[72,4096]{1,0:T(8,128)(2,1)S(1)} %collective-permute-done.15.refs_1_.refs_3_) | copy-start | bytes 1769476
  95.2 13.7 %collective-permute-start.19 = (bf16[72,4096]{1,0:T(8,128)(2,1)S(1)}, bf16[72,4096]{1,0:T(8,128)(2,1)}, u32[]{:S(2)}, u32[]{:S(2)}) collective-permute-start(bf16[72,4096]{1,0:T(8,128)(2,1)S(1)} %collective-permute-done.15.refs_1_.refs_3_), channel_id=1, source_target_pairs={{0,4},{2,6},{8,0},{10,2},{16,8},{18,10},{24,16},{26,18},{28,24},{3... | collective-permute-start | bytes 1769480 | tf_op jit(solution)/shard_map/ppermute | solution.py:427
  97.2 10.1 %collective-permute-start.17 = (f32[128,144]{1,0:T(8,128)S(1)}, f32[128,144]{1,0:T(8,128)S(1)}, u32[]{:S(2)}, u32[]{:S(2)}) collective-permute-start(f32[128,144]{1,0:T(8,128)S(1)} %shard_map.110.refs_0_), channel_id=1, source_target_pairs={{0,1},{1,0},{2,3},{3,2},{4,5},{5,4},{6,7},{7,6},{8,9},{9,8},{10,11... | collective-permute-start | bytes 221192 | tf_op jit(solution)/shard_map/ppermute | solution.py:416
  98.9 4.1 %collective-permute-start.16 = (f32[128,72]{1,0:T(8,128)S(1)}, f32[128,72]{1,0:T(8,128)S(1)}, u32[]{:S(2)}, u32[]{:S(2)}) collective-permute-start(f32[128,72]{1,0:T(8,128)S(1)} %shard_map.111.own_ref), channel_id=1, source_target_pairs={{0,1},{1,0},{2,3},{3,2},{4,5},{5,4},{6,7},{7,6},{8,9},{9,8},{10,11... | collective-permute-start | bytes 110600 | tf_op jit(solution)/shard_map/ppermute | solution.py:416
  107.9 33.1 %collective-permute-start.18 = (bf16[72,4096]{1,0:T(8,128)(2,1)}, bf16[72,4096]{1,0:T(8,128)(2,1)}, u32[]{:S(2)}, u32[]{:S(2)}) collective-permute-start(bf16[72,4096]{1,0:T(8,128)(2,1)} %collective-permute-done.12.refs_0_.refs_4_), channel_id=1, source_target_pairs={{0,8},{2,10},{8,16},{10,18},{16,24},{18,26},{24,28},{26,30},{28,20... | collective-permute-start | bytes 1769480 | tf_op jit(solution)/shard_map/ppermute | solution.py:427
  108.9 32.1 %collective-permute-start.20 = (bf16[72,4096]{1,0:T(8,128)(2,1)}, bf16[72,4096]{1,0:T(8,128)(2,1)}, u32[]{:S(2)}, u32[]{:S(2)}) collective-permute-start(bf16[72,4096]{1,0:T(8,128)(2,1)} %collective-permute-done.19.refs_1_.refs_5_), channel_id=1, source_target_pairs={{0,4},{2,6},{8,0},{10,2},{16,8},{18,10},{24,16},{26,18},{28,24},{3... | collective-permute-start | bytes 1769480 | tf_op jit(solution)/shard_map/ppermute | solution.py:427
  110.8 16.0 %all-to-all-start.1 = ((bf16[8,16,576]{2,1,0:T(8,128)(2,1)}), bf16[8,16,576]{2,1,0:T(8,128)(2,1)S(1)}, u32[]{:S(2)}, u32[]{:S(2)}) async-start(bf16[8,16,576]{2,1,0:T(8,128)(2,1)} %bitcast.4), calls=%async_computation.1 | async-start | bytes 327680 | tf_op jit(solution)/shard_map/all_to_all | solution.py:605
  118.9 11.5 %copy-start.2 = (bf16[72,4608]{1,0:T(8,128)(2,1)S(1)}, bf16[72,4608]{1,0:T(8,128)(2,1)}, u32[]{:S(2)}) copy-start(bf16[72,4608]{1,0:T(8,128)(2,1)} %copy-done) | copy-start | bytes 1990660
  118.9 11.5 %copy-start.41 = (s32[5]{0:T(128)S(1)}, s32[5]{0:T(128)}, u32[]{:S(2)}) copy-start(s32[5]{0:T(128)} %shard_map.104.facts_ref) | copy-start | bytes 64
  118.9 13.1 %collective-permute-start.22 = (f32[128,144]{1,0:T(8,128)}, f32[128,144]{1,0:T(8,128)}, u32[]{:S(2)}, u32[]{:S(2)}) collective-permute-start(f32[128,144]{1,0:T(8,128)} %shard_map.115.refs_0_), channel_id=1, source_target_pairs={{0,1},{1,0},{2,3},{3,2},{4,5},{5,4},{6,7},{7,6},{8,9},{9,8},{10,11... | collective-permute-start | bytes 221192 | tf_op jit(solution)/shard_map/ppermute | solution.py:416
  126.9 7.5 %copy-start.25 = (bf16[8,16,576]{2,1,0:T(8,128)(2,1)}, bf16[8,16,576]{2,1,0:T(8,128)(2,1)S(1)}, u32[]{:S(2)}) copy-start(bf16[8,16,576]{2,1,0:T(8,128)(2,1)S(1)} %all-to-all-done.1) | copy-start | bytes 442372
  126.9 3.5 %copy-start.13 = (bf16[72,4608]{1,0:T(8,128)(2,1)S(1)}, bf16[72,4608]{1,0:T(8,128)(2,1)}, u32[]{:S(2)}) copy-start(bf16[72,4608]{1,0:T(8,128)(2,1)} %copy-done.11) | copy-start | bytes 1990660
  126.9 3.5 %copy-start.30 = (f32[128,144]{1,0:T(8,128)S(1)}, f32[128,144]{1,0:T(8,128)}, u32[]{:S(2)}) copy-start(f32[128,144]{1,0:T(8,128)} %copy-done.29) | copy-start | bytes 221188
  126.9 3.5 %copy-start.38 = (f32[128,144]{1,0:T(8,128)S(1)}, f32[128,144]{1,0:T(8,128)}, u32[]{:S(2)}) copy-start(f32[128,144]{1,0:T(8,128)} %copy-done.37) | copy-start | bytes 221188
  129.0 3.0 %copy-start.7 = (bf16[72,4608]{1,0:T(8,128)(2,1)S(1)}, bf16[72,4608]{1,0:T(8,128)(2,1)}, u32[]{:S(2)}) copy-start(bf16[72,4608]{1,0:T(8,128)(2,1)} %copy-done.5) | copy-start | bytes 1990660
  129.0 9.9 %collective-permute-start.21 = (f32[128,144]{1,0:T(8,128)S(1)}, f32[128,144]{1,0:T(8,128)S(1)}, u32[]{:S(2)}, u32[]{:S(2)}) collective-permute-start(f32[128,144]{1,0:T(8,128)S(1)} %shard_map.114.refs_0_), channel_id=1, source_target_pairs={{0,1},{1,0},{2,3},{3,2},{4,5},{5,4},{6,7},{7,6},{8,9},{9,8},{10,11... | collective-permute-start | bytes 221192 | tf_op jit(solution)/shard_map/ppermute | solution.py:416
  132.0 2.4 %copy-start.15 = (bf16[72,4096]{1,0:T(8,128)(2,1)S(1)}, bf16[72,4096]{1,0:T(8,128)(2,1)}, u32[]{:S(2)}) copy-start(bf16[72,4096]{1,0:T(8,128)(2,1)} %refs_0_.1) | copy-start | bytes 1769476
  132.0 2.4 %copy-start.19 = (bf16[72,4096]{1,0:T(8,128)(2,1)S(1)}, bf16[72,4096]{1,0:T(8,128)(2,1)}, u32[]{:S(2)}) copy-start(bf16[72,4096]{1,0:T(8,128)(2,1)} %copy-done.16) | copy-start | bytes 1769476
  134.4 4.4 %copy-start.10 = (bf16[72,4608]{1,0:T(8,128)(2,1)S(1)}, bf16[72,4608]{1,0:T(8,128)(2,1)}, u32[]{:S(2)}) copy-start(bf16[72,4608]{1,0:T(8,128)(2,1)} %copy-done.8) | copy-start | bytes 1990660
  143.0 10.5 %copy-start.42 = (s32[5]{0:T(128)S(1)}, s32[5]{0:T(128)}, u32[]{:S(2)}) copy-start(s32[5]{0:T(128)} %shard_map.104.facts_ref) | copy-start | bytes 64
  143.0 3.9 %collective-permute-start.23 = (f32[128,144]{1,0:T(8,128)S(1)}, f32[128,144]{1,0:T(8,128)S(1)}, u32[]{:S(2)}, u32[]{:S(2)}) collective-permute-start(f32[128,144]{1,0:T(8,128)S(1)} %shard_map.120.refs_0_), channel_id=1, source_target_pairs={{0,1},{1,0},{2,3},{3,2},{4,5},{5,4},{6,7},{7,6},{8,9},{9,8},{10,11... | collective-permute-start | bytes 221192 | tf_op jit(solution)/shard_map/ppermute | solution.py:416
  148.2 6.8 %collective-permute-start.24 = (bf16[64,2304]{1,0:T(8,128)(2,1)S(1)}, bf16[64,2304]{1,0:T(8,128)(2,1)S(1)}, u32[]{:S(2)}, u32[]{:S(2)}) collective-permute-start(bf16[64,2304]{1,0:T(8,128)(2,1)S(1)} %get-tuple-element.133), channel_id=1, source_target_pairs={{0,2},{2,0},{4,6},{6,4},{8,10},{10,8},{12,14},{14,12},{16,18},{18,... | collective-permute-start | bytes 884744 | tf_op jit(solution)/shard_map/ppermute | solution.py:408
  154.8 5.7 %copy-start.26 = (bf16[8,16,576]{2,1,0:T(8,128)(2,1)S(1)}, bf16[8,16,576]{2,1,0:T(8,128)(2,1)}, u32[]{:S(2)}) copy-start(bf16[8,16,576]{2,1,0:T(8,128)(2,1)} %copy-done.25) | copy-start | bytes 442372
  154.8 4.2 %collective-permute-start.25 = (bf16[64,2304]{1,0:T(8,128)(2,1)S(1)}, bf16[64,2304]{1,0:T(8,128)(2,1)S(1)}, u32[]{:S(2)}, u32[]{:S(2)}) collective-permute-start(bf16[64,2304]{1,0:T(8,128)(2,1)S(1)} %get-tuple-element.139), channel_id=1, source_target_pairs={{0,2},{2,0},{4,6},{6,4},{8,10},{10,8},{12,14},{14,12},{16,18},{18,... | collective-permute-start | bytes 884744 | tf_op jit(solution)/shard_map/ppermute | solution.py:408
  156.4 9.3 %collective-permute-start.27 = (bf16[256,576]{1,0:T(8,128)(2,1)S(1)}, bf16[256,576]{1,0:T(8,128)(2,1)S(1)}, u32[]{:S(2)}, u32[]{:S(2)}) collective-permute-start(bf16[256,576]{1,0:T(8,128)(2,1)S(1)} %get-tuple-element.146), channel_id=1, source_target_pairs={{2,0},{4,2},{6,4},{8,6},{10,8},{12,10},{14,12},{16,14},{18,16},{20... | collective-permute-start | bytes 884744 | tf_op jit(solution)/shard_map/ppermute | solution.py:391
  160.5 5.2 %copy-start.4 = (f32[512,576]{1,0:T(8,128)S(1)}, f32[512,576]{1,0:T(8,128)}, u32[]{:S(2)}) copy-start(f32[512,576]{1,0:T(8,128)} %copy-done.3) | copy-start | bytes 3538948
  160.5 5.2 %copy-start.24 = (bf16[288,576]{1,0:T(8,128)(2,1)S(1)}, bf16[288,576]{1,0:T(8,128)(2,1)}, u32[]{:S(2)}) copy-start(bf16[288,576]{1,0:T(8,128)(2,1)} %expand_ref.3) | copy-start | bytes 995332
  160.5 5.2 %copy-start.46 = (f32[2,576]{1,0:T(2,128)S(1)}, f32[2,576]{1,0:T(2,128)}, u32[]{:S(2)}) copy-start(f32[2,576]{1,0:T(2,128)} %copy-done.45) | copy-start | bytes 13828
  163.1 11.7 %collective-permute-start.26 = (bf16[64,4096]{1,0:T(8,128)(2,1)S(1)}, bf16[64,4096]{1,0:T(8,128)(2,1)S(1)}, u32[]{:S(2)}, u32[]{:S(2)}) collective-permute-start(bf16[64,4096]{1,0:T(8,128)(2,1)S(1)} %get-tuple-element.144), channel_id=1, source_target_pairs={{0,2},{2,0},{4,6},{6,4},{8,10},{10,8},{12,14},{14,12},{16,18},{18,... | collective-permute-start | bytes 1572872 | tf_op jit(solution)/shard_map/ppermute | solution.py:408
  165.7 3.5 %copy-start.28 = (bf16[9,576,48]{1,2,0:T(8,128)(2,1)S(1)}, bf16[9,576,48]{1,2,0:T(8,128)(2,1)}, u32[]{:S(2)}) copy-start(bf16[9,576,48]{1,2,0:T(8,128)(2,1)} %param.10) | copy-start | bytes 1492996
  165.7 3.4 %copy-start.32 = (bf16[576,288]{0,1:T(8,128)(2,1)S(1)}, bf16[576,288]{0,1:T(8,128)(2,1)}, u32[]{:S(2)}) copy-start(bf16[576,288]{0,1:T(8,128)(2,1)} %param.11) | copy-start | bytes 995332
  165.7 3.4 %copy-start.44 = (f32[2,288]{1,0:T(2,128)S(1)}, f32[2,288]{1,0:T(2,128)}, u32[]{:S(2)}) copy-start(f32[2,288]{1,0:T(2,128)} %copy-done.43) | copy-start | bytes 6916
  166.7 2.5 %collective-permute-start.28 = (f32[2,288]{1,0:T(2,128)S(1)}, f32[2,288]{1,0:T(2,128)S(1)}, u32[]{:S(2)}, u32[]{:S(2)}) collective-permute-start(f32[2,288]{1,0:T(2,128)S(1)} %shard_map.126), channel_id=1, source_target_pairs={{0,1},{1,0},{2,3},{3,2},{4,5},{5,4},{6,7},{7,6},{8,9},{9,8},{10,11... | collective-permute-start | bytes 6920 | tf_op jit(solution)/shard_map/ppermute | solution.py:416
  (15 other events, 15.0 us)

commit v9 on v8

--- a/solution.py
+++ b/solution.py
@@ -443,6 +443,13 @@
     out_ref[...] = jnp.concatenate([contract_last(back, ref[...]) for ref in blocks], axis=1)
 
 
+def late_kernel(facts_ref, keep_ref, send_ref, *refs):
+    *refs, out_ref, facts_out_ref = refs
+    for place in range(facts_ref.shape[0]):
+        facts_out_ref[place] = facts_ref[place]
+    back_kernel(keep_ref, send_ref, *refs, out_ref)
+
+
 def live_rows(facts_ref, rows, unit):
     block, token = token_place(
         lax.broadcasted_iota(jnp.int32, (rows, 1), 0), facts_ref[0], unit
@@ -519,11 +526,10 @@
     out_ref[...] = total
 
 
-def token_kernel(offsets, chips, unit, first, facts_ref, act_ref, *refs):
-    count, held = len(offsets), 2 if first else 4
+def token_kernel(offsets, chips, unit, facts_ref, act_ref, *refs):
+    count = len(offsets)
     blocks, refs = refs[:count], refs[count:]
-    before, after = refs[: held - 2], refs[held - 2 : held]
-    buffers, sems = refs[held:-1], refs[-1]
+    keep_ref, send_ref, *buffers, sems = refs
     copies = [
         pltpu.make_async_copy(ref, buffer, sems.at[place])
         for place, (ref, buffer) in enumerate(zip(blocks, buffers))
@@ -539,16 +545,29 @@
         piece = contract_last(act, columns).astype(jnp.bfloat16)
         copy.wait()
         total += jnp.dot(piece, buffer[...], preferred_element_type=jnp.float32)
-    rows = after[0].shape[0]
-    for half, ref in enumerate(after):
-        value = total[half * rows : (half + 1) * rows]
-        value = value if first else before[half][...] + value
-        ref[...] = value.astype(ref.dtype)
+    rows = keep_ref.shape[0]
+    keep_ref[...] = total[:rows]
+    send_ref[...] = total[rows:].astype(jnp.bfloat16)
 
 
 def block_products(kernel, left, blocks):
     rows = 2 * OUT_SIDE * OUT_SIDE
     return whole_call(kernel, f32(rows, len(blocks) * blocks[0].shape[0]), [])(*left, *blocks)
+
+
+def late_products(facts, back, blocks):
+    rows = 2 * OUT_SIDE * OUT_SIDE
+    return pl.pallas_call(
+        late_kernel,
+        out_shape=(
+            f32(rows, len(blocks) * blocks[0].shape[0]),
+            jax.ShapeDtypeStruct(facts.shape, jnp.int32),
+        ),
+        in_specs=vmem_specs(2 + len(blocks)),
+        out_specs=vmem_specs(1)[::-1],
+        compiler_params=pltpu.CompilerParams(vmem_limit_bytes=VMEM_BYTES),
+        cost_estimate=FREE,
+    )(facts, *back, *blocks)
 
 
 def facts_call(kernel, outs, facts, operands, cost=FREE):
@@ -578,25 +597,17 @@
     return facts_call(kernel, outs, facts, (*terms, *before))
 
 
-def add_tokens(facts, act, offsets, chips, blocks, before, unit):
+def token_products(facts, act, offsets, chips, blocks, unit):
     rows, columns = act.shape[0] // 2, blocks[0].shape[1]
-    kernel = functools.partial(token_kernel, offsets, chips, unit, not before)
-    cost = pl.CostEstimate(
-        flops=40 * len(blocks) * act.shape[1] * act.shape[0] * columns // chips,
-        bytes_accessed=0,
-        transcendentals=0,
-    )
-    vmem = pl.BlockSpec(memory_space=pltpu.VMEM)
-    anywhere = pl.BlockSpec(memory_space=pl.ANY)
     return pl.pallas_call(
-        kernel,
-        out_shape=(f32(rows, columns), (bf16 if before else f32)(rows, columns)),
-        in_specs=vmem_specs(1) + [anywhere] * len(blocks) + [vmem] * len(before),
+        functools.partial(token_kernel, offsets, chips, unit),
+        out_shape=(f32(rows, columns), bf16(rows, columns)),
+        in_specs=vmem_specs(1) + [pl.BlockSpec(memory_space=pl.ANY)] * len(blocks),
         scratch_shapes=[pltpu.VMEM(block.shape, block.dtype) for block in blocks]
         + [pltpu.SemaphoreType.DMA((len(blocks),))],
         compiler_params=pltpu.CompilerParams(vmem_limit_bytes=VMEM_BYTES),
-        cost_estimate=cost if before else FREE,
-    )(facts, act, *blocks, *before)
+        cost_estimate=FREE,
+    )(facts, act, *blocks)
 
 
 def chips_exchange(value):
@@ -642,62 +653,58 @@
         s_down.append(ring_send(s_down[-1], -1))
         if step == 2:
             halo, s_up[2], s_down[2] = tie(halo, s_up[2], s_down[2])
-            r_up = [readout_kernel, ring_send(readout_kernel, 1)]
             r_down = [readout_kernel, ring_send(readout_kernel, -1)]
             patches = take_patches(facts, halo, even)
-            mate_patches, r_up[1], r_down[1] = tie(swap_cores(patches), r_up[1], r_down[1])
-            patches = order_rows(facts, patches, mate_patches, unit)
-            r_down.append(ring_send(r_down[1], -1))
-    held = tie(s_up[-1], s_down[-1], r_up[1], back, patches)
-    s_up[-1], s_down[-1], r_up[1], back, patches = held
+            patches = order_rows(facts, patches, swap_cores(patches), unit)
+    s_up[-1], s_down[-1], back, readout_kernel = tie(s_up[-1], s_down[-1], back, readout_kernel)
     back = (back, swap_cores(back))
     s_last = ring_send(s_up[-1], 1)
+    r_up = [readout_kernel, ring_send(readout_kernel, 1)]
     samplers = [flat_sampler] + [block for pair in zip(s_up[1:], s_down[1:]) for block in pair]
     offsets = ring_offsets(chips)
-    first_pre = block_products(pre_kernel, (patches,), samplers)
-    r_up.append(ring_send(r_up[1], 1))
-    sums = block_products(back_kernel, back, [r_up[0], r_down[1]])
-    held = tie(*tp_terms(first_pre), sums, s_last, r_down[2])
-    first_pre, sums, s_last, r_down[2] = held[:2], *held[2:]
-    first_slope, first_act = act_and_slope(facts, first_pre, offsets[:-1], chips, (), unit)
-    last_pre = tp_terms(block_products(pre_kernel, (patches,), [s_last]))
-    last_slope, act = act_and_slope(facts, last_pre, offsets[-1:], chips, (first_act,), unit)
+    count = 2 * steps - 3
+    first_pre = tp_terms(block_products(pre_kernel, (patches,), samplers[:count]))
+    r_down[1], s_last, *first_pre = tie(r_down[1], s_last, *first_pre)
+    for step in range(1, steps - 2):
+        r_down.append(ring_send(r_down[-1], -1))
+        r_up.append(ring_send(r_up[-1], 1))
+    first_slope, first_act = act_and_slope(facts, first_pre, offsets[:count], chips, (), unit)
+    last_pre = block_products(pre_kernel, (patches,), [*samplers[count:], s_last])
+    last_slope, act = act_and_slope(
+        facts, tp_terms(last_pre), offsets[count:], chips, (first_act,), unit
+    )
     slopes = first_slope, last_slope
-    r_up[2], act, *terms = tie(r_up[2], act, *tp_terms(sums))
+    r_down[-1], act = tie(r_down[-1], act)
+    r_down.append(ring_send(r_down[-1], -1))
+    early = r_down[: steps - 1]
+    sums = block_products(back_kernel, back, early)
+    r_up[-1], act, sums = tie(r_up[-1], act, sums)
+    r_up.append(ring_send(r_up[-1], 1))
     act = chips_exchange(act)
     halo_lanes, even_lanes = slice(0, 4 * chans), slice(4 * chans, 8 * chans)
-    grads = ()
-    pieces, blocks = [(0, 0), (0, 2)], [samplers[0], samplers[2]]
-    for step in range(2, steps):
-        r_down.append(ring_send(r_down[step], -1))
-        group = r_up[step - 1], r_down[step]
-        if step == steps - 1:
-            *group, act = tie(*group, act)
-        sums = block_products(back_kernel, back, group)
-        grads = add_gradients(
-            facts, terms, slopes, pieces, blocks, grads, unit, (halo_lanes, even_lanes), False
-        )
-        if step < steps - 1:
-            if step > 2:
-                r_up[step], sums, *grads = tie(r_up[step], sums, *grads)
-            r_up.append(ring_send(r_up[step], 1))
-        terms = tp_terms(sums)
-        pieces = [(0, 2 * step - 3), (0, 2 * step)]
-        blocks = [samplers[2 * step - 3], samplers[2 * step]]
-    grads = add_gradients(
-        facts, terms, slopes, pieces, blocks, grads, unit, (halo_lanes, even_lanes), False
-    )
-    places, blocks = [0], [r_up[0]]
-    for step in range(1, steps):
-        places, blocks = places + [step], blocks + [r_down[step]]
-        if step < steps - 1:
-            places, blocks = places + [-step], blocks + [r_up[step]]
-    tokens = add_tokens(facts, act, places, chips, blocks, (), unit)
-
-    held = tie(r_up[-1], r_down[-1], *grads, *tokens)
-    late, grads, tokens = held[:2], held[2:6], held[6:]
-    terms = tp_terms(block_products(back_kernel, back, late))
-    pieces, blocks = [(0, 2 * steps - 3), (1, 0)], [samplers[2 * steps - 3], s_last]
+    both = halo_lanes, even_lanes
+    terms = tp_terms(sums)
+    pieces = [(0, 2 * step) for step in range(steps - 1)]
+    blocks = [flat_sampler] + s_down[1 : steps - 1]
+    grads = add_gradients(facts, terms, slopes, pieces, blocks, (), unit, both, False)
+    middle = r_up[1 : steps - 1] + [r_down[steps - 1]]
+    *middle, act = tie(*middle, act)
+    r_down.append(ring_send(r_down[-1], -1))
+    terms = tp_terms(block_products(back_kernel, back, middle))
+    pieces = [(0, 2 * step - 1) for step in range(1, steps - 1)] + [(1, 1)]
+    blocks = s_up[1 : steps - 1] + [s_down[steps - 1]]
+    grads = add_gradients(facts, terms, slopes, pieces, blocks, grads, unit, both, False)
+
+    late_up, late_down, *grads = tie(r_up[-1], r_down[-1], *grads)
+    sums, facts_late = late_products(facts, back, [late_up, late_down])
+    terms = tp_terms(sums)
+    places = [*range(steps - 1), *range(-1, 1 - steps, -1), steps - 1, 1 - steps, steps]
+    tokens = token_products(
+        facts_late, act, places, chips, [*early, *middle, late_up, late_down], unit
+    )
+    other_term, *tokens = tie(terms[1], *tokens)
+    terms = terms[0], other_term
+    pieces, blocks = [(1, 0), (1, 2)], [s_up[-1], s_last]
     halo_own, halo_mate = add_gradients(
         facts, terms, slopes, pieces, blocks, grads[:2], unit, (halo_lanes,), True
     )
@@ -707,14 +714,11 @@
     )
     lead, facts_late = return_patches(facts, halo_own, swap_cores(halo_mate), chans, jnp.bfloat16)
     grad_odd = shifted(lead, "ctx", -1)
-    grad_even, facts_late = return_patches(
+    grad_even, _ = return_patches(
         facts_late, even_own, swap_cores(even_mate), chans, jnp.float32
     )
     grad_relaxed = sum_tp(excite_grad(grad_even, grad_odd, conv, excite, squeeze_out))
-    tokens, send = add_tokens(
-        facts_late, act, [1 - steps, steps], chips, late, tokens, unit
-    )
-    llm_tokens = (tokens + swap_cores(send).astype(jnp.float32)).astype(jnp.bfloat16)
+    llm_tokens = (tokens[0] + swap_cores(tokens[1]).astype(jnp.float32)).astype(jnp.bfloat16)
     grad_features = conv_backward(
         grad_even, grad_odd, conv, excite, squeezed, grad_relaxed, squeeze_in, group_kernel
     )

time: 177 us -> 174 us (0.983)
  local copies, waits for them, and re-layouts: 15.7 us -> 7.99 us
  waiting for transfers between devices: 58.9 us -> 66.4 us
    ppermute x14, waiting for transfers between devices: 27.5 us -> 39.6 us  [ring_send(): return lax.ppermute(value, 'ctx', ring_pairs(lax.axis_size('ctx'), by))]
    ppermute x8 -> x7, waiting for transfers between devices: 14.2 us -> 2.92 us  [tp_terms(): other = lax.ppermute(value, 'tp', [(i, i ^ reach) for i in range(size)])]
    unnamed x98 -> x64, local copies, waits for them, and re-layouts: 13.9 us -> 6.26 us
    pallas_call x6 -> x4, Pallas kernels: 11.5 us -> 8.49 us  [block_products(): whole_call(kernel, f32(rows, len(blocks) * blocks[0].shape[0]), [])]
    ppermute x2, waiting for transfers between devices: 10.4 us -> 13.2 us  [shifted(): return lax.ppermute(value, axis, pairs)]
    all_to_all x2, waiting for transfers between devices: 6.74 us -> 9.16 us  [chips_exchange(): lax.all_to_all(value, 'ctx', split_axis=0, concat_axis=0, tiled=True, axi...]
    pallas_call x7 -> x6, Pallas kernels: 11.3 us -> 9.65 us  [facts_call(): pl.pallas_call(kernel, out_shape=outs, in_specs=vmem_specs(len(operands))...]
    ppermute x8 -> x7, starting transfers between devices: 7.18 us -> 7.93 us  [tp_terms(): other = lax.ppermute(value, 'tp', [(i, i ^ reach) for i in range(size)])]
  transfers between devices with their start and end apart: 31 -> 30, of which waited for: 13 -> 17; matrix products, arithmetic and copies ran while one was open for 1% -> 1% of each run, Pallas kernels for 25% -> 21%
where the time goes in v9:
time: 174 us; the launch traced here: 173 us
  waiting for transfers between devices  66.4 us (38%)
  starting transfers between devices  51.6 us (30%)
  Pallas kernels  45.2 us (26%)
  local copies, waits for them, and re-layouts  7.99 us (5%)
    ppermute x14, waiting for transfers between devices, ring_send(): return lax.ppermute(value, 'ctx', ring_pairs(lax.axis_size('ctx'), by))  39.6 us
    ppermute x14, starting transfers between devices, ring_send(): return lax.ppermute(value, 'ctx', ring_pairs(lax.axis_size('ctx'), by))  16.9 us
    ppermute x2, waiting for transfers between devices, shifted(): return lax.ppermute(value, axis, pairs)  13.2 us
    all_to_all x2, starting transfers between devices, chips_exchange(): lax.all_to_all(value, 'ctx', split_axis=0, concat_axis=0, tiled=True, axi...  9.71 us
    pallas_call x6, Pallas kernels, facts_call(): pl.pallas_call(kernel, out_shape=outs, in_specs=vmem_specs(len(operands))...  9.65 us
    all_to_all x2, waiting for transfers between devices, chips_exchange(): lax.all_to_all(value, 'ctx', split_axis=0, concat_axis=0, tiled=True, axi...  9.16 us
    ppermute x2, starting transfers between devices, shifted(): return lax.ppermute(value, axis, pairs)  8.59 us
    ppermute x5, starting transfers between devices, swap_cores(): lax.ppermute(value, 'ctx', [(i, i ^ 1) for i in range(lax.axis_size('ctx'...  8.54 us
  transfers between devices with their start and end apart: 30, of which 17 were waited for; matrix products, arithmetic and copies ran while one was open for 1% of the time, Pallas kernels for 21%

profile of v9, /device:TPU:3, one launch (start us, length us, event | category | flops | bytes accessed | tf_op | source)
XLA Modules:
  0.0 173.2 jit_solution(6302935760464645422)
XLA Ops:
  0.7 1.7 reshape.11.refs_0_.refs_4_
  2.5 1.5 collective-permute-start.3
  3.9 1.1 copy.11.feat_ref
  5.0 4.4 %shard_map.105 = (f32[512,576]{1,0:T(8,128)S(1)}, bf16[512,576]{1,0:T(8,128)(2,1)S(1)}, f32[2,288]{1,0:T(2,128)S(1)}) custom-call(bf16[2,196,576]{2,1,0:T(8,128)(2,1)S(1)} %copy.11.feat_ref, bf16[9,48,576]{2,1,0:T(8,128)(2,1)S(1)} %bitcast.11, bf16[288,576]{1,0:T(8,128)(2,1)S(1)} %bitcast.13), custom_call_target="tpu_custom_call" | custom-call | tf_op jit(solution)/shard_map/pallas_call | solution.py:292
  9.5 1.3 collective-permute-start
  10.8 1.5 collective-permute-done
  12.3 1.5 shard_map.106
  13.7 4.5 %collective-permute-done.2.refs_1_.refs_4_ = bf16[72,4608]{1,0:T(8,128)(2,1)S(1)} collective-permute-done((bf16[72,4608]{1,0:T(8,128)(2,1)S(1)}, bf16[72,4608]{1,0:T(8,128)(2,1)S(1)}, u32[]{:S(2)}, u32[]{:S(2)}) %collective-permute-start.2) | collective-permute-done | bytes 663584 | tf_op jit(solution)/shard_map/ppermute | solution.py:427
  18.3 1.1 collective-permute-start.4
  19.8 0.9 copy-done.7
  20.6 6.4 %collective-permute-start.1 = (bf16[256,576]{1,0:T(8,128)(2,1)}, bf16[256,576]{1,0:T(8,128)(2,1)}, u32[]{:S(2)}, u32[]{:S(2)}) collective-permute-start(bf16[256,576]{1,0:T(8,128)(2,1)} %get-tuple-element.72), channel_id=1, source_target_pairs={{0,2},{2,4},{4,6},{6,8},{8,10},{10,12},{12,14},{14,16},{16,18},{18... | collective-permute-start | bytes 884744 | tf_op jit(solution)/shard_map/ppermute | solution.py:391
  27.0 4.7 %all-to-all-start = ((bf16[8,8,4096]{2,1,0:T(8,128)(2,1)}), bf16[8,8,4096]{2,1,0:T(8,128)(2,1)S(1)}, u32[]{:S(2)}, u32[]{:S(2)}) async-start(bf16[8,8,4096]{2,1,0:T(8,128)(2,1)} %bitcast.16), calls=%async_computation | async-start | bytes 1048576 | tf_op jit(solution)/shard_map/all_to_all | solution.py:616
  31.7 7.6 %collective-permute-done.1.halo_ref = bf16[256,576]{1,0:T(8,128)(2,1)} collective-permute-done((bf16[256,576]{1,0:T(8,128)(2,1)}, bf16[256,576]{1,0:T(8,128)(2,1)}, u32[]{:S(2)}, u32[]{:S(2)}) %collective-permute-start.1) | collective-permute-done | bytes 294944 | tf_op jit(solution)/shard_map/ppermute | solution.py:391
  39.3 3.5 %collective-permute-start.6 = (bf16[72,4608]{1,0:T(8,128)(2,1)S(1)}, bf16[72,4608]{1,0:T(8,128)(2,1)S(1)}, u32[]{:S(2)}, u32[]{:S(2)}) collective-permute-start(bf16[72,4608]{1,0:T(8,128)(2,1)S(1)} %collective-permute-done.4.refs_3_.refs_5_), channel_id=1, source_target_pairs={{0,8},{2,10},{8,16},{10,18},{16,24},{18,26},{24,28},{26,30},{28,20... | collective-permute-start | bytes 1990664 | tf_op jit(solution)/shard_map/ppermute | solution.py:427
  42.8 0.9 collective-permute-start.7
  43.8 1.3 shard_map.104.facts_ref
  45.7 2.2 %shard_map.107.own_ref = bf16[64,4608]{1,0:T(8,128)(2,1)} custom-call(s32[5]{0:T(128)S(1)} %copy-done.28, bf16[256,576]{1,0:T(8,128)(2,1)} %collective-permute-done.1.halo_ref, bf16[256,576]{1,0:T(8,128)(2,1)S(1)} %get-tuple-element.84.even_ref), custom_call_target="tpu_custom_call" | custom-call | tf_op jit(solution)/shard_map/pallas_call | solution.py:340
  47.9 2.2 %collective-permute-start.13 = (bf16[64,4608]{1,0:T(8,128)(2,1)}, bf16[64,4608]{1,0:T(8,128)(2,1)}, u32[]{:S(2)}, u32[]{:S(2)}) collective-permute-start(bf16[64,4608]{1,0:T(8,128)(2,1)} %shard_map.107.own_ref), channel_id=1, source_target_pairs={{0,2},{2,0},{4,6},{6,4},{8,10},{10,8},{12,14},{14,12},{16,18},{18,... | collective-permute-start | bytes 1769480 | tf_op jit(solution)/shard_map/ppermute | solution.py:408
  50.2 8.5 %collective-permute-done.6.refs_0_.refs_4_ = bf16[72,4608]{1,0:T(8,128)(2,1)S(1)} collective-permute-done((bf16[72,4608]{1,0:T(8,128)(2,1)S(1)}, bf16[72,4608]{1,0:T(8,128)(2,1)S(1)}, u32[]{:S(2)}, u32[]{:S(2)}) %collective-permute-start.6) | collective-permute-done | bytes 663584 | tf_op jit(solution)/shard_map/ppermute | solution.py:427
  58.7 1.6 collective-permute-done.7.refs_1_.refs_6_
  60.3 4.6 %collective-permute-start.11 = (bf16[72,4096]{1,0:T(8,128)(2,1)}, bf16[72,4096]{1,0:T(8,128)(2,1)S(1)}, u32[]{:S(2)}, u32[]{:S(2)}) collective-permute-start(bf16[72,4096]{1,0:T(8,128)(2,1)} %refs_0_.1), channel_id=1, source_target_pairs={{0,4},{2,6},{8,0},{10,2},{16,8},{18,10},{24,16},{26,18},{28,24},{3... | collective-permute-start | bytes 1769480 | tf_op jit(solution)/shard_map/ppermute | solution.py:427
  64.9 0.7 copy-done.29
  65.5 1.7 shard_map.108.patch_ref
  67.3 2.9 %shard_map.109.own_ref = f32[128,360]{1,0:T(8,128)S(1)} custom-call(bf16[128,4608]{1,0:T(8,128)(2,1)S(1)} %shard_map.108.patch_ref, bf16[72,4608]{1,0:T(8,128)(2,1)S(1)} %reshape.11.refs_0_.refs_4_, bf16[72,4608]{1,0:T(8,128)(2,1)S(1)} %collective-permute-done.2.refs_1_.refs_4_, bf16[72,4608]{1,0:T(8,128)(2,1)S(1)} %copy-done.8, ...), custom_call_target="tpu_custom_call" | custom-call | tf_op jit(solution)/shard_map/pallas_call | solution.py:555
  70.2 1.3 collective-permute-start.14
  71.5 6.6 %collective-permute-done.11.refs_1_ = bf16[72,4096]{1,0:T(8,128)(2,1)S(1)} collective-permute-done((bf16[72,4096]{1,0:T(8,128)(2,1)}, bf16[72,4096]{1,0:T(8,128)(2,1)S(1)}, u32[]{:S(2)}, u32[]{:S(2)}) %collective-permute-start.11) | collective-permute-done | bytes 589856 | tf_op jit(solution)/shard_map/ppermute | solution.py:427
  78.1 2.1 %collective-permute-done.12.refs_2_.refs_5_ = bf16[72,4608]{1,0:T(8,128)(2,1)S(1)} collective-permute-done((bf16[72,4608]{1,0:T(8,128)(2,1)S(1)}, bf16[72,4608]{1,0:T(8,128)(2,1)S(1)}, u32[]{:S(2)}, u32[]{:S(2)}) %collective-permute-start.12) | collective-permute-done | bytes 663584 | tf_op jit(solution)/shard_map/ppermute | solution.py:427
  80.3 2.0 %collective-permute-start.15 = (bf16[72,4096]{1,0:T(8,128)(2,1)S(1)}, bf16[72,4096]{1,0:T(8,128)(2,1)S(1)}, u32[]{:S(2)}, u32[]{:S(2)}) collective-permute-start(bf16[72,4096]{1,0:T(8,128)(2,1)S(1)} %collective-permute-done.11.refs_1_), channel_id=1, source_target_pairs={{0,4},{2,6},{8,0},{10,2},{16,8},{18,10},{24,16},{26,18},{28,24},{3... | collective-permute-start | bytes 1769480 | tf_op jit(solution)/shard_map/ppermute | solution.py:427
  82.2 2.2 %shard_map.110.own_ref = f32[128,216]{1,0:T(8,128)S(1)} custom-call(bf16[128,4608]{1,0:T(8,128)(2,1)S(1)} %shard_map.108.patch_ref, bf16[72,4608]{1,0:T(8,128)(2,1)S(1)} %collective-permute-done.6.refs_0_.refs_4_, bf16[72,4608]{1,0:T(8,128)(2,1)} %collective-permute-done.7.refs_1_.refs_6_, bf16[72,4608]{1,0:T(8,128)(2,1)S(1)} %collective-permute-done.12.refs_2_.refs_5_), custom_call_target="tpu_custom_call" | custom-call | tf_op jit(solution)/shard_map/pallas_call | solution.py:555
  84.5 1.3 collective-permute-start.16
  85.8 6.7 %collective-permute-done.9.refs_0_.refs_3_ = bf16[72,4096]{1,0:T(8,128)(2,1)S(1)} collective-permute-done((bf16[72,4096]{1,0:T(8,128)(2,1)S(1)}, bf16[72,4096]{1,0:T(8,128)(2,1)S(1)}, u32[]{:S(2)}, u32[]{:S(2)}) %collective-permute-start.9) | collective-permute-done | bytes 589856 | tf_op jit(solution)/shard_map/ppermute | solution.py:427
  92.5 1.0 shard_map.111
  93.6 1.1 shard_map.112
  94.6 0.9 collective-permute-done.15.refs_2_
  95.6 1.6 collective-permute-start.18
  97.2 1.1 collective-permute-start.8
  98.3 1.5 collective-permute-done.8.send_ref
  99.8 1.0 shard_map.113.refs_0_
  101.5 6.9 %collective-permute-done.10.refs_1_.refs_4_ = bf16[72,4096]{1,0:T(8,128)(2,1)} collective-permute-done((bf16[72,4096]{1,0:T(8,128)(2,1)S(1)}, bf16[72,4096]{1,0:T(8,128)(2,1)}, u32[]{:S(2)}, u32[]{:S(2)}) %collective-permute-start.10) | collective-permute-done | bytes 589856 | tf_op jit(solution)/shard_map/ppermute | solution.py:427
  108.4 1.7 collective-permute-done.18.refs_2_.refs_5_
  110.1 1.2 collective-permute-start.19
  111.3 5.0 %all-to-all-start.1 = ((bf16[8,16,576]{2,1,0:T(8,128)(2,1)}), bf16[8,16,576]{2,1,0:T(8,128)(2,1)S(1)}, u32[]{:S(2)}, u32[]{:S(2)}) async-start(bf16[8,16,576]{2,1,0:T(8,128)(2,1)} %bitcast.15), calls=%async_computation.1 | async-start | bytes 327680 | tf_op jit(solution)/shard_map/all_to_all | solution.py:616
  116.3 1.2 collective-permute-start.21
  117.6 9.2 %all-to-all-done.1 = bf16[8,16,576]{2,1,0:T(8,128)(2,1)S(1)} async-done(((bf16[8,16,576]{2,1,0:T(8,128)(2,1)}), bf16[8,16,576]{2,1,0:T(8,128)(2,1)S(1)}, u32[]{:S(2)}, u32[]{:S(2)}) %all-to-all-start.1) | async-done | bytes 147488 | tf_op jit(solution)/shard_map/all_to_all | solution.py:616
  126.7 1.1 copy-done.15
  127.8 2.4 %shard_map.114.refs_0_ = f32[128,216]{1,0:T(8,128)S(1)} custom-call(bf16[64,4096]{1,0:T(8,128)(2,1)S(1)} %bitcast.8, bf16[64,4096]{1,0:T(8,128)(2,1)S(1)} %collective-permute-done.8.send_ref, bf16[72,4096]{1,0:T(8,128)(2,1)S(1)} %copy-done.15, bf16[72,4096]{1,0:T(8,128)(2,1)} %collective-permute-done.10.refs_1_.refs_4_, ...), custom_call_target="tpu_custom_call" | custom-call | tf_op jit(solution)/shard_map/pallas_call | solution.py:555
  130.2 1.3 collective-permute-start.20
  131.4 2.5 %shard_map.115 = (f32[64,2304]{1,0:T(8,128)S(1)}, f32[64,2304]{1,0:T(8,128)S(1)}, f32[64,2304]{1,0:T(8,128)S(1)}, f32[64,2304]{1,0:T(8,128)S(1)}) custom-call(s32[5]{0:T(128)S(1)} %copy-done.30, f32[128,216]{1,0:T(8,128)S(1)} %copy-done.24, f32[128,216]{1,0:T(8,128)} %collective-permute-done.21.refs_1_, f32[128,360]{1,0:T(8,128)S(1)} %get-tuple-element.99.refs_2_, ...), custom_call_target="tpu_custom_call" | custom-call | tf_op jit(solution)/shard_map/pallas_call | solution.py:574
  134.0 2.5 %shard_map.116 = (f32[64,2304]{1,0:T(8,128)S(1)}, f32[64,2304]{1,0:T(8,128)S(1)}, f32[64,2304]{1,0:T(8,128)S(1)}, f32[64,2304]{1,0:T(8,128)S(1)}) custom-call(s32[5]{0:T(128)S(1)} %copy-done.30, f32[128,216]{1,0:T(8,128)S(1)} %shard_map.114.refs_0_, f32[128,216]{1,0:T(8,128)S(1)} %collective-permute-done.20.refs_1_, ...), custom_call_target="tpu_custom_call" | custom-call | tf_op jit(solution)/shard_map/pallas_call | solution.py:574
  136.6 2.5 %shard_map.117 = (f32[128,144]{1,0:T(8,128)S(1)}, s32[5]{0:T(128)S(1)}) custom-call(s32[5]{0:T(128)S(1)} %copy-done.30, bf16[64,4096]{1,0:T(8,128)(2,1)S(1)} %bitcast.9, bf16[64,4096]{1,0:T(8,128)(2,1)S(1)} %collective-permute-done.8.send_ref, bf16[72,4096]{1,0:T(8,128)(2,1)} %collective-permute-done.17.refs_0_.refs_6_, ...), custom_call_target="tpu_custom_call" | custom-call | tf_op jit(solution)/shard_map/pallas_call | solution.py:560
  139.1 1.3 collective-permute-start.22
  140.4 5.3 %shard_map.118 = (f32[64,4096]{1,0:T(8,128)S(1)}, bf16[64,4096]{1,0:T(8,128)(2,1)S(1)}) custom-call(s32[5]{0:T(128)S(1)} %get-tuple-element.113.facts_ref, bf16[128,576]{1,0:T(8,128)(2,1)S(1)} %bitcast.10, bf16[72,4096]{1,0:T(8,128)(2,1)S(1)} %copy-done.11, bf16[72,4096]{1,0:T(8,128)(2,1)S(1)} %copy-done.13, bf16[72,4096]{1,0:T(8,128)(2,1)S(1)} %copy-done.18, ...), custom_call_target="tpu_custom_call" | custom-call | tf_op jit(solution)/shard_map/pallas_call | solution.py:602
  145.7 1.3 shard_map.119
  146.9 4.7 %collective-permute-start.24 = (bf16[64,2304]{1,0:T(8,128)(2,1)S(1)}, bf16[64,2304]{1,0:T(8,128)(2,1)S(1)}, u32[]{:S(2)}, u32[]{:S(2)}) collective-permute-start(bf16[64,2304]{1,0:T(8,128)(2,1)S(1)} %get-tuple-element.124), channel_id=1, source_target_pairs={{0,2},{2,0},{4,6},{6,4},{8,10},{10,8},{12,14},{14,12},{16,18},{18,... | collective-permute-start | bytes 884744 | tf_op jit(solution)/shard_map/ppermute | solution.py:408
  151.7 1.3 shard_map.121
  153.4 1.4 shard_map.120
  154.9 2.2 %collective-permute-start.26 = (bf16[256,576]{1,0:T(8,128)(2,1)S(1)}, bf16[256,576]{1,0:T(8,128)(2,1)S(1)}, u32[]{:S(2)}, u32[]{:S(2)}) collective-permute-start(bf16[256,576]{1,0:T(8,128)(2,1)S(1)} %get-tuple-element.132), channel_id=1, source_target_pairs={{2,0},{4,2},{6,4},{8,6},{10,8},{12,10},{14,12},{16,14},{18,16},{20... | collective-permute-start | bytes 884744 | tf_op jit(solution)/shard_map/ppermute | solution.py:391
  157.1 1.4 shard_map.122
  158.6 5.6 %collective-permute-done.26.odd_ref = bf16[256,576]{1,0:T(8,128)(2,1)S(1)} collective-permute-done((bf16[256,576]{1,0:T(8,128)(2,1)S(1)}, bf16[256,576]{1,0:T(8,128)(2,1)S(1)}, u32[]{:S(2)}, u32[]{:S(2)}) %collective-permute-start.26) | collective-permute-done | bytes 294944 | tf_op jit(solution)/shard_map/ppermute | solution.py:391
  164.2 0.9 shard_map.123
  165.4 0.9 add_convert_fusion
  166.3 1.3 collective-permute-done.27
  167.6 4.4 %shard_map.124 = bf16[2,196,576]{2,1,0:T(8,128)(2,1)S(1)} custom-call(f32[256,576]{1,0:T(8,128)S(1)} %get-tuple-element.131.even_ref, bf16[256,576]{1,0:T(8,128)(2,1)S(1)} %collective-permute-done.26.odd_ref, f32[512,576]{1,0:T(8,128)S(1)} %copy-done.1, f32[2,576]{1,0:T(2,128)S(1)} %get-tuple-element.133.excite_ref, f32[2,288]{1,0:T(2,128)S(1)} %add.9.sq_ref, ...), custom_call_target="tpu_custom_call" | custom-call | flops 2717908992 | bytes 4718592 | tf_op jit(solution)/shard_map/pallas_call | solution.py:375
  172.1 1.2 copy.12
  (85 shorter events, 3.0 us)
Async XLA Ops:
  0.6 4.4 %copy-start.21 = (bf16[9,576,48]{1,2,0:T(8,128)(2,1)S(1)}, bf16[9,576,48]{1,2,0:T(8,128)(2,1)}, u32[]{:S(2)}) copy-start(bf16[9,576,48]{1,2,0:T(8,128)(2,1)} %param.10) | copy-start | bytes 1492996
  0.6 4.4 %copy-start.25 = (bf16[576,288]{0,1:T(8,128)(2,1)S(1)}, bf16[576,288]{0,1:T(8,128)(2,1)}, u32[]{:S(2)}) copy-start(bf16[576,288]{0,1:T(8,128)(2,1)} %param.11) | copy-start | bytes 995332
  2.4 9.9 %copy-start.19 = (bf16[288,576]{1,0:T(8,128)(2,1)S(1)}, bf16[288,576]{1,0:T(8,128)(2,1)}, u32[]{:S(2)}) copy-start(bf16[288,576]{1,0:T(8,128)(2,1)} %expand_ref.3) | copy-start | bytes 995332
  2.4 15.8 %collective-permute-start.2 = (bf16[72,4608]{1,0:T(8,128)(2,1)S(1)}, bf16[72,4608]{1,0:T(8,128)(2,1)S(1)}, u32[]{:S(2)}, u32[]{:S(2)}) collective-permute-start(bf16[72,4608]{1,0:T(8,128)(2,1)S(1)} %reshape.11.refs_0_.refs_4_), channel_id=1, source_target_pairs={{0,8},{2,10},{8,16},{10,18},{16,24},{18,26},{24,28},{26,30},{28,20... | collective-permute-start | bytes 1990664 | tf_op jit(solution)/shard_map/ppermute | solution.py:427
  2.5 15.9 %collective-permute-start.3 = (bf16[72,4608]{1,0:T(8,128)(2,1)S(1)}, bf16[72,4608]{1,0:T(8,128)(2,1)S(1)}, u32[]{:S(2)}, u32[]{:S(2)}) collective-permute-start(bf16[72,4608]{1,0:T(8,128)(2,1)S(1)} %reshape.11.refs_0_.refs_4_), channel_id=1, source_target_pairs={{0,4},{2,6},{8,0},{10,2},{16,8},{18,10},{24,16},{26,18},{28,24},{3... | collective-permute-start | bytes 1990664 | tf_op jit(solution)/shard_map/ppermute | solution.py:427
  9.5 8.8 %copy-start = (f32[512,576]{1,0:T(8,128)}, f32[512,576]{1,0:T(8,128)S(1)}, u32[]{:S(2)}) copy-start(f32[512,576]{1,0:T(8,128)S(1)} %get-tuple-element.68.conv_ref) | copy-start | bytes 3538948
  9.5 2.8 %collective-permute-start = (f32[2,288]{1,0:T(2,128)S(1)}, f32[2,288]{1,0:T(2,128)S(1)}, u32[]{:S(2)}, u32[]{:S(2)}) collective-permute-start(f32[2,288]{1,0:T(2,128)S(1)} %get-tuple-element.71), channel_id=1, source_target_pairs={{0,1},{1,0},{2,3},{3,2},{4,5},{5,4},{6,7},{7,6},{8,9},{9,8},{10,11... | collective-permute-start | bytes 6920 | tf_op jit(solution)/shard_map/ppermute | solution.py:416
  18.2 49.0 %copy-start.2 = (bf16[72,4608]{1,0:T(8,128)(2,1)}, bf16[72,4608]{1,0:T(8,128)(2,1)S(1)}, u32[]{:S(2)}) copy-start(bf16[72,4608]{1,0:T(8,128)(2,1)S(1)} %collective-permute-done.2.refs_1_.refs_4_) | copy-start | bytes 1990660
  18.3 21.0 %collective-permute-start.4 = (bf16[72,4608]{1,0:T(8,128)(2,1)S(1)}, bf16[72,4608]{1,0:T(8,128)(2,1)S(1)}, u32[]{:S(2)}, u32[]{:S(2)}) collective-permute-start(bf16[72,4608]{1,0:T(8,128)(2,1)S(1)} %collective-permute-done.2.refs_1_.refs_4_), channel_id=1, source_target_pairs={{0,8},{2,10},{8,16},{10,18},{16,24},{18,26},{24,28},{26,30},{28,20... | collective-permute-start | bytes 1990664 | tf_op jit(solution)/shard_map/ppermute | solution.py:427
  19.5 19.8 %collective-permute-start.5 = (bf16[72,4608]{1,0:T(8,128)(2,1)S(1)}, bf16[72,4608]{1,0:T(8,128)(2,1)}, u32[]{:S(2)}, u32[]{:S(2)}) collective-permute-start(bf16[72,4608]{1,0:T(8,128)(2,1)S(1)} %collective-permute-done.3.refs_2_.refs_5_), channel_id=1, source_target_pairs={{0,4},{2,6},{8,0},{10,2},{16,8},{18,10},{24,16},{26,18},{28,24},{3... | collective-permute-start | bytes 1990664 | tf_op jit(solution)/shard_map/ppermute | solution.py:427
  19.8 0.9 copy-start.7
  20.6 18.6 %collective-permute-start.1 = (bf16[256,576]{1,0:T(8,128)(2,1)}, bf16[256,576]{1,0:T(8,128)(2,1)}, u32[]{:S(2)}, u32[]{:S(2)}) collective-permute-start(bf16[256,576]{1,0:T(8,128)(2,1)} %get-tuple-element.72), channel_id=1, source_target_pairs={{0,2},{2,4},{4,6},{6,8},{8,10},{10,12},{12,14},{14,16},{16,18},{18... | collective-permute-start | bytes 884744 | tf_op jit(solution)/shard_map/ppermute | solution.py:391
  27.0 23.2 %all-to-all-start = ((bf16[8,8,4096]{2,1,0:T(8,128)(2,1)}), bf16[8,8,4096]{2,1,0:T(8,128)(2,1)S(1)}, u32[]{:S(2)}, u32[]{:S(2)}) async-start(bf16[8,8,4096]{2,1,0:T(8,128)(2,1)} %bitcast.16), calls=%async_computation | async-start | bytes 1048576 | tf_op jit(solution)/shard_map/all_to_all | solution.py:616
  39.3 21.0 %copy-start.4 = (bf16[72,4608]{1,0:T(8,128)(2,1)}, bf16[72,4608]{1,0:T(8,128)(2,1)S(1)}, u32[]{:S(2)}) copy-start(bf16[72,4608]{1,0:T(8,128)(2,1)S(1)} %collective-permute-done.4.refs_3_.refs_5_) | copy-start | bytes 1990660
  39.3 19.4 %collective-permute-start.6 = (bf16[72,4608]{1,0:T(8,128)(2,1)S(1)}, bf16[72,4608]{1,0:T(8,128)(2,1)S(1)}, u32[]{:S(2)}, u32[]{:S(2)}) collective-permute-start(bf16[72,4608]{1,0:T(8,128)(2,1)S(1)} %collective-permute-done.4.refs_3_.refs_5_), channel_id=1, source_target_pairs={{0,8},{2,10},{8,16},{10,18},{16,24},{18,26},{24,28},{26,30},{28,20... | collective-permute-start | bytes 1990664 | tf_op jit(solution)/shard_map/ppermute | solution.py:427
  42.8 17.4 %collective-permute-start.7 = (bf16[72,4608]{1,0:T(8,128)(2,1)}, bf16[72,4608]{1,0:T(8,128)(2,1)}, u32[]{:S(2)}, u32[]{:S(2)}) collective-permute-start(bf16[72,4608]{1,0:T(8,128)(2,1)} %collective-permute-done.5.refs_4_.refs_6_), channel_id=1, source_target_pairs={{0,4},{2,6},{8,0},{10,2},{16,8},{18,10},{24,16},{26,18},{28,24},{3... | collective-permute-start | bytes 1990664 | tf_op jit(solution)/shard_map/ppermute | solution.py:427
  45.0 0.7 copy-start.28
  47.9 16.9 %collective-permute-start.13 = (bf16[64,4608]{1,0:T(8,128)(2,1)}, bf16[64,4608]{1,0:T(8,128)(2,1)}, u32[]{:S(2)}, u32[]{:S(2)}) collective-permute-start(bf16[64,4608]{1,0:T(8,128)(2,1)} %shard_map.107.own_ref), channel_id=1, source_target_pairs={{0,2},{2,0},{4,6},{6,4},{8,10},{10,8},{12,14},{14,12},{16,18},{18,... | collective-permute-start | bytes 1769480 | tf_op jit(solution)/shard_map/ppermute | solution.py:408
  50.2 17.1 %copy-start.8 = (bf16[72,4608]{1,0:T(8,128)(2,1)S(1)}, bf16[72,4608]{1,0:T(8,128)(2,1)}, u32[]{:S(2)}) copy-start(bf16[72,4608]{1,0:T(8,128)(2,1)} %copy-done.7) | copy-start | bytes 1990660
  60.3 7.0 %copy-start.5 = (bf16[72,4608]{1,0:T(8,128)(2,1)S(1)}, bf16[72,4608]{1,0:T(8,128)(2,1)}, u32[]{:S(2)}) copy-start(bf16[72,4608]{1,0:T(8,128)(2,1)} %copy-done.4) | copy-start | bytes 1990660
  60.3 20.0 %collective-permute-start.12 = (bf16[72,4608]{1,0:T(8,128)(2,1)S(1)}, bf16[72,4608]{1,0:T(8,128)(2,1)S(1)}, u32[]{:S(2)}, u32[]{:S(2)}) collective-permute-start(bf16[72,4608]{1,0:T(8,128)(2,1)S(1)} %collective-permute-done.6.refs_0_.refs_4_), channel_id=1, source_target_pairs={{0,8},{2,10},{8,16},{10,18},{16,24},{18,26},{24,28},{26,30},{28,20... | collective-permute-start | bytes 1990664 | tf_op jit(solution)/shard_map/ppermute | solution.py:427
  60.3 17.9 %collective-permute-start.11 = (bf16[72,4096]{1,0:T(8,128)(2,1)}, bf16[72,4096]{1,0:T(8,128)(2,1)S(1)}, u32[]{:S(2)}, u32[]{:S(2)}) collective-permute-start(bf16[72,4096]{1,0:T(8,128)(2,1)} %refs_0_.1), channel_id=1, source_target_pairs={{0,4},{2,6},{8,0},{10,2},{16,8},{18,10},{24,16},{26,18},{28,24},{3... | collective-permute-start | bytes 1769480 | tf_op jit(solution)/shard_map/ppermute | solution.py:427
  64.9 0.7 copy-start.29
  67.3 4.2 %copy-start.10 = (bf16[72,4096]{1,0:T(8,128)(2,1)S(1)}, bf16[72,4096]{1,0:T(8,128)(2,1)}, u32[]{:S(2)}) copy-start(bf16[72,4096]{1,0:T(8,128)(2,1)} %refs_0_.1) | copy-start | bytes 1769476
  70.2 22.3 %copy-start.30 = (s32[5]{0:T(128)S(1)}, s32[5]{0:T(128)}, u32[]{:S(2)}) copy-start(s32[5]{0:T(128)} %shard_map.104.facts_ref) | copy-start | bytes 64
  70.2 7.9 %collective-permute-start.14 = (f32[128,360]{1,0:T(8,128)S(1)}, f32[128,360]{1,0:T(8,128)S(1)}, u32[]{:S(2)}, u32[]{:S(2)}) collective-permute-start(f32[128,360]{1,0:T(8,128)S(1)} %shard_map.109.own_ref), channel_id=1, source_target_pairs={{0,1},{1,0},{2,3},{3,2},{4,5},{5,4},{6,7},{7,6},{8,9},{9,8},{10,11... | collective-permute-start | bytes 552968 | tf_op jit(solution)/shard_map/ppermute | solution.py:416
  71.5 21.0 %collective-permute-start.9 = (bf16[72,4096]{1,0:T(8,128)(2,1)S(1)}, bf16[72,4096]{1,0:T(8,128)(2,1)S(1)}, u32[]{:S(2)}, u32[]{:S(2)}) collective-permute-start(bf16[72,4096]{1,0:T(8,128)(2,1)S(1)} %copy-done.10), channel_id=1, source_target_pairs={{0,8},{2,10},{8,16},{10,18},{16,24},{18,26},{24,28},{26,30},{28,20... | collective-permute-start | bytes 1769480 | tf_op jit(solution)/shard_map/ppermute | solution.py:427
  78.1 21.7 %copy-start.12 = (bf16[72,4096]{1,0:T(8,128)(2,1)}, bf16[72,4096]{1,0:T(8,128)(2,1)S(1)}, u32[]{:S(2)}) copy-start(bf16[72,4096]{1,0:T(8,128)(2,1)S(1)} %collective-permute-done.11.refs_1_) | copy-start | bytes 1769476
  80.3 15.3 %collective-permute-start.15 = (bf16[72,4096]{1,0:T(8,128)(2,1)S(1)}, bf16[72,4096]{1,0:T(8,128)(2,1)S(1)}, u32[]{:S(2)}, u32[]{:S(2)}) collective-permute-start(bf16[72,4096]{1,0:T(8,128)(2,1)S(1)} %collective-permute-done.11.refs_1_), channel_id=1, source_target_pairs={{0,4},{2,6},{8,0},{10,2},{16,8},{18,10},{24,16},{26,18},{28,24},{3... | collective-permute-start | bytes 1769480 | tf_op jit(solution)/shard_map/ppermute | solution.py:427
  84.5 9.1 %collective-permute-start.16 = (f32[128,216]{1,0:T(8,128)S(1)}, f32[128,216]{1,0:T(8,128)S(1)}, u32[]{:S(2)}, u32[]{:S(2)}) collective-permute-start(f32[128,216]{1,0:T(8,128)S(1)} %shard_map.110.own_ref), channel_id=1, source_target_pairs={{0,1},{1,0},{2,3},{3,2},{4,5},{5,4},{6,7},{7,6},{8,9},{9,8},{10,11... | collective-permute-start | bytes 331784 | tf_op jit(solution)/shard_map/ppermute | solution.py:416
  92.5 8.4 %copy-start.14 = (bf16[72,4096]{1,0:T(8,128)(2,1)}, bf16[72,4096]{1,0:T(8,128)(2,1)S(1)}, u32[]{:S(2)}) copy-start(bf16[72,4096]{1,0:T(8,128)(2,1)S(1)} %collective-permute-done.9.refs_0_.refs_3_) | copy-start | bytes 1769476
  92.5 15.9 %collective-permute-start.10 = (bf16[72,4096]{1,0:T(8,128)(2,1)S(1)}, bf16[72,4096]{1,0:T(8,128)(2,1)}, u32[]{:S(2)}, u32[]{:S(2)}) collective-permute-start(bf16[72,4096]{1,0:T(8,128)(2,1)S(1)} %collective-permute-done.9.refs_0_.refs_3_), channel_id=1, source_target_pairs={{0,8},{2,10},{8,16},{10,18},{16,24},{18,26},{24,28},{26,30},{28,20... | collective-permute-start | bytes 1769480 | tf_op jit(solution)/shard_map/ppermute | solution.py:427
  94.6 6.2 %copy-start.27 = (bf16[128,576]{1,0:T(8,128)(2,1)}, bf16[128,576]{1,0:T(8,128)(2,1)S(1)}, u32[]{:S(2)}) copy-start(bf16[128,576]{1,0:T(8,128)(2,1)S(1)} %get-tuple-element.95) | copy-start | bytes 442372
  95.5 5.3 %copy-start.17 = (bf16[72,4096]{1,0:T(8,128)(2,1)}, bf16[72,4096]{1,0:T(8,128)(2,1)S(1)}, u32[]{:S(2)}) copy-start(bf16[72,4096]{1,0:T(8,128)(2,1)S(1)} %collective-permute-done.15.refs_2_) | copy-start | bytes 1769476
  95.6 14.6 %collective-permute-start.18 = (bf16[72,4096]{1,0:T(8,128)(2,1)S(1)}, bf16[72,4096]{1,0:T(8,128)(2,1)}, u32[]{:S(2)}, u32[]{:S(2)}) collective-permute-start(bf16[72,4096]{1,0:T(8,128)(2,1)S(1)} %collective-permute-done.15.refs_2_), channel_id=1, source_target_pairs={{0,4},{2,6},{8,0},{10,2},{16,8},{18,10},{24,16},{26,18},{28,24},{3... | collective-permute-start | bytes 1769480 | tf_op jit(solution)/shard_map/ppermute | solution.py:427
  97.2 2.6 %collective-permute-start.8 = (bf16[64,4096]{1,0:T(8,128)(2,1)S(1)}, bf16[64,4096]{1,0:T(8,128)(2,1)S(1)}, u32[]{:S(2)}, u32[]{:S(2)}) collective-permute-start(bf16[64,4096]{1,0:T(8,128)(2,1)S(1)} %bitcast.6), channel_id=1, source_target_pairs={{0,2},{2,0},{4,6},{6,4},{8,10},{10,8},{12,14},{14,12},{16,18},{18,... | collective-permute-start | bytes 1572872 | tf_op jit(solution)/shard_map/ppermute | solution.py:408
  100.9 0.7 copy-start.23
  108.4 28.2 %collective-permute-start.17 = (bf16[72,4096]{1,0:T(8,128)(2,1)}, bf16[72,4096]{1,0:T(8,128)(2,1)}, u32[]{:S(2)}, u32[]{:S(2)}) collective-permute-start(bf16[72,4096]{1,0:T(8,128)(2,1)} %collective-permute-done.10.refs_1_.refs_4_), channel_id=1, source_target_pairs={{0,8},{2,10},{8,16},{10,18},{16,24},{18,26},{24,28},{26,30},{28,20... | collective-permute-start | bytes 1769480 | tf_op jit(solution)/shard_map/ppermute | solution.py:427
  110.1 26.5 %collective-permute-start.19 = (bf16[72,4096]{1,0:T(8,128)(2,1)}, bf16[72,4096]{1,0:T(8,128)(2,1)}, u32[]{:S(2)}, u32[]{:S(2)}) collective-permute-start(bf16[72,4096]{1,0:T(8,128)(2,1)} %collective-permute-done.18.refs_2_.refs_5_), channel_id=1, source_target_pairs={{0,4},{2,6},{8,0},{10,2},{16,8},{18,10},{24,16},{26,18},{28,24},{3... | collective-permute-start | bytes 1769480 | tf_op jit(solution)/shard_map/ppermute | solution.py:427
  111.3 15.4 %all-to-all-start.1 = ((bf16[8,16,576]{2,1,0:T(8,128)(2,1)}), bf16[8,16,576]{2,1,0:T(8,128)(2,1)S(1)}, u32[]{:S(2)}, u32[]{:S(2)}) async-start(bf16[8,16,576]{2,1,0:T(8,128)(2,1)} %bitcast.15), calls=%async_computation.1 | async-start | bytes 327680 | tf_op jit(solution)/shard_map/all_to_all | solution.py:616
  116.3 15.1 %collective-permute-start.21 = (f32[128,216]{1,0:T(8,128)}, f32[128,216]{1,0:T(8,128)}, u32[]{:S(2)}, u32[]{:S(2)}) collective-permute-start(f32[128,216]{1,0:T(8,128)} %copy-done.23), channel_id=1, source_target_pairs={{0,1},{1,0},{2,3},{3,2},{4,5},{5,4},{6,7},{7,6},{8,9},{9,8},{10,11... | collective-permute-start | bytes 331784 | tf_op jit(solution)/shard_map/ppermute | solution.py:416
  126.7 1.1 copy-start.15
  127.8 3.6 %copy-start.9 = (bf16[72,4608]{1,0:T(8,128)(2,1)S(1)}, bf16[72,4608]{1,0:T(8,128)(2,1)}, u32[]{:S(2)}) copy-start(bf16[72,4608]{1,0:T(8,128)(2,1)} %copy-done.7) | copy-start | bytes 1990660
  127.8 3.6 %copy-start.24 = (f32[128,216]{1,0:T(8,128)S(1)}, f32[128,216]{1,0:T(8,128)}, u32[]{:S(2)}) copy-start(f32[128,216]{1,0:T(8,128)} %copy-done.23) | copy-start | bytes 331780
  130.1 3.9 %copy-start.3 = (bf16[72,4608]{1,0:T(8,128)(2,1)S(1)}, bf16[72,4608]{1,0:T(8,128)(2,1)}, u32[]{:S(2)}) copy-start(bf16[72,4608]{1,0:T(8,128)(2,1)} %copy-done.2) | copy-start | bytes 1990660
  130.1 3.9 %copy-start.6 = (bf16[72,4608]{1,0:T(8,128)(2,1)S(1)}, bf16[72,4608]{1,0:T(8,128)(2,1)}, u32[]{:S(2)}) copy-start(bf16[72,4608]{1,0:T(8,128)(2,1)} %copy-done.4) | copy-start | bytes 1990660
  130.2 3.9 %collective-permute-start.20 = (f32[128,216]{1,0:T(8,128)S(1)}, f32[128,216]{1,0:T(8,128)S(1)}, u32[]{:S(2)}, u32[]{:S(2)}) collective-permute-start(f32[128,216]{1,0:T(8,128)S(1)} %shard_map.114.refs_0_), channel_id=1, source_target_pairs={{0,1},{1,0},{2,3},{3,2},{4,5},{5,4},{6,7},{7,6},{8,9},{9,8},{10,11... | collective-permute-start | bytes 331784 | tf_op jit(solution)/shard_map/ppermute | solution.py:416
  134.0 6.4 %copy-start.18 = (bf16[72,4096]{1,0:T(8,128)(2,1)S(1)}, bf16[72,4096]{1,0:T(8,128)(2,1)}, u32[]{:S(2)}) copy-start(bf16[72,4096]{1,0:T(8,128)(2,1)} %copy-done.17) | copy-start | bytes 1769476
  136.6 3.8 %copy-start.11 = (bf16[72,4096]{1,0:T(8,128)(2,1)S(1)}, bf16[72,4096]{1,0:T(8,128)(2,1)}, u32[]{:S(2)}) copy-start(bf16[72,4096]{1,0:T(8,128)(2,1)} %refs_0_.1) | copy-start | bytes 1769476
  136.6 3.8 %copy-start.13 = (bf16[72,4096]{1,0:T(8,128)(2,1)S(1)}, bf16[72,4096]{1,0:T(8,128)(2,1)}, u32[]{:S(2)}) copy-start(bf16[72,4096]{1,0:T(8,128)(2,1)} %copy-done.12) | copy-start | bytes 1769476
  136.6 3.8 %copy-start.16 = (bf16[72,4096]{1,0:T(8,128)(2,1)S(1)}, bf16[72,4096]{1,0:T(8,128)(2,1)}, u32[]{:S(2)}) copy-start(bf16[72,4096]{1,0:T(8,128)(2,1)} %copy-done.14) | copy-start | bytes 1769476
  139.1 6.5 %collective-permute-start.22 = (f32[128,144]{1,0:T(8,128)S(1)}, f32[128,144]{1,0:T(8,128)S(1)}, u32[]{:S(2)}, u32[]{:S(2)}) collective-permute-start(f32[128,144]{1,0:T(8,128)S(1)} %get-tuple-element.126.refs_0_), channel_id=1, source_target_pairs={{0,1},{1,0},{2,3},{3,2},{4,5},{5,4},{6,7},{7,6},{8,9},{9,8},{10,11... | collective-permute-start | bytes 221192 | tf_op jit(solution)/shard_map/ppermute | solution.py:416
  146.9 6.5 %collective-permute-start.24 = (bf16[64,2304]{1,0:T(8,128)(2,1)S(1)}, bf16[64,2304]{1,0:T(8,128)(2,1)S(1)}, u32[]{:S(2)}, u32[]{:S(2)}) collective-permute-start(bf16[64,2304]{1,0:T(8,128)(2,1)S(1)} %get-tuple-element.124), channel_id=1, source_target_pairs={{0,2},{2,0},{4,6},{6,4},{8,10},{10,8},{12,14},{14,12},{16,18},{18,... | collective-permute-start | bytes 884744 | tf_op jit(solution)/shard_map/ppermute | solution.py:408
  151.6 13.8 %collective-permute-start.23 = (bf16[64,4096]{1,0:T(8,128)(2,1)S(1)}, bf16[64,4096]{1,0:T(8,128)(2,1)S(1)}, u32[]{:S(2)}, u32[]{:S(2)}) collective-permute-start(bf16[64,4096]{1,0:T(8,128)(2,1)S(1)} %get-tuple-element.118), channel_id=1, source_target_pairs={{0,2},{2,0},{4,6},{6,4},{8,10},{10,8},{12,14},{14,12},{16,18},{18,... | collective-permute-start | bytes 1572872 | tf_op jit(solution)/shard_map/ppermute | solution.py:408
  152.9 11.3 %copy-start.1 = (f32[512,576]{1,0:T(8,128)S(1)}, f32[512,576]{1,0:T(8,128)}, u32[]{:S(2)}) copy-start(f32[512,576]{1,0:T(8,128)} %copy-done) | copy-start | bytes 3538948
  152.9 11.2 %copy-start.20 = (bf16[288,576]{1,0:T(8,128)(2,1)S(1)}, bf16[288,576]{1,0:T(8,128)(2,1)}, u32[]{:S(2)}) copy-start(bf16[288,576]{1,0:T(8,128)(2,1)} %expand_ref.3) | copy-start | bytes 995332
  152.9 4.2 %collective-permute-start.25 = (bf16[64,2304]{1,0:T(8,128)(2,1)S(1)}, bf16[64,2304]{1,0:T(8,128)(2,1)S(1)}, u32[]{:S(2)}, u32[]{:S(2)}) collective-permute-start(bf16[64,2304]{1,0:T(8,128)(2,1)S(1)} %get-tuple-element.130), channel_id=1, source_target_pairs={{0,2},{2,0},{4,6},{6,4},{8,10},{10,8},{12,14},{14,12},{16,18},{18,... | collective-permute-start | bytes 884744 | tf_op jit(solution)/shard_map/ppermute | solution.py:408
  154.9 9.3 %collective-permute-start.26 = (bf16[256,576]{1,0:T(8,128)(2,1)S(1)}, bf16[256,576]{1,0:T(8,128)(2,1)S(1)}, u32[]{:S(2)}, u32[]{:S(2)}) collective-permute-start(bf16[256,576]{1,0:T(8,128)(2,1)S(1)} %get-tuple-element.132), channel_id=1, source_target_pairs={{2,0},{4,2},{6,4},{8,6},{10,8},{12,10},{14,12},{16,14},{18,16},{20... | collective-permute-start | bytes 884744 | tf_op jit(solution)/shard_map/ppermute | solution.py:391
  165.1 2.5 %copy-start.22 = (bf16[9,576,48]{1,2,0:T(8,128)(2,1)S(1)}, bf16[9,576,48]{1,2,0:T(8,128)(2,1)}, u32[]{:S(2)}) copy-start(bf16[9,576,48]{1,2,0:T(8,128)(2,1)} %param.10) | copy-start | bytes 1492996
  165.1 2.5 %copy-start.26 = (bf16[576,288]{0,1:T(8,128)(2,1)S(1)}, bf16[576,288]{0,1:T(8,128)(2,1)}, u32[]{:S(2)}) copy-start(bf16[576,288]{0,1:T(8,128)(2,1)} %param.11) | copy-start | bytes 995332
  165.1 2.5 %collective-permute-start.27 = (f32[2,288]{1,0:T(2,128)S(1)}, f32[2,288]{1,0:T(2,128)S(1)}, u32[]{:S(2)}, u32[]{:S(2)}) collective-permute-start(f32[2,288]{1,0:T(2,128)S(1)} %shard_map.123), channel_id=1, source_target_pairs={{0,1},{1,0},{2,3},{3,2},{4,5},{5,4},{6,7},{7,6},{8,9},{9,8},{10,11... | collective-permute-start | bytes 6920 | tf_op jit(solution)/shard_map/ppermute | solution.py:416

commit v10 on v9

--- a/solution.py
+++ b/solution.py
@@ -678,17 +678,14 @@
     r_down.append(ring_send(r_down[-1], -1))
     early = r_down[: steps - 1]
     sums = block_products(back_kernel, back, early)
-    r_up[-1], act, sums = tie(r_up[-1], act, sums)
+    r_up[-1], act, *terms = tie(r_up[-1], chips_exchange(act), *tp_terms(sums))
     r_up.append(ring_send(r_up[-1], 1))
-    act = chips_exchange(act)
     halo_lanes, even_lanes = slice(0, 4 * chans), slice(4 * chans, 8 * chans)
     both = halo_lanes, even_lanes
-    terms = tp_terms(sums)
     pieces = [(0, 2 * step) for step in range(steps - 1)]
     blocks = [flat_sampler] + s_down[1 : steps - 1]
     grads = add_gradients(facts, terms, slopes, pieces, blocks, (), unit, both, False)
     middle = r_up[1 : steps - 1] + [r_down[steps - 1]]
-    *middle, act = tie(*middle, act)
     r_down.append(ring_send(r_down[-1], -1))
     terms = tp_terms(block_products(back_kernel, back, middle))
     pieces = [(0, 2 * step - 1) for step in range(1, steps - 1)] + [(1, 1)]

time: 174 us -> 164 us (0.943)
  waiting for transfers between devices: 66.4 us -> 52.7 us
  local copies, waits for them, and re-layouts: 7.99 us -> 10.3 us
    all_to_all x2, waiting for transfers between devices: 9.16 us -> 0.71 us  [chips_exchange(): lax.all_to_all(value, 'ctx', split_axis=0, concat_axis=0, tiled=True, axi...]
    ppermute x14, waiting for transfers between devices: 39.6 us -> 32.4 us  [ring_send(): return lax.ppermute(value, 'ctx', ring_pairs(lax.axis_size('ctx'), by))]
    ppermute x7, waiting for transfers between devices: 2.92 us -> 5.61 us  [tp_terms(): other = lax.ppermute(value, 'tp', [(i, i ^ reach) for i in range(size)])]
    unnamed x64 -> x62, local copies, waits for them, and re-layouts: 6.26 us -> 8.62 us
  transfers between devices with their start and end apart: 30 -> 30, of which waited for: 17 -> 17; matrix products, arithmetic and copies ran while one was open for 1% -> 1% of each run, Pallas kernels for 21% -> 23%
where the time goes in v10:
time: 164 us; the launch traced here: 162 us
  waiting for transfers between devices  52.7 us (32%)
  starting transfers between devices  51.7 us (32%)
  Pallas kernels  45.4 us (28%)
  local copies, waits for them, and re-layouts  10.3 us (6%)
    ppermute x14, waiting for transfers between devices, ring_send(): return lax.ppermute(value, 'ctx', ring_pairs(lax.axis_size('ctx'), by))  32.4 us
    ppermute x14, starting transfers between devices, ring_send(): return lax.ppermute(value, 'ctx', ring_pairs(lax.axis_size('ctx'), by))  18.2 us
    ppermute x2, waiting for transfers between devices, shifted(): return lax.ppermute(value, axis, pairs)  14 us
    all_to_all x2, starting transfers between devices, chips_exchange(): lax.all_to_all(value, 'ctx', split_axis=0, concat_axis=0, tiled=True, axi...  9.86 us
    pallas_call x4, Pallas kernels, block_products(): whole_call(kernel, f32(rows, len(blocks) * blocks[0].shape[0]), [])  9.65 us
    pallas_call x6, Pallas kernels, facts_call(): pl.pallas_call(kernel, out_shape=outs, in_specs=vmem_specs(len(operands))...  9.49 us
    unnamed x62, local copies, waits for them, and re-layouts  8.62 us
    ppermute x2, starting transfers between devices, shifted(): return lax.ppermute(value, axis, pairs)  8.59 us
  transfers between devices with their start and end apart: 30, of which 17 were waited for; matrix products, arithmetic and copies ran while one was open for 1% of the time, Pallas kernels for 23%

profile of v10, /device:TPU:3, one launch (start us, length us, event | category | flops | bytes accessed | tf_op | source)
XLA Modules:
  0.0 162.0 jit_solution(16088110500439113951)
XLA Ops:
  0.7 1.7 %reshape.11.refs_0_.refs_4_ = bf16[72,4608]{1,0:T(8,128)(2,1)S(1)} reshape(bf16[72,8,576]{2,1,0:T(8,128)(2,1)} %param.13) | data formatting | bytes 1327104 | tf_op jit(solution)/shard_map/reshape | solution.py:635
  2.5 1.5 collective-permute-start.3
  3.9 1.1 copy.11.feat_ref
  5.0 4.4 %shard_map.105 = (f32[512,576]{1,0:T(8,128)S(1)}, bf16[512,576]{1,0:T(8,128)(2,1)S(1)}, f32[2,288]{1,0:T(2,128)S(1)}) custom-call(bf16[2,196,576]{2,1,0:T(8,128)(2,1)S(1)} %copy.11.feat_ref, bf16[9,48,576]{2,1,0:T(8,128)(2,1)S(1)} %bitcast.11, bf16[288,576]{1,0:T(8,128)(2,1)S(1)} %bitcast.13), custom_call_target="tpu_custom_call" | custom-call | tf_op jit(solution)/shard_map/pallas_call | solution.py:292
  9.5 1.3 collective-permute-start
  10.8 1.5 collective-permute-done
  12.3 1.5 shard_map.106
  13.7 4.5 %collective-permute-done.2.refs_1_.refs_4_ = bf16[72,4608]{1,0:T(8,128)(2,1)S(1)} collective-permute-done((bf16[72,4608]{1,0:T(8,128)(2,1)S(1)}, bf16[72,4608]{1,0:T(8,128)(2,1)S(1)}, u32[]{:S(2)}, u32[]{:S(2)}) %collective-permute-start.2) | collective-permute-done | bytes 663584 | tf_op jit(solution)/shard_map/ppermute | solution.py:427
  18.3 1.1 collective-permute-start.4
  19.8 0.8 copy-done.7
  20.6 6.4 %collective-permute-start.1 = (bf16[256,576]{1,0:T(8,128)(2,1)}, bf16[256,576]{1,0:T(8,128)(2,1)}, u32[]{:S(2)}, u32[]{:S(2)}) collective-permute-start(bf16[256,576]{1,0:T(8,128)(2,1)} %get-tuple-element.69), channel_id=1, source_target_pairs={{0,2},{2,4},{4,6},{6,8},{8,10},{10,12},{12,14},{14,16},{16,18},{18... | collective-permute-start | bytes 884744 | tf_op jit(solution)/shard_map/ppermute | solution.py:391
  27.0 4.7 %all-to-all-start = ((bf16[8,8,4096]{2,1,0:T(8,128)(2,1)}), bf16[8,8,4096]{2,1,0:T(8,128)(2,1)S(1)}, u32[]{:S(2)}, u32[]{:S(2)}) async-start(bf16[8,8,4096]{2,1,0:T(8,128)(2,1)} %bitcast.16), calls=%async_computation | async-start | bytes 1048576 | tf_op jit(solution)/shard_map/all_to_all | solution.py:616
  31.7 7.6 %collective-permute-done.1.halo_ref = bf16[256,576]{1,0:T(8,128)(2,1)} collective-permute-done((bf16[256,576]{1,0:T(8,128)(2,1)}, bf16[256,576]{1,0:T(8,128)(2,1)}, u32[]{:S(2)}, u32[]{:S(2)}) %collective-permute-start.1) | collective-permute-done | bytes 294944 | tf_op jit(solution)/shard_map/ppermute | solution.py:391
  39.3 3.5 %collective-permute-start.6 = (bf16[72,4608]{1,0:T(8,128)(2,1)S(1)}, bf16[72,4608]{1,0:T(8,128)(2,1)S(1)}, u32[]{:S(2)}, u32[]{:S(2)}) collective-permute-start(bf16[72,4608]{1,0:T(8,128)(2,1)S(1)} %collective-permute-done.4.refs_3_.refs_5_), channel_id=1, source_target_pairs={{0,8},{2,10},{8,16},{10,18},{16,24},{18,26},{24,28},{26,30},{28,20... | collective-permute-start | bytes 1990664 | tf_op jit(solution)/shard_map/ppermute | solution.py:427
  42.8 0.9 collective-permute-start.7
  43.8 1.3 shard_map.104.facts_ref
  45.7 2.2 %shard_map.107.own_ref = bf16[64,4608]{1,0:T(8,128)(2,1)} custom-call(s32[5]{0:T(128)S(1)} %copy-done.27, bf16[256,576]{1,0:T(8,128)(2,1)} %collective-permute-done.1.halo_ref, bf16[256,576]{1,0:T(8,128)(2,1)S(1)} %get-tuple-element.81.even_ref), custom_call_target="tpu_custom_call" | custom-call | tf_op jit(solution)/shard_map/pallas_call | solution.py:340
  47.9 2.2 %collective-permute-start.13 = (bf16[64,4608]{1,0:T(8,128)(2,1)}, bf16[64,4608]{1,0:T(8,128)(2,1)}, u32[]{:S(2)}, u32[]{:S(2)}) collective-permute-start(bf16[64,4608]{1,0:T(8,128)(2,1)} %shard_map.107.own_ref), channel_id=1, source_target_pairs={{0,2},{2,0},{4,6},{6,4},{8,10},{10,8},{12,14},{14,12},{16,18},{18,... | collective-permute-start | bytes 1769480 | tf_op jit(solution)/shard_map/ppermute | solution.py:408
  50.2 8.5 %collective-permute-done.6.refs_0_.refs_4_ = bf16[72,4608]{1,0:T(8,128)(2,1)S(1)} collective-permute-done((bf16[72,4608]{1,0:T(8,128)(2,1)S(1)}, bf16[72,4608]{1,0:T(8,128)(2,1)S(1)}, u32[]{:S(2)}, u32[]{:S(2)}) %collective-permute-start.6) | collective-permute-done | bytes 663584 | tf_op jit(solution)/shard_map/ppermute | solution.py:427
  58.7 1.6 collective-permute-done.7.refs_1_.refs_6_
  60.3 4.6 %collective-permute-start.11 = (bf16[72,4096]{1,0:T(8,128)(2,1)}, bf16[72,4096]{1,0:T(8,128)(2,1)S(1)}, u32[]{:S(2)}, u32[]{:S(2)}) collective-permute-start(bf16[72,4096]{1,0:T(8,128)(2,1)} %refs_0_.1), channel_id=1, source_target_pairs={{0,4},{2,6},{8,0},{10,2},{16,8},{18,10},{24,16},{26,18},{28,24},{3... | collective-permute-start | bytes 1769480 | tf_op jit(solution)/shard_map/ppermute | solution.py:427
  64.9 0.7 copy-done.28
  65.5 1.7 %shard_map.108.patch_ref = bf16[128,4608]{1,0:T(8,128)(2,1)S(1)} custom-call(s32[5]{0:T(128)S(1)} %copy-done.28, bf16[64,4608]{1,0:T(8,128)(2,1)} %shard_map.107.own_ref, bf16[64,4608]{1,0:T(8,128)(2,1)} %collective-permute-done.13.mate_ref), custom_call_target="tpu_custom_call" | custom-call | tf_op jit(solution)/shard_map/pallas_call | solution.py:329
  67.3 2.9 %shard_map.109.own_ref = f32[128,360]{1,0:T(8,128)S(1)} custom-call(bf16[128,4608]{1,0:T(8,128)(2,1)S(1)} %shard_map.108.patch_ref, bf16[72,4608]{1,0:T(8,128)(2,1)S(1)} %reshape.11.refs_0_.refs_4_, bf16[72,4608]{1,0:T(8,128)(2,1)S(1)} %collective-permute-done.2.refs_1_.refs_4_, bf16[72,4608]{1,0:T(8,128)(2,1)S(1)} %copy-done.8, ...), custom_call_target="tpu_custom_call" | custom-call | tf_op jit(solution)/shard_map/pallas_call | solution.py:555
  70.2 1.3 collective-permute-start.14
  71.5 6.6 %collective-permute-done.11.refs_1_ = bf16[72,4096]{1,0:T(8,128)(2,1)S(1)} collective-permute-done((bf16[72,4096]{1,0:T(8,128)(2,1)}, bf16[72,4096]{1,0:T(8,128)(2,1)S(1)}, u32[]{:S(2)}, u32[]{:S(2)}) %collective-permute-start.11) | collective-permute-done | bytes 589856 | tf_op jit(solution)/shard_map/ppermute | solution.py:427
  78.1 2.2 %collective-permute-done.12.refs_2_.refs_5_ = bf16[72,4608]{1,0:T(8,128)(2,1)S(1)} collective-permute-done((bf16[72,4608]{1,0:T(8,128)(2,1)S(1)}, bf16[72,4608]{1,0:T(8,128)(2,1)S(1)}, u32[]{:S(2)}, u32[]{:S(2)}) %collective-permute-start.12) | collective-permute-done | bytes 663584 | tf_op jit(solution)/shard_map/ppermute | solution.py:427
  80.4 2.0 %collective-permute-start.15 = (bf16[72,4096]{1,0:T(8,128)(2,1)S(1)}, bf16[72,4096]{1,0:T(8,128)(2,1)}, u32[]{:S(2)}, u32[]{:S(2)}) collective-permute-start(bf16[72,4096]{1,0:T(8,128)(2,1)S(1)} %collective-permute-done.11.refs_1_), channel_id=1, source_target_pairs={{0,4},{2,6},{8,0},{10,2},{16,8},{18,10},{24,16},{26,18},{28,24},{3... | collective-permute-start | bytes 1769480 | tf_op jit(solution)/shard_map/ppermute | solution.py:427
  82.3 2.2 %shard_map.110.own_ref = f32[128,216]{1,0:T(8,128)S(1)} custom-call(bf16[128,4608]{1,0:T(8,128)(2,1)S(1)} %shard_map.108.patch_ref, bf16[72,4608]{1,0:T(8,128)(2,1)S(1)} %collective-permute-done.6.refs_0_.refs_4_, bf16[72,4608]{1,0:T(8,128)(2,1)} %collective-permute-done.7.refs_1_.refs_6_, bf16[72,4608]{1,0:T(8,128)(2,1)S(1)} %collective-permute-done.12.refs_2_.refs_5_), custom_call_target="tpu_custom_call" | custom-call | tf_op jit(solution)/shard_map/pallas_call | solution.py:555
  84.6 1.3 collective-permute-start.16
  86.4 6.2 %collective-permute-done.9.refs_0_.refs_3_ = bf16[72,4096]{1,0:T(8,128)(2,1)} collective-permute-done((bf16[72,4096]{1,0:T(8,128)(2,1)S(1)}, bf16[72,4096]{1,0:T(8,128)(2,1)}, u32[]{:S(2)}, u32[]{:S(2)}) %collective-permute-start.9) | collective-permute-done | bytes 589856 | tf_op jit(solution)/shard_map/ppermute | solution.py:427
  92.6 1.0 shard_map.111
  93.7 1.1 shard_map.112
  94.7 0.7 copy-done.24
  95.7 1.9 %collective-permute-start.19 = (bf16[72,4096]{1,0:T(8,128)(2,1)}, bf16[72,4096]{1,0:T(8,128)(2,1)}, u32[]{:S(2)}, u32[]{:S(2)}) collective-permute-start(bf16[72,4096]{1,0:T(8,128)(2,1)} %collective-permute-done.15.refs_2_), channel_id=1, source_target_pairs={{0,4},{2,6},{8,0},{10,2},{16,8},{18,10},{24,16},{26,18},{28,24},{3... | collective-permute-start | bytes 1769480 | tf_op jit(solution)/shard_map/ppermute | solution.py:427
  97.6 5.2 %all-to-all-start.1 = ((bf16[8,16,576]{2,1,0:T(8,128)(2,1)}), bf16[8,16,576]{2,1,0:T(8,128)(2,1)S(1)}, u32[]{:S(2)}, u32[]{:S(2)}) async-start(bf16[8,16,576]{2,1,0:T(8,128)(2,1)} %bitcast.15), calls=%async_computation.1 | async-start | bytes 327680 | tf_op jit(solution)/shard_map/all_to_all | solution.py:616
  102.8 1.1 copy-done.11
  103.9 1.1 copy-done.14
  104.9 2.1 %shard_map.113.refs_0_ = f32[128,216]{1,0:T(8,128)S(1)} custom-call(bf16[64,4096]{1,0:T(8,128)(2,1)S(1)} %bitcast.7, bf16[64,4096]{1,0:T(8,128)(2,1)S(1)} %collective-permute-done.8.send_ref, bf16[72,4096]{1,0:T(8,128)(2,1)S(1)} %copy-done.11, bf16[72,4096]{1,0:T(8,128)(2,1)S(1)} %copy-done.14, bf16[72,4096]{1,0:T(8,128)(2,1)} %collective-permute-done.15.refs_2_), custom_call_target="tpu_custom_call" | custom-call | tf_op jit(solution)/shard_map/pallas_call | solution.py:555
  107.0 1.3 collective-permute-start.17
  109.0 2.3 %collective-permute-done.17.refs_1_ = f32[128,216]{1,0:T(8,128)S(1)} collective-permute-done((f32[128,216]{1,0:T(8,128)S(1)}, f32[128,216]{1,0:T(8,128)S(1)}, u32[]{:S(2)}, u32[]{:S(2)}) %collective-permute-start.17) | collective-permute-done | bytes 110624 | tf_op jit(solution)/shard_map/ppermute | solution.py:416
  112.0 0.7 all-to-all-done.1
  112.7 1.2 collective-permute-start.18
  113.8 1.1 collective-permute-start.20
  115.0 2.5 %shard_map.114.refs_0_ = f32[128,216]{1,0:T(8,128)S(1)} custom-call(bf16[64,4096]{1,0:T(8,128)(2,1)S(1)} %bitcast.8, bf16[64,4096]{1,0:T(8,128)(2,1)S(1)} %collective-permute-done.8.send_ref, bf16[72,4096]{1,0:T(8,128)(2,1)} %collective-permute-done.9.refs_0_.refs_3_, bf16[72,4096]{1,0:T(8,128)(2,1)} %collective-permute-done.10.refs_1_.refs_4_, ...), custom_call_target="tpu_custom_call" | custom-call | tf_op jit(solution)/shard_map/pallas_call | solution.py:555
  117.5 1.3 collective-permute-start.21
  118.8 2.4 %shard_map.115 = (f32[64,2304]{1,0:T(8,128)S(1)}, f32[64,2304]{1,0:T(8,128)S(1)}, f32[64,2304]{1,0:T(8,128)S(1)}, f32[64,2304]{1,0:T(8,128)S(1)}) custom-call(s32[5]{0:T(128)S(1)} %copy-done.29, f32[128,216]{1,0:T(8,128)S(1)} %copy-done.21, f32[128,216]{1,0:T(8,128)S(1)} %copy-done.26, f32[128,360]{1,0:T(8,128)S(1)} %get-tuple-element.92.refs_2_, ...), custom_call_target="tpu_custom_call" | custom-call | tf_op jit(solution)/shard_map/pallas_call | solution.py:574
  121.6 2.5 %shard_map.116 = (f32[64,2304]{1,0:T(8,128)S(1)}, f32[64,2304]{1,0:T(8,128)S(1)}, f32[64,2304]{1,0:T(8,128)S(1)}, f32[64,2304]{1,0:T(8,128)S(1)}) custom-call(s32[5]{0:T(128)S(1)} %copy-done.29, f32[128,216]{1,0:T(8,128)S(1)} %shard_map.114.refs_0_, f32[128,216]{1,0:T(8,128)S(1)} %collective-permute-done.21.refs_1_, ...), custom_call_target="tpu_custom_call" | custom-call | tf_op jit(solution)/shard_map/pallas_call | solution.py:574
  124.1 2.2 %collective-permute-done.18.refs_0_.refs_6_ = bf16[72,4096]{1,0:T(8,128)(2,1)S(1)} collective-permute-done((bf16[72,4096]{1,0:T(8,128)(2,1)}, bf16[72,4096]{1,0:T(8,128)(2,1)S(1)}, u32[]{:S(2)}, u32[]{:S(2)}) %collective-permute-start.18) | collective-permute-done | bytes 589856 | tf_op jit(solution)/shard_map/ppermute | solution.py:427
  126.5 1.7 %shard_map.117 = (f32[128,144]{1,0:T(8,128)S(1)}, s32[5]{0:T(128)S(1)}) custom-call(s32[5]{0:T(128)S(1)} %copy-done.29, bf16[64,4096]{1,0:T(8,128)(2,1)S(1)} %bitcast.9, bf16[64,4096]{1,0:T(8,128)(2,1)S(1)} %collective-permute-done.8.send_ref, bf16[72,4096]{1,0:T(8,128)(2,1)S(1)} %collective-permute-done.18.refs_0_.refs_6_, ...), custom_call_target="tpu_custom_call" | custom-call | tf_op jit(solution)/shard_map/pallas_call | solution.py:560
  128.2 1.3 collective-permute-start.22
  129.5 5.3 %shard_map.118 = (f32[64,4096]{1,0:T(8,128)S(1)}, bf16[64,4096]{1,0:T(8,128)(2,1)S(1)}) custom-call(s32[5]{0:T(128)S(1)} %get-tuple-element.107.facts_ref, bf16[128,576]{1,0:T(8,128)(2,1)S(1)} %bitcast.10, bf16[72,4096]{1,0:T(8,128)(2,1)S(1)} %copy-done.12, bf16[72,4096]{1,0:T(8,128)(2,1)S(1)} %copy-done.15, ...), custom_call_target="tpu_custom_call" | custom-call | tf_op jit(solution)/shard_map/pallas_call | solution.py:602
  134.7 1.3 shard_map.119
  136.0 3.6 %collective-permute-start.24 = (bf16[64,2304]{1,0:T(8,128)(2,1)S(1)}, bf16[64,2304]{1,0:T(8,128)(2,1)S(1)}, u32[]{:S(2)}, u32[]{:S(2)}) collective-permute-start(bf16[64,2304]{1,0:T(8,128)(2,1)S(1)} %get-tuple-element.118), channel_id=1, source_target_pairs={{0,2},{2,0},{4,6},{6,4},{8,10},{10,8},{12,14},{14,12},{16,18},{18,... | collective-permute-start | bytes 884744 | tf_op jit(solution)/shard_map/ppermute | solution.py:408
  139.7 1.3 shard_map.121
  141.5 1.4 shard_map.120
  142.9 2.2 %collective-permute-start.26 = (bf16[256,576]{1,0:T(8,128)(2,1)S(1)}, bf16[256,576]{1,0:T(8,128)(2,1)S(1)}, u32[]{:S(2)}, u32[]{:S(2)}) collective-permute-start(bf16[256,576]{1,0:T(8,128)(2,1)S(1)} %get-tuple-element.126), channel_id=1, source_target_pairs={{2,0},{4,2},{6,4},{8,6},{10,8},{12,10},{14,12},{16,14},{18,16},{20... | collective-permute-start | bytes 884744 | tf_op jit(solution)/shard_map/ppermute | solution.py:391
  145.2 1.4 shard_map.122
  146.6 6.4 %collective-permute-done.26.odd_ref = bf16[256,576]{1,0:T(8,128)(2,1)S(1)} collective-permute-done((bf16[256,576]{1,0:T(8,128)(2,1)S(1)}, bf16[256,576]{1,0:T(8,128)(2,1)S(1)}, u32[]{:S(2)}, u32[]{:S(2)}) %collective-permute-start.26) | collective-permute-done | bytes 294944 | tf_op jit(solution)/shard_map/ppermute | solution.py:391
  153.0 0.9 shard_map.123
  154.2 0.9 add_convert_fusion
  155.1 1.3 collective-permute-done.27
  156.4 4.4 %shard_map.124 = bf16[2,196,576]{2,1,0:T(8,128)(2,1)S(1)} custom-call(f32[256,576]{1,0:T(8,128)S(1)} %get-tuple-element.125.even_ref, bf16[256,576]{1,0:T(8,128)(2,1)S(1)} %collective-permute-done.26.odd_ref, f32[512,576]{1,0:T(8,128)S(1)} %copy-done.1, f32[2,576]{1,0:T(2,128)S(1)} %get-tuple-element.127.excite_ref, f32[2,288]{1,0:T(2,128)S(1)} %add.9.sq_ref, ...), custom_call_target="tpu_custom_call" | custom-call | flops 2717908992 | bytes 4718592 | tf_op jit(solution)/shard_map/pallas_call | solution.py:375
  160.9 1.2 copy.12
  (83 shorter events, 4.8 us)
Async XLA Ops:
  0.6 4.4 %copy-start.18 = (bf16[9,576,48]{1,2,0:T(8,128)(2,1)S(1)}, bf16[9,576,48]{1,2,0:T(8,128)(2,1)}, u32[]{:S(2)}) copy-start(bf16[9,576,48]{1,2,0:T(8,128)(2,1)} %param.10) | copy-start | bytes 1492996
  0.6 4.4 %copy-start.22 = (bf16[576,288]{0,1:T(8,128)(2,1)S(1)}, bf16[576,288]{0,1:T(8,128)(2,1)}, u32[]{:S(2)}) copy-start(bf16[576,288]{0,1:T(8,128)(2,1)} %param.11) | copy-start | bytes 995332
  2.4 9.9 %copy-start.16 = (bf16[288,576]{1,0:T(8,128)(2,1)S(1)}, bf16[288,576]{1,0:T(8,128)(2,1)}, u32[]{:S(2)}) copy-start(bf16[288,576]{1,0:T(8,128)(2,1)} %expand_ref.3) | copy-start | bytes 995332
  2.4 15.8 %collective-permute-start.2 = (bf16[72,4608]{1,0:T(8,128)(2,1)S(1)}, bf16[72,4608]{1,0:T(8,128)(2,1)S(1)}, u32[]{:S(2)}, u32[]{:S(2)}) collective-permute-start(bf16[72,4608]{1,0:T(8,128)(2,1)S(1)} %reshape.11.refs_0_.refs_4_), channel_id=1, source_target_pairs={{0,8},{2,10},{8,16},{10,18},{16,24},{18,26},{24,28},{26,30},{28,20... | collective-permute-start | bytes 1990664 | tf_op jit(solution)/shard_map/ppermute | solution.py:427
  2.5 15.9 %collective-permute-start.3 = (bf16[72,4608]{1,0:T(8,128)(2,1)S(1)}, bf16[72,4608]{1,0:T(8,128)(2,1)S(1)}, u32[]{:S(2)}, u32[]{:S(2)}) collective-permute-start(bf16[72,4608]{1,0:T(8,128)(2,1)S(1)} %reshape.11.refs_0_.refs_4_), channel_id=1, source_target_pairs={{0,4},{2,6},{8,0},{10,2},{16,8},{18,10},{24,16},{26,18},{28,24},{3... | collective-permute-start | bytes 1990664 | tf_op jit(solution)/shard_map/ppermute | solution.py:427
  9.5 8.8 %copy-start = (f32[512,576]{1,0:T(8,128)}, f32[512,576]{1,0:T(8,128)S(1)}, u32[]{:S(2)}) copy-start(f32[512,576]{1,0:T(8,128)S(1)} %get-tuple-element.65.conv_ref) | copy-start | bytes 3538948
  9.5 2.8 %collective-permute-start = (f32[2,288]{1,0:T(2,128)S(1)}, f32[2,288]{1,0:T(2,128)S(1)}, u32[]{:S(2)}, u32[]{:S(2)}) collective-permute-start(f32[2,288]{1,0:T(2,128)S(1)} %get-tuple-element.68), channel_id=1, source_target_pairs={{0,1},{1,0},{2,3},{3,2},{4,5},{5,4},{6,7},{7,6},{8,9},{9,8},{10,11... | collective-permute-start | bytes 6920 | tf_op jit(solution)/shard_map/ppermute | solution.py:416
  18.2 49.0 %copy-start.2 = (bf16[72,4608]{1,0:T(8,128)(2,1)}, bf16[72,4608]{1,0:T(8,128)(2,1)S(1)}, u32[]{:S(2)}) copy-start(bf16[72,4608]{1,0:T(8,128)(2,1)S(1)} %collective-permute-done.2.refs_1_.refs_4_) | copy-start | bytes 1990660
  18.3 21.0 %collective-permute-start.4 = (bf16[72,4608]{1,0:T(8,128)(2,1)S(1)}, bf16[72,4608]{1,0:T(8,128)(2,1)S(1)}, u32[]{:S(2)}, u32[]{:S(2)}) collective-permute-start(bf16[72,4608]{1,0:T(8,128)(2,1)S(1)} %collective-permute-done.2.refs_1_.refs_4_), channel_id=1, source_target_pairs={{0,8},{2,10},{8,16},{10,18},{16,24},{18,26},{24,28},{26,30},{28,20... | collective-permute-start | bytes 1990664 | tf_op jit(solution)/shard_map/ppermute | solution.py:427
  19.5 19.8 %collective-permute-start.5 = (bf16[72,4608]{1,0:T(8,128)(2,1)S(1)}, bf16[72,4608]{1,0:T(8,128)(2,1)}, u32[]{:S(2)}, u32[]{:S(2)}) collective-permute-start(bf16[72,4608]{1,0:T(8,128)(2,1)S(1)} %collective-permute-done.3.refs_2_.refs_5_), channel_id=1, source_target_pairs={{0,4},{2,6},{8,0},{10,2},{16,8},{18,10},{24,16},{26,18},{28,24},{3... | collective-permute-start | bytes 1990664 | tf_op jit(solution)/shard_map/ppermute | solution.py:427
  19.8 0.8 copy-start.7
  20.6 18.7 %collective-permute-start.1 = (bf16[256,576]{1,0:T(8,128)(2,1)}, bf16[256,576]{1,0:T(8,128)(2,1)}, u32[]{:S(2)}, u32[]{:S(2)}) collective-permute-start(bf16[256,576]{1,0:T(8,128)(2,1)} %get-tuple-element.69), channel_id=1, source_target_pairs={{0,2},{2,4},{4,6},{6,8},{8,10},{10,12},{12,14},{14,16},{16,18},{18... | collective-permute-start | bytes 884744 | tf_op jit(solution)/shard_map/ppermute | solution.py:391
  27.0 23.2 %all-to-all-start = ((bf16[8,8,4096]{2,1,0:T(8,128)(2,1)}), bf16[8,8,4096]{2,1,0:T(8,128)(2,1)S(1)}, u32[]{:S(2)}, u32[]{:S(2)}) async-start(bf16[8,8,4096]{2,1,0:T(8,128)(2,1)} %bitcast.16), calls=%async_computation | async-start | bytes 1048576 | tf_op jit(solution)/shard_map/all_to_all | solution.py:616
  39.3 21.0 %copy-start.4 = (bf16[72,4608]{1,0:T(8,128)(2,1)}, bf16[72,4608]{1,0:T(8,128)(2,1)S(1)}, u32[]{:S(2)}) copy-start(bf16[72,4608]{1,0:T(8,128)(2,1)S(1)} %collective-permute-done.4.refs_3_.refs_5_) | copy-start | bytes 1990660
  39.3 19.4 %collective-permute-start.6 = (bf16[72,4608]{1,0:T(8,128)(2,1)S(1)}, bf16[72,4608]{1,0:T(8,128)(2,1)S(1)}, u32[]{:S(2)}, u32[]{:S(2)}) collective-permute-start(bf16[72,4608]{1,0:T(8,128)(2,1)S(1)} %collective-permute-done.4.refs_3_.refs_5_), channel_id=1, source_target_pairs={{0,8},{2,10},{8,16},{10,18},{16,24},{18,26},{24,28},{26,30},{28,20... | collective-permute-start | bytes 1990664 | tf_op jit(solution)/shard_map/ppermute | solution.py:427
  42.8 17.4 %collective-permute-start.7 = (bf16[72,4608]{1,0:T(8,128)(2,1)}, bf16[72,4608]{1,0:T(8,128)(2,1)}, u32[]{:S(2)}, u32[]{:S(2)}) collective-permute-start(bf16[72,4608]{1,0:T(8,128)(2,1)} %collective-permute-done.5.refs_4_.refs_6_), channel_id=1, source_target_pairs={{0,4},{2,6},{8,0},{10,2},{16,8},{18,10},{24,16},{26,18},{28,24},{3... | collective-permute-start | bytes 1990664 | tf_op jit(solution)/shard_map/ppermute | solution.py:427
  45.0 0.7 copy-start.27
  47.9 16.9 %collective-permute-start.13 = (bf16[64,4608]{1,0:T(8,128)(2,1)}, bf16[64,4608]{1,0:T(8,128)(2,1)}, u32[]{:S(2)}, u32[]{:S(2)}) collective-permute-start(bf16[64,4608]{1,0:T(8,128)(2,1)} %shard_map.107.own_ref), channel_id=1, source_target_pairs={{0,2},{2,0},{4,6},{6,4},{8,10},{10,8},{12,14},{14,12},{16,18},{18,... | collective-permute-start | bytes 1769480 | tf_op jit(solution)/shard_map/ppermute | solution.py:408
  50.2 17.1 %copy-start.8 = (bf16[72,4608]{1,0:T(8,128)(2,1)S(1)}, bf16[72,4608]{1,0:T(8,128)(2,1)}, u32[]{:S(2)}) copy-start(bf16[72,4608]{1,0:T(8,128)(2,1)} %copy-done.7) | copy-start | bytes 1990660
  60.3 7.0 %copy-start.5 = (bf16[72,4608]{1,0:T(8,128)(2,1)S(1)}, bf16[72,4608]{1,0:T(8,128)(2,1)}, u32[]{:S(2)}) copy-start(bf16[72,4608]{1,0:T(8,128)(2,1)} %copy-done.4) | copy-start | bytes 1990660
  60.3 20.1 %collective-permute-start.12 = (bf16[72,4608]{1,0:T(8,128)(2,1)S(1)}, bf16[72,4608]{1,0:T(8,128)(2,1)S(1)}, u32[]{:S(2)}, u32[]{:S(2)}) collective-permute-start(bf16[72,4608]{1,0:T(8,128)(2,1)S(1)} %collective-permute-done.6.refs_0_.refs_4_), channel_id=1, source_target_pairs={{0,8},{2,10},{8,16},{10,18},{16,24},{18,26},{24,28},{26,30},{28,20... | collective-permute-start | bytes 1990664 | tf_op jit(solution)/shard_map/ppermute | solution.py:427
  60.3 17.9 %collective-permute-start.11 = (bf16[72,4096]{1,0:T(8,128)(2,1)}, bf16[72,4096]{1,0:T(8,128)(2,1)S(1)}, u32[]{:S(2)}, u32[]{:S(2)}) collective-permute-start(bf16[72,4096]{1,0:T(8,128)(2,1)} %refs_0_.1), channel_id=1, source_target_pairs={{0,4},{2,6},{8,0},{10,2},{16,8},{18,10},{24,16},{26,18},{28,24},{3... | collective-permute-start | bytes 1769480 | tf_op jit(solution)/shard_map/ppermute | solution.py:427
  64.9 0.7 copy-start.28
  67.3 4.2 %copy-start.10 = (bf16[72,4096]{1,0:T(8,128)(2,1)S(1)}, bf16[72,4096]{1,0:T(8,128)(2,1)}, u32[]{:S(2)}) copy-start(bf16[72,4096]{1,0:T(8,128)(2,1)} %refs_0_.1) | copy-start | bytes 1769476
  70.2 22.4 %copy-start.29 = (s32[5]{0:T(128)S(1)}, s32[5]{0:T(128)}, u32[]{:S(2)}) copy-start(s32[5]{0:T(128)} %shard_map.104.facts_ref) | copy-start | bytes 64
  70.2 7.9 %collective-permute-start.14 = (f32[128,360]{1,0:T(8,128)S(1)}, f32[128,360]{1,0:T(8,128)S(1)}, u32[]{:S(2)}, u32[]{:S(2)}) collective-permute-start(f32[128,360]{1,0:T(8,128)S(1)} %shard_map.109.own_ref), channel_id=1, source_target_pairs={{0,1},{1,0},{2,3},{3,2},{4,5},{5,4},{6,7},{7,6},{8,9},{9,8},{10,11... | collective-permute-start | bytes 552968 | tf_op jit(solution)/shard_map/ppermute | solution.py:416
  71.5 21.1 %collective-permute-start.9 = (bf16[72,4096]{1,0:T(8,128)(2,1)S(1)}, bf16[72,4096]{1,0:T(8,128)(2,1)}, u32[]{:S(2)}, u32[]{:S(2)}) collective-permute-start(bf16[72,4096]{1,0:T(8,128)(2,1)S(1)} %copy-done.10), channel_id=1, source_target_pairs={{0,8},{2,10},{8,16},{10,18},{16,24},{18,26},{24,28},{26,30},{28,20... | collective-permute-start | bytes 1769480 | tf_op jit(solution)/shard_map/ppermute | solution.py:427
  78.1 6.4 %copy-start.13 = (bf16[72,4096]{1,0:T(8,128)(2,1)}, bf16[72,4096]{1,0:T(8,128)(2,1)S(1)}, u32[]{:S(2)}) copy-start(bf16[72,4096]{1,0:T(8,128)(2,1)S(1)} %collective-permute-done.11.refs_1_) | copy-start | bytes 1769476
  80.4 15.3 %collective-permute-start.15 = (bf16[72,4096]{1,0:T(8,128)(2,1)S(1)}, bf16[72,4096]{1,0:T(8,128)(2,1)}, u32[]{:S(2)}, u32[]{:S(2)}) collective-permute-start(bf16[72,4096]{1,0:T(8,128)(2,1)S(1)} %collective-permute-done.11.refs_1_), channel_id=1, source_target_pairs={{0,4},{2,6},{8,0},{10,2},{16,8},{18,10},{24,16},{26,18},{28,24},{3... | collective-permute-start | bytes 1769480 | tf_op jit(solution)/shard_map/ppermute | solution.py:427
  84.6 9.1 %collective-permute-start.16 = (f32[128,216]{1,0:T(8,128)S(1)}, f32[128,216]{1,0:T(8,128)S(1)}, u32[]{:S(2)}, u32[]{:S(2)}) collective-permute-start(f32[128,216]{1,0:T(8,128)S(1)} %shard_map.110.own_ref), channel_id=1, source_target_pairs={{0,1},{1,0},{2,3},{3,2},{4,5},{5,4},{6,7},{7,6},{8,9},{9,8},{10,11... | collective-permute-start | bytes 331784 | tf_op jit(solution)/shard_map/ppermute | solution.py:416
  85.9 16.9 %collective-permute-start.8 = (bf16[64,4096]{1,0:T(8,128)(2,1)S(1)}, bf16[64,4096]{1,0:T(8,128)(2,1)S(1)}, u32[]{:S(2)}, u32[]{:S(2)}) collective-permute-start(bf16[64,4096]{1,0:T(8,128)(2,1)S(1)} %bitcast.6), channel_id=1, source_target_pairs={{0,2},{2,0},{4,6},{6,4},{8,10},{10,8},{12,14},{14,12},{16,18},{18,... | collective-permute-start | bytes 1572872 | tf_op jit(solution)/shard_map/ppermute | solution.py:408
  92.6 16.4 %collective-permute-start.10 = (bf16[72,4096]{1,0:T(8,128)(2,1)}, bf16[72,4096]{1,0:T(8,128)(2,1)}, u32[]{:S(2)}, u32[]{:S(2)}) collective-permute-start(bf16[72,4096]{1,0:T(8,128)(2,1)} %collective-permute-done.9.refs_0_.refs_3_), channel_id=1, source_target_pairs={{0,8},{2,10},{8,16},{10,18},{16,24},{18,26},{24,28},{26,30},{28,20... | collective-permute-start | bytes 1769480 | tf_op jit(solution)/shard_map/ppermute | solution.py:427
  94.7 0.7 copy-start.24
  95.7 18.2 %collective-permute-start.19 = (bf16[72,4096]{1,0:T(8,128)(2,1)}, bf16[72,4096]{1,0:T(8,128)(2,1)}, u32[]{:S(2)}, u32[]{:S(2)}) collective-permute-start(bf16[72,4096]{1,0:T(8,128)(2,1)} %collective-permute-done.15.refs_2_), channel_id=1, source_target_pairs={{0,4},{2,6},{8,0},{10,2},{16,8},{18,10},{24,16},{26,18},{28,24},{3... | collective-permute-start | bytes 1769480 | tf_op jit(solution)/shard_map/ppermute | solution.py:427
  97.6 15.1 %all-to-all-start.1 = ((bf16[8,16,576]{2,1,0:T(8,128)(2,1)}), bf16[8,16,576]{2,1,0:T(8,128)(2,1)S(1)}, u32[]{:S(2)}, u32[]{:S(2)}) async-start(bf16[8,16,576]{2,1,0:T(8,128)(2,1)} %bitcast.15), calls=%async_computation.1 | async-start | bytes 327680 | tf_op jit(solution)/shard_map/all_to_all | solution.py:616
  102.8 1.1 copy-start.11
  103.9 1.1 copy-start.14
  107.0 4.3 %collective-permute-start.17 = (f32[128,216]{1,0:T(8,128)S(1)}, f32[128,216]{1,0:T(8,128)S(1)}, u32[]{:S(2)}, u32[]{:S(2)}) collective-permute-start(f32[128,216]{1,0:T(8,128)S(1)} %shard_map.113.refs_0_), channel_id=1, source_target_pairs={{0,1},{1,0},{2,3},{3,2},{4,5},{5,4},{6,7},{7,6},{8,9},{9,8},{10,11... | collective-permute-start | bytes 331784 | tf_op jit(solution)/shard_map/ppermute | solution.py:416
  108.3 0.7 copy-start.20
  111.3 0.7 copy-start.25
  112.7 6.1 %copy-start.9 = (bf16[72,4608]{1,0:T(8,128)(2,1)S(1)}, bf16[72,4608]{1,0:T(8,128)(2,1)}, u32[]{:S(2)}) copy-start(bf16[72,4608]{1,0:T(8,128)(2,1)} %copy-done.7) | copy-start | bytes 1990660
  112.7 6.1 %copy-start.21 = (f32[128,216]{1,0:T(8,128)S(1)}, f32[128,216]{1,0:T(8,128)}, u32[]{:S(2)}) copy-start(f32[128,216]{1,0:T(8,128)} %copy-done.20) | copy-start | bytes 331780
  112.7 6.1 %copy-start.26 = (f32[128,216]{1,0:T(8,128)S(1)}, f32[128,216]{1,0:T(8,128)}, u32[]{:S(2)}) copy-start(f32[128,216]{1,0:T(8,128)} %copy-done.25) | copy-start | bytes 331780
  112.7 13.7 %collective-permute-start.18 = (bf16[72,4096]{1,0:T(8,128)(2,1)}, bf16[72,4096]{1,0:T(8,128)(2,1)S(1)}, u32[]{:S(2)}, u32[]{:S(2)}) collective-permute-start(bf16[72,4096]{1,0:T(8,128)(2,1)} %collective-permute-done.10.refs_1_.refs_4_), channel_id=1, source_target_pairs={{0,8},{2,10},{8,16},{10,18},{16,24},{18,26},{24,28},{26,30},{28,20... | collective-permute-start | bytes 1769480 | tf_op jit(solution)/shard_map/ppermute | solution.py:427
  113.8 12.7 %collective-permute-start.20 = (bf16[72,4096]{1,0:T(8,128)(2,1)}, bf16[72,4096]{1,0:T(8,128)(2,1)S(1)}, u32[]{:S(2)}, u32[]{:S(2)}) collective-permute-start(bf16[72,4096]{1,0:T(8,128)(2,1)} %collective-permute-done.19.refs_2_.refs_5_), channel_id=1, source_target_pairs={{0,4},{2,6},{8,0},{10,2},{16,8},{18,10},{24,16},{26,18},{28,24},{3... | collective-permute-start | bytes 1769480 | tf_op jit(solution)/shard_map/ppermute | solution.py:427
  117.4 4.2 %copy-start.3 = (bf16[72,4608]{1,0:T(8,128)(2,1)S(1)}, bf16[72,4608]{1,0:T(8,128)(2,1)}, u32[]{:S(2)}) copy-start(bf16[72,4608]{1,0:T(8,128)(2,1)} %copy-done.2) | copy-start | bytes 1990660
  117.4 4.2 %copy-start.6 = (bf16[72,4608]{1,0:T(8,128)(2,1)S(1)}, bf16[72,4608]{1,0:T(8,128)(2,1)}, u32[]{:S(2)}) copy-start(bf16[72,4608]{1,0:T(8,128)(2,1)} %copy-done.4) | copy-start | bytes 1990660
  117.5 4.2 %collective-permute-start.21 = (f32[128,216]{1,0:T(8,128)S(1)}, f32[128,216]{1,0:T(8,128)S(1)}, u32[]{:S(2)}, u32[]{:S(2)}) collective-permute-start(f32[128,216]{1,0:T(8,128)S(1)} %shard_map.114.refs_0_), channel_id=1, source_target_pairs={{0,1},{1,0},{2,3},{3,2},{4,5},{5,4},{6,7},{7,6},{8,9},{9,8},{10,11... | collective-permute-start | bytes 331784 | tf_op jit(solution)/shard_map/ppermute | solution.py:416
  124.1 5.3 %copy-start.12 = (bf16[72,4096]{1,0:T(8,128)(2,1)S(1)}, bf16[72,4096]{1,0:T(8,128)(2,1)}, u32[]{:S(2)}) copy-start(bf16[72,4096]{1,0:T(8,128)(2,1)} %refs_0_.1) | copy-start | bytes 1769476
  124.1 5.3 %copy-start.15 = (bf16[72,4096]{1,0:T(8,128)(2,1)S(1)}, bf16[72,4096]{1,0:T(8,128)(2,1)}, u32[]{:S(2)}) copy-start(bf16[72,4096]{1,0:T(8,128)(2,1)} %copy-done.13) | copy-start | bytes 1769476
  128.2 6.5 %collective-permute-start.22 = (f32[128,144]{1,0:T(8,128)S(1)}, f32[128,144]{1,0:T(8,128)S(1)}, u32[]{:S(2)}, u32[]{:S(2)}) collective-permute-start(f32[128,144]{1,0:T(8,128)S(1)} %get-tuple-element.120.refs_0_), channel_id=1, source_target_pairs={{0,1},{1,0},{2,3},{3,2},{4,5},{5,4},{6,7},{7,6},{8,9},{9,8},{10,11... | collective-permute-start | bytes 221192 | tf_op jit(solution)/shard_map/ppermute | solution.py:416
  136.0 5.5 %collective-permute-start.24 = (bf16[64,2304]{1,0:T(8,128)(2,1)S(1)}, bf16[64,2304]{1,0:T(8,128)(2,1)S(1)}, u32[]{:S(2)}, u32[]{:S(2)}) collective-permute-start(bf16[64,2304]{1,0:T(8,128)(2,1)S(1)} %get-tuple-element.118), channel_id=1, source_target_pairs={{0,2},{2,0},{4,6},{6,4},{8,10},{10,8},{12,14},{14,12},{16,18},{18,... | collective-permute-start | bytes 884744 | tf_op jit(solution)/shard_map/ppermute | solution.py:408
  139.6 14.6 %collective-permute-start.23 = (bf16[64,4096]{1,0:T(8,128)(2,1)S(1)}, bf16[64,4096]{1,0:T(8,128)(2,1)S(1)}, u32[]{:S(2)}, u32[]{:S(2)}) collective-permute-start(bf16[64,4096]{1,0:T(8,128)(2,1)S(1)} %get-tuple-element.112), channel_id=1, source_target_pairs={{0,2},{2,0},{4,6},{6,4},{8,10},{10,8},{12,14},{14,12},{16,18},{18,... | collective-permute-start | bytes 1572872 | tf_op jit(solution)/shard_map/ppermute | solution.py:408
  141.0 12.0 %copy-start.1 = (f32[512,576]{1,0:T(8,128)S(1)}, f32[512,576]{1,0:T(8,128)}, u32[]{:S(2)}) copy-start(f32[512,576]{1,0:T(8,128)} %copy-done) | copy-start | bytes 3538948
  141.0 12.0 %copy-start.17 = (bf16[288,576]{1,0:T(8,128)(2,1)S(1)}, bf16[288,576]{1,0:T(8,128)(2,1)}, u32[]{:S(2)}) copy-start(bf16[288,576]{1,0:T(8,128)(2,1)} %expand_ref.3) | copy-start | bytes 995332
  141.0 4.2 %collective-permute-start.25 = (bf16[64,2304]{1,0:T(8,128)(2,1)S(1)}, bf16[64,2304]{1,0:T(8,128)(2,1)S(1)}, u32[]{:S(2)}, u32[]{:S(2)}) collective-permute-start(bf16[64,2304]{1,0:T(8,128)(2,1)S(1)} %get-tuple-element.124), channel_id=1, source_target_pairs={{0,2},{2,0},{4,6},{6,4},{8,10},{10,8},{12,14},{14,12},{16,18},{18,... | collective-permute-start | bytes 884744 | tf_op jit(solution)/shard_map/ppermute | solution.py:408
  142.9 10.1 %collective-permute-start.26 = (bf16[256,576]{1,0:T(8,128)(2,1)S(1)}, bf16[256,576]{1,0:T(8,128)(2,1)S(1)}, u32[]{:S(2)}, u32[]{:S(2)}) collective-permute-start(bf16[256,576]{1,0:T(8,128)(2,1)S(1)} %get-tuple-element.126), channel_id=1, source_target_pairs={{2,0},{4,2},{6,4},{8,6},{10,8},{12,10},{14,12},{16,14},{18,16},{20... | collective-permute-start | bytes 884744 | tf_op jit(solution)/shard_map/ppermute | solution.py:391
  153.9 2.5 %copy-start.19 = (bf16[9,576,48]{1,2,0:T(8,128)(2,1)S(1)}, bf16[9,576,48]{1,2,0:T(8,128)(2,1)}, u32[]{:S(2)}) copy-start(bf16[9,576,48]{1,2,0:T(8,128)(2,1)} %param.10) | copy-start | bytes 1492996
  153.9 2.5 %copy-start.23 = (bf16[576,288]{0,1:T(8,128)(2,1)S(1)}, bf16[576,288]{0,1:T(8,128)(2,1)}, u32[]{:S(2)}) copy-start(bf16[576,288]{0,1:T(8,128)(2,1)} %param.11) | copy-start | bytes 995332
  153.9 2.5 %collective-permute-start.27 = (f32[2,288]{1,0:T(2,128)S(1)}, f32[2,288]{1,0:T(2,128)S(1)}, u32[]{:S(2)}, u32[]{:S(2)}) collective-permute-start(f32[2,288]{1,0:T(2,128)S(1)} %shard_map.123), channel_id=1, source_target_pairs={{0,1},{1,0},{2,3},{3,2},{4,5},{5,4},{6,7},{7,6},{8,9},{9,8},{10,11... | collective-permute-start | bytes 6920 | tf_op jit(solution)/shard_map/ppermute | solution.py:416

commit v11 on v10

--- a/solution.py
+++ b/solution.py
@@ -13,6 +13,7 @@
 FRAME_ROWS = WIDE * WIDE
 EDGE = 8
 LANES = 128
+WINDOW = 256
 VMEM_BYTES = 16 * 2**20
 FREE = pl.CostEstimate(flops=0, bytes_accessed=0, transcendentals=0)
 
@@ -91,7 +92,11 @@
     rows = shift_ref.shape[1]
     for col in range(3):
         at = EDGE + sign * (col - 1)
-        shift_ref[col] = wide_ref[at : at + rows, :].astype(jnp.bfloat16)
+        chans = wide_ref.shape[1]
+        shift_ref[col, :, 0:chans] = wide_ref[at : at + rows, :].astype(jnp.bfloat16)
+        if shift_ref.shape[2] > chans:
+            blank = jnp.zeros((rows, shift_ref.shape[2] - chans), jnp.bfloat16)
+            shift_ref[col, :, chans:] = blank
 
 
 def conv_kernel(feat_ref, group_ref, squeeze_ref, *refs):
@@ -218,12 +223,16 @@
     chans = out_ref.shape[1]
     rows = own_ref[...] + mate_ref[...].astype(jnp.float32)
     pieces = [rows[:, tap * chans : (tap + 1) * chans] for tap in range(4)]
-    frame = jnp.dot(
-        select_rows(False), jnp.concatenate(pieces, axis=0), precision=lax.Precision.HIGHEST
-    ) * inside(FRAME_ROWS)
+    rows = jnp.concatenate(pieces, axis=0)
+    select = select_rows(False).astype(jnp.bfloat16)
+    coarse = rows.astype(jnp.bfloat16)
+    frame = jnp.dot(select, coarse, preferred_element_type=jnp.float32)
     if out_ref.dtype == jnp.bfloat16:
         frame = frame * facts_ref[3].astype(jnp.float32)
-    out_ref[...] = frame.astype(out_ref.dtype)
+    else:
+        rest = (rows - coarse.astype(jnp.float32)).astype(jnp.bfloat16)
+        frame += jnp.dot(select, rest, preferred_element_type=jnp.float32)
+    out_ref[...] = (frame * inside(FRAME_ROWS)).astype(out_ref.dtype)
 
 
 def excite_grad_kernel(even_ref, odd_ref, conv_ref, excite_ref, expand_ref, out_ref):
@@ -238,11 +247,10 @@
 
 
 def conv_grad_kernel(
-    even_ref, odd_ref, conv_ref, excite_ref, sq_ref, relaxed_ref, squeeze_ref, group_ref,
-    out_ref, flat_ref, wide_ref, shift_ref, grad_ref,
+    width, even_ref, odd_ref, conv_ref, excite_ref, sq_ref, relaxed_ref, squeeze_ref, *refs
 ):
+    *dense_refs, out_ref, flat_ref, wide_ref, shift_ref, grad_ref = refs
     frames, _, chans = out_ref.shape
-    width = group_ref.shape[1]
     rows = frames * FRAME_ROWS
     grad_squeezed = relaxed_ref[...] * silu_slope(sq_ref[...])
     pooled = jnp.dot(
@@ -260,17 +268,18 @@
         wide_ref[EDGE + at : EDGE + at + FRAME_ROWS, :] = active * slope * good
     store_shifts(wide_ref, shift_ref, -1)
     body = rows - 2 * WIDE
-    for block in channel_blocks(chans, width):
-        _, _, start, end = block
-        spread, same = block_tools(block, width)
-        total = jnp.zeros((body, end - start), jnp.float32)
+    for block, dense_ref in zip(channel_blocks(chans, width), dense_refs):
+        start = block[2]
+        sources = []
         for tap in range(9):
             down, across = divmod(tap, 3)
-            weights = dense_tap(group_ref, tap, block, spread, same)
             at = (2 - down) * WIDE
-            source = shift_ref[across, at : at + body, start:end]
-            total += jnp.dot(source, weights, preferred_element_type=jnp.float32)
-        grad_ref[WIDE : WIDE + body, start:end] += total
+            sources.append(shift_ref[across, at : at + body, start : start + WINDOW])
+        total = jnp.dot(
+            jnp.concatenate(sources, axis=1), dense_ref[...], preferred_element_type=jnp.float32
+        )
+        end = min(chans, start + WINDOW)
+        grad_ref[WIDE : WIDE + body, start:end] += total[:, : end - start]
     for frame in range(frames):
         for y in range(SIDE):
             at = frame * FRAME_ROWS + (y + 1) * WIDE + 1
@@ -369,20 +378,40 @@
     )(even, odd, conv, excite, squeeze_out)
 
 
-def conv_backward(even, odd, conv, excite, squeezed, grad_relaxed, squeeze_in, group_kernel):
+def conv_backward(even, odd, conv, excite, squeezed, grad_relaxed, squeeze_in, dense, width):
     rows, chans = conv.shape
     frames = rows // FRAME_ROWS
+    lanes = channel_blocks(chans, width)[-1][2] + WINDOW
     return whole_call(
-        conv_grad_kernel,
+        functools.partial(conv_grad_kernel, width),
         bf16(frames, SIDE * SIDE, chans),
         [
             pltpu.VMEM((SIDE * SIDE, chans), jnp.float32),
             pltpu.VMEM((rows + 2 * EDGE, chans), jnp.float32),
-            pltpu.VMEM((3, rows, chans), jnp.bfloat16),
+            pltpu.VMEM((3, rows, lanes), jnp.bfloat16),
             pltpu.VMEM((rows, chans), jnp.float32),
         ],
         pl.CostEstimate(flops=rows * chans * 9216, bytes_accessed=16 * rows * chans, transcendentals=0),
-    )(even, odd, conv, excite, squeezed, grad_relaxed, squeeze_in, group_kernel)
+    )(even, odd, conv, excite, squeezed, grad_relaxed, squeeze_in, *dense)
+
+
+def dense_kernel(facts_ref, group_ref, *dense_refs):
+    _, width, chans = group_ref.shape
+    for block, dense_ref in zip(channel_blocks(chans, width), dense_refs):
+        low, high, start, _ = block
+        end = min(chans, start + WINDOW)
+        spread, same = block_tools((low, high, start, start + WINDOW), width)
+        dense_ref[...] = jnp.zeros_like(dense_ref)
+        for tap in range(9):
+            full = jnp.dot(spread, group_ref[tap, :, start:end], preferred_element_type=jnp.float32)
+            rows = slice(tap * WINDOW, (tap + 1) * WINDOW)
+            dense_ref[rows, 0 : end - start] = (full * same[:, : end - start]).astype(jnp.bfloat16)
+
+
+def dense_weights(facts, group_kernel):
+    _, width, chans = group_kernel.shape
+    outs = (bf16(9 * WINDOW, WINDOW),) * len(channel_blocks(chans, width))
+    return facts_call(dense_kernel, outs, facts, (group_kernel,))
 
 
 def shifted(value, axis, by):
@@ -457,23 +486,33 @@
     return (token < jnp.where(block == 0, facts_ref[1], facts_ref[2])).astype(jnp.float32)
 
 
+def stacked_dot(pieces, blocks):
+    if blocks[0].shape[0] % 8 == 0:
+        pieces = [jnp.concatenate(pieces, axis=1)]
+        blocks = [jnp.concatenate(blocks, axis=0)]
+    total = 0.0
+    for piece, block in zip(pieces, blocks):
+        total += jnp.dot(piece, block, preferred_element_type=jnp.float32)
+    return total
+
+
 def totals_kernel(pieces, unit, parts, first, facts_ref, *refs):
     grad_act = refs[0][...] + refs[1][...]
     count = len(pieces)
     slopes, blocks = refs[2:4], refs[4 : 4 + count]
     before, after = refs[4 + count : -2 * len(parts)], refs[-2 * len(parts) :]
     rows, width = grad_act.shape[0], blocks[0].shape[0]
-    matrix = reorder_matrix(facts_ref[0], unit, False)
-    factors = []
-    for place, (source, index) in enumerate(pieces):
-        piece = grad_act[:, place * width : (place + 1) * width]
-        piece = piece * slopes[source][:, index * width : (index + 1) * width]
-        piece = jnp.dot(matrix, piece.astype(jnp.bfloat16), preferred_element_type=jnp.float32)
-        factors.append(piece.astype(jnp.bfloat16))
+    slope = jnp.concatenate(
+        [slopes[source][:, index * width : (index + 1) * width] for source, index in pieces], axis=1
+    )
+    factor = jnp.dot(
+        reorder_matrix(facts_ref[0], unit, False),
+        (grad_act * slope).astype(jnp.bfloat16),
+        preferred_element_type=jnp.float32,
+    ).astype(jnp.bfloat16)
+    factors = [factor[:, place * width : (place + 1) * width] for place in range(count)]
     for part, lanes in enumerate(parts):
-        total = 0.0
-        for factor, ref in zip(factors, blocks):
-            total += jnp.dot(factor, ref[:, lanes], preferred_element_type=jnp.float32)
+        total = stacked_dot(factors, [ref[:, lanes] for ref in blocks])
         for half in range(2):
             value = total[half * rows // 2 : (half + 1) * rows // 2]
             value = value if first else before[2 * part + half][...] + value
@@ -539,12 +578,13 @@
     width = buffers[0].shape[0]
     matrix = exchange_matrix(facts_ref[0], unit, False)
     act = jnp.dot(matrix, act_ref[...], preferred_element_type=jnp.float32).astype(jnp.bfloat16)
-    total = 0.0
-    for offset, copy, buffer in zip(offsets, copies, buffers):
-        columns = block_columns(facts_ref, offset, chips, width)
-        piece = contract_last(act, columns).astype(jnp.bfloat16)
+    pieces = [
+        contract_last(act, block_columns(facts_ref, offset, chips, width)).astype(jnp.bfloat16)
+        for offset in offsets
+    ]
+    for copy in copies:
         copy.wait()
-        total += jnp.dot(piece, buffer[...], preferred_element_type=jnp.float32)
+    total = stacked_dot(pieces, [buffer[...] for buffer in buffers])
     rows = keep_ref.shape[0]
     keep_ref[...] = total[:rows]
     send_ref[...] = total[rows:].astype(jnp.bfloat16)
@@ -711,13 +751,14 @@
     )
     lead, facts_late = return_patches(facts, halo_own, swap_cores(halo_mate), chans, jnp.bfloat16)
     grad_odd = shifted(lead, "ctx", -1)
-    grad_even, _ = return_patches(
+    grad_even, facts_late = return_patches(
         facts_late, even_own, swap_cores(even_mate), chans, jnp.float32
     )
     grad_relaxed = sum_tp(excite_grad(grad_even, grad_odd, conv, excite, squeeze_out))
     llm_tokens = (tokens[0] + swap_cores(tokens[1]).astype(jnp.float32)).astype(jnp.bfloat16)
     grad_features = conv_backward(
-        grad_even, grad_odd, conv, excite, squeezed, grad_relaxed, squeeze_in, group_kernel
+        grad_even, grad_odd, conv, excite, squeezed, grad_relaxed, squeeze_in,
+        dense_weights(facts_late, group_kernel), group_kernel.shape[1],
     )
     return (llm_tokens, grad_features)
 

time: 164 us -> 160 us (0.976)
  Pallas kernels: 45.4 us -> 41.7 us
    pallas_call x1, Pallas kernels: 5.25 us -> 3.49 us  [token_products(): pl.pallas_call(functools.partial(token_kernel, offsets, chips, unit), out...]
    pallas_call x1, Pallas kernels: 4.43 us -> 2.74 us  [conv_backward(): whole_call(functools.partial(conv_grad_kernel, width), bf16(frames, SIDE...]
    unnamed x62 -> x60, local copies, waits for them, and re-layouts: 8.62 us -> 7.95 us
    pallas_call x6 -> x7, Pallas kernels: 9.49 us -> 9.58 us  [facts_call(): pl.pallas_call(kernel, out_shape=outs, in_specs=vmem_specs(len(operands))...]
where the time goes in v11:
time: 160 us; the launch traced here: 158 us
  starting transfers between devices  52.4 us (33%)
  waiting for transfers between devices  52.2 us (33%)
  Pallas kernels  41.7 us (26%)
  local copies, waits for them, and re-layouts  9.68 us (6%)
    ppermute x14, waiting for transfers between devices, ring_send(): return lax.ppermute(value, 'ctx', ring_pairs(lax.axis_size('ctx'), by))  33.7 us
    ppermute x14, starting transfers between devices, ring_send(): return lax.ppermute(value, 'ctx', ring_pairs(lax.axis_size('ctx'), by))  18.3 us
    ppermute x2, waiting for transfers between devices, shifted(): return lax.ppermute(value, axis, pairs)  12.7 us
    all_to_all x2, starting transfers between devices, chips_exchange(): lax.all_to_all(value, 'ctx', split_axis=0, concat_axis=0, tiled=True, axi...  9.87 us
    pallas_call x4, Pallas kernels, block_products(): whole_call(kernel, f32(rows, len(blocks) * blocks[0].shape[0]), [])  9.64 us
    pallas_call x7, Pallas kernels, facts_call(): pl.pallas_call(kernel, out_shape=outs, in_specs=vmem_specs(len(operands))...  9.58 us
    ppermute x7, starting transfers between devices, tp_terms(): other = lax.ppermute(value, 'tp', [(i, i ^ reach) for i in range(size)])  8.99 us
    ppermute x2, starting transfers between devices, shifted(): return lax.ppermute(value, axis, pairs)  8.36 us
  transfers between devices with their start and end apart: 30, of which 17 were waited for; matrix products, arithmetic and copies ran while one was open for 1% of the time, Pallas kernels for 23%

profile of v11, /device:TPU:3, one launch (start us, length us, event | category | flops | bytes accessed | tf_op | source)
XLA Modules:
  0.0 158.0 jit_solution(16841509804766887873)
XLA Ops:
  0.7 1.7 %reshape.11.refs_0_.refs_4_ = bf16[72,4608]{1,0:T(8,128)(2,1)S(1)} reshape(bf16[72,8,576]{2,1,0:T(8,128)(2,1)} %param.13) | data formatting | bytes 1327104 | tf_op jit(solution)/shard_map/reshape | solution.py:675
  2.5 1.5 collective-permute-start.3
  3.9 1.1 copy.11.feat_ref
  5.0 4.4 %shard_map.105 = (f32[512,576]{1,0:T(8,128)S(1)}, bf16[512,576]{1,0:T(8,128)(2,1)S(1)}, f32[2,288]{1,0:T(2,128)S(1)}) custom-call(bf16[2,196,576]{2,1,0:T(8,128)(2,1)S(1)} %copy.11.feat_ref, bf16[9,48,576]{2,1,0:T(8,128)(2,1)S(1)} %bitcast.10, bf16[288,576]{1,0:T(8,128)(2,1)S(1)} %bitcast.13), custom_call_target="tpu_custom_call" | custom-call | tf_op jit(solution)/shard_map/pallas_call | solution.py:301
  9.5 1.3 collective-permute-start
  10.8 1.5 collective-permute-done
  12.3 1.5 shard_map.106
  13.7 4.5 %collective-permute-done.2.refs_1_.refs_4_ = bf16[72,4608]{1,0:T(8,128)(2,1)S(1)} collective-permute-done((bf16[72,4608]{1,0:T(8,128)(2,1)S(1)}, bf16[72,4608]{1,0:T(8,128)(2,1)S(1)}, u32[]{:S(2)}, u32[]{:S(2)}) %collective-permute-start.2) | collective-permute-done | bytes 663584 | tf_op jit(solution)/shard_map/ppermute | solution.py:456
  18.3 1.1 collective-permute-start.4
  19.8 0.8 copy-done.7
  20.6 6.4 %collective-permute-start.1 = (bf16[256,576]{1,0:T(8,128)(2,1)}, bf16[256,576]{1,0:T(8,128)(2,1)}, u32[]{:S(2)}, u32[]{:S(2)}) collective-permute-start(bf16[256,576]{1,0:T(8,128)(2,1)} %get-tuple-element.73), channel_id=1, source_target_pairs={{0,2},{2,4},{4,6},{6,8},{8,10},{10,12},{12,14},{14,16},{16,18},{18... | collective-permute-start | bytes 884744 | tf_op jit(solution)/shard_map/ppermute | solution.py:420
  27.0 4.7 %all-to-all-start = ((bf16[8,8,4096]{2,1,0:T(8,128)(2,1)}), bf16[8,8,4096]{2,1,0:T(8,128)(2,1)S(1)}, u32[]{:S(2)}, u32[]{:S(2)}) async-start(bf16[8,8,4096]{2,1,0:T(8,128)(2,1)} %bitcast.16), calls=%async_computation | async-start | bytes 1048576 | tf_op jit(solution)/shard_map/all_to_all | solution.py:656
  31.7 7.6 %collective-permute-done.1.halo_ref = bf16[256,576]{1,0:T(8,128)(2,1)} collective-permute-done((bf16[256,576]{1,0:T(8,128)(2,1)}, bf16[256,576]{1,0:T(8,128)(2,1)}, u32[]{:S(2)}, u32[]{:S(2)}) %collective-permute-start.1) | collective-permute-done | bytes 294944 | tf_op jit(solution)/shard_map/ppermute | solution.py:420
  39.3 3.5 %collective-permute-start.6 = (bf16[72,4608]{1,0:T(8,128)(2,1)S(1)}, bf16[72,4608]{1,0:T(8,128)(2,1)S(1)}, u32[]{:S(2)}, u32[]{:S(2)}) collective-permute-start(bf16[72,4608]{1,0:T(8,128)(2,1)S(1)} %collective-permute-done.4.refs_3_.refs_5_), channel_id=1, source_target_pairs={{0,8},{2,10},{8,16},{10,18},{16,24},{18,26},{24,28},{26,30},{28,20... | collective-permute-start | bytes 1990664 | tf_op jit(solution)/shard_map/ppermute | solution.py:456
  42.8 0.9 collective-permute-start.7
  43.8 1.3 shard_map.104.facts_ref
  45.7 2.3 %shard_map.107.own_ref = bf16[64,4608]{1,0:T(8,128)(2,1)} custom-call(s32[5]{0:T(128)S(1)} %copy-done.27, bf16[256,576]{1,0:T(8,128)(2,1)} %collective-permute-done.1.halo_ref, bf16[256,576]{1,0:T(8,128)(2,1)S(1)} %get-tuple-element.85.even_ref), custom_call_target="tpu_custom_call" | custom-call | tf_op jit(solution)/shard_map/pallas_call | solution.py:349
  47.9 2.2 %collective-permute-start.13 = (bf16[64,4608]{1,0:T(8,128)(2,1)}, bf16[64,4608]{1,0:T(8,128)(2,1)}, u32[]{:S(2)}, u32[]{:S(2)}) collective-permute-start(bf16[64,4608]{1,0:T(8,128)(2,1)} %shard_map.107.own_ref), channel_id=1, source_target_pairs={{0,2},{2,0},{4,6},{6,4},{8,10},{10,8},{12,14},{14,12},{16,18},{18,... | collective-permute-start | bytes 1769480 | tf_op jit(solution)/shard_map/ppermute | solution.py:437
  50.2 8.5 %collective-permute-done.6.refs_0_.refs_4_ = bf16[72,4608]{1,0:T(8,128)(2,1)S(1)} collective-permute-done((bf16[72,4608]{1,0:T(8,128)(2,1)S(1)}, bf16[72,4608]{1,0:T(8,128)(2,1)S(1)}, u32[]{:S(2)}, u32[]{:S(2)}) %collective-permute-start.6) | collective-permute-done | bytes 663584 | tf_op jit(solution)/shard_map/ppermute | solution.py:456
  58.7 1.6 collective-permute-done.7.refs_1_.refs_6_
  60.3 4.6 %collective-permute-start.11 = (bf16[72,4096]{1,0:T(8,128)(2,1)}, bf16[72,4096]{1,0:T(8,128)(2,1)S(1)}, u32[]{:S(2)}, u32[]{:S(2)}) collective-permute-start(bf16[72,4096]{1,0:T(8,128)(2,1)} %refs_0_.1), channel_id=1, source_target_pairs={{0,4},{2,6},{8,0},{10,2},{16,8},{18,10},{24,16},{26,18},{28,24},{3... | collective-permute-start | bytes 1769480 | tf_op jit(solution)/shard_map/ppermute | solution.py:456
  64.9 1.7 %shard_map.108.patch_ref = bf16[128,4608]{1,0:T(8,128)(2,1)S(1)} custom-call(s32[5]{0:T(128)S(1)} %copy-done.28, bf16[64,4608]{1,0:T(8,128)(2,1)} %shard_map.107.own_ref, bf16[64,4608]{1,0:T(8,128)(2,1)} %collective-permute-done.13.mate_ref), custom_call_target="tpu_custom_call" | custom-call | tf_op jit(solution)/shard_map/pallas_call | solution.py:338
  66.7 2.9 %shard_map.109.own_ref = f32[128,360]{1,0:T(8,128)S(1)} custom-call(bf16[128,4608]{1,0:T(8,128)(2,1)S(1)} %shard_map.108.patch_ref, bf16[72,4608]{1,0:T(8,128)(2,1)S(1)} %reshape.11.refs_0_.refs_4_, bf16[72,4608]{1,0:T(8,128)(2,1)S(1)} %collective-permute-done.2.refs_1_.refs_4_, bf16[72,4608]{1,0:T(8,128)(2,1)S(1)} %copy-done.8, ...), custom_call_target="tpu_custom_call" | custom-call | tf_op jit(solution)/shard_map/pallas_call | solution.py:595
  69.6 1.3 collective-permute-start.14
  70.9 7.3 %collective-permute-done.11.refs_1_ = bf16[72,4096]{1,0:T(8,128)(2,1)S(1)} collective-permute-done((bf16[72,4096]{1,0:T(8,128)(2,1)}, bf16[72,4096]{1,0:T(8,128)(2,1)S(1)}, u32[]{:S(2)}, u32[]{:S(2)}) %collective-permute-start.11) | collective-permute-done | bytes 589856 | tf_op jit(solution)/shard_map/ppermute | solution.py:456
  78.2 2.2 %collective-permute-done.12.refs_2_.refs_5_ = bf16[72,4608]{1,0:T(8,128)(2,1)S(1)} collective-permute-done((bf16[72,4608]{1,0:T(8,128)(2,1)S(1)}, bf16[72,4608]{1,0:T(8,128)(2,1)S(1)}, u32[]{:S(2)}, u32[]{:S(2)}) %collective-permute-start.12) | collective-permute-done | bytes 663584 | tf_op jit(solution)/shard_map/ppermute | solution.py:456
  80.4 2.0 %collective-permute-start.15 = (bf16[72,4096]{1,0:T(8,128)(2,1)S(1)}, bf16[72,4096]{1,0:T(8,128)(2,1)}, u32[]{:S(2)}, u32[]{:S(2)}) collective-permute-start(bf16[72,4096]{1,0:T(8,128)(2,1)S(1)} %collective-permute-done.11.refs_1_), channel_id=1, source_target_pairs={{0,4},{2,6},{8,0},{10,2},{16,8},{18,10},{24,16},{26,18},{28,24},{3... | collective-permute-start | bytes 1769480 | tf_op jit(solution)/shard_map/ppermute | solution.py:456
  82.3 2.2 %shard_map.110.own_ref = f32[128,216]{1,0:T(8,128)S(1)} custom-call(bf16[128,4608]{1,0:T(8,128)(2,1)S(1)} %shard_map.108.patch_ref, bf16[72,4608]{1,0:T(8,128)(2,1)S(1)} %collective-permute-done.6.refs_0_.refs_4_, bf16[72,4608]{1,0:T(8,128)(2,1)} %collective-permute-done.7.refs_1_.refs_6_, bf16[72,4608]{1,0:T(8,128)(2,1)S(1)} %collective-permute-done.12.refs_2_.refs_5_), custom_call_target="tpu_custom_call" | custom-call | tf_op jit(solution)/shard_map/pallas_call | solution.py:595
  84.6 1.3 collective-permute-start.16
  86.4 6.2 %collective-permute-done.9.refs_0_.refs_3_ = bf16[72,4096]{1,0:T(8,128)(2,1)} collective-permute-done((bf16[72,4096]{1,0:T(8,128)(2,1)S(1)}, bf16[72,4096]{1,0:T(8,128)(2,1)}, u32[]{:S(2)}, u32[]{:S(2)}) %collective-permute-start.9) | collective-permute-done | bytes 589856 | tf_op jit(solution)/shard_map/ppermute | solution.py:456
  92.6 1.0 shard_map.111
  93.7 1.1 shard_map.112
  95.7 1.9 %collective-permute-start.19 = (bf16[72,4096]{1,0:T(8,128)(2,1)}, bf16[72,4096]{1,0:T(8,128)(2,1)}, u32[]{:S(2)}, u32[]{:S(2)}) collective-permute-start(bf16[72,4096]{1,0:T(8,128)(2,1)} %collective-permute-done.15.refs_2_), channel_id=1, source_target_pairs={{0,4},{2,6},{8,0},{10,2},{16,8},{18,10},{24,16},{26,18},{28,24},{3... | collective-permute-start | bytes 1769480 | tf_op jit(solution)/shard_map/ppermute | solution.py:456
  97.6 5.2 %all-to-all-start.1 = ((bf16[8,16,576]{2,1,0:T(8,128)(2,1)}), bf16[8,16,576]{2,1,0:T(8,128)(2,1)S(1)}, u32[]{:S(2)}, u32[]{:S(2)}) async-start(bf16[8,16,576]{2,1,0:T(8,128)(2,1)} %bitcast.15), calls=%async_computation.1 | async-start | bytes 327680 | tf_op jit(solution)/shard_map/all_to_all | solution.py:656
  102.8 1.1 copy-done.11
  103.9 1.1 copy-done.14
  104.9 2.1 %shard_map.113.refs_0_ = f32[128,216]{1,0:T(8,128)S(1)} custom-call(bf16[64,4096]{1,0:T(8,128)(2,1)S(1)} %bitcast.7, bf16[64,4096]{1,0:T(8,128)(2,1)S(1)} %collective-permute-done.8.send_ref, bf16[72,4096]{1,0:T(8,128)(2,1)S(1)} %copy-done.11, bf16[72,4096]{1,0:T(8,128)(2,1)S(1)} %copy-done.14, bf16[72,4096]{1,0:T(8,128)(2,1)} %collective-permute-done.15.refs_2_), custom_call_target="tpu_custom_call" | custom-call | tf_op jit(solution)/shard_map/pallas_call | solution.py:595
  107.0 1.3 collective-permute-start.17
  109.0 2.3 %collective-permute-done.17.refs_1_ = f32[128,216]{1,0:T(8,128)S(1)} collective-permute-done((f32[128,216]{1,0:T(8,128)S(1)}, f32[128,216]{1,0:T(8,128)S(1)}, u32[]{:S(2)}, u32[]{:S(2)}) %collective-permute-start.17) | collective-permute-done | bytes 110624 | tf_op jit(solution)/shard_map/ppermute | solution.py:445
  112.0 0.7 all-to-all-done.1
  112.7 1.2 collective-permute-start.18
  113.8 1.1 collective-permute-start.20
  115.0 2.5 %shard_map.114.refs_0_ = f32[128,216]{1,0:T(8,128)S(1)} custom-call(bf16[64,4096]{1,0:T(8,128)(2,1)S(1)} %bitcast.8, bf16[64,4096]{1,0:T(8,128)(2,1)S(1)} %collective-permute-done.8.send_ref, bf16[72,4096]{1,0:T(8,128)(2,1)} %collective-permute-done.9.refs_0_.refs_3_, bf16[72,4096]{1,0:T(8,128)(2,1)} %collective-permute-done.10.refs_1_.refs_4_, ...), custom_call_target="tpu_custom_call" | custom-call | tf_op jit(solution)/shard_map/pallas_call | solution.py:595
  117.4 1.3 collective-permute-start.21
  118.8 1.9 %shard_map.115 = (f32[64,2304]{1,0:T(8,128)S(1)}, f32[64,2304]{1,0:T(8,128)S(1)}, f32[64,2304]{1,0:T(8,128)S(1)}, f32[64,2304]{1,0:T(8,128)S(1)}) custom-call(s32[5]{0:T(128)S(1)} %copy-done.28, f32[128,216]{1,0:T(8,128)S(1)} %copy-done.21, f32[128,216]{1,0:T(8,128)S(1)} %copy-done.26, f32[128,360]{1,0:T(8,128)S(1)} %get-tuple-element.96.refs_2_, ...), custom_call_target="tpu_custom_call" | custom-call | tf_op jit(solution)/shard_map/pallas_call | solution.py:614
  120.6 1.0 collective-permute-done.21.refs_1_
  121.6 1.8 %shard_map.116 = (f32[64,2304]{1,0:T(8,128)S(1)}, f32[64,2304]{1,0:T(8,128)S(1)}, f32[64,2304]{1,0:T(8,128)S(1)}, f32[64,2304]{1,0:T(8,128)S(1)}) custom-call(s32[5]{0:T(128)S(1)} %copy-done.28, f32[128,216]{1,0:T(8,128)S(1)} %shard_map.114.refs_0_, f32[128,216]{1,0:T(8,128)S(1)} %collective-permute-done.21.refs_1_, ...), custom_call_target="tpu_custom_call" | custom-call | tf_op jit(solution)/shard_map/pallas_call | solution.py:614
  123.5 2.9 %collective-permute-done.18.refs_0_.refs_6_ = bf16[72,4096]{1,0:T(8,128)(2,1)S(1)} collective-permute-done((bf16[72,4096]{1,0:T(8,128)(2,1)}, bf16[72,4096]{1,0:T(8,128)(2,1)S(1)}, u32[]{:S(2)}, u32[]{:S(2)}) %collective-permute-start.18) | collective-permute-done | bytes 589856 | tf_op jit(solution)/shard_map/ppermute | solution.py:456
  126.5 1.7 %shard_map.117 = (f32[128,144]{1,0:T(8,128)S(1)}, s32[5]{0:T(128)S(1)}) custom-call(s32[5]{0:T(128)S(1)} %copy-done.28, bf16[64,4096]{1,0:T(8,128)(2,1)S(1)} %bitcast.9, bf16[64,4096]{1,0:T(8,128)(2,1)S(1)} %collective-permute-done.8.send_ref, bf16[72,4096]{1,0:T(8,128)(2,1)S(1)} %collective-permute-done.18.refs_0_.refs_6_, ...), custom_call_target="tpu_custom_call" | custom-call | tf_op jit(solution)/shard_map/pallas_call | solution.py:600
  128.2 1.3 collective-permute-start.22
  129.5 3.5 %shard_map.118 = (f32[64,4096]{1,0:T(8,128)S(1)}, bf16[64,4096]{1,0:T(8,128)(2,1)S(1)}) custom-call(s32[5]{0:T(128)S(1)} %get-tuple-element.111.facts_ref, bf16[128,576]{1,0:T(8,128)(2,1)S(1)} %bitcast.12, bf16[72,4096]{1,0:T(8,128)(2,1)S(1)} %copy-done.12, bf16[72,4096]{1,0:T(8,128)(2,1)S(1)} %copy-done.15, ...), custom_call_target="tpu_custom_call" | custom-call | tf_op jit(solution)/shard_map/pallas_call | solution.py:642
  133.0 1.1 shard_map.119
  134.1 3.6 %collective-permute-start.24 = (bf16[64,2304]{1,0:T(8,128)(2,1)S(1)}, bf16[64,2304]{1,0:T(8,128)(2,1)S(1)}, u32[]{:S(2)}, u32[]{:S(2)}) collective-permute-start(bf16[64,2304]{1,0:T(8,128)(2,1)S(1)} %get-tuple-element.122), channel_id=1, source_target_pairs={{0,2},{2,0},{4,6},{6,4},{8,10},{10,8},{12,14},{14,12},{16,18},{18,... | collective-permute-start | bytes 884744 | tf_op jit(solution)/shard_map/ppermute | solution.py:437
  137.8 1.0 shard_map.121
  139.3 1.3 shard_map.120
  140.7 2.0 %collective-permute-start.26 = (bf16[256,576]{1,0:T(8,128)(2,1)S(1)}, bf16[256,576]{1,0:T(8,128)(2,1)S(1)}, u32[]{:S(2)}, u32[]{:S(2)}) collective-permute-start(bf16[256,576]{1,0:T(8,128)(2,1)S(1)} %get-tuple-element.130), channel_id=1, source_target_pairs={{2,0},{4,2},{6,4},{8,6},{10,8},{12,10},{14,12},{16,14},{18,16},{20... | collective-permute-start | bytes 884744 | tf_op jit(solution)/shard_map/ppermute | solution.py:420
  142.7 1.2 shard_map.122
  143.9 1.7 %shard_map.124 = (bf16[2304,256]{1,0:T(8,128)(2,1)S(1)}, bf16[2304,256]{1,0:T(8,128)(2,1)S(1)}, bf16[2304,256]{1,0:T(8,128)(2,1)S(1)}) custom-call(s32[5]{0:T(128)S(1)} %get-tuple-element.132.facts_ref, bf16[9,48,576]{2,1,0:T(8,128)(2,1)S(1)} %bitcast.11), custom_call_target="tpu_custom_call" | custom-call | tf_op jit(solution)/shard_map/pallas_call | solution.py:614
  145.6 5.1 %collective-permute-done.26.odd_ref = bf16[256,576]{1,0:T(8,128)(2,1)S(1)} collective-permute-done((bf16[256,576]{1,0:T(8,128)(2,1)S(1)}, bf16[256,576]{1,0:T(8,128)(2,1)S(1)}, u32[]{:S(2)}, u32[]{:S(2)}) %collective-permute-start.26) | collective-permute-done | bytes 294944 | tf_op jit(solution)/shard_map/ppermute | solution.py:420
  150.7 0.9 shard_map.123
  151.6 1.2 collective-permute-start.27
  152.8 0.9 add_convert_fusion
  154.1 2.7 %shard_map.125 = bf16[2,196,576]{2,1,0:T(8,128)(2,1)S(1)} custom-call(f32[256,576]{1,0:T(8,128)S(1)} %get-tuple-element.129.even_ref, bf16[256,576]{1,0:T(8,128)(2,1)S(1)} %collective-permute-done.26.odd_ref, f32[512,576]{1,0:T(8,128)S(1)} %copy-done.1, f32[2,576]{1,0:T(2,128)S(1)} %get-tuple-element.131.excite_ref, f32[2,288]{1,0:T(2,128)S(1)} %add.9.sq_ref, ...), custom_call_target="tpu_custom_call" | custom-call | flops 2717908992 | bytes 4718592 | tf_op jit(solution)/shard_map/pallas_call | solution.py:385
  156.8 1.2 copy.12
  (82 shorter events, 5.1 us)
Async XLA Ops:
  0.6 4.4 %copy-start.16 = (bf16[9,576,48]{1,2,0:T(8,128)(2,1)S(1)}, bf16[9,576,48]{1,2,0:T(8,128)(2,1)}, u32[]{:S(2)}) copy-start(bf16[9,576,48]{1,2,0:T(8,128)(2,1)} %param.10) | copy-start | bytes 1492996
  0.6 4.4 %copy-start.22 = (bf16[576,288]{0,1:T(8,128)(2,1)S(1)}, bf16[576,288]{0,1:T(8,128)(2,1)}, u32[]{:S(2)}) copy-start(bf16[576,288]{0,1:T(8,128)(2,1)} %param.11) | copy-start | bytes 995332
  2.4 9.9 %copy-start.18 = (bf16[288,576]{1,0:T(8,128)(2,1)S(1)}, bf16[288,576]{1,0:T(8,128)(2,1)}, u32[]{:S(2)}) copy-start(bf16[288,576]{1,0:T(8,128)(2,1)} %expand_ref.3) | copy-start | bytes 995332
  2.4 15.8 %collective-permute-start.2 = (bf16[72,4608]{1,0:T(8,128)(2,1)S(1)}, bf16[72,4608]{1,0:T(8,128)(2,1)S(1)}, u32[]{:S(2)}, u32[]{:S(2)}) collective-permute-start(bf16[72,4608]{1,0:T(8,128)(2,1)S(1)} %reshape.11.refs_0_.refs_4_), channel_id=1, source_target_pairs={{0,8},{2,10},{8,16},{10,18},{16,24},{18,26},{24,28},{26,30},{28,20... | collective-permute-start | bytes 1990664 | tf_op jit(solution)/shard_map/ppermute | solution.py:456
  2.5 15.9 %collective-permute-start.3 = (bf16[72,4608]{1,0:T(8,128)(2,1)S(1)}, bf16[72,4608]{1,0:T(8,128)(2,1)S(1)}, u32[]{:S(2)}, u32[]{:S(2)}) collective-permute-start(bf16[72,4608]{1,0:T(8,128)(2,1)S(1)} %reshape.11.refs_0_.refs_4_), channel_id=1, source_target_pairs={{0,4},{2,6},{8,0},{10,2},{16,8},{18,10},{24,16},{26,18},{28,24},{3... | collective-permute-start | bytes 1990664 | tf_op jit(solution)/shard_map/ppermute | solution.py:456
  9.5 8.8 %copy-start = (f32[512,576]{1,0:T(8,128)}, f32[512,576]{1,0:T(8,128)S(1)}, u32[]{:S(2)}) copy-start(f32[512,576]{1,0:T(8,128)S(1)} %get-tuple-element.69.conv_ref) | copy-start | bytes 3538948
  9.5 2.8 %collective-permute-start = (f32[2,288]{1,0:T(2,128)S(1)}, f32[2,288]{1,0:T(2,128)S(1)}, u32[]{:S(2)}, u32[]{:S(2)}) collective-permute-start(f32[2,288]{1,0:T(2,128)S(1)} %get-tuple-element.72), channel_id=1, source_target_pairs={{0,1},{1,0},{2,3},{3,2},{4,5},{5,4},{6,7},{7,6},{8,9},{9,8},{10,11... | collective-permute-start | bytes 6920 | tf_op jit(solution)/shard_map/ppermute | solution.py:445
  18.2 48.4 %copy-start.2 = (bf16[72,4608]{1,0:T(8,128)(2,1)}, bf16[72,4608]{1,0:T(8,128)(2,1)S(1)}, u32[]{:S(2)}) copy-start(bf16[72,4608]{1,0:T(8,128)(2,1)S(1)} %collective-permute-done.2.refs_1_.refs_4_) | copy-start | bytes 1990660
  18.3 21.0 %collective-permute-start.4 = (bf16[72,4608]{1,0:T(8,128)(2,1)S(1)}, bf16[72,4608]{1,0:T(8,128)(2,1)S(1)}, u32[]{:S(2)}, u32[]{:S(2)}) collective-permute-start(bf16[72,4608]{1,0:T(8,128)(2,1)S(1)} %collective-permute-done.2.refs_1_.refs_4_), channel_id=1, source_target_pairs={{0,8},{2,10},{8,16},{10,18},{16,24},{18,26},{24,28},{26,30},{28,20... | collective-permute-start | bytes 1990664 | tf_op jit(solution)/shard_map/ppermute | solution.py:456
  19.5 19.8 %collective-permute-start.5 = (bf16[72,4608]{1,0:T(8,128)(2,1)S(1)}, bf16[72,4608]{1,0:T(8,128)(2,1)}, u32[]{:S(2)}, u32[]{:S(2)}) collective-permute-start(bf16[72,4608]{1,0:T(8,128)(2,1)S(1)} %collective-permute-done.3.refs_2_.refs_5_), channel_id=1, source_target_pairs={{0,4},{2,6},{8,0},{10,2},{16,8},{18,10},{24,16},{26,18},{28,24},{3... | collective-permute-start | bytes 1990664 | tf_op jit(solution)/shard_map/ppermute | solution.py:456
  19.8 0.8 copy-start.7
  20.6 18.7 %collective-permute-start.1 = (bf16[256,576]{1,0:T(8,128)(2,1)}, bf16[256,576]{1,0:T(8,128)(2,1)}, u32[]{:S(2)}, u32[]{:S(2)}) collective-permute-start(bf16[256,576]{1,0:T(8,128)(2,1)} %get-tuple-element.73), channel_id=1, source_target_pairs={{0,2},{2,4},{4,6},{6,8},{8,10},{10,12},{12,14},{14,16},{16,18},{18... | collective-permute-start | bytes 884744 | tf_op jit(solution)/shard_map/ppermute | solution.py:420
  27.0 23.2 %all-to-all-start = ((bf16[8,8,4096]{2,1,0:T(8,128)(2,1)}), bf16[8,8,4096]{2,1,0:T(8,128)(2,1)S(1)}, u32[]{:S(2)}, u32[]{:S(2)}) async-start(bf16[8,8,4096]{2,1,0:T(8,128)(2,1)} %bitcast.16), calls=%async_computation | async-start | bytes 1048576 | tf_op jit(solution)/shard_map/all_to_all | solution.py:656
  39.3 21.0 %copy-start.4 = (bf16[72,4608]{1,0:T(8,128)(2,1)}, bf16[72,4608]{1,0:T(8,128)(2,1)S(1)}, u32[]{:S(2)}) copy-start(bf16[72,4608]{1,0:T(8,128)(2,1)S(1)} %collective-permute-done.4.refs_3_.refs_5_) | copy-start | bytes 1990660
  39.3 19.4 %collective-permute-start.6 = (bf16[72,4608]{1,0:T(8,128)(2,1)S(1)}, bf16[72,4608]{1,0:T(8,128)(2,1)S(1)}, u32[]{:S(2)}, u32[]{:S(2)}) collective-permute-start(bf16[72,4608]{1,0:T(8,128)(2,1)S(1)} %collective-permute-done.4.refs_3_.refs_5_), channel_id=1, source_target_pairs={{0,8},{2,10},{8,16},{10,18},{16,24},{18,26},{24,28},{26,30},{28,20... | collective-permute-start | bytes 1990664 | tf_op jit(solution)/shard_map/ppermute | solution.py:456
  42.8 17.4 %collective-permute-start.7 = (bf16[72,4608]{1,0:T(8,128)(2,1)}, bf16[72,4608]{1,0:T(8,128)(2,1)}, u32[]{:S(2)}, u32[]{:S(2)}) collective-permute-start(bf16[72,4608]{1,0:T(8,128)(2,1)} %collective-permute-done.5.refs_4_.refs_6_), channel_id=1, source_target_pairs={{0,4},{2,6},{8,0},{10,2},{16,8},{18,10},{24,16},{26,18},{28,24},{3... | collective-permute-start | bytes 1990664 | tf_op jit(solution)/shard_map/ppermute | solution.py:456
  45.0 0.7 copy-start.27
  45.7 19.2 %copy-start.28 = (s32[5]{0:T(128)S(1)}, s32[5]{0:T(128)}, u32[]{:S(2)}) copy-start(s32[5]{0:T(128)} %shard_map.104.facts_ref) | copy-start | bytes 64
  47.9 17.0 %collective-permute-start.13 = (bf16[64,4608]{1,0:T(8,128)(2,1)}, bf16[64,4608]{1,0:T(8,128)(2,1)}, u32[]{:S(2)}, u32[]{:S(2)}) collective-permute-start(bf16[64,4608]{1,0:T(8,128)(2,1)} %shard_map.107.own_ref), channel_id=1, source_target_pairs={{0,2},{2,0},{4,6},{6,4},{8,10},{10,8},{12,14},{14,12},{16,18},{18,... | collective-permute-start | bytes 1769480 | tf_op jit(solution)/shard_map/ppermute | solution.py:437
  60.3 6.4 %copy-start.5 = (bf16[72,4608]{1,0:T(8,128)(2,1)S(1)}, bf16[72,4608]{1,0:T(8,128)(2,1)}, u32[]{:S(2)}) copy-start(bf16[72,4608]{1,0:T(8,128)(2,1)} %copy-done.4) | copy-start | bytes 1990660
  60.3 6.4 %copy-start.8 = (bf16[72,4608]{1,0:T(8,128)(2,1)S(1)}, bf16[72,4608]{1,0:T(8,128)(2,1)}, u32[]{:S(2)}) copy-start(bf16[72,4608]{1,0:T(8,128)(2,1)} %copy-done.7) | copy-start | bytes 1990660
  60.3 20.1 %collective-permute-start.12 = (bf16[72,4608]{1,0:T(8,128)(2,1)S(1)}, bf16[72,4608]{1,0:T(8,128)(2,1)S(1)}, u32[]{:S(2)}, u32[]{:S(2)}) collective-permute-start(bf16[72,4608]{1,0:T(8,128)(2,1)S(1)} %collective-permute-done.6.refs_0_.refs_4_), channel_id=1, source_target_pairs={{0,8},{2,10},{8,16},{10,18},{16,24},{18,26},{24,28},{26,30},{28,20... | collective-permute-start | bytes 1990664 | tf_op jit(solution)/shard_map/ppermute | solution.py:456
  60.3 17.9 %collective-permute-start.11 = (bf16[72,4096]{1,0:T(8,128)(2,1)}, bf16[72,4096]{1,0:T(8,128)(2,1)S(1)}, u32[]{:S(2)}, u32[]{:S(2)}) collective-permute-start(bf16[72,4096]{1,0:T(8,128)(2,1)} %refs_0_.1), channel_id=1, source_target_pairs={{0,4},{2,6},{8,0},{10,2},{16,8},{18,10},{24,16},{26,18},{28,24},{3... | collective-permute-start | bytes 1769480 | tf_op jit(solution)/shard_map/ppermute | solution.py:456
  66.7 4.2 %copy-start.10 = (bf16[72,4096]{1,0:T(8,128)(2,1)S(1)}, bf16[72,4096]{1,0:T(8,128)(2,1)}, u32[]{:S(2)}) copy-start(bf16[72,4096]{1,0:T(8,128)(2,1)} %refs_0_.1) | copy-start | bytes 1769476
  69.6 8.6 %collective-permute-start.14 = (f32[128,360]{1,0:T(8,128)S(1)}, f32[128,360]{1,0:T(8,128)S(1)}, u32[]{:S(2)}, u32[]{:S(2)}) collective-permute-start(f32[128,360]{1,0:T(8,128)S(1)} %shard_map.109.own_ref), channel_id=1, source_target_pairs={{0,1},{1,0},{2,3},{3,2},{4,5},{5,4},{6,7},{7,6},{8,9},{9,8},{10,11... | collective-permute-start | bytes 552968 | tf_op jit(solution)/shard_map/ppermute | solution.py:445
  70.9 21.7 %collective-permute-start.9 = (bf16[72,4096]{1,0:T(8,128)(2,1)S(1)}, bf16[72,4096]{1,0:T(8,128)(2,1)}, u32[]{:S(2)}, u32[]{:S(2)}) collective-permute-start(bf16[72,4096]{1,0:T(8,128)(2,1)S(1)} %copy-done.10), channel_id=1, source_target_pairs={{0,8},{2,10},{8,16},{10,18},{16,24},{18,26},{24,28},{26,30},{28,20... | collective-permute-start | bytes 1769480 | tf_op jit(solution)/shard_map/ppermute | solution.py:456
  78.2 6.4 %copy-start.13 = (bf16[72,4096]{1,0:T(8,128)(2,1)}, bf16[72,4096]{1,0:T(8,128)(2,1)S(1)}, u32[]{:S(2)}) copy-start(bf16[72,4096]{1,0:T(8,128)(2,1)S(1)} %collective-permute-done.11.refs_1_) | copy-start | bytes 1769476
  80.4 15.3 %collective-permute-start.15 = (bf16[72,4096]{1,0:T(8,128)(2,1)S(1)}, bf16[72,4096]{1,0:T(8,128)(2,1)}, u32[]{:S(2)}, u32[]{:S(2)}) collective-permute-start(bf16[72,4096]{1,0:T(8,128)(2,1)S(1)} %collective-permute-done.11.refs_1_), channel_id=1, source_target_pairs={{0,4},{2,6},{8,0},{10,2},{16,8},{18,10},{24,16},{26,18},{28,24},{3... | collective-permute-start | bytes 1769480 | tf_op jit(solution)/shard_map/ppermute | solution.py:456
  84.6 9.1 %collective-permute-start.16 = (f32[128,216]{1,0:T(8,128)S(1)}, f32[128,216]{1,0:T(8,128)S(1)}, u32[]{:S(2)}, u32[]{:S(2)}) collective-permute-start(f32[128,216]{1,0:T(8,128)S(1)} %shard_map.110.own_ref), channel_id=1, source_target_pairs={{0,1},{1,0},{2,3},{3,2},{4,5},{5,4},{6,7},{7,6},{8,9},{9,8},{10,11... | collective-permute-start | bytes 331784 | tf_op jit(solution)/shard_map/ppermute | solution.py:445
  85.9 16.9 %collective-permute-start.8 = (bf16[64,4096]{1,0:T(8,128)(2,1)S(1)}, bf16[64,4096]{1,0:T(8,128)(2,1)S(1)}, u32[]{:S(2)}, u32[]{:S(2)}) collective-permute-start(bf16[64,4096]{1,0:T(8,128)(2,1)S(1)} %bitcast.6), channel_id=1, source_target_pairs={{0,2},{2,0},{4,6},{6,4},{8,10},{10,8},{12,14},{14,12},{16,18},{18,... | collective-permute-start | bytes 1572872 | tf_op jit(solution)/shard_map/ppermute | solution.py:437
  92.6 16.4 %collective-permute-start.10 = (bf16[72,4096]{1,0:T(8,128)(2,1)}, bf16[72,4096]{1,0:T(8,128)(2,1)}, u32[]{:S(2)}, u32[]{:S(2)}) collective-permute-start(bf16[72,4096]{1,0:T(8,128)(2,1)} %collective-permute-done.9.refs_0_.refs_3_), channel_id=1, source_target_pairs={{0,8},{2,10},{8,16},{10,18},{16,24},{18,26},{24,28},{26,30},{28,20... | collective-permute-start | bytes 1769480 | tf_op jit(solution)/shard_map/ppermute | solution.py:456
  94.7 0.7 copy-start.24
  95.7 18.1 %collective-permute-start.19 = (bf16[72,4096]{1,0:T(8,128)(2,1)}, bf16[72,4096]{1,0:T(8,128)(2,1)}, u32[]{:S(2)}, u32[]{:S(2)}) collective-permute-start(bf16[72,4096]{1,0:T(8,128)(2,1)} %collective-permute-done.15.refs_2_), channel_id=1, source_target_pairs={{0,4},{2,6},{8,0},{10,2},{16,8},{18,10},{24,16},{26,18},{28,24},{3... | collective-permute-start | bytes 1769480 | tf_op jit(solution)/shard_map/ppermute | solution.py:456
  97.6 15.1 %all-to-all-start.1 = ((bf16[8,16,576]{2,1,0:T(8,128)(2,1)}), bf16[8,16,576]{2,1,0:T(8,128)(2,1)S(1)}, u32[]{:S(2)}, u32[]{:S(2)}) async-start(bf16[8,16,576]{2,1,0:T(8,128)(2,1)} %bitcast.15), calls=%async_computation.1 | async-start | bytes 327680 | tf_op jit(solution)/shard_map/all_to_all | solution.py:656
  102.8 1.1 copy-start.11
  103.9 1.1 copy-start.14
  107.0 4.3 %collective-permute-start.17 = (f32[128,216]{1,0:T(8,128)S(1)}, f32[128,216]{1,0:T(8,128)S(1)}, u32[]{:S(2)}, u32[]{:S(2)}) collective-permute-start(f32[128,216]{1,0:T(8,128)S(1)} %shard_map.113.refs_0_), channel_id=1, source_target_pairs={{0,1},{1,0},{2,3},{3,2},{4,5},{5,4},{6,7},{7,6},{8,9},{9,8},{10,11... | collective-permute-start | bytes 331784 | tf_op jit(solution)/shard_map/ppermute | solution.py:445
  108.3 0.7 copy-start.20
  111.3 0.7 copy-start.25
  112.7 6.1 %copy-start.9 = (bf16[72,4608]{1,0:T(8,128)(2,1)S(1)}, bf16[72,4608]{1,0:T(8,128)(2,1)}, u32[]{:S(2)}) copy-start(bf16[72,4608]{1,0:T(8,128)(2,1)} %copy-done.7) | copy-start | bytes 1990660
  112.7 6.1 %copy-start.21 = (f32[128,216]{1,0:T(8,128)S(1)}, f32[128,216]{1,0:T(8,128)}, u32[]{:S(2)}) copy-start(f32[128,216]{1,0:T(8,128)} %copy-done.20) | copy-start | bytes 331780
  112.7 6.1 %copy-start.26 = (f32[128,216]{1,0:T(8,128)S(1)}, f32[128,216]{1,0:T(8,128)}, u32[]{:S(2)}) copy-start(f32[128,216]{1,0:T(8,128)} %copy-done.25) | copy-start | bytes 331780
  112.7 13.7 %collective-permute-start.18 = (bf16[72,4096]{1,0:T(8,128)(2,1)}, bf16[72,4096]{1,0:T(8,128)(2,1)S(1)}, u32[]{:S(2)}, u32[]{:S(2)}) collective-permute-start(bf16[72,4096]{1,0:T(8,128)(2,1)} %collective-permute-done.10.refs_1_.refs_4_), channel_id=1, source_target_pairs={{0,8},{2,10},{8,16},{10,18},{16,24},{18,26},{24,28},{26,30},{28,20... | collective-permute-start | bytes 1769480 | tf_op jit(solution)/shard_map/ppermute | solution.py:456
  113.8 12.7 %collective-permute-start.20 = (bf16[72,4096]{1,0:T(8,128)(2,1)}, bf16[72,4096]{1,0:T(8,128)(2,1)S(1)}, u32[]{:S(2)}, u32[]{:S(2)}) collective-permute-start(bf16[72,4096]{1,0:T(8,128)(2,1)} %collective-permute-done.19.refs_2_.refs_5_), channel_id=1, source_target_pairs={{0,4},{2,6},{8,0},{10,2},{16,8},{18,10},{24,16},{26,18},{28,24},{3... | collective-permute-start | bytes 1769480 | tf_op jit(solution)/shard_map/ppermute | solution.py:456
  117.4 4.2 %collective-permute-start.21 = (f32[128,216]{1,0:T(8,128)S(1)}, f32[128,216]{1,0:T(8,128)S(1)}, u32[]{:S(2)}, u32[]{:S(2)}) collective-permute-start(f32[128,216]{1,0:T(8,128)S(1)} %shard_map.114.refs_0_), channel_id=1, source_target_pairs={{0,1},{1,0},{2,3},{3,2},{4,5},{5,4},{6,7},{7,6},{8,9},{9,8},{10,11... | collective-permute-start | bytes 331784 | tf_op jit(solution)/shard_map/ppermute | solution.py:445
  118.7 2.9 %copy-start.3 = (bf16[72,4608]{1,0:T(8,128)(2,1)S(1)}, bf16[72,4608]{1,0:T(8,128)(2,1)}, u32[]{:S(2)}) copy-start(bf16[72,4608]{1,0:T(8,128)(2,1)} %copy-done.2) | copy-start | bytes 1990660
  118.8 2.9 %copy-start.6 = (bf16[72,4608]{1,0:T(8,128)(2,1)S(1)}, bf16[72,4608]{1,0:T(8,128)(2,1)}, u32[]{:S(2)}) copy-start(bf16[72,4608]{1,0:T(8,128)(2,1)} %copy-done.4) | copy-start | bytes 1990660
  123.5 6.0 %copy-start.12 = (bf16[72,4096]{1,0:T(8,128)(2,1)S(1)}, bf16[72,4096]{1,0:T(8,128)(2,1)}, u32[]{:S(2)}) copy-start(bf16[72,4096]{1,0:T(8,128)(2,1)} %refs_0_.1) | copy-start | bytes 1769476
  123.5 6.0 %copy-start.15 = (bf16[72,4096]{1,0:T(8,128)(2,1)S(1)}, bf16[72,4096]{1,0:T(8,128)(2,1)}, u32[]{:S(2)}) copy-start(bf16[72,4096]{1,0:T(8,128)(2,1)} %copy-done.13) | copy-start | bytes 1769476
  128.2 4.8 %collective-permute-start.22 = (f32[128,144]{1,0:T(8,128)S(1)}, f32[128,144]{1,0:T(8,128)S(1)}, u32[]{:S(2)}, u32[]{:S(2)}) collective-permute-start(f32[128,144]{1,0:T(8,128)S(1)} %get-tuple-element.124.refs_0_), channel_id=1, source_target_pairs={{0,1},{1,0},{2,3},{3,2},{4,5},{5,4},{6,7},{7,6},{8,9},{9,8},{10,11... | collective-permute-start | bytes 221192 | tf_op jit(solution)/shard_map/ppermute | solution.py:445
  134.1 5.3 %collective-permute-start.24 = (bf16[64,2304]{1,0:T(8,128)(2,1)S(1)}, bf16[64,2304]{1,0:T(8,128)(2,1)S(1)}, u32[]{:S(2)}, u32[]{:S(2)}) collective-permute-start(bf16[64,2304]{1,0:T(8,128)(2,1)S(1)} %get-tuple-element.122), channel_id=1, source_target_pairs={{0,2},{2,0},{4,6},{6,4},{8,10},{10,8},{12,14},{14,12},{16,18},{18,... | collective-permute-start | bytes 884744 | tf_op jit(solution)/shard_map/ppermute | solution.py:437
  137.7 15.1 %collective-permute-start.23 = (bf16[64,4096]{1,0:T(8,128)(2,1)S(1)}, bf16[64,4096]{1,0:T(8,128)(2,1)S(1)}, u32[]{:S(2)}, u32[]{:S(2)}) collective-permute-start(bf16[64,4096]{1,0:T(8,128)(2,1)S(1)} %get-tuple-element.116), channel_id=1, source_target_pairs={{0,2},{2,0},{4,6},{6,4},{8,10},{10,8},{12,14},{14,12},{16,18},{18,... | collective-permute-start | bytes 1572872 | tf_op jit(solution)/shard_map/ppermute | solution.py:437
  137.8 6.2 %copy-start.17 = (bf16[9,576,48]{1,2,0:T(8,128)(2,1)S(1)}, bf16[9,576,48]{1,2,0:T(8,128)(2,1)}, u32[]{:S(2)}) copy-start(bf16[9,576,48]{1,2,0:T(8,128)(2,1)} %param.10) | copy-start | bytes 1492996
  138.8 11.9 %copy-start.1 = (f32[512,576]{1,0:T(8,128)S(1)}, f32[512,576]{1,0:T(8,128)}, u32[]{:S(2)}) copy-start(f32[512,576]{1,0:T(8,128)} %copy-done) | copy-start | bytes 3538948
  138.8 11.9 %copy-start.19 = (bf16[288,576]{1,0:T(8,128)(2,1)S(1)}, bf16[288,576]{1,0:T(8,128)(2,1)}, u32[]{:S(2)}) copy-start(bf16[288,576]{1,0:T(8,128)(2,1)} %expand_ref.3) | copy-start | bytes 995332
  138.8 3.8 %collective-permute-start.25 = (bf16[64,2304]{1,0:T(8,128)(2,1)S(1)}, bf16[64,2304]{1,0:T(8,128)(2,1)S(1)}, u32[]{:S(2)}, u32[]{:S(2)}) collective-permute-start(bf16[64,2304]{1,0:T(8,128)(2,1)S(1)} %get-tuple-element.128), channel_id=1, source_target_pairs={{0,2},{2,0},{4,6},{6,4},{8,10},{10,8},{12,14},{14,12},{16,18},{18,... | collective-permute-start | bytes 884744 | tf_op jit(solution)/shard_map/ppermute | solution.py:437
  140.7 10.0 %collective-permute-start.26 = (bf16[256,576]{1,0:T(8,128)(2,1)S(1)}, bf16[256,576]{1,0:T(8,128)(2,1)S(1)}, u32[]{:S(2)}, u32[]{:S(2)}) collective-permute-start(bf16[256,576]{1,0:T(8,128)(2,1)S(1)} %get-tuple-element.130), channel_id=1, source_target_pairs={{2,0},{4,2},{6,4},{8,6},{10,8},{12,10},{14,12},{16,14},{18,16},{20... | collective-permute-start | bytes 884744 | tf_op jit(solution)/shard_map/ppermute | solution.py:420
  151.6 2.5 %copy-start.23 = (bf16[576,288]{0,1:T(8,128)(2,1)S(1)}, bf16[576,288]{0,1:T(8,128)(2,1)}, u32[]{:S(2)}) copy-start(bf16[576,288]{0,1:T(8,128)(2,1)} %param.11) | copy-start | bytes 995332
  151.6 2.5 %collective-permute-start.27 = (f32[2,288]{1,0:T(2,128)S(1)}, f32[2,288]{1,0:T(2,128)S(1)}, u32[]{:S(2)}, u32[]{:S(2)}) collective-permute-start(f32[2,288]{1,0:T(2,128)S(1)} %shard_map.123), channel_id=1, source_target_pairs={{0,1},{1,0},{2,3},{3,2},{4,5},{5,4},{6,7},{7,6},{8,9},{9,8},{10,11... | collective-permute-start | bytes 6920 | tf_op jit(solution)/shard_map/ppermute | solution.py:445

commit v12 on v11

--- a/solution.py
+++ b/solution.py
@@ -460,23 +460,22 @@
     return lax.optimization_barrier(values)
 
 
+def stacked_contract(left, blocks):
+    blocks = [ref[...] for ref in blocks]
+    if blocks[0].shape[0] % 8 == 0:
+        blocks = [jnp.concatenate(blocks, axis=0)]
+    return jnp.concatenate([contract_last(left, block) for block in blocks], axis=1)
+
+
 def pre_kernel(patch_ref, *refs):
     *blocks, out_ref = refs
-    products = [contract_last(patch_ref[...], ref[...]) for ref in blocks]
-    out_ref[...] = jnp.concatenate(products, axis=1)
+    out_ref[...] = stacked_contract(patch_ref[...], blocks)
 
 
 def back_kernel(keep_ref, send_ref, *refs):
     *blocks, out_ref = refs
     back = jnp.concatenate([keep_ref[...], send_ref[...]], axis=0)
-    out_ref[...] = jnp.concatenate([contract_last(back, ref[...]) for ref in blocks], axis=1)
-
-
-def late_kernel(facts_ref, keep_ref, send_ref, *refs):
-    *refs, out_ref, facts_out_ref = refs
-    for place in range(facts_ref.shape[0]):
-        facts_out_ref[place] = facts_ref[place]
-    back_kernel(keep_ref, send_ref, *refs, out_ref)
+    out_ref[...] = stacked_contract(back, blocks)
 
 
 def live_rows(facts_ref, rows, unit):
@@ -593,21 +592,6 @@
 def block_products(kernel, left, blocks):
     rows = 2 * OUT_SIDE * OUT_SIDE
     return whole_call(kernel, f32(rows, len(blocks) * blocks[0].shape[0]), [])(*left, *blocks)
-
-
-def late_products(facts, back, blocks):
-    rows = 2 * OUT_SIDE * OUT_SIDE
-    return pl.pallas_call(
-        late_kernel,
-        out_shape=(
-            f32(rows, len(blocks) * blocks[0].shape[0]),
-            jax.ShapeDtypeStruct(facts.shape, jnp.int32),
-        ),
-        in_specs=vmem_specs(2 + len(blocks)),
-        out_specs=vmem_specs(1)[::-1],
-        compiler_params=pltpu.CompilerParams(vmem_limit_bytes=VMEM_BYTES),
-        cost_estimate=FREE,
-    )(facts, *back, *blocks)
 
 
 def facts_call(kernel, outs, facts, operands, cost=FREE):
@@ -733,14 +717,7 @@
     grads = add_gradients(facts, terms, slopes, pieces, blocks, grads, unit, both, False)
 
     late_up, late_down, *grads = tie(r_up[-1], r_down[-1], *grads)
-    sums, facts_late = late_products(facts, back, [late_up, late_down])
-    terms = tp_terms(sums)
-    places = [*range(steps - 1), *range(-1, 1 - steps, -1), steps - 1, 1 - steps, steps]
-    tokens = token_products(
-        facts_late, act, places, chips, [*early, *middle, late_up, late_down], unit
-    )
-    other_term, *tokens = tie(terms[1], *tokens)
-    terms = terms[0], other_term
+    terms = tp_terms(block_products(back_kernel, back, [late_up, late_down]))
     pieces, blocks = [(1, 0), (1, 2)], [s_up[-1], s_last]
     halo_own, halo_mate = add_gradients(
         facts, terms, slopes, pieces, blocks, grads[:2], unit, (halo_lanes,), True
@@ -753,6 +730,10 @@
     grad_odd = shifted(lead, "ctx", -1)
     grad_even, facts_late = return_patches(
         facts_late, even_own, swap_cores(even_mate), chans, jnp.float32
+    )
+    places = [*range(steps - 1), *range(-1, 1 - steps, -1), steps - 1, 1 - steps, steps]
+    tokens = token_products(
+        facts_late, act, places, chips, [*early, *middle, late_up, late_down], unit
     )
     grad_relaxed = sum_tp(excite_grad(grad_even, grad_odd, conv, excite, squeeze_out))
     llm_tokens = (tokens[0] + swap_cores(tokens[1]).astype(jnp.float32)).astype(jnp.bfloat16)

time: 160 us -> 160 us (level)
  starting transfers between devices: 52.4 us -> 55.5 us
  Pallas kernels: 41.7 us -> 39.1 us
    ppermute x2, waiting for transfers between devices: 12.7 us -> 8.57 us  [shifted(): return lax.ppermute(value, axis, pairs)]
    ppermute x5, starting transfers between devices: 6.9 us -> 9.55 us  [swap_cores(): lax.ppermute(value, 'ctx', [(i, i ^ 1) for i in range(lax.axis_size('ctx'...]
    ppermute x7, waiting for transfers between devices: 5.16 us -> 7.4 us  [tp_terms(): other = lax.ppermute(value, 'tp', [(i, i ^ reach) for i in range(size)])]
    pallas_call x1 -> x0, Pallas kernels: 1.66 us -> none  [late_products(): pl.pallas_call(late_kernel, out_shape=(f32(rows, len(blocks) * blocks[0]....]
    pallas_call x4 -> x5, Pallas kernels: 9.64 us -> 8.68 us  [block_products(): whole_call(kernel, f32(rows, len(blocks) * blocks[0].shape[0]), [])]
  transfers between devices with their start and end apart: 30 -> 30, of which waited for: 17 -> 18; matrix products, arithmetic and copies ran while one was open for 1% -> 1% of each run, Pallas kernels for 23% -> 24%
where the time goes in v12:
time: 160 us; the launch traced here: 158 us
  starting transfers between devices  55.5 us (35%)
  waiting for transfers between devices  51.8 us (32%)
  Pallas kernels  39.1 us (24%)
  local copies, waits for them, and re-layouts  9.65 us (6%)
    ppermute x14, waiting for transfers between devices, ring_send(): return lax.ppermute(value, 'ctx', ring_pairs(lax.axis_size('ctx'), by))  34.8 us
    ppermute x14, starting transfers between devices, ring_send(): return lax.ppermute(value, 'ctx', ring_pairs(lax.axis_size('ctx'), by))  18.3 us
    all_to_all x2, starting transfers between devices, chips_exchange(): lax.all_to_all(value, 'ctx', split_axis=0, concat_axis=0, tiled=True, axi...  9.87 us
    pallas_call x7, Pallas kernels, facts_call(): pl.pallas_call(kernel, out_shape=outs, in_specs=vmem_specs(len(operands))...  9.61 us
    ppermute x5, starting transfers between devices, swap_cores(): lax.ppermute(value, 'ctx', [(i, i ^ 1) for i in range(lax.axis_size('ctx'...  9.55 us
    ppermute x7, starting transfers between devices, tp_terms(): other = lax.ppermute(value, 'tp', [(i, i ^ reach) for i in range(size)])  9 us
    ppermute x2, starting transfers between devices, shifted(): return lax.ppermute(value, axis, pairs)  8.72 us
    pallas_call x5, Pallas kernels, block_products(): whole_call(kernel, f32(rows, len(blocks) * blocks[0].shape[0]), [])  8.68 us
  transfers between devices with their start and end apart: 30, of which 18 were waited for; matrix products, arithmetic and copies ran while one was open for 1% of the time, Pallas kernels for 24%

profile of v12, /device:TPU:3, one launch (start us, length us, event | category | flops | bytes accessed | tf_op | source)
XLA Modules:
  0.0 157.9 jit_solution(12509603082366747292)
XLA Ops:
  0.6 1.7 %reshape.11.refs_0_.refs_4_ = bf16[72,4608]{1,0:T(8,128)(2,1)S(1)} reshape(bf16[72,8,576]{2,1,0:T(8,128)(2,1)} %param.13) | data formatting | bytes 1327104 | tf_op jit(solution)/shard_map/reshape | solution.py:659
  2.4 1.5 collective-permute-start.3
  3.9 1.1 copy.11.feat_ref
  5.0 4.5 %shard_map.105 = (f32[512,576]{1,0:T(8,128)S(1)}, bf16[512,576]{1,0:T(8,128)(2,1)S(1)}, f32[2,288]{1,0:T(2,128)S(1)}) custom-call(bf16[2,196,576]{2,1,0:T(8,128)(2,1)S(1)} %copy.11.feat_ref, bf16[9,48,576]{2,1,0:T(8,128)(2,1)S(1)} %bitcast.10, bf16[288,576]{1,0:T(8,128)(2,1)S(1)} %bitcast.13), custom_call_target="tpu_custom_call" | custom-call | tf_op jit(solution)/shard_map/pallas_call | solution.py:301
  9.5 1.3 collective-permute-start
  10.7 1.5 collective-permute-done
  12.2 1.5 shard_map.106
  13.7 4.5 %collective-permute-done.2.refs_1_.refs_4_ = bf16[72,4608]{1,0:T(8,128)(2,1)S(1)} collective-permute-done((bf16[72,4608]{1,0:T(8,128)(2,1)S(1)}, bf16[72,4608]{1,0:T(8,128)(2,1)S(1)}, u32[]{:S(2)}, u32[]{:S(2)}) %collective-permute-start.2) | collective-permute-done | bytes 663584 | tf_op jit(solution)/shard_map/ppermute | solution.py:456
  18.3 1.1 collective-permute-start.4
  20.6 6.4 %collective-permute-start.1 = (bf16[256,576]{1,0:T(8,128)(2,1)}, bf16[256,576]{1,0:T(8,128)(2,1)}, u32[]{:S(2)}, u32[]{:S(2)}) collective-permute-start(bf16[256,576]{1,0:T(8,128)(2,1)} %get-tuple-element.68), channel_id=1, source_target_pairs={{0,2},{2,4},{4,6},{6,8},{8,10},{10,12},{12,14},{14,16},{16,18},{18... | collective-permute-start | bytes 884744 | tf_op jit(solution)/shard_map/ppermute | solution.py:420
  27.0 4.7 %all-to-all-start = ((bf16[8,8,4096]{2,1,0:T(8,128)(2,1)}), bf16[8,8,4096]{2,1,0:T(8,128)(2,1)S(1)}, u32[]{:S(2)}, u32[]{:S(2)}) async-start(bf16[8,8,4096]{2,1,0:T(8,128)(2,1)} %bitcast.16), calls=%async_computation | async-start | bytes 1048576 | tf_op jit(solution)/shard_map/all_to_all | solution.py:640
  31.7 7.6 %collective-permute-done.1.halo_ref = bf16[256,576]{1,0:T(8,128)(2,1)} collective-permute-done((bf16[256,576]{1,0:T(8,128)(2,1)}, bf16[256,576]{1,0:T(8,128)(2,1)}, u32[]{:S(2)}, u32[]{:S(2)}) %collective-permute-start.1) | collective-permute-done | bytes 294944 | tf_op jit(solution)/shard_map/ppermute | solution.py:420
  39.3 3.5 %collective-permute-start.6 = (bf16[72,4608]{1,0:T(8,128)(2,1)S(1)}, bf16[72,4608]{1,0:T(8,128)(2,1)S(1)}, u32[]{:S(2)}, u32[]{:S(2)}) collective-permute-start(bf16[72,4608]{1,0:T(8,128)(2,1)S(1)} %collective-permute-done.4.refs_3_.refs_5_), channel_id=1, source_target_pairs={{0,8},{2,10},{8,16},{10,18},{16,24},{18,26},{24,28},{26,30},{28,20... | collective-permute-start | bytes 1990664 | tf_op jit(solution)/shard_map/ppermute | solution.py:456
  42.8 0.9 collective-permute-start.7
  43.7 1.3 shard_map.104.facts_ref
  45.7 2.3 %shard_map.107.own_ref = bf16[64,4608]{1,0:T(8,128)(2,1)} custom-call(s32[5]{0:T(128)S(1)} %copy-done.27, bf16[256,576]{1,0:T(8,128)(2,1)} %collective-permute-done.1.halo_ref, bf16[256,576]{1,0:T(8,128)(2,1)S(1)} %get-tuple-element.80.even_ref), custom_call_target="tpu_custom_call" | custom-call | tf_op jit(solution)/shard_map/pallas_call | solution.py:349
  47.9 2.2 %collective-permute-start.13 = (bf16[64,4608]{1,0:T(8,128)(2,1)}, bf16[64,4608]{1,0:T(8,128)(2,1)}, u32[]{:S(2)}, u32[]{:S(2)}) collective-permute-start(bf16[64,4608]{1,0:T(8,128)(2,1)} %shard_map.107.own_ref), channel_id=1, source_target_pairs={{0,2},{2,0},{4,6},{6,4},{8,10},{10,8},{12,14},{14,12},{16,18},{18,... | collective-permute-start | bytes 1769480 | tf_op jit(solution)/shard_map/ppermute | solution.py:437
  50.2 8.5 %collective-permute-done.6.refs_0_.refs_4_ = bf16[72,4608]{1,0:T(8,128)(2,1)S(1)} collective-permute-done((bf16[72,4608]{1,0:T(8,128)(2,1)S(1)}, bf16[72,4608]{1,0:T(8,128)(2,1)S(1)}, u32[]{:S(2)}, u32[]{:S(2)}) %collective-permute-start.6) | collective-permute-done | bytes 663584 | tf_op jit(solution)/shard_map/ppermute | solution.py:456
  58.7 1.6 collective-permute-done.7.refs_1_.refs_6_
  60.2 4.6 %collective-permute-start.11 = (bf16[72,4096]{1,0:T(8,128)(2,1)}, bf16[72,4096]{1,0:T(8,128)(2,1)S(1)}, u32[]{:S(2)}, u32[]{:S(2)}) collective-permute-start(bf16[72,4096]{1,0:T(8,128)(2,1)} %refs_0_.1), channel_id=1, source_target_pairs={{0,4},{2,6},{8,0},{10,2},{16,8},{18,10},{24,16},{26,18},{28,24},{3... | collective-permute-start | bytes 1769480 | tf_op jit(solution)/shard_map/ppermute | solution.py:456
  64.9 1.7 %shard_map.108.patch_ref = bf16[128,4608]{1,0:T(8,128)(2,1)S(1)} custom-call(s32[5]{0:T(128)S(1)} %copy-done.28, bf16[64,4608]{1,0:T(8,128)(2,1)} %shard_map.107.own_ref, bf16[64,4608]{1,0:T(8,128)(2,1)} %collective-permute-done.13.mate_ref), custom_call_target="tpu_custom_call" | custom-call | tf_op jit(solution)/shard_map/pallas_call | solution.py:338
  66.7 2.3 %shard_map.109.own_ref = f32[128,360]{1,0:T(8,128)S(1)} custom-call(bf16[128,4608]{1,0:T(8,128)(2,1)S(1)} %shard_map.108.patch_ref, bf16[72,4608]{1,0:T(8,128)(2,1)S(1)} %reshape.11.refs_0_.refs_4_, bf16[72,4608]{1,0:T(8,128)(2,1)S(1)} %collective-permute-done.2.refs_1_.refs_4_, bf16[72,4608]{1,0:T(8,128)(2,1)S(1)} %copy-done.8, ...), custom_call_target="tpu_custom_call" | custom-call | tf_op jit(solution)/shard_map/pallas_call | solution.py:594
  69.0 1.3 collective-permute-start.14
  70.3 7.8 %collective-permute-done.11.refs_1_ = bf16[72,4096]{1,0:T(8,128)(2,1)S(1)} collective-permute-done((bf16[72,4096]{1,0:T(8,128)(2,1)}, bf16[72,4096]{1,0:T(8,128)(2,1)S(1)}, u32[]{:S(2)}, u32[]{:S(2)}) %collective-permute-start.11) | collective-permute-done | bytes 589856 | tf_op jit(solution)/shard_map/ppermute | solution.py:456
  78.2 2.2 %collective-permute-done.12.refs_2_.refs_5_ = bf16[72,4608]{1,0:T(8,128)(2,1)S(1)} collective-permute-done((bf16[72,4608]{1,0:T(8,128)(2,1)S(1)}, bf16[72,4608]{1,0:T(8,128)(2,1)S(1)}, u32[]{:S(2)}, u32[]{:S(2)}) %collective-permute-start.12) | collective-permute-done | bytes 663584 | tf_op jit(solution)/shard_map/ppermute | solution.py:456
  80.3 2.0 %collective-permute-start.15 = (bf16[72,4096]{1,0:T(8,128)(2,1)S(1)}, bf16[72,4096]{1,0:T(8,128)(2,1)}, u32[]{:S(2)}, u32[]{:S(2)}) collective-permute-start(bf16[72,4096]{1,0:T(8,128)(2,1)S(1)} %collective-permute-done.11.refs_1_), channel_id=1, source_target_pairs={{0,4},{2,6},{8,0},{10,2},{16,8},{18,10},{24,16},{26,18},{28,24},{3... | collective-permute-start | bytes 1769480 | tf_op jit(solution)/shard_map/ppermute | solution.py:456
  82.3 1.9 %shard_map.110.own_ref = f32[128,216]{1,0:T(8,128)S(1)} custom-call(bf16[128,4608]{1,0:T(8,128)(2,1)S(1)} %shard_map.108.patch_ref, bf16[72,4608]{1,0:T(8,128)(2,1)S(1)} %collective-permute-done.6.refs_0_.refs_4_, bf16[72,4608]{1,0:T(8,128)(2,1)} %collective-permute-done.7.refs_1_.refs_6_, bf16[72,4608]{1,0:T(8,128)(2,1)S(1)} %collective-permute-done.12.refs_2_.refs_5_), custom_call_target="tpu_custom_call" | custom-call | tf_op jit(solution)/shard_map/pallas_call | solution.py:594
  84.2 1.3 collective-permute-start.16
  86.0 6.6 %collective-permute-done.9.refs_0_.refs_3_ = bf16[72,4096]{1,0:T(8,128)(2,1)} collective-permute-done((bf16[72,4096]{1,0:T(8,128)(2,1)S(1)}, bf16[72,4096]{1,0:T(8,128)(2,1)}, u32[]{:S(2)}, u32[]{:S(2)}) %collective-permute-start.9) | collective-permute-done | bytes 589856 | tf_op jit(solution)/shard_map/ppermute | solution.py:456
  92.6 1.0 shard_map.111
  93.6 1.1 shard_map.112
  95.7 1.9 %collective-permute-start.19 = (bf16[72,4096]{1,0:T(8,128)(2,1)}, bf16[72,4096]{1,0:T(8,128)(2,1)}, u32[]{:S(2)}, u32[]{:S(2)}) collective-permute-start(bf16[72,4096]{1,0:T(8,128)(2,1)} %collective-permute-done.15.refs_2_), channel_id=1, source_target_pairs={{0,4},{2,6},{8,0},{10,2},{16,8},{18,10},{24,16},{26,18},{28,24},{3... | collective-permute-start | bytes 1769480 | tf_op jit(solution)/shard_map/ppermute | solution.py:456
  97.6 5.2 %all-to-all-start.1 = ((bf16[8,16,576]{2,1,0:T(8,128)(2,1)}), bf16[8,16,576]{2,1,0:T(8,128)(2,1)S(1)}, u32[]{:S(2)}, u32[]{:S(2)}) async-start(bf16[8,16,576]{2,1,0:T(8,128)(2,1)} %bitcast.15), calls=%async_computation.1 | async-start | bytes 327680 | tf_op jit(solution)/shard_map/all_to_all | solution.py:640
  102.8 1.1 copy-done.11
  103.8 1.1 copy-done.14
  104.9 1.8 %shard_map.113.refs_0_ = f32[128,216]{1,0:T(8,128)S(1)} custom-call(bf16[64,4096]{1,0:T(8,128)(2,1)S(1)} %bitcast.7, bf16[64,4096]{1,0:T(8,128)(2,1)S(1)} %collective-permute-done.8.send_ref, bf16[72,4096]{1,0:T(8,128)(2,1)S(1)} %copy-done.11, bf16[72,4096]{1,0:T(8,128)(2,1)S(1)} %copy-done.14, bf16[72,4096]{1,0:T(8,128)(2,1)} %collective-permute-done.15.refs_2_), custom_call_target="tpu_custom_call" | custom-call | tf_op jit(solution)/shard_map/pallas_call | solution.py:594
  106.7 1.3 collective-permute-start.17
  108.7 2.3 %collective-permute-done.17.refs_1_ = f32[128,216]{1,0:T(8,128)S(1)} collective-permute-done((f32[128,216]{1,0:T(8,128)S(1)}, f32[128,216]{1,0:T(8,128)S(1)}, u32[]{:S(2)}, u32[]{:S(2)}) %collective-permute-start.17) | collective-permute-done | bytes 110624 | tf_op jit(solution)/shard_map/ppermute | solution.py:445
  111.6 1.0 all-to-all-done.1
  112.6 1.2 collective-permute-start.18
  113.8 1.2 collective-permute-start.20
  115.0 2.2 %shard_map.114.refs_0_ = f32[128,216]{1,0:T(8,128)S(1)} custom-call(bf16[64,4096]{1,0:T(8,128)(2,1)S(1)} %bitcast.8, bf16[64,4096]{1,0:T(8,128)(2,1)S(1)} %collective-permute-done.8.send_ref, bf16[72,4096]{1,0:T(8,128)(2,1)} %collective-permute-done.9.refs_0_.refs_3_, bf16[72,4096]{1,0:T(8,128)(2,1)} %collective-permute-done.10.refs_1_.refs_4_, ...), custom_call_target="tpu_custom_call" | custom-call | tf_op jit(solution)/shard_map/pallas_call | solution.py:594
  117.1 1.3 collective-permute-start.21
  118.4 1.9 %shard_map.115 = (f32[64,2304]{1,0:T(8,128)S(1)}, f32[64,2304]{1,0:T(8,128)S(1)}, f32[64,2304]{1,0:T(8,128)S(1)}, f32[64,2304]{1,0:T(8,128)S(1)}) custom-call(s32[5]{0:T(128)S(1)} %copy-done.28, f32[128,216]{1,0:T(8,128)S(1)} %copy-done.21, f32[128,216]{1,0:T(8,128)S(1)} %copy-done.26, f32[128,360]{1,0:T(8,128)S(1)} %get-tuple-element.91.refs_2_, ...), custom_call_target="tpu_custom_call" | custom-call | tf_op jit(solution)/shard_map/pallas_call | solution.py:598
  120.3 1.0 collective-permute-done.21.refs_1_
  121.3 1.9 %shard_map.116 = (f32[64,2304]{1,0:T(8,128)S(1)}, f32[64,2304]{1,0:T(8,128)S(1)}, f32[64,2304]{1,0:T(8,128)S(1)}, f32[64,2304]{1,0:T(8,128)S(1)}) custom-call(s32[5]{0:T(128)S(1)} %copy-done.28, f32[128,216]{1,0:T(8,128)S(1)} %shard_map.114.refs_0_, f32[128,216]{1,0:T(8,128)S(1)} %collective-permute-done.21.refs_1_, ...), custom_call_target="tpu_custom_call" | custom-call | tf_op jit(solution)/shard_map/pallas_call | solution.py:598
  123.2 3.2 %collective-permute-done.18.refs_0_.refs_6_ = bf16[72,4096]{1,0:T(8,128)(2,1)S(1)} collective-permute-done((bf16[72,4096]{1,0:T(8,128)(2,1)}, bf16[72,4096]{1,0:T(8,128)(2,1)S(1)}, u32[]{:S(2)}, u32[]{:S(2)}) %collective-permute-start.18) | collective-permute-done | bytes 589856 | tf_op jit(solution)/shard_map/ppermute | solution.py:456
  127.0 1.3 collective-permute-start.22
  128.3 2.6 %collective-permute-done.22.refs_1_ = f32[128,144]{1,0:T(8,128)S(1)} collective-permute-done((f32[128,144]{1,0:T(8,128)S(1)}, f32[128,144]{1,0:T(8,128)S(1)}, u32[]{:S(2)}, u32[]{:S(2)}) %collective-permute-start.22) | collective-permute-done | bytes 73760 | tf_op jit(solution)/shard_map/ppermute | solution.py:445
  130.8 1.0 shard_map.118
  131.9 4.5 %collective-permute-start.23 = (bf16[64,2304]{1,0:T(8,128)(2,1)S(1)}, bf16[64,2304]{1,0:T(8,128)(2,1)S(1)}, u32[]{:S(2)}, u32[]{:S(2)}) collective-permute-start(bf16[64,2304]{1,0:T(8,128)(2,1)S(1)} %get-tuple-element.109), channel_id=1, source_target_pairs={{0,2},{2,0},{4,6},{6,4},{8,10},{10,8},{12,14},{14,12},{16,18},{18,... | collective-permute-start | bytes 884744 | tf_op jit(solution)/shard_map/ppermute | solution.py:437
  136.4 1.0 shard_map.120
  137.6 1.3 shard_map.119
  138.9 2.4 %collective-permute-start.26 = (bf16[256,576]{1,0:T(8,128)(2,1)S(1)}, bf16[256,576]{1,0:T(8,128)(2,1)S(1)}, u32[]{:S(2)}, u32[]{:S(2)}) collective-permute-start(bf16[256,576]{1,0:T(8,128)(2,1)S(1)} %get-tuple-element.121), channel_id=1, source_target_pairs={{2,0},{4,2},{6,4},{8,6},{10,8},{12,10},{14,12},{16,14},{18,16},{20... | collective-permute-start | bytes 884744 | tf_op jit(solution)/shard_map/ppermute | solution.py:420
  141.3 1.2 shard_map.121
  142.6 3.5 %shard_map.122 = (f32[64,4096]{1,0:T(8,128)S(1)}, bf16[64,4096]{1,0:T(8,128)(2,1)S(1)}) custom-call(s32[5]{0:T(128)S(1)} %get-tuple-element.116.facts_ref, bf16[128,576]{1,0:T(8,128)(2,1)S(1)} %bitcast.12, bf16[72,4096]{1,0:T(8,128)(2,1)S(1)} %copy-done.12, bf16[72,4096]{1,0:T(8,128)(2,1)S(1)} %copy-done.15, ...), custom_call_target="tpu_custom_call" | custom-call | tf_op jit(solution)/shard_map/pallas_call | solution.py:626
  146.1 2.3 %collective-permute-start.25 = (bf16[64,4096]{1,0:T(8,128)(2,1)S(1)}, bf16[64,4096]{1,0:T(8,128)(2,1)S(1)}, u32[]{:S(2)}, u32[]{:S(2)}) collective-permute-start(bf16[64,4096]{1,0:T(8,128)(2,1)S(1)} %get-tuple-element.119), channel_id=1, source_target_pairs={{0,2},{2,0},{4,6},{6,4},{8,10},{10,8},{12,14},{14,12},{16,18},{18,... | collective-permute-start | bytes 1572872 | tf_op jit(solution)/shard_map/ppermute | solution.py:437
  148.4 1.0 collective-permute-done.26.odd_ref
  149.4 0.9 shard_map.123
  150.3 1.2 collective-permute-start.27
  151.5 1.7 %shard_map.124 = (bf16[2304,256]{1,0:T(8,128)(2,1)S(1)}, bf16[2304,256]{1,0:T(8,128)(2,1)S(1)}, bf16[2304,256]{1,0:T(8,128)(2,1)S(1)}) custom-call(s32[5]{0:T(128)S(1)} %get-tuple-element.116.facts_ref, bf16[9,48,576]{2,1,0:T(8,128)(2,1)S(1)} %bitcast.11), custom_call_target="tpu_custom_call" | custom-call | tf_op jit(solution)/shard_map/pallas_call | solution.py:598
  153.2 2.7 %shard_map.125 = bf16[2,196,576]{2,1,0:T(8,128)(2,1)S(1)} custom-call(f32[256,576]{1,0:T(8,128)S(1)} %get-tuple-element.120.even_ref, bf16[256,576]{1,0:T(8,128)(2,1)S(1)} %collective-permute-done.26.odd_ref, f32[512,576]{1,0:T(8,128)S(1)} %copy-done.1, f32[2,576]{1,0:T(2,128)S(1)} %get-tuple-element.122.excite_ref, f32[2,288]{1,0:T(2,128)S(1)} %add.9.sq_ref, ...), custom_call_target="tpu_custom_call" | custom-call | flops 2717908992 | bytes 4718592 | tf_op jit(solution)/shard_map/pallas_call | solution.py:385
  155.9 1.2 copy.12
  157.0 0.9 add_convert_fusion
  (82 shorter events, 5.6 us)
Async XLA Ops:
  0.6 4.4 %copy-start.22 = (bf16[576,288]{0,1:T(8,128)(2,1)S(1)}, bf16[576,288]{0,1:T(8,128)(2,1)}, u32[]{:S(2)}) copy-start(bf16[576,288]{0,1:T(8,128)(2,1)} %param.11) | copy-start | bytes 995332
  2.3 2.6 %copy-start.16 = (bf16[9,576,48]{1,2,0:T(8,128)(2,1)S(1)}, bf16[9,576,48]{1,2,0:T(8,128)(2,1)}, u32[]{:S(2)}) copy-start(bf16[9,576,48]{1,2,0:T(8,128)(2,1)} %param.10) | copy-start | bytes 1492996
  2.4 9.9 %copy-start.18 = (bf16[288,576]{1,0:T(8,128)(2,1)S(1)}, bf16[288,576]{1,0:T(8,128)(2,1)}, u32[]{:S(2)}) copy-start(bf16[288,576]{1,0:T(8,128)(2,1)} %expand_ref.3) | copy-start | bytes 995332
  2.4 15.8 %collective-permute-start.2 = (bf16[72,4608]{1,0:T(8,128)(2,1)S(1)}, bf16[72,4608]{1,0:T(8,128)(2,1)S(1)}, u32[]{:S(2)}, u32[]{:S(2)}) collective-permute-start(bf16[72,4608]{1,0:T(8,128)(2,1)S(1)} %reshape.11.refs_0_.refs_4_), channel_id=1, source_target_pairs={{0,8},{2,10},{8,16},{10,18},{16,24},{18,26},{24,28},{26,30},{28,20... | collective-permute-start | bytes 1990664 | tf_op jit(solution)/shard_map/ppermute | solution.py:456
  2.4 15.9 %collective-permute-start.3 = (bf16[72,4608]{1,0:T(8,128)(2,1)S(1)}, bf16[72,4608]{1,0:T(8,128)(2,1)S(1)}, u32[]{:S(2)}, u32[]{:S(2)}) collective-permute-start(bf16[72,4608]{1,0:T(8,128)(2,1)S(1)} %reshape.11.refs_0_.refs_4_), channel_id=1, source_target_pairs={{0,4},{2,6},{8,0},{10,2},{16,8},{18,10},{24,16},{26,18},{28,24},{3... | collective-permute-start | bytes 1990664 | tf_op jit(solution)/shard_map/ppermute | solution.py:456
  9.5 8.8 %copy-start = (f32[512,576]{1,0:T(8,128)}, f32[512,576]{1,0:T(8,128)S(1)}, u32[]{:S(2)}) copy-start(f32[512,576]{1,0:T(8,128)S(1)} %get-tuple-element.64.conv_ref) | copy-start | bytes 3538948
  9.5 2.8 %collective-permute-start = (f32[2,288]{1,0:T(2,128)S(1)}, f32[2,288]{1,0:T(2,128)S(1)}, u32[]{:S(2)}, u32[]{:S(2)}) collective-permute-start(f32[2,288]{1,0:T(2,128)S(1)} %get-tuple-element.67), channel_id=1, source_target_pairs={{0,1},{1,0},{2,3},{3,2},{4,5},{5,4},{6,7},{7,6},{8,9},{9,8},{10,11... | collective-permute-start | bytes 6920 | tf_op jit(solution)/shard_map/ppermute | solution.py:445
  18.2 48.4 %copy-start.2 = (bf16[72,4608]{1,0:T(8,128)(2,1)}, bf16[72,4608]{1,0:T(8,128)(2,1)S(1)}, u32[]{:S(2)}) copy-start(bf16[72,4608]{1,0:T(8,128)(2,1)S(1)} %collective-permute-done.2.refs_1_.refs_4_) | copy-start | bytes 1990660
  18.3 21.0 %collective-permute-start.4 = (bf16[72,4608]{1,0:T(8,128)(2,1)S(1)}, bf16[72,4608]{1,0:T(8,128)(2,1)S(1)}, u32[]{:S(2)}, u32[]{:S(2)}) collective-permute-start(bf16[72,4608]{1,0:T(8,128)(2,1)S(1)} %collective-permute-done.2.refs_1_.refs_4_), channel_id=1, source_target_pairs={{0,8},{2,10},{8,16},{10,18},{16,24},{18,26},{24,28},{26,30},{28,20... | collective-permute-start | bytes 1990664 | tf_op jit(solution)/shard_map/ppermute | solution.py:456
  19.4 19.8 %collective-permute-start.5 = (bf16[72,4608]{1,0:T(8,128)(2,1)S(1)}, bf16[72,4608]{1,0:T(8,128)(2,1)}, u32[]{:S(2)}, u32[]{:S(2)}) collective-permute-start(bf16[72,4608]{1,0:T(8,128)(2,1)S(1)} %collective-permute-done.3.refs_2_.refs_5_), channel_id=1, source_target_pairs={{0,4},{2,6},{8,0},{10,2},{16,8},{18,10},{24,16},{26,18},{28,24},{3... | collective-permute-start | bytes 1990664 | tf_op jit(solution)/shard_map/ppermute | solution.py:456
  19.8 0.9 copy-start.7
  20.6 18.6 %collective-permute-start.1 = (bf16[256,576]{1,0:T(8,128)(2,1)}, bf16[256,576]{1,0:T(8,128)(2,1)}, u32[]{:S(2)}, u32[]{:S(2)}) collective-permute-start(bf16[256,576]{1,0:T(8,128)(2,1)} %get-tuple-element.68), channel_id=1, source_target_pairs={{0,2},{2,4},{4,6},{6,8},{8,10},{10,12},{12,14},{14,16},{16,18},{18... | collective-permute-start | bytes 884744 | tf_op jit(solution)/shard_map/ppermute | solution.py:420
  27.0 23.2 %all-to-all-start = ((bf16[8,8,4096]{2,1,0:T(8,128)(2,1)}), bf16[8,8,4096]{2,1,0:T(8,128)(2,1)S(1)}, u32[]{:S(2)}, u32[]{:S(2)}) async-start(bf16[8,8,4096]{2,1,0:T(8,128)(2,1)} %bitcast.16), calls=%async_computation | async-start | bytes 1048576 | tf_op jit(solution)/shard_map/all_to_all | solution.py:640
  39.3 21.0 %copy-start.4 = (bf16[72,4608]{1,0:T(8,128)(2,1)}, bf16[72,4608]{1,0:T(8,128)(2,1)S(1)}, u32[]{:S(2)}) copy-start(bf16[72,4608]{1,0:T(8,128)(2,1)S(1)} %collective-permute-done.4.refs_3_.refs_5_) | copy-start | bytes 1990660
  39.3 19.4 %collective-permute-start.6 = (bf16[72,4608]{1,0:T(8,128)(2,1)S(1)}, bf16[72,4608]{1,0:T(8,128)(2,1)S(1)}, u32[]{:S(2)}, u32[]{:S(2)}) collective-permute-start(bf16[72,4608]{1,0:T(8,128)(2,1)S(1)} %collective-permute-done.4.refs_3_.refs_5_), channel_id=1, source_target_pairs={{0,8},{2,10},{8,16},{10,18},{16,24},{18,26},{24,28},{26,30},{28,20... | collective-permute-start | bytes 1990664 | tf_op jit(solution)/shard_map/ppermute | solution.py:456
  42.8 17.4 %collective-permute-start.7 = (bf16[72,4608]{1,0:T(8,128)(2,1)}, bf16[72,4608]{1,0:T(8,128)(2,1)}, u32[]{:S(2)}, u32[]{:S(2)}) collective-permute-start(bf16[72,4608]{1,0:T(8,128)(2,1)} %collective-permute-done.5.refs_4_.refs_6_), channel_id=1, source_target_pairs={{0,4},{2,6},{8,0},{10,2},{16,8},{18,10},{24,16},{26,18},{28,24},{3... | collective-permute-start | bytes 1990664 | tf_op jit(solution)/shard_map/ppermute | solution.py:456
  45.0 0.7 copy-start.27
  45.7 19.2 %copy-start.28 = (s32[5]{0:T(128)S(1)}, s32[5]{0:T(128)}, u32[]{:S(2)}) copy-start(s32[5]{0:T(128)} %shard_map.104.facts_ref) | copy-start | bytes 64
  47.9 17.0 %collective-permute-start.13 = (bf16[64,4608]{1,0:T(8,128)(2,1)}, bf16[64,4608]{1,0:T(8,128)(2,1)}, u32[]{:S(2)}, u32[]{:S(2)}) collective-permute-start(bf16[64,4608]{1,0:T(8,128)(2,1)} %shard_map.107.own_ref), channel_id=1, source_target_pairs={{0,2},{2,0},{4,6},{6,4},{8,10},{10,8},{12,14},{14,12},{16,18},{18,... | collective-permute-start | bytes 1769480 | tf_op jit(solution)/shard_map/ppermute | solution.py:437
  60.2 6.4 %copy-start.5 = (bf16[72,4608]{1,0:T(8,128)(2,1)S(1)}, bf16[72,4608]{1,0:T(8,128)(2,1)}, u32[]{:S(2)}) copy-start(bf16[72,4608]{1,0:T(8,128)(2,1)} %copy-done.4) | copy-start | bytes 1990660
  60.2 6.4 %copy-start.8 = (bf16[72,4608]{1,0:T(8,128)(2,1)S(1)}, bf16[72,4608]{1,0:T(8,128)(2,1)}, u32[]{:S(2)}) copy-start(bf16[72,4608]{1,0:T(8,128)(2,1)} %copy-done.7) | copy-start | bytes 1990660
  60.2 20.1 %collective-permute-start.12 = (bf16[72,4608]{1,0:T(8,128)(2,1)S(1)}, bf16[72,4608]{1,0:T(8,128)(2,1)S(1)}, u32[]{:S(2)}, u32[]{:S(2)}) collective-permute-start(bf16[72,4608]{1,0:T(8,128)(2,1)S(1)} %collective-permute-done.6.refs_0_.refs_4_), channel_id=1, source_target_pairs={{0,8},{2,10},{8,16},{10,18},{16,24},{18,26},{24,28},{26,30},{28,20... | collective-permute-start | bytes 1990664 | tf_op jit(solution)/shard_map/ppermute | solution.py:456
  60.2 17.9 %collective-permute-start.11 = (bf16[72,4096]{1,0:T(8,128)(2,1)}, bf16[72,4096]{1,0:T(8,128)(2,1)S(1)}, u32[]{:S(2)}, u32[]{:S(2)}) collective-permute-start(bf16[72,4096]{1,0:T(8,128)(2,1)} %refs_0_.1), channel_id=1, source_target_pairs={{0,4},{2,6},{8,0},{10,2},{16,8},{18,10},{24,16},{26,18},{28,24},{3... | collective-permute-start | bytes 1769480 | tf_op jit(solution)/shard_map/ppermute | solution.py:456
  66.7 3.7 %copy-start.10 = (bf16[72,4096]{1,0:T(8,128)(2,1)S(1)}, bf16[72,4096]{1,0:T(8,128)(2,1)}, u32[]{:S(2)}) copy-start(bf16[72,4096]{1,0:T(8,128)(2,1)} %refs_0_.1) | copy-start | bytes 1769476
  69.0 9.2 %collective-permute-start.14 = (f32[128,360]{1,0:T(8,128)S(1)}, f32[128,360]{1,0:T(8,128)S(1)}, u32[]{:S(2)}, u32[]{:S(2)}) collective-permute-start(f32[128,360]{1,0:T(8,128)S(1)} %shard_map.109.own_ref), channel_id=1, source_target_pairs={{0,1},{1,0},{2,3},{3,2},{4,5},{5,4},{6,7},{7,6},{8,9},{9,8},{10,11... | collective-permute-start | bytes 552968 | tf_op jit(solution)/shard_map/ppermute | solution.py:445
  70.3 22.2 %collective-permute-start.9 = (bf16[72,4096]{1,0:T(8,128)(2,1)S(1)}, bf16[72,4096]{1,0:T(8,128)(2,1)}, u32[]{:S(2)}, u32[]{:S(2)}) collective-permute-start(bf16[72,4096]{1,0:T(8,128)(2,1)S(1)} %copy-done.10), channel_id=1, source_target_pairs={{0,8},{2,10},{8,16},{10,18},{16,24},{18,26},{24,28},{26,30},{28,20... | collective-permute-start | bytes 1769480 | tf_op jit(solution)/shard_map/ppermute | solution.py:456
  78.2 6.0 %copy-start.13 = (bf16[72,4096]{1,0:T(8,128)(2,1)}, bf16[72,4096]{1,0:T(8,128)(2,1)S(1)}, u32[]{:S(2)}) copy-start(bf16[72,4096]{1,0:T(8,128)(2,1)S(1)} %collective-permute-done.11.refs_1_) | copy-start | bytes 1769476
  80.3 15.3 %collective-permute-start.15 = (bf16[72,4096]{1,0:T(8,128)(2,1)S(1)}, bf16[72,4096]{1,0:T(8,128)(2,1)}, u32[]{:S(2)}, u32[]{:S(2)}) collective-permute-start(bf16[72,4096]{1,0:T(8,128)(2,1)S(1)} %collective-permute-done.11.refs_1_), channel_id=1, source_target_pairs={{0,4},{2,6},{8,0},{10,2},{16,8},{18,10},{24,16},{26,18},{28,24},{3... | collective-permute-start | bytes 1769480 | tf_op jit(solution)/shard_map/ppermute | solution.py:456
  84.2 9.4 %collective-permute-start.16 = (f32[128,216]{1,0:T(8,128)S(1)}, f32[128,216]{1,0:T(8,128)S(1)}, u32[]{:S(2)}, u32[]{:S(2)}) collective-permute-start(f32[128,216]{1,0:T(8,128)S(1)} %shard_map.110.own_ref), channel_id=1, source_target_pairs={{0,1},{1,0},{2,3},{3,2},{4,5},{5,4},{6,7},{7,6},{8,9},{9,8},{10,11... | collective-permute-start | bytes 331784 | tf_op jit(solution)/shard_map/ppermute | solution.py:445
  85.5 17.2 %collective-permute-start.8 = (bf16[64,4096]{1,0:T(8,128)(2,1)S(1)}, bf16[64,4096]{1,0:T(8,128)(2,1)S(1)}, u32[]{:S(2)}, u32[]{:S(2)}) collective-permute-start(bf16[64,4096]{1,0:T(8,128)(2,1)S(1)} %bitcast.6), channel_id=1, source_target_pairs={{0,2},{2,0},{4,6},{6,4},{8,10},{10,8},{12,14},{14,12},{16,18},{18,... | collective-permute-start | bytes 1572872 | tf_op jit(solution)/shard_map/ppermute | solution.py:437
  92.6 16.1 %collective-permute-start.10 = (bf16[72,4096]{1,0:T(8,128)(2,1)}, bf16[72,4096]{1,0:T(8,128)(2,1)}, u32[]{:S(2)}, u32[]{:S(2)}) collective-permute-start(bf16[72,4096]{1,0:T(8,128)(2,1)} %collective-permute-done.9.refs_0_.refs_3_), channel_id=1, source_target_pairs={{0,8},{2,10},{8,16},{10,18},{16,24},{18,26},{24,28},{26,30},{28,20... | collective-permute-start | bytes 1769480 | tf_op jit(solution)/shard_map/ppermute | solution.py:456
  94.7 0.7 copy-start.24
  95.7 18.1 %collective-permute-start.19 = (bf16[72,4096]{1,0:T(8,128)(2,1)}, bf16[72,4096]{1,0:T(8,128)(2,1)}, u32[]{:S(2)}, u32[]{:S(2)}) collective-permute-start(bf16[72,4096]{1,0:T(8,128)(2,1)} %collective-permute-done.15.refs_2_), channel_id=1, source_target_pairs={{0,4},{2,6},{8,0},{10,2},{16,8},{18,10},{24,16},{26,18},{28,24},{3... | collective-permute-start | bytes 1769480 | tf_op jit(solution)/shard_map/ppermute | solution.py:456
  97.6 15.1 %all-to-all-start.1 = ((bf16[8,16,576]{2,1,0:T(8,128)(2,1)}), bf16[8,16,576]{2,1,0:T(8,128)(2,1)S(1)}, u32[]{:S(2)}, u32[]{:S(2)}) async-start(bf16[8,16,576]{2,1,0:T(8,128)(2,1)} %bitcast.15), calls=%async_computation.1 | async-start | bytes 327680 | tf_op jit(solution)/shard_map/all_to_all | solution.py:640
  102.8 1.1 copy-start.11
  103.8 1.1 copy-start.14
  106.7 4.3 %collective-permute-start.17 = (f32[128,216]{1,0:T(8,128)S(1)}, f32[128,216]{1,0:T(8,128)S(1)}, u32[]{:S(2)}, u32[]{:S(2)}) collective-permute-start(f32[128,216]{1,0:T(8,128)S(1)} %shard_map.113.refs_0_), channel_id=1, source_target_pairs={{0,1},{1,0},{2,3},{3,2},{4,5},{5,4},{6,7},{7,6},{8,9},{9,8},{10,11... | collective-permute-start | bytes 331784 | tf_op jit(solution)/shard_map/ppermute | solution.py:445
  108.0 0.7 copy-start.20
  111.0 0.6 copy-start.25
  112.6 5.8 %copy-start.9 = (bf16[72,4608]{1,0:T(8,128)(2,1)S(1)}, bf16[72,4608]{1,0:T(8,128)(2,1)}, u32[]{:S(2)}) copy-start(bf16[72,4608]{1,0:T(8,128)(2,1)} %copy-done.7) | copy-start | bytes 1990660
  112.6 5.8 %copy-start.21 = (f32[128,216]{1,0:T(8,128)S(1)}, f32[128,216]{1,0:T(8,128)}, u32[]{:S(2)}) copy-start(f32[128,216]{1,0:T(8,128)} %copy-done.20) | copy-start | bytes 331780
  112.6 5.8 %copy-start.26 = (f32[128,216]{1,0:T(8,128)S(1)}, f32[128,216]{1,0:T(8,128)}, u32[]{:S(2)}) copy-start(f32[128,216]{1,0:T(8,128)} %copy-done.25) | copy-start | bytes 331780
  112.6 13.7 %collective-permute-start.18 = (bf16[72,4096]{1,0:T(8,128)(2,1)}, bf16[72,4096]{1,0:T(8,128)(2,1)S(1)}, u32[]{:S(2)}, u32[]{:S(2)}) collective-permute-start(bf16[72,4096]{1,0:T(8,128)(2,1)} %collective-permute-done.10.refs_1_.refs_4_), channel_id=1, source_target_pairs={{0,8},{2,10},{8,16},{10,18},{16,24},{18,26},{24,28},{26,30},{28,20... | collective-permute-start | bytes 1769480 | tf_op jit(solution)/shard_map/ppermute | solution.py:456
  113.8 12.7 %collective-permute-start.20 = (bf16[72,4096]{1,0:T(8,128)(2,1)}, bf16[72,4096]{1,0:T(8,128)(2,1)S(1)}, u32[]{:S(2)}, u32[]{:S(2)}) collective-permute-start(bf16[72,4096]{1,0:T(8,128)(2,1)} %collective-permute-done.19.refs_2_.refs_5_), channel_id=1, source_target_pairs={{0,4},{2,6},{8,0},{10,2},{16,8},{18,10},{24,16},{26,18},{28,24},{3... | collective-permute-start | bytes 1769480 | tf_op jit(solution)/shard_map/ppermute | solution.py:456
  117.1 4.2 %collective-permute-start.21 = (f32[128,216]{1,0:T(8,128)S(1)}, f32[128,216]{1,0:T(8,128)S(1)}, u32[]{:S(2)}, u32[]{:S(2)}) collective-permute-start(f32[128,216]{1,0:T(8,128)S(1)} %shard_map.114.refs_0_), channel_id=1, source_target_pairs={{0,1},{1,0},{2,3},{3,2},{4,5},{5,4},{6,7},{7,6},{8,9},{9,8},{10,11... | collective-permute-start | bytes 331784 | tf_op jit(solution)/shard_map/ppermute | solution.py:445
  118.4 2.9 %copy-start.3 = (bf16[72,4608]{1,0:T(8,128)(2,1)S(1)}, bf16[72,4608]{1,0:T(8,128)(2,1)}, u32[]{:S(2)}) copy-start(bf16[72,4608]{1,0:T(8,128)(2,1)} %copy-done.2) | copy-start | bytes 1990660
  118.4 2.9 %copy-start.6 = (bf16[72,4608]{1,0:T(8,128)(2,1)S(1)}, bf16[72,4608]{1,0:T(8,128)(2,1)}, u32[]{:S(2)}) copy-start(bf16[72,4608]{1,0:T(8,128)(2,1)} %copy-done.4) | copy-start | bytes 1990660
  127.0 3.9 %collective-permute-start.22 = (f32[128,144]{1,0:T(8,128)S(1)}, f32[128,144]{1,0:T(8,128)S(1)}, u32[]{:S(2)}, u32[]{:S(2)}) collective-permute-start(f32[128,144]{1,0:T(8,128)S(1)} %shard_map.117.refs_0_), channel_id=1, source_target_pairs={{0,1},{1,0},{2,3},{3,2},{4,5},{5,4},{6,7},{7,6},{8,9},{9,8},{10,11... | collective-permute-start | bytes 221192 | tf_op jit(solution)/shard_map/ppermute | solution.py:445
  131.9 5.7 %collective-permute-start.23 = (bf16[64,2304]{1,0:T(8,128)(2,1)S(1)}, bf16[64,2304]{1,0:T(8,128)(2,1)S(1)}, u32[]{:S(2)}, u32[]{:S(2)}) collective-permute-start(bf16[64,2304]{1,0:T(8,128)(2,1)S(1)} %get-tuple-element.109), channel_id=1, source_target_pairs={{0,2},{2,0},{4,6},{6,4},{8,10},{10,8},{12,14},{14,12},{16,18},{18,... | collective-permute-start | bytes 884744 | tf_op jit(solution)/shard_map/ppermute | solution.py:437
  137.4 5.1 %copy-start.12 = (bf16[72,4096]{1,0:T(8,128)(2,1)S(1)}, bf16[72,4096]{1,0:T(8,128)(2,1)}, u32[]{:S(2)}) copy-start(bf16[72,4096]{1,0:T(8,128)(2,1)} %refs_0_.1) | copy-start | bytes 1769476
  137.4 5.1 %copy-start.15 = (bf16[72,4096]{1,0:T(8,128)(2,1)S(1)}, bf16[72,4096]{1,0:T(8,128)(2,1)}, u32[]{:S(2)}) copy-start(bf16[72,4096]{1,0:T(8,128)(2,1)} %copy-done.13) | copy-start | bytes 1769476
  137.5 3.8 %collective-permute-start.24 = (bf16[64,2304]{1,0:T(8,128)(2,1)S(1)}, bf16[64,2304]{1,0:T(8,128)(2,1)S(1)}, u32[]{:S(2)}, u32[]{:S(2)}) collective-permute-start(bf16[64,2304]{1,0:T(8,128)(2,1)S(1)} %get-tuple-element.115), channel_id=1, source_target_pairs={{0,2},{2,0},{4,6},{6,4},{8,10},{10,8},{12,14},{14,12},{16,18},{18,... | collective-permute-start | bytes 884744 | tf_op jit(solution)/shard_map/ppermute | solution.py:437
  138.9 10.4 %collective-permute-start.26 = (bf16[256,576]{1,0:T(8,128)(2,1)S(1)}, bf16[256,576]{1,0:T(8,128)(2,1)S(1)}, u32[]{:S(2)}, u32[]{:S(2)}) collective-permute-start(bf16[256,576]{1,0:T(8,128)(2,1)S(1)} %get-tuple-element.121), channel_id=1, source_target_pairs={{2,0},{4,2},{6,4},{8,6},{10,8},{12,10},{14,12},{16,14},{18,16},{20... | collective-permute-start | bytes 884744 | tf_op jit(solution)/shard_map/ppermute | solution.py:420
  142.6 6.8 %copy-start.1 = (f32[512,576]{1,0:T(8,128)S(1)}, f32[512,576]{1,0:T(8,128)}, u32[]{:S(2)}) copy-start(f32[512,576]{1,0:T(8,128)} %copy-done) | copy-start | bytes 3538948
  142.6 6.8 %copy-start.19 = (bf16[288,576]{1,0:T(8,128)(2,1)S(1)}, bf16[288,576]{1,0:T(8,128)(2,1)}, u32[]{:S(2)}) copy-start(bf16[288,576]{1,0:T(8,128)(2,1)} %expand_ref.3) | copy-start | bytes 995332
  146.1 10.9 %collective-permute-start.25 = (bf16[64,4096]{1,0:T(8,128)(2,1)S(1)}, bf16[64,4096]{1,0:T(8,128)(2,1)S(1)}, u32[]{:S(2)}, u32[]{:S(2)}) collective-permute-start(bf16[64,4096]{1,0:T(8,128)(2,1)S(1)} %get-tuple-element.119), channel_id=1, source_target_pairs={{0,2},{2,0},{4,6},{6,4},{8,10},{10,8},{12,14},{14,12},{16,18},{18,... | collective-permute-start | bytes 1572872 | tf_op jit(solution)/shard_map/ppermute | solution.py:437
  149.3 2.1 %copy-start.17 = (bf16[9,576,48]{1,2,0:T(8,128)(2,1)S(1)}, bf16[9,576,48]{1,2,0:T(8,128)(2,1)}, u32[]{:S(2)}) copy-start(bf16[9,576,48]{1,2,0:T(8,128)(2,1)} %param.10) | copy-start | bytes 1492996
  149.3 3.8 %copy-start.23 = (bf16[576,288]{0,1:T(8,128)(2,1)S(1)}, bf16[576,288]{0,1:T(8,128)(2,1)}, u32[]{:S(2)}) copy-start(bf16[576,288]{0,1:T(8,128)(2,1)} %param.11) | copy-start | bytes 995332
  150.3 2.9 %collective-permute-start.27 = (f32[2,288]{1,0:T(2,128)S(1)}, f32[2,288]{1,0:T(2,128)S(1)}, u32[]{:S(2)}, u32[]{:S(2)}) collective-permute-start(f32[2,288]{1,0:T(2,128)S(1)} %shard_map.123), channel_id=1, source_target_pairs={{0,1},{1,0},{2,3},{3,2},{4,5},{5,4},{6,7},{7,6},{8,9},{9,8},{10,11... | collective-permute-start | bytes 6920 | tf_op jit(solution)/shard_map/ppermute | solution.py:445

commit v13 on v12

--- a/solution.py
+++ b/solution.py
@@ -461,7 +461,6 @@
 
 
 def stacked_contract(left, blocks):
-    blocks = [ref[...] for ref in blocks]
     if blocks[0].shape[0] % 8 == 0:
         blocks = [jnp.concatenate(blocks, axis=0)]
     return jnp.concatenate([contract_last(left, block) for block in blocks], axis=1)
@@ -469,11 +468,14 @@
 
 def pre_kernel(patch_ref, *refs):
     *blocks, out_ref = refs
-    out_ref[...] = stacked_contract(patch_ref[...], blocks)
-
-
-def back_kernel(keep_ref, send_ref, *refs):
+    out_ref[...] = stacked_contract(patch_ref[...], [ref[...] for ref in blocks])
+
+
+def back_kernel(halves, keep_ref, send_ref, *refs):
     *blocks, out_ref = refs
+    blocks = [ref[...] for ref in blocks]
+    if halves:
+        blocks = blocks[:-2] + [jnp.concatenate(blocks[-2:], axis=1)]
     back = jnp.concatenate([keep_ref[...], send_ref[...]], axis=0)
     out_ref[...] = stacked_contract(back, blocks)
 
@@ -565,12 +567,14 @@
 
 
 def token_kernel(offsets, chips, unit, facts_ref, act_ref, *refs):
-    count = len(offsets)
+    count = len(offsets) + 1
     blocks, refs = refs[:count], refs[count:]
     keep_ref, send_ref, *buffers, sems = refs
+    half = buffers[-1].shape[1] // 2
+    targets = [*buffers[:-1], buffers[-1].at[:, :half], buffers[-1].at[:, half:]]
     copies = [
-        pltpu.make_async_copy(ref, buffer, sems.at[place])
-        for place, (ref, buffer) in enumerate(zip(blocks, buffers))
+        pltpu.make_async_copy(ref, target, sems.at[place])
+        for place, (ref, target) in enumerate(zip(blocks, targets))
     ]
     for copy in copies:
         copy.start()
@@ -594,6 +598,13 @@
     return whole_call(kernel, f32(rows, len(blocks) * blocks[0].shape[0]), [])(*left, *blocks)
 
 
+def back_products(back, blocks, halves=()):
+    rows, count = 2 * OUT_SIDE * OUT_SIDE, len(blocks) + (1 if halves else 0)
+    kernel = functools.partial(back_kernel, bool(halves))
+    operands = *back, *blocks, *halves
+    return whole_call(kernel, f32(rows, count * blocks[0].shape[0]), [])(*operands)
+
+
 def facts_call(kernel, outs, facts, operands, cost=FREE):
     return pl.pallas_call(
         kernel,
@@ -627,7 +638,7 @@
         functools.partial(token_kernel, offsets, chips, unit),
         out_shape=(f32(rows, columns), bf16(rows, columns)),
         in_specs=vmem_specs(1) + [pl.BlockSpec(memory_space=pl.ANY)] * len(blocks),
-        scratch_shapes=[pltpu.VMEM(block.shape, block.dtype) for block in blocks]
+        scratch_shapes=[pltpu.VMEM(blocks[0].shape, jnp.bfloat16)] * len(offsets)
         + [pltpu.SemaphoreType.DMA((len(blocks),))],
         compiler_params=pltpu.CompilerParams(vmem_limit_bytes=VMEM_BYTES),
         cost_estimate=FREE,
@@ -682,43 +693,50 @@
             patches = order_rows(facts, patches, swap_cores(patches), unit)
     s_up[-1], s_down[-1], back, readout_kernel = tie(s_up[-1], s_down[-1], back, readout_kernel)
     back = (back, swap_cores(back))
-    s_last = ring_send(s_up[-1], 1)
-    r_up = [readout_kernel, ring_send(readout_kernel, 1)]
+    cut = 4 * chans
+    s_last = ring_send(s_up[-1][:, :cut], 1), ring_send(s_down[-1][:, cut:], -1)
     samplers = [flat_sampler] + [block for pair in zip(s_up[1:], s_down[1:]) for block in pair]
     offsets = ring_offsets(chips)
     count = 2 * steps - 3
+    r_up, r_down = [ring_send(readout_kernel, 1)], [ring_send(readout_kernel, -1)]
     first_pre = tp_terms(block_products(pre_kernel, (patches,), samplers[:count]))
-    r_down[1], s_last, *first_pre = tie(r_down[1], s_last, *first_pre)
-    for step in range(1, steps - 2):
+    held = tie(r_up[0], r_down[0], *s_last, *first_pre)
+    r_up[0], r_down[0], s_last, first_pre = held[0], held[1], held[2:4], held[4:]
+    for step in range(2, steps - 1):
+        r_up.append(ring_send(r_up[-1], 1))
         r_down.append(ring_send(r_down[-1], -1))
-        r_up.append(ring_send(r_up[-1], 1))
+    samplers.append(jnp.concatenate(s_last, axis=1))
     first_slope, first_act = act_and_slope(facts, first_pre, offsets[:count], chips, (), unit)
-    last_pre = block_products(pre_kernel, (patches,), [*samplers[count:], s_last])
+    last_pre = block_products(pre_kernel, (patches,), samplers[count:])
     last_slope, act = act_and_slope(
         facts, tp_terms(last_pre), offsets[count:], chips, (first_act,), unit
     )
     slopes = first_slope, last_slope
-    r_down[-1], act = tie(r_down[-1], act)
+    halo_lanes, even_lanes = slice(0, cut), slice(cut, 2 * cut)
+    both = halo_lanes, even_lanes
+    readouts = [readout_kernel] + [block for pair in zip(r_up, r_down) for block in pair]
+    sums = back_products(back, readouts[: count - 2])
+    r_up[-1], r_down[-1], act, sums = tie(r_up[-1], r_down[-1], act, sums)
+    readouts[count - 2 :] = r_up[-1], r_down[-1]
+    r_up.append(ring_send(r_up[-1], 1))
     r_down.append(ring_send(r_down[-1], -1))
-    early = r_down[: steps - 1]
-    sums = block_products(back_kernel, back, early)
-    r_up[-1], act, *terms = tie(r_up[-1], chips_exchange(act), *tp_terms(sums))
-    r_up.append(ring_send(r_up[-1], 1))
-    halo_lanes, even_lanes = slice(0, 4 * chans), slice(4 * chans, 8 * chans)
-    both = halo_lanes, even_lanes
-    pieces = [(0, 2 * step) for step in range(steps - 1)]
-    blocks = [flat_sampler] + s_down[1 : steps - 1]
-    grads = add_gradients(facts, terms, slopes, pieces, blocks, (), unit, both, False)
-    middle = r_up[1 : steps - 1] + [r_down[steps - 1]]
-    r_down.append(ring_send(r_down[-1], -1))
-    terms = tp_terms(block_products(back_kernel, back, middle))
-    pieces = [(0, 2 * step - 1) for step in range(1, steps - 1)] + [(1, 1)]
-    blocks = s_up[1 : steps - 1] + [s_down[steps - 1]]
-    grads = add_gradients(facts, terms, slopes, pieces, blocks, grads, unit, both, False)
-
-    late_up, late_down, *grads = tie(r_up[-1], r_down[-1], *grads)
-    terms = tp_terms(block_products(back_kernel, back, [late_up, late_down]))
-    pieces, blocks = [(1, 0), (1, 2)], [s_up[-1], s_last]
+    held = tie(r_up[-1], r_down[-1], chips_exchange(act), *tp_terms(sums))
+    r_up[-1], r_down[-1], act, terms = *held[:3], held[3:]
+    pieces = [(0, place) for place in range(count - 2)]
+    grads = add_gradients(
+        facts, terms, slopes, pieces, samplers[: count - 2], (), unit, both, False
+    )
+    terms = tp_terms(back_products(back, readouts[count - 2 :]))
+    pieces = [(0, count - 2), (0, count - 1)]
+    grads = add_gradients(
+        facts, terms, slopes, pieces, samplers[count - 2 : count], grads, unit, both, False
+    )
+    cut = readout_kernel.shape[1] // 2
+    r_last = ring_send(r_up[-1][:, :cut], 1), ring_send(r_down[-1][:, cut:], -1)
+    held = tie(r_up[-1], r_down[-1], *r_last, *grads)
+    late, r_last, grads = held[:2], held[2:4], held[4:]
+    terms = tp_terms(back_products(back, late, r_last))
+    pieces, blocks = [(1, 0), (1, 1), (1, 2)], samplers[count:]
     halo_own, halo_mate = add_gradients(
         facts, terms, slopes, pieces, blocks, grads[:2], unit, (halo_lanes,), True
     )
@@ -731,9 +749,8 @@
     grad_even, facts_late = return_patches(
         facts_late, even_own, swap_cores(even_mate), chans, jnp.float32
     )
-    places = [*range(steps - 1), *range(-1, 1 - steps, -1), steps - 1, 1 - steps, steps]
     tokens = token_products(
-        facts_late, act, places, chips, [*early, *middle, late_up, late_down], unit
+        facts_late, act, offsets, chips, [*readouts, *late, *r_last], unit
     )
     grad_relaxed = sum_tp(excite_grad(grad_even, grad_odd, conv, excite, squeeze_out))
     llm_tokens = (tokens[0] + swap_cores(tokens[1]).astype(jnp.float32)).astype(jnp.bfloat16)

time: 160 us -> 168 us (1.050)
  waiting for transfers between devices: 51.8 us -> 61.6 us
    ppermute x7, waiting for transfers between devices: 7.4 us -> 14.2 us  [tp_terms(): other = lax.ppermute(value, 'tp', [(i, i ^ reach) for i in range(size)])]
    pallas_call x5 -> x2, Pallas kernels: 8.68 us -> 3.08 us  [block_products(): whole_call(kernel, f32(rows, len(blocks) * blocks[0].shape[0]), [])]
    pallas_call x0 -> x3, Pallas kernels: none -> 4.51 us  [back_products(): whole_call(kernel, f32(rows, count * blocks[0].shape[0]), [])(*operands)]
    all_to_all x2, waiting for transfers between devices: 0.98 us -> 5.3 us  [chips_exchange(): lax.all_to_all(value, 'ctx', split_axis=0, concat_axis=0, tiled=True, axi...]
    ppermute x14 -> x16, waiting for transfers between devices: 34.8 us -> 31.5 us  [ring_send(): return lax.ppermute(value, 'ctx', ring_pairs(lax.axis_size('ctx'), by))]
    ppermute x5, starting transfers between devices: 9.55 us -> 12 us  [swap_cores(): lax.ppermute(value, 'ctx', [(i, i ^ 1) for i in range(lax.axis_size('ctx'...]
    ppermute x2, starting transfers between devices: 8.72 us -> 6.55 us  [shifted(): return lax.ppermute(value, axis, pairs)]
    unnamed x60 -> x65, local copies, waits for them, and re-layouts: 7.95 us -> 5.87 us
  transfers between devices with their start and end apart: 30 -> 32, of which waited for: 18 -> 18; matrix products, arithmetic and copies ran while one was open for 1% -> 1% of each run, Pallas kernels for 24% -> 21%
where the time goes in v13:
time: 168 us; the launch traced here: 166 us
  waiting for transfers between devices  61.6 us (37%)
  starting transfers between devices  54.4 us (32%)
  Pallas kernels  37.9 us (23%)
  local copies, waits for them, and re-layouts  9.7 us (6%)
    ppermute x16, waiting for transfers between devices, ring_send(): return lax.ppermute(value, 'ctx', ring_pairs(lax.axis_size('ctx'), by))  31.5 us
    ppermute x16, starting transfers between devices, ring_send(): return lax.ppermute(value, 'ctx', ring_pairs(lax.axis_size('ctx'), by))  17.4 us
    ppermute x7, waiting for transfers between devices, tp_terms(): other = lax.ppermute(value, 'tp', [(i, i ^ reach) for i in range(size)])  14.2 us
    ppermute x5, starting transfers between devices, swap_cores(): lax.ppermute(value, 'ctx', [(i, i ^ 1) for i in range(lax.axis_size('ctx'...  12 us
    ppermute x2, waiting for transfers between devices, shifted(): return lax.ppermute(value, axis, pairs)  10.5 us
    all_to_all x2, starting transfers between devices, chips_exchange(): lax.all_to_all(value, 'ctx', split_axis=0, concat_axis=0, tiled=True, axi...  9.43 us
    ppermute x7, starting transfers between devices, tp_terms(): other = lax.ppermute(value, 'tp', [(i, i ^ reach) for i in range(size)])  8.99 us
    pallas_call x7, Pallas kernels, facts_call(): pl.pallas_call(kernel, out_shape=outs, in_specs=vmem_specs(len(operands))...  8.65 us
  transfers between devices with their start and end apart: 32, of which 18 were waited for; matrix products, arithmetic and copies ran while one was open for 1% of the time, Pallas kernels for 21%

profile of v13, /device:TPU:3, one launch (start us, length us, event | category | flops | bytes accessed | tf_op | source)
XLA Modules:
  0.0 165.7 jit_solution(11935662700710968252)
XLA Ops:
  0.7 1.7 %reshape.11.refs_0_.refs_4_ = bf16[72,4608]{1,0:T(8,128)(2,1)S(1)} reshape(bf16[72,8,576]{2,1,0:T(8,128)(2,1)} %param.13) | data formatting | bytes 1327104 | tf_op jit(solution)/shard_map/reshape | solution.py:670
  2.4 1.3 collective-permute-start.3
  3.9 1.1 copy.11.feat_ref
  5.0 4.5 %shard_map.105 = (f32[512,576]{1,0:T(8,128)S(1)}, bf16[512,576]{1,0:T(8,128)(2,1)S(1)}, f32[2,288]{1,0:T(2,128)S(1)}) custom-call(bf16[2,196,576]{2,1,0:T(8,128)(2,1)S(1)} %copy.11.feat_ref, bf16[9,48,576]{2,1,0:T(8,128)(2,1)S(1)} %bitcast.10, bf16[288,576]{1,0:T(8,128)(2,1)S(1)} %bitcast.12), custom_call_target="tpu_custom_call" | custom-call | tf_op jit(solution)/shard_map/pallas_call | solution.py:301
  9.5 1.3 collective-permute-start
  10.8 1.5 collective-permute-done
  12.3 1.5 shard_map.106
  13.8 4.5 %collective-permute-done.3.refs_2_.refs_6_ = bf16[72,4608]{1,0:T(8,128)(2,1)S(1)} collective-permute-done((bf16[72,4608]{1,0:T(8,128)(2,1)S(1)}, bf16[72,4608]{1,0:T(8,128)(2,1)S(1)}, u32[]{:S(2)}, u32[]{:S(2)}) %collective-permute-start.3) | collective-permute-done | bytes 663584 | tf_op jit(solution)/shard_map/ppermute | solution.py:456
  18.2 1.0 collective-permute-done.2.refs_1_.refs_5_
  19.4 0.8 copy-done.9
  20.2 1.3 collective-permute-start.5
  21.5 4.2 %collective-permute-start.1 = (bf16[256,576]{1,0:T(8,128)(2,1)}, bf16[256,576]{1,0:T(8,128)(2,1)}, u32[]{:S(2)}, u32[]{:S(2)}) collective-permute-start(bf16[256,576]{1,0:T(8,128)(2,1)} %get-tuple-element.75), channel_id=1, source_target_pairs={{0,2},{2,4},{4,6},{6,8},{8,10},{10,12},{12,14},{14,16},{16,18},{18... | collective-permute-start | bytes 884744 | tf_op jit(solution)/shard_map/ppermute | solution.py:420
  25.8 5.0 %all-to-all-start = ((bf16[8,8,4096]{2,1,0:T(8,128)(2,1)}), bf16[8,8,4096]{2,1,0:T(8,128)(2,1)S(1)}, u32[]{:S(2)}, u32[]{:S(2)}) async-start(bf16[8,8,4096]{2,1,0:T(8,128)(2,1)} %bitcast.15), calls=%async_computation | async-start | bytes 1048576 | tf_op jit(solution)/shard_map/all_to_all | solution.py:651
  30.8 9.9 %collective-permute-done.1.halo_ref = bf16[256,576]{1,0:T(8,128)(2,1)} collective-permute-done((bf16[256,576]{1,0:T(8,128)(2,1)}, bf16[256,576]{1,0:T(8,128)(2,1)}, u32[]{:S(2)}, u32[]{:S(2)}) %collective-permute-start.1) | collective-permute-done | bytes 294944 | tf_op jit(solution)/shard_map/ppermute | solution.py:420
  40.7 3.5 %collective-permute-start.6 = (bf16[72,4608]{1,0:T(8,128)(2,1)S(1)}, bf16[72,4608]{1,0:T(8,128)(2,1)S(1)}, u32[]{:S(2)}, u32[]{:S(2)}) collective-permute-start(bf16[72,4608]{1,0:T(8,128)(2,1)S(1)} %collective-permute-done.4.refs_3_.refs_4_), channel_id=1, source_target_pairs={{0,8},{2,10},{8,16},{10,18},{16,24},{18,26},{24,28},{26,30},{28,20... | collective-permute-start | bytes 1990664 | tf_op jit(solution)/shard_map/ppermute | solution.py:456
  44.5 1.3 shard_map.104.facts_ref
  46.4 2.3 %shard_map.107.own_ref = bf16[64,4608]{1,0:T(8,128)(2,1)} custom-call(s32[5]{0:T(128)S(1)} %copy-done.29, bf16[256,576]{1,0:T(8,128)(2,1)} %collective-permute-done.1.halo_ref, bf16[256,576]{1,0:T(8,128)(2,1)S(1)} %get-tuple-element.88.even_ref), custom_call_target="tpu_custom_call" | custom-call | tf_op jit(solution)/shard_map/pallas_call | solution.py:349
  48.7 3.0 %collective-permute-start.13 = (bf16[64,4608]{1,0:T(8,128)(2,1)}, bf16[64,4608]{1,0:T(8,128)(2,1)}, u32[]{:S(2)}, u32[]{:S(2)}) collective-permute-start(bf16[64,4608]{1,0:T(8,128)(2,1)} %shard_map.107.own_ref), channel_id=1, source_target_pairs={{0,2},{2,0},{4,6},{6,4},{8,10},{10,8},{12,14},{14,12},{16,18},{18,... | collective-permute-start | bytes 1769480 | tf_op jit(solution)/shard_map/ppermute | solution.py:437
  51.7 6.6 %collective-permute-done.6.refs_0_.refs_4_ = bf16[72,4608]{1,0:T(8,128)(2,1)S(1)} collective-permute-done((bf16[72,4608]{1,0:T(8,128)(2,1)S(1)}, bf16[72,4608]{1,0:T(8,128)(2,1)S(1)}, u32[]{:S(2)}, u32[]{:S(2)}) %collective-permute-start.6) | collective-permute-done | bytes 663584 | tf_op jit(solution)/shard_map/ppermute | solution.py:456
  58.3 4.0 %collective-permute-done.7.refs_1_.refs_5_ = bf16[72,4608]{1,0:T(8,128)(2,1)S(1)} collective-permute-done((bf16[72,4608]{1,0:T(8,128)(2,1)}, bf16[72,4608]{1,0:T(8,128)(2,1)S(1)}, u32[]{:S(2)}, u32[]{:S(2)}) %collective-permute-start.7) | collective-permute-done | bytes 663584 | tf_op jit(solution)/shard_map/ppermute | solution.py:456
  62.4 4.3 %collective-permute-start.10 = (bf16[72,4096]{1,0:T(8,128)(2,1)}, bf16[72,4096]{1,0:T(8,128)(2,1)S(1)}, u32[]{:S(2)}, u32[]{:S(2)}) collective-permute-start(bf16[72,4096]{1,0:T(8,128)(2,1)} %refs_0_.1), channel_id=1, source_target_pairs={{0,4},{2,6},{8,0},{10,2},{16,8},{18,10},{24,16},{26,18},{28,24},{3... | collective-permute-start | bytes 1769480 | tf_op jit(solution)/shard_map/ppermute | solution.py:456
  66.7 1.9 %collective-permute-start.12 = (bf16[72,2304]{1,0:T(8,128)(2,1)S(1)}, bf16[72,2304]{1,0:T(8,128)(2,1)S(1)}, u32[]{:S(2)}, u32[]{:S(2)}) collective-permute-start(bf16[72,2304]{1,0:T(8,128)(2,1)S(1)} %slice.13), channel_id=1, source_target_pairs={{0,4},{2,6},{8,0},{10,2},{16,8},{18,10},{24,16},{26,18},{28,24},{3... | collective-permute-start | bytes 995336 | tf_op jit(solution)/shard_map/ppermute | solution.py:456
  68.6 1.7 %shard_map.108.patch_ref = bf16[128,4608]{1,0:T(8,128)(2,1)S(1)} custom-call(s32[5]{0:T(128)S(1)} %copy-done.30, bf16[64,4608]{1,0:T(8,128)(2,1)} %shard_map.107.own_ref, bf16[64,4608]{1,0:T(8,128)(2,1)} %collective-permute-done.13.mate_ref), custom_call_target="tpu_custom_call" | custom-call | tf_op jit(solution)/shard_map/pallas_call | solution.py:338
  70.3 2.3 %shard_map.109.own_ref = f32[128,360]{1,0:T(8,128)S(1)} custom-call(bf16[128,4608]{1,0:T(8,128)(2,1)S(1)} %shard_map.108.patch_ref, bf16[72,4608]{1,0:T(8,128)(2,1)S(1)} %reshape.11.refs_0_.refs_4_, bf16[72,4608]{1,0:T(8,128)(2,1)S(1)} %copy-done.10, bf16[72,4608]{1,0:T(8,128)(2,1)S(1)} %copy-done.7, ...), custom_call_target="tpu_custom_call" | custom-call | tf_op jit(solution)/shard_map/pallas_call | solution.py:598
  72.6 1.3 collective-permute-start.14
  73.9 4.8 %collective-permute-done.14.other_ref = f32[128,360]{1,0:T(8,128)S(1)} collective-permute-done((f32[128,360]{1,0:T(8,128)S(1)}, f32[128,360]{1,0:T(8,128)S(1)}, u32[]{:S(2)}, u32[]{:S(2)}) %collective-permute-start.14) | collective-permute-done | bytes 184352 | tf_op jit(solution)/shard_map/ppermute | solution.py:445
  78.8 1.3 collective-permute-start.8
  80.0 7.1 %collective-permute-done.12 = bf16[72,2304]{1,0:T(8,128)(2,1)S(1)} collective-permute-done((bf16[72,2304]{1,0:T(8,128)(2,1)S(1)}, bf16[72,2304]{1,0:T(8,128)(2,1)S(1)}, u32[]{:S(2)}, u32[]{:S(2)}) %collective-permute-start.12) | collective-permute-done | bytes 331808 | tf_op jit(solution)/shard_map/ppermute | solution.py:456
  87.1 2.3 %collective-permute-done.11 = bf16[72,2304]{1,0:T(8,128)(2,1)S(1)} collective-permute-done((bf16[72,2304]{1,0:T(8,128)(2,1)S(1)}, bf16[72,2304]{1,0:T(8,128)(2,1)S(1)}, u32[]{:S(2)}, u32[]{:S(2)}) %collective-permute-start.11) | collective-permute-done | bytes 331808 | tf_op jit(solution)/shard_map/ppermute | solution.py:456
  89.4 1.5 collective-permute-start.16
  91.8 1.3 collective-permute-start.17
  93.1 1.0 shard_map.111
  96.1 1.1 shard_map.112
  97.8 5.9 %collective-permute-done.15.refs_0_.refs_3_ = bf16[72,4096]{1,0:T(8,128)(2,1)} collective-permute-done((bf16[72,4096]{1,0:T(8,128)(2,1)S(1)}, bf16[72,4096]{1,0:T(8,128)(2,1)}, u32[]{:S(2)}, u32[]{:S(2)}) %collective-permute-start.15) | collective-permute-done | bytes 589856 | tf_op jit(solution)/shard_map/ppermute | solution.py:456
  104.1 1.2 collective-permute-start.19
  105.2 4.4 %all-to-all-start.1 = ((bf16[8,16,576]{2,1,0:T(8,128)(2,1)}), bf16[8,16,576]{2,1,0:T(8,128)(2,1)}, u32[]{:S(2)}, u32[]{:S(2)}) async-start(bf16[8,16,576]{2,1,0:T(8,128)(2,1)} %bitcast.14), calls=%async_computation.1 | async-start | bytes 327680 | tf_op jit(solution)/shard_map/all_to_all | solution.py:651
  109.6 1.2 collective-permute-start.20
  110.9 3.2 %collective-permute-done.20.refs_1_ = f32[128,216]{1,0:T(8,128)S(1)} collective-permute-done((f32[128,216]{1,0:T(8,128)}, f32[128,216]{1,0:T(8,128)S(1)}, u32[]{:S(2)}, u32[]{:S(2)}) %collective-permute-start.20) | collective-permute-done | bytes 110624 | tf_op jit(solution)/shard_map/ppermute | solution.py:445
  114.7 5.3 %all-to-all-done.1 = bf16[8,16,576]{2,1,0:T(8,128)(2,1)} async-done(((bf16[8,16,576]{2,1,0:T(8,128)(2,1)}), bf16[8,16,576]{2,1,0:T(8,128)(2,1)}, u32[]{:S(2)}, u32[]{:S(2)}) %all-to-all-start.1) | async-done | bytes 147488 | tf_op jit(solution)/shard_map/all_to_all | solution.py:651
  120.0 1.0 slice.14
  121.1 1.0 slice.15
  122.1 1.5 collective-permute-start.22
  123.7 1.7 %shard_map.114.refs_0_ = f32[128,144]{1,0:T(8,128)S(1)} custom-call(bf16[64,4096]{1,0:T(8,128)(2,1)S(1)} %bitcast.8, bf16[64,4096]{1,0:T(8,128)(2,1)S(1)} %copy-done.3, bf16[72,4096]{1,0:T(8,128)(2,1)} %collective-permute-done.15.refs_0_.refs_3_, bf16[72,4096]{1,0:T(8,128)(2,1)} %collective-permute-done.16.refs_1_.refs_4_), custom_call_target="tpu_custom_call" | custom-call | tf_op jit(solution)/shard_map/pallas_call | solution.py:605
  125.4 1.3 collective-permute-start.23
  126.7 1.1 shard_map.115
  127.9 1.7 %collective-permute-done.23.refs_1_ = f32[128,144]{1,0:T(8,128)S(1)} collective-permute-done((f32[128,144]{1,0:T(8,128)S(1)}, f32[128,144]{1,0:T(8,128)S(1)}, u32[]{:S(2)}, u32[]{:S(2)}) %collective-permute-start.23) | collective-permute-done | bytes 73760 | tf_op jit(solution)/shard_map/ppermute | solution.py:445
  129.6 1.8 %shard_map.116 = (f32[64,2304]{1,0:T(8,128)S(1)}, f32[64,2304]{1,0:T(8,128)S(1)}, f32[64,2304]{1,0:T(8,128)S(1)}, f32[64,2304]{1,0:T(8,128)S(1)}) custom-call(s32[5]{0:T(128)S(1)} %copy-done.30, f32[128,144]{1,0:T(8,128)S(1)} %shard_map.114.refs_0_, f32[128,144]{1,0:T(8,128)S(1)} %collective-permute-done.23.refs_1_, ...), custom_call_target="tpu_custom_call" | custom-call | tf_op jit(solution)/shard_map/pallas_call | solution.py:609
  131.4 2.0 %shard_map.117.refs_0_ = f32[128,216]{1,0:T(8,128)S(1)} custom-call(bf16[64,4096]{1,0:T(8,128)(2,1)S(1)} %bitcast.9, bf16[64,4096]{1,0:T(8,128)(2,1)S(1)} %copy-done.3, bf16[72,4096]{1,0:T(8,128)(2,1)} %collective-permute-done.18.refs_0_.refs_5_, bf16[72,4096]{1,0:T(8,128)(2,1)} %collective-permute-done.19.refs_1_.refs_6_, ...), custom_call_target="tpu_custom_call" | custom-call | tf_op jit(solution)/shard_map/pallas_call | solution.py:605
  133.4 1.3 collective-permute-start.24
  134.7 2.6 %collective-permute-done.24.refs_1_ = f32[128,216]{1,0:T(8,128)S(1)} collective-permute-done((f32[128,216]{1,0:T(8,128)S(1)}, f32[128,216]{1,0:T(8,128)S(1)}, u32[]{:S(2)}, u32[]{:S(2)}) %collective-permute-start.24) | collective-permute-done | bytes 110624 | tf_op jit(solution)/shard_map/ppermute | solution.py:445
  137.3 1.0 shard_map.118
  138.3 6.7 %collective-permute-start.25 = (bf16[64,2304]{1,0:T(8,128)(2,1)S(1)}, bf16[64,2304]{1,0:T(8,128)(2,1)S(1)}, u32[]{:S(2)}, u32[]{:S(2)}) collective-permute-start(bf16[64,2304]{1,0:T(8,128)(2,1)S(1)} %get-tuple-element.123), channel_id=1, source_target_pairs={{0,2},{2,0},{4,6},{6,4},{8,10},{10,8},{12,14},{14,12},{16,18},{18,... | collective-permute-start | bytes 884744 | tf_op jit(solution)/shard_map/ppermute | solution.py:437
  145.0 1.0 shard_map.120
  146.2 1.3 shard_map.119
  147.5 2.3 %collective-permute-start.28 = (bf16[256,576]{1,0:T(8,128)(2,1)S(1)}, bf16[256,576]{1,0:T(8,128)(2,1)S(1)}, u32[]{:S(2)}, u32[]{:S(2)}) collective-permute-start(bf16[256,576]{1,0:T(8,128)(2,1)S(1)} %get-tuple-element.135), channel_id=1, source_target_pairs={{2,0},{4,2},{6,4},{8,6},{10,8},{12,10},{14,12},{16,14},{18,16},{20... | collective-permute-start | bytes 884744 | tf_op jit(solution)/shard_map/ppermute | solution.py:420
  149.9 1.2 shard_map.121
  151.2 4.1 %shard_map.122 = (f32[64,4096]{1,0:T(8,128)S(1)}, bf16[64,4096]{1,0:T(8,128)(2,1)S(1)}) custom-call(s32[5]{0:T(128)S(1)} %get-tuple-element.130.facts_ref, bf16[128,576]{1,0:T(8,128)(2,1)} %bitcast.5.act_ref, bf16[72,4096]{1,0:T(8,128)(2,1)S(1)} %copy-done.13, bf16[72,4096]{1,0:T(8,128)(2,1)S(1)} %copy-done.17, bf16[72,4096]{1,0:T(8,128)(2,1)S(1)} %copy-done.15, ...), custom_call_target="tpu_custom_call" | custom-call | tf_op jit(solution)/shard_map/pallas_call | solution.py:637
  155.3 1.0 collective-permute-start.27
  156.8 0.9 shard_map.123
  157.8 1.3 collective-permute-start.29
  159.0 1.7 %shard_map.124 = (bf16[2304,256]{1,0:T(8,128)(2,1)S(1)}, bf16[2304,256]{1,0:T(8,128)(2,1)S(1)}, bf16[2304,256]{1,0:T(8,128)(2,1)S(1)}) custom-call(s32[5]{0:T(128)S(1)} %get-tuple-element.130.facts_ref, bf16[9,48,576]{2,1,0:T(8,128)(2,1)S(1)} %bitcast.11), custom_call_target="tpu_custom_call" | custom-call | tf_op jit(solution)/shard_map/pallas_call | solution.py:609
  160.8 2.8 %shard_map.125 = bf16[2,196,576]{2,1,0:T(8,128)(2,1)S(1)} custom-call(f32[256,576]{1,0:T(8,128)S(1)} %get-tuple-element.134.even_ref, bf16[256,576]{1,0:T(8,128)(2,1)S(1)} %collective-permute-done.28.odd_ref, f32[512,576]{1,0:T(8,128)S(1)} %copy-done.1, f32[2,576]{1,0:T(2,128)S(1)} %get-tuple-element.136.excite_ref, f32[2,288]{1,0:T(2,128)S(1)} %add.9.sq_ref, ...), custom_call_target="tpu_custom_call" | custom-call | flops 2717908992 | bytes 4718592 | tf_op jit(solution)/shard_map/pallas_call | solution.py:385
  163.6 1.2 copy.12
  164.7 0.9 add_convert_fusion
  (96 shorter events, 6.7 us)
Async XLA Ops:
  0.6 4.4 %copy-start.24 = (bf16[576,288]{0,1:T(8,128)(2,1)S(1)}, bf16[576,288]{0,1:T(8,128)(2,1)}, u32[]{:S(2)}) copy-start(bf16[576,288]{0,1:T(8,128)(2,1)} %param.11) | copy-start | bytes 995332
  0.6 4.4 %copy-start.18 = (bf16[9,576,48]{1,2,0:T(8,128)(2,1)S(1)}, bf16[9,576,48]{1,2,0:T(8,128)(2,1)}, u32[]{:S(2)}) copy-start(bf16[9,576,48]{1,2,0:T(8,128)(2,1)} %param.10) | copy-start | bytes 1492996
  2.4 9.9 %copy-start.20 = (bf16[288,576]{1,0:T(8,128)(2,1)S(1)}, bf16[288,576]{1,0:T(8,128)(2,1)}, u32[]{:S(2)}) copy-start(bf16[288,576]{1,0:T(8,128)(2,1)} %expand_ref.3) | copy-start | bytes 995332
  2.4 15.8 %collective-permute-start.3 = (bf16[72,4608]{1,0:T(8,128)(2,1)S(1)}, bf16[72,4608]{1,0:T(8,128)(2,1)S(1)}, u32[]{:S(2)}, u32[]{:S(2)}) collective-permute-start(bf16[72,4608]{1,0:T(8,128)(2,1)S(1)} %reshape.11.refs_0_.refs_4_), channel_id=1, source_target_pairs={{0,4},{2,6},{8,0},{10,2},{16,8},{18,10},{24,16},{26,18},{28,24},{3... | collective-permute-start | bytes 1990664 | tf_op jit(solution)/shard_map/ppermute | solution.py:456
  3.8 15.5 %collective-permute-start.2 = (bf16[72,4608]{1,0:T(8,128)(2,1)S(1)}, bf16[72,4608]{1,0:T(8,128)(2,1)S(1)}, u32[]{:S(2)}, u32[]{:S(2)}) collective-permute-start(bf16[72,4608]{1,0:T(8,128)(2,1)S(1)} %reshape.11.refs_0_.refs_4_), channel_id=1, source_target_pairs={{0,8},{2,10},{8,16},{10,18},{16,24},{18,26},{24,28},{26,30},{28,20... | collective-permute-start | bytes 1990664 | tf_op jit(solution)/shard_map/ppermute | solution.py:456
  9.5 9.7 %copy-start = (f32[512,576]{1,0:T(8,128)}, f32[512,576]{1,0:T(8,128)S(1)}, u32[]{:S(2)}) copy-start(f32[512,576]{1,0:T(8,128)S(1)} %get-tuple-element.71.conv_ref) | copy-start | bytes 3538948
  9.5 2.8 %collective-permute-start = (f32[2,288]{1,0:T(2,128)S(1)}, f32[2,288]{1,0:T(2,128)S(1)}, u32[]{:S(2)}, u32[]{:S(2)}) collective-permute-start(f32[2,288]{1,0:T(2,128)S(1)} %get-tuple-element.74), channel_id=1, source_target_pairs={{0,1},{1,0},{2,3},{3,2},{4,5},{5,4},{6,7},{7,6},{8,9},{9,8},{10,11... | collective-permute-start | bytes 6920 | tf_op jit(solution)/shard_map/ppermute | solution.py:445
  18.2 22.5 %copy-start.6 = (bf16[72,4608]{1,0:T(8,128)(2,1)}, bf16[72,4608]{1,0:T(8,128)(2,1)S(1)}, u32[]{:S(2)}) copy-start(bf16[72,4608]{1,0:T(8,128)(2,1)S(1)} %collective-permute-done.3.refs_2_.refs_6_) | copy-start | bytes 1990660
  19.2 21.5 %collective-permute-start.4 = (bf16[72,4608]{1,0:T(8,128)(2,1)S(1)}, bf16[72,4608]{1,0:T(8,128)(2,1)S(1)}, u32[]{:S(2)}, u32[]{:S(2)}) collective-permute-start(bf16[72,4608]{1,0:T(8,128)(2,1)S(1)} %collective-permute-done.2.refs_1_.refs_5_), channel_id=1, source_target_pairs={{0,8},{2,10},{8,16},{10,18},{16,24},{18,26},{24,28},{26,30},{28,20... | collective-permute-start | bytes 1990664 | tf_op jit(solution)/shard_map/ppermute | solution.py:456
  19.4 0.8 copy-start.9
  20.2 20.5 %collective-permute-start.5 = (bf16[72,4608]{1,0:T(8,128)(2,1)S(1)}, bf16[72,4608]{1,0:T(8,128)(2,1)}, u32[]{:S(2)}, u32[]{:S(2)}) collective-permute-start(bf16[72,4608]{1,0:T(8,128)(2,1)S(1)} %collective-permute-done.3.refs_2_.refs_6_), channel_id=1, source_target_pairs={{0,4},{2,6},{8,0},{10,2},{16,8},{18,10},{24,16},{26,18},{28,24},{3... | collective-permute-start | bytes 1990664 | tf_op jit(solution)/shard_map/ppermute | solution.py:456
  21.5 19.2 %collective-permute-start.1 = (bf16[256,576]{1,0:T(8,128)(2,1)}, bf16[256,576]{1,0:T(8,128)(2,1)}, u32[]{:S(2)}, u32[]{:S(2)}) collective-permute-start(bf16[256,576]{1,0:T(8,128)(2,1)} %get-tuple-element.75), channel_id=1, source_target_pairs={{0,2},{2,4},{4,6},{6,8},{8,10},{10,12},{12,14},{14,16},{16,18},{18... | collective-permute-start | bytes 884744 | tf_op jit(solution)/shard_map/ppermute | solution.py:420
  25.8 25.9 %all-to-all-start = ((bf16[8,8,4096]{2,1,0:T(8,128)(2,1)}), bf16[8,8,4096]{2,1,0:T(8,128)(2,1)S(1)}, u32[]{:S(2)}, u32[]{:S(2)}) async-start(bf16[8,8,4096]{2,1,0:T(8,128)(2,1)} %bitcast.15), calls=%async_computation | async-start | bytes 1048576 | tf_op jit(solution)/shard_map/all_to_all | solution.py:651
  40.7 29.6 %copy-start.4 = (bf16[72,4608]{1,0:T(8,128)(2,1)}, bf16[72,4608]{1,0:T(8,128)(2,1)S(1)}, u32[]{:S(2)}) copy-start(bf16[72,4608]{1,0:T(8,128)(2,1)S(1)} %collective-permute-done.4.refs_3_.refs_4_) | copy-start | bytes 1990660
  40.7 17.6 %collective-permute-start.6 = (bf16[72,4608]{1,0:T(8,128)(2,1)S(1)}, bf16[72,4608]{1,0:T(8,128)(2,1)S(1)}, u32[]{:S(2)}, u32[]{:S(2)}) collective-permute-start(bf16[72,4608]{1,0:T(8,128)(2,1)S(1)} %collective-permute-done.4.refs_3_.refs_4_), channel_id=1, source_target_pairs={{0,8},{2,10},{8,16},{10,18},{16,24},{18,26},{24,28},{26,30},{28,20... | collective-permute-start | bytes 1990664 | tf_op jit(solution)/shard_map/ppermute | solution.py:456
  44.2 18.1 %collective-permute-start.7 = (bf16[72,4608]{1,0:T(8,128)(2,1)}, bf16[72,4608]{1,0:T(8,128)(2,1)S(1)}, u32[]{:S(2)}, u32[]{:S(2)}) collective-permute-start(bf16[72,4608]{1,0:T(8,128)(2,1)} %collective-permute-done.5.refs_4_.refs_5_), channel_id=1, source_target_pairs={{0,4},{2,6},{8,0},{10,2},{16,8},{18,10},{24,16},{26,18},{28,24},{3... | collective-permute-start | bytes 1990664 | tf_op jit(solution)/shard_map/ppermute | solution.py:456
  45.8 0.7 copy-start.29
  46.4 22.1 %copy-start.30 = (s32[5]{0:T(128)S(1)}, s32[5]{0:T(128)}, u32[]{:S(2)}) copy-start(s32[5]{0:T(128)} %shard_map.104.facts_ref) | copy-start | bytes 64
  48.7 19.8 %collective-permute-start.13 = (bf16[64,4608]{1,0:T(8,128)(2,1)}, bf16[64,4608]{1,0:T(8,128)(2,1)}, u32[]{:S(2)}, u32[]{:S(2)}) collective-permute-start(bf16[64,4608]{1,0:T(8,128)(2,1)} %shard_map.107.own_ref), channel_id=1, source_target_pairs={{0,2},{2,0},{4,6},{6,4},{8,10},{10,8},{12,14},{14,12},{16,18},{18,... | collective-permute-start | bytes 1769480 | tf_op jit(solution)/shard_map/ppermute | solution.py:437
  62.4 27.0 %collective-permute-start.10 = (bf16[72,4096]{1,0:T(8,128)(2,1)}, bf16[72,4096]{1,0:T(8,128)(2,1)S(1)}, u32[]{:S(2)}, u32[]{:S(2)}) collective-permute-start(bf16[72,4096]{1,0:T(8,128)(2,1)} %refs_0_.1), channel_id=1, source_target_pairs={{0,4},{2,6},{8,0},{10,2},{16,8},{18,10},{24,16},{26,18},{28,24},{3... | collective-permute-start | bytes 1769480 | tf_op jit(solution)/shard_map/ppermute | solution.py:456
  66.6 22.7 %collective-permute-start.9 = (bf16[72,4096]{1,0:T(8,128)(2,1)}, bf16[72,4096]{1,0:T(8,128)(2,1)S(1)}, u32[]{:S(2)}, u32[]{:S(2)}) collective-permute-start(bf16[72,4096]{1,0:T(8,128)(2,1)} %refs_0_.1), channel_id=1, source_target_pairs={{0,8},{2,10},{8,16},{10,18},{16,24},{18,26},{24,28},{26,30},{28,20... | collective-permute-start | bytes 1769480 | tf_op jit(solution)/shard_map/ppermute | solution.py:456
  66.7 3.6 %copy-start.7 = (bf16[72,4608]{1,0:T(8,128)(2,1)S(1)}, bf16[72,4608]{1,0:T(8,128)(2,1)}, u32[]{:S(2)}) copy-start(bf16[72,4608]{1,0:T(8,128)(2,1)} %copy-done.6) | copy-start | bytes 1990660
  66.7 3.6 %copy-start.10 = (bf16[72,4608]{1,0:T(8,128)(2,1)S(1)}, bf16[72,4608]{1,0:T(8,128)(2,1)}, u32[]{:S(2)}) copy-start(bf16[72,4608]{1,0:T(8,128)(2,1)} %copy-done.9) | copy-start | bytes 1990660
  66.7 20.4 %collective-permute-start.12 = (bf16[72,2304]{1,0:T(8,128)(2,1)S(1)}, bf16[72,2304]{1,0:T(8,128)(2,1)S(1)}, u32[]{:S(2)}, u32[]{:S(2)}) collective-permute-start(bf16[72,2304]{1,0:T(8,128)(2,1)S(1)} %slice.13), channel_id=1, source_target_pairs={{0,4},{2,6},{8,0},{10,2},{16,8},{18,10},{24,16},{26,18},{28,24},{3... | collective-permute-start | bytes 995336 | tf_op jit(solution)/shard_map/ppermute | solution.py:456
  68.6 20.8 %collective-permute-start.11 = (bf16[72,2304]{1,0:T(8,128)(2,1)S(1)}, bf16[72,2304]{1,0:T(8,128)(2,1)S(1)}, u32[]{:S(2)}, u32[]{:S(2)}) collective-permute-start(bf16[72,2304]{1,0:T(8,128)(2,1)S(1)} %slice.12), channel_id=1, source_target_pairs={{0,8},{2,10},{8,16},{10,18},{16,24},{18,26},{24,28},{26,30},{28,20... | collective-permute-start | bytes 995336 | tf_op jit(solution)/shard_map/ppermute | solution.py:456
  72.6 6.1 %collective-permute-start.14 = (f32[128,360]{1,0:T(8,128)S(1)}, f32[128,360]{1,0:T(8,128)S(1)}, u32[]{:S(2)}, u32[]{:S(2)}) collective-permute-start(f32[128,360]{1,0:T(8,128)S(1)} %shard_map.109.own_ref), channel_id=1, source_target_pairs={{0,1},{1,0},{2,3},{3,2},{4,5},{5,4},{6,7},{7,6},{8,9},{9,8},{10,11... | collective-permute-start | bytes 552968 | tf_op jit(solution)/shard_map/ppermute | solution.py:445
  78.8 15.4 %collective-permute-start.8 = (bf16[64,4096]{1,0:T(8,128)(2,1)S(1)}, bf16[64,4096]{1,0:T(8,128)(2,1)S(1)}, u32[]{:S(2)}, u32[]{:S(2)}) collective-permute-start(bf16[64,4096]{1,0:T(8,128)(2,1)S(1)} %bitcast.6), channel_id=1, source_target_pairs={{0,2},{2,0},{4,6},{6,4},{8,10},{10,8},{12,14},{14,12},{16,18},{18,... | collective-permute-start | bytes 1572872 | tf_op jit(solution)/shard_map/ppermute | solution.py:437
  89.4 4.8 %copy-start.14 = (bf16[72,4096]{1,0:T(8,128)(2,1)}, bf16[72,4096]{1,0:T(8,128)(2,1)S(1)}, u32[]{:S(2)}) copy-start(bf16[72,4096]{1,0:T(8,128)(2,1)S(1)} %collective-permute-done.10.refs_2_) | copy-start | bytes 1769476
  89.4 4.8 %copy-start.16 = (bf16[72,4096]{1,0:T(8,128)(2,1)}, bf16[72,4096]{1,0:T(8,128)(2,1)S(1)}, u32[]{:S(2)}) copy-start(bf16[72,4096]{1,0:T(8,128)(2,1)S(1)} %collective-permute-done.9.refs_1_) | copy-start | bytes 1769476
  89.4 14.3 %collective-permute-start.15 = (bf16[72,4096]{1,0:T(8,128)(2,1)S(1)}, bf16[72,4096]{1,0:T(8,128)(2,1)}, u32[]{:S(2)}, u32[]{:S(2)}) collective-permute-start(bf16[72,4096]{1,0:T(8,128)(2,1)S(1)} %collective-permute-done.9.refs_1_), channel_id=1, source_target_pairs={{0,8},{2,10},{8,16},{10,18},{16,24},{18,26},{24,28},{26,30},{28,20... | collective-permute-start | bytes 1769480 | tf_op jit(solution)/shard_map/ppermute | solution.py:456
  89.4 14.3 %collective-permute-start.16 = (bf16[72,4096]{1,0:T(8,128)(2,1)S(1)}, bf16[72,4096]{1,0:T(8,128)(2,1)}, u32[]{:S(2)}, u32[]{:S(2)}) collective-permute-start(bf16[72,4096]{1,0:T(8,128)(2,1)S(1)} %collective-permute-done.10.refs_2_), channel_id=1, source_target_pairs={{0,4},{2,6},{8,0},{10,2},{16,8},{18,10},{24,16},{26,18},{28,24},{3... | collective-permute-start | bytes 1769480 | tf_op jit(solution)/shard_map/ppermute | solution.py:456
  91.0 3.2 %copy-start.12 = (bf16[72,4096]{1,0:T(8,128)(2,1)S(1)}, bf16[72,4096]{1,0:T(8,128)(2,1)}, u32[]{:S(2)}) copy-start(bf16[72,4096]{1,0:T(8,128)(2,1)} %refs_0_.1) | copy-start | bytes 1769476
  91.8 4.3 %collective-permute-start.17 = (f32[128,216]{1,0:T(8,128)S(1)}, f32[128,216]{1,0:T(8,128)S(1)}, u32[]{:S(2)}, u32[]{:S(2)}) collective-permute-start(f32[128,216]{1,0:T(8,128)S(1)} %shard_map.110.own_ref), channel_id=1, source_target_pairs={{0,1},{1,0},{2,3},{3,2},{4,5},{5,4},{6,7},{7,6},{8,9},{9,8},{10,11... | collective-permute-start | bytes 331784 | tf_op jit(solution)/shard_map/ppermute | solution.py:445
  94.2 0.8 copy-start.2
  95.0 0.6 copy-start.22
  97.1 0.7 copy-start.26
  103.8 16.3 %collective-permute-start.18 = (bf16[72,4096]{1,0:T(8,128)(2,1)}, bf16[72,4096]{1,0:T(8,128)(2,1)}, u32[]{:S(2)}, u32[]{:S(2)}) collective-permute-start(bf16[72,4096]{1,0:T(8,128)(2,1)} %collective-permute-done.15.refs_0_.refs_3_), channel_id=1, source_target_pairs={{0,8},{2,10},{8,16},{10,18},{16,24},{18,26},{24,28},{26,30},{28,20... | collective-permute-start | bytes 1769480 | tf_op jit(solution)/shard_map/ppermute | solution.py:456
  104.1 16.0 %collective-permute-start.19 = (bf16[72,4096]{1,0:T(8,128)(2,1)}, bf16[72,4096]{1,0:T(8,128)(2,1)}, u32[]{:S(2)}, u32[]{:S(2)}) collective-permute-start(bf16[72,4096]{1,0:T(8,128)(2,1)} %collective-permute-done.16.refs_1_.refs_4_), channel_id=1, source_target_pairs={{0,4},{2,6},{8,0},{10,2},{16,8},{18,10},{24,16},{26,18},{28,24},{3... | collective-permute-start | bytes 1769480 | tf_op jit(solution)/shard_map/ppermute | solution.py:456
  105.2 14.8 %all-to-all-start.1 = ((bf16[8,16,576]{2,1,0:T(8,128)(2,1)}), bf16[8,16,576]{2,1,0:T(8,128)(2,1)}, u32[]{:S(2)}, u32[]{:S(2)}) async-start(bf16[8,16,576]{2,1,0:T(8,128)(2,1)} %bitcast.14), calls=%async_computation.1 | async-start | bytes 327680 | tf_op jit(solution)/shard_map/all_to_all | solution.py:651
  109.6 4.4 %collective-permute-start.20 = (f32[128,216]{1,0:T(8,128)}, f32[128,216]{1,0:T(8,128)S(1)}, u32[]{:S(2)}, u32[]{:S(2)}) collective-permute-start(f32[128,216]{1,0:T(8,128)} %copy-done.22), channel_id=1, source_target_pairs={{0,1},{1,0},{2,3},{3,2},{4,5},{5,4},{6,7},{7,6},{8,9},{9,8},{10,11... | collective-permute-start | bytes 331784 | tf_op jit(solution)/shard_map/ppermute | solution.py:445
  114.1 0.7 copy-start.27
  120.0 3.6 %copy-start.3 = (bf16[64,4096]{1,0:T(8,128)(2,1)S(1)}, bf16[64,4096]{1,0:T(8,128)(2,1)}, u32[]{:S(2)}) copy-start(bf16[64,4096]{1,0:T(8,128)(2,1)} %copy-done.2) | copy-start | bytes 1572868
  122.1 4.7 %copy-start.8 = (bf16[72,4608]{1,0:T(8,128)(2,1)S(1)}, bf16[72,4608]{1,0:T(8,128)(2,1)}, u32[]{:S(2)}) copy-start(bf16[72,4608]{1,0:T(8,128)(2,1)} %copy-done.6) | copy-start | bytes 1990660
  122.1 4.6 %copy-start.11 = (bf16[72,4608]{1,0:T(8,128)(2,1)S(1)}, bf16[72,4608]{1,0:T(8,128)(2,1)}, u32[]{:S(2)}) copy-start(bf16[72,4608]{1,0:T(8,128)(2,1)} %copy-done.9) | copy-start | bytes 1990660
  122.1 4.6 %copy-start.23 = (f32[128,216]{1,0:T(8,128)S(1)}, f32[128,216]{1,0:T(8,128)}, u32[]{:S(2)}) copy-start(f32[128,216]{1,0:T(8,128)} %copy-done.22) | copy-start | bytes 331780
  122.1 4.6 %copy-start.28 = (f32[128,216]{1,0:T(8,128)S(1)}, f32[128,216]{1,0:T(8,128)}, u32[]{:S(2)}) copy-start(f32[128,216]{1,0:T(8,128)} %copy-done.27) | copy-start | bytes 331780
  122.1 9.2 %collective-permute-start.22 = (bf16[72,2048]{1,0:T(8,128)(2,1)S(1)}, bf16[72,2048]{1,0:T(8,128)(2,1)S(1)}, u32[]{:S(2)}, u32[]{:S(2)}) collective-permute-start(bf16[72,2048]{1,0:T(8,128)(2,1)S(1)} %slice.15), channel_id=1, source_target_pairs={{0,4},{2,6},{8,0},{10,2},{16,8},{18,10},{24,16},{26,18},{28,24},{3... | collective-permute-start | bytes 884744 | tf_op jit(solution)/shard_map/ppermute | solution.py:456
  123.6 7.7 %collective-permute-start.21 = (bf16[72,2048]{1,0:T(8,128)(2,1)S(1)}, bf16[72,2048]{1,0:T(8,128)(2,1)S(1)}, u32[]{:S(2)}, u32[]{:S(2)}) collective-permute-start(bf16[72,2048]{1,0:T(8,128)(2,1)S(1)} %slice.14), channel_id=1, source_target_pairs={{0,8},{2,10},{8,16},{10,18},{16,24},{18,26},{24,28},{26,30},{28,20... | collective-permute-start | bytes 884744 | tf_op jit(solution)/shard_map/ppermute | solution.py:456
  125.4 4.2 %collective-permute-start.23 = (f32[128,144]{1,0:T(8,128)S(1)}, f32[128,144]{1,0:T(8,128)S(1)}, u32[]{:S(2)}, u32[]{:S(2)}) collective-permute-start(f32[128,144]{1,0:T(8,128)S(1)} %shard_map.114.refs_0_), channel_id=1, source_target_pairs={{0,1},{1,0},{2,3},{3,2},{4,5},{5,4},{6,7},{7,6},{8,9},{9,8},{10,11... | collective-permute-start | bytes 221192 | tf_op jit(solution)/shard_map/ppermute | solution.py:445
  126.7 2.9 %copy-start.5 = (bf16[72,4608]{1,0:T(8,128)(2,1)S(1)}, bf16[72,4608]{1,0:T(8,128)(2,1)}, u32[]{:S(2)}) copy-start(bf16[72,4608]{1,0:T(8,128)(2,1)} %copy-done.4) | copy-start | bytes 1990660
  133.4 3.9 %collective-permute-start.24 = (f32[128,216]{1,0:T(8,128)S(1)}, f32[128,216]{1,0:T(8,128)S(1)}, u32[]{:S(2)}, u32[]{:S(2)}) collective-permute-start(f32[128,216]{1,0:T(8,128)S(1)} %shard_map.117.refs_0_), channel_id=1, source_target_pairs={{0,1},{1,0},{2,3},{3,2},{4,5},{5,4},{6,7},{7,6},{8,9},{9,8},{10,11... | collective-permute-start | bytes 331784 | tf_op jit(solution)/shard_map/ppermute | solution.py:445
  138.3 7.9 %collective-permute-start.25 = (bf16[64,2304]{1,0:T(8,128)(2,1)S(1)}, bf16[64,2304]{1,0:T(8,128)(2,1)S(1)}, u32[]{:S(2)}, u32[]{:S(2)}) collective-permute-start(bf16[64,2304]{1,0:T(8,128)(2,1)S(1)} %get-tuple-element.123), channel_id=1, source_target_pairs={{0,2},{2,0},{4,6},{6,4},{8,10},{10,8},{12,14},{14,12},{16,18},{18,... | collective-permute-start | bytes 884744 | tf_op jit(solution)/shard_map/ppermute | solution.py:437
  146.0 5.1 %copy-start.13 = (bf16[72,4096]{1,0:T(8,128)(2,1)S(1)}, bf16[72,4096]{1,0:T(8,128)(2,1)}, u32[]{:S(2)}) copy-start(bf16[72,4096]{1,0:T(8,128)(2,1)} %refs_0_.1) | copy-start | bytes 1769476
  146.0 5.1 %copy-start.15 = (bf16[72,4096]{1,0:T(8,128)(2,1)S(1)}, bf16[72,4096]{1,0:T(8,128)(2,1)}, u32[]{:S(2)}) copy-start(bf16[72,4096]{1,0:T(8,128)(2,1)} %copy-done.14) | copy-start | bytes 1769476
  146.0 5.1 %copy-start.17 = (bf16[72,4096]{1,0:T(8,128)(2,1)S(1)}, bf16[72,4096]{1,0:T(8,128)(2,1)}, u32[]{:S(2)}) copy-start(bf16[72,4096]{1,0:T(8,128)(2,1)} %copy-done.16) | copy-start | bytes 1769476
  146.0 3.8 %collective-permute-start.26 = (bf16[64,2304]{1,0:T(8,128)(2,1)S(1)}, bf16[64,2304]{1,0:T(8,128)(2,1)S(1)}, u32[]{:S(2)}, u32[]{:S(2)}) collective-permute-start(bf16[64,2304]{1,0:T(8,128)(2,1)S(1)} %get-tuple-element.129), channel_id=1, source_target_pairs={{0,2},{2,0},{4,6},{6,4},{8,10},{10,8},{12,14},{14,12},{16,18},{18,... | collective-permute-start | bytes 884744 | tf_op jit(solution)/shard_map/ppermute | solution.py:437
  147.5 9.3 %collective-permute-start.28 = (bf16[256,576]{1,0:T(8,128)(2,1)S(1)}, bf16[256,576]{1,0:T(8,128)(2,1)S(1)}, u32[]{:S(2)}, u32[]{:S(2)}) collective-permute-start(bf16[256,576]{1,0:T(8,128)(2,1)S(1)} %get-tuple-element.135), channel_id=1, source_target_pairs={{2,0},{4,2},{6,4},{8,6},{10,8},{12,10},{14,12},{16,14},{18,16},{20... | collective-permute-start | bytes 884744 | tf_op jit(solution)/shard_map/ppermute | solution.py:420
  151.1 5.7 %copy-start.1 = (f32[512,576]{1,0:T(8,128)S(1)}, f32[512,576]{1,0:T(8,128)}, u32[]{:S(2)}) copy-start(f32[512,576]{1,0:T(8,128)} %copy-done) | copy-start | bytes 3538948
  151.2 5.7 %copy-start.21 = (bf16[288,576]{1,0:T(8,128)(2,1)S(1)}, bf16[288,576]{1,0:T(8,128)(2,1)}, u32[]{:S(2)}) copy-start(bf16[288,576]{1,0:T(8,128)(2,1)} %expand_ref.3) | copy-start | bytes 995332
  155.3 9.4 %collective-permute-start.27 = (bf16[64,4096]{1,0:T(8,128)(2,1)S(1)}, bf16[64,4096]{1,0:T(8,128)(2,1)S(1)}, u32[]{:S(2)}, u32[]{:S(2)}) collective-permute-start(bf16[64,4096]{1,0:T(8,128)(2,1)S(1)} %get-tuple-element.133), channel_id=1, source_target_pairs={{0,2},{2,0},{4,6},{6,4},{8,10},{10,8},{12,14},{14,12},{16,18},{18,... | collective-permute-start | bytes 1572872 | tf_op jit(solution)/shard_map/ppermute | solution.py:437
  156.8 2.2 %copy-start.19 = (bf16[9,576,48]{1,2,0:T(8,128)(2,1)S(1)}, bf16[9,576,48]{1,2,0:T(8,128)(2,1)}, u32[]{:S(2)}) copy-start(bf16[9,576,48]{1,2,0:T(8,128)(2,1)} %param.10) | copy-start | bytes 1492996
  156.8 3.9 %copy-start.25 = (bf16[576,288]{0,1:T(8,128)(2,1)S(1)}, bf16[576,288]{0,1:T(8,128)(2,1)}, u32[]{:S(2)}) copy-start(bf16[576,288]{0,1:T(8,128)(2,1)} %param.11) | copy-start | bytes 995332
  157.8 2.9 %collective-permute-start.29 = (f32[2,288]{1,0:T(2,128)S(1)}, f32[2,288]{1,0:T(2,128)S(1)}, u32[]{:S(2)}, u32[]{:S(2)}) collective-permute-start(f32[2,288]{1,0:T(2,128)S(1)} %shard_map.123), channel_id=1, source_target_pairs={{0,1},{1,0},{2,3},{3,2},{4,5},{5,4},{6,7},{7,6},{8,9},{9,8},{10,11... | collective-permute-start | bytes 6920 | tf_op jit(solution)/shard_map/ppermute | solution.py:445

commit v14 on v13

--- a/solution.py
+++ b/solution.py
@@ -700,8 +700,7 @@
     count = 2 * steps - 3
     r_up, r_down = [ring_send(readout_kernel, 1)], [ring_send(readout_kernel, -1)]
     first_pre = tp_terms(block_products(pre_kernel, (patches,), samplers[:count]))
-    held = tie(r_up[0], r_down[0], *s_last, *first_pre)
-    r_up[0], r_down[0], s_last, first_pre = held[0], held[1], held[2:4], held[4:]
+    r_up[0], r_down[0], *first_pre = tie(r_up[0], r_down[0], *first_pre)
     for step in range(2, steps - 1):
         r_up.append(ring_send(r_up[-1], 1))
         r_down.append(ring_send(r_down[-1], -1))

time: 168 us -> 166 us (0.988)
  starting transfers between devices: 54.4 us -> 52 us
    ppermute x5, starting transfers between devices: 12 us -> 9.95 us  [swap_cores(): lax.ppermute(value, 'ctx', [(i, i ^ 1) for i in range(lax.axis_size('ctx'...]
where the time goes in v14:
time: 166 us; the launch traced here: 164 us
  waiting for transfers between devices  62.4 us (38%)
  starting transfers between devices  52 us (31%)
  Pallas kernels  38 us (23%)
  local copies, waits for them, and re-layouts  9.69 us (6%)
    ppermute x16, waiting for transfers between devices, ring_send(): return lax.ppermute(value, 'ctx', ring_pairs(lax.axis_size('ctx'), by))  31.6 us
    ppermute x16, starting transfers between devices, ring_send(): return lax.ppermute(value, 'ctx', ring_pairs(lax.axis_size('ctx'), by))  17.5 us
    ppermute x7, waiting for transfers between devices, tp_terms(): other = lax.ppermute(value, 'tp', [(i, i ^ reach) for i in range(size)])  12.9 us
    ppermute x2, waiting for transfers between devices, shifted(): return lax.ppermute(value, axis, pairs)  10.9 us
    ppermute x5, starting transfers between devices, swap_cores(): lax.ppermute(value, 'ctx', [(i, i ^ 1) for i in range(lax.axis_size('ctx'...  9.95 us
    ppermute x7, starting transfers between devices, tp_terms(): other = lax.ppermute(value, 'tp', [(i, i ^ reach) for i in range(size)])  9.04 us
    all_to_all x2, starting transfers between devices, chips_exchange(): lax.all_to_all(value, 'ctx', split_axis=0, concat_axis=0, tiled=True, axi...  8.98 us
    pallas_call x7, Pallas kernels, facts_call(): pl.pallas_call(kernel, out_shape=outs, in_specs=vmem_specs(len(operands))...  8.64 us
  transfers between devices with their start and end apart: 32, of which 18 were waited for; matrix products, arithmetic and copies ran while one was open for 1% of the time, Pallas kernels for 21%

profile of v14, /device:TPU:3, one launch (start us, length us, event | category | flops | bytes accessed | tf_op | source)
XLA Modules:
  0.0 164.1 jit_solution(6727004504780537680)
XLA Ops:
  0.7 1.7 %reshape.11.refs_0_.refs_4_ = bf16[72,4608]{1,0:T(8,128)(2,1)S(1)} reshape(bf16[72,8,576]{2,1,0:T(8,128)(2,1)} %param.13) | data formatting | bytes 1327104 | tf_op jit(solution)/shard_map/reshape | solution.py:670
  2.4 1.3 collective-permute-start.3
  3.9 1.1 copy.11.feat_ref
  5.0 4.5 %shard_map.105 = (f32[512,576]{1,0:T(8,128)S(1)}, bf16[512,576]{1,0:T(8,128)(2,1)S(1)}, f32[2,288]{1,0:T(2,128)S(1)}) custom-call(bf16[2,196,576]{2,1,0:T(8,128)(2,1)S(1)} %copy.11.feat_ref, bf16[9,48,576]{2,1,0:T(8,128)(2,1)S(1)} %bitcast.10, bf16[288,576]{1,0:T(8,128)(2,1)S(1)} %bitcast.12), custom_call_target="tpu_custom_call" | custom-call | tf_op jit(solution)/shard_map/pallas_call | solution.py:301
  9.5 1.3 collective-permute-start
  10.8 1.5 collective-permute-done
  12.3 1.5 shard_map.106
  13.8 4.5 %collective-permute-done.3.refs_2_.refs_6_ = bf16[72,4608]{1,0:T(8,128)(2,1)S(1)} collective-permute-done((bf16[72,4608]{1,0:T(8,128)(2,1)S(1)}, bf16[72,4608]{1,0:T(8,128)(2,1)S(1)}, u32[]{:S(2)}, u32[]{:S(2)}) %collective-permute-start.3) | collective-permute-done | bytes 663584 | tf_op jit(solution)/shard_map/ppermute | solution.py:456
  18.2 1.0 collective-permute-done.2.refs_1_.refs_5_
  19.4 0.8 copy-done.9
  20.2 1.3 collective-permute-start.5
  21.5 4.2 %collective-permute-start.1 = (bf16[256,576]{1,0:T(8,128)(2,1)}, bf16[256,576]{1,0:T(8,128)(2,1)}, u32[]{:S(2)}, u32[]{:S(2)}) collective-permute-start(bf16[256,576]{1,0:T(8,128)(2,1)} %get-tuple-element.73), channel_id=1, source_target_pairs={{0,2},{2,4},{4,6},{6,8},{8,10},{10,12},{12,14},{14,16},{16,18},{18... | collective-permute-start | bytes 884744 | tf_op jit(solution)/shard_map/ppermute | solution.py:420
  25.8 5.0 %all-to-all-start = ((bf16[8,8,4096]{2,1,0:T(8,128)(2,1)}), bf16[8,8,4096]{2,1,0:T(8,128)(2,1)S(1)}, u32[]{:S(2)}, u32[]{:S(2)}) async-start(bf16[8,8,4096]{2,1,0:T(8,128)(2,1)} %bitcast.15), calls=%async_computation | async-start | bytes 1048576 | tf_op jit(solution)/shard_map/all_to_all | solution.py:651
  30.8 9.9 %collective-permute-done.1.halo_ref = bf16[256,576]{1,0:T(8,128)(2,1)} collective-permute-done((bf16[256,576]{1,0:T(8,128)(2,1)}, bf16[256,576]{1,0:T(8,128)(2,1)}, u32[]{:S(2)}, u32[]{:S(2)}) %collective-permute-start.1) | collective-permute-done | bytes 294944 | tf_op jit(solution)/shard_map/ppermute | solution.py:420
  40.7 3.5 %collective-permute-start.6 = (bf16[72,4608]{1,0:T(8,128)(2,1)S(1)}, bf16[72,4608]{1,0:T(8,128)(2,1)S(1)}, u32[]{:S(2)}, u32[]{:S(2)}) collective-permute-start(bf16[72,4608]{1,0:T(8,128)(2,1)S(1)} %collective-permute-done.4.refs_3_.refs_4_), channel_id=1, source_target_pairs={{0,8},{2,10},{8,16},{10,18},{16,24},{18,26},{24,28},{26,30},{28,20... | collective-permute-start | bytes 1990664 | tf_op jit(solution)/shard_map/ppermute | solution.py:456
  44.5 1.3 shard_map.104.facts_ref
  46.4 2.3 %shard_map.107.own_ref = bf16[64,4608]{1,0:T(8,128)(2,1)} custom-call(s32[5]{0:T(128)S(1)} %copy-done.29, bf16[256,576]{1,0:T(8,128)(2,1)} %collective-permute-done.1.halo_ref, bf16[256,576]{1,0:T(8,128)(2,1)S(1)} %get-tuple-element.84.even_ref), custom_call_target="tpu_custom_call" | custom-call | tf_op jit(solution)/shard_map/pallas_call | solution.py:349
  48.7 3.0 %collective-permute-start.11 = (bf16[64,4608]{1,0:T(8,128)(2,1)}, bf16[64,4608]{1,0:T(8,128)(2,1)}, u32[]{:S(2)}, u32[]{:S(2)}) collective-permute-start(bf16[64,4608]{1,0:T(8,128)(2,1)} %shard_map.107.own_ref), channel_id=1, source_target_pairs={{0,2},{2,0},{4,6},{6,4},{8,10},{10,8},{12,14},{14,12},{16,18},{18,... | collective-permute-start | bytes 1769480 | tf_op jit(solution)/shard_map/ppermute | solution.py:437
  51.7 6.6 %collective-permute-done.6.refs_0_.refs_4_ = bf16[72,4608]{1,0:T(8,128)(2,1)S(1)} collective-permute-done((bf16[72,4608]{1,0:T(8,128)(2,1)S(1)}, bf16[72,4608]{1,0:T(8,128)(2,1)S(1)}, u32[]{:S(2)}, u32[]{:S(2)}) %collective-permute-start.6) | collective-permute-done | bytes 663584 | tf_op jit(solution)/shard_map/ppermute | solution.py:456
  58.3 4.0 %collective-permute-done.7.refs_1_.refs_5_ = bf16[72,4608]{1,0:T(8,128)(2,1)S(1)} collective-permute-done((bf16[72,4608]{1,0:T(8,128)(2,1)}, bf16[72,4608]{1,0:T(8,128)(2,1)S(1)}, u32[]{:S(2)}, u32[]{:S(2)}) %collective-permute-start.7) | collective-permute-done | bytes 663584 | tf_op jit(solution)/shard_map/ppermute | solution.py:456
  62.4 4.3 %collective-permute-start.10 = (bf16[72,4096]{1,0:T(8,128)(2,1)}, bf16[72,4096]{1,0:T(8,128)(2,1)S(1)}, u32[]{:S(2)}, u32[]{:S(2)}) collective-permute-start(bf16[72,4096]{1,0:T(8,128)(2,1)} %refs_0_.1), channel_id=1, source_target_pairs={{0,4},{2,6},{8,0},{10,2},{16,8},{18,10},{24,16},{26,18},{28,24},{3... | collective-permute-start | bytes 1769480 | tf_op jit(solution)/shard_map/ppermute | solution.py:456
  66.8 1.8 %shard_map.108.patch_ref = bf16[128,4608]{1,0:T(8,128)(2,1)S(1)} custom-call(s32[5]{0:T(128)S(1)} %copy-done.30, bf16[64,4608]{1,0:T(8,128)(2,1)} %shard_map.107.own_ref, bf16[64,4608]{1,0:T(8,128)(2,1)} %collective-permute-done.11.mate_ref), custom_call_target="tpu_custom_call" | custom-call | tf_op jit(solution)/shard_map/pallas_call | solution.py:338
  68.6 2.3 %shard_map.109.own_ref = f32[128,360]{1,0:T(8,128)S(1)} custom-call(bf16[128,4608]{1,0:T(8,128)(2,1)S(1)} %shard_map.108.patch_ref, bf16[72,4608]{1,0:T(8,128)(2,1)S(1)} %reshape.11.refs_0_.refs_4_, bf16[72,4608]{1,0:T(8,128)(2,1)S(1)} %copy-done.10, bf16[72,4608]{1,0:T(8,128)(2,1)S(1)} %copy-done.7, ...), custom_call_target="tpu_custom_call" | custom-call | tf_op jit(solution)/shard_map/pallas_call | solution.py:598
  70.9 1.3 collective-permute-start.12
  72.2 1.9 %collective-permute-start.16 = (bf16[72,2304]{1,0:T(8,128)(2,1)S(1)}, bf16[72,2304]{1,0:T(8,128)(2,1)S(1)}, u32[]{:S(2)}, u32[]{:S(2)}) collective-permute-start(bf16[72,2304]{1,0:T(8,128)(2,1)S(1)} %slice.13), channel_id=1, source_target_pairs={{0,4},{2,6},{8,0},{10,2},{16,8},{18,10},{24,16},{26,18},{28,24},{3... | collective-permute-start | bytes 995336 | tf_op jit(solution)/shard_map/ppermute | solution.py:456
  74.1 3.5 %collective-permute-done.12.other_ref = f32[128,360]{1,0:T(8,128)S(1)} collective-permute-done((f32[128,360]{1,0:T(8,128)S(1)}, f32[128,360]{1,0:T(8,128)S(1)}, u32[]{:S(2)}, u32[]{:S(2)}) %collective-permute-start.12) | collective-permute-done | bytes 184352 | tf_op jit(solution)/shard_map/ppermute | solution.py:445
  78.3 1.8 %collective-permute-done.10.refs_2_ = bf16[72,4096]{1,0:T(8,128)(2,1)S(1)} collective-permute-done((bf16[72,4096]{1,0:T(8,128)(2,1)}, bf16[72,4096]{1,0:T(8,128)(2,1)S(1)}, u32[]{:S(2)}, u32[]{:S(2)}) %collective-permute-start.10) | collective-permute-done | bytes 589856 | tf_op jit(solution)/shard_map/ppermute | solution.py:456
  80.1 2.2 %collective-permute-done.9.refs_1_ = bf16[72,4096]{1,0:T(8,128)(2,1)S(1)} collective-permute-done((bf16[72,4096]{1,0:T(8,128)(2,1)}, bf16[72,4096]{1,0:T(8,128)(2,1)S(1)}, u32[]{:S(2)}, u32[]{:S(2)}) %collective-permute-start.9) | collective-permute-done | bytes 589856 | tf_op jit(solution)/shard_map/ppermute | solution.py:456
  82.3 1.5 collective-permute-start.14
  83.7 5.7 %collective-permute-done.15 = bf16[72,2304]{1,0:T(8,128)(2,1)S(1)} collective-permute-done((bf16[72,2304]{1,0:T(8,128)(2,1)S(1)}, bf16[72,2304]{1,0:T(8,128)(2,1)S(1)}, u32[]{:S(2)}, u32[]{:S(2)}) %collective-permute-start.15) | collective-permute-done | bytes 331808 | tf_op jit(solution)/shard_map/ppermute | solution.py:456
  90.3 1.3 collective-permute-start.17
  91.7 1.0 shard_map.111
  94.6 1.1 shard_map.112
  96.4 5.7 %collective-permute-done.13.refs_0_.refs_3_ = bf16[72,4096]{1,0:T(8,128)(2,1)} collective-permute-done((bf16[72,4096]{1,0:T(8,128)(2,1)S(1)}, bf16[72,4096]{1,0:T(8,128)(2,1)}, u32[]{:S(2)}, u32[]{:S(2)}) %collective-permute-start.13) | collective-permute-done | bytes 589856 | tf_op jit(solution)/shard_map/ppermute | solution.py:456
  102.1 1.5 collective-permute-start.19
  103.6 4.0 %all-to-all-start.1 = ((bf16[8,16,576]{2,1,0:T(8,128)(2,1)}), bf16[8,16,576]{2,1,0:T(8,128)(2,1)}, u32[]{:S(2)}, u32[]{:S(2)}) async-start(bf16[8,16,576]{2,1,0:T(8,128)(2,1)} %bitcast.14), calls=%async_computation.1 | async-start | bytes 327680 | tf_op jit(solution)/shard_map/all_to_all | solution.py:651
  107.5 1.3 collective-permute-start.20
  108.8 3.2 %collective-permute-done.20.refs_1_ = f32[128,216]{1,0:T(8,128)S(1)} collective-permute-done((f32[128,216]{1,0:T(8,128)}, f32[128,216]{1,0:T(8,128)S(1)}, u32[]{:S(2)}, u32[]{:S(2)}) %collective-permute-start.20) | collective-permute-done | bytes 110624 | tf_op jit(solution)/shard_map/ppermute | solution.py:445
  112.7 6.9 %all-to-all-done.1 = bf16[8,16,576]{2,1,0:T(8,128)(2,1)} async-done(((bf16[8,16,576]{2,1,0:T(8,128)(2,1)}), bf16[8,16,576]{2,1,0:T(8,128)(2,1)}, u32[]{:S(2)}, u32[]{:S(2)}) %all-to-all-start.1) | async-done | bytes 147488 | tf_op jit(solution)/shard_map/all_to_all | solution.py:651
  119.6 1.0 slice.14
  120.6 1.0 slice.15
  122.3 0.9 collective-permute-start.21
  123.2 1.7 %shard_map.114.refs_0_ = f32[128,144]{1,0:T(8,128)S(1)} custom-call(bf16[64,4096]{1,0:T(8,128)(2,1)S(1)} %bitcast.8, bf16[64,4096]{1,0:T(8,128)(2,1)S(1)} %copy-done.3, bf16[72,4096]{1,0:T(8,128)(2,1)} %collective-permute-done.13.refs_0_.refs_3_, bf16[72,4096]{1,0:T(8,128)(2,1)} %collective-permute-done.14.refs_1_.refs_4_), custom_call_target="tpu_custom_call" | custom-call | tf_op jit(solution)/shard_map/pallas_call | solution.py:605
  124.9 1.3 collective-permute-start.23
  126.3 1.1 shard_map.115
  127.4 1.7 %collective-permute-done.23.refs_1_ = f32[128,144]{1,0:T(8,128)S(1)} collective-permute-done((f32[128,144]{1,0:T(8,128)S(1)}, f32[128,144]{1,0:T(8,128)S(1)}, u32[]{:S(2)}, u32[]{:S(2)}) %collective-permute-start.23) | collective-permute-done | bytes 73760 | tf_op jit(solution)/shard_map/ppermute | solution.py:445
  129.1 1.8 %shard_map.116 = (f32[64,2304]{1,0:T(8,128)S(1)}, f32[64,2304]{1,0:T(8,128)S(1)}, f32[64,2304]{1,0:T(8,128)S(1)}, f32[64,2304]{1,0:T(8,128)S(1)}) custom-call(s32[5]{0:T(128)S(1)} %copy-done.30, f32[128,144]{1,0:T(8,128)S(1)} %shard_map.114.refs_0_, f32[128,144]{1,0:T(8,128)S(1)} %collective-permute-done.23.refs_1_, ...), custom_call_target="tpu_custom_call" | custom-call | tf_op jit(solution)/shard_map/pallas_call | solution.py:609
  130.9 2.0 %shard_map.117.refs_0_ = f32[128,216]{1,0:T(8,128)S(1)} custom-call(bf16[64,4096]{1,0:T(8,128)(2,1)S(1)} %bitcast.9, bf16[64,4096]{1,0:T(8,128)(2,1)S(1)} %copy-done.3, bf16[72,4096]{1,0:T(8,128)(2,1)} %collective-permute-done.18.refs_0_.refs_5_, bf16[72,4096]{1,0:T(8,128)(2,1)} %collective-permute-done.19.refs_1_.refs_6_, ...), custom_call_target="tpu_custom_call" | custom-call | tf_op jit(solution)/shard_map/pallas_call | solution.py:605
  132.9 1.3 collective-permute-start.24
  134.2 2.6 %collective-permute-done.24.refs_1_ = f32[128,216]{1,0:T(8,128)S(1)} collective-permute-done((f32[128,216]{1,0:T(8,128)S(1)}, f32[128,216]{1,0:T(8,128)S(1)}, u32[]{:S(2)}, u32[]{:S(2)}) %collective-permute-start.24) | collective-permute-done | bytes 110624 | tf_op jit(solution)/shard_map/ppermute | solution.py:445
  136.8 1.0 shard_map.118
  137.8 5.6 %collective-permute-start.25 = (bf16[64,2304]{1,0:T(8,128)(2,1)S(1)}, bf16[64,2304]{1,0:T(8,128)(2,1)S(1)}, u32[]{:S(2)}, u32[]{:S(2)}) collective-permute-start(bf16[64,2304]{1,0:T(8,128)(2,1)S(1)} %get-tuple-element.119), channel_id=1, source_target_pairs={{0,2},{2,0},{4,6},{6,4},{8,10},{10,8},{12,14},{14,12},{16,18},{18,... | collective-permute-start | bytes 884744 | tf_op jit(solution)/shard_map/ppermute | solution.py:437
  143.4 1.0 shard_map.120
  144.7 1.3 shard_map.119
  146.0 2.3 %collective-permute-start.28 = (bf16[256,576]{1,0:T(8,128)(2,1)S(1)}, bf16[256,576]{1,0:T(8,128)(2,1)S(1)}, u32[]{:S(2)}, u32[]{:S(2)}) collective-permute-start(bf16[256,576]{1,0:T(8,128)(2,1)S(1)} %get-tuple-element.131), channel_id=1, source_target_pairs={{2,0},{4,2},{6,4},{8,6},{10,8},{12,10},{14,12},{16,14},{18,16},{20... | collective-permute-start | bytes 884744 | tf_op jit(solution)/shard_map/ppermute | solution.py:420
  148.3 1.2 shard_map.121
  149.6 4.1 %shard_map.122 = (f32[64,4096]{1,0:T(8,128)S(1)}, bf16[64,4096]{1,0:T(8,128)(2,1)S(1)}) custom-call(s32[5]{0:T(128)S(1)} %get-tuple-element.126.facts_ref, bf16[128,576]{1,0:T(8,128)(2,1)} %bitcast.5.act_ref, bf16[72,4096]{1,0:T(8,128)(2,1)S(1)} %copy-done.13, bf16[72,4096]{1,0:T(8,128)(2,1)S(1)} %copy-done.17, bf16[72,4096]{1,0:T(8,128)(2,1)S(1)} %copy-done.15, ...), custom_call_target="tpu_custom_call" | custom-call | tf_op jit(solution)/shard_map/pallas_call | solution.py:637
  154.3 1.0 collective-permute-done.28.odd_ref
  155.3 0.9 shard_map.123
  156.2 1.3 collective-permute-start.29
  157.5 1.7 %shard_map.124 = (bf16[2304,256]{1,0:T(8,128)(2,1)S(1)}, bf16[2304,256]{1,0:T(8,128)(2,1)S(1)}, bf16[2304,256]{1,0:T(8,128)(2,1)S(1)}) custom-call(s32[5]{0:T(128)S(1)} %get-tuple-element.126.facts_ref, bf16[9,48,576]{2,1,0:T(8,128)(2,1)S(1)} %bitcast.11), custom_call_target="tpu_custom_call" | custom-call | tf_op jit(solution)/shard_map/pallas_call | solution.py:609
  159.2 2.8 %shard_map.125 = bf16[2,196,576]{2,1,0:T(8,128)(2,1)S(1)} custom-call(f32[256,576]{1,0:T(8,128)S(1)} %get-tuple-element.130.even_ref, bf16[256,576]{1,0:T(8,128)(2,1)S(1)} %collective-permute-done.28.odd_ref, f32[512,576]{1,0:T(8,128)S(1)} %copy-done.1, f32[2,576]{1,0:T(2,128)S(1)} %get-tuple-element.132.excite_ref, f32[2,288]{1,0:T(2,128)S(1)} %add.9.sq_ref, ...), custom_call_target="tpu_custom_call" | custom-call | flops 2717908992 | bytes 4718592 | tf_op jit(solution)/shard_map/pallas_call | solution.py:385
  162.0 1.2 copy.12
  163.2 0.9 add_convert_fusion
  (96 shorter events, 7.6 us)
Async XLA Ops:
  0.6 4.4 %copy-start.24 = (bf16[576,288]{0,1:T(8,128)(2,1)S(1)}, bf16[576,288]{0,1:T(8,128)(2,1)}, u32[]{:S(2)}) copy-start(bf16[576,288]{0,1:T(8,128)(2,1)} %param.11) | copy-start | bytes 995332
  0.6 4.4 %copy-start.18 = (bf16[9,576,48]{1,2,0:T(8,128)(2,1)S(1)}, bf16[9,576,48]{1,2,0:T(8,128)(2,1)}, u32[]{:S(2)}) copy-start(bf16[9,576,48]{1,2,0:T(8,128)(2,1)} %param.10) | copy-start | bytes 1492996
  2.4 9.9 %copy-start.20 = (bf16[288,576]{1,0:T(8,128)(2,1)S(1)}, bf16[288,576]{1,0:T(8,128)(2,1)}, u32[]{:S(2)}) copy-start(bf16[288,576]{1,0:T(8,128)(2,1)} %expand_ref.3) | copy-start | bytes 995332
  2.4 15.8 %collective-permute-start.3 = (bf16[72,4608]{1,0:T(8,128)(2,1)S(1)}, bf16[72,4608]{1,0:T(8,128)(2,1)S(1)}, u32[]{:S(2)}, u32[]{:S(2)}) collective-permute-start(bf16[72,4608]{1,0:T(8,128)(2,1)S(1)} %reshape.11.refs_0_.refs_4_), channel_id=1, source_target_pairs={{0,4},{2,6},{8,0},{10,2},{16,8},{18,10},{24,16},{26,18},{28,24},{3... | collective-permute-start | bytes 1990664 | tf_op jit(solution)/shard_map/ppermute | solution.py:456
  3.8 15.5 %collective-permute-start.2 = (bf16[72,4608]{1,0:T(8,128)(2,1)S(1)}, bf16[72,4608]{1,0:T(8,128)(2,1)S(1)}, u32[]{:S(2)}, u32[]{:S(2)}) collective-permute-start(bf16[72,4608]{1,0:T(8,128)(2,1)S(1)} %reshape.11.refs_0_.refs_4_), channel_id=1, source_target_pairs={{0,8},{2,10},{8,16},{10,18},{16,24},{18,26},{24,28},{26,30},{28,20... | collective-permute-start | bytes 1990664 | tf_op jit(solution)/shard_map/ppermute | solution.py:456
  9.5 9.7 %copy-start = (f32[512,576]{1,0:T(8,128)}, f32[512,576]{1,0:T(8,128)S(1)}, u32[]{:S(2)}) copy-start(f32[512,576]{1,0:T(8,128)S(1)} %get-tuple-element.69.conv_ref) | copy-start | bytes 3538948
  9.5 2.8 %collective-permute-start = (f32[2,288]{1,0:T(2,128)S(1)}, f32[2,288]{1,0:T(2,128)S(1)}, u32[]{:S(2)}, u32[]{:S(2)}) collective-permute-start(f32[2,288]{1,0:T(2,128)S(1)} %get-tuple-element.72), channel_id=1, source_target_pairs={{0,1},{1,0},{2,3},{3,2},{4,5},{5,4},{6,7},{7,6},{8,9},{9,8},{10,11... | collective-permute-start | bytes 6920 | tf_op jit(solution)/shard_map/ppermute | solution.py:445
  18.2 22.5 %copy-start.6 = (bf16[72,4608]{1,0:T(8,128)(2,1)}, bf16[72,4608]{1,0:T(8,128)(2,1)S(1)}, u32[]{:S(2)}) copy-start(bf16[72,4608]{1,0:T(8,128)(2,1)S(1)} %collective-permute-done.3.refs_2_.refs_6_) | copy-start | bytes 1990660
  19.2 21.5 %collective-permute-start.4 = (bf16[72,4608]{1,0:T(8,128)(2,1)S(1)}, bf16[72,4608]{1,0:T(8,128)(2,1)S(1)}, u32[]{:S(2)}, u32[]{:S(2)}) collective-permute-start(bf16[72,4608]{1,0:T(8,128)(2,1)S(1)} %collective-permute-done.2.refs_1_.refs_5_), channel_id=1, source_target_pairs={{0,8},{2,10},{8,16},{10,18},{16,24},{18,26},{24,28},{26,30},{28,20... | collective-permute-start | bytes 1990664 | tf_op jit(solution)/shard_map/ppermute | solution.py:456
  19.4 0.8 copy-start.9
  20.2 20.5 %collective-permute-start.5 = (bf16[72,4608]{1,0:T(8,128)(2,1)S(1)}, bf16[72,4608]{1,0:T(8,128)(2,1)}, u32[]{:S(2)}, u32[]{:S(2)}) collective-permute-start(bf16[72,4608]{1,0:T(8,128)(2,1)S(1)} %collective-permute-done.3.refs_2_.refs_6_), channel_id=1, source_target_pairs={{0,4},{2,6},{8,0},{10,2},{16,8},{18,10},{24,16},{26,18},{28,24},{3... | collective-permute-start | bytes 1990664 | tf_op jit(solution)/shard_map/ppermute | solution.py:456
  21.5 19.2 %collective-permute-start.1 = (bf16[256,576]{1,0:T(8,128)(2,1)}, bf16[256,576]{1,0:T(8,128)(2,1)}, u32[]{:S(2)}, u32[]{:S(2)}) collective-permute-start(bf16[256,576]{1,0:T(8,128)(2,1)} %get-tuple-element.73), channel_id=1, source_target_pairs={{0,2},{2,4},{4,6},{6,8},{8,10},{10,12},{12,14},{14,16},{16,18},{18... | collective-permute-start | bytes 884744 | tf_op jit(solution)/shard_map/ppermute | solution.py:420
  25.8 25.9 %all-to-all-start = ((bf16[8,8,4096]{2,1,0:T(8,128)(2,1)}), bf16[8,8,4096]{2,1,0:T(8,128)(2,1)S(1)}, u32[]{:S(2)}, u32[]{:S(2)}) async-start(bf16[8,8,4096]{2,1,0:T(8,128)(2,1)} %bitcast.15), calls=%async_computation | async-start | bytes 1048576 | tf_op jit(solution)/shard_map/all_to_all | solution.py:651
  40.7 27.9 %copy-start.4 = (bf16[72,4608]{1,0:T(8,128)(2,1)}, bf16[72,4608]{1,0:T(8,128)(2,1)S(1)}, u32[]{:S(2)}) copy-start(bf16[72,4608]{1,0:T(8,128)(2,1)S(1)} %collective-permute-done.4.refs_3_.refs_4_) | copy-start | bytes 1990660
  40.7 17.6 %collective-permute-start.6 = (bf16[72,4608]{1,0:T(8,128)(2,1)S(1)}, bf16[72,4608]{1,0:T(8,128)(2,1)S(1)}, u32[]{:S(2)}, u32[]{:S(2)}) collective-permute-start(bf16[72,4608]{1,0:T(8,128)(2,1)S(1)} %collective-permute-done.4.refs_3_.refs_4_), channel_id=1, source_target_pairs={{0,8},{2,10},{8,16},{10,18},{16,24},{18,26},{24,28},{26,30},{28,20... | collective-permute-start | bytes 1990664 | tf_op jit(solution)/shard_map/ppermute | solution.py:456
  44.2 18.1 %collective-permute-start.7 = (bf16[72,4608]{1,0:T(8,128)(2,1)}, bf16[72,4608]{1,0:T(8,128)(2,1)S(1)}, u32[]{:S(2)}, u32[]{:S(2)}) collective-permute-start(bf16[72,4608]{1,0:T(8,128)(2,1)} %collective-permute-done.5.refs_4_.refs_5_), channel_id=1, source_target_pairs={{0,4},{2,6},{8,0},{10,2},{16,8},{18,10},{24,16},{26,18},{28,24},{3... | collective-permute-start | bytes 1990664 | tf_op jit(solution)/shard_map/ppermute | solution.py:456
  45.8 0.7 copy-start.29
  46.4 20.3 %copy-start.30 = (s32[5]{0:T(128)S(1)}, s32[5]{0:T(128)}, u32[]{:S(2)}) copy-start(s32[5]{0:T(128)} %shard_map.104.facts_ref) | copy-start | bytes 64
  48.7 18.0 %collective-permute-start.11 = (bf16[64,4608]{1,0:T(8,128)(2,1)}, bf16[64,4608]{1,0:T(8,128)(2,1)}, u32[]{:S(2)}, u32[]{:S(2)}) collective-permute-start(bf16[64,4608]{1,0:T(8,128)(2,1)} %shard_map.107.own_ref), channel_id=1, source_target_pairs={{0,2},{2,0},{4,6},{6,4},{8,10},{10,8},{12,14},{14,12},{16,18},{18,... | collective-permute-start | bytes 1769480 | tf_op jit(solution)/shard_map/ppermute | solution.py:437
  62.4 17.7 %collective-permute-start.10 = (bf16[72,4096]{1,0:T(8,128)(2,1)}, bf16[72,4096]{1,0:T(8,128)(2,1)S(1)}, u32[]{:S(2)}, u32[]{:S(2)}) collective-permute-start(bf16[72,4096]{1,0:T(8,128)(2,1)} %refs_0_.1), channel_id=1, source_target_pairs={{0,4},{2,6},{8,0},{10,2},{16,8},{18,10},{24,16},{26,18},{28,24},{3... | collective-permute-start | bytes 1769480 | tf_op jit(solution)/shard_map/ppermute | solution.py:456
  66.6 15.6 %collective-permute-start.9 = (bf16[72,4096]{1,0:T(8,128)(2,1)}, bf16[72,4096]{1,0:T(8,128)(2,1)S(1)}, u32[]{:S(2)}, u32[]{:S(2)}) collective-permute-start(bf16[72,4096]{1,0:T(8,128)(2,1)} %refs_0_.1), channel_id=1, source_target_pairs={{0,8},{2,10},{8,16},{10,18},{16,24},{18,26},{24,28},{26,30},{28,20... | collective-permute-start | bytes 1769480 | tf_op jit(solution)/shard_map/ppermute | solution.py:456
  66.7 1.9 %copy-start.7 = (bf16[72,4608]{1,0:T(8,128)(2,1)S(1)}, bf16[72,4608]{1,0:T(8,128)(2,1)}, u32[]{:S(2)}) copy-start(bf16[72,4608]{1,0:T(8,128)(2,1)} %copy-done.6) | copy-start | bytes 1990660
  66.7 1.9 %copy-start.10 = (bf16[72,4608]{1,0:T(8,128)(2,1)S(1)}, bf16[72,4608]{1,0:T(8,128)(2,1)}, u32[]{:S(2)}) copy-start(bf16[72,4608]{1,0:T(8,128)(2,1)} %copy-done.9) | copy-start | bytes 1990660
  66.7 22.8 %collective-permute-start.15 = (bf16[72,2304]{1,0:T(8,128)(2,1)S(1)}, bf16[72,2304]{1,0:T(8,128)(2,1)S(1)}, u32[]{:S(2)}, u32[]{:S(2)}) collective-permute-start(bf16[72,2304]{1,0:T(8,128)(2,1)S(1)} %slice.12), channel_id=1, source_target_pairs={{0,8},{2,10},{8,16},{10,18},{16,24},{18,26},{24,28},{26,30},{28,20... | collective-permute-start | bytes 995336 | tf_op jit(solution)/shard_map/ppermute | solution.py:456
  70.9 6.7 %collective-permute-start.12 = (f32[128,360]{1,0:T(8,128)S(1)}, f32[128,360]{1,0:T(8,128)S(1)}, u32[]{:S(2)}, u32[]{:S(2)}) collective-permute-start(f32[128,360]{1,0:T(8,128)S(1)} %shard_map.109.own_ref), channel_id=1, source_target_pairs={{0,1},{1,0},{2,3},{3,2},{4,5},{5,4},{6,7},{7,6},{8,9},{9,8},{10,11... | collective-permute-start | bytes 552968 | tf_op jit(solution)/shard_map/ppermute | solution.py:445
  72.2 17.3 %collective-permute-start.16 = (bf16[72,2304]{1,0:T(8,128)(2,1)S(1)}, bf16[72,2304]{1,0:T(8,128)(2,1)S(1)}, u32[]{:S(2)}, u32[]{:S(2)}) collective-permute-start(bf16[72,2304]{1,0:T(8,128)(2,1)S(1)} %slice.13), channel_id=1, source_target_pairs={{0,4},{2,6},{8,0},{10,2},{16,8},{18,10},{24,16},{26,18},{28,24},{3... | collective-permute-start | bytes 995336 | tf_op jit(solution)/shard_map/ppermute | solution.py:456
  77.6 15.1 %collective-permute-start.8 = (bf16[64,4096]{1,0:T(8,128)(2,1)S(1)}, bf16[64,4096]{1,0:T(8,128)(2,1)S(1)}, u32[]{:S(2)}, u32[]{:S(2)}) collective-permute-start(bf16[64,4096]{1,0:T(8,128)(2,1)S(1)} %bitcast.6), channel_id=1, source_target_pairs={{0,2},{2,0},{4,6},{6,4},{8,10},{10,8},{12,14},{14,12},{16,18},{18,... | collective-permute-start | bytes 1572872 | tf_op jit(solution)/shard_map/ppermute | solution.py:437
  80.1 12.6 %copy-start.14 = (bf16[72,4096]{1,0:T(8,128)(2,1)}, bf16[72,4096]{1,0:T(8,128)(2,1)S(1)}, u32[]{:S(2)}) copy-start(bf16[72,4096]{1,0:T(8,128)(2,1)S(1)} %collective-permute-done.10.refs_2_) | copy-start | bytes 1769476
  82.3 10.5 %copy-start.16 = (bf16[72,4096]{1,0:T(8,128)(2,1)}, bf16[72,4096]{1,0:T(8,128)(2,1)S(1)}, u32[]{:S(2)}) copy-start(bf16[72,4096]{1,0:T(8,128)(2,1)S(1)} %collective-permute-done.9.refs_1_) | copy-start | bytes 1769476
  82.3 19.9 %collective-permute-start.13 = (bf16[72,4096]{1,0:T(8,128)(2,1)S(1)}, bf16[72,4096]{1,0:T(8,128)(2,1)}, u32[]{:S(2)}, u32[]{:S(2)}) collective-permute-start(bf16[72,4096]{1,0:T(8,128)(2,1)S(1)} %collective-permute-done.9.refs_1_), channel_id=1, source_target_pairs={{0,8},{2,10},{8,16},{10,18},{16,24},{18,26},{24,28},{26,30},{28,20... | collective-permute-start | bytes 1769480 | tf_op jit(solution)/shard_map/ppermute | solution.py:456
  82.3 19.9 %collective-permute-start.14 = (bf16[72,4096]{1,0:T(8,128)(2,1)S(1)}, bf16[72,4096]{1,0:T(8,128)(2,1)}, u32[]{:S(2)}, u32[]{:S(2)}) collective-permute-start(bf16[72,4096]{1,0:T(8,128)(2,1)S(1)} %collective-permute-done.10.refs_2_), channel_id=1, source_target_pairs={{0,4},{2,6},{8,0},{10,2},{16,8},{18,10},{24,16},{26,18},{28,24},{3... | collective-permute-start | bytes 1769480 | tf_op jit(solution)/shard_map/ppermute | solution.py:456
  89.5 3.2 %copy-start.12 = (bf16[72,4096]{1,0:T(8,128)(2,1)S(1)}, bf16[72,4096]{1,0:T(8,128)(2,1)}, u32[]{:S(2)}) copy-start(bf16[72,4096]{1,0:T(8,128)(2,1)} %refs_0_.1) | copy-start | bytes 1769476
  90.3 4.3 %collective-permute-start.17 = (f32[128,216]{1,0:T(8,128)S(1)}, f32[128,216]{1,0:T(8,128)S(1)}, u32[]{:S(2)}, u32[]{:S(2)}) collective-permute-start(f32[128,216]{1,0:T(8,128)S(1)} %shard_map.110.own_ref), channel_id=1, source_target_pairs={{0,1},{1,0},{2,3},{3,2},{4,5},{5,4},{6,7},{7,6},{8,9},{9,8},{10,11... | collective-permute-start | bytes 331784 | tf_op jit(solution)/shard_map/ppermute | solution.py:445
  92.7 0.8 copy-start.2
  93.5 0.6 copy-start.22
  95.7 0.7 copy-start.26
  102.1 17.5 %collective-permute-start.18 = (bf16[72,4096]{1,0:T(8,128)(2,1)}, bf16[72,4096]{1,0:T(8,128)(2,1)}, u32[]{:S(2)}, u32[]{:S(2)}) collective-permute-start(bf16[72,4096]{1,0:T(8,128)(2,1)} %collective-permute-done.13.refs_0_.refs_3_), channel_id=1, source_target_pairs={{0,8},{2,10},{8,16},{10,18},{16,24},{18,26},{24,28},{26,30},{28,20... | collective-permute-start | bytes 1769480 | tf_op jit(solution)/shard_map/ppermute | solution.py:456
  102.1 17.5 %collective-permute-start.19 = (bf16[72,4096]{1,0:T(8,128)(2,1)}, bf16[72,4096]{1,0:T(8,128)(2,1)}, u32[]{:S(2)}, u32[]{:S(2)}) collective-permute-start(bf16[72,4096]{1,0:T(8,128)(2,1)} %collective-permute-done.14.refs_1_.refs_4_), channel_id=1, source_target_pairs={{0,4},{2,6},{8,0},{10,2},{16,8},{18,10},{24,16},{26,18},{28,24},{3... | collective-permute-start | bytes 1769480 | tf_op jit(solution)/shard_map/ppermute | solution.py:456
  103.6 16.0 %all-to-all-start.1 = ((bf16[8,16,576]{2,1,0:T(8,128)(2,1)}), bf16[8,16,576]{2,1,0:T(8,128)(2,1)}, u32[]{:S(2)}, u32[]{:S(2)}) async-start(bf16[8,16,576]{2,1,0:T(8,128)(2,1)} %bitcast.14), calls=%async_computation.1 | async-start | bytes 327680 | tf_op jit(solution)/shard_map/all_to_all | solution.py:651
  107.5 4.5 %collective-permute-start.20 = (f32[128,216]{1,0:T(8,128)}, f32[128,216]{1,0:T(8,128)S(1)}, u32[]{:S(2)}, u32[]{:S(2)}) collective-permute-start(f32[128,216]{1,0:T(8,128)} %copy-done.22), channel_id=1, source_target_pairs={{0,1},{1,0},{2,3},{3,2},{4,5},{5,4},{6,7},{7,6},{8,9},{9,8},{10,11... | collective-permute-start | bytes 331784 | tf_op jit(solution)/shard_map/ppermute | solution.py:445
  112.0 0.7 copy-start.27
  119.6 3.6 %copy-start.3 = (bf16[64,4096]{1,0:T(8,128)(2,1)S(1)}, bf16[64,4096]{1,0:T(8,128)(2,1)}, u32[]{:S(2)}) copy-start(bf16[64,4096]{1,0:T(8,128)(2,1)} %copy-done.2) | copy-start | bytes 1572868
  121.6 4.6 %copy-start.8 = (bf16[72,4608]{1,0:T(8,128)(2,1)S(1)}, bf16[72,4608]{1,0:T(8,128)(2,1)}, u32[]{:S(2)}) copy-start(bf16[72,4608]{1,0:T(8,128)(2,1)} %copy-done.6) | copy-start | bytes 1990660
  121.6 4.6 %copy-start.11 = (bf16[72,4608]{1,0:T(8,128)(2,1)S(1)}, bf16[72,4608]{1,0:T(8,128)(2,1)}, u32[]{:S(2)}) copy-start(bf16[72,4608]{1,0:T(8,128)(2,1)} %copy-done.9) | copy-start | bytes 1990660
  121.7 4.6 %copy-start.23 = (f32[128,216]{1,0:T(8,128)S(1)}, f32[128,216]{1,0:T(8,128)}, u32[]{:S(2)}) copy-start(f32[128,216]{1,0:T(8,128)} %copy-done.22) | copy-start | bytes 331780
  121.7 4.6 %copy-start.28 = (f32[128,216]{1,0:T(8,128)S(1)}, f32[128,216]{1,0:T(8,128)}, u32[]{:S(2)}) copy-start(f32[128,216]{1,0:T(8,128)} %copy-done.27) | copy-start | bytes 331780
  121.7 9.2 %collective-permute-start.22 = (bf16[72,2048]{1,0:T(8,128)(2,1)S(1)}, bf16[72,2048]{1,0:T(8,128)(2,1)S(1)}, u32[]{:S(2)}, u32[]{:S(2)}) collective-permute-start(bf16[72,2048]{1,0:T(8,128)(2,1)S(1)} %slice.15), channel_id=1, source_target_pairs={{0,4},{2,6},{8,0},{10,2},{16,8},{18,10},{24,16},{26,18},{28,24},{3... | collective-permute-start | bytes 884744 | tf_op jit(solution)/shard_map/ppermute | solution.py:456
  122.3 8.6 %collective-permute-start.21 = (bf16[72,2048]{1,0:T(8,128)(2,1)S(1)}, bf16[72,2048]{1,0:T(8,128)(2,1)S(1)}, u32[]{:S(2)}, u32[]{:S(2)}) collective-permute-start(bf16[72,2048]{1,0:T(8,128)(2,1)S(1)} %slice.14), channel_id=1, source_target_pairs={{0,8},{2,10},{8,16},{10,18},{16,24},{18,26},{24,28},{26,30},{28,20... | collective-permute-start | bytes 884744 | tf_op jit(solution)/shard_map/ppermute | solution.py:456
  124.9 4.2 %collective-permute-start.23 = (f32[128,144]{1,0:T(8,128)S(1)}, f32[128,144]{1,0:T(8,128)S(1)}, u32[]{:S(2)}, u32[]{:S(2)}) collective-permute-start(f32[128,144]{1,0:T(8,128)S(1)} %shard_map.114.refs_0_), channel_id=1, source_target_pairs={{0,1},{1,0},{2,3},{3,2},{4,5},{5,4},{6,7},{7,6},{8,9},{9,8},{10,11... | collective-permute-start | bytes 221192 | tf_op jit(solution)/shard_map/ppermute | solution.py:445
  126.2 2.9 %copy-start.5 = (bf16[72,4608]{1,0:T(8,128)(2,1)S(1)}, bf16[72,4608]{1,0:T(8,128)(2,1)}, u32[]{:S(2)}) copy-start(bf16[72,4608]{1,0:T(8,128)(2,1)} %copy-done.4) | copy-start | bytes 1990660
  132.9 3.9 %collective-permute-start.24 = (f32[128,216]{1,0:T(8,128)S(1)}, f32[128,216]{1,0:T(8,128)S(1)}, u32[]{:S(2)}, u32[]{:S(2)}) collective-permute-start(f32[128,216]{1,0:T(8,128)S(1)} %shard_map.117.refs_0_), channel_id=1, source_target_pairs={{0,1},{1,0},{2,3},{3,2},{4,5},{5,4},{6,7},{7,6},{8,9},{9,8},{10,11... | collective-permute-start | bytes 331784 | tf_op jit(solution)/shard_map/ppermute | solution.py:445
  137.8 6.9 %collective-permute-start.25 = (bf16[64,2304]{1,0:T(8,128)(2,1)S(1)}, bf16[64,2304]{1,0:T(8,128)(2,1)S(1)}, u32[]{:S(2)}, u32[]{:S(2)}) collective-permute-start(bf16[64,2304]{1,0:T(8,128)(2,1)S(1)} %get-tuple-element.119), channel_id=1, source_target_pairs={{0,2},{2,0},{4,6},{6,4},{8,10},{10,8},{12,14},{14,12},{16,18},{18,... | collective-permute-start | bytes 884744 | tf_op jit(solution)/shard_map/ppermute | solution.py:437
  144.4 5.1 %copy-start.13 = (bf16[72,4096]{1,0:T(8,128)(2,1)S(1)}, bf16[72,4096]{1,0:T(8,128)(2,1)}, u32[]{:S(2)}) copy-start(bf16[72,4096]{1,0:T(8,128)(2,1)} %refs_0_.1) | copy-start | bytes 1769476
  144.5 5.1 %copy-start.15 = (bf16[72,4096]{1,0:T(8,128)(2,1)S(1)}, bf16[72,4096]{1,0:T(8,128)(2,1)}, u32[]{:S(2)}) copy-start(bf16[72,4096]{1,0:T(8,128)(2,1)} %copy-done.14) | copy-start | bytes 1769476
  144.5 5.1 %copy-start.17 = (bf16[72,4096]{1,0:T(8,128)(2,1)S(1)}, bf16[72,4096]{1,0:T(8,128)(2,1)}, u32[]{:S(2)}) copy-start(bf16[72,4096]{1,0:T(8,128)(2,1)} %copy-done.16) | copy-start | bytes 1769476
  144.5 3.8 %collective-permute-start.26 = (bf16[64,2304]{1,0:T(8,128)(2,1)S(1)}, bf16[64,2304]{1,0:T(8,128)(2,1)S(1)}, u32[]{:S(2)}, u32[]{:S(2)}) collective-permute-start(bf16[64,2304]{1,0:T(8,128)(2,1)S(1)} %get-tuple-element.125), channel_id=1, source_target_pairs={{0,2},{2,0},{4,6},{6,4},{8,10},{10,8},{12,14},{14,12},{16,18},{18,... | collective-permute-start | bytes 884744 | tf_op jit(solution)/shard_map/ppermute | solution.py:437
  146.0 9.3 %collective-permute-start.28 = (bf16[256,576]{1,0:T(8,128)(2,1)S(1)}, bf16[256,576]{1,0:T(8,128)(2,1)S(1)}, u32[]{:S(2)}, u32[]{:S(2)}) collective-permute-start(bf16[256,576]{1,0:T(8,128)(2,1)S(1)} %get-tuple-element.131), channel_id=1, source_target_pairs={{2,0},{4,2},{6,4},{8,6},{10,8},{12,10},{14,12},{16,14},{18,16},{20... | collective-permute-start | bytes 884744 | tf_op jit(solution)/shard_map/ppermute | solution.py:420
  149.6 5.7 %copy-start.1 = (f32[512,576]{1,0:T(8,128)S(1)}, f32[512,576]{1,0:T(8,128)}, u32[]{:S(2)}) copy-start(f32[512,576]{1,0:T(8,128)} %copy-done) | copy-start | bytes 3538948
  149.6 5.7 %copy-start.21 = (bf16[288,576]{1,0:T(8,128)(2,1)S(1)}, bf16[288,576]{1,0:T(8,128)(2,1)}, u32[]{:S(2)}) copy-start(bf16[288,576]{1,0:T(8,128)(2,1)} %expand_ref.3) | copy-start | bytes 995332
  153.8 9.4 %collective-permute-start.27 = (bf16[64,4096]{1,0:T(8,128)(2,1)S(1)}, bf16[64,4096]{1,0:T(8,128)(2,1)S(1)}, u32[]{:S(2)}, u32[]{:S(2)}) collective-permute-start(bf16[64,4096]{1,0:T(8,128)(2,1)S(1)} %get-tuple-element.129), channel_id=1, source_target_pairs={{0,2},{2,0},{4,6},{6,4},{8,10},{10,8},{12,14},{14,12},{16,18},{18,... | collective-permute-start | bytes 1572872 | tf_op jit(solution)/shard_map/ppermute | solution.py:437
  155.3 2.2 %copy-start.19 = (bf16[9,576,48]{1,2,0:T(8,128)(2,1)S(1)}, bf16[9,576,48]{1,2,0:T(8,128)(2,1)}, u32[]{:S(2)}) copy-start(bf16[9,576,48]{1,2,0:T(8,128)(2,1)} %param.10) | copy-start | bytes 1492996
  155.3 3.9 %copy-start.25 = (bf16[576,288]{0,1:T(8,128)(2,1)S(1)}, bf16[576,288]{0,1:T(8,128)(2,1)}, u32[]{:S(2)}) copy-start(bf16[576,288]{0,1:T(8,128)(2,1)} %param.11) | copy-start | bytes 995332
  156.2 2.9 %collective-permute-start.29 = (f32[2,288]{1,0:T(2,128)S(1)}, f32[2,288]{1,0:T(2,128)S(1)}, u32[]{:S(2)}, u32[]{:S(2)}) collective-permute-start(f32[2,288]{1,0:T(2,128)S(1)} %shard_map.123), channel_id=1, source_target_pairs={{0,1},{1,0},{2,3},{3,2},{4,5},{5,4},{6,7},{7,6},{8,9},{9,8},{10,11... | collective-permute-start | bytes 6920 | tf_op jit(solution)/shard_map/ppermute | solution.py:445

commit v15 on v12

--- a/solution.py
+++ b/solution.py
@@ -664,8 +664,6 @@
     facts = facts_of(frame_clip, clip_keep)
 
     conv, padded, squeezed = conv_forward(features, group_kernel, squeeze_in)
-    token_cotangent, squeezed = tie(token_cotangent, squeezed)
-    back = chips_exchange(token_cotangent)
     squeezed = sum_tp(squeezed)
     even, odd, excite = hidden_frames(conv, padded, squeezed, squeeze_out)
     halo = shifted(odd, "ctx", 1)
@@ -680,7 +678,9 @@
             r_down = [readout_kernel, ring_send(readout_kernel, -1)]
             patches = take_patches(facts, halo, even)
             patches = order_rows(facts, patches, swap_cores(patches), unit)
-    s_up[-1], s_down[-1], back, readout_kernel = tie(s_up[-1], s_down[-1], back, readout_kernel)
+    held = tie(s_up[-1], s_down[-1], token_cotangent, readout_kernel)
+    s_up[-1], s_down[-1], token_cotangent, readout_kernel = held
+    back = chips_exchange(token_cotangent)
     back = (back, swap_cores(back))
     s_last = ring_send(s_up[-1], 1)
     r_up = [readout_kernel, ring_send(readout_kernel, 1)]
@@ -689,20 +689,20 @@
     count = 2 * steps - 3
     first_pre = tp_terms(block_products(pre_kernel, (patches,), samplers[:count]))
     r_down[1], s_last, *first_pre = tie(r_down[1], s_last, *first_pre)
-    for step in range(1, steps - 2):
-        r_down.append(ring_send(r_down[-1], -1))
-        r_up.append(ring_send(r_up[-1], 1))
     first_slope, first_act = act_and_slope(facts, first_pre, offsets[:count], chips, (), unit)
     last_pre = block_products(pre_kernel, (patches,), [*samplers[count:], s_last])
     last_slope, act = act_and_slope(
         facts, tp_terms(last_pre), offsets[count:], chips, (first_act,), unit
     )
     slopes = first_slope, last_slope
-    r_down[-1], act = tie(r_down[-1], act)
+    r_up[1], act = tie(r_up[1], chips_exchange(act))
+    for step in range(1, steps - 2):
+        r_down.append(ring_send(r_down[-1], -1))
+        r_up.append(ring_send(r_up[-1], 1))
     r_down.append(ring_send(r_down[-1], -1))
     early = r_down[: steps - 1]
     sums = block_products(back_kernel, back, early)
-    r_up[-1], act, *terms = tie(r_up[-1], chips_exchange(act), *tp_terms(sums))
+    r_up[-1], *terms = tie(r_up[-1], *tp_terms(sums))
     r_up.append(ring_send(r_up[-1], 1))
     halo_lanes, even_lanes = slice(0, 4 * chans), slice(4 * chans, 8 * chans)
     both = halo_lanes, even_lanes

time: 160 us -> 154 us (0.963)
  local copies, waits for them, and re-layouts: 9.65 us -> 5.41 us
  waiting for transfers between devices: 51.8 us -> 49.4 us
  starting transfers between devices: 55.5 us -> 57.5 us
    ppermute x14, waiting for transfers between devices: 34.8 us -> 23.7 us  [ring_send(): return lax.ppermute(value, 'ctx', ring_pairs(lax.axis_size('ctx'), by))]
    ppermute x5, starting transfers between devices: 9.55 us -> 19.7 us  [swap_cores(): lax.ppermute(value, 'ctx', [(i, i ^ 1) for i in range(lax.axis_size('ctx'...]
    ppermute x14, starting transfers between devices: 18.3 us -> 10.1 us  [ring_send(): return lax.ppermute(value, 'ctx', ring_pairs(lax.axis_size('ctx'), by))]
    unnamed x60 -> x40, local copies, waits for them, and re-layouts: 7.95 us -> 3.65 us
    ppermute x2, waiting for transfers between devices: 8.57 us -> 12.8 us  [shifted(): return lax.ppermute(value, axis, pairs)]
    ppermute x7, waiting for transfers between devices: 7.4 us -> 11.1 us  [tp_terms(): other = lax.ppermute(value, 'tp', [(i, i ^ reach) for i in range(size)])]
  transfers between devices with their start and end apart: 30 -> 30, of which waited for: 18 -> 17; matrix products, arithmetic and copies ran while one was open for 1% -> 1% of each run, Pallas kernels for 24% -> 24%
where the time goes in v15:
time: 154 us; the launch traced here: 153 us
  starting transfers between devices  57.5 us (37%)
  waiting for transfers between devices  49.4 us (32%)
  Pallas kernels  38.5 us (25%)
  local copies, waits for them, and re-layouts  5.41 us (4%)
    ppermute x14, waiting for transfers between devices, ring_send(): return lax.ppermute(value, 'ctx', ring_pairs(lax.axis_size('ctx'), by))  23.7 us
    ppermute x5, starting transfers between devices, swap_cores(): lax.ppermute(value, 'ctx', [(i, i ^ 1) for i in range(lax.axis_size('ctx'...  19.7 us
    ppermute x2, waiting for transfers between devices, shifted(): return lax.ppermute(value, axis, pairs)  12.8 us
    ppermute x7, waiting for transfers between devices, tp_terms(): other = lax.ppermute(value, 'tp', [(i, i ^ reach) for i in range(size)])  11.1 us
    pallas_call x7, Pallas kernels, facts_call(): pl.pallas_call(kernel, out_shape=outs, in_specs=vmem_specs(len(operands))...  10.3 us
    ppermute x14, starting transfers between devices, ring_send(): return lax.ppermute(value, 'ctx', ring_pairs(lax.axis_size('ctx'), by))  10.1 us
    ppermute x7, starting transfers between devices, tp_terms(): other = lax.ppermute(value, 'tp', [(i, i ^ reach) for i in range(size)])  9.53 us
    all_to_all x2, starting transfers between devices, chips_exchange(): lax.all_to_all(value, 'ctx', split_axis=0, concat_axis=0, tiled=True, axi...  9.5 us
  transfers between devices with their start and end apart: 30, of which 17 were waited for; matrix products, arithmetic and copies ran while one was open for 1% of the time, Pallas kernels for 24%

profile of v15, /device:TPU:3, one launch (start us, length us, event | category | flops | bytes accessed | tf_op | source)
XLA Modules:
  0.0 152.7 jit_solution(6719964030284175346)
XLA Ops:
  0.7 1.8 %reshape.11.refs_0_.refs_4_ = bf16[72,4608]{1,0:T(8,128)(2,1)S(1)} reshape(bf16[72,8,576]{2,1,0:T(8,128)(2,1)} %param.13) | data formatting | bytes 1327104 | tf_op jit(solution)/shard_map/reshape | solution.py:659
  2.5 1.5 collective-permute-start.3
  4.0 4.4 %shard_map.105 = (f32[512,576]{1,0:T(8,128)S(1)}, bf16[512,576]{1,0:T(8,128)(2,1)S(1)}, f32[2,288]{1,0:T(2,128)S(1)}) custom-call(bf16[2,196,576]{2,1,0:T(8,128)(2,1)S(1)} %copy.11.feat_ref, bf16[9,48,576]{2,1,0:T(8,128)(2,1)S(1)} %bitcast.10, bf16[288,576]{1,0:T(8,128)(2,1)S(1)} %bitcast.13), custom_call_target="tpu_custom_call" | custom-call | tf_op jit(solution)/shard_map/pallas_call | solution.py:301
  8.5 1.3 collective-permute-start
  9.8 1.5 collective-permute-done
  11.3 0.7 shard_map.106
  12.0 6.3 %collective-permute-done.2.refs_1_.refs_4_ = bf16[72,4608]{1,0:T(8,128)(2,1)S(1)} collective-permute-done((bf16[72,4608]{1,0:T(8,128)(2,1)S(1)}, bf16[72,4608]{1,0:T(8,128)(2,1)S(1)}, u32[]{:S(2)}, u32[]{:S(2)}) %collective-permute-start.2) | collective-permute-done | bytes 663584 | tf_op jit(solution)/shard_map/ppermute | solution.py:456
  18.4 1.1 collective-permute-start.4
  19.8 0.9 copy-done.7
  20.7 6.4 %collective-permute-start.1 = (bf16[256,576]{1,0:T(8,128)(2,1)S(1)}, bf16[256,576]{1,0:T(8,128)(2,1)S(1)}, u32[]{:S(2)}, u32[]{:S(2)}) collective-permute-start(bf16[256,576]{1,0:T(8,128)(2,1)S(1)} %get-tuple-element.64), channel_id=1, source_target_pairs={{0,2},{2,4},{4,6},{6,8},{8,10},{10,12},{12,14},{14,16},{16,18},{18... | collective-permute-start | bytes 884744 | tf_op jit(solution)/shard_map/ppermute | solution.py:420
  27.1 11.0 %collective-permute-done.1.halo_ref = bf16[256,576]{1,0:T(8,128)(2,1)S(1)} collective-permute-done((bf16[256,576]{1,0:T(8,128)(2,1)S(1)}, bf16[256,576]{1,0:T(8,128)(2,1)S(1)}, u32[]{:S(2)}, u32[]{:S(2)}) %collective-permute-start.1) | collective-permute-done | bytes 294944 | tf_op jit(solution)/shard_map/ppermute | solution.py:420
  38.1 1.2 collective-permute-start.6
  39.3 0.8 copy-done.4
  40.4 1.3 shard_map.104.facts_ref
  41.7 0.6 copy-done.16
  42.4 1.8 %shard_map.107.own_ref = bf16[64,4608]{1,0:T(8,128)(2,1)} custom-call(s32[5]{0:T(128)S(1)} %copy-done.16, bf16[256,576]{1,0:T(8,128)(2,1)S(1)} %collective-permute-done.1.halo_ref, bf16[256,576]{1,0:T(8,128)(2,1)S(1)} %get-tuple-element.74.even_ref), custom_call_target="tpu_custom_call" | custom-call | tf_op jit(solution)/shard_map/pallas_call | solution.py:349
  44.2 2.8 %collective-permute-start.10 = (bf16[64,4608]{1,0:T(8,128)(2,1)}, bf16[64,4608]{1,0:T(8,128)(2,1)}, u32[]{:S(2)}, u32[]{:S(2)}) collective-permute-start(bf16[64,4608]{1,0:T(8,128)(2,1)} %shard_map.107.own_ref), channel_id=1, source_target_pairs={{0,2},{2,0},{4,6},{6,4},{8,10},{10,8},{12,14},{14,12},{16,18},{18,... | collective-permute-start | bytes 1769480 | tf_op jit(solution)/shard_map/ppermute | solution.py:437
  47.0 5.6 %collective-permute-done.6.refs_0_.refs_4_ = bf16[72,4608]{1,0:T(8,128)(2,1)S(1)} collective-permute-done((bf16[72,4608]{1,0:T(8,128)(2,1)S(1)}, bf16[72,4608]{1,0:T(8,128)(2,1)S(1)}, u32[]{:S(2)}, u32[]{:S(2)}) %collective-permute-start.6) | collective-permute-done | bytes 663584 | tf_op jit(solution)/shard_map/ppermute | solution.py:456
  52.6 3.0 %collective-permute-done.7.refs_1_.refs_6_ = bf16[72,4608]{1,0:T(8,128)(2,1)} collective-permute-done((bf16[72,4608]{1,0:T(8,128)(2,1)}, bf16[72,4608]{1,0:T(8,128)(2,1)}, u32[]{:S(2)}, u32[]{:S(2)}) %collective-permute-start.7) | collective-permute-done | bytes 663584 | tf_op jit(solution)/shard_map/ppermute | solution.py:456
  55.7 1.5 collective-permute-start.11
  57.1 4.9 %all-to-all-start = ((bf16[8,8,4096]{2,1,0:T(8,128)(2,1)}), bf16[8,8,4096]{2,1,0:T(8,128)(2,1)S(1)}, u32[]{:S(2)}, u32[]{:S(2)}) async-start(bf16[8,8,4096]{2,1,0:T(8,128)(2,1)} %bitcast.15), calls=%async_computation | async-start | bytes 1048576 | tf_op jit(solution)/shard_map/all_to_all | solution.py:640
  62.1 1.8 %shard_map.108.patch_ref = bf16[128,4608]{1,0:T(8,128)(2,1)S(1)} custom-call(s32[5]{0:T(128)S(1)} %copy-done.17, bf16[64,4608]{1,0:T(8,128)(2,1)} %shard_map.107.own_ref, bf16[64,4608]{1,0:T(8,128)(2,1)} %collective-permute-done.10.mate_ref), custom_call_target="tpu_custom_call" | custom-call | tf_op jit(solution)/shard_map/pallas_call | solution.py:338
  63.9 2.3 %shard_map.109.own_ref = f32[128,360]{1,0:T(8,128)S(1)} custom-call(bf16[128,4608]{1,0:T(8,128)(2,1)S(1)} %shard_map.108.patch_ref, bf16[72,4608]{1,0:T(8,128)(2,1)S(1)} %reshape.11.refs_0_.refs_4_, bf16[72,4608]{1,0:T(8,128)(2,1)S(1)} %collective-permute-done.2.refs_1_.refs_4_, bf16[72,4608]{1,0:T(8,128)(2,1)S(1)} %copy-done.8, ...), custom_call_target="tpu_custom_call" | custom-call | tf_op jit(solution)/shard_map/pallas_call | solution.py:594
  66.2 1.3 collective-permute-start.13
  67.5 1.6 %collective-permute-done.11.refs_1_ = bf16[72,4096]{1,0:T(8,128)(2,1)} collective-permute-done((bf16[72,4096]{1,0:T(8,128)(2,1)}, bf16[72,4096]{1,0:T(8,128)(2,1)}, u32[]{:S(2)}, u32[]{:S(2)}) %collective-permute-start.11) | collective-permute-done | bytes 589856 | tf_op jit(solution)/shard_map/ppermute | solution.py:456
  69.1 2.1 %collective-permute-done.13.other_ref = f32[128,360]{1,0:T(8,128)S(1)} collective-permute-done((f32[128,360]{1,0:T(8,128)S(1)}, f32[128,360]{1,0:T(8,128)S(1)}, u32[]{:S(2)}, u32[]{:S(2)}) %collective-permute-start.13) | collective-permute-done | bytes 184352 | tf_op jit(solution)/shard_map/ppermute | solution.py:445
  71.2 1.2 collective-permute-start.16
  72.4 1.9 %shard_map.110.own_ref = f32[128,216]{1,0:T(8,128)S(1)} custom-call(bf16[128,4608]{1,0:T(8,128)(2,1)S(1)} %shard_map.108.patch_ref, bf16[72,4608]{1,0:T(8,128)(2,1)S(1)} %collective-permute-done.6.refs_0_.refs_4_, bf16[72,4608]{1,0:T(8,128)(2,1)} %collective-permute-done.7.refs_1_.refs_6_, bf16[72,4608]{1,0:T(8,128)(2,1)S(1)} %collective-permute-done.12.refs_2_.refs_5_), custom_call_target="tpu_custom_call" | custom-call | tf_op jit(solution)/shard_map/pallas_call | solution.py:594
  74.3 1.3 collective-permute-start.14
  75.6 1.0 shard_map.111
  76.6 1.8 %collective-permute-done.14.other_ref = f32[128,216]{1,0:T(8,128)S(1)} collective-permute-done((f32[128,216]{1,0:T(8,128)S(1)}, f32[128,216]{1,0:T(8,128)S(1)}, u32[]{:S(2)}, u32[]{:S(2)}) %collective-permute-start.14) | collective-permute-done | bytes 110624 | tf_op jit(solution)/shard_map/ppermute | solution.py:445
  78.4 1.7 %shard_map.112 = (f32[128,216]{1,0:T(8,128)S(1)}, bf16[128,576]{1,0:T(8,128)(2,1)}) custom-call(s32[5]{0:T(128)S(1)} %copy-done.17, f32[128,216]{1,0:T(8,128)S(1)} %shard_map.110.own_ref, f32[128,216]{1,0:T(8,128)S(1)} %collective-permute-done.14.other_ref, bf16[128,576]{1,0:T(8,128)(2,1)S(1)} %get-tuple-element.80.refs_0_), custom_call_target="tpu_custom_call" | custom-call | tf_op jit(solution)/shard_map/pallas_call | solution.py:598
  80.2 4.6 %all-to-all-start.1 = ((bf16[8,16,576]{2,1,0:T(8,128)(2,1)}), bf16[8,16,576]{2,1,0:T(8,128)(2,1)S(1)}, u32[]{:S(2)}, u32[]{:S(2)}) async-start(bf16[8,16,576]{2,1,0:T(8,128)(2,1)} %bitcast.4), calls=%async_computation.1 | async-start | bytes 327680 | tf_op jit(solution)/shard_map/all_to_all | solution.py:640
  84.8 9.4 %collective-permute-start.8 = (bf16[64,4096]{1,0:T(8,128)(2,1)S(1)}, bf16[64,4096]{1,0:T(8,128)(2,1)S(1)}, u32[]{:S(2)}, u32[]{:S(2)}) collective-permute-start(bf16[64,4096]{1,0:T(8,128)(2,1)S(1)} %bitcast.6), channel_id=1, source_target_pairs={{0,2},{2,0},{4,6},{6,4},{8,10},{10,8},{12,14},{14,12},{16,18},{18,... | collective-permute-start | bytes 1572872 | tf_op jit(solution)/shard_map/ppermute | solution.py:437
  94.2 1.8 %all-to-all-done.1 = bf16[8,16,576]{2,1,0:T(8,128)(2,1)S(1)} async-done(((bf16[8,16,576]{2,1,0:T(8,128)(2,1)}), bf16[8,16,576]{2,1,0:T(8,128)(2,1)S(1)}, u32[]{:S(2)}, u32[]{:S(2)}) %all-to-all-start.1) | async-done | bytes 147488 | tf_op jit(solution)/shard_map/all_to_all | solution.py:640
  95.9 1.5 collective-permute-start.19
  97.4 2.2 %shard_map.113.refs_0_ = f32[128,216]{1,0:T(8,128)S(1)} custom-call(bf16[64,4096]{1,0:T(8,128)(2,1)S(1)} %bitcast.7, bf16[64,4096]{1,0:T(8,128)(2,1)S(1)} %collective-permute-done.8.send_ref, bf16[72,4096]{1,0:T(8,128)(2,1)} %refs_0_.1, bf16[72,4096]{1,0:T(8,128)(2,1)} %collective-permute-done.11.refs_1_, bf16[72,4096]{1,0:T(8,128)(2,1)} %collective-permute-done.16.refs_2_), custom_call_target="tpu_custom_call" | custom-call | tf_op jit(solution)/shard_map/pallas_call | solution.py:594
  99.6 1.4 collective-permute-start.17
  101.0 2.5 %collective-permute-done.17.refs_1_ = f32[128,216]{1,0:T(8,128)S(1)} collective-permute-done((f32[128,216]{1,0:T(8,128)S(1)}, f32[128,216]{1,0:T(8,128)S(1)}, u32[]{:S(2)}, u32[]{:S(2)}) %collective-permute-start.17) | collective-permute-done | bytes 110624 | tf_op jit(solution)/shard_map/ppermute | solution.py:445
  103.5 4.3 %collective-permute-done.15.refs_1_.refs_4_ = bf16[72,4096]{1,0:T(8,128)(2,1)S(1)} collective-permute-done((bf16[72,4096]{1,0:T(8,128)(2,1)}, bf16[72,4096]{1,0:T(8,128)(2,1)S(1)}, u32[]{:S(2)}, u32[]{:S(2)}) %collective-permute-start.15) | collective-permute-done | bytes 589856 | tf_op jit(solution)/shard_map/ppermute | solution.py:456
  107.8 1.5 collective-permute-start.20
  109.3 1.8 %shard_map.114.refs_0_ = f32[128,216]{1,0:T(8,128)S(1)} custom-call(bf16[64,4096]{1,0:T(8,128)(2,1)S(1)} %bitcast.8, bf16[64,4096]{1,0:T(8,128)(2,1)S(1)} %collective-permute-done.8.send_ref, bf16[72,4096]{1,0:T(8,128)(2,1)} %collective-permute-done.9.refs_0_.refs_3_, bf16[72,4096]{1,0:T(8,128)(2,1)S(1)} %collective-permute-done.15.refs_1_.refs_4_, ...), custom_call_target="tpu_custom_call" | custom-call | tf_op jit(solution)/shard_map/pallas_call | solution.py:594
  111.1 1.5 collective-permute-start.21
  112.6 1.9 %shard_map.115 = (f32[64,2304]{1,0:T(8,128)S(1)}, f32[64,2304]{1,0:T(8,128)S(1)}, f32[64,2304]{1,0:T(8,128)S(1)}, f32[64,2304]{1,0:T(8,128)S(1)}) custom-call(s32[5]{0:T(128)S(1)} %copy-done.17, f32[128,216]{1,0:T(8,128)S(1)} %shard_map.113.refs_0_, f32[128,216]{1,0:T(8,128)S(1)} %collective-permute-done.17.refs_1_, ...), custom_call_target="tpu_custom_call" | custom-call | tf_op jit(solution)/shard_map/pallas_call | solution.py:598
  115.0 1.9 %shard_map.116 = (f32[64,2304]{1,0:T(8,128)S(1)}, f32[64,2304]{1,0:T(8,128)S(1)}, f32[64,2304]{1,0:T(8,128)S(1)}, f32[64,2304]{1,0:T(8,128)S(1)}) custom-call(s32[5]{0:T(128)S(1)} %copy-done.17, f32[128,216]{1,0:T(8,128)S(1)} %shard_map.114.refs_0_, f32[128,216]{1,0:T(8,128)S(1)} %collective-permute-done.21.refs_1_, ...), custom_call_target="tpu_custom_call" | custom-call | tf_op jit(solution)/shard_map/pallas_call | solution.py:598
  116.9 2.7 %collective-permute-done.18.refs_0_.refs_6_ = bf16[72,4096]{1,0:T(8,128)(2,1)S(1)} collective-permute-done((bf16[72,4096]{1,0:T(8,128)(2,1)S(1)}, bf16[72,4096]{1,0:T(8,128)(2,1)S(1)}, u32[]{:S(2)}, u32[]{:S(2)}) %collective-permute-start.18) | collective-permute-done | bytes 589856 | tf_op jit(solution)/shard_map/ppermute | solution.py:456
  119.6 0.5 shard_map.117.refs_0_
  120.1 1.5 collective-permute-start.22
  121.6 2.7 %collective-permute-done.22.refs_1_ = f32[128,144]{1,0:T(8,128)S(1)} collective-permute-done((f32[128,144]{1,0:T(8,128)S(1)}, f32[128,144]{1,0:T(8,128)S(1)}, u32[]{:S(2)}, u32[]{:S(2)}) %collective-permute-start.22) | collective-permute-done | bytes 73760 | tf_op jit(solution)/shard_map/ppermute | solution.py:445
  124.3 1.1 shard_map.118
  125.4 6.8 %collective-permute-start.23 = (bf16[64,2304]{1,0:T(8,128)(2,1)S(1)}, bf16[64,2304]{1,0:T(8,128)(2,1)S(1)}, u32[]{:S(2)}, u32[]{:S(2)}) collective-permute-start(bf16[64,2304]{1,0:T(8,128)(2,1)S(1)} %get-tuple-element.103), channel_id=1, source_target_pairs={{0,2},{2,0},{4,6},{6,4},{8,10},{10,8},{12,14},{14,12},{16,18},{18,... | collective-permute-start | bytes 884744 | tf_op jit(solution)/shard_map/ppermute | solution.py:437
  132.1 1.1 shard_map.120
  133.3 1.3 shard_map.119
  134.7 2.3 %collective-permute-start.26 = (bf16[256,576]{1,0:T(8,128)(2,1)S(1)}, bf16[256,576]{1,0:T(8,128)(2,1)S(1)}, u32[]{:S(2)}, u32[]{:S(2)}) collective-permute-start(bf16[256,576]{1,0:T(8,128)(2,1)S(1)} %get-tuple-element.115), channel_id=1, source_target_pairs={{2,0},{4,2},{6,4},{8,6},{10,8},{12,10},{14,12},{16,14},{18,16},{20... | collective-permute-start | bytes 884744 | tf_op jit(solution)/shard_map/ppermute | solution.py:420
  137.0 1.2 shard_map.121
  138.3 3.3 %shard_map.122 = (f32[64,4096]{1,0:T(8,128)S(1)}, bf16[64,4096]{1,0:T(8,128)(2,1)S(1)}) custom-call(s32[5]{0:T(128)S(1)} %get-tuple-element.110.facts_ref, bf16[128,576]{1,0:T(8,128)(2,1)S(1)} %bitcast.12, bf16[72,4096]{1,0:T(8,128)(2,1)} %refs_0_.1, bf16[72,4096]{1,0:T(8,128)(2,1)} %collective-permute-done.11.refs_1_, ...), custom_call_target="tpu_custom_call" | custom-call | tf_op jit(solution)/shard_map/pallas_call | solution.py:626
  141.6 0.6 collective-permute-start.25
  142.2 1.8 %collective-permute-done.26.odd_ref = bf16[256,576]{1,0:T(8,128)(2,1)S(1)} collective-permute-done((bf16[256,576]{1,0:T(8,128)(2,1)S(1)}, bf16[256,576]{1,0:T(8,128)(2,1)S(1)}, u32[]{:S(2)}, u32[]{:S(2)}) %collective-permute-start.26) | collective-permute-done | bytes 294944 | tf_op jit(solution)/shard_map/ppermute | solution.py:420
  144.0 0.9 shard_map.123
  144.9 1.3 collective-permute-start.27
  146.2 1.7 %shard_map.124 = (bf16[2304,256]{1,0:T(8,128)(2,1)S(1)}, bf16[2304,256]{1,0:T(8,128)(2,1)S(1)}, bf16[2304,256]{1,0:T(8,128)(2,1)S(1)}) custom-call(s32[5]{0:T(128)S(1)} %get-tuple-element.110.facts_ref, bf16[9,48,576]{2,1,0:T(8,128)(2,1)S(1)} %bitcast.11), custom_call_target="tpu_custom_call" | custom-call | tf_op jit(solution)/shard_map/pallas_call | solution.py:598
  147.9 2.8 %shard_map.125 = bf16[2,196,576]{2,1,0:T(8,128)(2,1)S(1)} custom-call(f32[256,576]{1,0:T(8,128)S(1)} %get-tuple-element.114.even_ref, bf16[256,576]{1,0:T(8,128)(2,1)S(1)} %collective-permute-done.26.odd_ref, f32[512,576]{1,0:T(8,128)S(1)} %copy-done.1, f32[2,576]{1,0:T(2,128)S(1)} %get-tuple-element.116.excite_ref, f32[2,288]{1,0:T(2,128)S(1)} %add.9.sq_ref, ...), custom_call_target="tpu_custom_call" | custom-call | flops 2717908992 | bytes 4718592 | tf_op jit(solution)/shard_map/pallas_call | solution.py:385
  150.6 1.2 copy.12
  151.8 0.9 add_convert_fusion
  (62 shorter events, 1.6 us)
Async XLA Ops:
  0.6 3.3 %copy-start.18 = (bf16[2,196,576]{2,0,1:T(2,128)(2,1)S(1)}, bf16[2,196,576]{2,0,1:T(2,128)(2,1)}, u32[]{:S(2)}) copy-start(bf16[2,196,576]{2,0,1:T(2,128)(2,1)} %param.9) | copy-start | bytes 1354756
  0.6 3.4 %copy-start.10 = (bf16[9,576,48]{1,2,0:T(8,128)(2,1)S(1)}, bf16[9,576,48]{1,2,0:T(8,128)(2,1)}, u32[]{:S(2)}) copy-start(bf16[9,576,48]{1,2,0:T(8,128)(2,1)} %param.10) | copy-start | bytes 1492996
  0.7 3.4 %copy-start.14 = (bf16[576,288]{0,1:T(8,128)(2,1)S(1)}, bf16[576,288]{0,1:T(8,128)(2,1)}, u32[]{:S(2)}) copy-start(bf16[576,288]{0,1:T(8,128)(2,1)} %param.11) | copy-start | bytes 995332
  2.4 8.8 %copy-start.12 = (bf16[288,576]{1,0:T(8,128)(2,1)S(1)}, bf16[288,576]{1,0:T(8,128)(2,1)}, u32[]{:S(2)}) copy-start(bf16[288,576]{1,0:T(8,128)(2,1)} %expand_ref.3) | copy-start | bytes 995332
  2.4 15.8 %collective-permute-start.2 = (bf16[72,4608]{1,0:T(8,128)(2,1)S(1)}, bf16[72,4608]{1,0:T(8,128)(2,1)S(1)}, u32[]{:S(2)}, u32[]{:S(2)}) collective-permute-start(bf16[72,4608]{1,0:T(8,128)(2,1)S(1)} %reshape.11.refs_0_.refs_4_), channel_id=1, source_target_pairs={{0,8},{2,10},{8,16},{10,18},{16,24},{18,26},{24,28},{26,30},{28,20... | collective-permute-start | bytes 1990664 | tf_op jit(solution)/shard_map/ppermute | solution.py:456
  2.5 15.9 %collective-permute-start.3 = (bf16[72,4608]{1,0:T(8,128)(2,1)S(1)}, bf16[72,4608]{1,0:T(8,128)(2,1)S(1)}, u32[]{:S(2)}, u32[]{:S(2)}) collective-permute-start(bf16[72,4608]{1,0:T(8,128)(2,1)S(1)} %reshape.11.refs_0_.refs_4_), channel_id=1, source_target_pairs={{0,4},{2,6},{8,0},{10,2},{16,8},{18,10},{24,16},{26,18},{28,24},{3... | collective-permute-start | bytes 1990664 | tf_op jit(solution)/shard_map/ppermute | solution.py:456
  8.5 29.6 %copy-start = (f32[512,576]{1,0:T(8,128)}, f32[512,576]{1,0:T(8,128)S(1)}, u32[]{:S(2)}) copy-start(f32[512,576]{1,0:T(8,128)S(1)} %get-tuple-element.61.conv_ref) | copy-start | bytes 3538948
  8.5 2.8 %collective-permute-start = (f32[2,288]{1,0:T(2,128)S(1)}, f32[2,288]{1,0:T(2,128)S(1)}, u32[]{:S(2)}, u32[]{:S(2)}) collective-permute-start(f32[2,288]{1,0:T(2,128)S(1)} %get-tuple-element.63), channel_id=1, source_target_pairs={{0,1},{1,0},{2,3},{3,2},{4,5},{5,4},{6,7},{7,6},{8,9},{9,8},{10,11... | collective-permute-start | bytes 6920 | tf_op jit(solution)/shard_map/ppermute | solution.py:445
  18.3 45.6 %copy-start.2 = (bf16[72,4608]{1,0:T(8,128)(2,1)}, bf16[72,4608]{1,0:T(8,128)(2,1)S(1)}, u32[]{:S(2)}) copy-start(bf16[72,4608]{1,0:T(8,128)(2,1)S(1)} %collective-permute-done.2.refs_1_.refs_4_) | copy-start | bytes 1990660
  18.4 19.7 %collective-permute-start.4 = (bf16[72,4608]{1,0:T(8,128)(2,1)S(1)}, bf16[72,4608]{1,0:T(8,128)(2,1)S(1)}, u32[]{:S(2)}, u32[]{:S(2)}) collective-permute-start(bf16[72,4608]{1,0:T(8,128)(2,1)S(1)} %collective-permute-done.2.refs_1_.refs_4_), channel_id=1, source_target_pairs={{0,8},{2,10},{8,16},{10,18},{16,24},{18,26},{24,28},{26,30},{28,20... | collective-permute-start | bytes 1990664 | tf_op jit(solution)/shard_map/ppermute | solution.py:456
  19.5 18.6 %collective-permute-start.5 = (bf16[72,4608]{1,0:T(8,128)(2,1)S(1)}, bf16[72,4608]{1,0:T(8,128)(2,1)}, u32[]{:S(2)}, u32[]{:S(2)}) collective-permute-start(bf16[72,4608]{1,0:T(8,128)(2,1)S(1)} %collective-permute-done.3.refs_2_.refs_5_), channel_id=1, source_target_pairs={{0,4},{2,6},{8,0},{10,2},{16,8},{18,10},{24,16},{26,18},{28,24},{3... | collective-permute-start | bytes 1990664 | tf_op jit(solution)/shard_map/ppermute | solution.py:456
  19.8 0.9 copy-start.7
  20.7 17.4 %collective-permute-start.1 = (bf16[256,576]{1,0:T(8,128)(2,1)S(1)}, bf16[256,576]{1,0:T(8,128)(2,1)S(1)}, u32[]{:S(2)}, u32[]{:S(2)}) collective-permute-start(bf16[256,576]{1,0:T(8,128)(2,1)S(1)} %get-tuple-element.64), channel_id=1, source_target_pairs={{0,2},{2,4},{4,6},{6,8},{8,10},{10,12},{12,14},{14,16},{16,18},{18... | collective-permute-start | bytes 884744 | tf_op jit(solution)/shard_map/ppermute | solution.py:420
  38.1 14.6 %collective-permute-start.6 = (bf16[72,4608]{1,0:T(8,128)(2,1)S(1)}, bf16[72,4608]{1,0:T(8,128)(2,1)S(1)}, u32[]{:S(2)}, u32[]{:S(2)}) collective-permute-start(bf16[72,4608]{1,0:T(8,128)(2,1)S(1)} %collective-permute-done.4.refs_3_.refs_5_), channel_id=1, source_target_pairs={{0,8},{2,10},{8,16},{10,18},{16,24},{18,26},{24,28},{26,30},{28,20... | collective-permute-start | bytes 1990664 | tf_op jit(solution)/shard_map/ppermute | solution.py:456
  39.3 0.8 copy-start.4
  40.1 15.5 %collective-permute-start.7 = (bf16[72,4608]{1,0:T(8,128)(2,1)}, bf16[72,4608]{1,0:T(8,128)(2,1)}, u32[]{:S(2)}, u32[]{:S(2)}) collective-permute-start(bf16[72,4608]{1,0:T(8,128)(2,1)} %collective-permute-done.5.refs_4_.refs_6_), channel_id=1, source_target_pairs={{0,4},{2,6},{8,0},{10,2},{16,8},{18,10},{24,16},{26,18},{28,24},{3... | collective-permute-start | bytes 1990664 | tf_op jit(solution)/shard_map/ppermute | solution.py:456
  41.7 0.7 copy-start.16
  42.4 19.7 %copy-start.17 = (s32[5]{0:T(128)S(1)}, s32[5]{0:T(128)}, u32[]{:S(2)}) copy-start(s32[5]{0:T(128)} %shard_map.104.facts_ref) | copy-start | bytes 64
  44.2 17.9 %collective-permute-start.10 = (bf16[64,4608]{1,0:T(8,128)(2,1)}, bf16[64,4608]{1,0:T(8,128)(2,1)}, u32[]{:S(2)}, u32[]{:S(2)}) collective-permute-start(bf16[64,4608]{1,0:T(8,128)(2,1)} %shard_map.107.own_ref), channel_id=1, source_target_pairs={{0,2},{2,0},{4,6},{6,4},{8,10},{10,8},{12,14},{14,12},{16,18},{18,... | collective-permute-start | bytes 1769480 | tf_op jit(solution)/shard_map/ppermute | solution.py:437
  55.7 15.5 %collective-permute-start.12 = (bf16[72,4608]{1,0:T(8,128)(2,1)S(1)}, bf16[72,4608]{1,0:T(8,128)(2,1)S(1)}, u32[]{:S(2)}, u32[]{:S(2)}) collective-permute-start(bf16[72,4608]{1,0:T(8,128)(2,1)S(1)} %collective-permute-done.6.refs_0_.refs_4_), channel_id=1, source_target_pairs={{0,8},{2,10},{8,16},{10,18},{16,24},{18,26},{24,28},{26,30},{28,20... | collective-permute-start | bytes 1990664 | tf_op jit(solution)/shard_map/ppermute | solution.py:456
  55.7 13.5 %collective-permute-start.11 = (bf16[72,4096]{1,0:T(8,128)(2,1)}, bf16[72,4096]{1,0:T(8,128)(2,1)}, u32[]{:S(2)}, u32[]{:S(2)}) collective-permute-start(bf16[72,4096]{1,0:T(8,128)(2,1)} %refs_0_.1), channel_id=1, source_target_pairs={{0,4},{2,6},{8,0},{10,2},{16,8},{18,10},{24,16},{26,18},{28,24},{3... | collective-permute-start | bytes 1769480 | tf_op jit(solution)/shard_map/ppermute | solution.py:456
  57.1 23.0 %all-to-all-start = ((bf16[8,8,4096]{2,1,0:T(8,128)(2,1)}), bf16[8,8,4096]{2,1,0:T(8,128)(2,1)S(1)}, u32[]{:S(2)}, u32[]{:S(2)}) async-start(bf16[8,8,4096]{2,1,0:T(8,128)(2,1)} %bitcast.15), calls=%async_computation | async-start | bytes 1048576 | tf_op jit(solution)/shard_map/all_to_all | solution.py:640
  62.1 1.9 %copy-start.5 = (bf16[72,4608]{1,0:T(8,128)(2,1)S(1)}, bf16[72,4608]{1,0:T(8,128)(2,1)}, u32[]{:S(2)}) copy-start(bf16[72,4608]{1,0:T(8,128)(2,1)} %copy-done.4) | copy-start | bytes 1990660
  62.1 1.9 %copy-start.8 = (bf16[72,4608]{1,0:T(8,128)(2,1)S(1)}, bf16[72,4608]{1,0:T(8,128)(2,1)}, u32[]{:S(2)}) copy-start(bf16[72,4608]{1,0:T(8,128)(2,1)} %copy-done.7) | copy-start | bytes 1990660
  66.2 5.0 %collective-permute-start.13 = (f32[128,360]{1,0:T(8,128)S(1)}, f32[128,360]{1,0:T(8,128)S(1)}, u32[]{:S(2)}, u32[]{:S(2)}) collective-permute-start(f32[128,360]{1,0:T(8,128)S(1)} %shard_map.109.own_ref), channel_id=1, source_target_pairs={{0,1},{1,0},{2,3},{3,2},{4,5},{5,4},{6,7},{7,6},{8,9},{9,8},{10,11... | collective-permute-start | bytes 552968 | tf_op jit(solution)/shard_map/ppermute | solution.py:445
  67.5 26.6 %collective-permute-start.9 = (bf16[72,4096]{1,0:T(8,128)(2,1)}, bf16[72,4096]{1,0:T(8,128)(2,1)}, u32[]{:S(2)}, u32[]{:S(2)}) collective-permute-start(bf16[72,4096]{1,0:T(8,128)(2,1)} %refs_0_.1), channel_id=1, source_target_pairs={{0,8},{2,10},{8,16},{10,18},{16,24},{18,26},{24,28},{26,30},{28,20... | collective-permute-start | bytes 1769480 | tf_op jit(solution)/shard_map/ppermute | solution.py:456
  71.2 24.7 %collective-permute-start.16 = (bf16[72,4096]{1,0:T(8,128)(2,1)}, bf16[72,4096]{1,0:T(8,128)(2,1)}, u32[]{:S(2)}, u32[]{:S(2)}) collective-permute-start(bf16[72,4096]{1,0:T(8,128)(2,1)} %collective-permute-done.11.refs_1_), channel_id=1, source_target_pairs={{0,4},{2,6},{8,0},{10,2},{16,8},{18,10},{24,16},{26,18},{28,24},{3... | collective-permute-start | bytes 1769480 | tf_op jit(solution)/shard_map/ppermute | solution.py:456
  74.3 4.2 %collective-permute-start.14 = (f32[128,216]{1,0:T(8,128)S(1)}, f32[128,216]{1,0:T(8,128)S(1)}, u32[]{:S(2)}, u32[]{:S(2)}) collective-permute-start(f32[128,216]{1,0:T(8,128)S(1)} %shard_map.110.own_ref), channel_id=1, source_target_pairs={{0,1},{1,0},{2,3},{3,2},{4,5},{5,4},{6,7},{7,6},{8,9},{9,8},{10,11... | collective-permute-start | bytes 331784 | tf_op jit(solution)/shard_map/ppermute | solution.py:445
  80.2 15.8 %all-to-all-start.1 = ((bf16[8,16,576]{2,1,0:T(8,128)(2,1)}), bf16[8,16,576]{2,1,0:T(8,128)(2,1)S(1)}, u32[]{:S(2)}, u32[]{:S(2)}) async-start(bf16[8,16,576]{2,1,0:T(8,128)(2,1)} %bitcast.4), calls=%async_computation.1 | async-start | bytes 327680 | tf_op jit(solution)/shard_map/all_to_all | solution.py:640
  84.8 12.6 %collective-permute-start.8 = (bf16[64,4096]{1,0:T(8,128)(2,1)S(1)}, bf16[64,4096]{1,0:T(8,128)(2,1)S(1)}, u32[]{:S(2)}, u32[]{:S(2)}) collective-permute-start(bf16[64,4096]{1,0:T(8,128)(2,1)S(1)} %bitcast.6), channel_id=1, source_target_pairs={{0,2},{2,0},{4,6},{6,4},{8,10},{10,8},{12,14},{14,12},{16,18},{18,... | collective-permute-start | bytes 1572872 | tf_op jit(solution)/shard_map/ppermute | solution.py:437
  95.9 11.9 %collective-permute-start.15 = (bf16[72,4096]{1,0:T(8,128)(2,1)}, bf16[72,4096]{1,0:T(8,128)(2,1)S(1)}, u32[]{:S(2)}, u32[]{:S(2)}) collective-permute-start(bf16[72,4096]{1,0:T(8,128)(2,1)} %collective-permute-done.9.refs_0_.refs_3_), channel_id=1, source_target_pairs={{0,8},{2,10},{8,16},{10,18},{16,24},{18,26},{24,28},{26,30},{28,20... | collective-permute-start | bytes 1769480 | tf_op jit(solution)/shard_map/ppermute | solution.py:456
  95.9 11.9 %collective-permute-start.19 = (bf16[72,4096]{1,0:T(8,128)(2,1)}, bf16[72,4096]{1,0:T(8,128)(2,1)S(1)}, u32[]{:S(2)}, u32[]{:S(2)}) collective-permute-start(bf16[72,4096]{1,0:T(8,128)(2,1)} %collective-permute-done.16.refs_2_), channel_id=1, source_target_pairs={{0,4},{2,6},{8,0},{10,2},{16,8},{18,10},{24,16},{26,18},{28,24},{3... | collective-permute-start | bytes 1769480 | tf_op jit(solution)/shard_map/ppermute | solution.py:456
  99.6 13.0 %copy-start.9 = (bf16[72,4608]{1,0:T(8,128)(2,1)S(1)}, bf16[72,4608]{1,0:T(8,128)(2,1)}, u32[]{:S(2)}) copy-start(bf16[72,4608]{1,0:T(8,128)(2,1)} %copy-done.7) | copy-start | bytes 1990660
  99.6 3.9 %collective-permute-start.17 = (f32[128,216]{1,0:T(8,128)S(1)}, f32[128,216]{1,0:T(8,128)S(1)}, u32[]{:S(2)}, u32[]{:S(2)}) collective-permute-start(f32[128,216]{1,0:T(8,128)S(1)} %shard_map.113.refs_0_), channel_id=1, source_target_pairs={{0,1},{1,0},{2,3},{3,2},{4,5},{5,4},{6,7},{7,6},{8,9},{9,8},{10,11... | collective-permute-start | bytes 331784 | tf_op jit(solution)/shard_map/ppermute | solution.py:445
  107.8 11.8 %collective-permute-start.18 = (bf16[72,4096]{1,0:T(8,128)(2,1)S(1)}, bf16[72,4096]{1,0:T(8,128)(2,1)S(1)}, u32[]{:S(2)}, u32[]{:S(2)}) collective-permute-start(bf16[72,4096]{1,0:T(8,128)(2,1)S(1)} %collective-permute-done.15.refs_1_.refs_4_), channel_id=1, source_target_pairs={{0,8},{2,10},{8,16},{10,18},{16,24},{18,26},{24,28},{26,30},{28,20... | collective-permute-start | bytes 1769480 | tf_op jit(solution)/shard_map/ppermute | solution.py:456
  107.8 11.8 %collective-permute-start.20 = (bf16[72,4096]{1,0:T(8,128)(2,1)S(1)}, bf16[72,4096]{1,0:T(8,128)(2,1)S(1)}, u32[]{:S(2)}, u32[]{:S(2)}) collective-permute-start(bf16[72,4096]{1,0:T(8,128)(2,1)S(1)} %collective-permute-done.19.refs_2_.refs_5_), channel_id=1, source_target_pairs={{0,4},{2,6},{8,0},{10,2},{16,8},{18,10},{24,16},{26,18},{28,24},{3... | collective-permute-start | bytes 1769480 | tf_op jit(solution)/shard_map/ppermute | solution.py:456
  111.1 3.9 %collective-permute-start.21 = (f32[128,216]{1,0:T(8,128)S(1)}, f32[128,216]{1,0:T(8,128)S(1)}, u32[]{:S(2)}, u32[]{:S(2)}) collective-permute-start(f32[128,216]{1,0:T(8,128)S(1)} %shard_map.114.refs_0_), channel_id=1, source_target_pairs={{0,1},{1,0},{2,3},{3,2},{4,5},{5,4},{6,7},{7,6},{8,9},{9,8},{10,11... | collective-permute-start | bytes 331784 | tf_op jit(solution)/shard_map/ppermute | solution.py:445
  112.6 2.4 %copy-start.3 = (bf16[72,4608]{1,0:T(8,128)(2,1)S(1)}, bf16[72,4608]{1,0:T(8,128)(2,1)}, u32[]{:S(2)}) copy-start(bf16[72,4608]{1,0:T(8,128)(2,1)} %copy-done.2) | copy-start | bytes 1990660
  112.6 2.4 %copy-start.6 = (bf16[72,4608]{1,0:T(8,128)(2,1)S(1)}, bf16[72,4608]{1,0:T(8,128)(2,1)}, u32[]{:S(2)}) copy-start(bf16[72,4608]{1,0:T(8,128)(2,1)} %copy-done.4) | copy-start | bytes 1990660
  120.1 4.2 %collective-permute-start.22 = (f32[128,144]{1,0:T(8,128)S(1)}, f32[128,144]{1,0:T(8,128)S(1)}, u32[]{:S(2)}, u32[]{:S(2)}) collective-permute-start(f32[128,144]{1,0:T(8,128)S(1)} %shard_map.117.refs_0_), channel_id=1, source_target_pairs={{0,1},{1,0},{2,3},{3,2},{4,5},{5,4},{6,7},{7,6},{8,9},{9,8},{10,11... | collective-permute-start | bytes 221192 | tf_op jit(solution)/shard_map/ppermute | solution.py:445
  125.4 8.0 %collective-permute-start.23 = (bf16[64,2304]{1,0:T(8,128)(2,1)S(1)}, bf16[64,2304]{1,0:T(8,128)(2,1)S(1)}, u32[]{:S(2)}, u32[]{:S(2)}) collective-permute-start(bf16[64,2304]{1,0:T(8,128)(2,1)S(1)} %get-tuple-element.103), channel_id=1, source_target_pairs={{0,2},{2,0},{4,6},{6,4},{8,10},{10,8},{12,14},{14,12},{16,18},{18,... | collective-permute-start | bytes 884744 | tf_op jit(solution)/shard_map/ppermute | solution.py:437
  133.2 3.8 %collective-permute-start.24 = (bf16[64,2304]{1,0:T(8,128)(2,1)S(1)}, bf16[64,2304]{1,0:T(8,128)(2,1)S(1)}, u32[]{:S(2)}, u32[]{:S(2)}) collective-permute-start(bf16[64,2304]{1,0:T(8,128)(2,1)S(1)} %get-tuple-element.109), channel_id=1, source_target_pairs={{0,2},{2,0},{4,6},{6,4},{8,10},{10,8},{12,14},{14,12},{16,18},{18,... | collective-permute-start | bytes 884744 | tf_op jit(solution)/shard_map/ppermute | solution.py:437
  134.7 9.3 %collective-permute-start.26 = (bf16[256,576]{1,0:T(8,128)(2,1)S(1)}, bf16[256,576]{1,0:T(8,128)(2,1)S(1)}, u32[]{:S(2)}, u32[]{:S(2)}) collective-permute-start(bf16[256,576]{1,0:T(8,128)(2,1)S(1)} %get-tuple-element.115), channel_id=1, source_target_pairs={{2,0},{4,2},{6,4},{8,6},{10,8},{12,10},{14,12},{16,14},{18,16},{20... | collective-permute-start | bytes 884744 | tf_op jit(solution)/shard_map/ppermute | solution.py:420
  138.3 5.7 %copy-start.1 = (f32[512,576]{1,0:T(8,128)S(1)}, f32[512,576]{1,0:T(8,128)}, u32[]{:S(2)}) copy-start(f32[512,576]{1,0:T(8,128)} %copy-done) | copy-start | bytes 3538948
  138.3 5.7 %copy-start.13 = (bf16[288,576]{1,0:T(8,128)(2,1)S(1)}, bf16[288,576]{1,0:T(8,128)(2,1)}, u32[]{:S(2)}) copy-start(bf16[288,576]{1,0:T(8,128)(2,1)} %expand_ref.3) | copy-start | bytes 995332
  141.6 10.3 %collective-permute-start.25 = (bf16[64,4096]{1,0:T(8,128)(2,1)S(1)}, bf16[64,4096]{1,0:T(8,128)(2,1)S(1)}, u32[]{:S(2)}, u32[]{:S(2)}) collective-permute-start(bf16[64,4096]{1,0:T(8,128)(2,1)S(1)} %get-tuple-element.113), channel_id=1, source_target_pairs={{0,2},{2,0},{4,6},{6,4},{8,10},{10,8},{12,14},{14,12},{16,18},{18,... | collective-permute-start | bytes 1572872 | tf_op jit(solution)/shard_map/ppermute | solution.py:437
  144.0 2.2 %copy-start.11 = (bf16[9,576,48]{1,2,0:T(8,128)(2,1)S(1)}, bf16[9,576,48]{1,2,0:T(8,128)(2,1)}, u32[]{:S(2)}) copy-start(bf16[9,576,48]{1,2,0:T(8,128)(2,1)} %param.10) | copy-start | bytes 1492996
  144.0 3.9 %copy-start.15 = (bf16[576,288]{0,1:T(8,128)(2,1)S(1)}, bf16[576,288]{0,1:T(8,128)(2,1)}, u32[]{:S(2)}) copy-start(bf16[576,288]{0,1:T(8,128)(2,1)} %param.11) | copy-start | bytes 995332
  144.9 2.9 %collective-permute-start.27 = (f32[2,288]{1,0:T(2,128)S(1)}, f32[2,288]{1,0:T(2,128)S(1)}, u32[]{:S(2)}, u32[]{:S(2)}) collective-permute-start(f32[2,288]{1,0:T(2,128)S(1)} %shard_map.123), channel_id=1, source_target_pairs={{0,1},{1,0},{2,3},{3,2},{4,5},{5,4},{6,7},{7,6},{8,9},{9,8},{10,11... | collective-permute-start | bytes 6920 | tf_op jit(solution)/shard_map/ppermute | solution.py:445

commit v16 on v15

--- a/solution.py
+++ b/solution.py
@@ -686,7 +686,7 @@
     r_up = [readout_kernel, ring_send(readout_kernel, 1)]
     samplers = [flat_sampler] + [block for pair in zip(s_up[1:], s_down[1:]) for block in pair]
     offsets = ring_offsets(chips)
-    count = 2 * steps - 3
+    count = 2 * steps - 1
     first_pre = tp_terms(block_products(pre_kernel, (patches,), samplers[:count]))
     r_down[1], s_last, *first_pre = tie(r_down[1], s_last, *first_pre)
     first_slope, first_act = act_and_slope(facts, first_pre, offsets[:count], chips, (), unit)
@@ -712,13 +712,13 @@
     middle = r_up[1 : steps - 1] + [r_down[steps - 1]]
     r_down.append(ring_send(r_down[-1], -1))
     terms = tp_terms(block_products(back_kernel, back, middle))
-    pieces = [(0, 2 * step - 1) for step in range(1, steps - 1)] + [(1, 1)]
+    pieces = [(0, 2 * step - 1) for step in range(1, steps - 1)] + [(0, 2 * steps - 2)]
     blocks = s_up[1 : steps - 1] + [s_down[steps - 1]]
     grads = add_gradients(facts, terms, slopes, pieces, blocks, grads, unit, both, False)
 
     late_up, late_down, *grads = tie(r_up[-1], r_down[-1], *grads)
     terms = tp_terms(block_products(back_kernel, back, [late_up, late_down]))
-    pieces, blocks = [(1, 0), (1, 2)], [s_up[-1], s_last]
+    pieces, blocks = [(0, 2 * steps - 3), (1, 0)], [s_up[-1], s_last]
     halo_own, halo_mate = add_gradients(
         facts, terms, slopes, pieces, blocks, grads[:2], unit, (halo_lanes,), True
     )

time: 154 us -> 155 us (level)
  waiting for transfers between devices: 49.4 us -> 52.1 us
    all_to_all x2, waiting for transfers between devices: 1.78 us -> 4.28 us  [chips_exchange(): lax.all_to_all(value, 'ctx', split_axis=0, concat_axis=0, tiled=True, axi...]
  transfers between devices with their start and end apart: 30 -> 30, of which waited for: 17 -> 15; matrix products, arithmetic and copies ran while one was open for 1% -> 1% of each run, Pallas kernels for 24% -> 23%
where the time goes in v16:
time: 155 us; the launch traced here: 154 us
  starting transfers between devices  57.4 us (37%)
  waiting for transfers between devices  52.1 us (34%)
  Pallas kernels  37.7 us (24%)
  local copies, waits for them, and re-layouts  5.41 us (3%)
    ppermute x14, waiting for transfers between devices, ring_send(): return lax.ppermute(value, 'ctx', ring_pairs(lax.axis_size('ctx'), by))  23.6 us
    ppermute x5, starting transfers between devices, swap_cores(): lax.ppermute(value, 'ctx', [(i, i ^ 1) for i in range(lax.axis_size('ctx'...  19.1 us
    ppermute x2, waiting for transfers between devices, shifted(): return lax.ppermute(value, axis, pairs)  13.3 us
    ppermute x7, waiting for transfers between devices, tp_terms(): other = lax.ppermute(value, 'tp', [(i, i ^ reach) for i in range(size)])  10.9 us
    ppermute x14, starting transfers between devices, ring_send(): return lax.ppermute(value, 'ctx', ring_pairs(lax.axis_size('ctx'), by))  10.6 us
    pallas_call x7, Pallas kernels, facts_call(): pl.pallas_call(kernel, out_shape=outs, in_specs=vmem_specs(len(operands))...  10.3 us
    all_to_all x2, starting transfers between devices, chips_exchange(): lax.all_to_all(value, 'ctx', split_axis=0, concat_axis=0, tiled=True, axi...  9.56 us
    ppermute x7, starting transfers between devices, tp_terms(): other = lax.ppermute(value, 'tp', [(i, i ^ reach) for i in range(size)])  9.37 us
  transfers between devices with their start and end apart: 30, of which 15 were waited for; matrix products, arithmetic and copies ran while one was open for 1% of the time, Pallas kernels for 23%

profile of v16, /device:TPU:3, one launch (start us, length us, event | category | flops | bytes accessed | tf_op | source)
XLA Modules:
  0.0 154.5 jit_solution(2026260860955333779)
XLA Ops:
  0.7 1.8 %reshape.11.refs_0_.refs_4_ = bf16[72,4608]{1,0:T(8,128)(2,1)S(1)} reshape(bf16[72,8,576]{2,1,0:T(8,128)(2,1)} %param.13) | data formatting | bytes 1327104 | tf_op jit(solution)/shard_map/reshape | solution.py:659
  2.5 1.5 collective-permute-start.3
  4.0 4.4 %shard_map.105 = (f32[512,576]{1,0:T(8,128)S(1)}, bf16[512,576]{1,0:T(8,128)(2,1)S(1)}, f32[2,288]{1,0:T(2,128)S(1)}) custom-call(bf16[2,196,576]{2,1,0:T(8,128)(2,1)S(1)} %copy.11.feat_ref, bf16[9,48,576]{2,1,0:T(8,128)(2,1)S(1)} %bitcast.10, bf16[288,576]{1,0:T(8,128)(2,1)S(1)} %bitcast.13), custom_call_target="tpu_custom_call" | custom-call | tf_op jit(solution)/shard_map/pallas_call | solution.py:301
  8.5 1.3 collective-permute-start
  9.8 1.5 collective-permute-done
  11.3 0.7 shard_map.106
  12.0 6.3 %collective-permute-done.2.refs_1_.refs_4_ = bf16[72,4608]{1,0:T(8,128)(2,1)S(1)} collective-permute-done((bf16[72,4608]{1,0:T(8,128)(2,1)S(1)}, bf16[72,4608]{1,0:T(8,128)(2,1)S(1)}, u32[]{:S(2)}, u32[]{:S(2)}) %collective-permute-start.2) | collective-permute-done | bytes 663584 | tf_op jit(solution)/shard_map/ppermute | solution.py:456
  18.4 1.1 collective-permute-start.4
  19.5 0.3 collective-permute-start.5
  19.8 0.9 copy-done.7
  20.7 6.4 %collective-permute-start.1 = (bf16[256,576]{1,0:T(8,128)(2,1)S(1)}, bf16[256,576]{1,0:T(8,128)(2,1)S(1)}, u32[]{:S(2)}, u32[]{:S(2)}) collective-permute-start(bf16[256,576]{1,0:T(8,128)(2,1)S(1)} %get-tuple-element.64), channel_id=1, source_target_pairs={{0,2},{2,4},{4,6},{6,8},{8,10},{10,12},{12,14},{14,16},{16,18},{18... | collective-permute-start | bytes 884744 | tf_op jit(solution)/shard_map/ppermute | solution.py:420
  27.1 11.0 %collective-permute-done.1.halo_ref = bf16[256,576]{1,0:T(8,128)(2,1)S(1)} collective-permute-done((bf16[256,576]{1,0:T(8,128)(2,1)S(1)}, bf16[256,576]{1,0:T(8,128)(2,1)S(1)}, u32[]{:S(2)}, u32[]{:S(2)}) %collective-permute-start.1) | collective-permute-done | bytes 294944 | tf_op jit(solution)/shard_map/ppermute | solution.py:420
  38.1 1.2 collective-permute-start.6
  39.3 0.8 copy-done.4
  40.4 1.3 shard_map.104.facts_ref
  41.7 0.6 copy-done.16
  42.4 1.8 %shard_map.107.own_ref = bf16[64,4608]{1,0:T(8,128)(2,1)} custom-call(s32[5]{0:T(128)S(1)} %copy-done.16, bf16[256,576]{1,0:T(8,128)(2,1)S(1)} %collective-permute-done.1.halo_ref, bf16[256,576]{1,0:T(8,128)(2,1)S(1)} %get-tuple-element.74.even_ref), custom_call_target="tpu_custom_call" | custom-call | tf_op jit(solution)/shard_map/pallas_call | solution.py:349
  44.2 2.8 %collective-permute-start.10 = (bf16[64,4608]{1,0:T(8,128)(2,1)}, bf16[64,4608]{1,0:T(8,128)(2,1)}, u32[]{:S(2)}, u32[]{:S(2)}) collective-permute-start(bf16[64,4608]{1,0:T(8,128)(2,1)} %shard_map.107.own_ref), channel_id=1, source_target_pairs={{0,2},{2,0},{4,6},{6,4},{8,10},{10,8},{12,14},{14,12},{16,18},{18,... | collective-permute-start | bytes 1769480 | tf_op jit(solution)/shard_map/ppermute | solution.py:437
  47.0 5.6 %collective-permute-done.6.refs_5_.refs_4_ = bf16[72,4608]{1,0:T(8,128)(2,1)S(1)} collective-permute-done((bf16[72,4608]{1,0:T(8,128)(2,1)S(1)}, bf16[72,4608]{1,0:T(8,128)(2,1)S(1)}, u32[]{:S(2)}, u32[]{:S(2)}) %collective-permute-start.6) | collective-permute-done | bytes 663584 | tf_op jit(solution)/shard_map/ppermute | solution.py:456
  52.6 3.0 %collective-permute-done.7.refs_6_ = bf16[72,4608]{1,0:T(8,128)(2,1)} collective-permute-done((bf16[72,4608]{1,0:T(8,128)(2,1)}, bf16[72,4608]{1,0:T(8,128)(2,1)}, u32[]{:S(2)}, u32[]{:S(2)}) %collective-permute-start.7) | collective-permute-done | bytes 663584 | tf_op jit(solution)/shard_map/ppermute | solution.py:456
  55.7 1.5 collective-permute-start.11
  57.1 4.9 %all-to-all-start = ((bf16[8,8,4096]{2,1,0:T(8,128)(2,1)}), bf16[8,8,4096]{2,1,0:T(8,128)(2,1)S(1)}, u32[]{:S(2)}, u32[]{:S(2)}) async-start(bf16[8,8,4096]{2,1,0:T(8,128)(2,1)} %bitcast.15), calls=%async_computation | async-start | bytes 1048576 | tf_op jit(solution)/shard_map/all_to_all | solution.py:640
  62.1 1.8 %shard_map.108.patch_ref = bf16[128,4608]{1,0:T(8,128)(2,1)S(1)} custom-call(s32[5]{0:T(128)S(1)} %copy-done.17, bf16[64,4608]{1,0:T(8,128)(2,1)} %shard_map.107.own_ref, bf16[64,4608]{1,0:T(8,128)(2,1)} %collective-permute-done.10.mate_ref), custom_call_target="tpu_custom_call" | custom-call | tf_op jit(solution)/shard_map/pallas_call | solution.py:338
  63.9 2.9 %shard_map.109.own_ref = f32[128,504]{1,0:T(8,128)S(1)} custom-call(bf16[128,4608]{1,0:T(8,128)(2,1)S(1)} %shard_map.108.patch_ref, bf16[72,4608]{1,0:T(8,128)(2,1)S(1)} %reshape.11.refs_0_.refs_4_, bf16[72,4608]{1,0:T(8,128)(2,1)S(1)} %collective-permute-done.2.refs_1_.refs_4_, bf16[72,4608]{1,0:T(8,128)(2,1)S(1)} %copy-done.8, ...), custom_call_target="tpu_custom_call" | custom-call | tf_op jit(solution)/shard_map/pallas_call | solution.py:594
  66.9 1.3 collective-permute-start.13
  68.2 0.9 collective-permute-done.11.refs_1_
  69.1 3.4 %collective-permute-done.13.other_ref = f32[128,504]{1,0:T(8,128)S(1)} collective-permute-done((f32[128,504]{1,0:T(8,128)S(1)}, f32[128,504]{1,0:T(8,128)S(1)}, u32[]{:S(2)}, u32[]{:S(2)}) %collective-permute-start.13) | collective-permute-done | bytes 258080 | tf_op jit(solution)/shard_map/ppermute | solution.py:445
  72.6 1.2 collective-permute-start.16
  73.7 0.4 shard_map.110.own_ref
  74.2 1.3 collective-permute-start.14
  75.5 1.1 shard_map.111
  76.6 1.0 collective-permute-done.14.other_ref
  77.7 1.6 %shard_map.112 = (f32[128,72]{1,0:T(8,128)S(1)}, bf16[128,576]{1,0:T(8,128)(2,1)}) custom-call(s32[5]{0:T(128)S(1)} %copy-done.17, f32[128,72]{1,0:T(8,128)S(1)} %shard_map.110.own_ref, f32[128,72]{1,0:T(8,128)S(1)} %collective-permute-done.14.other_ref, bf16[128,576]{1,0:T(8,128)(2,1)S(1)} %get-tuple-element.80.refs_0_), custom_call_target="tpu_custom_call" | custom-call | tf_op jit(solution)/shard_map/pallas_call | solution.py:598
  79.3 4.6 %all-to-all-start.1 = ((bf16[8,16,576]{2,1,0:T(8,128)(2,1)}), bf16[8,16,576]{2,1,0:T(8,128)(2,1)S(1)}, u32[]{:S(2)}, u32[]{:S(2)}) async-start(bf16[8,16,576]{2,1,0:T(8,128)(2,1)} %bitcast.4), calls=%async_computation.1 | async-start | bytes 327680 | tf_op jit(solution)/shard_map/all_to_all | solution.py:640
  83.9 8.1 %collective-permute-start.8 = (bf16[64,4096]{1,0:T(8,128)(2,1)S(1)}, bf16[64,4096]{1,0:T(8,128)(2,1)S(1)}, u32[]{:S(2)}, u32[]{:S(2)}) collective-permute-start(bf16[64,4096]{1,0:T(8,128)(2,1)S(1)} %bitcast.6), channel_id=1, source_target_pairs={{0,2},{2,0},{4,6},{6,4},{8,10},{10,8},{12,14},{14,12},{16,18},{18,... | collective-permute-start | bytes 1572872 | tf_op jit(solution)/shard_map/ppermute | solution.py:437
  92.0 4.3 %all-to-all-done.1 = bf16[8,16,576]{2,1,0:T(8,128)(2,1)S(1)} async-done(((bf16[8,16,576]{2,1,0:T(8,128)(2,1)}), bf16[8,16,576]{2,1,0:T(8,128)(2,1)S(1)}, u32[]{:S(2)}, u32[]{:S(2)}) %all-to-all-start.1) | async-done | bytes 147488 | tf_op jit(solution)/shard_map/all_to_all | solution.py:640
  96.2 1.5 collective-permute-start.19
  97.7 2.2 %shard_map.113.refs_0_ = f32[128,216]{1,0:T(8,128)S(1)} custom-call(bf16[64,4096]{1,0:T(8,128)(2,1)S(1)} %bitcast.7, bf16[64,4096]{1,0:T(8,128)(2,1)S(1)} %collective-permute-done.8.send_ref, bf16[72,4096]{1,0:T(8,128)(2,1)} %refs_0_.1, bf16[72,4096]{1,0:T(8,128)(2,1)} %collective-permute-done.11.refs_1_, bf16[72,4096]{1,0:T(8,128)(2,1)} %collective-permute-done.16.refs_2_), custom_call_target="tpu_custom_call" | custom-call | tf_op jit(solution)/shard_map/pallas_call | solution.py:594
  99.9 1.4 collective-permute-start.17
  101.3 5.4 %collective-permute-done.15.refs_1_.refs_4_ = bf16[72,4096]{1,0:T(8,128)(2,1)S(1)} collective-permute-done((bf16[72,4096]{1,0:T(8,128)(2,1)}, bf16[72,4096]{1,0:T(8,128)(2,1)S(1)}, u32[]{:S(2)}, u32[]{:S(2)}) %collective-permute-start.15) | collective-permute-done | bytes 589856 | tf_op jit(solution)/shard_map/ppermute | solution.py:456
  106.7 2.0 %collective-permute-start.20 = (bf16[72,4096]{1,0:T(8,128)(2,1)S(1)}, bf16[72,4096]{1,0:T(8,128)(2,1)S(1)}, u32[]{:S(2)}, u32[]{:S(2)}) collective-permute-start(bf16[72,4096]{1,0:T(8,128)(2,1)S(1)} %collective-permute-done.19.refs_2_.refs_5_), channel_id=1, source_target_pairs={{0,4},{2,6},{8,0},{10,2},{16,8},{18,10},{24,16},{26,18},{28,24},{3... | collective-permute-start | bytes 1769480 | tf_op jit(solution)/shard_map/ppermute | solution.py:456
  108.7 1.8 %shard_map.114.refs_0_ = f32[128,216]{1,0:T(8,128)S(1)} custom-call(bf16[64,4096]{1,0:T(8,128)(2,1)S(1)} %bitcast.8, bf16[64,4096]{1,0:T(8,128)(2,1)S(1)} %collective-permute-done.8.send_ref, bf16[72,4096]{1,0:T(8,128)(2,1)} %collective-permute-done.9.refs_0_.refs_3_, bf16[72,4096]{1,0:T(8,128)(2,1)S(1)} %collective-permute-done.15.refs_1_.refs_4_, ...), custom_call_target="tpu_custom_call" | custom-call | tf_op jit(solution)/shard_map/pallas_call | solution.py:594
  110.5 1.4 collective-permute-start.21
  111.9 1.9 %shard_map.115 = (f32[64,2304]{1,0:T(8,128)S(1)}, f32[64,2304]{1,0:T(8,128)S(1)}, f32[64,2304]{1,0:T(8,128)S(1)}, f32[64,2304]{1,0:T(8,128)S(1)}) custom-call(s32[5]{0:T(128)S(1)} %copy-done.17, f32[128,216]{1,0:T(8,128)S(1)} %shard_map.113.refs_0_, f32[128,216]{1,0:T(8,128)S(1)} %collective-permute-done.17.refs_1_, ...), custom_call_target="tpu_custom_call" | custom-call | tf_op jit(solution)/shard_map/pallas_call | solution.py:598
  113.8 0.9 collective-permute-done.21.refs_1_
  114.7 1.8 %shard_map.116 = (f32[64,2304]{1,0:T(8,128)S(1)}, f32[64,2304]{1,0:T(8,128)S(1)}, f32[64,2304]{1,0:T(8,128)S(1)}, f32[64,2304]{1,0:T(8,128)S(1)}) custom-call(s32[5]{0:T(128)S(1)} %copy-done.17, f32[128,216]{1,0:T(8,128)S(1)} %shard_map.114.refs_0_, f32[128,216]{1,0:T(8,128)S(1)} %collective-permute-done.21.refs_1_, ...), custom_call_target="tpu_custom_call" | custom-call | tf_op jit(solution)/shard_map/pallas_call | solution.py:598
  116.5 2.2 %collective-permute-done.18.refs_0_.refs_6_ = bf16[72,4096]{1,0:T(8,128)(2,1)S(1)} collective-permute-done((bf16[72,4096]{1,0:T(8,128)(2,1)S(1)}, bf16[72,4096]{1,0:T(8,128)(2,1)S(1)}, u32[]{:S(2)}, u32[]{:S(2)}) %collective-permute-start.18) | collective-permute-done | bytes 589856 | tf_op jit(solution)/shard_map/ppermute | solution.py:456
  118.7 0.5 shard_map.117.refs_0_
  119.2 1.4 collective-permute-start.22
  120.6 4.0 %collective-permute-done.22.refs_1_ = f32[128,144]{1,0:T(8,128)S(1)} collective-permute-done((f32[128,144]{1,0:T(8,128)S(1)}, f32[128,144]{1,0:T(8,128)S(1)}, u32[]{:S(2)}, u32[]{:S(2)}) %collective-permute-start.22) | collective-permute-done | bytes 73760 | tf_op jit(solution)/shard_map/ppermute | solution.py:445
  124.6 1.1 shard_map.118
  125.7 8.1 %collective-permute-start.23 = (bf16[64,2304]{1,0:T(8,128)(2,1)S(1)}, bf16[64,2304]{1,0:T(8,128)(2,1)S(1)}, u32[]{:S(2)}, u32[]{:S(2)}) collective-permute-start(bf16[64,2304]{1,0:T(8,128)(2,1)S(1)} %get-tuple-element.103), channel_id=1, source_target_pairs={{0,2},{2,0},{4,6},{6,4},{8,10},{10,8},{12,14},{14,12},{16,18},{18,... | collective-permute-start | bytes 884744 | tf_op jit(solution)/shard_map/ppermute | solution.py:437
  133.8 1.1 shard_map.120
  135.0 1.3 shard_map.119
  136.3 2.4 %collective-permute-start.26 = (bf16[256,576]{1,0:T(8,128)(2,1)S(1)}, bf16[256,576]{1,0:T(8,128)(2,1)S(1)}, u32[]{:S(2)}, u32[]{:S(2)}) collective-permute-start(bf16[256,576]{1,0:T(8,128)(2,1)S(1)} %get-tuple-element.115), channel_id=1, source_target_pairs={{2,0},{4,2},{6,4},{8,6},{10,8},{12,10},{14,12},{16,14},{18,16},{20... | collective-permute-start | bytes 884744 | tf_op jit(solution)/shard_map/ppermute | solution.py:420
  138.7 1.2 shard_map.121
  140.0 3.3 %shard_map.122 = (f32[64,4096]{1,0:T(8,128)S(1)}, bf16[64,4096]{1,0:T(8,128)(2,1)S(1)}) custom-call(s32[5]{0:T(128)S(1)} %get-tuple-element.110.facts_ref, bf16[128,576]{1,0:T(8,128)(2,1)S(1)} %bitcast.12, bf16[72,4096]{1,0:T(8,128)(2,1)} %refs_0_.1, bf16[72,4096]{1,0:T(8,128)(2,1)} %collective-permute-done.11.refs_1_, ...), custom_call_target="tpu_custom_call" | custom-call | tf_op jit(solution)/shard_map/pallas_call | solution.py:626
  143.3 2.3 %collective-permute-done.26.odd_ref = bf16[256,576]{1,0:T(8,128)(2,1)S(1)} collective-permute-done((bf16[256,576]{1,0:T(8,128)(2,1)S(1)}, bf16[256,576]{1,0:T(8,128)(2,1)S(1)}, u32[]{:S(2)}, u32[]{:S(2)}) %collective-permute-start.26) | collective-permute-done | bytes 294944 | tf_op jit(solution)/shard_map/ppermute | solution.py:420
  145.6 0.9 shard_map.123
  146.6 1.3 collective-permute-start.27
  147.9 1.7 %shard_map.124 = (bf16[2304,256]{1,0:T(8,128)(2,1)S(1)}, bf16[2304,256]{1,0:T(8,128)(2,1)S(1)}, bf16[2304,256]{1,0:T(8,128)(2,1)S(1)}) custom-call(s32[5]{0:T(128)S(1)} %get-tuple-element.110.facts_ref, bf16[9,48,576]{2,1,0:T(8,128)(2,1)S(1)} %bitcast.11), custom_call_target="tpu_custom_call" | custom-call | tf_op jit(solution)/shard_map/pallas_call | solution.py:598
  149.6 2.8 %shard_map.125 = bf16[2,196,576]{2,1,0:T(8,128)(2,1)S(1)} custom-call(f32[256,576]{1,0:T(8,128)S(1)} %get-tuple-element.114.even_ref, bf16[256,576]{1,0:T(8,128)(2,1)S(1)} %collective-permute-done.26.odd_ref, f32[512,576]{1,0:T(8,128)S(1)} %copy-done.1, f32[2,576]{1,0:T(2,128)S(1)} %get-tuple-element.116.excite_ref, f32[2,288]{1,0:T(2,128)S(1)} %add.9.sq_ref, ...), custom_call_target="tpu_custom_call" | custom-call | flops 2717908992 | bytes 4718592 | tf_op jit(solution)/shard_map/pallas_call | solution.py:385
  152.4 1.2 copy.12
  153.6 0.9 add_convert_fusion
  (62 shorter events, 0.9 us)
Async XLA Ops:
  0.6 3.3 %copy-start.18 = (bf16[2,196,576]{2,0,1:T(2,128)(2,1)S(1)}, bf16[2,196,576]{2,0,1:T(2,128)(2,1)}, u32[]{:S(2)}) copy-start(bf16[2,196,576]{2,0,1:T(2,128)(2,1)} %param.9) | copy-start | bytes 1354756
  0.6 3.4 %copy-start.10 = (bf16[9,576,48]{1,2,0:T(8,128)(2,1)S(1)}, bf16[9,576,48]{1,2,0:T(8,128)(2,1)}, u32[]{:S(2)}) copy-start(bf16[9,576,48]{1,2,0:T(8,128)(2,1)} %param.10) | copy-start | bytes 1492996
  0.7 3.4 %copy-start.14 = (bf16[576,288]{0,1:T(8,128)(2,1)S(1)}, bf16[576,288]{0,1:T(8,128)(2,1)}, u32[]{:S(2)}) copy-start(bf16[576,288]{0,1:T(8,128)(2,1)} %param.11) | copy-start | bytes 995332
  2.4 8.8 %copy-start.12 = (bf16[288,576]{1,0:T(8,128)(2,1)S(1)}, bf16[288,576]{1,0:T(8,128)(2,1)}, u32[]{:S(2)}) copy-start(bf16[288,576]{1,0:T(8,128)(2,1)} %expand_ref.3) | copy-start | bytes 995332
  2.4 15.8 %collective-permute-start.2 = (bf16[72,4608]{1,0:T(8,128)(2,1)S(1)}, bf16[72,4608]{1,0:T(8,128)(2,1)S(1)}, u32[]{:S(2)}, u32[]{:S(2)}) collective-permute-start(bf16[72,4608]{1,0:T(8,128)(2,1)S(1)} %reshape.11.refs_0_.refs_4_), channel_id=1, source_target_pairs={{0,8},{2,10},{8,16},{10,18},{16,24},{18,26},{24,28},{26,30},{28,20... | collective-permute-start | bytes 1990664 | tf_op jit(solution)/shard_map/ppermute | solution.py:456
  2.5 15.9 %collective-permute-start.3 = (bf16[72,4608]{1,0:T(8,128)(2,1)S(1)}, bf16[72,4608]{1,0:T(8,128)(2,1)S(1)}, u32[]{:S(2)}, u32[]{:S(2)}) collective-permute-start(bf16[72,4608]{1,0:T(8,128)(2,1)S(1)} %reshape.11.refs_0_.refs_4_), channel_id=1, source_target_pairs={{0,4},{2,6},{8,0},{10,2},{16,8},{18,10},{24,16},{26,18},{28,24},{3... | collective-permute-start | bytes 1990664 | tf_op jit(solution)/shard_map/ppermute | solution.py:456
  8.5 29.6 %copy-start = (f32[512,576]{1,0:T(8,128)}, f32[512,576]{1,0:T(8,128)S(1)}, u32[]{:S(2)}) copy-start(f32[512,576]{1,0:T(8,128)S(1)} %get-tuple-element.61.conv_ref) | copy-start | bytes 3538948
  8.5 2.8 %collective-permute-start = (f32[2,288]{1,0:T(2,128)S(1)}, f32[2,288]{1,0:T(2,128)S(1)}, u32[]{:S(2)}, u32[]{:S(2)}) collective-permute-start(f32[2,288]{1,0:T(2,128)S(1)} %get-tuple-element.63), channel_id=1, source_target_pairs={{0,1},{1,0},{2,3},{3,2},{4,5},{5,4},{6,7},{7,6},{8,9},{9,8},{10,11... | collective-permute-start | bytes 6920 | tf_op jit(solution)/shard_map/ppermute | solution.py:445
  18.3 45.6 %copy-start.2 = (bf16[72,4608]{1,0:T(8,128)(2,1)}, bf16[72,4608]{1,0:T(8,128)(2,1)S(1)}, u32[]{:S(2)}) copy-start(bf16[72,4608]{1,0:T(8,128)(2,1)S(1)} %collective-permute-done.2.refs_1_.refs_4_) | copy-start | bytes 1990660
  18.4 19.7 %collective-permute-start.4 = (bf16[72,4608]{1,0:T(8,128)(2,1)S(1)}, bf16[72,4608]{1,0:T(8,128)(2,1)S(1)}, u32[]{:S(2)}, u32[]{:S(2)}) collective-permute-start(bf16[72,4608]{1,0:T(8,128)(2,1)S(1)} %collective-permute-done.2.refs_1_.refs_4_), channel_id=1, source_target_pairs={{0,8},{2,10},{8,16},{10,18},{16,24},{18,26},{24,28},{26,30},{28,20... | collective-permute-start | bytes 1990664 | tf_op jit(solution)/shard_map/ppermute | solution.py:456
  19.5 18.6 %collective-permute-start.5 = (bf16[72,4608]{1,0:T(8,128)(2,1)S(1)}, bf16[72,4608]{1,0:T(8,128)(2,1)}, u32[]{:S(2)}, u32[]{:S(2)}) collective-permute-start(bf16[72,4608]{1,0:T(8,128)(2,1)S(1)} %collective-permute-done.3.refs_2_.refs_5_), channel_id=1, source_target_pairs={{0,4},{2,6},{8,0},{10,2},{16,8},{18,10},{24,16},{26,18},{28,24},{3... | collective-permute-start | bytes 1990664 | tf_op jit(solution)/shard_map/ppermute | solution.py:456
  19.8 0.9 copy-start.7
  20.7 17.4 %collective-permute-start.1 = (bf16[256,576]{1,0:T(8,128)(2,1)S(1)}, bf16[256,576]{1,0:T(8,128)(2,1)S(1)}, u32[]{:S(2)}, u32[]{:S(2)}) collective-permute-start(bf16[256,576]{1,0:T(8,128)(2,1)S(1)} %get-tuple-element.64), channel_id=1, source_target_pairs={{0,2},{2,4},{4,6},{6,8},{8,10},{10,12},{12,14},{14,16},{16,18},{18... | collective-permute-start | bytes 884744 | tf_op jit(solution)/shard_map/ppermute | solution.py:420
  38.1 14.6 %collective-permute-start.6 = (bf16[72,4608]{1,0:T(8,128)(2,1)S(1)}, bf16[72,4608]{1,0:T(8,128)(2,1)S(1)}, u32[]{:S(2)}, u32[]{:S(2)}) collective-permute-start(bf16[72,4608]{1,0:T(8,128)(2,1)S(1)} %collective-permute-done.4.refs_3_.refs_5_), channel_id=1, source_target_pairs={{0,8},{2,10},{8,16},{10,18},{16,24},{18,26},{24,28},{26,30},{28,20... | collective-permute-start | bytes 1990664 | tf_op jit(solution)/shard_map/ppermute | solution.py:456
  39.3 0.8 copy-start.4
  40.1 15.5 %collective-permute-start.7 = (bf16[72,4608]{1,0:T(8,128)(2,1)}, bf16[72,4608]{1,0:T(8,128)(2,1)}, u32[]{:S(2)}, u32[]{:S(2)}) collective-permute-start(bf16[72,4608]{1,0:T(8,128)(2,1)} %collective-permute-done.5.refs_4_.refs_6_), channel_id=1, source_target_pairs={{0,4},{2,6},{8,0},{10,2},{16,8},{18,10},{24,16},{26,18},{28,24},{3... | collective-permute-start | bytes 1990664 | tf_op jit(solution)/shard_map/ppermute | solution.py:456
  41.7 0.7 copy-start.16
  42.4 19.7 %copy-start.17 = (s32[5]{0:T(128)S(1)}, s32[5]{0:T(128)}, u32[]{:S(2)}) copy-start(s32[5]{0:T(128)} %shard_map.104.facts_ref) | copy-start | bytes 64
  44.2 17.9 %collective-permute-start.10 = (bf16[64,4608]{1,0:T(8,128)(2,1)}, bf16[64,4608]{1,0:T(8,128)(2,1)}, u32[]{:S(2)}, u32[]{:S(2)}) collective-permute-start(bf16[64,4608]{1,0:T(8,128)(2,1)} %shard_map.107.own_ref), channel_id=1, source_target_pairs={{0,2},{2,0},{4,6},{6,4},{8,10},{10,8},{12,14},{14,12},{16,18},{18,... | collective-permute-start | bytes 1769480 | tf_op jit(solution)/shard_map/ppermute | solution.py:437
  55.7 16.9 %collective-permute-start.12 = (bf16[72,4608]{1,0:T(8,128)(2,1)S(1)}, bf16[72,4608]{1,0:T(8,128)(2,1)S(1)}, u32[]{:S(2)}, u32[]{:S(2)}) collective-permute-start(bf16[72,4608]{1,0:T(8,128)(2,1)S(1)} %collective-permute-done.6.refs_5_.refs_4_), channel_id=1, source_target_pairs={{0,8},{2,10},{8,16},{10,18},{16,24},{18,26},{24,28},{26,30},{28,20... | collective-permute-start | bytes 1990664 | tf_op jit(solution)/shard_map/ppermute | solution.py:456
  55.7 13.5 %collective-permute-start.11 = (bf16[72,4096]{1,0:T(8,128)(2,1)}, bf16[72,4096]{1,0:T(8,128)(2,1)}, u32[]{:S(2)}, u32[]{:S(2)}) collective-permute-start(bf16[72,4096]{1,0:T(8,128)(2,1)} %refs_0_.1), channel_id=1, source_target_pairs={{0,4},{2,6},{8,0},{10,2},{16,8},{18,10},{24,16},{26,18},{28,24},{3... | collective-permute-start | bytes 1769480 | tf_op jit(solution)/shard_map/ppermute | solution.py:456
  57.1 22.1 %all-to-all-start = ((bf16[8,8,4096]{2,1,0:T(8,128)(2,1)}), bf16[8,8,4096]{2,1,0:T(8,128)(2,1)S(1)}, u32[]{:S(2)}, u32[]{:S(2)}) async-start(bf16[8,8,4096]{2,1,0:T(8,128)(2,1)} %bitcast.15), calls=%async_computation | async-start | bytes 1048576 | tf_op jit(solution)/shard_map/all_to_all | solution.py:640
  62.1 1.9 %copy-start.5 = (bf16[72,4608]{1,0:T(8,128)(2,1)S(1)}, bf16[72,4608]{1,0:T(8,128)(2,1)}, u32[]{:S(2)}) copy-start(bf16[72,4608]{1,0:T(8,128)(2,1)} %copy-done.4) | copy-start | bytes 1990660
  62.1 1.9 %copy-start.8 = (bf16[72,4608]{1,0:T(8,128)(2,1)S(1)}, bf16[72,4608]{1,0:T(8,128)(2,1)}, u32[]{:S(2)}) copy-start(bf16[72,4608]{1,0:T(8,128)(2,1)} %copy-done.7) | copy-start | bytes 1990660
  66.9 5.7 %collective-permute-start.13 = (f32[128,504]{1,0:T(8,128)S(1)}, f32[128,504]{1,0:T(8,128)S(1)}, u32[]{:S(2)}, u32[]{:S(2)}) collective-permute-start(f32[128,504]{1,0:T(8,128)S(1)} %shard_map.109.own_ref), channel_id=1, source_target_pairs={{0,1},{1,0},{2,3},{3,2},{4,5},{5,4},{6,7},{7,6},{8,9},{9,8},{10,11... | collective-permute-start | bytes 774152 | tf_op jit(solution)/shard_map/ppermute | solution.py:445
  68.2 23.8 %collective-permute-start.9 = (bf16[72,4096]{1,0:T(8,128)(2,1)}, bf16[72,4096]{1,0:T(8,128)(2,1)}, u32[]{:S(2)}, u32[]{:S(2)}) collective-permute-start(bf16[72,4096]{1,0:T(8,128)(2,1)} %refs_0_.1), channel_id=1, source_target_pairs={{0,8},{2,10},{8,16},{10,18},{16,24},{18,26},{24,28},{26,30},{28,20... | collective-permute-start | bytes 1769480 | tf_op jit(solution)/shard_map/ppermute | solution.py:456
  72.6 23.7 %collective-permute-start.16 = (bf16[72,4096]{1,0:T(8,128)(2,1)}, bf16[72,4096]{1,0:T(8,128)(2,1)}, u32[]{:S(2)}, u32[]{:S(2)}) collective-permute-start(bf16[72,4096]{1,0:T(8,128)(2,1)} %collective-permute-done.11.refs_1_), channel_id=1, source_target_pairs={{0,4},{2,6},{8,0},{10,2},{16,8},{18,10},{24,16},{26,18},{28,24},{3... | collective-permute-start | bytes 1769480 | tf_op jit(solution)/shard_map/ppermute | solution.py:456
  74.2 3.5 %collective-permute-start.14 = (f32[128,72]{1,0:T(8,128)S(1)}, f32[128,72]{1,0:T(8,128)S(1)}, u32[]{:S(2)}, u32[]{:S(2)}) collective-permute-start(f32[128,72]{1,0:T(8,128)S(1)} %shard_map.110.own_ref), channel_id=1, source_target_pairs={{0,1},{1,0},{2,3},{3,2},{4,5},{5,4},{6,7},{7,6},{8,9},{9,8},{10,11... | collective-permute-start | bytes 110600 | tf_op jit(solution)/shard_map/ppermute | solution.py:445
  79.3 17.0 %all-to-all-start.1 = ((bf16[8,16,576]{2,1,0:T(8,128)(2,1)}), bf16[8,16,576]{2,1,0:T(8,128)(2,1)S(1)}, u32[]{:S(2)}, u32[]{:S(2)}) async-start(bf16[8,16,576]{2,1,0:T(8,128)(2,1)} %bitcast.4), calls=%async_computation.1 | async-start | bytes 327680 | tf_op jit(solution)/shard_map/all_to_all | solution.py:640
  83.9 13.8 %collective-permute-start.8 = (bf16[64,4096]{1,0:T(8,128)(2,1)S(1)}, bf16[64,4096]{1,0:T(8,128)(2,1)S(1)}, u32[]{:S(2)}, u32[]{:S(2)}) collective-permute-start(bf16[64,4096]{1,0:T(8,128)(2,1)S(1)} %bitcast.6), channel_id=1, source_target_pairs={{0,2},{2,0},{4,6},{6,4},{8,10},{10,8},{12,14},{14,12},{16,18},{18,... | collective-permute-start | bytes 1572872 | tf_op jit(solution)/shard_map/ppermute | solution.py:437
  96.2 10.4 %collective-permute-start.15 = (bf16[72,4096]{1,0:T(8,128)(2,1)}, bf16[72,4096]{1,0:T(8,128)(2,1)S(1)}, u32[]{:S(2)}, u32[]{:S(2)}) collective-permute-start(bf16[72,4096]{1,0:T(8,128)(2,1)} %collective-permute-done.9.refs_0_.refs_3_), channel_id=1, source_target_pairs={{0,8},{2,10},{8,16},{10,18},{16,24},{18,26},{24,28},{26,30},{28,20... | collective-permute-start | bytes 1769480 | tf_op jit(solution)/shard_map/ppermute | solution.py:456
  96.2 10.4 %collective-permute-start.19 = (bf16[72,4096]{1,0:T(8,128)(2,1)}, bf16[72,4096]{1,0:T(8,128)(2,1)S(1)}, u32[]{:S(2)}, u32[]{:S(2)}) collective-permute-start(bf16[72,4096]{1,0:T(8,128)(2,1)} %collective-permute-done.16.refs_2_), channel_id=1, source_target_pairs={{0,4},{2,6},{8,0},{10,2},{16,8},{18,10},{24,16},{26,18},{28,24},{3... | collective-permute-start | bytes 1769480 | tf_op jit(solution)/shard_map/ppermute | solution.py:456
  99.9 12.0 %copy-start.9 = (bf16[72,4608]{1,0:T(8,128)(2,1)S(1)}, bf16[72,4608]{1,0:T(8,128)(2,1)}, u32[]{:S(2)}) copy-start(bf16[72,4608]{1,0:T(8,128)(2,1)} %copy-done.7) | copy-start | bytes 1990660
  99.9 6.8 %collective-permute-start.17 = (f32[128,216]{1,0:T(8,128)S(1)}, f32[128,216]{1,0:T(8,128)S(1)}, u32[]{:S(2)}, u32[]{:S(2)}) collective-permute-start(f32[128,216]{1,0:T(8,128)S(1)} %shard_map.113.refs_0_), channel_id=1, source_target_pairs={{0,1},{1,0},{2,3},{3,2},{4,5},{5,4},{6,7},{7,6},{8,9},{9,8},{10,11... | collective-permute-start | bytes 331784 | tf_op jit(solution)/shard_map/ppermute | solution.py:445
  106.7 12.0 %collective-permute-start.18 = (bf16[72,4096]{1,0:T(8,128)(2,1)S(1)}, bf16[72,4096]{1,0:T(8,128)(2,1)S(1)}, u32[]{:S(2)}, u32[]{:S(2)}) collective-permute-start(bf16[72,4096]{1,0:T(8,128)(2,1)S(1)} %collective-permute-done.15.refs_1_.refs_4_), channel_id=1, source_target_pairs={{0,8},{2,10},{8,16},{10,18},{16,24},{18,26},{24,28},{26,30},{28,20... | collective-permute-start | bytes 1769480 | tf_op jit(solution)/shard_map/ppermute | solution.py:456
  106.7 12.0 %collective-permute-start.20 = (bf16[72,4096]{1,0:T(8,128)(2,1)S(1)}, bf16[72,4096]{1,0:T(8,128)(2,1)S(1)}, u32[]{:S(2)}, u32[]{:S(2)}) collective-permute-start(bf16[72,4096]{1,0:T(8,128)(2,1)S(1)} %collective-permute-done.19.refs_2_.refs_5_), channel_id=1, source_target_pairs={{0,4},{2,6},{8,0},{10,2},{16,8},{18,10},{24,16},{26,18},{28,24},{3... | collective-permute-start | bytes 1769480 | tf_op jit(solution)/shard_map/ppermute | solution.py:456
  110.5 4.2 %collective-permute-start.21 = (f32[128,216]{1,0:T(8,128)S(1)}, f32[128,216]{1,0:T(8,128)S(1)}, u32[]{:S(2)}, u32[]{:S(2)}) collective-permute-start(f32[128,216]{1,0:T(8,128)S(1)} %shard_map.114.refs_0_), channel_id=1, source_target_pairs={{0,1},{1,0},{2,3},{3,2},{4,5},{5,4},{6,7},{7,6},{8,9},{9,8},{10,11... | collective-permute-start | bytes 331784 | tf_op jit(solution)/shard_map/ppermute | solution.py:445
  111.9 2.8 %copy-start.3 = (bf16[72,4608]{1,0:T(8,128)(2,1)S(1)}, bf16[72,4608]{1,0:T(8,128)(2,1)}, u32[]{:S(2)}) copy-start(bf16[72,4608]{1,0:T(8,128)(2,1)} %copy-done.2) | copy-start | bytes 1990660
  111.9 2.8 %copy-start.6 = (bf16[72,4608]{1,0:T(8,128)(2,1)S(1)}, bf16[72,4608]{1,0:T(8,128)(2,1)}, u32[]{:S(2)}) copy-start(bf16[72,4608]{1,0:T(8,128)(2,1)} %copy-done.4) | copy-start | bytes 1990660
  119.2 5.4 %collective-permute-start.22 = (f32[128,144]{1,0:T(8,128)S(1)}, f32[128,144]{1,0:T(8,128)S(1)}, u32[]{:S(2)}, u32[]{:S(2)}) collective-permute-start(f32[128,144]{1,0:T(8,128)S(1)} %shard_map.117.refs_0_), channel_id=1, source_target_pairs={{0,1},{1,0},{2,3},{3,2},{4,5},{5,4},{6,7},{7,6},{8,9},{9,8},{10,11... | collective-permute-start | bytes 221192 | tf_op jit(solution)/shard_map/ppermute | solution.py:445
  125.7 9.3 %collective-permute-start.23 = (bf16[64,2304]{1,0:T(8,128)(2,1)S(1)}, bf16[64,2304]{1,0:T(8,128)(2,1)S(1)}, u32[]{:S(2)}, u32[]{:S(2)}) collective-permute-start(bf16[64,2304]{1,0:T(8,128)(2,1)S(1)} %get-tuple-element.103), channel_id=1, source_target_pairs={{0,2},{2,0},{4,6},{6,4},{8,10},{10,8},{12,14},{14,12},{16,18},{18,... | collective-permute-start | bytes 884744 | tf_op jit(solution)/shard_map/ppermute | solution.py:437
  134.9 3.8 %collective-permute-start.24 = (bf16[64,2304]{1,0:T(8,128)(2,1)S(1)}, bf16[64,2304]{1,0:T(8,128)(2,1)S(1)}, u32[]{:S(2)}, u32[]{:S(2)}) collective-permute-start(bf16[64,2304]{1,0:T(8,128)(2,1)S(1)} %get-tuple-element.109), channel_id=1, source_target_pairs={{0,2},{2,0},{4,6},{6,4},{8,10},{10,8},{12,14},{14,12},{16,18},{18,... | collective-permute-start | bytes 884744 | tf_op jit(solution)/shard_map/ppermute | solution.py:437
  136.3 9.3 %collective-permute-start.26 = (bf16[256,576]{1,0:T(8,128)(2,1)S(1)}, bf16[256,576]{1,0:T(8,128)(2,1)S(1)}, u32[]{:S(2)}, u32[]{:S(2)}) collective-permute-start(bf16[256,576]{1,0:T(8,128)(2,1)S(1)} %get-tuple-element.115), channel_id=1, source_target_pairs={{2,0},{4,2},{6,4},{8,6},{10,8},{12,10},{14,12},{16,14},{18,16},{20... | collective-permute-start | bytes 884744 | tf_op jit(solution)/shard_map/ppermute | solution.py:420
  140.0 5.7 %copy-start.1 = (f32[512,576]{1,0:T(8,128)S(1)}, f32[512,576]{1,0:T(8,128)}, u32[]{:S(2)}) copy-start(f32[512,576]{1,0:T(8,128)} %copy-done) | copy-start | bytes 3538948
  140.0 5.7 %copy-start.13 = (bf16[288,576]{1,0:T(8,128)(2,1)S(1)}, bf16[288,576]{1,0:T(8,128)(2,1)}, u32[]{:S(2)}) copy-start(bf16[288,576]{1,0:T(8,128)(2,1)} %expand_ref.3) | copy-start | bytes 995332
  143.3 10.3 %collective-permute-start.25 = (bf16[64,4096]{1,0:T(8,128)(2,1)S(1)}, bf16[64,4096]{1,0:T(8,128)(2,1)S(1)}, u32[]{:S(2)}, u32[]{:S(2)}) collective-permute-start(bf16[64,4096]{1,0:T(8,128)(2,1)S(1)} %get-tuple-element.113), channel_id=1, source_target_pairs={{0,2},{2,0},{4,6},{6,4},{8,10},{10,8},{12,14},{14,12},{16,18},{18,... | collective-permute-start | bytes 1572872 | tf_op jit(solution)/shard_map/ppermute | solution.py:437
  145.6 2.3 %copy-start.11 = (bf16[9,576,48]{1,2,0:T(8,128)(2,1)S(1)}, bf16[9,576,48]{1,2,0:T(8,128)(2,1)}, u32[]{:S(2)}) copy-start(bf16[9,576,48]{1,2,0:T(8,128)(2,1)} %param.10) | copy-start | bytes 1492996
  145.6 4.0 %copy-start.15 = (bf16[576,288]{0,1:T(8,128)(2,1)S(1)}, bf16[576,288]{0,1:T(8,128)(2,1)}, u32[]{:S(2)}) copy-start(bf16[576,288]{0,1:T(8,128)(2,1)} %param.11) | copy-start | bytes 995332
  146.6 3.0 %collective-permute-start.27 = (f32[2,288]{1,0:T(2,128)S(1)}, f32[2,288]{1,0:T(2,128)S(1)}, u32[]{:S(2)}, u32[]{:S(2)}) collective-permute-start(f32[2,288]{1,0:T(2,128)S(1)} %shard_map.123), channel_id=1, source_target_pairs={{0,1},{1,0},{2,3},{3,2},{4,5},{5,4},{6,7},{7,6},{8,9},{9,8},{10,11... | collective-permute-start | bytes 6920 | tf_op jit(solution)/shard_map/ppermute | solution.py:445

commit v17 on v15

--- a/solution.py
+++ b/solution.py
@@ -250,7 +250,7 @@
     width, even_ref, odd_ref, conv_ref, excite_ref, sq_ref, relaxed_ref, squeeze_ref, *refs
 ):
     *dense_refs, out_ref, flat_ref, wide_ref, shift_ref, grad_ref = refs
-    frames, _, chans = out_ref.shape
+    _, frames, chans = out_ref.shape
     rows = frames * FRAME_ROWS
     grad_squeezed = relaxed_ref[...] * silu_slope(sq_ref[...])
     pooled = jnp.dot(
@@ -280,11 +280,13 @@
         )
         end = min(chans, start + WINDOW)
         grad_ref[WIDE : WIDE + body, start:end] += total[:, : end - start]
+    cells = []
     for frame in range(frames):
         for y in range(SIDE):
             at = frame * FRAME_ROWS + (y + 1) * WIDE + 1
             flat_ref[y * SIDE : (y + 1) * SIDE, :] = grad_ref[at : at + SIDE, :]
-        out_ref[frame] = flat_ref[...].astype(jnp.bfloat16)
+        cells.append(flat_ref[...].astype(jnp.bfloat16))
+    out_ref[...] = jnp.stack(cells, axis=1)
 
 
 def f32(*shape):
@@ -384,7 +386,7 @@
     lanes = channel_blocks(chans, width)[-1][2] + WINDOW
     return whole_call(
         functools.partial(conv_grad_kernel, width),
-        bf16(frames, SIDE * SIDE, chans),
+        bf16(SIDE * SIDE, frames, chans),
         [
             pltpu.VMEM((SIDE * SIDE, chans), jnp.float32),
             pltpu.VMEM((rows + 2 * EDGE, chans), jnp.float32),
@@ -741,7 +743,7 @@
         grad_even, grad_odd, conv, excite, squeezed, grad_relaxed, squeeze_in,
         dense_weights(facts_late, group_kernel), group_kernel.shape[1],
     )
-    return (llm_tokens, grad_features)
+    return (llm_tokens, jnp.swapaxes(grad_features, 0, 1))
 
 
 def solution(mesh):

time: 154 us -> 154 us (level)
  Pallas kernels: 38.5 us -> 40.2 us
    pallas_call x1, Pallas kernels: 2.78 us -> 4.45 us  [conv_backward(): whole_call(functools.partial(conv_grad_kernel, width), bf16(SIDE * SIDE,...]
    unnamed x40 -> x39, local copies, waits for them, and re-layouts: 3.65 us -> 2.48 us
  transfers between devices with their start and end apart: 30 -> 30, of which waited for: 17 -> 17; matrix products, arithmetic and copies ran while one was open for 1% -> 0% of each run, Pallas kernels for 24% -> 25%
where the time goes in v17:
time: 154 us; the launch traced here: 153 us
  starting transfers between devices  57.5 us (37%)
  waiting for transfers between devices  49.4 us (32%)
  Pallas kernels  40.2 us (26%)
  local copies, waits for them, and re-layouts  4.24 us (3%)
    ppermute x14, waiting for transfers between devices, ring_send(): return lax.ppermute(value, 'ctx', ring_pairs(lax.axis_size('ctx'), by))  23.7 us
    ppermute x5, starting transfers between devices, swap_cores(): lax.ppermute(value, 'ctx', [(i, i ^ 1) for i in range(lax.axis_size('ctx'...  19.7 us
    ppermute x2, waiting for transfers between devices, shifted(): return lax.ppermute(value, axis, pairs)  12.8 us
    ppermute x7, waiting for transfers between devices, tp_terms(): other = lax.ppermute(value, 'tp', [(i, i ^ reach) for i in range(size)])  11.1 us
    pallas_call x7, Pallas kernels, facts_call(): pl.pallas_call(kernel, out_shape=outs, in_specs=vmem_specs(len(operands))...  10.3 us
    ppermute x14, starting transfers between devices, ring_send(): return lax.ppermute(value, 'ctx', ring_pairs(lax.axis_size('ctx'), by))  10.1 us
    ppermute x7, starting transfers between devices, tp_terms(): other = lax.ppermute(value, 'tp', [(i, i ^ reach) for i in range(size)])  9.52 us
    all_to_all x2, starting transfers between devices, chips_exchange(): lax.all_to_all(value, 'ctx', split_axis=0, concat_axis=0, tiled=True, axi...  9.5 us
  transfers between devices with their start and end apart: 30, of which 17 were waited for; matrix products, arithmetic and copies ran while one was open for 0% of the time, Pallas kernels for 25%

profile of v17, /device:TPU:3, one launch (start us, length us, event | category | flops | bytes accessed | tf_op | source)
XLA Modules:
  0.0 153.2 jit_solution(8304565816871885213)
XLA Ops:
  0.7 1.8 %reshape.11.refs_0_.refs_4_ = bf16[72,4608]{1,0:T(8,128)(2,1)S(1)} reshape(bf16[72,8,576]{2,1,0:T(8,128)(2,1)} %param.13) | data formatting | bytes 1327104 | tf_op jit(solution)/shard_map/reshape | solution.py:661
  2.5 1.5 collective-permute-start.3
  4.0 4.4 %shard_map.105 = (f32[512,576]{1,0:T(8,128)S(1)}, bf16[512,576]{1,0:T(8,128)(2,1)S(1)}, f32[2,288]{1,0:T(2,128)S(1)}) custom-call(bf16[2,196,576]{2,1,0:T(8,128)(2,1)S(1)} %copy.11.feat_ref, bf16[9,48,576]{2,1,0:T(8,128)(2,1)S(1)} %bitcast.11, bf16[288,576]{1,0:T(8,128)(2,1)S(1)} %bitcast.14), custom_call_target="tpu_custom_call" | custom-call | tf_op jit(solution)/shard_map/pallas_call | solution.py:303
  8.5 1.3 collective-permute-start
  9.8 1.5 collective-permute-done
  11.3 0.7 shard_map.106
  12.0 6.3 %collective-permute-done.2.refs_1_.refs_4_ = bf16[72,4608]{1,0:T(8,128)(2,1)S(1)} collective-permute-done((bf16[72,4608]{1,0:T(8,128)(2,1)S(1)}, bf16[72,4608]{1,0:T(8,128)(2,1)S(1)}, u32[]{:S(2)}, u32[]{:S(2)}) %collective-permute-start.2) | collective-permute-done | bytes 663584 | tf_op jit(solution)/shard_map/ppermute | solution.py:458
  18.4 1.1 collective-permute-start.4
  19.8 0.9 copy-done.7
  20.7 6.4 %collective-permute-start.1 = (bf16[256,576]{1,0:T(8,128)(2,1)S(1)}, bf16[256,576]{1,0:T(8,128)(2,1)S(1)}, u32[]{:S(2)}, u32[]{:S(2)}) collective-permute-start(bf16[256,576]{1,0:T(8,128)(2,1)S(1)} %get-tuple-element.64), channel_id=1, source_target_pairs={{0,2},{2,4},{4,6},{6,8},{8,10},{10,12},{12,14},{14,16},{16,18},{18... | collective-permute-start | bytes 884744 | tf_op jit(solution)/shard_map/ppermute | solution.py:422
  27.1 11.0 %collective-permute-done.1.halo_ref = bf16[256,576]{1,0:T(8,128)(2,1)S(1)} collective-permute-done((bf16[256,576]{1,0:T(8,128)(2,1)S(1)}, bf16[256,576]{1,0:T(8,128)(2,1)S(1)}, u32[]{:S(2)}, u32[]{:S(2)}) %collective-permute-start.1) | collective-permute-done | bytes 294944 | tf_op jit(solution)/shard_map/ppermute | solution.py:422
  38.1 1.2 collective-permute-start.6
  39.3 0.8 copy-done.4
  40.4 1.3 shard_map.104.facts_ref
  41.7 0.6 copy-done.16
  42.4 1.8 %shard_map.107.own_ref = bf16[64,4608]{1,0:T(8,128)(2,1)} custom-call(s32[5]{0:T(128)S(1)} %copy-done.16, bf16[256,576]{1,0:T(8,128)(2,1)S(1)} %collective-permute-done.1.halo_ref, bf16[256,576]{1,0:T(8,128)(2,1)S(1)} %get-tuple-element.74.even_ref), custom_call_target="tpu_custom_call" | custom-call | tf_op jit(solution)/shard_map/pallas_call | solution.py:351
  44.2 2.8 %collective-permute-start.10 = (bf16[64,4608]{1,0:T(8,128)(2,1)}, bf16[64,4608]{1,0:T(8,128)(2,1)}, u32[]{:S(2)}, u32[]{:S(2)}) collective-permute-start(bf16[64,4608]{1,0:T(8,128)(2,1)} %shard_map.107.own_ref), channel_id=1, source_target_pairs={{0,2},{2,0},{4,6},{6,4},{8,10},{10,8},{12,14},{14,12},{16,18},{18,... | collective-permute-start | bytes 1769480 | tf_op jit(solution)/shard_map/ppermute | solution.py:439
  47.0 5.6 %collective-permute-done.6.refs_0_.refs_4_ = bf16[72,4608]{1,0:T(8,128)(2,1)S(1)} collective-permute-done((bf16[72,4608]{1,0:T(8,128)(2,1)S(1)}, bf16[72,4608]{1,0:T(8,128)(2,1)S(1)}, u32[]{:S(2)}, u32[]{:S(2)}) %collective-permute-start.6) | collective-permute-done | bytes 663584 | tf_op jit(solution)/shard_map/ppermute | solution.py:458
  52.6 3.0 %collective-permute-done.7.refs_1_.refs_6_ = bf16[72,4608]{1,0:T(8,128)(2,1)} collective-permute-done((bf16[72,4608]{1,0:T(8,128)(2,1)}, bf16[72,4608]{1,0:T(8,128)(2,1)}, u32[]{:S(2)}, u32[]{:S(2)}) %collective-permute-start.7) | collective-permute-done | bytes 663584 | tf_op jit(solution)/shard_map/ppermute | solution.py:458
  55.7 1.5 collective-permute-start.11
  57.1 4.9 %all-to-all-start = ((bf16[8,8,4096]{2,1,0:T(8,128)(2,1)}), bf16[8,8,4096]{2,1,0:T(8,128)(2,1)S(1)}, u32[]{:S(2)}, u32[]{:S(2)}) async-start(bf16[8,8,4096]{2,1,0:T(8,128)(2,1)} %bitcast.16), calls=%async_computation | async-start | bytes 1048576 | tf_op jit(solution)/shard_map/all_to_all | solution.py:642
  62.1 1.8 %shard_map.108.patch_ref = bf16[128,4608]{1,0:T(8,128)(2,1)S(1)} custom-call(s32[5]{0:T(128)S(1)} %copy-done.17, bf16[64,4608]{1,0:T(8,128)(2,1)} %shard_map.107.own_ref, bf16[64,4608]{1,0:T(8,128)(2,1)} %collective-permute-done.10.mate_ref), custom_call_target="tpu_custom_call" | custom-call | tf_op jit(solution)/shard_map/pallas_call | solution.py:340
  63.9 2.3 %shard_map.109.own_ref = f32[128,360]{1,0:T(8,128)S(1)} custom-call(bf16[128,4608]{1,0:T(8,128)(2,1)S(1)} %shard_map.108.patch_ref, bf16[72,4608]{1,0:T(8,128)(2,1)S(1)} %reshape.11.refs_0_.refs_4_, bf16[72,4608]{1,0:T(8,128)(2,1)S(1)} %collective-permute-done.2.refs_1_.refs_4_, bf16[72,4608]{1,0:T(8,128)(2,1)S(1)} %copy-done.8, ...), custom_call_target="tpu_custom_call" | custom-call | tf_op jit(solution)/shard_map/pallas_call | solution.py:596
  66.2 1.3 collective-permute-start.13
  67.5 1.6 %collective-permute-done.11.refs_1_ = bf16[72,4096]{1,0:T(8,128)(2,1)} collective-permute-done((bf16[72,4096]{1,0:T(8,128)(2,1)}, bf16[72,4096]{1,0:T(8,128)(2,1)}, u32[]{:S(2)}, u32[]{:S(2)}) %collective-permute-start.11) | collective-permute-done | bytes 589856 | tf_op jit(solution)/shard_map/ppermute | solution.py:458
  69.1 2.1 %collective-permute-done.13.other_ref = f32[128,360]{1,0:T(8,128)S(1)} collective-permute-done((f32[128,360]{1,0:T(8,128)S(1)}, f32[128,360]{1,0:T(8,128)S(1)}, u32[]{:S(2)}, u32[]{:S(2)}) %collective-permute-start.13) | collective-permute-done | bytes 184352 | tf_op jit(solution)/shard_map/ppermute | solution.py:447
  71.2 1.2 collective-permute-start.16
  72.4 1.9 %shard_map.110.own_ref = f32[128,216]{1,0:T(8,128)S(1)} custom-call(bf16[128,4608]{1,0:T(8,128)(2,1)S(1)} %shard_map.108.patch_ref, bf16[72,4608]{1,0:T(8,128)(2,1)S(1)} %collective-permute-done.6.refs_0_.refs_4_, bf16[72,4608]{1,0:T(8,128)(2,1)} %collective-permute-done.7.refs_1_.refs_6_, bf16[72,4608]{1,0:T(8,128)(2,1)S(1)} %collective-permute-done.12.refs_2_.refs_5_), custom_call_target="tpu_custom_call" | custom-call | tf_op jit(solution)/shard_map/pallas_call | solution.py:596
  74.3 1.3 collective-permute-start.14
  75.6 1.0 shard_map.111
  76.6 1.8 %collective-permute-done.14.other_ref = f32[128,216]{1,0:T(8,128)S(1)} collective-permute-done((f32[128,216]{1,0:T(8,128)S(1)}, f32[128,216]{1,0:T(8,128)S(1)}, u32[]{:S(2)}, u32[]{:S(2)}) %collective-permute-start.14) | collective-permute-done | bytes 110624 | tf_op jit(solution)/shard_map/ppermute | solution.py:447
  78.4 1.7 %shard_map.112 = (f32[128,216]{1,0:T(8,128)S(1)}, bf16[128,576]{1,0:T(8,128)(2,1)}) custom-call(s32[5]{0:T(128)S(1)} %copy-done.17, f32[128,216]{1,0:T(8,128)S(1)} %shard_map.110.own_ref, f32[128,216]{1,0:T(8,128)S(1)} %collective-permute-done.14.other_ref, bf16[128,576]{1,0:T(8,128)(2,1)S(1)} %get-tuple-element.80.refs_0_), custom_call_target="tpu_custom_call" | custom-call | tf_op jit(solution)/shard_map/pallas_call | solution.py:600
  80.2 4.6 %all-to-all-start.1 = ((bf16[8,16,576]{2,1,0:T(8,128)(2,1)}), bf16[8,16,576]{2,1,0:T(8,128)(2,1)S(1)}, u32[]{:S(2)}, u32[]{:S(2)}) async-start(bf16[8,16,576]{2,1,0:T(8,128)(2,1)} %bitcast.4), calls=%async_computation.1 | async-start | bytes 327680 | tf_op jit(solution)/shard_map/all_to_all | solution.py:642
  84.8 9.4 %collective-permute-start.8 = (bf16[64,4096]{1,0:T(8,128)(2,1)S(1)}, bf16[64,4096]{1,0:T(8,128)(2,1)S(1)}, u32[]{:S(2)}, u32[]{:S(2)}) collective-permute-start(bf16[64,4096]{1,0:T(8,128)(2,1)S(1)} %bitcast.7), channel_id=1, source_target_pairs={{0,2},{2,0},{4,6},{6,4},{8,10},{10,8},{12,14},{14,12},{16,18},{18,... | collective-permute-start | bytes 1572872 | tf_op jit(solution)/shard_map/ppermute | solution.py:439
  94.2 1.8 %all-to-all-done.1 = bf16[8,16,576]{2,1,0:T(8,128)(2,1)S(1)} async-done(((bf16[8,16,576]{2,1,0:T(8,128)(2,1)}), bf16[8,16,576]{2,1,0:T(8,128)(2,1)S(1)}, u32[]{:S(2)}, u32[]{:S(2)}) %all-to-all-start.1) | async-done | bytes 147488 | tf_op jit(solution)/shard_map/all_to_all | solution.py:642
  95.9 1.5 collective-permute-start.19
  97.4 2.2 %shard_map.113.refs_0_ = f32[128,216]{1,0:T(8,128)S(1)} custom-call(bf16[64,4096]{1,0:T(8,128)(2,1)S(1)} %bitcast.8, bf16[64,4096]{1,0:T(8,128)(2,1)S(1)} %collective-permute-done.8.send_ref, bf16[72,4096]{1,0:T(8,128)(2,1)} %refs_0_.1, bf16[72,4096]{1,0:T(8,128)(2,1)} %collective-permute-done.11.refs_1_, bf16[72,4096]{1,0:T(8,128)(2,1)} %collective-permute-done.16.refs_2_), custom_call_target="tpu_custom_call" | custom-call | tf_op jit(solution)/shard_map/pallas_call | solution.py:596
  99.6 1.4 collective-permute-start.17
  101.0 2.5 %collective-permute-done.17.refs_1_ = f32[128,216]{1,0:T(8,128)S(1)} collective-permute-done((f32[128,216]{1,0:T(8,128)S(1)}, f32[128,216]{1,0:T(8,128)S(1)}, u32[]{:S(2)}, u32[]{:S(2)}) %collective-permute-start.17) | collective-permute-done | bytes 110624 | tf_op jit(solution)/shard_map/ppermute | solution.py:447
  103.5 4.3 %collective-permute-done.15.refs_1_.refs_4_ = bf16[72,4096]{1,0:T(8,128)(2,1)S(1)} collective-permute-done((bf16[72,4096]{1,0:T(8,128)(2,1)}, bf16[72,4096]{1,0:T(8,128)(2,1)S(1)}, u32[]{:S(2)}, u32[]{:S(2)}) %collective-permute-start.15) | collective-permute-done | bytes 589856 | tf_op jit(solution)/shard_map/ppermute | solution.py:458
  107.8 1.5 collective-permute-start.20
  109.3 1.8 %shard_map.114.refs_0_ = f32[128,216]{1,0:T(8,128)S(1)} custom-call(bf16[64,4096]{1,0:T(8,128)(2,1)S(1)} %bitcast.9, bf16[64,4096]{1,0:T(8,128)(2,1)S(1)} %collective-permute-done.8.send_ref, bf16[72,4096]{1,0:T(8,128)(2,1)} %collective-permute-done.9.refs_0_.refs_3_, bf16[72,4096]{1,0:T(8,128)(2,1)S(1)} %collective-permute-done.15.refs_1_.refs_4_, ...), custom_call_target="tpu_custom_call" | custom-call | tf_op jit(solution)/shard_map/pallas_call | solution.py:596
  111.2 1.5 collective-permute-start.21
  112.7 1.9 %shard_map.115 = (f32[64,2304]{1,0:T(8,128)S(1)}, f32[64,2304]{1,0:T(8,128)S(1)}, f32[64,2304]{1,0:T(8,128)S(1)}, f32[64,2304]{1,0:T(8,128)S(1)}) custom-call(s32[5]{0:T(128)S(1)} %copy-done.17, f32[128,216]{1,0:T(8,128)S(1)} %shard_map.113.refs_0_, f32[128,216]{1,0:T(8,128)S(1)} %collective-permute-done.17.refs_1_, ...), custom_call_target="tpu_custom_call" | custom-call | tf_op jit(solution)/shard_map/pallas_call | solution.py:600
  114.5 0.5 collective-permute-done.21.refs_1_
  115.0 1.9 %shard_map.116 = (f32[64,2304]{1,0:T(8,128)S(1)}, f32[64,2304]{1,0:T(8,128)S(1)}, f32[64,2304]{1,0:T(8,128)S(1)}, f32[64,2304]{1,0:T(8,128)S(1)}) custom-call(s32[5]{0:T(128)S(1)} %copy-done.17, f32[128,216]{1,0:T(8,128)S(1)} %shard_map.114.refs_0_, f32[128,216]{1,0:T(8,128)S(1)} %collective-permute-done.21.refs_1_, ...), custom_call_target="tpu_custom_call" | custom-call | tf_op jit(solution)/shard_map/pallas_call | solution.py:600
  116.9 2.7 %collective-permute-done.18.refs_0_.refs_6_ = bf16[72,4096]{1,0:T(8,128)(2,1)S(1)} collective-permute-done((bf16[72,4096]{1,0:T(8,128)(2,1)S(1)}, bf16[72,4096]{1,0:T(8,128)(2,1)S(1)}, u32[]{:S(2)}, u32[]{:S(2)}) %collective-permute-start.18) | collective-permute-done | bytes 589856 | tf_op jit(solution)/shard_map/ppermute | solution.py:458
  119.6 0.5 shard_map.117.refs_0_
  120.1 1.5 collective-permute-start.22
  121.6 2.7 %collective-permute-done.22.refs_1_ = f32[128,144]{1,0:T(8,128)S(1)} collective-permute-done((f32[128,144]{1,0:T(8,128)S(1)}, f32[128,144]{1,0:T(8,128)S(1)}, u32[]{:S(2)}, u32[]{:S(2)}) %collective-permute-start.22) | collective-permute-done | bytes 73760 | tf_op jit(solution)/shard_map/ppermute | solution.py:447
  124.3 1.0 shard_map.118
  125.3 6.8 %collective-permute-start.23 = (bf16[64,2304]{1,0:T(8,128)(2,1)S(1)}, bf16[64,2304]{1,0:T(8,128)(2,1)S(1)}, u32[]{:S(2)}, u32[]{:S(2)}) collective-permute-start(bf16[64,2304]{1,0:T(8,128)(2,1)S(1)} %get-tuple-element.103), channel_id=1, source_target_pairs={{0,2},{2,0},{4,6},{6,4},{8,10},{10,8},{12,14},{14,12},{16,18},{18,... | collective-permute-start | bytes 884744 | tf_op jit(solution)/shard_map/ppermute | solution.py:439
  132.1 1.1 shard_map.120
  133.3 1.3 shard_map.119
  134.7 2.3 %collective-permute-start.26 = (bf16[256,576]{1,0:T(8,128)(2,1)S(1)}, bf16[256,576]{1,0:T(8,128)(2,1)S(1)}, u32[]{:S(2)}, u32[]{:S(2)}) collective-permute-start(bf16[256,576]{1,0:T(8,128)(2,1)S(1)} %get-tuple-element.115), channel_id=1, source_target_pairs={{2,0},{4,2},{6,4},{8,6},{10,8},{12,10},{14,12},{16,14},{18,16},{20... | collective-permute-start | bytes 884744 | tf_op jit(solution)/shard_map/ppermute | solution.py:422
  137.0 1.2 shard_map.121
  138.3 3.3 %shard_map.122 = (f32[64,4096]{1,0:T(8,128)S(1)}, bf16[64,4096]{1,0:T(8,128)(2,1)S(1)}) custom-call(s32[5]{0:T(128)S(1)} %get-tuple-element.110.facts_ref, bf16[128,576]{1,0:T(8,128)(2,1)S(1)} %bitcast.13, bf16[72,4096]{1,0:T(8,128)(2,1)} %refs_0_.1, bf16[72,4096]{1,0:T(8,128)(2,1)} %collective-permute-done.11.refs_1_, ...), custom_call_target="tpu_custom_call" | custom-call | tf_op jit(solution)/shard_map/pallas_call | solution.py:628
  141.6 0.6 collective-permute-start.25
  142.2 1.8 %collective-permute-done.26.odd_ref = bf16[256,576]{1,0:T(8,128)(2,1)S(1)} collective-permute-done((bf16[256,576]{1,0:T(8,128)(2,1)S(1)}, bf16[256,576]{1,0:T(8,128)(2,1)S(1)}, u32[]{:S(2)}, u32[]{:S(2)}) %collective-permute-start.26) | collective-permute-done | bytes 294944 | tf_op jit(solution)/shard_map/ppermute | solution.py:422
  144.0 0.9 shard_map.123
  144.9 1.3 collective-permute-start.27
  146.1 1.7 %shard_map.124 = (bf16[2304,256]{1,0:T(8,128)(2,1)S(1)}, bf16[2304,256]{1,0:T(8,128)(2,1)S(1)}, bf16[2304,256]{1,0:T(8,128)(2,1)S(1)}) custom-call(s32[5]{0:T(128)S(1)} %get-tuple-element.110.facts_ref, bf16[9,48,576]{2,1,0:T(8,128)(2,1)S(1)} %bitcast.12), custom_call_target="tpu_custom_call" | custom-call | tf_op jit(solution)/shard_map/pallas_call | solution.py:600
  147.8 4.4 %shard_map.125 = bf16[196,2,576]{2,1,0:T(2,128)(2,1)} custom-call(f32[256,576]{1,0:T(8,128)S(1)} %get-tuple-element.114.even_ref, bf16[256,576]{1,0:T(8,128)(2,1)S(1)} %collective-permute-done.26.odd_ref, f32[512,576]{1,0:T(8,128)S(1)} %copy-done.1, f32[2,576]{1,0:T(2,128)S(1)} %get-tuple-element.116.excite_ref, f32[2,288]{1,0:T(2,128)S(1)} %add.9.sq_ref, ...), custom_call_target="tpu_custom_call" | custom-call | flops 2717908992 | bytes 4718592 | tf_op jit(solution)/shard_map/pallas_call | solution.py:387
  152.3 0.9 add_convert_fusion
  (61 shorter events, 1.1 us)
Async XLA Ops:
  0.6 3.3 %copy-start.18 = (bf16[2,196,576]{2,0,1:T(2,128)(2,1)S(1)}, bf16[2,196,576]{2,0,1:T(2,128)(2,1)}, u32[]{:S(2)}) copy-start(bf16[2,196,576]{2,0,1:T(2,128)(2,1)} %param.9) | copy-start | bytes 1354756
  0.6 3.4 %copy-start.10 = (bf16[9,576,48]{1,2,0:T(8,128)(2,1)S(1)}, bf16[9,576,48]{1,2,0:T(8,128)(2,1)}, u32[]{:S(2)}) copy-start(bf16[9,576,48]{1,2,0:T(8,128)(2,1)} %param.10) | copy-start | bytes 1492996
  0.7 3.4 %copy-start.14 = (bf16[576,288]{0,1:T(8,128)(2,1)S(1)}, bf16[576,288]{0,1:T(8,128)(2,1)}, u32[]{:S(2)}) copy-start(bf16[576,288]{0,1:T(8,128)(2,1)} %param.11) | copy-start | bytes 995332
  2.4 8.8 %copy-start.12 = (bf16[288,576]{1,0:T(8,128)(2,1)S(1)}, bf16[288,576]{1,0:T(8,128)(2,1)}, u32[]{:S(2)}) copy-start(bf16[288,576]{1,0:T(8,128)(2,1)} %expand_ref.3) | copy-start | bytes 995332
  2.4 15.8 %collective-permute-start.2 = (bf16[72,4608]{1,0:T(8,128)(2,1)S(1)}, bf16[72,4608]{1,0:T(8,128)(2,1)S(1)}, u32[]{:S(2)}, u32[]{:S(2)}) collective-permute-start(bf16[72,4608]{1,0:T(8,128)(2,1)S(1)} %reshape.11.refs_0_.refs_4_), channel_id=1, source_target_pairs={{0,8},{2,10},{8,16},{10,18},{16,24},{18,26},{24,28},{26,30},{28,20... | collective-permute-start | bytes 1990664 | tf_op jit(solution)/shard_map/ppermute | solution.py:458
  2.5 15.9 %collective-permute-start.3 = (bf16[72,4608]{1,0:T(8,128)(2,1)S(1)}, bf16[72,4608]{1,0:T(8,128)(2,1)S(1)}, u32[]{:S(2)}, u32[]{:S(2)}) collective-permute-start(bf16[72,4608]{1,0:T(8,128)(2,1)S(1)} %reshape.11.refs_0_.refs_4_), channel_id=1, source_target_pairs={{0,4},{2,6},{8,0},{10,2},{16,8},{18,10},{24,16},{26,18},{28,24},{3... | collective-permute-start | bytes 1990664 | tf_op jit(solution)/shard_map/ppermute | solution.py:458
  8.5 29.6 %copy-start = (f32[512,576]{1,0:T(8,128)}, f32[512,576]{1,0:T(8,128)S(1)}, u32[]{:S(2)}) copy-start(f32[512,576]{1,0:T(8,128)S(1)} %get-tuple-element.61.conv_ref) | copy-start | bytes 3538948
  8.5 2.8 %collective-permute-start = (f32[2,288]{1,0:T(2,128)S(1)}, f32[2,288]{1,0:T(2,128)S(1)}, u32[]{:S(2)}, u32[]{:S(2)}) collective-permute-start(f32[2,288]{1,0:T(2,128)S(1)} %get-tuple-element.63), channel_id=1, source_target_pairs={{0,1},{1,0},{2,3},{3,2},{4,5},{5,4},{6,7},{7,6},{8,9},{9,8},{10,11... | collective-permute-start | bytes 6920 | tf_op jit(solution)/shard_map/ppermute | solution.py:447
  18.3 45.6 %copy-start.2 = (bf16[72,4608]{1,0:T(8,128)(2,1)}, bf16[72,4608]{1,0:T(8,128)(2,1)S(1)}, u32[]{:S(2)}) copy-start(bf16[72,4608]{1,0:T(8,128)(2,1)S(1)} %collective-permute-done.2.refs_1_.refs_4_) | copy-start | bytes 1990660
  18.4 19.7 %collective-permute-start.4 = (bf16[72,4608]{1,0:T(8,128)(2,1)S(1)}, bf16[72,4608]{1,0:T(8,128)(2,1)S(1)}, u32[]{:S(2)}, u32[]{:S(2)}) collective-permute-start(bf16[72,4608]{1,0:T(8,128)(2,1)S(1)} %collective-permute-done.2.refs_1_.refs_4_), channel_id=1, source_target_pairs={{0,8},{2,10},{8,16},{10,18},{16,24},{18,26},{24,28},{26,30},{28,20... | collective-permute-start | bytes 1990664 | tf_op jit(solution)/shard_map/ppermute | solution.py:458
  19.5 18.6 %collective-permute-start.5 = (bf16[72,4608]{1,0:T(8,128)(2,1)S(1)}, bf16[72,4608]{1,0:T(8,128)(2,1)}, u32[]{:S(2)}, u32[]{:S(2)}) collective-permute-start(bf16[72,4608]{1,0:T(8,128)(2,1)S(1)} %collective-permute-done.3.refs_2_.refs_5_), channel_id=1, source_target_pairs={{0,4},{2,6},{8,0},{10,2},{16,8},{18,10},{24,16},{26,18},{28,24},{3... | collective-permute-start | bytes 1990664 | tf_op jit(solution)/shard_map/ppermute | solution.py:458
  19.8 0.9 copy-start.7
  20.7 17.4 %collective-permute-start.1 = (bf16[256,576]{1,0:T(8,128)(2,1)S(1)}, bf16[256,576]{1,0:T(8,128)(2,1)S(1)}, u32[]{:S(2)}, u32[]{:S(2)}) collective-permute-start(bf16[256,576]{1,0:T(8,128)(2,1)S(1)} %get-tuple-element.64), channel_id=1, source_target_pairs={{0,2},{2,4},{4,6},{6,8},{8,10},{10,12},{12,14},{14,16},{16,18},{18... | collective-permute-start | bytes 884744 | tf_op jit(solution)/shard_map/ppermute | solution.py:422
  38.1 14.6 %collective-permute-start.6 = (bf16[72,4608]{1,0:T(8,128)(2,1)S(1)}, bf16[72,4608]{1,0:T(8,128)(2,1)S(1)}, u32[]{:S(2)}, u32[]{:S(2)}) collective-permute-start(bf16[72,4608]{1,0:T(8,128)(2,1)S(1)} %collective-permute-done.4.refs_3_.refs_5_), channel_id=1, source_target_pairs={{0,8},{2,10},{8,16},{10,18},{16,24},{18,26},{24,28},{26,30},{28,20... | collective-permute-start | bytes 1990664 | tf_op jit(solution)/shard_map/ppermute | solution.py:458
  39.3 0.8 copy-start.4
  40.1 15.5 %collective-permute-start.7 = (bf16[72,4608]{1,0:T(8,128)(2,1)}, bf16[72,4608]{1,0:T(8,128)(2,1)}, u32[]{:S(2)}, u32[]{:S(2)}) collective-permute-start(bf16[72,4608]{1,0:T(8,128)(2,1)} %collective-permute-done.5.refs_4_.refs_6_), channel_id=1, source_target_pairs={{0,4},{2,6},{8,0},{10,2},{16,8},{18,10},{24,16},{26,18},{28,24},{3... | collective-permute-start | bytes 1990664 | tf_op jit(solution)/shard_map/ppermute | solution.py:458
  41.7 0.7 copy-start.16
  42.4 19.7 %copy-start.17 = (s32[5]{0:T(128)S(1)}, s32[5]{0:T(128)}, u32[]{:S(2)}) copy-start(s32[5]{0:T(128)} %shard_map.104.facts_ref) | copy-start | bytes 64
  44.2 17.9 %collective-permute-start.10 = (bf16[64,4608]{1,0:T(8,128)(2,1)}, bf16[64,4608]{1,0:T(8,128)(2,1)}, u32[]{:S(2)}, u32[]{:S(2)}) collective-permute-start(bf16[64,4608]{1,0:T(8,128)(2,1)} %shard_map.107.own_ref), channel_id=1, source_target_pairs={{0,2},{2,0},{4,6},{6,4},{8,10},{10,8},{12,14},{14,12},{16,18},{18,... | collective-permute-start | bytes 1769480 | tf_op jit(solution)/shard_map/ppermute | solution.py:439
  55.7 15.5 %collective-permute-start.12 = (bf16[72,4608]{1,0:T(8,128)(2,1)S(1)}, bf16[72,4608]{1,0:T(8,128)(2,1)S(1)}, u32[]{:S(2)}, u32[]{:S(2)}) collective-permute-start(bf16[72,4608]{1,0:T(8,128)(2,1)S(1)} %collective-permute-done.6.refs_0_.refs_4_), channel_id=1, source_target_pairs={{0,8},{2,10},{8,16},{10,18},{16,24},{18,26},{24,28},{26,30},{28,20... | collective-permute-start | bytes 1990664 | tf_op jit(solution)/shard_map/ppermute | solution.py:458
  55.7 13.5 %collective-permute-start.11 = (bf16[72,4096]{1,0:T(8,128)(2,1)}, bf16[72,4096]{1,0:T(8,128)(2,1)}, u32[]{:S(2)}, u32[]{:S(2)}) collective-permute-start(bf16[72,4096]{1,0:T(8,128)(2,1)} %refs_0_.1), channel_id=1, source_target_pairs={{0,4},{2,6},{8,0},{10,2},{16,8},{18,10},{24,16},{26,18},{28,24},{3... | collective-permute-start | bytes 1769480 | tf_op jit(solution)/shard_map/ppermute | solution.py:458
  57.1 23.0 %all-to-all-start = ((bf16[8,8,4096]{2,1,0:T(8,128)(2,1)}), bf16[8,8,4096]{2,1,0:T(8,128)(2,1)S(1)}, u32[]{:S(2)}, u32[]{:S(2)}) async-start(bf16[8,8,4096]{2,1,0:T(8,128)(2,1)} %bitcast.16), calls=%async_computation | async-start | bytes 1048576 | tf_op jit(solution)/shard_map/all_to_all | solution.py:642
  62.1 1.9 %copy-start.5 = (bf16[72,4608]{1,0:T(8,128)(2,1)S(1)}, bf16[72,4608]{1,0:T(8,128)(2,1)}, u32[]{:S(2)}) copy-start(bf16[72,4608]{1,0:T(8,128)(2,1)} %copy-done.4) | copy-start | bytes 1990660
  62.1 1.9 %copy-start.8 = (bf16[72,4608]{1,0:T(8,128)(2,1)S(1)}, bf16[72,4608]{1,0:T(8,128)(2,1)}, u32[]{:S(2)}) copy-start(bf16[72,4608]{1,0:T(8,128)(2,1)} %copy-done.7) | copy-start | bytes 1990660
  66.2 5.0 %collective-permute-start.13 = (f32[128,360]{1,0:T(8,128)S(1)}, f32[128,360]{1,0:T(8,128)S(1)}, u32[]{:S(2)}, u32[]{:S(2)}) collective-permute-start(f32[128,360]{1,0:T(8,128)S(1)} %shard_map.109.own_ref), channel_id=1, source_target_pairs={{0,1},{1,0},{2,3},{3,2},{4,5},{5,4},{6,7},{7,6},{8,9},{9,8},{10,11... | collective-permute-start | bytes 552968 | tf_op jit(solution)/shard_map/ppermute | solution.py:447
  67.5 26.6 %collective-permute-start.9 = (bf16[72,4096]{1,0:T(8,128)(2,1)}, bf16[72,4096]{1,0:T(8,128)(2,1)}, u32[]{:S(2)}, u32[]{:S(2)}) collective-permute-start(bf16[72,4096]{1,0:T(8,128)(2,1)} %refs_0_.1), channel_id=1, source_target_pairs={{0,8},{2,10},{8,16},{10,18},{16,24},{18,26},{24,28},{26,30},{28,20... | collective-permute-start | bytes 1769480 | tf_op jit(solution)/shard_map/ppermute | solution.py:458
  71.2 24.7 %collective-permute-start.16 = (bf16[72,4096]{1,0:T(8,128)(2,1)}, bf16[72,4096]{1,0:T(8,128)(2,1)}, u32[]{:S(2)}, u32[]{:S(2)}) collective-permute-start(bf16[72,4096]{1,0:T(8,128)(2,1)} %collective-permute-done.11.refs_1_), channel_id=1, source_target_pairs={{0,4},{2,6},{8,0},{10,2},{16,8},{18,10},{24,16},{26,18},{28,24},{3... | collective-permute-start | bytes 1769480 | tf_op jit(solution)/shard_map/ppermute | solution.py:458
  74.3 4.2 %collective-permute-start.14 = (f32[128,216]{1,0:T(8,128)S(1)}, f32[128,216]{1,0:T(8,128)S(1)}, u32[]{:S(2)}, u32[]{:S(2)}) collective-permute-start(f32[128,216]{1,0:T(8,128)S(1)} %shard_map.110.own_ref), channel_id=1, source_target_pairs={{0,1},{1,0},{2,3},{3,2},{4,5},{5,4},{6,7},{7,6},{8,9},{9,8},{10,11... | collective-permute-start | bytes 331784 | tf_op jit(solution)/shard_map/ppermute | solution.py:447
  80.2 15.8 %all-to-all-start.1 = ((bf16[8,16,576]{2,1,0:T(8,128)(2,1)}), bf16[8,16,576]{2,1,0:T(8,128)(2,1)S(1)}, u32[]{:S(2)}, u32[]{:S(2)}) async-start(bf16[8,16,576]{2,1,0:T(8,128)(2,1)} %bitcast.4), calls=%async_computation.1 | async-start | bytes 327680 | tf_op jit(solution)/shard_map/all_to_all | solution.py:642
  84.8 12.6 %collective-permute-start.8 = (bf16[64,4096]{1,0:T(8,128)(2,1)S(1)}, bf16[64,4096]{1,0:T(8,128)(2,1)S(1)}, u32[]{:S(2)}, u32[]{:S(2)}) collective-permute-start(bf16[64,4096]{1,0:T(8,128)(2,1)S(1)} %bitcast.7), channel_id=1, source_target_pairs={{0,2},{2,0},{4,6},{6,4},{8,10},{10,8},{12,14},{14,12},{16,18},{18,... | collective-permute-start | bytes 1572872 | tf_op jit(solution)/shard_map/ppermute | solution.py:439
  95.9 11.9 %collective-permute-start.15 = (bf16[72,4096]{1,0:T(8,128)(2,1)}, bf16[72,4096]{1,0:T(8,128)(2,1)S(1)}, u32[]{:S(2)}, u32[]{:S(2)}) collective-permute-start(bf16[72,4096]{1,0:T(8,128)(2,1)} %collective-permute-done.9.refs_0_.refs_3_), channel_id=1, source_target_pairs={{0,8},{2,10},{8,16},{10,18},{16,24},{18,26},{24,28},{26,30},{28,20... | collective-permute-start | bytes 1769480 | tf_op jit(solution)/shard_map/ppermute | solution.py:458
  95.9 11.9 %collective-permute-start.19 = (bf16[72,4096]{1,0:T(8,128)(2,1)}, bf16[72,4096]{1,0:T(8,128)(2,1)S(1)}, u32[]{:S(2)}, u32[]{:S(2)}) collective-permute-start(bf16[72,4096]{1,0:T(8,128)(2,1)} %collective-permute-done.16.refs_2_), channel_id=1, source_target_pairs={{0,4},{2,6},{8,0},{10,2},{16,8},{18,10},{24,16},{26,18},{28,24},{3... | collective-permute-start | bytes 1769480 | tf_op jit(solution)/shard_map/ppermute | solution.py:458
  99.6 13.1 %copy-start.9 = (bf16[72,4608]{1,0:T(8,128)(2,1)S(1)}, bf16[72,4608]{1,0:T(8,128)(2,1)}, u32[]{:S(2)}) copy-start(bf16[72,4608]{1,0:T(8,128)(2,1)} %copy-done.7) | copy-start | bytes 1990660
  99.6 3.9 %collective-permute-start.17 = (f32[128,216]{1,0:T(8,128)S(1)}, f32[128,216]{1,0:T(8,128)S(1)}, u32[]{:S(2)}, u32[]{:S(2)}) collective-permute-start(f32[128,216]{1,0:T(8,128)S(1)} %shard_map.113.refs_0_), channel_id=1, source_target_pairs={{0,1},{1,0},{2,3},{3,2},{4,5},{5,4},{6,7},{7,6},{8,9},{9,8},{10,11... | collective-permute-start | bytes 331784 | tf_op jit(solution)/shard_map/ppermute | solution.py:447
  107.8 11.8 %collective-permute-start.18 = (bf16[72,4096]{1,0:T(8,128)(2,1)S(1)}, bf16[72,4096]{1,0:T(8,128)(2,1)S(1)}, u32[]{:S(2)}, u32[]{:S(2)}) collective-permute-start(bf16[72,4096]{1,0:T(8,128)(2,1)S(1)} %collective-permute-done.15.refs_1_.refs_4_), channel_id=1, source_target_pairs={{0,8},{2,10},{8,16},{10,18},{16,24},{18,26},{24,28},{26,30},{28,20... | collective-permute-start | bytes 1769480 | tf_op jit(solution)/shard_map/ppermute | solution.py:458
  107.8 11.8 %collective-permute-start.20 = (bf16[72,4096]{1,0:T(8,128)(2,1)S(1)}, bf16[72,4096]{1,0:T(8,128)(2,1)S(1)}, u32[]{:S(2)}, u32[]{:S(2)}) collective-permute-start(bf16[72,4096]{1,0:T(8,128)(2,1)S(1)} %collective-permute-done.19.refs_2_.refs_5_), channel_id=1, source_target_pairs={{0,4},{2,6},{8,0},{10,2},{16,8},{18,10},{24,16},{26,18},{28,24},{3... | collective-permute-start | bytes 1769480 | tf_op jit(solution)/shard_map/ppermute | solution.py:458
  111.2 3.9 %collective-permute-start.21 = (f32[128,216]{1,0:T(8,128)S(1)}, f32[128,216]{1,0:T(8,128)S(1)}, u32[]{:S(2)}, u32[]{:S(2)}) collective-permute-start(f32[128,216]{1,0:T(8,128)S(1)} %shard_map.114.refs_0_), channel_id=1, source_target_pairs={{0,1},{1,0},{2,3},{3,2},{4,5},{5,4},{6,7},{7,6},{8,9},{9,8},{10,11... | collective-permute-start | bytes 331784 | tf_op jit(solution)/shard_map/ppermute | solution.py:447
  112.7 2.4 %copy-start.3 = (bf16[72,4608]{1,0:T(8,128)(2,1)S(1)}, bf16[72,4608]{1,0:T(8,128)(2,1)}, u32[]{:S(2)}) copy-start(bf16[72,4608]{1,0:T(8,128)(2,1)} %copy-done.2) | copy-start | bytes 1990660
  112.7 2.4 %copy-start.6 = (bf16[72,4608]{1,0:T(8,128)(2,1)S(1)}, bf16[72,4608]{1,0:T(8,128)(2,1)}, u32[]{:S(2)}) copy-start(bf16[72,4608]{1,0:T(8,128)(2,1)} %copy-done.4) | copy-start | bytes 1990660
  120.1 4.2 %collective-permute-start.22 = (f32[128,144]{1,0:T(8,128)S(1)}, f32[128,144]{1,0:T(8,128)S(1)}, u32[]{:S(2)}, u32[]{:S(2)}) collective-permute-start(f32[128,144]{1,0:T(8,128)S(1)} %shard_map.117.refs_0_), channel_id=1, source_target_pairs={{0,1},{1,0},{2,3},{3,2},{4,5},{5,4},{6,7},{7,6},{8,9},{9,8},{10,11... | collective-permute-start | bytes 221192 | tf_op jit(solution)/shard_map/ppermute | solution.py:447
  125.3 8.0 %collective-permute-start.23 = (bf16[64,2304]{1,0:T(8,128)(2,1)S(1)}, bf16[64,2304]{1,0:T(8,128)(2,1)S(1)}, u32[]{:S(2)}, u32[]{:S(2)}) collective-permute-start(bf16[64,2304]{1,0:T(8,128)(2,1)S(1)} %get-tuple-element.103), channel_id=1, source_target_pairs={{0,2},{2,0},{4,6},{6,4},{8,10},{10,8},{12,14},{14,12},{16,18},{18,... | collective-permute-start | bytes 884744 | tf_op jit(solution)/shard_map/ppermute | solution.py:439
  133.2 3.8 %collective-permute-start.24 = (bf16[64,2304]{1,0:T(8,128)(2,1)S(1)}, bf16[64,2304]{1,0:T(8,128)(2,1)S(1)}, u32[]{:S(2)}, u32[]{:S(2)}) collective-permute-start(bf16[64,2304]{1,0:T(8,128)(2,1)S(1)} %get-tuple-element.109), channel_id=1, source_target_pairs={{0,2},{2,0},{4,6},{6,4},{8,10},{10,8},{12,14},{14,12},{16,18},{18,... | collective-permute-start | bytes 884744 | tf_op jit(solution)/shard_map/ppermute | solution.py:439
  134.7 9.3 %collective-permute-start.26 = (bf16[256,576]{1,0:T(8,128)(2,1)S(1)}, bf16[256,576]{1,0:T(8,128)(2,1)S(1)}, u32[]{:S(2)}, u32[]{:S(2)}) collective-permute-start(bf16[256,576]{1,0:T(8,128)(2,1)S(1)} %get-tuple-element.115), channel_id=1, source_target_pairs={{2,0},{4,2},{6,4},{8,6},{10,8},{12,10},{14,12},{16,14},{18,16},{20... | collective-permute-start | bytes 884744 | tf_op jit(solution)/shard_map/ppermute | solution.py:422
  138.3 5.7 %copy-start.1 = (f32[512,576]{1,0:T(8,128)S(1)}, f32[512,576]{1,0:T(8,128)}, u32[]{:S(2)}) copy-start(f32[512,576]{1,0:T(8,128)} %copy-done) | copy-start | bytes 3538948
  138.3 5.7 %copy-start.13 = (bf16[288,576]{1,0:T(8,128)(2,1)S(1)}, bf16[288,576]{1,0:T(8,128)(2,1)}, u32[]{:S(2)}) copy-start(bf16[288,576]{1,0:T(8,128)(2,1)} %expand_ref.3) | copy-start | bytes 995332
  141.6 10.7 %collective-permute-start.25 = (bf16[64,4096]{1,0:T(8,128)(2,1)S(1)}, bf16[64,4096]{1,0:T(8,128)(2,1)S(1)}, u32[]{:S(2)}, u32[]{:S(2)}) collective-permute-start(bf16[64,4096]{1,0:T(8,128)(2,1)S(1)} %get-tuple-element.113), channel_id=1, source_target_pairs={{0,2},{2,0},{4,6},{6,4},{8,10},{10,8},{12,14},{14,12},{16,18},{18,... | collective-permute-start | bytes 1572872 | tf_op jit(solution)/shard_map/ppermute | solution.py:439
  143.9 2.2 %copy-start.11 = (bf16[9,576,48]{1,2,0:T(8,128)(2,1)S(1)}, bf16[9,576,48]{1,2,0:T(8,128)(2,1)}, u32[]{:S(2)}) copy-start(bf16[9,576,48]{1,2,0:T(8,128)(2,1)} %param.10) | copy-start | bytes 1492996
  144.0 3.9 %copy-start.15 = (bf16[576,288]{0,1:T(8,128)(2,1)S(1)}, bf16[576,288]{0,1:T(8,128)(2,1)}, u32[]{:S(2)}) copy-start(bf16[576,288]{0,1:T(8,128)(2,1)} %param.11) | copy-start | bytes 995332
  144.9 2.9 %collective-permute-start.27 = (f32[2,288]{1,0:T(2,128)S(1)}, f32[2,288]{1,0:T(2,128)S(1)}, u32[]{:S(2)}, u32[]{:S(2)}) collective-permute-start(f32[2,288]{1,0:T(2,128)S(1)} %shard_map.123), channel_id=1, source_target_pairs={{0,1},{1,0},{2,3},{3,2},{4,5},{5,4},{6,7},{7,6},{8,9},{9,8},{10,11... | collective-permute-start | bytes 6920 | tf_op jit(solution)/shard_map/ppermute | solution.py:447

commit v18 on v15

--- a/solution.py
+++ b/solution.py
@@ -695,14 +695,14 @@
         facts, tp_terms(last_pre), offsets[count:], chips, (first_act,), unit
     )
     slopes = first_slope, last_slope
-    r_up[1], act = tie(r_up[1], chips_exchange(act))
+    r_up[1], act = tie(r_up[1], act)
     for step in range(1, steps - 2):
         r_down.append(ring_send(r_down[-1], -1))
         r_up.append(ring_send(r_up[-1], 1))
     r_down.append(ring_send(r_down[-1], -1))
     early = r_down[: steps - 1]
     sums = block_products(back_kernel, back, early)
-    r_up[-1], *terms = tie(r_up[-1], *tp_terms(sums))
+    r_up[-1], act, *terms = tie(r_up[-1], chips_exchange(act), *tp_terms(sums))
     r_up.append(ring_send(r_up[-1], 1))
     halo_lanes, even_lanes = slice(0, 4 * chans), slice(4 * chans, 8 * chans)
     both = halo_lanes, even_lanes

time: 154 us -> 154 us (level)
  waiting for transfers between devices: 49.4 us -> 44.4 us
  starting transfers between devices: 57.5 us -> 60.3 us
  Pallas kernels: 38.5 us -> 40.4 us
    ppermute x14, waiting for transfers between devices: 23.7 us -> 17.4 us  [ring_send(): return lax.ppermute(value, 'ctx', ring_pairs(lax.axis_size('ctx'), by))]
    all_to_all x2, waiting for transfers between devices: 1.78 us -> 7.79 us  [chips_exchange(): lax.all_to_all(value, 'ctx', split_axis=0, concat_axis=0, tiled=True, axi...]
    ppermute x7, waiting for transfers between devices: 11.1 us -> 6.67 us  [tp_terms(): other = lax.ppermute(value, 'tp', [(i, i ^ reach) for i in range(size)])]
    ppermute x5, starting transfers between devices: 19.7 us -> 21.9 us  [swap_cores(): lax.ppermute(value, 'ctx', [(i, i ^ 1) for i in range(lax.axis_size('ctx'...]
    pallas_call x5, Pallas kernels: 8.63 us -> 10.3 us  [block_products(): whole_call(kernel, f32(rows, len(blocks) * blocks[0].shape[0]), [])]
    unnamed x40 -> x46, local copies, waits for them, and re-layouts: 3.65 us -> 4.58 us
  transfers between devices with their start and end apart: 30 -> 30, of which waited for: 17 -> 15; matrix products, arithmetic and copies ran while one was open for 1% -> 1% of each run, Pallas kernels for 24% -> 25%
where the time goes in v18:
time: 154 us; the launch traced here: 153 us
  starting transfers between devices  60.3 us (39%)
  waiting for transfers between devices  44.4 us (29%)
  Pallas kernels  40.4 us (26%)
  local copies, waits for them, and re-layouts  6.34 us (4%)
    ppermute x5, starting transfers between devices, swap_cores(): lax.ppermute(value, 'ctx', [(i, i ^ 1) for i in range(lax.axis_size('ctx'...  21.9 us
    ppermute x14, waiting for transfers between devices, ring_send(): return lax.ppermute(value, 'ctx', ring_pairs(lax.axis_size('ctx'), by))  17.4 us
    ppermute x2, waiting for transfers between devices, shifted(): return lax.ppermute(value, axis, pairs)  12.4 us
    ppermute x14, starting transfers between devices, ring_send(): return lax.ppermute(value, 'ctx', ring_pairs(lax.axis_size('ctx'), by))  11.5 us
    pallas_call x5, Pallas kernels, block_products(): whole_call(kernel, f32(rows, len(blocks) * blocks[0].shape[0]), [])  10.3 us
    pallas_call x7, Pallas kernels, facts_call(): pl.pallas_call(kernel, out_shape=outs, in_specs=vmem_specs(len(operands))...  10.2 us
    ppermute x7, starting transfers between devices, tp_terms(): other = lax.ppermute(value, 'tp', [(i, i ^ reach) for i in range(size)])  9.32 us
    all_to_all x2, starting transfers between devices, chips_exchange(): lax.all_to_all(value, 'ctx', split_axis=0, concat_axis=0, tiled=True, axi...  8.83 us
  transfers between devices with their start and end apart: 30, of which 15 were waited for; matrix products, arithmetic and copies ran while one was open for 1% of the time, Pallas kernels for 25%

profile of v18, /device:TPU:3, one launch (start us, length us, event | category | flops | bytes accessed | tf_op | source)
XLA Modules:
  0.0 153.4 jit_solution(1966066550476638323)
XLA Ops:
  0.7 1.8 %reshape.11.refs_0_.refs_4_ = bf16[72,4608]{1,0:T(8,128)(2,1)S(1)} reshape(bf16[72,8,576]{2,1,0:T(8,128)(2,1)} %param.13) | data formatting | bytes 1327104 | tf_op jit(solution)/shard_map/reshape | solution.py:659
  2.5 1.5 collective-permute-start.3
  4.0 4.4 %shard_map.105 = (f32[512,576]{1,0:T(8,128)S(1)}, bf16[512,576]{1,0:T(8,128)(2,1)S(1)}, f32[2,288]{1,0:T(2,128)S(1)}) custom-call(bf16[2,196,576]{2,1,0:T(8,128)(2,1)S(1)} %copy.11.feat_ref, bf16[9,48,576]{2,1,0:T(8,128)(2,1)S(1)} %bitcast.10, bf16[288,576]{1,0:T(8,128)(2,1)S(1)} %bitcast.13), custom_call_target="tpu_custom_call" | custom-call | tf_op jit(solution)/shard_map/pallas_call | solution.py:301
  8.5 1.3 collective-permute-start
  9.8 1.5 collective-permute-done
  11.3 0.7 shard_map.106
  12.0 6.3 %collective-permute-done.2.refs_1_.refs_4_ = bf16[72,4608]{1,0:T(8,128)(2,1)S(1)} collective-permute-done((bf16[72,4608]{1,0:T(8,128)(2,1)S(1)}, bf16[72,4608]{1,0:T(8,128)(2,1)S(1)}, u32[]{:S(2)}, u32[]{:S(2)}) %collective-permute-start.2) | collective-permute-done | bytes 663584 | tf_op jit(solution)/shard_map/ppermute | solution.py:456
  18.4 1.1 collective-permute-start.4
  19.8 0.8 copy-done.7
  20.7 6.4 %collective-permute-start.1 = (bf16[256,576]{1,0:T(8,128)(2,1)S(1)}, bf16[256,576]{1,0:T(8,128)(2,1)S(1)}, u32[]{:S(2)}, u32[]{:S(2)}) collective-permute-start(bf16[256,576]{1,0:T(8,128)(2,1)S(1)} %get-tuple-element.65), channel_id=1, source_target_pairs={{0,2},{2,4},{4,6},{6,8},{8,10},{10,12},{12,14},{14,16},{16,18},{18... | collective-permute-start | bytes 884744 | tf_op jit(solution)/shard_map/ppermute | solution.py:420
  27.0 11.0 %collective-permute-done.1.halo_ref = bf16[256,576]{1,0:T(8,128)(2,1)S(1)} collective-permute-done((bf16[256,576]{1,0:T(8,128)(2,1)S(1)}, bf16[256,576]{1,0:T(8,128)(2,1)S(1)}, u32[]{:S(2)}, u32[]{:S(2)}) %collective-permute-start.1) | collective-permute-done | bytes 294944 | tf_op jit(solution)/shard_map/ppermute | solution.py:420
  38.1 1.2 collective-permute-start.6
  39.3 0.8 copy-done.4
  40.4 1.3 shard_map.104.facts_ref
  41.7 0.6 copy-done.19
  42.4 1.8 %shard_map.107.own_ref = bf16[64,4608]{1,0:T(8,128)(2,1)} custom-call(s32[5]{0:T(128)S(1)} %copy-done.19, bf16[256,576]{1,0:T(8,128)(2,1)S(1)} %collective-permute-done.1.halo_ref, bf16[256,576]{1,0:T(8,128)(2,1)S(1)} %get-tuple-element.75.even_ref), custom_call_target="tpu_custom_call" | custom-call | tf_op jit(solution)/shard_map/pallas_call | solution.py:349
  44.2 2.8 %collective-permute-start.10 = (bf16[64,4608]{1,0:T(8,128)(2,1)}, bf16[64,4608]{1,0:T(8,128)(2,1)}, u32[]{:S(2)}, u32[]{:S(2)}) collective-permute-start(bf16[64,4608]{1,0:T(8,128)(2,1)} %shard_map.107.own_ref), channel_id=1, source_target_pairs={{0,2},{2,0},{4,6},{6,4},{8,10},{10,8},{12,14},{14,12},{16,18},{18,... | collective-permute-start | bytes 1769480 | tf_op jit(solution)/shard_map/ppermute | solution.py:437
  47.0 5.6 %collective-permute-done.6.refs_0_.refs_4_ = bf16[72,4608]{1,0:T(8,128)(2,1)S(1)} collective-permute-done((bf16[72,4608]{1,0:T(8,128)(2,1)S(1)}, bf16[72,4608]{1,0:T(8,128)(2,1)S(1)}, u32[]{:S(2)}, u32[]{:S(2)}) %collective-permute-start.6) | collective-permute-done | bytes 663584 | tf_op jit(solution)/shard_map/ppermute | solution.py:456
  52.6 3.0 %collective-permute-done.7.refs_1_.refs_6_ = bf16[72,4608]{1,0:T(8,128)(2,1)} collective-permute-done((bf16[72,4608]{1,0:T(8,128)(2,1)}, bf16[72,4608]{1,0:T(8,128)(2,1)}, u32[]{:S(2)}, u32[]{:S(2)}) %collective-permute-start.7) | collective-permute-done | bytes 663584 | tf_op jit(solution)/shard_map/ppermute | solution.py:456
  55.7 1.5 collective-permute-start.11
  57.1 4.9 %all-to-all-start = ((bf16[8,8,4096]{2,1,0:T(8,128)(2,1)}), bf16[8,8,4096]{2,1,0:T(8,128)(2,1)S(1)}, u32[]{:S(2)}, u32[]{:S(2)}) async-start(bf16[8,8,4096]{2,1,0:T(8,128)(2,1)} %bitcast.16), calls=%async_computation | async-start | bytes 1048576 | tf_op jit(solution)/shard_map/all_to_all | solution.py:640
  62.1 1.8 %shard_map.108.patch_ref = bf16[128,4608]{1,0:T(8,128)(2,1)S(1)} custom-call(s32[5]{0:T(128)S(1)} %copy-done.20, bf16[64,4608]{1,0:T(8,128)(2,1)} %shard_map.107.own_ref, bf16[64,4608]{1,0:T(8,128)(2,1)} %collective-permute-done.10.mate_ref), custom_call_target="tpu_custom_call" | custom-call | tf_op jit(solution)/shard_map/pallas_call | solution.py:338
  63.9 2.3 %shard_map.109.own_ref = f32[128,360]{1,0:T(8,128)S(1)} custom-call(bf16[128,4608]{1,0:T(8,128)(2,1)S(1)} %shard_map.108.patch_ref, bf16[72,4608]{1,0:T(8,128)(2,1)S(1)} %reshape.11.refs_0_.refs_4_, bf16[72,4608]{1,0:T(8,128)(2,1)S(1)} %collective-permute-done.2.refs_1_.refs_4_, bf16[72,4608]{1,0:T(8,128)(2,1)S(1)} %copy-done.8, ...), custom_call_target="tpu_custom_call" | custom-call | tf_op jit(solution)/shard_map/pallas_call | solution.py:594
  66.2 1.3 collective-permute-start.13
  67.5 1.6 %collective-permute-done.11.refs_1_ = bf16[72,4096]{1,0:T(8,128)(2,1)} collective-permute-done((bf16[72,4096]{1,0:T(8,128)(2,1)}, bf16[72,4096]{1,0:T(8,128)(2,1)}, u32[]{:S(2)}, u32[]{:S(2)}) %collective-permute-start.11) | collective-permute-done | bytes 589856 | tf_op jit(solution)/shard_map/ppermute | solution.py:456
  69.1 2.1 %collective-permute-done.13.other_ref = f32[128,360]{1,0:T(8,128)S(1)} collective-permute-done((f32[128,360]{1,0:T(8,128)S(1)}, f32[128,360]{1,0:T(8,128)S(1)}, u32[]{:S(2)}, u32[]{:S(2)}) %collective-permute-start.13) | collective-permute-done | bytes 184352 | tf_op jit(solution)/shard_map/ppermute | solution.py:445
  71.2 1.2 collective-permute-start.16
  72.4 2.5 %shard_map.110.own_ref = f32[128,216]{1,0:T(8,128)} custom-call(bf16[128,4608]{1,0:T(8,128)(2,1)S(1)} %shard_map.108.patch_ref, bf16[72,4608]{1,0:T(8,128)(2,1)S(1)} %collective-permute-done.6.refs_0_.refs_4_, bf16[72,4608]{1,0:T(8,128)(2,1)} %collective-permute-done.7.refs_1_.refs_6_, bf16[72,4608]{1,0:T(8,128)(2,1)S(1)} %collective-permute-done.12.refs_2_.refs_5_), custom_call_target="tpu_custom_call" | custom-call | tf_op jit(solution)/shard_map/pallas_call | solution.py:594
  74.9 1.2 collective-permute-start.14
  76.2 2.0 %all-to-all-done = bf16[8,8,4096]{2,1,0:T(8,128)(2,1)S(1)} async-done(((bf16[8,8,4096]{2,1,0:T(8,128)(2,1)}), bf16[8,8,4096]{2,1,0:T(8,128)(2,1)S(1)}, u32[]{:S(2)}, u32[]{:S(2)}) %all-to-all-start) | async-done | bytes 524320 | tf_op jit(solution)/shard_map/all_to_all | solution.py:640
  78.1 8.8 %collective-permute-start.8 = (bf16[64,4096]{1,0:T(8,128)(2,1)S(1)}, bf16[64,4096]{1,0:T(8,128)(2,1)S(1)}, u32[]{:S(2)}, u32[]{:S(2)}) collective-permute-start(bf16[64,4096]{1,0:T(8,128)(2,1)S(1)} %bitcast.6), channel_id=1, source_target_pairs={{0,2},{2,0},{4,6},{6,4},{8,10},{10,8},{12,14},{14,12},{16,18},{18,... | collective-permute-start | bytes 1572872 | tf_op jit(solution)/shard_map/ppermute | solution.py:437
  86.9 0.9 copy-done.17
  87.8 1.0 shard_map.111
  88.9 1.5 shard_map.112
  90.4 0.8 collective-permute-done.9.refs_0_.refs_3_
  91.2 2.8 %collective-permute-start.19 = (bf16[72,4096]{1,0:T(8,128)(2,1)}, bf16[72,4096]{1,0:T(8,128)(2,1)}, u32[]{:S(2)}, u32[]{:S(2)}) collective-permute-start(bf16[72,4096]{1,0:T(8,128)(2,1)} %collective-permute-done.16.refs_2_), channel_id=1, source_target_pairs={{0,4},{2,6},{8,0},{10,2},{16,8},{18,10},{24,16},{26,18},{28,24},{3... | collective-permute-start | bytes 1769480 | tf_op jit(solution)/shard_map/ppermute | solution.py:456
  94.0 3.9 %all-to-all-start.1 = ((bf16[8,16,576]{2,1,0:T(8,128)(2,1)}), bf16[8,16,576]{2,1,0:T(8,128)(2,1)S(1)}, u32[]{:S(2)}, u32[]{:S(2)}) async-start(bf16[8,16,576]{2,1,0:T(8,128)(2,1)} %bitcast.15), calls=%async_computation.1 | async-start | bytes 327680 | tf_op jit(solution)/shard_map/all_to_all | solution.py:640
  97.9 2.8 %shard_map.113.refs_0_ = f32[128,216]{1,0:T(8,128)} custom-call(bf16[64,4096]{1,0:T(8,128)(2,1)S(1)} %bitcast.7, bf16[64,4096]{1,0:T(8,128)(2,1)S(1)} %collective-permute-done.8.send_ref, bf16[72,4096]{1,0:T(8,128)(2,1)} %refs_0_.1, bf16[72,4096]{1,0:T(8,128)(2,1)} %collective-permute-done.11.refs_1_, bf16[72,4096]{1,0:T(8,128)(2,1)} %collective-permute-done.16.refs_2_), custom_call_target="tpu_custom_call" | custom-call | tf_op jit(solution)/shard_map/pallas_call | solution.py:594
  100.8 1.3 collective-permute-start.17
  102.1 5.8 %all-to-all-done.1 = bf16[8,16,576]{2,1,0:T(8,128)(2,1)S(1)} async-done(((bf16[8,16,576]{2,1,0:T(8,128)(2,1)}), bf16[8,16,576]{2,1,0:T(8,128)(2,1)S(1)}, u32[]{:S(2)}, u32[]{:S(2)}) %all-to-all-start.1) | async-done | bytes 147488 | tf_op jit(solution)/shard_map/all_to_all | solution.py:640
  108.0 1.4 collective-permute-start.20
  109.5 2.2 %shard_map.114.refs_0_ = f32[128,216]{1,0:T(8,128)S(1)} custom-call(bf16[64,4096]{1,0:T(8,128)(2,1)S(1)} %bitcast.8, bf16[64,4096]{1,0:T(8,128)(2,1)S(1)} %collective-permute-done.8.send_ref, bf16[72,4096]{1,0:T(8,128)(2,1)} %collective-permute-done.9.refs_0_.refs_3_, bf16[72,4096]{1,0:T(8,128)(2,1)} %collective-permute-done.15.refs_1_.refs_4_, ...), custom_call_target="tpu_custom_call" | custom-call | tf_op jit(solution)/shard_map/pallas_call | solution.py:594
  111.6 1.5 collective-permute-start.21
  113.1 2.0 %shard_map.115 = (f32[64,2304]{1,0:T(8,128)S(1)}, f32[64,2304]{1,0:T(8,128)S(1)}, f32[64,2304]{1,0:T(8,128)S(1)}, f32[64,2304]{1,0:T(8,128)S(1)}) custom-call(s32[5]{0:T(128)S(1)} %copy-done.20, f32[128,216]{1,0:T(8,128)} %shard_map.113.refs_0_, f32[128,216]{1,0:T(8,128)} %collective-permute-done.17.refs_1_, f32[128,360]{1,0:T(8,128)S(1)} %get-tuple-element.87.refs_2_, ...), custom_call_target="tpu_custom_call" | custom-call | tf_op jit(solution)/shard_map/pallas_call | solution.py:598
  115.1 0.4 collective-permute-done.21.refs_1_
  115.5 1.9 %shard_map.116 = (f32[64,2304]{1,0:T(8,128)S(1)}, f32[64,2304]{1,0:T(8,128)S(1)}, f32[64,2304]{1,0:T(8,128)S(1)}, f32[64,2304]{1,0:T(8,128)S(1)}) custom-call(s32[5]{0:T(128)S(1)} %copy-done.20, f32[128,216]{1,0:T(8,128)S(1)} %shard_map.114.refs_0_, f32[128,216]{1,0:T(8,128)S(1)} %collective-permute-done.21.refs_1_, ...), custom_call_target="tpu_custom_call" | custom-call | tf_op jit(solution)/shard_map/pallas_call | solution.py:598
  117.4 0.5 shard_map.117.refs_0_
  117.9 1.5 collective-permute-start.22
  119.4 2.7 %collective-permute-done.22.refs_1_ = f32[128,144]{1,0:T(8,128)S(1)} collective-permute-done((f32[128,144]{1,0:T(8,128)S(1)}, f32[128,144]{1,0:T(8,128)S(1)}, u32[]{:S(2)}, u32[]{:S(2)}) %collective-permute-start.22) | collective-permute-done | bytes 73760 | tf_op jit(solution)/shard_map/ppermute | solution.py:445
  122.1 1.1 shard_map.118
  123.2 9.7 %collective-permute-start.23 = (bf16[64,2304]{1,0:T(8,128)(2,1)S(1)}, bf16[64,2304]{1,0:T(8,128)(2,1)S(1)}, u32[]{:S(2)}, u32[]{:S(2)}) collective-permute-start(bf16[64,2304]{1,0:T(8,128)(2,1)S(1)} %get-tuple-element.105), channel_id=1, source_target_pairs={{0,2},{2,0},{4,6},{6,4},{8,10},{10,8},{12,14},{14,12},{16,18},{18,... | collective-permute-start | bytes 884744 | tf_op jit(solution)/shard_map/ppermute | solution.py:437
  132.8 1.0 shard_map.120
  134.0 1.3 shard_map.119
  135.4 2.3 %collective-permute-start.26 = (bf16[256,576]{1,0:T(8,128)(2,1)S(1)}, bf16[256,576]{1,0:T(8,128)(2,1)S(1)}, u32[]{:S(2)}, u32[]{:S(2)}) collective-permute-start(bf16[256,576]{1,0:T(8,128)(2,1)S(1)} %get-tuple-element.117), channel_id=1, source_target_pairs={{2,0},{4,2},{6,4},{8,6},{10,8},{12,10},{14,12},{16,14},{18,16},{20... | collective-permute-start | bytes 884744 | tf_op jit(solution)/shard_map/ppermute | solution.py:420
  137.7 1.2 shard_map.121
  139.0 3.6 %shard_map.122 = (f32[64,4096]{1,0:T(8,128)S(1)}, bf16[64,4096]{1,0:T(8,128)(2,1)S(1)}) custom-call(s32[5]{0:T(128)S(1)} %get-tuple-element.112.facts_ref, bf16[128,576]{1,0:T(8,128)(2,1)S(1)} %bitcast.12, bf16[72,4096]{1,0:T(8,128)(2,1)} %refs_0_.1, bf16[72,4096]{1,0:T(8,128)(2,1)} %collective-permute-done.11.refs_1_, ...), custom_call_target="tpu_custom_call" | custom-call | tf_op jit(solution)/shard_map/pallas_call | solution.py:626
  142.6 0.6 collective-permute-start.25
  143.2 1.4 collective-permute-done.26.odd_ref
  144.7 0.9 shard_map.123
  145.6 1.3 collective-permute-start.27
  146.9 1.7 %shard_map.124 = (bf16[2304,256]{1,0:T(8,128)(2,1)S(1)}, bf16[2304,256]{1,0:T(8,128)(2,1)S(1)}, bf16[2304,256]{1,0:T(8,128)(2,1)S(1)}) custom-call(s32[5]{0:T(128)S(1)} %get-tuple-element.112.facts_ref, bf16[9,48,576]{2,1,0:T(8,128)(2,1)S(1)} %bitcast.11), custom_call_target="tpu_custom_call" | custom-call | tf_op jit(solution)/shard_map/pallas_call | solution.py:598
  148.6 2.8 %shard_map.125 = bf16[2,196,576]{2,1,0:T(8,128)(2,1)S(1)} custom-call(f32[256,576]{1,0:T(8,128)S(1)} %get-tuple-element.116.even_ref, bf16[256,576]{1,0:T(8,128)(2,1)S(1)} %collective-permute-done.26.odd_ref, f32[512,576]{1,0:T(8,128)S(1)} %copy-done.1, f32[2,576]{1,0:T(2,128)S(1)} %get-tuple-element.118.excite_ref, f32[2,288]{1,0:T(2,128)S(1)} %add.9.sq_ref, ...), custom_call_target="tpu_custom_call" | custom-call | flops 2717908992 | bytes 4718592 | tf_op jit(solution)/shard_map/pallas_call | solution.py:385
  151.3 1.2 copy.12
  152.5 0.9 add_convert_fusion
  (68 shorter events, 1.2 us)
Async XLA Ops:
  0.6 3.3 %copy-start.21 = (bf16[2,196,576]{2,0,1:T(2,128)(2,1)S(1)}, bf16[2,196,576]{2,0,1:T(2,128)(2,1)}, u32[]{:S(2)}) copy-start(bf16[2,196,576]{2,0,1:T(2,128)(2,1)} %param.9) | copy-start | bytes 1354756
  0.6 3.4 %copy-start.10 = (bf16[9,576,48]{1,2,0:T(8,128)(2,1)S(1)}, bf16[9,576,48]{1,2,0:T(8,128)(2,1)}, u32[]{:S(2)}) copy-start(bf16[9,576,48]{1,2,0:T(8,128)(2,1)} %param.10) | copy-start | bytes 1492996
  0.7 3.4 %copy-start.14 = (bf16[576,288]{0,1:T(8,128)(2,1)S(1)}, bf16[576,288]{0,1:T(8,128)(2,1)}, u32[]{:S(2)}) copy-start(bf16[576,288]{0,1:T(8,128)(2,1)} %param.11) | copy-start | bytes 995332
  2.4 8.8 %copy-start.12 = (bf16[288,576]{1,0:T(8,128)(2,1)S(1)}, bf16[288,576]{1,0:T(8,128)(2,1)}, u32[]{:S(2)}) copy-start(bf16[288,576]{1,0:T(8,128)(2,1)} %expand_ref.3) | copy-start | bytes 995332
  2.4 15.8 %collective-permute-start.2 = (bf16[72,4608]{1,0:T(8,128)(2,1)S(1)}, bf16[72,4608]{1,0:T(8,128)(2,1)S(1)}, u32[]{:S(2)}, u32[]{:S(2)}) collective-permute-start(bf16[72,4608]{1,0:T(8,128)(2,1)S(1)} %reshape.11.refs_0_.refs_4_), channel_id=1, source_target_pairs={{0,8},{2,10},{8,16},{10,18},{16,24},{18,26},{24,28},{26,30},{28,20... | collective-permute-start | bytes 1990664 | tf_op jit(solution)/shard_map/ppermute | solution.py:456
  2.5 15.9 %collective-permute-start.3 = (bf16[72,4608]{1,0:T(8,128)(2,1)S(1)}, bf16[72,4608]{1,0:T(8,128)(2,1)S(1)}, u32[]{:S(2)}, u32[]{:S(2)}) collective-permute-start(bf16[72,4608]{1,0:T(8,128)(2,1)S(1)} %reshape.11.refs_0_.refs_4_), channel_id=1, source_target_pairs={{0,4},{2,6},{8,0},{10,2},{16,8},{18,10},{24,16},{26,18},{28,24},{3... | collective-permute-start | bytes 1990664 | tf_op jit(solution)/shard_map/ppermute | solution.py:456
  8.5 29.6 %copy-start = (f32[512,576]{1,0:T(8,128)}, f32[512,576]{1,0:T(8,128)S(1)}, u32[]{:S(2)}) copy-start(f32[512,576]{1,0:T(8,128)S(1)} %get-tuple-element.62.conv_ref) | copy-start | bytes 3538948
  8.5 2.8 %collective-permute-start = (f32[2,288]{1,0:T(2,128)S(1)}, f32[2,288]{1,0:T(2,128)S(1)}, u32[]{:S(2)}, u32[]{:S(2)}) collective-permute-start(f32[2,288]{1,0:T(2,128)S(1)} %get-tuple-element.64), channel_id=1, source_target_pairs={{0,1},{1,0},{2,3},{3,2},{4,5},{5,4},{6,7},{7,6},{8,9},{9,8},{10,11... | collective-permute-start | bytes 6920 | tf_op jit(solution)/shard_map/ppermute | solution.py:445
  18.3 45.6 %copy-start.2 = (bf16[72,4608]{1,0:T(8,128)(2,1)}, bf16[72,4608]{1,0:T(8,128)(2,1)S(1)}, u32[]{:S(2)}) copy-start(bf16[72,4608]{1,0:T(8,128)(2,1)S(1)} %collective-permute-done.2.refs_1_.refs_4_) | copy-start | bytes 1990660
  18.4 19.7 %collective-permute-start.4 = (bf16[72,4608]{1,0:T(8,128)(2,1)S(1)}, bf16[72,4608]{1,0:T(8,128)(2,1)S(1)}, u32[]{:S(2)}, u32[]{:S(2)}) collective-permute-start(bf16[72,4608]{1,0:T(8,128)(2,1)S(1)} %collective-permute-done.2.refs_1_.refs_4_), channel_id=1, source_target_pairs={{0,8},{2,10},{8,16},{10,18},{16,24},{18,26},{24,28},{26,30},{28,20... | collective-permute-start | bytes 1990664 | tf_op jit(solution)/shard_map/ppermute | solution.py:456
  19.5 18.6 %collective-permute-start.5 = (bf16[72,4608]{1,0:T(8,128)(2,1)S(1)}, bf16[72,4608]{1,0:T(8,128)(2,1)}, u32[]{:S(2)}, u32[]{:S(2)}) collective-permute-start(bf16[72,4608]{1,0:T(8,128)(2,1)S(1)} %collective-permute-done.3.refs_2_.refs_5_), channel_id=1, source_target_pairs={{0,4},{2,6},{8,0},{10,2},{16,8},{18,10},{24,16},{26,18},{28,24},{3... | collective-permute-start | bytes 1990664 | tf_op jit(solution)/shard_map/ppermute | solution.py:456
  19.8 0.8 copy-start.7
  20.7 17.4 %collective-permute-start.1 = (bf16[256,576]{1,0:T(8,128)(2,1)S(1)}, bf16[256,576]{1,0:T(8,128)(2,1)S(1)}, u32[]{:S(2)}, u32[]{:S(2)}) collective-permute-start(bf16[256,576]{1,0:T(8,128)(2,1)S(1)} %get-tuple-element.65), channel_id=1, source_target_pairs={{0,2},{2,4},{4,6},{6,8},{8,10},{10,12},{12,14},{14,16},{16,18},{18... | collective-permute-start | bytes 884744 | tf_op jit(solution)/shard_map/ppermute | solution.py:420
  38.1 14.6 %collective-permute-start.6 = (bf16[72,4608]{1,0:T(8,128)(2,1)S(1)}, bf16[72,4608]{1,0:T(8,128)(2,1)S(1)}, u32[]{:S(2)}, u32[]{:S(2)}) collective-permute-start(bf16[72,4608]{1,0:T(8,128)(2,1)S(1)} %collective-permute-done.4.refs_3_.refs_5_), channel_id=1, source_target_pairs={{0,8},{2,10},{8,16},{10,18},{16,24},{18,26},{24,28},{26,30},{28,20... | collective-permute-start | bytes 1990664 | tf_op jit(solution)/shard_map/ppermute | solution.py:456
  39.3 0.9 copy-start.4
  40.1 15.5 %collective-permute-start.7 = (bf16[72,4608]{1,0:T(8,128)(2,1)}, bf16[72,4608]{1,0:T(8,128)(2,1)}, u32[]{:S(2)}, u32[]{:S(2)}) collective-permute-start(bf16[72,4608]{1,0:T(8,128)(2,1)} %collective-permute-done.5.refs_4_.refs_6_), channel_id=1, source_target_pairs={{0,4},{2,6},{8,0},{10,2},{16,8},{18,10},{24,16},{26,18},{28,24},{3... | collective-permute-start | bytes 1990664 | tf_op jit(solution)/shard_map/ppermute | solution.py:456
  41.7 0.7 copy-start.19
  42.4 19.7 %copy-start.20 = (s32[5]{0:T(128)S(1)}, s32[5]{0:T(128)}, u32[]{:S(2)}) copy-start(s32[5]{0:T(128)} %shard_map.104.facts_ref) | copy-start | bytes 64
  44.2 17.9 %collective-permute-start.10 = (bf16[64,4608]{1,0:T(8,128)(2,1)}, bf16[64,4608]{1,0:T(8,128)(2,1)}, u32[]{:S(2)}, u32[]{:S(2)}) collective-permute-start(bf16[64,4608]{1,0:T(8,128)(2,1)} %shard_map.107.own_ref), channel_id=1, source_target_pairs={{0,2},{2,0},{4,6},{6,4},{8,10},{10,8},{12,14},{14,12},{16,18},{18,... | collective-permute-start | bytes 1769480 | tf_op jit(solution)/shard_map/ppermute | solution.py:437
  55.7 15.5 %collective-permute-start.12 = (bf16[72,4608]{1,0:T(8,128)(2,1)S(1)}, bf16[72,4608]{1,0:T(8,128)(2,1)S(1)}, u32[]{:S(2)}, u32[]{:S(2)}) collective-permute-start(bf16[72,4608]{1,0:T(8,128)(2,1)S(1)} %collective-permute-done.6.refs_0_.refs_4_), channel_id=1, source_target_pairs={{0,8},{2,10},{8,16},{10,18},{16,24},{18,26},{24,28},{26,30},{28,20... | collective-permute-start | bytes 1990664 | tf_op jit(solution)/shard_map/ppermute | solution.py:456
  55.7 13.5 %collective-permute-start.11 = (bf16[72,4096]{1,0:T(8,128)(2,1)}, bf16[72,4096]{1,0:T(8,128)(2,1)}, u32[]{:S(2)}, u32[]{:S(2)}) collective-permute-start(bf16[72,4096]{1,0:T(8,128)(2,1)} %refs_0_.1), channel_id=1, source_target_pairs={{0,4},{2,6},{8,0},{10,2},{16,8},{18,10},{24,16},{26,18},{28,24},{3... | collective-permute-start | bytes 1769480 | tf_op jit(solution)/shard_map/ppermute | solution.py:456
  57.1 21.0 %all-to-all-start = ((bf16[8,8,4096]{2,1,0:T(8,128)(2,1)}), bf16[8,8,4096]{2,1,0:T(8,128)(2,1)S(1)}, u32[]{:S(2)}, u32[]{:S(2)}) async-start(bf16[8,8,4096]{2,1,0:T(8,128)(2,1)} %bitcast.16), calls=%async_computation | async-start | bytes 1048576 | tf_op jit(solution)/shard_map/all_to_all | solution.py:640
  62.1 1.8 %copy-start.5 = (bf16[72,4608]{1,0:T(8,128)(2,1)S(1)}, bf16[72,4608]{1,0:T(8,128)(2,1)}, u32[]{:S(2)}) copy-start(bf16[72,4608]{1,0:T(8,128)(2,1)} %copy-done.4) | copy-start | bytes 1990660
  62.1 1.9 %copy-start.8 = (bf16[72,4608]{1,0:T(8,128)(2,1)S(1)}, bf16[72,4608]{1,0:T(8,128)(2,1)}, u32[]{:S(2)}) copy-start(bf16[72,4608]{1,0:T(8,128)(2,1)} %copy-done.7) | copy-start | bytes 1990660
  66.2 5.0 %collective-permute-start.13 = (f32[128,360]{1,0:T(8,128)S(1)}, f32[128,360]{1,0:T(8,128)S(1)}, u32[]{:S(2)}, u32[]{:S(2)}) collective-permute-start(f32[128,360]{1,0:T(8,128)S(1)} %shard_map.109.own_ref), channel_id=1, source_target_pairs={{0,1},{1,0},{2,3},{3,2},{4,5},{5,4},{6,7},{7,6},{8,9},{9,8},{10,11... | collective-permute-start | bytes 552968 | tf_op jit(solution)/shard_map/ppermute | solution.py:445
  67.5 23.6 %collective-permute-start.9 = (bf16[72,4096]{1,0:T(8,128)(2,1)}, bf16[72,4096]{1,0:T(8,128)(2,1)}, u32[]{:S(2)}, u32[]{:S(2)}) collective-permute-start(bf16[72,4096]{1,0:T(8,128)(2,1)} %refs_0_.1), channel_id=1, source_target_pairs={{0,8},{2,10},{8,16},{10,18},{16,24},{18,26},{24,28},{26,30},{28,20... | collective-permute-start | bytes 1769480 | tf_op jit(solution)/shard_map/ppermute | solution.py:456
  71.2 3.7 %copy-start.16 = (f32[128,360]{1,0:T(8,128)}, f32[128,360]{1,0:T(8,128)S(1)}, u32[]{:S(2)}) copy-start(f32[128,360]{1,0:T(8,128)S(1)} %collective-permute-done.13.other_ref) | copy-start | bytes 552964
  71.2 20.0 %collective-permute-start.16 = (bf16[72,4096]{1,0:T(8,128)(2,1)}, bf16[72,4096]{1,0:T(8,128)(2,1)}, u32[]{:S(2)}, u32[]{:S(2)}) collective-permute-start(bf16[72,4096]{1,0:T(8,128)(2,1)} %collective-permute-done.11.refs_1_), channel_id=1, source_target_pairs={{0,4},{2,6},{8,0},{10,2},{16,8},{18,10},{24,16},{26,18},{28,24},{3... | collective-permute-start | bytes 1769480 | tf_op jit(solution)/shard_map/ppermute | solution.py:456
  74.9 13.9 %collective-permute-start.14 = (f32[128,216]{1,0:T(8,128)}, f32[128,216]{1,0:T(8,128)}, u32[]{:S(2)}, u32[]{:S(2)}) collective-permute-start(f32[128,216]{1,0:T(8,128)} %shard_map.110.own_ref), channel_id=1, source_target_pairs={{0,1},{1,0},{2,3},{3,2},{4,5},{5,4},{6,7},{7,6},{8,9},{9,8},{10,11... | collective-permute-start | bytes 331784 | tf_op jit(solution)/shard_map/ppermute | solution.py:445
  78.1 19.8 %collective-permute-start.8 = (bf16[64,4096]{1,0:T(8,128)(2,1)S(1)}, bf16[64,4096]{1,0:T(8,128)(2,1)S(1)}, u32[]{:S(2)}, u32[]{:S(2)}) collective-permute-start(bf16[64,4096]{1,0:T(8,128)(2,1)S(1)} %bitcast.6), channel_id=1, source_target_pairs={{0,2},{2,0},{4,6},{6,4},{8,10},{10,8},{12,14},{14,12},{16,18},{18,... | collective-permute-start | bytes 1572872 | tf_op jit(solution)/shard_map/ppermute | solution.py:437
  86.9 0.9 copy-start.17
  90.4 3.6 %copy-start.18 = (bf16[128,576]{1,0:T(8,128)(2,1)}, bf16[128,576]{1,0:T(8,128)(2,1)S(1)}, u32[]{:S(2)}) copy-start(bf16[128,576]{1,0:T(8,128)(2,1)S(1)} %get-tuple-element.84) | copy-start | bytes 442372
  91.2 16.8 %collective-permute-start.15 = (bf16[72,4096]{1,0:T(8,128)(2,1)}, bf16[72,4096]{1,0:T(8,128)(2,1)}, u32[]{:S(2)}, u32[]{:S(2)}) collective-permute-start(bf16[72,4096]{1,0:T(8,128)(2,1)} %collective-permute-done.9.refs_0_.refs_3_), channel_id=1, source_target_pairs={{0,8},{2,10},{8,16},{10,18},{16,24},{18,26},{24,28},{26,30},{28,20... | collective-permute-start | bytes 1769480 | tf_op jit(solution)/shard_map/ppermute | solution.py:456
  91.2 16.8 %collective-permute-start.19 = (bf16[72,4096]{1,0:T(8,128)(2,1)}, bf16[72,4096]{1,0:T(8,128)(2,1)}, u32[]{:S(2)}, u32[]{:S(2)}) collective-permute-start(bf16[72,4096]{1,0:T(8,128)(2,1)} %collective-permute-done.16.refs_2_), channel_id=1, source_target_pairs={{0,4},{2,6},{8,0},{10,2},{16,8},{18,10},{24,16},{26,18},{28,24},{3... | collective-permute-start | bytes 1769480 | tf_op jit(solution)/shard_map/ppermute | solution.py:456
  94.0 13.9 %all-to-all-start.1 = ((bf16[8,16,576]{2,1,0:T(8,128)(2,1)}), bf16[8,16,576]{2,1,0:T(8,128)(2,1)S(1)}, u32[]{:S(2)}, u32[]{:S(2)}) async-start(bf16[8,16,576]{2,1,0:T(8,128)(2,1)} %bitcast.15), calls=%async_computation.1 | async-start | bytes 327680 | tf_op jit(solution)/shard_map/all_to_all | solution.py:640
  100.8 7.2 %collective-permute-start.17 = (f32[128,216]{1,0:T(8,128)}, f32[128,216]{1,0:T(8,128)}, u32[]{:S(2)}, u32[]{:S(2)}) collective-permute-start(f32[128,216]{1,0:T(8,128)} %shard_map.113.refs_0_), channel_id=1, source_target_pairs={{0,1},{1,0},{2,3},{3,2},{4,5},{5,4},{6,7},{7,6},{8,9},{9,8},{10,11... | collective-permute-start | bytes 331784 | tf_op jit(solution)/shard_map/ppermute | solution.py:445
  107.9 5.2 %copy-start.9 = (bf16[72,4608]{1,0:T(8,128)(2,1)S(1)}, bf16[72,4608]{1,0:T(8,128)(2,1)}, u32[]{:S(2)}) copy-start(bf16[72,4608]{1,0:T(8,128)(2,1)} %copy-done.7) | copy-start | bytes 1990660
  107.9 9.5 %collective-permute-start.18 = (bf16[72,4096]{1,0:T(8,128)(2,1)}, bf16[72,4096]{1,0:T(8,128)(2,1)S(1)}, u32[]{:S(2)}, u32[]{:S(2)}) collective-permute-start(bf16[72,4096]{1,0:T(8,128)(2,1)} %collective-permute-done.15.refs_1_.refs_4_), channel_id=1, source_target_pairs={{0,8},{2,10},{8,16},{10,18},{16,24},{18,26},{24,28},{26,30},{28,20... | collective-permute-start | bytes 1769480 | tf_op jit(solution)/shard_map/ppermute | solution.py:456
  108.0 9.4 %collective-permute-start.20 = (bf16[72,4096]{1,0:T(8,128)(2,1)}, bf16[72,4096]{1,0:T(8,128)(2,1)S(1)}, u32[]{:S(2)}, u32[]{:S(2)}) collective-permute-start(bf16[72,4096]{1,0:T(8,128)(2,1)} %collective-permute-done.19.refs_2_.refs_5_), channel_id=1, source_target_pairs={{0,4},{2,6},{8,0},{10,2},{16,8},{18,10},{24,16},{26,18},{28,24},{3... | collective-permute-start | bytes 1769480 | tf_op jit(solution)/shard_map/ppermute | solution.py:456
  111.6 3.9 %collective-permute-start.21 = (f32[128,216]{1,0:T(8,128)S(1)}, f32[128,216]{1,0:T(8,128)S(1)}, u32[]{:S(2)}, u32[]{:S(2)}) collective-permute-start(f32[128,216]{1,0:T(8,128)S(1)} %shard_map.114.refs_0_), channel_id=1, source_target_pairs={{0,1},{1,0},{2,3},{3,2},{4,5},{5,4},{6,7},{7,6},{8,9},{9,8},{10,11... | collective-permute-start | bytes 331784 | tf_op jit(solution)/shard_map/ppermute | solution.py:445
  113.1 2.4 %copy-start.3 = (bf16[72,4608]{1,0:T(8,128)(2,1)S(1)}, bf16[72,4608]{1,0:T(8,128)(2,1)}, u32[]{:S(2)}) copy-start(bf16[72,4608]{1,0:T(8,128)(2,1)} %copy-done.2) | copy-start | bytes 1990660
  113.1 2.4 %copy-start.6 = (bf16[72,4608]{1,0:T(8,128)(2,1)S(1)}, bf16[72,4608]{1,0:T(8,128)(2,1)}, u32[]{:S(2)}) copy-start(bf16[72,4608]{1,0:T(8,128)(2,1)} %copy-done.4) | copy-start | bytes 1990660
  117.9 4.2 %collective-permute-start.22 = (f32[128,144]{1,0:T(8,128)S(1)}, f32[128,144]{1,0:T(8,128)S(1)}, u32[]{:S(2)}, u32[]{:S(2)}) collective-permute-start(f32[128,144]{1,0:T(8,128)S(1)} %shard_map.117.refs_0_), channel_id=1, source_target_pairs={{0,1},{1,0},{2,3},{3,2},{4,5},{5,4},{6,7},{7,6},{8,9},{9,8},{10,11... | collective-permute-start | bytes 221192 | tf_op jit(solution)/shard_map/ppermute | solution.py:445
  123.2 10.9 %collective-permute-start.23 = (bf16[64,2304]{1,0:T(8,128)(2,1)S(1)}, bf16[64,2304]{1,0:T(8,128)(2,1)S(1)}, u32[]{:S(2)}, u32[]{:S(2)}) collective-permute-start(bf16[64,2304]{1,0:T(8,128)(2,1)S(1)} %get-tuple-element.105), channel_id=1, source_target_pairs={{0,2},{2,0},{4,6},{6,4},{8,10},{10,8},{12,14},{14,12},{16,18},{18,... | collective-permute-start | bytes 884744 | tf_op jit(solution)/shard_map/ppermute | solution.py:437
  133.9 3.8 %collective-permute-start.24 = (bf16[64,2304]{1,0:T(8,128)(2,1)S(1)}, bf16[64,2304]{1,0:T(8,128)(2,1)S(1)}, u32[]{:S(2)}, u32[]{:S(2)}) collective-permute-start(bf16[64,2304]{1,0:T(8,128)(2,1)S(1)} %get-tuple-element.111), channel_id=1, source_target_pairs={{0,2},{2,0},{4,6},{6,4},{8,10},{10,8},{12,14},{14,12},{16,18},{18,... | collective-permute-start | bytes 884744 | tf_op jit(solution)/shard_map/ppermute | solution.py:437
  135.4 9.3 %collective-permute-start.26 = (bf16[256,576]{1,0:T(8,128)(2,1)S(1)}, bf16[256,576]{1,0:T(8,128)(2,1)S(1)}, u32[]{:S(2)}, u32[]{:S(2)}) collective-permute-start(bf16[256,576]{1,0:T(8,128)(2,1)S(1)} %get-tuple-element.117), channel_id=1, source_target_pairs={{2,0},{4,2},{6,4},{8,6},{10,8},{12,10},{14,12},{16,14},{18,16},{20... | collective-permute-start | bytes 884744 | tf_op jit(solution)/shard_map/ppermute | solution.py:420
  139.0 5.7 %copy-start.1 = (f32[512,576]{1,0:T(8,128)S(1)}, f32[512,576]{1,0:T(8,128)}, u32[]{:S(2)}) copy-start(f32[512,576]{1,0:T(8,128)} %copy-done) | copy-start | bytes 3538948
  139.0 5.7 %copy-start.13 = (bf16[288,576]{1,0:T(8,128)(2,1)S(1)}, bf16[288,576]{1,0:T(8,128)(2,1)}, u32[]{:S(2)}) copy-start(bf16[288,576]{1,0:T(8,128)(2,1)} %expand_ref.3) | copy-start | bytes 995332
  142.6 9.9 %collective-permute-start.25 = (bf16[64,4096]{1,0:T(8,128)(2,1)S(1)}, bf16[64,4096]{1,0:T(8,128)(2,1)S(1)}, u32[]{:S(2)}, u32[]{:S(2)}) collective-permute-start(bf16[64,4096]{1,0:T(8,128)(2,1)S(1)} %get-tuple-element.115), channel_id=1, source_target_pairs={{0,2},{2,0},{4,6},{6,4},{8,10},{10,8},{12,14},{14,12},{16,18},{18,... | collective-permute-start | bytes 1572872 | tf_op jit(solution)/shard_map/ppermute | solution.py:437
  144.7 2.2 %copy-start.11 = (bf16[9,576,48]{1,2,0:T(8,128)(2,1)S(1)}, bf16[9,576,48]{1,2,0:T(8,128)(2,1)}, u32[]{:S(2)}) copy-start(bf16[9,576,48]{1,2,0:T(8,128)(2,1)} %param.10) | copy-start | bytes 1492996
  144.7 3.9 %copy-start.15 = (bf16[576,288]{0,1:T(8,128)(2,1)S(1)}, bf16[576,288]{0,1:T(8,128)(2,1)}, u32[]{:S(2)}) copy-start(bf16[576,288]{0,1:T(8,128)(2,1)} %param.11) | copy-start | bytes 995332
  145.6 2.9 %collective-permute-start.27 = (f32[2,288]{1,0:T(2,128)S(1)}, f32[2,288]{1,0:T(2,128)S(1)}, u32[]{:S(2)}, u32[]{:S(2)}) collective-permute-start(f32[2,288]{1,0:T(2,128)S(1)} %shard_map.123), channel_id=1, source_target_pairs={{0,1},{1,0},{2,3},{3,2},{4,5},{5,4},{6,7},{7,6},{8,9},{9,8},{10,11... | collective-permute-start | bytes 6920 | tf_op jit(solution)/shard_map/ppermute | solution.py:445

commit v19 on v15

--- a/solution.py
+++ b/solution.py
@@ -717,7 +717,15 @@
     grads = add_gradients(facts, terms, slopes, pieces, blocks, grads, unit, both, False)
 
     late_up, late_down, *grads = tie(r_up[-1], r_down[-1], *grads)
-    terms = tp_terms(block_products(back_kernel, back, [late_up, late_down]))
+    sums, act = tie(block_products(back_kernel, back, [late_up, late_down]), act)
+    terms = tp_terms(sums)
+    places = [*range(steps - 1), *range(-1, 1 - steps, -1), steps - 1, 1 - steps, steps]
+    tokens = token_products(
+        facts, act, places, chips, [*early, *middle, late_up, late_down], unit
+    )
+    other_term, *tokens = tie(terms[1], *tokens)
+    terms = terms[0], other_term
+    llm_tokens = (tokens[0] + swap_cores(tokens[1]).astype(jnp.float32)).astype(jnp.bfloat16)
     pieces, blocks = [(1, 0), (1, 2)], [s_up[-1], s_last]
     halo_own, halo_mate = add_gradients(
         facts, terms, slopes, pieces, blocks, grads[:2], unit, (halo_lanes,), True
@@ -731,12 +739,8 @@
     grad_even, facts_late = return_patches(
         facts_late, even_own, swap_cores(even_mate), chans, jnp.float32
     )
-    places = [*range(steps - 1), *range(-1, 1 - steps, -1), steps - 1, 1 - steps, steps]
-    tokens = token_products(
-        facts_late, act, places, chips, [*early, *middle, late_up, late_down], unit
-    )
+    llm_tokens, grad_odd = tie(llm_tokens, grad_odd)
     grad_relaxed = sum_tp(excite_grad(grad_even, grad_odd, conv, excite, squeeze_out))
-    llm_tokens = (tokens[0] + swap_cores(tokens[1]).astype(jnp.float32)).astype(jnp.bfloat16)
     grad_features = conv_backward(
         grad_even, grad_odd, conv, excite, squeezed, grad_relaxed, squeeze_in,
         dense_weights(facts_late, group_kernel), group_kernel.shape[1],

time: 154 us -> 153 us (level)
    ppermute x2, waiting for transfers between devices: 12.8 us -> 16.1 us  [shifted(): return lax.ppermute(value, axis, pairs)]
    ppermute x7, waiting for transfers between devices: 11.1 us -> 8.4 us  [tp_terms(): other = lax.ppermute(value, 'tp', [(i, i ^ reach) for i in range(size)])]
    unnamed x40 -> x38, local copies, waits for them, and re-layouts: 3.65 us -> 4.69 us
  transfers between devices with their start and end apart: 30 -> 30, of which waited for: 17 -> 15; matrix products, arithmetic and copies ran while one was open for 1% -> 1% of each run, Pallas kernels for 24% -> 23%
where the time goes in v19:
time: 153 us; the launch traced here: 152 us
  starting transfers between devices  56.4 us (37%)
  waiting for transfers between devices  49 us (32%)
  Pallas kernels  38.5 us (25%)
  local copies, waits for them, and re-layouts  6.42 us (4%)
    ppermute x14, waiting for transfers between devices, ring_send(): return lax.ppermute(value, 'ctx', ring_pairs(lax.axis_size('ctx'), by))  22.7 us
    ppermute x5, starting transfers between devices, swap_cores(): lax.ppermute(value, 'ctx', [(i, i ^ 1) for i in range(lax.axis_size('ctx'...  18.9 us
    ppermute x2, waiting for transfers between devices, shifted(): return lax.ppermute(value, axis, pairs)  16.1 us
    pallas_call x7, Pallas kernels, facts_call(): pl.pallas_call(kernel, out_shape=outs, in_specs=vmem_specs(len(operands))...  10.3 us
    ppermute x14, starting transfers between devices, ring_send(): return lax.ppermute(value, 'ctx', ring_pairs(lax.axis_size('ctx'), by))  10.1 us
    ppermute x7, starting transfers between devices, tp_terms(): other = lax.ppermute(value, 'tp', [(i, i ^ reach) for i in range(size)])  9.51 us
    all_to_all x2, starting transfers between devices, chips_exchange(): lax.all_to_all(value, 'ctx', split_axis=0, concat_axis=0, tiled=True, axi...  9.49 us
    pallas_call x5, Pallas kernels, block_products(): whole_call(kernel, f32(rows, len(blocks) * blocks[0].shape[0]), [])  8.63 us
  transfers between devices with their start and end apart: 30, of which 15 were waited for; matrix products, arithmetic and copies ran while one was open for 1% of the time, Pallas kernels for 23%

profile of v19, /device:TPU:3, one launch (start us, length us, event | category | flops | bytes accessed | tf_op | source)
XLA Modules:
  0.0 152.2 jit_solution(1990520486017883377)
XLA Ops:
  0.7 1.7 %reshape.11.refs_0_.refs_4_ = bf16[72,4608]{1,0:T(8,128)(2,1)S(1)} reshape(bf16[72,8,576]{2,1,0:T(8,128)(2,1)} %param.13) | data formatting | bytes 1327104 | tf_op jit(solution)/shard_map/reshape | solution.py:659
  2.5 1.5 collective-permute-start.3
  3.9 1.1 copy.11.feat_ref
  5.0 4.4 %shard_map.104 = (f32[512,576]{1,0:T(8,128)S(1)}, bf16[512,576]{1,0:T(8,128)(2,1)S(1)}, f32[2,288]{1,0:T(2,128)S(1)}) custom-call(bf16[2,196,576]{2,1,0:T(8,128)(2,1)S(1)} %copy.11.feat_ref, bf16[9,48,576]{2,1,0:T(8,128)(2,1)S(1)} %bitcast.10, bf16[288,576]{1,0:T(8,128)(2,1)S(1)} %bitcast.13), custom_call_target="tpu_custom_call" | custom-call | tf_op jit(solution)/shard_map/pallas_call | solution.py:301
  9.5 1.3 collective-permute-start
  10.8 1.5 collective-permute-done
  12.3 0.7 shard_map.105
  13.0 5.2 %collective-permute-done.2.refs_1_.refs_4_ = bf16[72,4608]{1,0:T(8,128)(2,1)S(1)} collective-permute-done((bf16[72,4608]{1,0:T(8,128)(2,1)S(1)}, bf16[72,4608]{1,0:T(8,128)(2,1)S(1)}, u32[]{:S(2)}, u32[]{:S(2)}) %collective-permute-start.2) | collective-permute-done | bytes 663584 | tf_op jit(solution)/shard_map/ppermute | solution.py:456
  18.3 1.1 collective-permute-start.4
  19.8 0.9 copy-done.7
  20.7 6.4 %collective-permute-start.1 = (bf16[256,576]{1,0:T(8,128)(2,1)S(1)}, bf16[256,576]{1,0:T(8,128)(2,1)S(1)}, u32[]{:S(2)}, u32[]{:S(2)}) collective-permute-start(bf16[256,576]{1,0:T(8,128)(2,1)S(1)} %get-tuple-element.71), channel_id=1, source_target_pairs={{0,2},{2,4},{4,6},{6,8},{8,10},{10,12},{12,14},{14,16},{16,18},{18... | collective-permute-start | bytes 884744 | tf_op jit(solution)/shard_map/ppermute | solution.py:420
  27.0 11.0 %collective-permute-done.1.halo_ref = bf16[256,576]{1,0:T(8,128)(2,1)S(1)} collective-permute-done((bf16[256,576]{1,0:T(8,128)(2,1)S(1)}, bf16[256,576]{1,0:T(8,128)(2,1)S(1)}, u32[]{:S(2)}, u32[]{:S(2)}) %collective-permute-start.1) | collective-permute-done | bytes 294944 | tf_op jit(solution)/shard_map/ppermute | solution.py:420
  38.0 1.2 collective-permute-start.6
  39.2 0.8 copy-done.4
  40.4 1.3 shard_map.106.facts_ref
  41.7 0.6 copy-done.16
  42.3 1.8 %shard_map.107.own_ref = bf16[64,4608]{1,0:T(8,128)(2,1)} custom-call(s32[5]{0:T(128)S(1)} %copy-done.16, bf16[256,576]{1,0:T(8,128)(2,1)S(1)} %collective-permute-done.1.halo_ref, bf16[256,576]{1,0:T(8,128)(2,1)S(1)} %get-tuple-element.81.even_ref), custom_call_target="tpu_custom_call" | custom-call | tf_op jit(solution)/shard_map/pallas_call | solution.py:349
  44.1 2.8 %collective-permute-start.10 = (bf16[64,4608]{1,0:T(8,128)(2,1)}, bf16[64,4608]{1,0:T(8,128)(2,1)}, u32[]{:S(2)}, u32[]{:S(2)}) collective-permute-start(bf16[64,4608]{1,0:T(8,128)(2,1)} %shard_map.107.own_ref), channel_id=1, source_target_pairs={{0,2},{2,0},{4,6},{6,4},{8,10},{10,8},{12,14},{14,12},{16,18},{18,... | collective-permute-start | bytes 1769480 | tf_op jit(solution)/shard_map/ppermute | solution.py:437
  47.0 5.6 %collective-permute-done.6.refs_0_.refs_4_ = bf16[72,4608]{1,0:T(8,128)(2,1)S(1)} collective-permute-done((bf16[72,4608]{1,0:T(8,128)(2,1)S(1)}, bf16[72,4608]{1,0:T(8,128)(2,1)S(1)}, u32[]{:S(2)}, u32[]{:S(2)}) %collective-permute-start.6) | collective-permute-done | bytes 663584 | tf_op jit(solution)/shard_map/ppermute | solution.py:456
  52.6 3.0 %collective-permute-done.7.refs_1_.refs_6_ = bf16[72,4608]{1,0:T(8,128)(2,1)} collective-permute-done((bf16[72,4608]{1,0:T(8,128)(2,1)}, bf16[72,4608]{1,0:T(8,128)(2,1)}, u32[]{:S(2)}, u32[]{:S(2)}) %collective-permute-start.7) | collective-permute-done | bytes 663584 | tf_op jit(solution)/shard_map/ppermute | solution.py:456
  55.6 1.5 collective-permute-start.11
  57.1 4.9 %all-to-all-start = ((bf16[8,8,4096]{2,1,0:T(8,128)(2,1)}), bf16[8,8,4096]{2,1,0:T(8,128)(2,1)S(1)}, u32[]{:S(2)}, u32[]{:S(2)}) async-start(bf16[8,8,4096]{2,1,0:T(8,128)(2,1)} %bitcast.15), calls=%async_computation | async-start | bytes 1048576 | tf_op jit(solution)/shard_map/all_to_all | solution.py:640
  62.0 1.8 %shard_map.108.patch_ref = bf16[128,4608]{1,0:T(8,128)(2,1)S(1)} custom-call(s32[5]{0:T(128)S(1)} %copy-done.17, bf16[64,4608]{1,0:T(8,128)(2,1)} %shard_map.107.own_ref, bf16[64,4608]{1,0:T(8,128)(2,1)} %collective-permute-done.10.mate_ref), custom_call_target="tpu_custom_call" | custom-call | tf_op jit(solution)/shard_map/pallas_call | solution.py:338
  63.9 2.3 %shard_map.109.own_ref = f32[128,360]{1,0:T(8,128)S(1)} custom-call(bf16[128,4608]{1,0:T(8,128)(2,1)S(1)} %shard_map.108.patch_ref, bf16[72,4608]{1,0:T(8,128)(2,1)S(1)} %reshape.11.refs_0_.refs_4_, bf16[72,4608]{1,0:T(8,128)(2,1)S(1)} %collective-permute-done.2.refs_1_.refs_4_, bf16[72,4608]{1,0:T(8,128)(2,1)S(1)} %copy-done.8, ...), custom_call_target="tpu_custom_call" | custom-call | tf_op jit(solution)/shard_map/pallas_call | solution.py:594
  66.2 1.3 collective-permute-start.13
  67.5 1.6 %collective-permute-done.11.refs_1_ = bf16[72,4096]{1,0:T(8,128)(2,1)} collective-permute-done((bf16[72,4096]{1,0:T(8,128)(2,1)}, bf16[72,4096]{1,0:T(8,128)(2,1)}, u32[]{:S(2)}, u32[]{:S(2)}) %collective-permute-start.11) | collective-permute-done | bytes 589856 | tf_op jit(solution)/shard_map/ppermute | solution.py:456
  69.1 2.1 %collective-permute-done.13.other_ref = f32[128,360]{1,0:T(8,128)S(1)} collective-permute-done((f32[128,360]{1,0:T(8,128)S(1)}, f32[128,360]{1,0:T(8,128)S(1)}, u32[]{:S(2)}, u32[]{:S(2)}) %collective-permute-start.13) | collective-permute-done | bytes 184352 | tf_op jit(solution)/shard_map/ppermute | solution.py:445
  71.2 1.2 collective-permute-start.16
  72.3 1.9 %shard_map.110.own_ref = f32[128,216]{1,0:T(8,128)S(1)} custom-call(bf16[128,4608]{1,0:T(8,128)(2,1)S(1)} %shard_map.108.patch_ref, bf16[72,4608]{1,0:T(8,128)(2,1)S(1)} %collective-permute-done.6.refs_0_.refs_4_, bf16[72,4608]{1,0:T(8,128)(2,1)} %collective-permute-done.7.refs_1_.refs_6_, bf16[72,4608]{1,0:T(8,128)(2,1)S(1)} %collective-permute-done.12.refs_2_.refs_5_), custom_call_target="tpu_custom_call" | custom-call | tf_op jit(solution)/shard_map/pallas_call | solution.py:594
  74.2 1.3 collective-permute-start.14
  75.5 1.0 shard_map.111
  76.6 1.8 %collective-permute-done.14.other_ref = f32[128,216]{1,0:T(8,128)S(1)} collective-permute-done((f32[128,216]{1,0:T(8,128)S(1)}, f32[128,216]{1,0:T(8,128)S(1)}, u32[]{:S(2)}, u32[]{:S(2)}) %collective-permute-start.14) | collective-permute-done | bytes 110624 | tf_op jit(solution)/shard_map/ppermute | solution.py:445
  78.4 1.7 %shard_map.112 = (f32[128,216]{1,0:T(8,128)S(1)}, bf16[128,576]{1,0:T(8,128)(2,1)}) custom-call(s32[5]{0:T(128)S(1)} %copy-done.17, f32[128,216]{1,0:T(8,128)S(1)} %shard_map.110.own_ref, f32[128,216]{1,0:T(8,128)S(1)} %collective-permute-done.14.other_ref, bf16[128,576]{1,0:T(8,128)(2,1)S(1)} %get-tuple-element.87.refs_0_), custom_call_target="tpu_custom_call" | custom-call | tf_op jit(solution)/shard_map/pallas_call | solution.py:598
  80.2 4.6 %all-to-all-start.1 = ((bf16[8,16,576]{2,1,0:T(8,128)(2,1)}), bf16[8,16,576]{2,1,0:T(8,128)(2,1)S(1)}, u32[]{:S(2)}, u32[]{:S(2)}) async-start(bf16[8,16,576]{2,1,0:T(8,128)(2,1)} %bitcast.4), calls=%async_computation.1 | async-start | bytes 327680 | tf_op jit(solution)/shard_map/all_to_all | solution.py:640
  84.7 9.4 %collective-permute-start.8 = (bf16[64,4096]{1,0:T(8,128)(2,1)S(1)}, bf16[64,4096]{1,0:T(8,128)(2,1)S(1)}, u32[]{:S(2)}, u32[]{:S(2)}) collective-permute-start(bf16[64,4096]{1,0:T(8,128)(2,1)S(1)} %bitcast.6), channel_id=1, source_target_pairs={{0,2},{2,0},{4,6},{6,4},{8,10},{10,8},{12,14},{14,12},{16,18},{18,... | collective-permute-start | bytes 1572872 | tf_op jit(solution)/shard_map/ppermute | solution.py:437
  94.1 1.8 %all-to-all-done.1 = bf16[8,16,576]{2,1,0:T(8,128)(2,1)S(1)} async-done(((bf16[8,16,576]{2,1,0:T(8,128)(2,1)}), bf16[8,16,576]{2,1,0:T(8,128)(2,1)S(1)}, u32[]{:S(2)}, u32[]{:S(2)}) %all-to-all-start.1) | async-done | bytes 147488 | tf_op jit(solution)/shard_map/all_to_all | solution.py:640
  95.9 1.5 collective-permute-start.19
  97.4 2.2 %shard_map.113.refs_0_ = f32[128,216]{1,0:T(8,128)S(1)} custom-call(bf16[64,4096]{1,0:T(8,128)(2,1)S(1)} %bitcast.7, bf16[64,4096]{1,0:T(8,128)(2,1)S(1)} %collective-permute-done.8.send_ref, bf16[72,4096]{1,0:T(8,128)(2,1)} %refs_0_.1, bf16[72,4096]{1,0:T(8,128)(2,1)} %collective-permute-done.11.refs_1_, bf16[72,4096]{1,0:T(8,128)(2,1)} %collective-permute-done.16.refs_2_), custom_call_target="tpu_custom_call" | custom-call | tf_op jit(solution)/shard_map/pallas_call | solution.py:594
  99.6 1.4 collective-permute-start.17
  101.0 2.5 %collective-permute-done.17.refs_1_ = f32[128,216]{1,0:T(8,128)S(1)} collective-permute-done((f32[128,216]{1,0:T(8,128)S(1)}, f32[128,216]{1,0:T(8,128)S(1)}, u32[]{:S(2)}, u32[]{:S(2)}) %collective-permute-start.17) | collective-permute-done | bytes 110624 | tf_op jit(solution)/shard_map/ppermute | solution.py:445
  103.5 4.3 %collective-permute-done.15.refs_1_.refs_4_ = bf16[72,4096]{1,0:T(8,128)(2,1)S(1)} collective-permute-done((bf16[72,4096]{1,0:T(8,128)(2,1)}, bf16[72,4096]{1,0:T(8,128)(2,1)S(1)}, u32[]{:S(2)}, u32[]{:S(2)}) %collective-permute-start.15) | collective-permute-done | bytes 589856 | tf_op jit(solution)/shard_map/ppermute | solution.py:456
  107.8 1.5 collective-permute-start.20
  109.3 1.8 %shard_map.114.refs_0_ = f32[128,216]{1,0:T(8,128)S(1)} custom-call(bf16[64,4096]{1,0:T(8,128)(2,1)S(1)} %bitcast.8, bf16[64,4096]{1,0:T(8,128)(2,1)S(1)} %collective-permute-done.8.send_ref, bf16[72,4096]{1,0:T(8,128)(2,1)} %collective-permute-done.9.refs_0_.refs_3_, bf16[72,4096]{1,0:T(8,128)(2,1)S(1)} %collective-permute-done.15.refs_1_.refs_4_, ...), custom_call_target="tpu_custom_call" | custom-call | tf_op jit(solution)/shard_map/pallas_call | solution.py:594
  111.1 1.5 collective-permute-start.21
  112.6 1.9 %shard_map.115 = (f32[64,2304]{1,0:T(8,128)S(1)}, f32[64,2304]{1,0:T(8,128)S(1)}, f32[64,2304]{1,0:T(8,128)S(1)}, f32[64,2304]{1,0:T(8,128)S(1)}) custom-call(s32[5]{0:T(128)S(1)} %copy-done.17, f32[128,216]{1,0:T(8,128)S(1)} %shard_map.113.refs_0_, f32[128,216]{1,0:T(8,128)S(1)} %collective-permute-done.17.refs_1_, ...), custom_call_target="tpu_custom_call" | custom-call | tf_op jit(solution)/shard_map/pallas_call | solution.py:598
  114.5 0.5 collective-permute-done.21.refs_1_
  115.0 1.9 %shard_map.116 = (f32[64,2304]{1,0:T(8,128)S(1)}, f32[64,2304]{1,0:T(8,128)S(1)}, f32[64,2304]{1,0:T(8,128)S(1)}, f32[64,2304]{1,0:T(8,128)S(1)}) custom-call(s32[5]{0:T(128)S(1)} %copy-done.17, f32[128,216]{1,0:T(8,128)S(1)} %shard_map.114.refs_0_, f32[128,216]{1,0:T(8,128)S(1)} %collective-permute-done.21.refs_1_, ...), custom_call_target="tpu_custom_call" | custom-call | tf_op jit(solution)/shard_map/pallas_call | solution.py:598
  116.9 2.7 %collective-permute-done.18.refs_0_.refs_6_ = bf16[72,4096]{1,0:T(8,128)(2,1)S(1)} collective-permute-done((bf16[72,4096]{1,0:T(8,128)(2,1)S(1)}, bf16[72,4096]{1,0:T(8,128)(2,1)S(1)}, u32[]{:S(2)}, u32[]{:S(2)}) %collective-permute-start.18) | collective-permute-done | bytes 589856 | tf_op jit(solution)/shard_map/ppermute | solution.py:456
  120.1 1.5 collective-permute-start.22
  121.6 3.3 %shard_map.118 = (f32[64,4096]{1,0:T(8,128)S(1)}, bf16[64,4096]{1,0:T(8,128)(2,1)S(1)}) custom-call(s32[5]{0:T(128)S(1)} %copy-done.17, bf16[128,576]{1,0:T(8,128)(2,1)S(1)} %bitcast.12, bf16[72,4096]{1,0:T(8,128)(2,1)} %refs_0_.1, bf16[72,4096]{1,0:T(8,128)(2,1)} %collective-permute-done.11.refs_1_, bf16[72,4096]{1,0:T(8,128)(2,1)} %collective-permute-done.16.refs_2_, ...), custom_call_target="tpu_custom_call" | custom-call | tf_op jit(solution)/shard_map/pallas_call | solution.py:626
  124.8 6.1 %collective-permute-start.23 = (bf16[64,4096]{1,0:T(8,128)(2,1)S(1)}, bf16[64,4096]{1,0:T(8,128)(2,1)S(1)}, u32[]{:S(2)}, u32[]{:S(2)}) collective-permute-start(bf16[64,4096]{1,0:T(8,128)(2,1)S(1)} %get-tuple-element.112), channel_id=1, source_target_pairs={{0,2},{2,0},{4,6},{6,4},{8,10},{10,8},{12,14},{14,12},{16,18},{18,... | collective-permute-start | bytes 1572872 | tf_op jit(solution)/shard_map/ppermute | solution.py:437
  130.9 1.0 shard_map.119
  132.1 1.1 shard_map.121
  133.1 0.6 collective-permute-start.26
  133.7 1.3 shard_map.120
  135.0 2.0 %collective-permute-start.25 = (bf16[256,576]{1,0:T(8,128)(2,1)S(1)}, bf16[256,576]{1,0:T(8,128)(2,1)S(1)}, u32[]{:S(2)}, u32[]{:S(2)}) collective-permute-start(bf16[256,576]{1,0:T(8,128)(2,1)S(1)} %get-tuple-element.119), channel_id=1, source_target_pairs={{2,0},{4,2},{6,4},{8,6},{10,8},{12,10},{14,12},{16,14},{18,16},{20... | collective-permute-start | bytes 884744 | tf_op jit(solution)/shard_map/ppermute | solution.py:420
  137.0 1.2 shard_map.122
  138.3 0.9 add_convert_fusion
  139.2 5.1 %collective-permute-done.25.odd_ref = bf16[256,576]{1,0:T(8,128)(2,1)S(1)} collective-permute-done((bf16[256,576]{1,0:T(8,128)(2,1)S(1)}, bf16[256,576]{1,0:T(8,128)(2,1)S(1)}, u32[]{:S(2)}, u32[]{:S(2)}) %collective-permute-start.25) | collective-permute-done | bytes 294944 | tf_op jit(solution)/shard_map/ppermute | solution.py:420
  144.3 0.9 shard_map.123
  145.2 1.3 collective-permute-start.27
  146.5 1.7 %shard_map.124 = (bf16[2304,256]{1,0:T(8,128)(2,1)S(1)}, bf16[2304,256]{1,0:T(8,128)(2,1)S(1)}, bf16[2304,256]{1,0:T(8,128)(2,1)S(1)}) custom-call(s32[5]{0:T(128)S(1)} %get-tuple-element.130.facts_ref, bf16[9,48,576]{2,1,0:T(8,128)(2,1)S(1)} %bitcast.11), custom_call_target="tpu_custom_call" | custom-call | tf_op jit(solution)/shard_map/pallas_call | solution.py:598
  148.2 2.8 %shard_map.125 = bf16[2,196,576]{2,1,0:T(8,128)(2,1)S(1)} custom-call(f32[256,576]{1,0:T(8,128)S(1)} %get-tuple-element.127.even_ref, bf16[256,576]{1,0:T(8,128)(2,1)S(1)} %collective-permute-done.25.odd_ref, f32[512,576]{1,0:T(8,128)S(1)} %copy-done.1, f32[2,576]{1,0:T(2,128)S(1)} %get-tuple-element.129.excite_ref, f32[2,288]{1,0:T(2,128)S(1)} %add.9.sq_ref, ...), custom_call_target="tpu_custom_call" | custom-call | flops 2717908992 | bytes 4718592 | tf_op jit(solution)/shard_map/pallas_call | solution.py:385
  151.0 1.2 copy.12
  (60 shorter events, 1.5 us)
Async XLA Ops:
  0.6 4.4 %copy-start.10 = (bf16[9,576,48]{1,2,0:T(8,128)(2,1)S(1)}, bf16[9,576,48]{1,2,0:T(8,128)(2,1)}, u32[]{:S(2)}) copy-start(bf16[9,576,48]{1,2,0:T(8,128)(2,1)} %param.10) | copy-start | bytes 1492996
  0.6 4.4 %copy-start.14 = (bf16[576,288]{0,1:T(8,128)(2,1)S(1)}, bf16[576,288]{0,1:T(8,128)(2,1)}, u32[]{:S(2)}) copy-start(bf16[576,288]{0,1:T(8,128)(2,1)} %param.11) | copy-start | bytes 995332
  2.4 9.9 %copy-start.12 = (bf16[288,576]{1,0:T(8,128)(2,1)S(1)}, bf16[288,576]{1,0:T(8,128)(2,1)}, u32[]{:S(2)}) copy-start(bf16[288,576]{1,0:T(8,128)(2,1)} %expand_ref.3) | copy-start | bytes 995332
  2.4 15.8 %collective-permute-start.2 = (bf16[72,4608]{1,0:T(8,128)(2,1)S(1)}, bf16[72,4608]{1,0:T(8,128)(2,1)S(1)}, u32[]{:S(2)}, u32[]{:S(2)}) collective-permute-start(bf16[72,4608]{1,0:T(8,128)(2,1)S(1)} %reshape.11.refs_0_.refs_4_), channel_id=1, source_target_pairs={{0,8},{2,10},{8,16},{10,18},{16,24},{18,26},{24,28},{26,30},{28,20... | collective-permute-start | bytes 1990664 | tf_op jit(solution)/shard_map/ppermute | solution.py:456
  2.5 15.9 %collective-permute-start.3 = (bf16[72,4608]{1,0:T(8,128)(2,1)S(1)}, bf16[72,4608]{1,0:T(8,128)(2,1)S(1)}, u32[]{:S(2)}, u32[]{:S(2)}) collective-permute-start(bf16[72,4608]{1,0:T(8,128)(2,1)S(1)} %reshape.11.refs_0_.refs_4_), channel_id=1, source_target_pairs={{0,4},{2,6},{8,0},{10,2},{16,8},{18,10},{24,16},{26,18},{28,24},{3... | collective-permute-start | bytes 1990664 | tf_op jit(solution)/shard_map/ppermute | solution.py:456
  9.5 28.6 %copy-start = (f32[512,576]{1,0:T(8,128)}, f32[512,576]{1,0:T(8,128)S(1)}, u32[]{:S(2)}) copy-start(f32[512,576]{1,0:T(8,128)S(1)} %get-tuple-element.68.conv_ref) | copy-start | bytes 3538948
  9.5 2.8 %collective-permute-start = (f32[2,288]{1,0:T(2,128)S(1)}, f32[2,288]{1,0:T(2,128)S(1)}, u32[]{:S(2)}, u32[]{:S(2)}) collective-permute-start(f32[2,288]{1,0:T(2,128)S(1)} %get-tuple-element.70), channel_id=1, source_target_pairs={{0,1},{1,0},{2,3},{3,2},{4,5},{5,4},{6,7},{7,6},{8,9},{9,8},{10,11... | collective-permute-start | bytes 6920 | tf_op jit(solution)/shard_map/ppermute | solution.py:445
  18.2 45.6 %copy-start.2 = (bf16[72,4608]{1,0:T(8,128)(2,1)}, bf16[72,4608]{1,0:T(8,128)(2,1)S(1)}, u32[]{:S(2)}) copy-start(bf16[72,4608]{1,0:T(8,128)(2,1)S(1)} %collective-permute-done.2.refs_1_.refs_4_) | copy-start | bytes 1990660
  18.3 19.7 %collective-permute-start.4 = (bf16[72,4608]{1,0:T(8,128)(2,1)S(1)}, bf16[72,4608]{1,0:T(8,128)(2,1)S(1)}, u32[]{:S(2)}, u32[]{:S(2)}) collective-permute-start(bf16[72,4608]{1,0:T(8,128)(2,1)S(1)} %collective-permute-done.2.refs_1_.refs_4_), channel_id=1, source_target_pairs={{0,8},{2,10},{8,16},{10,18},{16,24},{18,26},{24,28},{26,30},{28,20... | collective-permute-start | bytes 1990664 | tf_op jit(solution)/shard_map/ppermute | solution.py:456
  19.5 18.6 %collective-permute-start.5 = (bf16[72,4608]{1,0:T(8,128)(2,1)S(1)}, bf16[72,4608]{1,0:T(8,128)(2,1)}, u32[]{:S(2)}, u32[]{:S(2)}) collective-permute-start(bf16[72,4608]{1,0:T(8,128)(2,1)S(1)} %collective-permute-done.3.refs_2_.refs_5_), channel_id=1, source_target_pairs={{0,4},{2,6},{8,0},{10,2},{16,8},{18,10},{24,16},{26,18},{28,24},{3... | collective-permute-start | bytes 1990664 | tf_op jit(solution)/shard_map/ppermute | solution.py:456
  19.8 0.9 copy-start.7
  20.7 17.4 %collective-permute-start.1 = (bf16[256,576]{1,0:T(8,128)(2,1)S(1)}, bf16[256,576]{1,0:T(8,128)(2,1)S(1)}, u32[]{:S(2)}, u32[]{:S(2)}) collective-permute-start(bf16[256,576]{1,0:T(8,128)(2,1)S(1)} %get-tuple-element.71), channel_id=1, source_target_pairs={{0,2},{2,4},{4,6},{6,8},{8,10},{10,12},{12,14},{14,16},{16,18},{18... | collective-permute-start | bytes 884744 | tf_op jit(solution)/shard_map/ppermute | solution.py:420
  38.0 14.6 %collective-permute-start.6 = (bf16[72,4608]{1,0:T(8,128)(2,1)S(1)}, bf16[72,4608]{1,0:T(8,128)(2,1)S(1)}, u32[]{:S(2)}, u32[]{:S(2)}) collective-permute-start(bf16[72,4608]{1,0:T(8,128)(2,1)S(1)} %collective-permute-done.4.refs_3_.refs_5_), channel_id=1, source_target_pairs={{0,8},{2,10},{8,16},{10,18},{16,24},{18,26},{24,28},{26,30},{28,20... | collective-permute-start | bytes 1990664 | tf_op jit(solution)/shard_map/ppermute | solution.py:456
  39.2 0.8 copy-start.4
  40.1 15.5 %collective-permute-start.7 = (bf16[72,4608]{1,0:T(8,128)(2,1)}, bf16[72,4608]{1,0:T(8,128)(2,1)}, u32[]{:S(2)}, u32[]{:S(2)}) collective-permute-start(bf16[72,4608]{1,0:T(8,128)(2,1)} %collective-permute-done.5.refs_4_.refs_6_), channel_id=1, source_target_pairs={{0,4},{2,6},{8,0},{10,2},{16,8},{18,10},{24,16},{26,18},{28,24},{3... | collective-permute-start | bytes 1990664 | tf_op jit(solution)/shard_map/ppermute | solution.py:456
  41.7 0.7 copy-start.16
  42.3 19.7 %copy-start.17 = (s32[5]{0:T(128)S(1)}, s32[5]{0:T(128)}, u32[]{:S(2)}) copy-start(s32[5]{0:T(128)} %shard_map.106.facts_ref) | copy-start | bytes 64
  44.1 17.9 %collective-permute-start.10 = (bf16[64,4608]{1,0:T(8,128)(2,1)}, bf16[64,4608]{1,0:T(8,128)(2,1)}, u32[]{:S(2)}, u32[]{:S(2)}) collective-permute-start(bf16[64,4608]{1,0:T(8,128)(2,1)} %shard_map.107.own_ref), channel_id=1, source_target_pairs={{0,2},{2,0},{4,6},{6,4},{8,10},{10,8},{12,14},{14,12},{16,18},{18,... | collective-permute-start | bytes 1769480 | tf_op jit(solution)/shard_map/ppermute | solution.py:437
  55.6 15.5 %collective-permute-start.12 = (bf16[72,4608]{1,0:T(8,128)(2,1)S(1)}, bf16[72,4608]{1,0:T(8,128)(2,1)S(1)}, u32[]{:S(2)}, u32[]{:S(2)}) collective-permute-start(bf16[72,4608]{1,0:T(8,128)(2,1)S(1)} %collective-permute-done.6.refs_0_.refs_4_), channel_id=1, source_target_pairs={{0,8},{2,10},{8,16},{10,18},{16,24},{18,26},{24,28},{26,30},{28,20... | collective-permute-start | bytes 1990664 | tf_op jit(solution)/shard_map/ppermute | solution.py:456
  55.6 13.5 %collective-permute-start.11 = (bf16[72,4096]{1,0:T(8,128)(2,1)}, bf16[72,4096]{1,0:T(8,128)(2,1)}, u32[]{:S(2)}, u32[]{:S(2)}) collective-permute-start(bf16[72,4096]{1,0:T(8,128)(2,1)} %refs_0_.1), channel_id=1, source_target_pairs={{0,4},{2,6},{8,0},{10,2},{16,8},{18,10},{24,16},{26,18},{28,24},{3... | collective-permute-start | bytes 1769480 | tf_op jit(solution)/shard_map/ppermute | solution.py:456
  57.1 23.1 %all-to-all-start = ((bf16[8,8,4096]{2,1,0:T(8,128)(2,1)}), bf16[8,8,4096]{2,1,0:T(8,128)(2,1)S(1)}, u32[]{:S(2)}, u32[]{:S(2)}) async-start(bf16[8,8,4096]{2,1,0:T(8,128)(2,1)} %bitcast.15), calls=%async_computation | async-start | bytes 1048576 | tf_op jit(solution)/shard_map/all_to_all | solution.py:640
  62.0 1.8 %copy-start.5 = (bf16[72,4608]{1,0:T(8,128)(2,1)S(1)}, bf16[72,4608]{1,0:T(8,128)(2,1)}, u32[]{:S(2)}) copy-start(bf16[72,4608]{1,0:T(8,128)(2,1)} %copy-done.4) | copy-start | bytes 1990660
  62.0 1.9 %copy-start.8 = (bf16[72,4608]{1,0:T(8,128)(2,1)S(1)}, bf16[72,4608]{1,0:T(8,128)(2,1)}, u32[]{:S(2)}) copy-start(bf16[72,4608]{1,0:T(8,128)(2,1)} %copy-done.7) | copy-start | bytes 1990660
  66.2 5.0 %collective-permute-start.13 = (f32[128,360]{1,0:T(8,128)S(1)}, f32[128,360]{1,0:T(8,128)S(1)}, u32[]{:S(2)}, u32[]{:S(2)}) collective-permute-start(f32[128,360]{1,0:T(8,128)S(1)} %shard_map.109.own_ref), channel_id=1, source_target_pairs={{0,1},{1,0},{2,3},{3,2},{4,5},{5,4},{6,7},{7,6},{8,9},{9,8},{10,11... | collective-permute-start | bytes 552968 | tf_op jit(solution)/shard_map/ppermute | solution.py:445
  67.5 26.7 %collective-permute-start.9 = (bf16[72,4096]{1,0:T(8,128)(2,1)}, bf16[72,4096]{1,0:T(8,128)(2,1)}, u32[]{:S(2)}, u32[]{:S(2)}) collective-permute-start(bf16[72,4096]{1,0:T(8,128)(2,1)} %refs_0_.1), channel_id=1, source_target_pairs={{0,8},{2,10},{8,16},{10,18},{16,24},{18,26},{24,28},{26,30},{28,20... | collective-permute-start | bytes 1769480 | tf_op jit(solution)/shard_map/ppermute | solution.py:456
  71.2 24.8 %collective-permute-start.16 = (bf16[72,4096]{1,0:T(8,128)(2,1)}, bf16[72,4096]{1,0:T(8,128)(2,1)}, u32[]{:S(2)}, u32[]{:S(2)}) collective-permute-start(bf16[72,4096]{1,0:T(8,128)(2,1)} %collective-permute-done.11.refs_1_), channel_id=1, source_target_pairs={{0,4},{2,6},{8,0},{10,2},{16,8},{18,10},{24,16},{26,18},{28,24},{3... | collective-permute-start | bytes 1769480 | tf_op jit(solution)/shard_map/ppermute | solution.py:456
  74.2 4.2 %collective-permute-start.14 = (f32[128,216]{1,0:T(8,128)S(1)}, f32[128,216]{1,0:T(8,128)S(1)}, u32[]{:S(2)}, u32[]{:S(2)}) collective-permute-start(f32[128,216]{1,0:T(8,128)S(1)} %shard_map.110.own_ref), channel_id=1, source_target_pairs={{0,1},{1,0},{2,3},{3,2},{4,5},{5,4},{6,7},{7,6},{8,9},{9,8},{10,11... | collective-permute-start | bytes 331784 | tf_op jit(solution)/shard_map/ppermute | solution.py:445
  80.2 15.7 %all-to-all-start.1 = ((bf16[8,16,576]{2,1,0:T(8,128)(2,1)}), bf16[8,16,576]{2,1,0:T(8,128)(2,1)S(1)}, u32[]{:S(2)}, u32[]{:S(2)}) async-start(bf16[8,16,576]{2,1,0:T(8,128)(2,1)} %bitcast.4), calls=%async_computation.1 | async-start | bytes 327680 | tf_op jit(solution)/shard_map/all_to_all | solution.py:640
  84.7 12.7 %collective-permute-start.8 = (bf16[64,4096]{1,0:T(8,128)(2,1)S(1)}, bf16[64,4096]{1,0:T(8,128)(2,1)S(1)}, u32[]{:S(2)}, u32[]{:S(2)}) collective-permute-start(bf16[64,4096]{1,0:T(8,128)(2,1)S(1)} %bitcast.6), channel_id=1, source_target_pairs={{0,2},{2,0},{4,6},{6,4},{8,10},{10,8},{12,14},{14,12},{16,18},{18,... | collective-permute-start | bytes 1572872 | tf_op jit(solution)/shard_map/ppermute | solution.py:437
  95.9 11.9 %collective-permute-start.15 = (bf16[72,4096]{1,0:T(8,128)(2,1)}, bf16[72,4096]{1,0:T(8,128)(2,1)S(1)}, u32[]{:S(2)}, u32[]{:S(2)}) collective-permute-start(bf16[72,4096]{1,0:T(8,128)(2,1)} %collective-permute-done.9.refs_0_.refs_3_), channel_id=1, source_target_pairs={{0,8},{2,10},{8,16},{10,18},{16,24},{18,26},{24,28},{26,30},{28,20... | collective-permute-start | bytes 1769480 | tf_op jit(solution)/shard_map/ppermute | solution.py:456
  95.9 11.9 %collective-permute-start.19 = (bf16[72,4096]{1,0:T(8,128)(2,1)}, bf16[72,4096]{1,0:T(8,128)(2,1)S(1)}, u32[]{:S(2)}, u32[]{:S(2)}) collective-permute-start(bf16[72,4096]{1,0:T(8,128)(2,1)} %collective-permute-done.16.refs_2_), channel_id=1, source_target_pairs={{0,4},{2,6},{8,0},{10,2},{16,8},{18,10},{24,16},{26,18},{28,24},{3... | collective-permute-start | bytes 1769480 | tf_op jit(solution)/shard_map/ppermute | solution.py:456
  99.6 13.0 %copy-start.9 = (bf16[72,4608]{1,0:T(8,128)(2,1)S(1)}, bf16[72,4608]{1,0:T(8,128)(2,1)}, u32[]{:S(2)}) copy-start(bf16[72,4608]{1,0:T(8,128)(2,1)} %copy-done.7) | copy-start | bytes 1990660
  99.6 3.9 %collective-permute-start.17 = (f32[128,216]{1,0:T(8,128)S(1)}, f32[128,216]{1,0:T(8,128)S(1)}, u32[]{:S(2)}, u32[]{:S(2)}) collective-permute-start(f32[128,216]{1,0:T(8,128)S(1)} %shard_map.113.refs_0_), channel_id=1, source_target_pairs={{0,1},{1,0},{2,3},{3,2},{4,5},{5,4},{6,7},{7,6},{8,9},{9,8},{10,11... | collective-permute-start | bytes 331784 | tf_op jit(solution)/shard_map/ppermute | solution.py:445
  107.8 11.8 %collective-permute-start.18 = (bf16[72,4096]{1,0:T(8,128)(2,1)S(1)}, bf16[72,4096]{1,0:T(8,128)(2,1)S(1)}, u32[]{:S(2)}, u32[]{:S(2)}) collective-permute-start(bf16[72,4096]{1,0:T(8,128)(2,1)S(1)} %collective-permute-done.15.refs_1_.refs_4_), channel_id=1, source_target_pairs={{0,8},{2,10},{8,16},{10,18},{16,24},{18,26},{24,28},{26,30},{28,20... | collective-permute-start | bytes 1769480 | tf_op jit(solution)/shard_map/ppermute | solution.py:456
  107.8 11.8 %collective-permute-start.20 = (bf16[72,4096]{1,0:T(8,128)(2,1)S(1)}, bf16[72,4096]{1,0:T(8,128)(2,1)S(1)}, u32[]{:S(2)}, u32[]{:S(2)}) collective-permute-start(bf16[72,4096]{1,0:T(8,128)(2,1)S(1)} %collective-permute-done.19.refs_2_.refs_5_), channel_id=1, source_target_pairs={{0,4},{2,6},{8,0},{10,2},{16,8},{18,10},{24,16},{26,18},{28,24},{3... | collective-permute-start | bytes 1769480 | tf_op jit(solution)/shard_map/ppermute | solution.py:456
  111.1 3.9 %collective-permute-start.21 = (f32[128,216]{1,0:T(8,128)S(1)}, f32[128,216]{1,0:T(8,128)S(1)}, u32[]{:S(2)}, u32[]{:S(2)}) collective-permute-start(f32[128,216]{1,0:T(8,128)S(1)} %shard_map.114.refs_0_), channel_id=1, source_target_pairs={{0,1},{1,0},{2,3},{3,2},{4,5},{5,4},{6,7},{7,6},{8,9},{9,8},{10,11... | collective-permute-start | bytes 331784 | tf_op jit(solution)/shard_map/ppermute | solution.py:445
  112.6 2.4 %copy-start.3 = (bf16[72,4608]{1,0:T(8,128)(2,1)S(1)}, bf16[72,4608]{1,0:T(8,128)(2,1)}, u32[]{:S(2)}) copy-start(bf16[72,4608]{1,0:T(8,128)(2,1)} %copy-done.2) | copy-start | bytes 1990660
  112.6 2.4 %copy-start.6 = (bf16[72,4608]{1,0:T(8,128)(2,1)S(1)}, bf16[72,4608]{1,0:T(8,128)(2,1)}, u32[]{:S(2)}) copy-start(bf16[72,4608]{1,0:T(8,128)(2,1)} %copy-done.4) | copy-start | bytes 1990660
  120.1 4.8 %collective-permute-start.22 = (f32[128,144]{1,0:T(8,128)S(1)}, f32[128,144]{1,0:T(8,128)S(1)}, u32[]{:S(2)}, u32[]{:S(2)}) collective-permute-start(f32[128,144]{1,0:T(8,128)S(1)} %shard_map.117.refs_0_), channel_id=1, source_target_pairs={{0,1},{1,0},{2,3},{3,2},{4,5},{5,4},{6,7},{7,6},{8,9},{9,8},{10,11... | collective-permute-start | bytes 221192 | tf_op jit(solution)/shard_map/ppermute | solution.py:445
  124.8 13.5 %collective-permute-start.23 = (bf16[64,4096]{1,0:T(8,128)(2,1)S(1)}, bf16[64,4096]{1,0:T(8,128)(2,1)S(1)}, u32[]{:S(2)}, u32[]{:S(2)}) collective-permute-start(bf16[64,4096]{1,0:T(8,128)(2,1)S(1)} %get-tuple-element.112), channel_id=1, source_target_pairs={{0,2},{2,0},{4,6},{6,4},{8,10},{10,8},{12,14},{14,12},{16,18},{18,... | collective-permute-start | bytes 1572872 | tf_op jit(solution)/shard_map/ppermute | solution.py:437
  132.0 1.7 %collective-permute-start.24 = (bf16[64,2304]{1,0:T(8,128)(2,1)S(1)}, bf16[64,2304]{1,0:T(8,128)(2,1)S(1)}, u32[]{:S(2)}, u32[]{:S(2)}) collective-permute-start(bf16[64,2304]{1,0:T(8,128)(2,1)S(1)} %get-tuple-element.118), channel_id=1, source_target_pairs={{0,2},{2,0},{4,6},{6,4},{8,10},{10,8},{12,14},{14,12},{16,18},{18,... | collective-permute-start | bytes 884744 | tf_op jit(solution)/shard_map/ppermute | solution.py:437
  133.1 3.9 %collective-permute-start.26 = (bf16[64,2304]{1,0:T(8,128)(2,1)S(1)}, bf16[64,2304]{1,0:T(8,128)(2,1)S(1)}, u32[]{:S(2)}, u32[]{:S(2)}) collective-permute-start(bf16[64,2304]{1,0:T(8,128)(2,1)S(1)} %get-tuple-element.126), channel_id=1, source_target_pairs={{0,2},{2,0},{4,6},{6,4},{8,10},{10,8},{12,14},{14,12},{16,18},{18,... | collective-permute-start | bytes 884744 | tf_op jit(solution)/shard_map/ppermute | solution.py:437
  135.0 9.3 %collective-permute-start.25 = (bf16[256,576]{1,0:T(8,128)(2,1)S(1)}, bf16[256,576]{1,0:T(8,128)(2,1)S(1)}, u32[]{:S(2)}, u32[]{:S(2)}) collective-permute-start(bf16[256,576]{1,0:T(8,128)(2,1)S(1)} %get-tuple-element.119), channel_id=1, source_target_pairs={{2,0},{4,2},{6,4},{8,6},{10,8},{12,10},{14,12},{16,14},{18,16},{20... | collective-permute-start | bytes 884744 | tf_op jit(solution)/shard_map/ppermute | solution.py:420
  138.3 6.0 %copy-start.1 = (f32[512,576]{1,0:T(8,128)S(1)}, f32[512,576]{1,0:T(8,128)}, u32[]{:S(2)}) copy-start(f32[512,576]{1,0:T(8,128)} %copy-done) | copy-start | bytes 3538948
  138.3 6.0 %copy-start.13 = (bf16[288,576]{1,0:T(8,128)(2,1)S(1)}, bf16[288,576]{1,0:T(8,128)(2,1)}, u32[]{:S(2)}) copy-start(bf16[288,576]{1,0:T(8,128)(2,1)} %expand_ref.3) | copy-start | bytes 995332
  144.3 2.2 %copy-start.11 = (bf16[9,576,48]{1,2,0:T(8,128)(2,1)S(1)}, bf16[9,576,48]{1,2,0:T(8,128)(2,1)}, u32[]{:S(2)}) copy-start(bf16[9,576,48]{1,2,0:T(8,128)(2,1)} %param.10) | copy-start | bytes 1492996
  144.3 3.9 %copy-start.15 = (bf16[576,288]{0,1:T(8,128)(2,1)S(1)}, bf16[576,288]{0,1:T(8,128)(2,1)}, u32[]{:S(2)}) copy-start(bf16[576,288]{0,1:T(8,128)(2,1)} %param.11) | copy-start | bytes 995332
  145.2 2.9 %collective-permute-start.27 = (f32[2,288]{1,0:T(2,128)S(1)}, f32[2,288]{1,0:T(2,128)S(1)}, u32[]{:S(2)}, u32[]{:S(2)}) collective-permute-start(f32[2,288]{1,0:T(2,128)S(1)} %shard_map.123), channel_id=1, source_target_pairs={{0,1},{1,0},{2,3},{3,2},{4,5},{5,4},{6,7},{7,6},{8,9},{9,8},{10,11... | collective-permute-start | bytes 6920 | tf_op jit(solution)/shard_map/ppermute | solution.py:445
